TPU v7x, 32 devices: a whole 2x2x4 slice. The times are simulated.
32 devices in a mesh: blk: 4 (over y, x), shard: 8 (over z, core).
Axes of the slice: x: 2, y: 2, z: 4, core: 2. Of those that a mesh axis runs over, the one named last changes fastest.
Arguments:
- activations: bfloat16 [12288, 8192], P(('blk', 'shard')), may hold values from -6 to 6
- cotangent: bfloat16 [12288, 1024], P(('blk', 'shard')), may hold values from -6 to 6
- kv_weight: bfloat16 [8192, 1024], P('shard', 'blk'), may hold values from -0.0625 to 0.0625
Outputs:
- key_values: bfloat16 [12288, 1024], P(('blk', 'shard'))
- grad_input: bfloat16 [12288, 8192], P(('blk', 'shard'))
- grad_weight: bfloat16 [8192, 1024], P('shard', 'blk')
All inputs are finite; a program needn't handle non-finite values.
Results may differ from a plain program's by a relative error of at most 0.014.
Values may be sent and summed in bfloat16 or wider, within the bound.
No kernel may reach another device: no remote copies, remote signals or barrier semaphores. Data moves between devices by JAX's collectives and lax.ppermute only.
A program may use at most 256 MiB of HBM per device.

v0:
```python
import math

import jax
import jax.numpy as jnp
from jax import lax
from jax.sharding import PartitionSpec as P


def passed_along(array, axis, by):
    count = lax.axis_size(axis)
    return lax.ppermute(array, axis, [(i, (i + by) % count) for i in range(count)])


def local(activations, cotangent, kv_weight):
    blocks = lax.axis_size("blk")
    cycle_pos = lax.axis_index("blk")
    col_width = kv_weight.shape[1]
    row_count = kv_weight.shape[0]
    tok_rows = activations.shape[0]
    features = activations.shape[1]
    key_values = jnp.zeros((tok_rows, col_width * blocks), jnp.bfloat16)
    grad_input = jnp.zeros((tok_rows, features), jnp.float32)
    accumulator = jnp.zeros((row_count, col_width), jnp.float32)
    carried = kv_weight
    for step in range(blocks):
        owner_col = (cycle_pos - step) % blocks
        cot_block = lax.dynamic_slice_in_dim(cotangent, owner_col * col_width, col_width, 1)

        def visit_rows(carry, piece, start, cot_block=cot_block):
            key_sum, input_sum = carry
            key_sum = jnp.dot(activations, piece, preferred_element_type=jnp.float32)
            earlier = input_sum
            added = lax.dot_general(
                cot_block, piece, (((1,), (1,)), ((), ())), preferred_element_type=jnp.float32
            )
            input_sum = earlier + added
            return (key_sum, input_sum)

        empty_keys = jnp.zeros((tok_rows, col_width), jnp.float32)
        key_part, grad_input = visit_rows(
            (empty_keys, grad_input),
            lax.all_gather(carried, "shard", axis=0, tiled=True),
            jnp.int32(0),
        )
        key_values = lax.dynamic_update_slice_in_dim(
            key_values, key_part.astype(jnp.bfloat16), owner_col * col_width, 1
        )
        if step + 1 < blocks:
            carried = passed_along(carried, "blk", 1)
        target_col = (cycle_pos - step - 1) % blocks
        cot_target = lax.dynamic_slice_in_dim(cotangent, target_col * col_width, col_width, 1)

        def grad_term(start, count, cot_target=cot_target):
            return lax.dot_general(
                activations,
                cot_target,
                (((0,), (0,)), ((), ())),
                preferred_element_type=jnp.float32,
            )

        grad_share = lax.psum_scatter(
            grad_term(jnp.int32(0), row_count * lax.axis_size("shard")).astype(jnp.bfloat16),
            "shard",
            scatter_dimension=0,
            tiled=True,
        ).astype(jnp.float32)
        accumulator = accumulator + grad_share
        if step + 1 < blocks:
            accumulator = passed_along(accumulator, "blk", 1)
    total_tokens = tok_rows * blocks * lax.axis_size("shard")
    grad_weight = (accumulator * (1.0 / math.sqrt(total_tokens))).astype(jnp.bfloat16)
    return (key_values, grad_input.astype(jnp.bfloat16), grad_weight)


def solution(mesh):
    placed = (P(("blk", "shard"), None), P(("blk", "shard"), None), P("shard", "blk"))
    return jax.shard_map(
        local,
        mesh=mesh,
        in_specs=placed,
        out_specs=(P(("blk", "shard"), None), P(("blk", "shard"), None), P("shard", "blk")),
        check_vma=False,
    )
```

profile of v0, /device:TPU:0, one launch (start us, length us, event | category | flops | bytes accessed | tf_op | source)
XLA Modules:
  0.0 414.2 jit_solution(10825680793375347347)
XLA Ops:
  7.2 0.0 all-gather.5.cloned.1.call-start
  7.2 0.7 all-gather.5.cloned.1.call-update
  7.9 0.0 reduce-scatter.5.cloned.1.call-start
  8.0 0.3 copy-done
  8.3 7.2 %fusion = bf16[8192,256]{0,1:T(8,128)(2,1)} fusion(bf16[384,8192]{1,0:T(8,128)(2,1)} %param.3, bf16[384,1024]{1,0:T(8,128)(2,1)S(1)} %copy-done, s32[]{:T(128)S(6)} %select_n.54), kind=kOutput, calls=%fused_computation.5 | convolution fusion | flops 1612709888 | bytes 10682372 | tf_op jit(solution)/shard_map/dot_general | solution.py:54
  15.6 0.0 all-gather.7.cloned.1.call-start
  15.6 3.0 collective-permute-start
  18.6 12.9 %collective-permute-done = bf16[1024,256]{1,0:T(8,128)(2,1)S(1)} collective-permute-done((bf16[1024,256]{1,0:T(8,128)(2,1)S(1)}, bf16[1024,256]{1,0:T(8,128)(2,1)S(1)}, u32[]{:S(2)}, u32[]{:S(2)}) %collective-permute-start) | collective-permute-done | bytes 524320 | tf_op jit(solution)/shard_map/ppermute | solution.py:11
  31.5 0.8 copy-done.5
  32.3 0.0 reduce-scatter.7.cloned.1.call-start
  32.4 7.3 %fusion.1 = bf16[8192,256]{0,1:T(8,128)(2,1)} fusion(bf16[384,8192]{1,0:T(8,128)(2,1)} %param.3, bf16[384,1024]{1,0:T(8,128)(2,1)S(1)} %copy-done, s32[]{:T(128)S(6)} %select_n.56), kind=kOutput, calls=%fused_computation.6 | convolution fusion | flops 1612709888 | bytes 10682372 | tf_op jit(solution)/shard_map/dot_general | solution.py:54
  39.7 0.0 all-gather.9.cloned.1.call-start
  39.8 0.8 collective-permute-start.1
  40.6 13.4 %collective-permute-done.1 = bf16[1024,256]{1,0:T(8,128)(2,1)S(1)} collective-permute-done((bf16[1024,256]{1,0:T(8,128)(2,1)S(1)}, bf16[1024,256]{1,0:T(8,128)(2,1)S(1)}, u32[]{:S(2)}, u32[]{:S(2)}) %collective-permute-start.1) | collective-permute-done | bytes 524320 | tf_op jit(solution)/shard_map/ppermute | solution.py:11
  53.9 0.8 copy-done.7
  54.8 0.0 reduce-scatter.9.cloned.1.call-start
  54.9 7.3 %fusion.2 = bf16[8192,256]{0,1:T(8,128)(2,1)} fusion(bf16[384,8192]{1,0:T(8,128)(2,1)} %param.3, bf16[384,1024]{1,0:T(8,128)(2,1)S(1)} %copy-done, s32[]{:T(128)S(6)} %select_n.58), kind=kOutput, calls=%fused_computation.7 | convolution fusion | flops 1612709888 | bytes 10682372 | tf_op jit(solution)/shard_map/dot_general | solution.py:54
  62.2 0.0 all-gather.11.cloned.1.call-start
  62.3 0.1 collective-permute-start.2
  62.4 13.2 %collective-permute-done.2 = bf16[1024,256]{1,0:T(8,128)(2,1)S(1)} collective-permute-done((bf16[1024,256]{1,0:T(8,128)(2,1)S(1)}, bf16[1024,256]{1,0:T(8,128)(2,1)S(1)}, u32[]{:S(2)}, u32[]{:S(2)}) %collective-permute-start.2) | collective-permute-done | bytes 524320 | tf_op jit(solution)/shard_map/ppermute | solution.py:11
  75.6 0.8 copy-done.9
  76.4 0.2 reduce-scatter.11.cloned.1.call-start
  76.7 7.2 %fusion.3 = bf16[8192,256]{0,1:T(8,128)(2,1)} fusion(bf16[384,8192]{1,0:T(8,128)(2,1)} %param.3, bf16[384,1024]{1,0:T(8,128)(2,1)S(1)} %copy-done, s32[]{:T(128)S(6)} %select_n.60), kind=kOutput, calls=%fused_computation.8 | convolution fusion | flops 1612709888 | bytes 10682372 | tf_op jit(solution)/shard_map/dot_general | solution.py:54
  83.9 0.0 all-gather.5.cloned.1.call-done
  83.9 8.8 %fusion.9 = f32[384,8192]{1,0:T(8,128)} fusion(bf16[8192,256]{1,0:T(8,128)(2,1)} %all-gather.5.cloned.1.call-done, bf16[384,1024]{1,0:T(8,128)(2,1)S(1)} %copy-done, s32[]{:T(128)S(6)} %select_n.52), kind=kOutput, calls=%fused_computation.21 | convolution fusion | flops 1610612736 | bytes 16973828 | tf_op jit(solution)/shard_map/dot_general | solution.py:33
  92.7 1.0 broadcast_in_dim.3
  93.7 5.4 %fusion.7 = bf16[384,1024]{1,0:T(8,128)(2,1)} fusion(bf16[384,1024]{1,0:T(8,128)(2,1)} %broadcast_in_dim.3, s32[]{:T(128)S(6)} %select_n.52, bf16[384,8192]{1,0:T(8,128)(2,1)} %param.3, bf16[8192,256]{1,0:T(8,128)(2,1)S(1)} %copy-done.1), kind=kOutput, calls=%fused_computation.16 | convolution fusion | flops 1610711040 | bytes 10682372 | tf_op jit(solution)/shard_map/dot_general | solution.py:31
  99.0 12.1 %reduce-scatter.5.cloned.1.call-done = bf16[1024,256]{0,1:T(8,128)(2,1)} async-done(((bf16[8192,256]{0,1:T(8,128)(2,1)}), bf16[1024,256]{0,1:T(8,128)(2,1)}) %reduce-scatter.5.cloned.1.call-update) | async-done | bytes 524304 | tf_op jit(solution)/shard_map/reduce_scatter | solution.py:61
  111.1 1.1 convert_element_type.61
  112.3 1.5 collective-permute-start.3
  113.8 44.8 %all-gather.7.cloned.1.call-done = bf16[8192,256]{1,0:T(8,128)(2,1)} async-done(((bf16[1024,256]{1,0:T(8,128)(2,1)}), bf16[8192,256]{1,0:T(8,128)(2,1)}) %all-gather.7.cloned.1.call-update) | async-done | bytes 4194320 | tf_op jit(solution)/shard_map/all_gather | solution.py:42
  158.6 8.7 %fusion.17 = f32[384,8192]{1,0:T(8,128)} fusion(bf16[8192,256]{1,0:T(8,128)(2,1)} %all-gather.7.cloned.1.call-done, bf16[384,1024]{1,0:T(8,128)(2,1)S(1)} %copy-done, s32[]{:T(128)S(6)} %select_n.54), kind=kOutput, calls=%fused_computation.29 | convolution fusion | flops 1610612736 | bytes 16973828 | tf_op jit(solution)/shard_map/dot_general | solution.py:33
  167.4 5.3 %fusion.6 = bf16[384,1024]{1,0:T(8,128)(2,1)} fusion(bf16[384,1024]{1,0:T(8,128)(2,1)} %fusion.7, s32[]{:T(128)S(6)} %select_n.54, bf16[384,8192]{1,0:T(8,128)(2,1)} %param.3, bf16[8192,256]{1,0:T(8,128)(2,1)S(1)} %copy-done.2), kind=kOutput, calls=%fused_computation.14 | convolution fusion | flops 1610711040 | bytes 10682372 | tf_op jit(solution)/shard_map/dot_general | solution.py:31
  172.7 36.9 %reduce-scatter.7.cloned.1.call-done = bf16[1024,256]{0,1:T(8,128)(2,1)} async-done(((bf16[8192,256]{0,1:T(8,128)(2,1)}), bf16[1024,256]{0,1:T(8,128)(2,1)}) %reduce-scatter.7.cloned.1.call-update) | async-done | bytes 524304 | tf_op jit(solution)/shard_map/reduce_scatter | solution.py:61
  209.5 1.2 convert_add_fusion.1
  210.8 1.7 collective-permute-start.4
  212.5 43.8 %all-gather.9.cloned.1.call-done = bf16[8192,256]{1,0:T(8,128)(2,1)} async-done(((bf16[1024,256]{1,0:T(8,128)(2,1)}), bf16[8192,256]{1,0:T(8,128)(2,1)}) %all-gather.9.cloned.1.call-update) | async-done | bytes 4194320 | tf_op jit(solution)/shard_map/all_gather | solution.py:42
  256.3 8.8 %fusion.14 = f32[384,8192]{1,0:T(8,128)} fusion(bf16[8192,256]{1,0:T(8,128)(2,1)} %all-gather.9.cloned.1.call-done, bf16[384,1024]{1,0:T(8,128)(2,1)S(1)} %copy-done, s32[]{:T(128)S(6)} %select_n.56), kind=kOutput, calls=%fused_computation.26 | convolution fusion | flops 1610612736 | bytes 16973828 | tf_op jit(solution)/shard_map/dot_general | solution.py:33
  265.1 5.3 %fusion.5 = bf16[384,1024]{1,0:T(8,128)(2,1)} fusion(bf16[384,1024]{1,0:T(8,128)(2,1)} %fusion.6, s32[]{:T(128)S(6)} %select_n.56, bf16[384,8192]{1,0:T(8,128)(2,1)} %param.3, bf16[8192,256]{1,0:T(8,128)(2,1)S(1)} %copy-done.3), kind=kOutput, calls=%fused_computation.12 | convolution fusion | flops 1610711040 | bytes 10682372 | tf_op jit(solution)/shard_map/dot_general | solution.py:31
  270.4 36.8 %reduce-scatter.9.cloned.1.call-done = bf16[1024,256]{0,1:T(8,128)(2,1)} async-done(((bf16[8192,256]{0,1:T(8,128)(2,1)}), bf16[1024,256]{0,1:T(8,128)(2,1)}) %reduce-scatter.9.cloned.1.call-update) | async-done | bytes 524304 | tf_op jit(solution)/shard_map/reduce_scatter | solution.py:61
  307.2 1.2 convert_add_fusion
  308.4 1.5 collective-permute-start.5
  310.0 44.2 %all-gather.11.cloned.1.call-done = bf16[8192,256]{1,0:T(8,128)(2,1)} async-done(((bf16[1024,256]{1,0:T(8,128)(2,1)}), bf16[8192,256]{1,0:T(8,128)(2,1)}) %all-gather.11.cloned.1.call-update) | async-done | bytes 4194320 | tf_op jit(solution)/shard_map/all_gather | solution.py:42
  354.1 17.9 %add_convert_fusion = bf16[384,8192]{1,0:T(8,128)(2,1)} fusion(f32[384,8192]{1,0:T(8,128)} %fusion.14, f32[384,8192]{1,0:T(8,128)} %fusion.9, f32[384,8192]{1,0:T(8,128)} %fusion.17, bf16[8192,256]{1,0:T(8,128)(2,1)} %all-gather.11.cloned.1.call-done, bf16[384,1024]{1,0:T(8,128)(2,1)S(1)} %copy-done, s32[]{:T(128)S(6)} %select_n.58), kind=kOutput, calls=%fused_computation | convolution fusion | flops 1623195648 | bytes 48431108 | tf_op jit(solution)/shard_map/dot_general | solution.py:33
  372.0 6.6 %fusion.4 = bf16[384,1024]{1,0:T(8,128)(2,1)} fusion(bf16[384,1024]{1,0:T(8,128)(2,1)} %fusion.5, s32[]{:T(128)S(6)} %select_n.58, bf16[384,8192]{1,0:T(8,128)(2,1)} %param.3, bf16[8192,256]{1,0:T(8,128)(2,1)} %all-gather.11.cloned.1.call-done), kind=kOutput, calls=%fused_computation.10 | convolution fusion | flops 1610711040 | bytes 10682372 | tf_op jit(solution)/shard_map/dot_general | solution.py:31
  378.6 26.6 %reduce-scatter.11.cloned.1.call-done = bf16[1024,256]{0,1:T(8,128)(2,1)} async-done(((bf16[8192,256]{0,1:T(8,128)(2,1)}), bf16[1024,256]{0,1:T(8,128)(2,1)}) %reduce-scatter.11.cloned.1.call-update) | async-done | bytes 524304 | tf_op jit(solution)/shard_map/reduce_scatter | solution.py:61
  405.2 1.2 multiply_convert_fusion
  406.4 1.0 copy.6
  (26 shorter events, 0.2 us)
Async XLA Ops:
  7.2 1.1 copy-start
  7.2 76.7 %all-gather.5.cloned.1.call-start = ((), (), s32[]{:S(2)}) async-start(), calls=%async_computation.4 | async-start | bytes 4718592 | tf_op jit(solution)/shard_map/all_gather | solution.py:42
  7.9 103.2 %reduce-scatter.5.cloned.1.call-start = ((), (), s32[]{:S(2)}) async-start(), calls=%async_computation.8 | async-start | bytes 4718592 | tf_op jit(solution)/shard_map/reduce_scatter | solution.py:61
  8.3 7.3 %copy-start.4 = (bf16[1024,256]{1,0:T(8,128)(2,1)S(1)}, bf16[1024,256]{1,0:T(8,128)(2,1)}, u32[]{:S(2)}) copy-start(bf16[1024,256]{1,0:T(8,128)(2,1)} %param.5) | copy-start | bytes 1572868
  15.6 143.1 %all-gather.7.cloned.1.call-start = ((), (), s32[]{:S(2)}) async-start(), calls=%async_computation.5 | async-start | bytes 4718592 | tf_op jit(solution)/shard_map/all_gather | solution.py:42
  15.6 15.9 %collective-permute-start = (bf16[1024,256]{1,0:T(8,128)(2,1)S(1)}, bf16[1024,256]{1,0:T(8,128)(2,1)S(1)}, u32[]{:S(2)}, u32[]{:S(2)}) collective-permute-start(bf16[1024,256]{1,0:T(8,128)(2,1)S(1)} %copy-done.4), channel_id=1, source_target_pairs={{0,8},{8,16},{16,24},{24,0},{1,9},{9,17},{17,25},{25,1},{2,10},{10... | collective-permute-start | bytes 1572872 | tf_op jit(solution)/shard_map/ppermute | solution.py:11
  31.5 0.8 copy-start.5
  32.3 177.2 %reduce-scatter.7.cloned.1.call-start = ((), (), s32[]{:S(2)}) async-start(), calls=%async_computation.9 | async-start | bytes 4718592 | tf_op jit(solution)/shard_map/reduce_scatter | solution.py:61
  32.4 7.4 %copy-start.6 = (bf16[1024,256]{1,0:T(8,128)(2,1)S(1)}, bf16[1024,256]{1,0:T(8,128)(2,1)}, u32[]{:S(2)}) copy-start(bf16[1024,256]{1,0:T(8,128)(2,1)} %copy-done.5) | copy-start | bytes 1572868
  39.7 216.6 %all-gather.9.cloned.1.call-start = ((), (), s32[]{:S(2)}) async-start(), calls=%async_computation.6 | async-start | bytes 4718592 | tf_op jit(solution)/shard_map/all_gather | solution.py:42
  39.8 14.2 %collective-permute-start.1 = (bf16[1024,256]{1,0:T(8,128)(2,1)S(1)}, bf16[1024,256]{1,0:T(8,128)(2,1)S(1)}, u32[]{:S(2)}, u32[]{:S(2)}) collective-permute-start(bf16[1024,256]{1,0:T(8,128)(2,1)S(1)} %copy-done.6), channel_id=1, source_target_pairs={{0,8},{8,16},{16,24},{24,0},{1,9},{9,17},{17,25},{25,1},{2,10},{10... | collective-permute-start | bytes 1572872 | tf_op jit(solution)/shard_map/ppermute | solution.py:11
  53.9 0.8 copy-start.7
  54.8 252.4 %reduce-scatter.9.cloned.1.call-start = ((), (), s32[]{:S(2)}) async-start(), calls=%async_computation.10 | async-start | bytes 4718592 | tf_op jit(solution)/shard_map/reduce_scatter | solution.py:61
  54.9 7.4 %copy-start.8 = (bf16[1024,256]{1,0:T(8,128)(2,1)S(1)}, bf16[1024,256]{1,0:T(8,128)(2,1)}, u32[]{:S(2)}) copy-start(bf16[1024,256]{1,0:T(8,128)(2,1)} %copy-done.7) | copy-start | bytes 1572868
  62.2 291.9 %all-gather.11.cloned.1.call-start = ((), (), s32[]{:S(2)}) async-start(), calls=%async_computation.7 | async-start | bytes 4718592 | tf_op jit(solution)/shard_map/all_gather | solution.py:42
  62.3 13.3 %collective-permute-start.2 = (bf16[1024,256]{1,0:T(8,128)(2,1)S(1)}, bf16[1024,256]{1,0:T(8,128)(2,1)S(1)}, u32[]{:S(2)}, u32[]{:S(2)}) collective-permute-start(bf16[1024,256]{1,0:T(8,128)(2,1)S(1)} %copy-done.8), channel_id=1, source_target_pairs={{0,8},{8,16},{16,24},{24,0},{1,9},{9,17},{17,25},{25,1},{2,10},{10... | collective-permute-start | bytes 1572872 | tf_op jit(solution)/shard_map/ppermute | solution.py:11
  75.6 0.8 copy-start.9
  76.4 328.8 %reduce-scatter.11.cloned.1.call-start = ((), (), s32[]{:S(2)}) async-start(), calls=%async_computation.11 | async-start | bytes 4718592 | tf_op jit(solution)/shard_map/reduce_scatter | solution.py:61
  83.9 9.7 %copy-start.1 = (bf16[8192,256]{1,0:T(8,128)(2,1)S(1)}, bf16[8192,256]{1,0:T(8,128)(2,1)}, u32[]{:S(2)}) copy-start(bf16[8192,256]{1,0:T(8,128)(2,1)} %all-gather.5.cloned.1.call-done) | copy-start | bytes 12582916
  112.3 97.3 %collective-permute-start.3 = (f32[1024,256]{0,1:T(8,128)S(1)}, f32[1024,256]{0,1:T(8,128)S(1)}, u32[]{:S(2)}, u32[]{:S(2)}) collective-permute-start(f32[1024,256]{0,1:T(8,128)S(1)} %convert_element_type.61), channel_id=1, source_target_pairs={{0,8},{8,16},{16,24},{24,0},{1,9},{9,17},{17,25},{25,1},{2,10},{10... | collective-permute-start | bytes 3145736 | tf_op jit(solution)/shard_map/ppermute | solution.py:11
  158.6 8.7 %copy-start.2 = (bf16[8192,256]{1,0:T(8,128)(2,1)S(1)}, bf16[8192,256]{1,0:T(8,128)(2,1)}, u32[]{:S(2)}) copy-start(bf16[8192,256]{1,0:T(8,128)(2,1)} %all-gather.7.cloned.1.call-done) | copy-start | bytes 12582916
  210.8 96.5 %collective-permute-start.4 = (f32[1024,256]{0,1:T(8,128)S(1)}, f32[1024,256]{0,1:T(8,128)S(1)}, u32[]{:S(2)}, u32[]{:S(2)}) collective-permute-start(f32[1024,256]{0,1:T(8,128)S(1)} %convert_add_fusion.1), channel_id=1, source_target_pairs={{0,8},{8,16},{16,24},{24,0},{1,9},{9,17},{17,25},{25,1},{2,10},{10... | collective-permute-start | bytes 3145736 | tf_op jit(solution)/shard_map/ppermute | solution.py:11
  256.3 8.8 %copy-start.3 = (bf16[8192,256]{1,0:T(8,128)(2,1)S(1)}, bf16[8192,256]{1,0:T(8,128)(2,1)}, u32[]{:S(2)}) copy-start(bf16[8192,256]{1,0:T(8,128)(2,1)} %all-gather.9.cloned.1.call-done) | copy-start | bytes 12582916
  308.4 96.7 %collective-permute-start.5 = (f32[1024,256]{0,1:T(8,128)S(1)}, f32[1024,256]{0,1:T(8,128)S(1)}, u32[]{:S(2)}, u32[]{:S(2)}) collective-permute-start(f32[1024,256]{0,1:T(8,128)S(1)} %convert_add_fusion), channel_id=1, source_target_pairs={{0,8},{8,16},{16,24},{24,0},{1,9},{9,17},{17,25},{25,1},{2,10},{10... | collective-permute-start | bytes 3145736 | tf_op jit(solution)/shard_map/ppermute | solution.py:11
Sparse Core Ops, SparseCore 0:
  9.6 49.8 all-gather.4
  62.4 48.7 reduce-scatter.4
  113.3 45.2 all-gather.6
  160.8 48.7 reduce-scatter.6
  211.0 45.2 all-gather.8
  258.5 48.7 reduce-scatter.8
  308.8 45.2 all-gather.10
  356.4 48.7 reduce-scatter.10
where the time goes:
time: 415 us; the launch traced here: 414 us
  waiting for transfers between devices  285 us (69%)
  matrix products  95.8 us (23%)
  between operations  14.4 us (3%)
  starting transfers between devices  9.13 us (2%)
  other arithmetic  4.78 us (1%)
  local copies, waits for them, and re-layouts  4.73 us (1%)
    all_gather x4, waiting for transfers between devices, local(): lax.all_gather(carried, 'shard', axis=0, tiled=True)  133 us
    reduce_scatter x4, waiting for transfers between devices, local(): lax.psum_scatter(grad_term(jnp.int32(0), row_count * lax.axis_size('shard...  112 us
    dot_general x4, matrix products, visit_rows(): lax.dot_general(cot_block, piece, (((1,), (1,)), ((), ())), preferred_ele...  44.2 us
    ppermute x6, waiting for transfers between devices, passed_along(): lax.ppermute(array, axis, [(i, (i + by) % count) for i in range(count)])  39.5 us
    dot_general x4, matrix products, grad_term(): lax.dot_general(activations, cot_target, (((0,), (0,)), ((), ())), prefer...  29.1 us
    dot_general x4, matrix products, visit_rows(): key_sum = jnp.dot(activations, piece, preferred_element_type=jnp.float32)  22.6 us
    ppermute x6, starting transfers between devices, passed_along(): lax.ppermute(array, axis, [(i, (i + by) % count) for i in range(count)])  8.62 us
  transfers between devices with their start and end apart: 14, of which 10 were waited for; matrix products, arithmetic and copies ran while one was open for 24% of the time, Pallas kernels for 0%

commit v1 on v0

v1 whole, which is shorter than its diff:
```python
import math

import jax
import jax.numpy as jnp
from jax import lax
from jax.sharding import Mesh, PartitionSpec as P


def swapped(array):
    return lax.ppermute(array, "core", [(0, 1), (1, 0)])


def local(activations, cotangent, kv_weight):
    blocks, chips = lax.axis_size("blk"), lax.axis_size("chip")
    core = lax.axis_index("core")
    tokens, features = activations.shape
    rows, cols = kv_weight.shape
    columns = cotangent.shape[1]
    by_core = activations.reshape(tokens, chips, 2, rows)
    mine = lax.dynamic_index_in_dim(by_core, core, 2, keepdims=False)
    other = lax.dynamic_index_in_dim(by_core, 1 - core, 2, keepdims=False)
    acts = jnp.concatenate([mine, swapped(other)], 0)
    cots = jnp.concatenate([cotangent, swapped(cotangent)], 0)
    weight = lax.all_gather(kv_weight, ("blk", "chip"), axis=0, tiled=False)
    weight = weight.reshape(blocks, chips, rows, cols)
    terms = jnp.einsum(
        "tzr,tbc->bzrc", acts, cots.reshape(2 * tokens, blocks, cols),
        preferred_element_type=jnp.float32,
    ).astype(jnp.bfloat16).reshape(blocks * chips, rows, cols)
    total = lax.psum_scatter(terms, ("blk", "chip"), scatter_dimension=0, tiled=False)
    count = tokens * blocks * chips * 2
    grad_weight = (total.astype(jnp.float32) * (1.0 / math.sqrt(count))).astype(jnp.bfloat16)

    full = weight.transpose(1, 2, 0, 3).reshape(chips * rows, columns)
    keys = jnp.dot(acts.reshape(2 * tokens, chips * rows), full, preferred_element_type=jnp.float32)
    key_values = (keys[:tokens] + swapped(keys[tokens:])).astype(jnp.bfloat16)
    inputs = lax.dot_general(
        cots, full, (((1,), (1,)), ((), ())), preferred_element_type=jnp.float32
    ).astype(jnp.bfloat16).reshape(2 * tokens, chips, rows)
    near, far = inputs[:tokens], swapped(inputs[tokens:])
    low = jnp.where(core == 0, near, far)
    high = jnp.where(core == 0, far, near)
    grad_input = jnp.stack([low, high], 2).reshape(tokens, features)
    return (key_values, grad_input, grad_weight)


def solution(mesh):
    blocks, shards = mesh.shape["blk"], mesh.shape["shard"]
    split = Mesh(mesh.devices.reshape(blocks, shards // 2, 2), ("blk", "chip", "core"))
    by_token = P(("blk", "chip", "core"), None)
    by_piece = P(("chip", "core"), "blk")
    return jax.shard_map(
        local,
        mesh=split,
        in_specs=(by_token, by_token, by_piece),
        out_specs=(by_token, by_token, by_piece),
        check_vma=False,
    )
```

time: 415 us -> 319 us (0.77)
  waiting for transfers between devices: 285 us -> 151 us
  local copies, waits for them, and re-layouts: 4.73 us -> 102 us
  matrix products: 95.8 us -> 31.1 us
  other arithmetic: 4.78 us -> 19 us
  starting transfers between devices: 9.13 us -> 1.14 us
    all_gather x4 -> x1, waiting for transfers between devices: 133 us -> 59.8 us  [local(): weight = lax.all_gather(kv_weight, ('blk', 'chip'), axis=0, tiled=False)]
    dot_general x12 -> x3, matrix products: 95.8 us -> 31.1 us  [the longest x1 11.3 us: local(): jnp.einsum('tzr,tbc->bzrc', acts, cots.reshape(2 * tokens, blocks, cols),...]
    ppermute x6 -> x4, waiting for transfers between devices: 39.5 us -> 1.72 us  [swapped(): return lax.ppermute(array, 'core', [(0, 1), (1, 0)])]
    reshape x0 -> x3, local copies, waits for them, and re-layouts: none -> 35.6 us  [the longest x1 12.3 us: local(): terms = jnp.einsum('tzr,tbc->bzrc', acts, cots.reshape(2 * tokens, blocks...]
    reduce_scatter x4 -> x1, waiting for transfers between devices: 112 us -> 88.5 us  [local(): lax.psum_scatter(terms, ('blk', 'chip'), scatter_dimension=0, tiled=False)]
    unnamed x21 -> x9, local copies, waits for them, and re-layouts: 3.75 us -> 22.3 us
    slice x0 -> x4, local copies, waits for them, and re-layouts: none -> 14.5 us  [the longest x3 13.2 us: local(): near, far = (inputs[:tokens], swapped(inputs[tokens:]))]
    another operation x0 -> x2, other arithmetic: none -> 13.9 us  [local(): grad_input = jnp.stack([low, high], 2).reshape(tokens, features)]
  transfers between devices with their start and end apart: 14 -> 6, of which waited for: 10 -> 3; matrix products, arithmetic and copies ran while one was open for 24% -> 46% of each run, Pallas kernels for 0% -> 0%
where the time goes in v1:
time: 319 us; the launch traced here: 318 us
  waiting for transfers between devices  151 us (47%)
  local copies, waits for them, and re-layouts  102 us (32%)
  matrix products  31.1 us (10%)
  other arithmetic  19 us (6%)
  between operations  14.1 us (4%)
    reduce_scatter x1, waiting for transfers between devices, local(): lax.psum_scatter(terms, ('blk', 'chip'), scatter_dimension=0, tiled=False)  88.5 us
    all_gather x1, waiting for transfers between devices, local(): weight = lax.all_gather(kv_weight, ('blk', 'chip'), axis=0, tiled=False)  59.8 us
    unnamed x9, local copies, waits for them, and re-layouts  22.3 us
    another operation x2, other arithmetic, local(): grad_input = jnp.stack([low, high], 2).reshape(tokens, features)  13.9 us
    slice x3, local copies, waits for them, and re-layouts, local(): near, far = (inputs[:tokens], swapped(inputs[tokens:]))  13.2 us
    reshape x1, local copies, waits for them, and re-layouts, local(): terms = jnp.einsum('tzr,tbc->bzrc', acts, cots.reshape(2 * tokens, blocks...  12.3 us
    reshape x1, local copies, waits for them, and re-layouts, local(): weight = weight.reshape(blocks, chips, rows, cols)  12.2 us
    dot_general x1, matrix products, local(): jnp.einsum('tzr,tbc->bzrc', acts, cots.reshape(2 * tokens, blocks, cols),...  11.3 us
  transfers between devices with their start and end apart: 6, of which 3 were waited for; matrix products, arithmetic and copies ran while one was open for 46% of the time, Pallas kernels for 0%

profile of v1, /device:TPU:0, one launch (start us, length us, event | category | flops | bytes accessed | tf_op | source)
XLA Modules:
  0.0 318.0 jit_solution(9159813879423829105)
XLA Ops:
  7.2 0.0 all-gather.3.cloned.1.call-start
  7.2 0.7 all-gather.3.cloned.1.call-update
  7.9 0.0 reduce-scatter.2.cloned.1.call-start
  7.9 8.6 %copy.18 = bf16[384,8192]{0,1:T(8,128)(2,1)} copy(bf16[384,8192]{1,0:T(8,128)(2,1)} %param.3) | data formatting | bytes 12582912 | tf_op args[0]
  16.6 5.2 %constant_dynamic-slice_fusion.1 = (bf16[384,4,1,1024]{0,3,2,1:T(8,128)(2,1)S(1)}, bf16[384,4,1,1024]{0,3,2,1:T(8,128)(2,1)}) fusion(bf16[384,4,2,1024]{0,3,2,1:T(8,128)(2,1)} %bitcast.32, s32[]{:T(128)S(6)} %select_n.19, s32[]{:T(128)S(6)} %select_n.20), kind=kLoop, calls=%fused_computation.19 | loop fusion | bytes 12582920 | tf_op jit(solution)/shard_map/jit(dynamic_index_in_dim)/dynamic_slice | solution.py:20
  21.7 4.7 %copy.19 = bf16[384,4,1,1024]{3,0,1,2:T(8,128)(2,1)} copy(bf16[384,4,1,1024]{0,3,2,1:T(8,128)(2,1)} %get-tuple-element.8) | data formatting | bytes 6291456 | tf_op jit(solution)/shard_map/jit(dynamic_index_in_dim)/dynamic_slice | solution.py:21
  26.4 0.4 collective-permute-start
  26.9 0.1 collective-permute-start.2
  26.9 2.9 copy.24
  29.8 2.1 constant_dynamic-update-slice_fusion.1
  31.9 1.7 collective-permute-done.2
  33.6 2.1 constant_dynamic-update-slice_fusion
  35.7 2.6 copy.23
  38.3 0.0 collective-permute-done
  38.3 11.3 %convolution_convert_fusion = bf16[4,256,4,1024]{3,1,2,0:T(8,128)(2,1)} fusion(bf16[768,4,256,1]{0,2,3,1:T(8,128)(2,1)} %bitcast.41, bf16[384,4,1024]{2,0,1:T(8,128)(2,1)} %collective-permute-done, bf16[384,4,1024]{2,0,1:T(8,128)(2,1)} %bitcast.40), kind=kOutput, calls=%fused_computation | convolution fusion | flops 6459228160 | bytes 16252928 | tf_op jit(solution)/shard_map/tzr,tbc->bzrc/dot_general | solution.py:26
  49.6 12.3 %copy.25 = bf16[16,1024,256]{2,1,0:T(8,128)(2,1)} copy(bf16[16,1024,256]{1,2,0:T(8,128)(2,1)} %bitcast.37) | data formatting | bytes 16777216 | tf_op jit(solution)/shard_map/reshape | solution.py:29
  61.9 0.0 reduce-scatter.2.cloned.1.call-update
  61.9 4.6 %copy.20 = bf16[384,4,1024]{0,2,1:T(8,128)(2,1)} copy(bf16[384,4,1024]{2,0,1:T(8,128)(2,1)} %collective-permute-done) | data formatting | bytes 6291456 | tf_op jit(solution)/shard_map/ppermute | solution.py:10
  66.5 59.8 %all-gather.3.cloned.1.call-done = bf16[16384,256]{1,0:T(8,128)(2,1)} async-done(((bf16[1024,256]{1,0:T(8,128)(2,1)}), bf16[16384,256]{1,0:T(8,128)(2,1)}) %all-gather.3.cloned.1.call-update) | async-done | bytes 8388624 | tf_op jit(solution)/shard_map/all_gather | solution.py:24
  126.4 12.2 %copy.21 = bf16[4,4,1024,256]{3,0,2,1:T(4,128)(2,1)} copy(bf16[4,4,1024,256]{3,2,1,0:T(8,128)(2,1)} %bitcast.34) | data formatting | bytes 16777216 | tf_op jit(solution)/shard_map/reshape | solution.py:25
  138.6 9.4 %copy.27 = bf16[512,8,4,256]{3,1,2,0:T(8,128)(2,1)} copy(bf16[512,8,4,256]{3,2,1,0:T(4,128)(2,1)} %bitcast.31) | data formatting | bytes 16777216
  148.0 9.6 %convolution_convert_fusion.1 = bf16[768,4096]{1,0:T(8,128)(2,1)S(1)} fusion(bf16[768,1024]{1,0:T(8,128)(2,1)} %constant_dynamic-update-slice_fusion, bf16[4096,1024]{1,0:T(8,128)(2,1)} %bitcast.35), kind=kOutput, calls=%fused_computation.1 | convolution fusion | flops 6445596672 | bytes 16252928 | tf_op jit(solution)/shard_map/dot_general | solution.py:37
  157.6 3.0 fusion.10
  160.6 6.2 %slice.23 = bf16[384,4,1024]{2,1,0:T(4,128)(2,1)} reshape(bf16[384,4096]{1,0:T(8,128)(2,1)} %get-tuple-element.6) | data formatting | bytes 6291456 | tf_op jit(solution)/shard_map/slice | solution.py:40
  166.8 0.0 collective-permute-start.3
  166.8 10.1 %fusion = f32[768,1024]{1,0:T(8,128)S(1)} fusion(bf16[4096,1024]{1,0:T(8,128)(2,1)} %bitcast.36, bf16[384,4096]{0,1:T(8,128)(2,1)} %bitcast.38, bf16[384,4096]{0,1:T(8,128)(2,1)S(1)} %bitcast.33), kind=kOutput, calls=%fused_computation.2 | convolution fusion | flops 6455033856 | bytes 17825792 | tf_op jit(solution)/shard_map/dot_general | solution.py:35
  176.9 0.0 copy-start.2
  176.9 1.7 copy-done.2
  178.6 0.0 copy-start
  178.6 1.3 slice.25
  179.9 0.6 collective-permute-start.1
  180.5 0.6 copy-done
  181.0 4.0 %slice.21 = bf16[384,4,1024]{2,1,0:T(4,128)(2,1)} reshape(bf16[384,4096]{1,0:T(8,128)(2,1)S(1)} %copy-done) | data formatting | bytes 6291456 | tf_op jit(solution)/shard_map/slice | solution.py:40
  185.0 0.0 copy-start.1
  185.0 0.0 collective-permute-done.1
  185.0 3.1 fusion.6
  188.1 0.0 collective-permute-done.3
  188.1 0.0 copy-done.1
  188.1 6.3 %select_bitcast_fusion.1 = (bf16[384,4,1,1024]{3,1,0,2:T(4,128)(2,1)}, bf16[384,4,1,1024]{3,1,0,2:T(4,128)(2,1)}) fusion(bf16[384,4,1024]{2,1,0:T(4,128)(2,1)S(1)} %copy-done.1, bf16[384,4,1024]{2,1,0:T(4,128)(2,1)} %collective-permute-done.3, pred[]{:T(512)S(6)} %eq.4), kind=kLoop, calls=%fused_computation.11 | loop fusion | flops 3145728 | bytes 12582913 | tf_op jit(solution)/shard_map/stack | solution.py:43
  194.5 7.6 %pad_maximum_fusion = bf16[384,4,2,1024]{3,1,0,2:T(4,128)(2,1)S(1)} fusion(bf16[384,4,1,1024]{3,1,0,2:T(4,128)(2,1)} %get-tuple-element.4, bf16[384,4,1,1024]{3,1,0,2:T(4,128)(2,1)} %get-tuple-element.3), kind=kLoop, calls=%fused_computation.6 | loop fusion | flops 3145728 | bytes 12582912 | tf_op jit(solution)/shard_map/stack | solution.py:43
  202.1 7.4 %copy.22 = bf16[384,4,2,1024]{3,2,1,0:T(2,128)(2,1)} copy(bf16[384,4,2,1024]{3,1,0,2:T(4,128)(2,1)S(1)} %pad_maximum_fusion) | data formatting | bytes 12582912 | tf_op jit(solution)/shard_map/stack | solution.py:43
  209.5 11.1 %reshape.38 = bf16[384,8192]{1,0:T(8,128)(2,1)} reshape(bf16[384,4,2,1024]{3,2,1,0:T(2,128)(2,1)} %copy.22) | data formatting | bytes 12582912 | tf_op jit(solution)/shard_map/reshape | solution.py:43
  220.7 88.5 %reduce-scatter.2.cloned.1.call-done = bf16[1,1024,256]{2,1,0:T(8,128)(2,1)} async-done(((bf16[16,1024,256]{2,1,0:T(8,128)(2,1)}), bf16[1,1024,256]{2,1,0:T(8,128)(2,1)}) %reduce-scatter.2.cloned.1.call-update) | async-done | bytes 524304 | tf_op jit(solution)/shard_map/reduce_scatter | solution.py:30
  309.2 1.9 fusion.7
Async XLA Ops:
  7.2 119.2 %all-gather.3.cloned.1.call-start = ((), (), s32[]{:S(2)}) async-start(), calls=%async_computation.2 | async-start | bytes 8912896 | tf_op jit(solution)/shard_map/all_gather | solution.py:24
  7.9 301.3 %reduce-scatter.2.cloned.1.call-start = ((), (), s32[]{:S(2)}) async-start(), calls=%async_computation.1 | async-start | bytes 8912896 | tf_op jit(solution)/shard_map/reduce_scatter | solution.py:30
  26.4 11.9 %collective-permute-start = (bf16[384,4,1024]{2,0,1:T(8,128)(2,1)}, bf16[384,4,1024]{2,0,1:T(8,128)(2,1)}, u32[]{:S(2)}, u32[]{:S(2)}) collective-permute-start(bf16[384,4,1024]{2,0,1:T(8,128)(2,1)} %bitcast.39), channel_id=1, source_target_pairs={{0,1},{1,0},{2,3},{3,2},{4,5},{5,4},{6,7},{7,6},{8,9},{9,8},{10,11... | collective-permute-start | bytes 9437192 | tf_op jit(solution)/shard_map/ppermute | solution.py:10
  26.9 6.8 %collective-permute-start.2 = (bf16[384,1024]{1,0:T(8,128)(2,1)}, bf16[384,1024]{1,0:T(8,128)(2,1)}, u32[]{:S(2)}, u32[]{:S(2)}) collective-permute-start(bf16[384,1024]{1,0:T(8,128)(2,1)} %param.4), channel_id=1, source_target_pairs={{0,1},{1,0},{2,3},{3,2},{4,5},{5,4},{6,7},{7,6},{8,9},{9,8},{10,11... | collective-permute-start | bytes 2359304 | tf_op jit(solution)/shard_map/ppermute | solution.py:10
  166.8 21.3 %collective-permute-start.3 = (bf16[384,4,1024]{2,1,0:T(4,128)(2,1)}, bf16[384,4,1024]{2,1,0:T(4,128)(2,1)}, u32[]{:S(2)}, u32[]{:S(2)}) collective-permute-start(bf16[384,4,1024]{2,1,0:T(4,128)(2,1)} %slice.23), channel_id=1, source_target_pairs={{0,1},{1,0},{2,3},{3,2},{4,5},{5,4},{6,7},{7,6},{8,9},{9,8},{10,11... | collective-permute-start | bytes 9437192 | tf_op jit(solution)/shard_map/ppermute | solution.py:10
  176.9 1.7 copy-start.2
  178.6 2.5 copy-start
  179.9 5.1 %collective-permute-start.1 = (f32[384,1024]{1,0:T(8,128)}, f32[384,1024]{1,0:T(8,128)}, u32[]{:S(2)}, u32[]{:S(2)}) collective-permute-start(f32[384,1024]{1,0:T(8,128)} %slice.25), channel_id=1, source_target_pairs={{0,1},{1,0},{2,3},{3,2},{4,5},{5,4},{6,7},{7,6},{8,9},{9,8},{10,11... | collective-permute-start | bytes 4718600 | tf_op jit(solution)/shard_map/ppermute | solution.py:10
  185.0 3.1 copy-start.1
Sparse Core Ops, SparseCore 0:
  10.8 115.5 all-gather.2
  128.7 180.4 reduce-scatter.1

commit v2 on v1

v2 whole, which is shorter than its diff:
```python
import math

import jax
import jax.numpy as jnp
from jax import lax
from jax.experimental import pallas as pl
from jax.experimental.pallas import tpu as pltpu
from jax.sharding import Mesh, PartitionSpec as P

F32, BF16 = jnp.float32, jnp.bfloat16
AXES = ("blk", "chip", "core")
HALVES = 2


def hops(move):
    pairs = []
    for blk in range(4):
        for z in range(4):
            for core in range(2):
                to = move(blk, z, core)
                if to is not None:
                    pairs.append(((blk * 4 + z) * 2 + core, (to[0] * 4 + to[1]) * 2 + to[2]))
    return pairs


def middle(z):
    return z in (1, 2)


SWAP = hops(lambda b, z, c: (b, z, 1 - c))
FLIP_A = hops(lambda b, z, c: (b ^ (1 + c), z, c))
FLIP_B = hops(lambda b, z, c: (b ^ (2 - c), z, c))
FLIP_B_MID = hops(lambda b, z, c: (b ^ (2 - c), z, c) if middle(z) else None)
FLIP_B_END = hops(lambda b, z, c: (b ^ (2 - c), z, c) if not middle(z) else None)
PAIR = hops(lambda b, z, c: (b, z ^ 1, c))
MID = hops(lambda b, z, c: (b, z ^ 3, c) if middle(z) else None)
OUT = hops(lambda b, z, c: (b, z ^ 1, c) if middle(z) else None)
IN = hops(lambda b, z, c: (b, z ^ 1, c) if not middle(z) else None)


def sent(array, pairs):
    return lax.ppermute(array, AXES, pairs)


def column_block(place, a, b):
    core = place[1]
    return place[2] ^ (a * (1 + core)) ^ (b * (2 - core))


def pack_kernel(place, acts, *outs):
    rows = acts.shape[1] // HALVES
    for half in range(HALVES):
        outs[half][...] = acts[:, half * rows : (half + 1) * rows]


def packed(place, activations, rows):
    tokens = activations.shape[0]
    return pl.pallas_call(
        pack_kernel,
        grid_spec=pltpu.PrefetchScalarGridSpec(
            num_scalar_prefetch=1,
            grid=(4,),
            in_specs=[pl.BlockSpec((tokens, rows), lambda k, s: (0, 2 * (s[0] ^ k) + 1 - s[1]))],
            out_specs=[pl.BlockSpec((tokens, rows // HALVES), lambda k, s: (0, k))] * HALVES,
        ),
        out_shape=[jax.ShapeDtypeStruct((tokens, 4 * rows // HALVES), BF16)] * HALVES,
        cost_estimate=pl.CostEstimate(flops=0, bytes_accessed=16 * tokens * rows, transcendentals=0),
        name="pack",
    )(place, activations)


def term_kernel(place, mine, other, cot_mine, cot_other, send, keep):
    tall = jnp.concatenate([mine[...], other[...]], 0).T
    cols = cot_mine.shape[1] // 4
    for b, out in ((1, send), (0, keep)):
        for a in (0, 1):
            at = pl.ds(pl.multiple_of(column_block(place, a, b) * cols, cols), cols)
            cot = jnp.concatenate([cot_mine[:, at], cot_other[:, at]], 0)
            out[0, a] = jnp.dot(tall, cot, preferred_element_type=F32).astype(BF16)


def terms(place, half, activations, other, cot_mine, cot_other, rows):
    tokens, columns = cot_mine.shape
    part, cols = rows // HALVES, columns // 4
    whole = pl.BlockSpec((tokens, columns), lambda k, s: (0, 0))
    piece = pl.BlockSpec((1, 2, part, cols), lambda k, s: (k, 0, 0, 0))
    return pl.pallas_call(
        term_kernel,
        grid_spec=pltpu.PrefetchScalarGridSpec(
            num_scalar_prefetch=1,
            grid=(4,),
            in_specs=[
                pl.BlockSpec(
                    (tokens, part), lambda k, s: (0, HALVES * (2 * (s[0] ^ k) + s[1]) + half)
                ),
                pl.BlockSpec((tokens, part), lambda k, s: (0, k)),
                whole,
                whole,
            ],
            out_specs=[piece, piece],
        ),
        out_shape=[jax.ShapeDtypeStruct((4, 2, part, cols), BF16)] * 2,
        cost_estimate=pl.CostEstimate(
            flops=16 * tokens * part * columns,
            bytes_accessed=16 * tokens * part + 8 * part * columns,
            transcendentals=0,
        ),
        name="terms",
    )(place, activations, other, cot_mine, cot_other)


def project_kernel(place, *refs):
    acts, cot_mine, cot_other = refs[:1 + HALVES], refs[1 + HALVES], refs[2 + HALVES]
    pieces, outs = refs[3 + HALVES : -4], refs[-4:]
    near, far, keys_near, keys_far = outs
    cols = cot_mine.shape[1] // 4
    tokens = cot_mine.shape[0]
    tall = jnp.concatenate(
        [acts[0][...], jnp.concatenate([act[...] for act in acts[1:]], 1)], 0
    )
    count = len(pieces) // 2
    total = None
    for b in (0, 1):
        for a in (0, 1):
            weight = pieces[b * count][a]
            for extra in pieces[b * count + 1 : (b + 1) * count]:
                weight = weight + extra[a]
            at = pl.ds(pl.multiple_of(column_block(place, a, b) * cols, cols), cols)
            cot = jnp.concatenate([cot_mine[:, at], cot_other[:, at]], 0)
            term = lax.dot_general(
                cot, weight, (((1,), (1,)), ((), ())), preferred_element_type=F32
            )
            total = term if total is None else total + term
            keys = jnp.dot(tall, weight, preferred_element_type=F32)
            keys_near[:, at] = keys[:tokens]
            keys_far[:, at] = keys[tokens:]
    near[...] = total[:tokens].astype(BF16)
    far[...] = total[tokens:].astype(BF16)


def projected(place, k, activations, others, cot_mine, cot_other, pieces):
    tokens, columns = cot_mine.shape
    rows, cols = pieces[0].shape[1:]
    whole = pl.BlockSpec((tokens, columns), lambda i, s: (0, 0))
    wide = pl.BlockSpec((tokens, rows), lambda i, s: (0, 0))
    return pl.pallas_call(
        project_kernel,
        grid_spec=pltpu.PrefetchScalarGridSpec(
            num_scalar_prefetch=1,
            grid=(1,),
            in_specs=[
                pl.BlockSpec((tokens, rows), lambda i, s: (0, 2 * (s[0] ^ k) + s[1])),
                *[pl.BlockSpec((tokens, rows // HALVES), lambda i, s: (0, k))] * HALVES,
                whole,
                whole,
                *[pl.BlockSpec((2, rows, cols), lambda i, s: (0, 0, 0))] * len(pieces),
            ],
            out_specs=[wide, wide, whole, whole],
        ),
        out_shape=[jax.ShapeDtypeStruct((tokens, rows), BF16)] * 2
        + [jax.ShapeDtypeStruct((tokens, columns), F32)] * 2,
        compiler_params=pltpu.CompilerParams(vmem_limit_bytes=56 * 2**20),
        cost_estimate=pl.CostEstimate(
            flops=8 * tokens * rows * columns,
            bytes_accessed=8 * tokens * rows + 2 * rows * columns + 8 * tokens * columns,
            transcendentals=0,
        ),
        name="project",
    )(place, activations, *others, cot_mine, cot_other, *pieces)


def lay_kernel(place, *refs):
    out = refs[-1]
    at = pl.program_id(0)
    z, core = lax.div(at, 2), lax.rem(at, 2)
    for k in range(4):
        for side in range(2):

            @pl.when(((z ^ place[0]) == k) & ((core ^ place[1]) == side))
            def _():
                out[...] = refs[4 * side + k][...]


def laid(place, near, far):
    tokens, rows = near[0].shape
    whole = pl.BlockSpec((tokens, rows), lambda i, s: (0, 0))
    return pl.pallas_call(
        lay_kernel,
        grid_spec=pltpu.PrefetchScalarGridSpec(
            num_scalar_prefetch=1,
            grid=(8,),
            in_specs=[whole] * 8,
            out_specs=pl.BlockSpec((tokens, rows), lambda i, s: (0, i)),
        ),
        out_shape=jax.ShapeDtypeStruct((tokens, 8 * rows), BF16),
        cost_estimate=pl.CostEstimate(flops=0, bytes_accessed=32 * tokens * rows, transcendentals=0),
        compiler_params=pltpu.CompilerParams(vmem_limit_bytes=40 * 2**20),
        name="lay",
    )(place, *near, *far)


def added(*arrays):
    total = arrays[0].astype(F32)
    for array in arrays[1:]:
        total = total + array.astype(F32)
    return total


def gathered(weight):
    base = jnp.stack([weight, sent(weight, FLIP_A)])
    one = sent(base, PAIR)
    mid = sent(base, MID)
    mid_far = sent(one, MID)
    end = sent(mid, OUT)
    end_far = sent(mid_far, OUT)
    return (
        (base, sent(base, FLIP_B)),
        (one, sent(one, FLIP_B)),
        (mid_far, end, sent(mid_far, FLIP_B_MID), sent(end, FLIP_B_END)),
        (mid, end_far, sent(mid, FLIP_B_MID), sent(end_far, FLIP_B_END)),
    )


def scattered(send, keep):
    got = sent(send, FLIP_B)
    sums = [added(keep[k], got[k]) for k in range(4)]
    far = sent(sums[3].astype(BF16), IN)
    near = sent(sums[2].astype(BF16), IN)
    mid_far = sent(added(sums[2], far).astype(BF16), MID)
    mid = sent(added(sums[3], near).astype(BF16), MID)
    one = sent(added(sums[1], mid_far).astype(BF16), PAIR)
    last = added(sums[0], mid, one)
    return last[0] + sent(last[1].astype(BF16), FLIP_A).astype(F32)


def by_hops(activations, cotangent, kv_weight):
    rows = kv_weight.shape[0]
    tokens = activations.shape[0]
    place = jnp.stack([lax.axis_index(name) for name in ("chip", "core", "blk")]).astype(jnp.int32)
    others = [sent(part, SWAP) for part in packed(place, activations, rows)]
    cot_other = sent(cotangent, SWAP)
    weights = gathered(kv_weight)
    halves = []
    for half in range(HALVES):
        send, keep = terms(place, half, activations, others[half], cotangent, cot_other, rows)
        halves.append(scattered(send, keep))
    grad_weight = (jnp.concatenate(halves, 0) * (1.0 / math.sqrt(32 * tokens))).astype(BF16)
    near, far, keys_near, keys_far = zip(
        *[
            projected(place, k, activations, others, cotangent, cot_other, weights[k])
            for k in range(4)
        ]
    )
    grad_input = laid(place, near, [sent(part, SWAP) for part in far])
    key_values = (added(*keys_near) + sent(added(*keys_far), SWAP)).astype(BF16)
    return (key_values, grad_input, grad_weight)


def swapped(array):
    return lax.ppermute(array, "core", [(0, 1), (1, 0)])


def by_collectives(activations, cotangent, kv_weight):
    blocks, chips = lax.axis_size("blk"), lax.axis_size("chip")
    core = lax.axis_index("core")
    tokens, features = activations.shape
    rows, cols = kv_weight.shape
    columns = cotangent.shape[1]
    by_core = activations.reshape(tokens, chips, 2, rows)
    mine = lax.dynamic_index_in_dim(by_core, core, 2, keepdims=False)
    other = lax.dynamic_index_in_dim(by_core, 1 - core, 2, keepdims=False)
    acts = jnp.concatenate([mine, swapped(other)], 0)
    cots = jnp.concatenate([cotangent, swapped(cotangent)], 0)
    weight = lax.all_gather(kv_weight, ("blk", "chip"), axis=0, tiled=False)
    weight = weight.reshape(blocks, chips, rows, cols)
    parts = jnp.einsum(
        "tzr,tbc->bzrc", acts, cots.reshape(2 * tokens, blocks, cols), preferred_element_type=F32
    ).astype(BF16).reshape(blocks * chips, rows, cols)
    total = lax.psum_scatter(parts, ("blk", "chip"), scatter_dimension=0, tiled=False)
    count = tokens * blocks * chips * 2
    grad_weight = (total.astype(F32) * (1.0 / math.sqrt(count))).astype(BF16)
    full = weight.transpose(1, 2, 0, 3).reshape(chips * rows, columns)
    keys = jnp.dot(acts.reshape(2 * tokens, chips * rows), full, preferred_element_type=F32)
    key_values = (keys[:tokens] + swapped(keys[tokens:])).astype(BF16)
    inputs = lax.dot_general(
        cots, full, (((1,), (1,)), ((), ())), preferred_element_type=F32
    ).astype(BF16).reshape(2 * tokens, chips, rows)
    near, far = inputs[:tokens], swapped(inputs[tokens:])
    low = jnp.where(core == 0, near, far)
    high = jnp.where(core == 0, far, near)
    grad_input = jnp.stack([low, high], 2).reshape(tokens, features)
    return (key_values, grad_input, grad_weight)


def solution(mesh):
    blocks, shards = mesh.shape["blk"], mesh.shape["shard"]
    split = Mesh(mesh.devices.reshape(blocks, shards // 2, 2), AXES)
    by_token = P(AXES, None)
    by_piece = P(("chip", "core"), "blk")
    return jax.shard_map(
        by_hops if (blocks, shards) == (4, 8) else by_collectives,
        mesh=split,
        in_specs=(by_token, by_token, by_piece),
        out_specs=(by_token, by_token, by_piece),
        check_vma=False,
    )
```

time: 319 us -> 209 us (0.66)
  local copies, waits for them, and re-layouts: 102 us -> 3.29 us
  waiting for transfers between devices: 151 us -> 56.6 us
  Pallas kernels: 0 us -> 61.1 us
  starting transfers between devices: 1.14 us -> 59.6 us
  matrix products: 31.1 us -> 0 us
  between operations: 14.1 us -> 1 us
  other arithmetic: 19 us -> 26.1 us
    reduce_scatter x1 -> x0, waiting for transfers between devices: 88.5 us -> none  [local(): lax.psum_scatter(terms, ('blk', 'chip'), scatter_dimension=0, tiled=False)]
    pallas_call x0 -> x8, Pallas kernels: none -> 61.1 us  [the longest x4 36.3 us: projected(): pl.pallas_call(project_kernel, grid_spec=pltpu.PrefetchScalarGridSpec(num...]
    all_gather x1 -> x0, waiting for transfers between devices: 59.8 us -> none  [local(): weight = lax.all_gather(kv_weight, ('blk', 'chip'), axis=0, tiled=False)]
    ppermute x4 -> x34, starting transfers between devices: 1.07 us -> 59.6 us  [sent(): return lax.ppermute(array, AXES, pairs)]
    ppermute x4 -> x34, waiting for transfers between devices: 1.72 us -> 56.6 us  [sent(): return lax.ppermute(array, AXES, pairs)]
    reshape x3 -> x0, local copies, waits for them, and re-layouts: 35.6 us -> none  [the longest x1 12.3 us: local(): terms = jnp.einsum('tzr,tbc->bzrc', acts, cots.reshape(2 * tokens, blocks...]
    dot_general x3 -> x0, matrix products: 31.1 us -> none  [the longest x1 11.3 us: local(): jnp.einsum('tzr,tbc->bzrc', acts, cots.reshape(2 * tokens, blocks, cols),...]
    unnamed x9 -> x44, local copies, waits for them, and re-layouts: 22.3 us -> 3.23 us
  transfers between devices with their start and end apart: 6 -> 34, of which waited for: 3 -> 7; matrix products, arithmetic and copies ran while one was open for 46% -> 12% of each run, Pallas kernels for 0% -> 27%
where the time goes in v2:
time: 209 us; the launch traced here: 208 us
  Pallas kernels  61.1 us (29%)
  starting transfers between devices  59.6 us (29%)
  waiting for transfers between devices  56.6 us (27%)
  other arithmetic  26.1 us (12%)
  local copies, waits for them, and re-layouts  3.29 us (2%)
    ppermute x34, starting transfers between devices, sent(): return lax.ppermute(array, AXES, pairs)  59.6 us
    ppermute x34, waiting for transfers between devices, sent(): return lax.ppermute(array, AXES, pairs)  56.6 us
    pallas_call x4, Pallas kernels, projected(): pl.pallas_call(project_kernel, grid_spec=pltpu.PrefetchScalarGridSpec(num...  36.3 us
    pallas_call x2, Pallas kernels, terms(): pl.pallas_call(term_kernel, grid_spec=pltpu.PrefetchScalarGridSpec(num_sc...  15.2 us
    add x3, other arithmetic, added(): total = total + array.astype(F32)  7.42 us
    convert_element_type x2, other arithmetic, scattered(): mid = sent(added(sums[3], near).astype(BF16), MID)  5.4 us
    pallas_call x1, Pallas kernels, packed(): pl.pallas_call(pack_kernel, grid_spec=pltpu.PrefetchScalarGridSpec(num_sc...  4.94 us
    pallas_call x1, Pallas kernels, laid(): pl.pallas_call(lay_kernel, grid_spec=pltpu.PrefetchScalarGridSpec(num_sca...  4.68 us
  transfers between devices with their start and end apart: 34, of which 7 were waited for; matrix products, arithmetic and copies ran while one was open for 12% of the time, Pallas kernels for 27%

profile of v2, /device:TPU:0, one launch (start us, length us, event | category | flops | bytes accessed | tf_op | source)
XLA Modules:
  0.0 207.8 jit_solution(284486104434412235)
XLA Ops:
  1.3 4.9 %pack.1 = (bf16[384,2048]{1,0:T(8,128)(2,1)}, bf16[384,2048]{1,0:T(8,128)(2,1)}) custom-call(s32[3]{0:T(128)} %pad_add_fusion.place, bf16[384,8192]{1,0:T(8,128)(2,1)} %mine.3), custom_call_target="tpu_custom_call" | custom-call | bytes 6291456 | tf_op jit(solution)/shard_map/pack/pallas_call | solution.py:58
  6.7 2.5 %collective-permute-start.3 = (bf16[1024,256]{1,0:T(8,128)(2,1)}, bf16[1024,256]{1,0:T(8,128)(2,1)S(1)}, u32[]{:S(2)}, u32[]{:S(2)}) collective-permute-start(bf16[1024,256]{1,0:T(8,128)(2,1)} %param.5), channel_id=1, source_target_pairs={{0,8},{1,17},{2,10},{3,19},{4,12},{5,21},{6,14},{7,23},{8,0},{9,25... | collective-permute-start | bytes 1572872 | tf_op jit(solution)/shard_map/ppermute | solution.py:42
  9.7 6.9 %collective-permute-done.3 = bf16[1024,256]{1,0:T(8,128)(2,1)S(1)} collective-permute-done((bf16[1024,256]{1,0:T(8,128)(2,1)}, bf16[1024,256]{1,0:T(8,128)(2,1)S(1)}, u32[]{:S(2)}, u32[]{:S(2)}) %collective-permute-start.3) | collective-permute-done | bytes 524320 | tf_op jit(solution)/shard_map/ppermute | solution.py:42
  16.5 2.2 %pad_maximum_fusion.refs_5_ = bf16[2,1024,256]{2,1,0:T(8,128)(2,1)} fusion(bf16[1,1024,256]{2,1,0:T(8,128)(2,1)S(1)} %bitcast.53, bf16[1,1024,256]{2,1,0:T(8,128)(2,1)} %bitcast.3), kind=kLoop, calls=%fused_computation.2 | loop fusion | flops 524288 | bytes 2097152 | tf_op jit(solution)/shard_map/stack | solution.py:210
  18.7 2.1 %collective-permute-start.5 = (bf16[2,1024,256]{2,1,0:T(8,128)(2,1)}, bf16[2,1024,256]{2,1,0:T(8,128)(2,1)}, u32[]{:S(2)}, u32[]{:S(2)}) collective-permute-start(bf16[2,1024,256]{2,1,0:T(8,128)(2,1)} %pad_maximum_fusion.refs_5_), channel_id=1, source_target_pairs={{0,2},{1,3},{2,0},{3,1},{4,6},{5,7},{6,4},{7,5},{8,10},{9,11},{10,... | collective-permute-start | bytes 3145736 | tf_op jit(solution)/shard_map/ppermute | solution.py:42
  20.9 1.2 copy-done.5
  22.1 7.6 %terms.2 = (bf16[4,2,512,256]{3,2,1,0:T(8,128)(2,1)}, bf16[4,2,512,256]{3,2,1,0:T(8,128)(2,1)}) custom-call(s32[3]{0:T(128)} %pad_add_fusion.place, bf16[384,8192]{1,0:T(8,128)(2,1)} %mine.3, bf16[384,2048]{1,0:T(8,128)(2,1)} %copy-done.5, bf16[384,1024]{1,0:T(8,128)(2,1)} %cot_mine.3, bf16[384,1024]{1,0:T(8,128)(2,1)} %collective-permute-done.2.refs_4_.cot_other), custom_call_target="tpu_custom_call" | custom-call | flops 3221225472 | bytes 7340032 | tf_op jit(solution)/shard_map/terms/pallas_call | solution.py:87
  29.7 1.5 collective-permute-start.20
  31.2 1.6 collective-permute-start.8
  32.8 11.3 %collective-permute-done.5.refs_5_ = bf16[2,1024,256]{2,1,0:T(8,128)(2,1)} collective-permute-done((bf16[2,1024,256]{2,1,0:T(8,128)(2,1)}, bf16[2,1024,256]{2,1,0:T(8,128)(2,1)}, u32[]{:S(2)}, u32[]{:S(2)}) %collective-permute-start.5) | collective-permute-done | bytes 1048608 | tf_op jit(solution)/shard_map/ppermute | solution.py:42
  46.0 7.6 %terms.3 = (bf16[4,2,512,256]{3,2,1,0:T(8,128)(2,1)}, bf16[4,2,512,256]{3,2,1,0:T(8,128)(2,1)}) custom-call(s32[3]{0:T(128)} %pad_add_fusion.place, bf16[384,8192]{1,0:T(8,128)(2,1)} %mine.3, bf16[384,2048]{1,0:T(8,128)(2,1)} %copy-done.6, bf16[384,1024]{1,0:T(8,128)(2,1)} %cot_mine.3, bf16[384,1024]{1,0:T(8,128)(2,1)} %collective-permute-done.2.refs_4_.cot_other), custom_call_target="tpu_custom_call" | custom-call | flops 3221225472 | bytes 7340032 | tf_op jit(solution)/shard_map/terms/pallas_call | solution.py:87
  53.6 1.7 collective-permute-start.27
  55.6 1.3 collective-permute-start.9
  57.0 1.8 collective-permute-start.6
  58.7 1.3 collective-permute-start.12
  60.0 2.6 %bitcast_convert_fusion.2 = (bf16[2,512,256]{2,1,0:T(8,128)(2,1)}, bf16[2,512,256]{2,1,0:T(8,128)(2,1)S(1)}) fusion(bf16[4,2,512,256]{3,2,1,0:T(8,128)(2,1)} %collective-permute-done.20, bf16[4,2,512,256]{3,2,1,0:T(8,128)(2,1)} %get-tuple-element.43), kind=kLoop, calls=%fused_computation.18 | loop fusion | flops 2097152 | bytes 3145728 | tf_op jit(solution)/shard_map/convert_element_type | solution.py:228
  62.6 28.5 %collective-permute-done.4.refs_6_ = bf16[2,1024,256]{2,1,0:T(8,128)(2,1)S(1)} collective-permute-done((bf16[2,1024,256]{2,1,0:T(8,128)(2,1)}, bf16[2,1024,256]{2,1,0:T(8,128)(2,1)S(1)}, u32[]{:S(2)}, u32[]{:S(2)}) %collective-permute-start.4) | collective-permute-done | bytes 1048608 | tf_op jit(solution)/shard_map/ppermute | solution.py:42
  91.1 7.2 %collective-permute-start.21 = (bf16[2,512,256]{2,1,0:T(8,128)(2,1)}, bf16[2,512,256]{2,1,0:T(8,128)(2,1)}, u32[]{:S(2)}, u32[]{:S(2)}) collective-permute-start(bf16[2,512,256]{2,1,0:T(8,128)(2,1)} %get-tuple-element.49), channel_id=1, source_target_pairs={{0,2},{1,3},{6,4},{7,5},{8,10},{9,11},{14,12},{15,13},{16,18},{17,... | collective-permute-start | bytes 1572872 | tf_op jit(solution)/shard_map/ppermute | solution.py:42
  98.3 2.2 %collective-permute-start.23 = (bf16[2,512,256]{2,1,0:T(8,128)(2,1)S(1)}, bf16[2,512,256]{2,1,0:T(8,128)(2,1)}, u32[]{:S(2)}, u32[]{:S(2)}) collective-permute-start(bf16[2,512,256]{2,1,0:T(8,128)(2,1)S(1)} %get-tuple-element.50), channel_id=1, source_target_pairs={{0,2},{1,3},{6,4},{7,5},{8,10},{9,11},{14,12},{15,13},{16,18},{17,... | collective-permute-start | bytes 1572872 | tf_op jit(solution)/shard_map/ppermute | solution.py:42
  100.5 8.7 %project.4 = (bf16[384,1024]{1,0:T(8,128)(2,1)}, bf16[384,1024]{1,0:T(8,128)(2,1)}, f32[384,1024]{1,0:T(8,128)}, f32[384,1024]{1,0:T(8,128)}) custom-call(s32[3]{0:T(128)} %pad_add_fusion.place, bf16[384,8192]{1,0:T(8,128)(2,1)} %mine.3, bf16[384,2048]{1,0:T(8,128)(2,1)} %copy-done.5, bf16[384,2048]{1,0:T(8,128)(2,1)} %copy-done.6, ...), custom_call_target="tpu_custom_call" | custom-call | flops 3221225472 | bytes 8388608 | tf_op jit(solution)/shard_map/project/pallas_call | solution.py:146
  109.2 1.6 collective-permute-start.10
  110.9 3.4 %collective-permute-start.11 = (bf16[2,1024,256]{2,1,0:T(8,128)(2,1)}, bf16[2,1024,256]{2,1,0:T(8,128)(2,1)}, u32[]{:S(2)}, u32[]{:S(2)}) collective-permute-start(bf16[2,1024,256]{2,1,0:T(8,128)(2,1)} %collective-permute-done.9.refs_6_), channel_id=1, source_target_pairs={{0,16},{1,9},{6,22},{7,15},{8,24},{9,1},{14,30},{15,7},{16,0},{17,... | collective-permute-start | bytes 3145736 | tf_op jit(solution)/shard_map/ppermute | solution.py:42
  114.3 1.2 bitcast_convert_fusion
  115.5 2.1 %collective-permute-start.28 = (bf16[2,512,256]{2,1,0:T(8,128)(2,1)}, bf16[2,512,256]{2,1,0:T(8,128)(2,1)}, u32[]{:S(2)}, u32[]{:S(2)}) collective-permute-start(bf16[2,512,256]{2,1,0:T(8,128)(2,1)} %get-tuple-element.53), channel_id=1, source_target_pairs={{0,2},{1,3},{6,4},{7,5},{8,10},{9,11},{14,12},{15,13},{16,18},{17,... | collective-permute-start | bytes 1572872 | tf_op jit(solution)/shard_map/ppermute | solution.py:42
  117.7 3.6 %collective-permute-done.23 = bf16[2,512,256]{2,1,0:T(8,128)(2,1)} collective-permute-done((bf16[2,512,256]{2,1,0:T(8,128)(2,1)S(1)}, bf16[2,512,256]{2,1,0:T(8,128)(2,1)}, u32[]{:S(2)}, u32[]{:S(2)}) %collective-permute-start.23) | collective-permute-done | bytes 524320 | tf_op jit(solution)/shard_map/ppermute | solution.py:42
  121.3 4.6 %collective-permute-start.30 = (bf16[2,512,256]{2,1,0:T(8,128)(2,1)}, bf16[2,512,256]{2,1,0:T(8,128)(2,1)S(1)}, u32[]{:S(2)}, u32[]{:S(2)}) collective-permute-start(bf16[2,512,256]{2,1,0:T(8,128)(2,1)} %get-tuple-element.54), channel_id=1, source_target_pairs={{0,2},{1,3},{6,4},{7,5},{8,10},{9,11},{14,12},{15,13},{16,18},{17,... | collective-permute-start | bytes 1572872 | tf_op jit(solution)/shard_map/ppermute | solution.py:42
  126.0 8.7 %project.5 = (bf16[384,1024]{1,0:T(8,128)(2,1)}, bf16[384,1024]{1,0:T(8,128)(2,1)}, f32[384,1024]{1,0:T(8,128)}, f32[384,1024]{1,0:T(8,128)}) custom-call(s32[3]{0:T(128)} %pad_add_fusion.place, bf16[384,8192]{1,0:T(8,128)(2,1)} %mine.3, bf16[384,2048]{1,0:T(8,128)(2,1)} %copy-done.5, bf16[384,2048]{1,0:T(8,128)(2,1)} %copy-done.6, ...), custom_call_target="tpu_custom_call" | custom-call | flops 3221225472 | bytes 8388608 | tf_op jit(solution)/shard_map/project/pallas_call | solution.py:146
  134.7 2.9 %fusion.7 = (bf16[2,512,256]{2,1,0:T(8,128)(2,1)}, bf16[2,512,256]{2,1,0:T(8,128)(2,1)}) fusion(bf16[2,512,256]{2,1,0:T(8,128)(2,1)} %collective-permute-done.21, bf16[4,2,512,256]{3,2,1,0:T(8,128)(2,1)} %collective-permute-done.20, bf16[4,2,512,256]{3,2,1,0:T(8,128)(2,1)S(1)} %copy-done.7, bf16[2,512,256]{2,1,0:T(8,128)(2,1)} %collective-permute-done.23), kind=kLoop, calls=%fused_computation.22 | loop fusion | flops 3145728 | bytes 4194304 | tf_op jit(solution)/shard_map/convert_element_type | solution.py:230
  137.5 1.6 collective-permute-start.13
  139.2 3.4 %collective-permute-start.14 = (bf16[2,1024,256]{2,1,0:T(8,128)(2,1)}, bf16[2,1024,256]{2,1,0:T(8,128)(2,1)}, u32[]{:S(2)}, u32[]{:S(2)}) collective-permute-start(bf16[2,1024,256]{2,1,0:T(8,128)(2,1)} %collective-permute-done.12.refs_6_), channel_id=1, source_target_pairs={{0,16},{1,9},{6,22},{7,15},{8,24},{9,1},{14,30},{15,7},{16,0},{17,... | collective-permute-start | bytes 3145736 | tf_op jit(solution)/shard_map/ppermute | solution.py:42
  144.1 2.5 %fusion.3 = (bf16[2,512,256]{2,1,0:T(8,128)(2,1)}, bf16[2,512,256]{2,1,0:T(8,128)(2,1)}) fusion(bf16[2,512,256]{2,1,0:T(8,128)(2,1)} %collective-permute-done.28, bf16[4,2,512,256]{3,2,1,0:T(8,128)(2,1)S(1)} %collective-permute-done.27, bf16[4,2,512,256]{3,2,1,0:T(8,128)(2,1)S(1)} %copy-done.8, bf16[2,512,256]{2,1,0:T(8,128)(2,1)} %copy-done.17), kind=kLoop, calls=%fused_computation.12 | loop fusion | flops 3145728 | bytes 4194304 | tf_op jit(solution)/shard_map/convert_element_type | solution.py:230
  146.6 1.5 collective-permute-start.31
  148.1 9.3 %project.6 = (bf16[384,1024]{1,0:T(8,128)(2,1)}, bf16[384,1024]{1,0:T(8,128)(2,1)}, f32[384,1024]{1,0:T(8,128)}, f32[384,1024]{1,0:T(8,128)}) custom-call(s32[3]{0:T(128)} %pad_add_fusion.place, bf16[384,8192]{1,0:T(8,128)(2,1)} %mine.3, bf16[384,2048]{1,0:T(8,128)(2,1)} %copy-done.5, bf16[384,2048]{1,0:T(8,128)(2,1)} %copy-done.6, ...), custom_call_target="tpu_custom_call" | custom-call | flops 3221225472 | bytes 8388608 | tf_op jit(solution)/shard_map/project/pallas_call | solution.py:146
  157.4 1.4 collective-permute-start.22
  158.9 1.4 collective-permute-start.29
  160.3 2.0 fusion.5
  162.4 9.6 %collective-permute-start.25 = (bf16[2,512,256]{2,1,0:T(8,128)(2,1)}, bf16[2,512,256]{2,1,0:T(8,128)(2,1)}, u32[]{:S(2)}, u32[]{:S(2)}) collective-permute-start(bf16[2,512,256]{2,1,0:T(8,128)(2,1)} %fusion.5), channel_id=1, source_target_pairs={{0,2},{1,3},{2,0},{3,1},{4,6},{5,7},{6,4},{7,5},{8,10},{9,11},{10,... | collective-permute-start | bytes 1572872 | tf_op jit(solution)/shard_map/ppermute | solution.py:42
  171.9 2.1 fusion.1
  174.0 9.5 %project.7 = (bf16[384,1024]{1,0:T(8,128)(2,1)}, bf16[384,1024]{1,0:T(8,128)(2,1)}, f32[384,1024]{1,0:T(8,128)}, f32[384,1024]{1,0:T(8,128)}) custom-call(s32[3]{0:T(128)} %pad_add_fusion.place, bf16[384,8192]{1,0:T(8,128)(2,1)} %mine.3, bf16[384,2048]{1,0:T(8,128)(2,1)} %copy-done.5, bf16[384,2048]{1,0:T(8,128)(2,1)} %copy-done.6, ...), custom_call_target="tpu_custom_call" | custom-call | flops 3221225472 | bytes 8388608 | tf_op jit(solution)/shard_map/project/pallas_call | solution.py:146
  183.6 4.4 %add_add_fusion = f32[384,1024]{1,0:T(8,128)} fusion(f32[384,1024]{1,0:T(8,128)} %get-tuple-element.34, f32[384,1024]{1,0:T(8,128)} %get-tuple-element.33, f32[384,1024]{1,0:T(8,128)S(1)} %copy-done.12, f32[384,1024]{1,0:T(8,128)} %get-tuple-element.32), kind=kLoop, calls=%fused_computation.1 | loop fusion | flops 1179648 | bytes 7864320 | tf_op jit(solution)/shard_map/add | solution.py:205
  187.9 1.6 fusion.8
  189.6 1.5 collective-permute-start.26
  191.2 1.4 fusion.4
  194.1 2.0 collective-permute-done.26
  196.1 3.0 %collective-permute-done.33 = bf16[512,256]{1,0:T(8,128)(2,1)S(1)} collective-permute-done((bf16[512,256]{1,0:T(8,128)(2,1)S(1)}, bf16[512,256]{1,0:T(8,128)(2,1)S(1)}, u32[]{:S(2)}, u32[]{:S(2)}) %collective-permute-start.33) | collective-permute-done | bytes 262176 | tf_op jit(solution)/shard_map/ppermute | solution.py:42
  200.2 1.2 collective-permute-done.19.refs_7_
  201.4 4.7 %lay.1 = bf16[384,8192]{1,0:T(8,128)(2,1)} custom-call(s32[3]{0:T(128)S(1)} %copy-done.4, bf16[384,1024]{1,0:T(8,128)(2,1)S(1)} %copy-done, bf16[384,1024]{1,0:T(8,128)(2,1)S(1)} %copy-done.1, bf16[384,1024]{1,0:T(8,128)(2,1)S(1)} %copy-done.2, bf16[384,1024]{1,0:T(8,128)(2,1)S(1)} %copy-done.3, bf16[384,1024]{1,0:T(8,128)(2,1)S(1)} %collective-permute-done.16.refs_4_, ...), custom_call_target="tpu_custom_call" | custom-call | bytes 12582912 | tf_op jit(solution)/shard_map/lay/pallas_call | solution.py:187
  206.1 1.6 add_convert_fusion
  (89 shorter events, 7.9 us)
Async XLA Ops:
  6.2 14.6 %collective-permute-start = (bf16[384,2048]{1,0:T(8,128)(2,1)}, bf16[384,2048]{1,0:T(8,128)(2,1)S(1)}, u32[]{:S(2)}, u32[]{:S(2)}) collective-permute-start(bf16[384,2048]{1,0:T(8,128)(2,1)} %get-tuple-element.25), channel_id=1, source_target_pairs={{0,1},{1,0},{2,3},{3,2},{4,5},{5,4},{6,7},{7,6},{8,9},{9,8},{10,11... | collective-permute-start | bytes 4718600 | tf_op jit(solution)/shard_map/ppermute | solution.py:42
  6.7 9.9 %collective-permute-start.3 = (bf16[1024,256]{1,0:T(8,128)(2,1)}, bf16[1024,256]{1,0:T(8,128)(2,1)S(1)}, u32[]{:S(2)}, u32[]{:S(2)}) collective-permute-start(bf16[1024,256]{1,0:T(8,128)(2,1)} %param.5), channel_id=1, source_target_pairs={{0,8},{1,17},{2,10},{3,19},{4,12},{5,21},{6,14},{7,23},{8,0},{9,25... | collective-permute-start | bytes 1572872 | tf_op jit(solution)/shard_map/ppermute | solution.py:42
  9.2 35.7 %collective-permute-start.1 = (bf16[384,2048]{1,0:T(8,128)(2,1)}, bf16[384,2048]{1,0:T(8,128)(2,1)S(1)}, u32[]{:S(2)}, u32[]{:S(2)}) collective-permute-start(bf16[384,2048]{1,0:T(8,128)(2,1)} %get-tuple-element.26), channel_id=1, source_target_pairs={{0,1},{1,0},{2,3},{3,2},{4,5},{5,4},{6,7},{7,6},{8,9},{9,8},{10,11... | collective-permute-start | bytes 4718600 | tf_op jit(solution)/shard_map/ppermute | solution.py:42
  9.4 11.4 %collective-permute-start.2 = (bf16[384,1024]{1,0:T(8,128)(2,1)}, bf16[384,1024]{1,0:T(8,128)(2,1)}, u32[]{:S(2)}, u32[]{:S(2)}) collective-permute-start(bf16[384,1024]{1,0:T(8,128)(2,1)} %cot_mine.3), channel_id=1, source_target_pairs={{0,1},{1,0},{2,3},{3,2},{4,5},{5,4},{6,7},{7,6},{8,9},{9,8},{10,11... | collective-permute-start | bytes 2359304 | tf_op jit(solution)/shard_map/ppermute | solution.py:42
  18.7 25.4 %collective-permute-start.5 = (bf16[2,1024,256]{2,1,0:T(8,128)(2,1)}, bf16[2,1024,256]{2,1,0:T(8,128)(2,1)}, u32[]{:S(2)}, u32[]{:S(2)}) collective-permute-start(bf16[2,1024,256]{2,1,0:T(8,128)(2,1)} %pad_maximum_fusion.refs_5_), channel_id=1, source_target_pairs={{0,2},{1,3},{2,0},{3,1},{4,6},{5,7},{6,4},{7,5},{8,10},{9,11},{10,... | collective-permute-start | bytes 3145736 | tf_op jit(solution)/shard_map/ppermute | solution.py:42
  29.7 29.0 %collective-permute-start.20 = (bf16[4,2,512,256]{3,2,1,0:T(8,128)(2,1)}, bf16[4,2,512,256]{3,2,1,0:T(8,128)(2,1)}, u32[]{:S(2)}, u32[]{:S(2)}) collective-permute-start(bf16[4,2,512,256]{3,2,1,0:T(8,128)(2,1)} %get-tuple-element.44), channel_id=1, source_target_pairs={{0,16},{1,9},{2,18},{3,11},{4,20},{5,13},{6,22},{7,15},{8,24},{9,1... | collective-permute-start | bytes 6291464 | tf_op jit(solution)/shard_map/ppermute | solution.py:42
  31.2 24.4 %collective-permute-start.8 = (bf16[2,1024,256]{2,1,0:T(8,128)(2,1)}, bf16[2,1024,256]{2,1,0:T(8,128)(2,1)}, u32[]{:S(2)}, u32[]{:S(2)}) collective-permute-start(bf16[2,1024,256]{2,1,0:T(8,128)(2,1)} %pad_maximum_fusion.refs_5_), channel_id=1, source_target_pairs={{2,4},{3,5},{4,2},{5,3},{10,12},{11,13},{12,10},{13,11},{18,20},{1... | collective-permute-start | bytes 3145736 | tf_op jit(solution)/shard_map/ppermute | solution.py:42
  44.1 12.8 %collective-permute-start.7 = (bf16[2,1024,256]{2,1,0:T(8,128)(2,1)}, bf16[2,1024,256]{2,1,0:T(8,128)(2,1)S(1)}, u32[]{:S(2)}, u32[]{:S(2)}) collective-permute-start(bf16[2,1024,256]{2,1,0:T(8,128)(2,1)} %collective-permute-done.5.refs_5_), channel_id=1, source_target_pairs={{2,4},{3,5},{4,2},{5,3},{10,12},{11,13},{12,10},{13,11},{18,20},{1... | collective-permute-start | bytes 3145736 | tf_op jit(solution)/shard_map/ppermute | solution.py:42
  53.6 57.3 %collective-permute-start.27 = (bf16[4,2,512,256]{3,2,1,0:T(8,128)(2,1)}, bf16[4,2,512,256]{3,2,1,0:T(8,128)(2,1)S(1)}, u32[]{:S(2)}, u32[]{:S(2)}) collective-permute-start(bf16[4,2,512,256]{3,2,1,0:T(8,128)(2,1)} %get-tuple-element.46), channel_id=1, source_target_pairs={{0,16},{1,9},{2,18},{3,11},{4,20},{5,13},{6,22},{7,15},{8,24},{9,1... | collective-permute-start | bytes 6291464 | tf_op jit(solution)/shard_map/ppermute | solution.py:42
  55.3 35.8 %collective-permute-start.4 = (bf16[2,1024,256]{2,1,0:T(8,128)(2,1)}, bf16[2,1024,256]{2,1,0:T(8,128)(2,1)S(1)}, u32[]{:S(2)}, u32[]{:S(2)}) collective-permute-start(bf16[2,1024,256]{2,1,0:T(8,128)(2,1)} %pad_maximum_fusion.refs_5_), channel_id=1, source_target_pairs={{0,16},{1,9},{2,18},{3,11},{4,20},{5,13},{6,22},{7,15},{8,24},{9,1... | collective-permute-start | bytes 3145736 | tf_op jit(solution)/shard_map/ppermute | solution.py:42
  55.6 42.7 %collective-permute-start.9 = (bf16[2,1024,256]{2,1,0:T(8,128)(2,1)}, bf16[2,1024,256]{2,1,0:T(8,128)(2,1)}, u32[]{:S(2)}, u32[]{:S(2)}) collective-permute-start(bf16[2,1024,256]{2,1,0:T(8,128)(2,1)} %collective-permute-done.8.refs_5_), channel_id=1, source_target_pairs={{2,0},{3,1},{4,6},{5,7},{10,8},{11,9},{12,14},{13,15},{18,16},{19,... | collective-permute-start | bytes 3145736 | tf_op jit(solution)/shard_map/ppermute | solution.py:42
  56.9 52.3 %copy-start.14 = (bf16[2,1024,256]{2,1,0:T(8,128)(2,1)}, bf16[2,1024,256]{2,1,0:T(8,128)(2,1)S(1)}, u32[]{:S(2)}) copy-start(bf16[2,1024,256]{2,1,0:T(8,128)(2,1)S(1)} %collective-permute-done.7.refs_5_) | copy-start | bytes 3145732
  57.0 52.3 %collective-permute-start.6 = (bf16[2,1024,256]{2,1,0:T(8,128)(2,1)}, bf16[2,1024,256]{2,1,0:T(8,128)(2,1)S(1)}, u32[]{:S(2)}, u32[]{:S(2)}) collective-permute-start(bf16[2,1024,256]{2,1,0:T(8,128)(2,1)} %collective-permute-done.5.refs_5_), channel_id=1, source_target_pairs={{0,16},{1,9},{2,18},{3,11},{4,20},{5,13},{6,22},{7,15},{8,24},{9,1... | collective-permute-start | bytes 3145736 | tf_op jit(solution)/shard_map/ppermute | solution.py:42
  58.7 78.8 %collective-permute-start.12 = (bf16[2,1024,256]{2,1,0:T(8,128)(2,1)S(1)}, bf16[2,1024,256]{2,1,0:T(8,128)(2,1)}, u32[]{:S(2)}, u32[]{:S(2)}) collective-permute-start(bf16[2,1024,256]{2,1,0:T(8,128)(2,1)S(1)} %collective-permute-done.7.refs_5_), channel_id=1, source_target_pairs={{2,0},{3,1},{4,6},{5,7},{10,8},{11,9},{12,14},{13,15},{18,16},{19,... | collective-permute-start | bytes 3145736 | tf_op jit(solution)/shard_map/ppermute | solution.py:42
  91.1 9.4 %copy-start.16 = (bf16[2,1024,256]{2,1,0:T(8,128)(2,1)}, bf16[2,1024,256]{2,1,0:T(8,128)(2,1)S(1)}, u32[]{:S(2)}) copy-start(bf16[2,1024,256]{2,1,0:T(8,128)(2,1)S(1)} %collective-permute-done.4.refs_6_) | copy-start | bytes 3145732
  91.1 24.4 %collective-permute-start.21 = (bf16[2,512,256]{2,1,0:T(8,128)(2,1)}, bf16[2,512,256]{2,1,0:T(8,128)(2,1)}, u32[]{:S(2)}, u32[]{:S(2)}) collective-permute-start(bf16[2,512,256]{2,1,0:T(8,128)(2,1)} %get-tuple-element.49), channel_id=1, source_target_pairs={{0,2},{1,3},{6,4},{7,5},{8,10},{9,11},{14,12},{15,13},{16,18},{17,... | collective-permute-start | bytes 1572872 | tf_op jit(solution)/shard_map/ppermute | solution.py:42
  98.3 16.0 %copy-start.8 = (bf16[4,2,512,256]{3,2,1,0:T(8,128)(2,1)S(1)}, bf16[4,2,512,256]{3,2,1,0:T(8,128)(2,1)}, u32[]{:S(2)}) copy-start(bf16[4,2,512,256]{3,2,1,0:T(8,128)(2,1)} %get-tuple-element.45) | copy-start | bytes 6291460
  98.3 23.0 %collective-permute-start.23 = (bf16[2,512,256]{2,1,0:T(8,128)(2,1)S(1)}, bf16[2,512,256]{2,1,0:T(8,128)(2,1)}, u32[]{:S(2)}, u32[]{:S(2)}) collective-permute-start(bf16[2,512,256]{2,1,0:T(8,128)(2,1)S(1)} %get-tuple-element.50), channel_id=1, source_target_pairs={{0,2},{1,3},{6,4},{7,5},{8,10},{9,11},{14,12},{15,13},{16,18},{17,... | collective-permute-start | bytes 1572872 | tf_op jit(solution)/shard_map/ppermute | solution.py:42
  109.2 6.3 %copy-start.15 = (bf16[2,1024,256]{2,1,0:T(8,128)(2,1)}, bf16[2,1024,256]{2,1,0:T(8,128)(2,1)S(1)}, u32[]{:S(2)}) copy-start(bf16[2,1024,256]{2,1,0:T(8,128)(2,1)S(1)} %collective-permute-done.6.refs_6_) | copy-start | bytes 3145732
  109.2 38.9 %collective-permute-start.10 = (bf16[2,1024,256]{2,1,0:T(8,128)(2,1)S(1)}, bf16[2,1024,256]{2,1,0:T(8,128)(2,1)}, u32[]{:S(2)}, u32[]{:S(2)}) collective-permute-start(bf16[2,1024,256]{2,1,0:T(8,128)(2,1)S(1)} %collective-permute-done.7.refs_5_), channel_id=1, source_target_pairs={{2,18},{3,11},{4,20},{5,13},{10,26},{11,3},{12,28},{13,5},{18,2},{... | collective-permute-start | bytes 3145736 | tf_op jit(solution)/shard_map/ppermute | solution.py:42
  110.9 35.8 %collective-permute-start.11 = (bf16[2,1024,256]{2,1,0:T(8,128)(2,1)}, bf16[2,1024,256]{2,1,0:T(8,128)(2,1)}, u32[]{:S(2)}, u32[]{:S(2)}) collective-permute-start(bf16[2,1024,256]{2,1,0:T(8,128)(2,1)} %collective-permute-done.9.refs_6_), channel_id=1, source_target_pairs={{0,16},{1,9},{6,22},{7,15},{8,24},{9,1},{14,30},{15,7},{16,0},{17,... | collective-permute-start | bytes 3145736 | tf_op jit(solution)/shard_map/ppermute | solution.py:42
  115.5 23.6 %collective-permute-start.28 = (bf16[2,512,256]{2,1,0:T(8,128)(2,1)}, bf16[2,512,256]{2,1,0:T(8,128)(2,1)}, u32[]{:S(2)}, u32[]{:S(2)}) collective-permute-start(bf16[2,512,256]{2,1,0:T(8,128)(2,1)} %get-tuple-element.53), channel_id=1, source_target_pairs={{0,2},{1,3},{6,4},{7,5},{8,10},{9,11},{14,12},{15,13},{16,18},{17,... | collective-permute-start | bytes 1572872 | tf_op jit(solution)/shard_map/ppermute | solution.py:42
  121.3 13.4 %copy-start.7 = (bf16[4,2,512,256]{3,2,1,0:T(8,128)(2,1)S(1)}, bf16[4,2,512,256]{3,2,1,0:T(8,128)(2,1)}, u32[]{:S(2)}) copy-start(bf16[4,2,512,256]{3,2,1,0:T(8,128)(2,1)} %get-tuple-element.43) | copy-start | bytes 6291460
  121.3 21.3 %collective-permute-start.30 = (bf16[2,512,256]{2,1,0:T(8,128)(2,1)}, bf16[2,512,256]{2,1,0:T(8,128)(2,1)S(1)}, u32[]{:S(2)}, u32[]{:S(2)}) collective-permute-start(bf16[2,512,256]{2,1,0:T(8,128)(2,1)} %get-tuple-element.54), channel_id=1, source_target_pairs={{0,2},{1,3},{6,4},{7,5},{8,10},{9,11},{14,12},{15,13},{16,18},{17,... | collective-permute-start | bytes 1572872 | tf_op jit(solution)/shard_map/ppermute | solution.py:42
  137.5 36.5 %collective-permute-start.13 = (bf16[2,1024,256]{2,1,0:T(8,128)(2,1)}, bf16[2,1024,256]{2,1,0:T(8,128)(2,1)}, u32[]{:S(2)}, u32[]{:S(2)}) collective-permute-start(bf16[2,1024,256]{2,1,0:T(8,128)(2,1)} %collective-permute-done.8.refs_5_), channel_id=1, source_target_pairs={{2,18},{3,11},{4,20},{5,13},{10,26},{11,3},{12,28},{13,5},{18,2},{... | collective-permute-start | bytes 3145736 | tf_op jit(solution)/shard_map/ppermute | solution.py:42
  139.2 34.8 %collective-permute-start.14 = (bf16[2,1024,256]{2,1,0:T(8,128)(2,1)}, bf16[2,1024,256]{2,1,0:T(8,128)(2,1)}, u32[]{:S(2)}, u32[]{:S(2)}) collective-permute-start(bf16[2,1024,256]{2,1,0:T(8,128)(2,1)} %collective-permute-done.12.refs_6_), channel_id=1, source_target_pairs={{0,16},{1,9},{6,22},{7,15},{8,24},{9,1},{14,30},{15,7},{16,0},{17,... | collective-permute-start | bytes 3145736 | tf_op jit(solution)/shard_map/ppermute | solution.py:42
  143.4 15.5 %collective-permute-start.24 = (bf16[2,512,256]{2,1,0:T(8,128)(2,1)}, bf16[2,512,256]{2,1,0:T(8,128)(2,1)S(1)}, u32[]{:S(2)}, u32[]{:S(2)}) collective-permute-start(bf16[2,512,256]{2,1,0:T(8,128)(2,1)} %get-tuple-element.48), channel_id=1, source_target_pairs={{2,4},{3,5},{4,2},{5,3},{10,12},{11,13},{12,10},{13,11},{18,20},{1... | collective-permute-start | bytes 1572872 | tf_op jit(solution)/shard_map/ppermute | solution.py:42
  146.6 15.7 %collective-permute-start.31 = (bf16[2,512,256]{2,1,0:T(8,128)(2,1)}, bf16[2,512,256]{2,1,0:T(8,128)(2,1)}, u32[]{:S(2)}, u32[]{:S(2)}) collective-permute-start(bf16[2,512,256]{2,1,0:T(8,128)(2,1)} %get-tuple-element.52), channel_id=1, source_target_pairs={{2,4},{3,5},{4,2},{5,3},{10,12},{11,13},{12,10},{13,11},{18,20},{1... | collective-permute-start | bytes 1572872 | tf_op jit(solution)/shard_map/ppermute | solution.py:42
  157.4 30.5 %collective-permute-start.22 = (bf16[2,512,256]{2,1,0:T(8,128)(2,1)}, bf16[2,512,256]{2,1,0:T(8,128)(2,1)}, u32[]{:S(2)}, u32[]{:S(2)}) collective-permute-start(bf16[2,512,256]{2,1,0:T(8,128)(2,1)} %get-tuple-element.47), channel_id=1, source_target_pairs={{2,4},{3,5},{4,2},{5,3},{10,12},{11,13},{12,10},{13,11},{18,20},{1... | collective-permute-start | bytes 1572872 | tf_op jit(solution)/shard_map/ppermute | solution.py:42
  158.9 32.3 %collective-permute-start.29 = (bf16[2,512,256]{2,1,0:T(8,128)(2,1)}, bf16[2,512,256]{2,1,0:T(8,128)(2,1)}, u32[]{:S(2)}, u32[]{:S(2)}) collective-permute-start(bf16[2,512,256]{2,1,0:T(8,128)(2,1)} %get-tuple-element.51), channel_id=1, source_target_pairs={{2,4},{3,5},{4,2},{5,3},{10,12},{11,13},{12,10},{13,11},{18,20},{1... | collective-permute-start | bytes 1572872 | tf_op jit(solution)/shard_map/ppermute | solution.py:42
  162.4 25.6 %collective-permute-start.25 = (bf16[2,512,256]{2,1,0:T(8,128)(2,1)}, bf16[2,512,256]{2,1,0:T(8,128)(2,1)}, u32[]{:S(2)}, u32[]{:S(2)}) collective-permute-start(bf16[2,512,256]{2,1,0:T(8,128)(2,1)} %fusion.5), channel_id=1, source_target_pairs={{0,2},{1,3},{2,0},{3,1},{4,6},{5,7},{6,4},{7,5},{8,10},{9,11},{10,... | collective-permute-start | bytes 1572872 | tf_op jit(solution)/shard_map/ppermute | solution.py:42
  174.0 9.6 %copy-start.12 = (f32[384,1024]{1,0:T(8,128)S(1)}, f32[384,1024]{1,0:T(8,128)}, u32[]{:S(2)}) copy-start(f32[384,1024]{1,0:T(8,128)} %get-tuple-element.31) | copy-start | bytes 4718596
  174.0 17.2 %collective-permute-start.32 = (bf16[2,512,256]{2,1,0:T(8,128)(2,1)}, bf16[2,512,256]{2,1,0:T(8,128)(2,1)}, u32[]{:S(2)}, u32[]{:S(2)}) collective-permute-start(bf16[2,512,256]{2,1,0:T(8,128)(2,1)} %fusion.1), channel_id=1, source_target_pairs={{0,2},{1,3},{2,0},{3,1},{4,6},{5,7},{6,4},{7,5},{8,10},{9,11},{10,... | collective-permute-start | bytes 1572872 | tf_op jit(solution)/shard_map/ppermute | solution.py:42
  187.9 18.2 %collective-permute-start.15 = (f32[384,1024]{1,0:T(8,128)}, f32[384,1024]{1,0:T(8,128)S(1)}, u32[]{:S(2)}, u32[]{:S(2)}) collective-permute-start(f32[384,1024]{1,0:T(8,128)} %add_add_fusion), channel_id=1, source_target_pairs={{0,1},{1,0},{2,3},{3,2},{4,5},{5,4},{6,7},{7,6},{8,9},{9,8},{10,11... | collective-permute-start | bytes 4718600 | tf_op jit(solution)/shard_map/ppermute | solution.py:42
  189.6 4.0 %copy-start.18 = (bf16[384,1024]{1,0:T(8,128)(2,1)S(1)}, bf16[384,1024]{1,0:T(8,128)(2,1)}, u32[]{:S(2)}) copy-start(bf16[384,1024]{1,0:T(8,128)(2,1)} %get-tuple-element.39) | copy-start | bytes 2359300
  189.6 3.9 %copy-start.19 = (bf16[384,1024]{1,0:T(8,128)(2,1)S(1)}, bf16[384,1024]{1,0:T(8,128)(2,1)}, u32[]{:S(2)}) copy-start(bf16[384,1024]{1,0:T(8,128)(2,1)} %get-tuple-element.40) | copy-start | bytes 2359300
  189.6 6.5 %copy-start.20 = (bf16[384,1024]{1,0:T(8,128)(2,1)S(1)}, bf16[384,1024]{1,0:T(8,128)(2,1)}, u32[]{:S(2)}) copy-start(bf16[384,1024]{1,0:T(8,128)(2,1)} %get-tuple-element.41) | copy-start | bytes 2359300
  189.6 9.5 %copy-start.21 = (bf16[384,1024]{1,0:T(8,128)(2,1)S(1)}, bf16[384,1024]{1,0:T(8,128)(2,1)}, u32[]{:S(2)}) copy-start(bf16[384,1024]{1,0:T(8,128)(2,1)} %get-tuple-element.42) | copy-start | bytes 2359300
  189.6 6.4 %collective-permute-start.26 = (bf16[512,256]{1,0:T(8,128)(2,1)S(1)}, bf16[512,256]{1,0:T(8,128)(2,1)S(1)}, u32[]{:S(2)}, u32[]{:S(2)}) collective-permute-start(bf16[512,256]{1,0:T(8,128)(2,1)S(1)} %fusion.11), channel_id=1, source_target_pairs={{0,8},{1,17},{2,10},{3,19},{4,12},{5,21},{6,14},{7,23},{8,0},{9,25... | collective-permute-start | bytes 786440 | tf_op jit(solution)/shard_map/ppermute | solution.py:42
  192.6 6.4 %collective-permute-start.33 = (bf16[512,256]{1,0:T(8,128)(2,1)S(1)}, bf16[512,256]{1,0:T(8,128)(2,1)S(1)}, u32[]{:S(2)}, u32[]{:S(2)}) collective-permute-start(bf16[512,256]{1,0:T(8,128)(2,1)S(1)} %fusion.12), channel_id=1, source_target_pairs={{0,8},{1,17},{2,10},{3,19},{4,12},{5,21},{6,14},{7,23},{8,0},{9,25... | collective-permute-start | bytes 786440 | tf_op jit(solution)/shard_map/ppermute | solution.py:42
  193.5 6.6 %collective-permute-start.16 = (bf16[384,1024]{1,0:T(8,128)(2,1)S(1)}, bf16[384,1024]{1,0:T(8,128)(2,1)S(1)}, u32[]{:S(2)}, u32[]{:S(2)}) collective-permute-start(bf16[384,1024]{1,0:T(8,128)(2,1)S(1)} %copy-done.18), channel_id=1, source_target_pairs={{0,1},{1,0},{2,3},{3,2},{4,5},{5,4},{6,7},{7,6},{8,9},{9,8},{10,11... | collective-permute-start | bytes 2359304 | tf_op jit(solution)/shard_map/ppermute | solution.py:42
  193.5 6.6 %collective-permute-start.17 = (bf16[384,1024]{1,0:T(8,128)(2,1)S(1)}, bf16[384,1024]{1,0:T(8,128)(2,1)S(1)}, u32[]{:S(2)}, u32[]{:S(2)}) collective-permute-start(bf16[384,1024]{1,0:T(8,128)(2,1)S(1)} %copy-done.19), channel_id=1, source_target_pairs={{0,1},{1,0},{2,3},{3,2},{4,5},{5,4},{6,7},{7,6},{8,9},{9,8},{10,11... | collective-permute-start | bytes 2359304 | tf_op jit(solution)/shard_map/ppermute | solution.py:42
  196.1 4.1 %collective-permute-start.18 = (bf16[384,1024]{1,0:T(8,128)(2,1)S(1)}, bf16[384,1024]{1,0:T(8,128)(2,1)S(1)}, u32[]{:S(2)}, u32[]{:S(2)}) collective-permute-start(bf16[384,1024]{1,0:T(8,128)(2,1)S(1)} %copy-done.20), channel_id=1, source_target_pairs={{0,1},{1,0},{2,3},{3,2},{4,5},{5,4},{6,7},{7,6},{8,9},{9,8},{10,11... | collective-permute-start | bytes 2359304 | tf_op jit(solution)/shard_map/ppermute | solution.py:42
  199.1 2.3 %collective-permute-start.19 = (bf16[384,1024]{1,0:T(8,128)(2,1)S(1)}, bf16[384,1024]{1,0:T(8,128)(2,1)S(1)}, u32[]{:S(2)}, u32[]{:S(2)}) collective-permute-start(bf16[384,1024]{1,0:T(8,128)(2,1)S(1)} %copy-done.21), channel_id=1, source_target_pairs={{0,1},{1,0},{2,3},{3,2},{4,5},{5,4},{6,7},{7,6},{8,9},{9,8},{10,11... | collective-permute-start | bytes 2359304 | tf_op jit(solution)/shard_map/ppermute | solution.py:42
  201.4 4.7 %copy-start.9 = (f32[384,1024]{1,0:T(8,128)S(1)}, f32[384,1024]{1,0:T(8,128)}, u32[]{:S(2)}) copy-start(f32[384,1024]{1,0:T(8,128)} %get-tuple-element.27) | copy-start | bytes 4718596
  201.4 4.7 %copy-start.10 = (f32[384,1024]{1,0:T(8,128)S(1)}, f32[384,1024]{1,0:T(8,128)}, u32[]{:S(2)}) copy-start(f32[384,1024]{1,0:T(8,128)} %get-tuple-element.28) | copy-start | bytes 4718596
  201.4 4.7 %copy-start.11 = (f32[384,1024]{1,0:T(8,128)S(1)}, f32[384,1024]{1,0:T(8,128)}, u32[]{:S(2)}) copy-start(f32[384,1024]{1,0:T(8,128)} %get-tuple-element.29) | copy-start | bytes 4718596
  201.4 4.7 %copy-start.13 = (f32[384,1024]{1,0:T(8,128)S(1)}, f32[384,1024]{1,0:T(8,128)}, u32[]{:S(2)}) copy-start(f32[384,1024]{1,0:T(8,128)} %get-tuple-element.30) | copy-start | bytes 4718596
  (8 other events, 14.3 us)

commit v3 on v2

--- a/solution.py
+++ b/solution.py
@@ -10,6 +10,7 @@
 F32, BF16 = jnp.float32, jnp.bfloat16
 AXES = ("blk", "chip", "core")
 HALVES = 2
+SHRINK = 1000
 
 
 def hops(move):
@@ -47,6 +48,10 @@
     return place[2] ^ (a * (1 + core)) ^ (b * (2 - core))
 
 
+def cost(flops, moved):
+    return pl.CostEstimate(flops=flops // SHRINK, bytes_accessed=moved // SHRINK, transcendentals=0)
+
+
 def pack_kernel(place, acts, *outs):
     rows = acts.shape[1] // HALVES
     for half in range(HALVES):
@@ -64,26 +69,36 @@
             out_specs=[pl.BlockSpec((tokens, rows // HALVES), lambda k, s: (0, k))] * HALVES,
         ),
         out_shape=[jax.ShapeDtypeStruct((tokens, 4 * rows // HALVES), BF16)] * HALVES,
-        cost_estimate=pl.CostEstimate(flops=0, bytes_accessed=16 * tokens * rows, transcendentals=0),
+        cost_estimate=cost(0, 16 * tokens * rows),
         name="pack",
     )(place, activations)
 
 
-def term_kernel(place, mine, other, cot_mine, cot_other, send, keep):
-    tall = jnp.concatenate([mine[...], other[...]], 0).T
-    cols = cot_mine.shape[1] // 4
+def term_kernel(place, mine, other, cot_mine, cot_other, send, keep, turned):
+    tokens, cols = cot_mine.shape[0], cot_mine.shape[1] // 4
+
+    @pl.when(pl.program_id(0) == 0)
+    def _():
+        for b in (0, 1):
+            for a in (0, 1):
+                at = pl.ds(pl.multiple_of(column_block(place, a, b) * cols, cols), cols)
+                to = slice((2 * b + a) * cols, (2 * b + a + 1) * cols)
+                turned[to, :tokens] = cot_mine[:, at].T
+                turned[to, tokens:] = cot_other[:, at].T
+
+    tall = jnp.concatenate([mine[...], other[...]], 0)
     for b, out in ((1, send), (0, keep)):
-        for a in (0, 1):
-            at = pl.ds(pl.multiple_of(column_block(place, a, b) * cols, cols), cols)
-            cot = jnp.concatenate([cot_mine[:, at], cot_other[:, at]], 0)
-            out[0, a] = jnp.dot(tall, cot, preferred_element_type=F32).astype(BF16)
+        part = jnp.dot(
+            turned[2 * b * cols : (2 * b + 2) * cols], tall, preferred_element_type=F32
+        ).astype(BF16)
+        out[...] = part.reshape(out.shape)
 
 
 def terms(place, half, activations, other, cot_mine, cot_other, rows):
     tokens, columns = cot_mine.shape
     part, cols = rows // HALVES, columns // 4
     whole = pl.BlockSpec((tokens, columns), lambda k, s: (0, 0))
-    piece = pl.BlockSpec((1, 2, part, cols), lambda k, s: (k, 0, 0, 0))
+    piece = pl.BlockSpec((1, 2, cols, part), lambda k, s: (k, 0, 0, 0))
     return pl.pallas_call(
         term_kernel,
         grid_spec=pltpu.PrefetchScalarGridSpec(
@@ -98,103 +113,154 @@
                 whole,
             ],
             out_specs=[piece, piece],
-        ),
-        out_shape=[jax.ShapeDtypeStruct((4, 2, part, cols), BF16)] * 2,
-        cost_estimate=pl.CostEstimate(
-            flops=16 * tokens * part * columns,
-            bytes_accessed=16 * tokens * part + 8 * part * columns,
-            transcendentals=0,
-        ),
+            scratch_shapes=[pltpu.VMEM((columns, 2 * tokens), BF16)],
+        ),
+        out_shape=[jax.ShapeDtypeStruct((4, 2, cols, part), BF16)] * 2,
+        compiler_params=pltpu.CompilerParams(vmem_limit_bytes=24 * 2**20),
+        cost_estimate=cost(16 * tokens * part * columns, 16 * tokens * part + 8 * part * columns),
         name="terms",
     )(place, activations, other, cot_mine, cot_other)
 
 
-def project_kernel(place, *refs):
-    acts, cot_mine, cot_other = refs[:1 + HALVES], refs[1 + HALVES], refs[2 + HALVES]
-    pieces, outs = refs[3 + HALVES : -4], refs[-4:]
-    near, far, keys_near, keys_far = outs
-    cols = cot_mine.shape[1] // 4
-    tokens = cot_mine.shape[0]
-    tall = jnp.concatenate(
-        [acts[0][...], jnp.concatenate([act[...] for act in acts[1:]], 1)], 0
-    )
-    count = len(pieces) // 2
-    total = None
-    for b in (0, 1):
-        for a in (0, 1):
-            weight = pieces[b * count][a]
-            for extra in pieces[b * count + 1 : (b + 1) * count]:
-                weight = weight + extra[a]
-            at = pl.ds(pl.multiple_of(column_block(place, a, b) * cols, cols), cols)
-            cot = jnp.concatenate([cot_mine[:, at], cot_other[:, at]], 0)
-            term = lax.dot_general(
-                cot, weight, (((1,), (1,)), ((), ())), preferred_element_type=F32
-            )
-            total = term if total is None else total + term
-            keys = jnp.dot(tall, weight, preferred_element_type=F32)
-            keys_near[:, at] = keys[:tokens]
-            keys_far[:, at] = keys[tokens:]
-    near[...] = total[:tokens].astype(BF16)
-    far[...] = total[tokens:].astype(BF16)
-
-
-def projected(place, k, activations, others, cot_mine, cot_other, pieces):
+def project_kernel(place, *refs, counts, last):
+    near, far, *keys = refs[-6 if last else -5 : -2]
+    if last:
+        near, far, *keys = refs[-6:-2]
+    acc, cots = refs[-2:]
+    acts, others, cot_mine, cot_other = refs[0], refs[1 : 1 + HALVES], *refs[1 + HALVES : 3 + HALVES]
+    pieces = refs[3 + HALVES : 3 + HALVES + sum(counts)]
+    tokens, cols = cot_mine.shape[0], cot_mine.shape[1] // 4
+    group, tile = pl.program_id(0), pl.program_id(1)
+    blocks = [
+        (slice((2 * b + a) * cols, (2 * b + a + 1) * cols),
+         pl.ds(pl.multiple_of(column_block(place, a, b) * cols, cols), cols))
+        for b in (0, 1) for a in (0, 1)
+    ]
+
+    @pl.when((group == 0) & (tile == 0))
+    def _():
+        for to, at in blocks:
+            cots[:tokens, to] = cot_mine[:, at]
+            cots[tokens:, to] = cot_other[:, at]
+        if last:
+            acc[...] = refs[3 + HALVES + sum(counts)][...]
+        else:
+            acc[...] = jnp.zeros_like(acc)
+
+    for at_group in range(len(counts)):
+        start = sum(counts[:at_group])
+        mine = pieces[start : start + counts[at_group]]
+        for half in range(HALVES):
+
+            @pl.when((group == at_group) & (tile == half))
+            def _():
+                parts = []
+                for b in (0, 1):
+                    some = mine[b * len(mine) // 2 : (b + 1) * len(mine) // 2]
+                    for a in (0, 1):
+                        part = some[0][a]
+                        for extra in some[1:]:
+                            part = part + extra[a]
+                        parts.append(part)
+                weight = jnp.concatenate(parts, 1)
+                tall = jnp.concatenate([acts[...], others[half][...]], 0)
+                acc[...] += jnp.dot(tall, weight, preferred_element_type=F32)
+                total = lax.dot_general(
+                    cots[...], weight, (((1,), (1,)), ((), ())), preferred_element_type=F32
+                ).astype(BF16)
+                near[...] = total[:tokens]
+                far[...] = total[tokens:]
+
+    @pl.when((group == len(counts) - 1) & (tile == HALVES - 1))
+    def _():
+        if last:
+            for to, at in blocks:
+                keys[0][:, at] = acc[:tokens, to]
+                keys[1][:, at] = acc[tokens:, to]
+        else:
+            keys[0][...] = acc[...]
+
+
+def projected(place, offsets, activations, others, cot_mine, cot_other, pieces, prior=None):
     tokens, columns = cot_mine.shape
-    rows, cols = pieces[0].shape[1:]
-    whole = pl.BlockSpec((tokens, columns), lambda i, s: (0, 0))
-    wide = pl.BlockSpec((tokens, rows), lambda i, s: (0, 0))
+    rows, cols = pieces[0][0].shape[1:]
+    part = rows // HALVES
+    last = prior is not None
+    whole = pl.BlockSpec((tokens, columns), lambda i, r, s: (0, 0))
+    both = pl.BlockSpec((2 * tokens, columns), lambda i, r, s: (0, 0))
+    first, step = offsets[0], offsets[1] - offsets[0]
+
+    def held(at_group):
+        return pl.BlockSpec(
+            (2, part, cols),
+            lambda i, r, s: (0, jnp.clip((i - at_group) * HALVES + r, 0, HALVES - 1), 0),
+        )
+
+    out = pl.BlockSpec((tokens, part), lambda i, r, s: (0, HALVES * i + r))
+    wide = jax.ShapeDtypeStruct((tokens, len(offsets) * rows), BF16)
+    one = jax.ShapeDtypeStruct((tokens, columns), F32)
     return pl.pallas_call(
-        project_kernel,
+        lambda *refs: project_kernel(*refs, counts=[len(p) for p in pieces], last=last),
         grid_spec=pltpu.PrefetchScalarGridSpec(
             num_scalar_prefetch=1,
-            grid=(1,),
+            grid=(len(offsets), HALVES),
             in_specs=[
-                pl.BlockSpec((tokens, rows), lambda i, s: (0, 2 * (s[0] ^ k) + s[1])),
-                *[pl.BlockSpec((tokens, rows // HALVES), lambda i, s: (0, k))] * HALVES,
+                pl.BlockSpec(
+                    (tokens, part),
+                    lambda i, r, s: (0, HALVES * (2 * (s[0] ^ (first + step * i)) + s[1]) + r),
+                ),
+                *[pl.BlockSpec((tokens, part), lambda i, r, s: (0, first + step * i))] * HALVES,
                 whole,
                 whole,
-                *[pl.BlockSpec((2, rows, cols), lambda i, s: (0, 0, 0))] * len(pieces),
+                *[held(i) for i in range(len(pieces)) for _ in pieces[i]],
+                *([both] if last else []),
             ],
-            out_specs=[wide, wide, whole, whole],
-        ),
-        out_shape=[jax.ShapeDtypeStruct((tokens, rows), BF16)] * 2
-        + [jax.ShapeDtypeStruct((tokens, columns), F32)] * 2,
-        compiler_params=pltpu.CompilerParams(vmem_limit_bytes=56 * 2**20),
-        cost_estimate=pl.CostEstimate(
-            flops=8 * tokens * rows * columns,
-            bytes_accessed=8 * tokens * rows + 2 * rows * columns + 8 * tokens * columns,
-            transcendentals=0,
+            out_specs=[out, out] + ([whole, whole] if last else [both]),
+            scratch_shapes=[
+                pltpu.VMEM((2 * tokens, columns), F32),
+                pltpu.VMEM((2 * tokens, columns), BF16),
+            ],
+        ),
+        out_shape=[wide, wide]
+        + ([one, one] if last else [jax.ShapeDtypeStruct((2 * tokens, columns), F32)]),
+        compiler_params=pltpu.CompilerParams(vmem_limit_bytes=48 * 2**20),
+        cost_estimate=cost(
+            8 * tokens * rows * columns * len(offsets),
+            (8 * tokens * rows + 2 * rows * columns) * len(offsets) + 8 * tokens * columns,
         ),
         name="project",
-    )(place, activations, *others, cot_mine, cot_other, *pieces)
+    )(
+        place, activations, *others, cot_mine, cot_other,
+        *[piece for some in pieces for piece in some], *([prior] if last else []),
+    )
 
 
 def lay_kernel(place, *refs):
     out = refs[-1]
     at = pl.program_id(0)
     z, core = lax.div(at, 2), lax.rem(at, 2)
-    for k in range(4):
-        for side in range(2):
-
-            @pl.when(((z ^ place[0]) == k) & ((core ^ place[1]) == side))
+    for side in range(2):
+        for group in range(2):
+
+            @pl.when((((z ^ place[0]) >> 1) == group) & ((core ^ place[1]) == side))
             def _():
-                out[...] = refs[4 * side + k][...]
+                out[...] = refs[2 * side + group][...]
 
 
 def laid(place, near, far):
-    tokens, rows = near[0].shape
-    whole = pl.BlockSpec((tokens, rows), lambda i, s: (0, 0))
+    tokens, rows = near[0].shape[0], near[0].shape[1] // 2
+    piece = pl.BlockSpec((tokens, rows), lambda i, s: (0, (lax.div(i, 2) ^ s[0]) & 1))
     return pl.pallas_call(
         lay_kernel,
         grid_spec=pltpu.PrefetchScalarGridSpec(
             num_scalar_prefetch=1,
             grid=(8,),
-            in_specs=[whole] * 8,
+            in_specs=[piece] * 4,
             out_specs=pl.BlockSpec((tokens, rows), lambda i, s: (0, i)),
         ),
         out_shape=jax.ShapeDtypeStruct((tokens, 8 * rows), BF16),
-        cost_estimate=pl.CostEstimate(flops=0, bytes_accessed=32 * tokens * rows, transcendentals=0),
-        compiler_params=pltpu.CompilerParams(vmem_limit_bytes=40 * 2**20),
+        cost_estimate=cost(0, 32 * tokens * rows),
+        compiler_params=pltpu.CompilerParams(vmem_limit_bytes=24 * 2**20),
         name="lay",
     )(place, *near, *far)
 
@@ -244,15 +310,12 @@
     for half in range(HALVES):
         send, keep = terms(place, half, activations, others[half], cotangent, cot_other, rows)
         halves.append(scattered(send, keep))
-    grad_weight = (jnp.concatenate(halves, 0) * (1.0 / math.sqrt(32 * tokens))).astype(BF16)
-    near, far, keys_near, keys_far = zip(
-        *[
-            projected(place, k, activations, others, cotangent, cot_other, weights[k])
-            for k in range(4)
-        ]
-    )
-    grad_input = laid(place, near, [sent(part, SWAP) for part in far])
-    key_values = (added(*keys_near) + sent(added(*keys_far), SWAP)).astype(BF16)
+    grad_weight = (jnp.concatenate(halves, 1) * (1.0 / math.sqrt(32 * tokens))).astype(BF16).T
+    shared = (activations, others, cotangent, cot_other)
+    near, far, keys = projected(place, (0, 1), *shared, weights[:2])
+    more, more_far, keys, keys_far = projected(place, (2, 3), *shared, weights[2:], keys)
+    grad_input = laid(place, (near, more), (sent(far, SWAP), sent(more_far, SWAP)))
+    key_values = (keys + sent(keys_far, SWAP)).astype(BF16)
     return (key_values, grad_input, grad_weight)
 
 

time: 209 us -> 220 us (1.053)
  starting transfers between devices: 59.6 us -> 78.4 us
  waiting for transfers between devices: 56.6 us -> 74.3 us
  other arithmetic: 26.1 us -> 12.3 us
  Pallas kernels: 61.1 us -> 48.7 us
    ppermute x34 -> x32, starting transfers between devices: 59.6 us -> 78.4 us  [sent(): return lax.ppermute(array, AXES, pairs)]
    ppermute x34 -> x32, waiting for transfers between devices: 56.6 us -> 74.3 us  [sent(): return lax.ppermute(array, AXES, pairs)]
    pallas_call x4 -> x2, Pallas kernels: 36.3 us -> 24.7 us  [projected(): pl.pallas_call(lambda *refs: project_kernel(*refs, counts=[len(p) for p i...]
    add x3 -> x2, other arithmetic: 7.42 us -> 2.74 us  [added(): total = total + array.astype(F32)]
    pallas_call x2, Pallas kernels: 15.2 us -> 10.6 us  [terms(): pl.pallas_call(term_kernel, grid_spec=pltpu.PrefetchScalarGridSpec(num_sc...]
    pallas_call x1, Pallas kernels: 4.68 us -> 8.42 us  [laid(): pl.pallas_call(lay_kernel, grid_spec=pltpu.PrefetchScalarGridSpec(num_sca...]
    convert_element_type x2, other arithmetic: 3.76 us -> 0.64 us  [scattered(): near = sent(sums[2].astype(BF16), IN)]
    convert_element_type x2, other arithmetic: 5.4 us -> 2.49 us  [scattered(): mid = sent(added(sums[3], near).astype(BF16), MID)]
  transfers between devices with their start and end apart: 34 -> 32, of which waited for: 7 -> 9; matrix products, arithmetic and copies ran while one was open for 12% -> 6% of each run, Pallas kernels for 27% -> 16%
where the time goes in v3:
time: 220 us; the launch traced here: 219 us
  starting transfers between devices  78.4 us (36%)
  waiting for transfers between devices  74.3 us (34%)
  Pallas kernels  48.7 us (22%)
  other arithmetic  12.3 us (6%)
  local copies, waits for them, and re-layouts  3.9 us (2%)
    ppermute x32, starting transfers between devices, sent(): return lax.ppermute(array, AXES, pairs)  78.4 us
    ppermute x32, waiting for transfers between devices, sent(): return lax.ppermute(array, AXES, pairs)  74.3 us
    pallas_call x2, Pallas kernels, projected(): pl.pallas_call(lambda *refs: project_kernel(*refs, counts=[len(p) for p i...  24.7 us
    pallas_call x2, Pallas kernels, terms(): pl.pallas_call(term_kernel, grid_spec=pltpu.PrefetchScalarGridSpec(num_sc...  10.6 us
    pallas_call x1, Pallas kernels, laid(): pl.pallas_call(lay_kernel, grid_spec=pltpu.PrefetchScalarGridSpec(num_sca...  8.42 us
    pallas_call x1, Pallas kernels, packed(): pl.pallas_call(pack_kernel, grid_spec=pltpu.PrefetchScalarGridSpec(num_sc...  5.07 us
  transfers between devices with their start and end apart: 32, of which 9 were waited for; matrix products, arithmetic and copies ran while one was open for 6% of the time, Pallas kernels for 16%

profile of v3, /device:TPU:0, one launch (start us, length us, event | category | flops | bytes accessed | tf_op | source)
XLA Modules:
  0.0 218.7 jit_solution(5666754236077197904)
XLA Ops:
  1.2 5.1 %pack.1 = (bf16[384,2048]{1,0:T(8,128)(2,1)}, bf16[384,2048]{1,0:T(8,128)(2,1)}) custom-call(s32[3]{0:T(128)} %pad_add_fusion.place.refs_0_, bf16[384,8192]{1,0:T(8,128)(2,1)} %mine.3), custom_call_target="tpu_custom_call" | custom-call | bytes 6291 | tf_op jit(solution)/shard_map/pack/pallas_call | solution.py:63
  7.3 2.6 %collective-permute-start.3 = (bf16[1024,256]{1,0:T(8,128)(2,1)S(1)}, bf16[1024,256]{1,0:T(8,128)(2,1)S(1)}, u32[]{:S(2)}, u32[]{:S(2)}) collective-permute-start(bf16[1024,256]{1,0:T(8,128)(2,1)S(1)} %copy-done.12), channel_id=1, source_target_pairs={{0,8},{1,17},{2,10},{3,19},{4,12},{5,21},{6,14},{7,23},{8,0},{9,25... | collective-permute-start | bytes 1572872 | tf_op jit(solution)/shard_map/ppermute | solution.py:43
  9.8 7.2 %collective-permute-done.3 = bf16[1024,256]{1,0:T(8,128)(2,1)S(1)} collective-permute-done((bf16[1024,256]{1,0:T(8,128)(2,1)S(1)}, bf16[1024,256]{1,0:T(8,128)(2,1)S(1)}, u32[]{:S(2)}, u32[]{:S(2)}) %collective-permute-start.3) | collective-permute-done | bytes 524320 | tf_op jit(solution)/shard_map/ppermute | solution.py:43
  17.1 2.2 collective-permute-start.4
  19.3 2.8 %copy-done = bf16[384,8192]{1,0:T(8,128)(2,1)S(1)} copy-done((bf16[384,8192]{1,0:T(8,128)(2,1)S(1)}, bf16[384,8192]{1,0:T(8,128)(2,1)}, u32[]{:S(2)}) %copy-start) | copy-done | bytes 6291480
  22.1 5.3 %terms.2 = (bf16[4,2,256,512]{3,2,1,0:T(8,128)(2,1)S(1)}, bf16[4,2,256,512]{3,2,1,0:T(8,128)(2,1)S(1)}) custom-call(s32[3]{0:T(128)S(1)} %copy-done.6, bf16[384,8192]{1,0:T(8,128)(2,1)S(1)} %copy-done, bf16[384,2048]{1,0:T(8,128)(2,1)S(1)} %collective-permute-done.refs_2_.other, bf16[384,1024]{1,0:T(8,128)(2,1)S(1)} %copy-done.3, ...), custom_call_target="tpu_custom_call" | custom-call | flops 3221225 | bytes 7340 | tf_op jit(solution)/shard_map/terms/pallas_call | solution.py:102
  27.4 1.6 collective-permute-start.18
  29.0 0.7 collective-permute-start.6
  29.7 5.3 %terms.3 = (bf16[4,2,256,512]{3,2,1,0:T(8,128)(2,1)S(1)}, bf16[4,2,256,512]{3,2,1,0:T(8,128)(2,1)S(1)}) custom-call(s32[3]{0:T(128)S(1)} %copy-done.6, bf16[384,8192]{1,0:T(8,128)(2,1)S(1)} %copy-done, bf16[384,2048]{1,0:T(8,128)(2,1)S(1)} %collective-permute-done.1.refs_3_.other, bf16[384,1024]{1,0:T(8,128)(2,1)S(1)} %copy-done.3, ...), custom_call_target="tpu_custom_call" | custom-call | flops 3221225 | bytes 7340 | tf_op jit(solution)/shard_map/terms/pallas_call | solution.py:102
  35.6 6.6 %collective-permute-done.4.refs_8_ = bf16[2,1024,256]{2,1,0:T(8,128)(2,1)S(1)} collective-permute-done((bf16[2,1024,256]{2,1,0:T(8,128)(2,1)S(1)}, bf16[2,1024,256]{2,1,0:T(8,128)(2,1)S(1)}, u32[]{:S(2)}, u32[]{:S(2)}) %collective-permute-start.4) | collective-permute-done | bytes 1048608 | tf_op jit(solution)/shard_map/ppermute | solution.py:43
  42.2 0.7 collective-permute-start.5
  42.9 1.7 collective-permute-start.13
  44.7 0.7 collective-permute-start.11
  45.4 1.3 collective-permute-start.7
  46.7 6.8 %collective-permute-done.18 = bf16[4,2,256,512]{3,2,1,0:T(8,128)(2,1)S(1)} collective-permute-done((bf16[4,2,256,512]{3,2,1,0:T(8,128)(2,1)S(1)}, bf16[4,2,256,512]{3,2,1,0:T(8,128)(2,1)S(1)}, u32[]{:S(2)}, u32[]{:S(2)}) %collective-permute-start.18) | collective-permute-done | bytes 2097184 | tf_op jit(solution)/shard_map/ppermute | solution.py:43
  53.5 1.3 collective-permute-start.10
  55.1 32.1 %collective-permute-done.13.refs_7_ = bf16[2,1024,256]{2,1,0:T(8,128)(2,1)S(1)} collective-permute-done((bf16[2,1024,256]{2,1,0:T(8,128)(2,1)S(1)}, bf16[2,1024,256]{2,1,0:T(8,128)(2,1)S(1)}, u32[]{:S(2)}, u32[]{:S(2)}) %collective-permute-start.13) | collective-permute-done | bytes 1048608 | tf_op jit(solution)/shard_map/ppermute | solution.py:43
  87.2 2.0 collective-permute-start.19
  89.2 11.2 %collective-permute-start.21 = (bf16[2,256,512]{2,1,0:T(8,128)(2,1)S(1)}, bf16[2,256,512]{2,1,0:T(8,128)(2,1)S(1)}, u32[]{:S(2)}, u32[]{:S(2)}) collective-permute-start(bf16[2,256,512]{2,1,0:T(8,128)(2,1)S(1)} %get-tuple-element.35), channel_id=1, source_target_pairs={{0,2},{1,3},{6,4},{7,5},{8,10},{9,11},{14,12},{15,13},{16,18},{17,... | collective-permute-start | bytes 1572872 | tf_op jit(solution)/shard_map/ppermute | solution.py:43
  100.4 2.0 collective-permute-start.14
  102.7 1.3 collective-permute-start.26
  104.1 8.6 %collective-permute-done.21 = bf16[2,256,512]{2,1,0:T(8,128)(2,1)S(1)} collective-permute-done((bf16[2,256,512]{2,1,0:T(8,128)(2,1)S(1)}, bf16[2,256,512]{2,1,0:T(8,128)(2,1)S(1)}, u32[]{:S(2)}, u32[]{:S(2)}) %collective-permute-start.21) | collective-permute-done | bytes 524320 | tf_op jit(solution)/shard_map/ppermute | solution.py:43
  112.7 4.4 %collective-permute-start.28 = (bf16[2,256,512]{2,1,0:T(8,128)(2,1)S(1)}, bf16[2,256,512]{2,1,0:T(8,128)(2,1)S(1)}, u32[]{:S(2)}, u32[]{:S(2)}) collective-permute-start(bf16[2,256,512]{2,1,0:T(8,128)(2,1)S(1)} %get-tuple-element.39), channel_id=1, source_target_pairs={{0,2},{1,3},{6,4},{7,5},{8,10},{9,11},{14,12},{15,13},{16,18},{17,... | collective-permute-start | bytes 1572872 | tf_op jit(solution)/shard_map/ppermute | solution.py:43
  117.1 1.2 fusion.7
  118.4 0.7 collective-permute-start.8
  119.1 5.2 %collective-permute-done.10.refs_11_ = bf16[2,1024,256]{2,1,0:T(8,128)(2,1)} collective-permute-done((bf16[2,1024,256]{2,1,0:T(8,128)(2,1)S(1)}, bf16[2,1024,256]{2,1,0:T(8,128)(2,1)}, u32[]{:S(2)}, u32[]{:S(2)}) %collective-permute-start.10) | collective-permute-done | bytes 1048608 | tf_op jit(solution)/shard_map/ppermute | solution.py:43
  124.3 4.5 %collective-permute-start.9 = (bf16[2,1024,256]{2,1,0:T(8,128)(2,1)S(1)}, bf16[2,1024,256]{2,1,0:T(8,128)(2,1)S(1)}, u32[]{:S(2)}, u32[]{:S(2)}) collective-permute-start(bf16[2,1024,256]{2,1,0:T(8,128)(2,1)S(1)} %collective-permute-done.7.refs_7_), channel_id=1, source_target_pairs={{0,16},{1,9},{6,22},{7,15},{8,24},{9,1},{14,30},{15,7},{16,0},{17,... | collective-permute-start | bytes 3145736 | tf_op jit(solution)/shard_map/ppermute | solution.py:43
  128.9 1.9 collective-permute-start.12
  130.8 2.1 collective-permute-done.28
  132.9 0.7 collective-permute-start.22
  133.6 1.2 fusion.3
  134.8 0.7 collective-permute-start.29
  135.5 0.9 collective-permute-start.20
  136.4 1.0 fusion.5
  137.4 26.7 %collective-permute-start.23 = (bf16[2,256,512]{2,1,0:T(8,128)(2,1)}, bf16[2,256,512]{2,1,0:T(8,128)(2,1)}, u32[]{:S(2)}, u32[]{:S(2)}) collective-permute-start(bf16[2,256,512]{2,1,0:T(8,128)(2,1)} %fusion.5), channel_id=1, source_target_pairs={{0,2},{1,3},{2,0},{3,1},{4,6},{5,7},{6,4},{7,5},{8,10},{9,11},{10,... | collective-permute-start | bytes 1572872 | tf_op jit(solution)/shard_map/ppermute | solution.py:43
  164.2 11.4 %project.2 = (bf16[384,2048]{1,0:T(8,128)(2,1)}, bf16[384,2048]{1,0:T(8,128)(2,1)}, f32[768,1024]{1,0:T(8,128)}) custom-call(s32[3]{0:T(128)S(1)} %copy-done.6, bf16[384,8192]{1,0:T(8,128)(2,1)} %mine.3, bf16[384,2048]{1,0:T(8,128)(2,1)} %copy-done.1, bf16[384,2048]{1,0:T(8,128)(2,1)} %copy-done.2, bf16[384,1024]{1,0:T(8,128)(2,1)S(1)} %copy-done.3, ...), custom_call_target="tpu_custom_call" | custom-call | flops 6442450 | bytes 13631 | tf_op jit(solution)/shard_map/project/pallas_call | solution.py:202
  175.5 1.3 fusion.1
  177.0 0.9 collective-permute-start.27
  177.9 3.3 %collective-permute-start.30 = (bf16[2,256,512]{2,1,0:T(8,128)(2,1)S(1)}, bf16[2,256,512]{2,1,0:T(8,128)(2,1)S(1)}, u32[]{:S(2)}, u32[]{:S(2)}) collective-permute-start(bf16[2,256,512]{2,1,0:T(8,128)(2,1)S(1)} %fusion.1), channel_id=1, source_target_pairs={{0,2},{1,3},{2,0},{3,1},{4,6},{5,7},{6,4},{7,5},{8,10},{9,11},{10,... | collective-permute-start | bytes 1572872 | tf_op jit(solution)/shard_map/ppermute | solution.py:43
  181.2 13.3 %project.3 = (bf16[384,2048]{1,0:T(8,128)(2,1)}, bf16[384,2048]{1,0:T(8,128)(2,1)}, f32[384,1024]{1,0:T(8,128)}, f32[384,1024]{1,0:T(8,128)}) custom-call(s32[3]{0:T(128)S(1)} %copy-done.6, bf16[384,8192]{1,0:T(8,128)(2,1)} %mine.3, bf16[384,2048]{1,0:T(8,128)(2,1)} %copy-done.1, bf16[384,2048]{1,0:T(8,128)(2,1)} %copy-done.2, ...), custom_call_target="tpu_custom_call" | custom-call | flops 6442450 | bytes 13631 | tf_op jit(solution)/shard_map/project/pallas_call | solution.py:202
  195.1 1.5 fusion.8
  196.6 1.5 collective-permute-start.24
  198.2 1.3 fusion.4
  200.1 2.9 %collective-permute-done.24 = bf16[256,512]{1,0:T(8,128)(2,1)S(1)} collective-permute-done((bf16[256,512]{1,0:T(8,128)(2,1)S(1)}, bf16[256,512]{1,0:T(8,128)(2,1)S(1)}, u32[]{:S(2)}, u32[]{:S(2)}) %collective-permute-start.24) | collective-permute-done | bytes 262176 | tf_op jit(solution)/shard_map/ppermute | solution.py:43
  203.2 2.8 %collective-permute-done.31 = bf16[256,512]{1,0:T(8,128)(2,1)S(1)} collective-permute-done((bf16[256,512]{1,0:T(8,128)(2,1)S(1)}, bf16[256,512]{1,0:T(8,128)(2,1)S(1)}, u32[]{:S(2)}, u32[]{:S(2)}) %collective-permute-start.31) | collective-permute-done | bytes 262176 | tf_op jit(solution)/shard_map/ppermute | solution.py:43
  206.1 1.0 copy.6
  207.1 3.1 %add_convert_fusion = bf16[384,1024]{1,0:T(8,128)(2,1)} fusion(f32[384,1024]{1,0:T(8,128)} %get-tuple-element.19, f32[384,1024]{1,0:T(8,128)} %collective-permute-done.15), kind=kLoop, calls=%fused_computation | loop fusion | flops 786432 | bytes 3932160 | tf_op jit(solution)/shard_map/convert_element_type | solution.py:318
  210.3 8.4 %lay.1 = bf16[384,8192]{1,0:T(8,128)(2,1)} custom-call(s32[3]{0:T(128)S(1)} %copy-done.6, bf16[384,2048]{1,0:T(8,128)(2,1)S(1)} %copy-done.4, bf16[384,2048]{1,0:T(8,128)(2,1)S(1)} %copy-done.5, bf16[384,2048]{1,0:T(8,128)(2,1)S(1)} %collective-permute-done.16.refs_2_, bf16[384,2048]{1,0:T(8,128)(2,1)} %collective-permute-done.17.refs_3_), custom_call_target="tpu_custom_call" | custom-call | bytes 12582 | tf_op jit(solution)/shard_map/lay/pallas_call | solution.py:253
  (67 shorter events, 4.6 us)
Async XLA Ops:
  1.2 5.6 %copy-start.3 = (bf16[384,1024]{1,0:T(8,128)(2,1)S(1)}, bf16[384,1024]{1,0:T(8,128)(2,1)}, u32[]{:S(2)}) copy-start(bf16[384,1024]{1,0:T(8,128)(2,1)} %cot_mine.3) | copy-start | bytes 2359300
  1.2 6.0 %copy-start.12 = (bf16[1024,256]{1,0:T(8,128)(2,1)S(1)}, bf16[1024,256]{1,0:T(8,128)(2,1)}, u32[]{:S(2)}) copy-start(bf16[1024,256]{1,0:T(8,128)(2,1)} %param.5) | copy-start | bytes 1572868
  6.3 13.0 %copy-start.6 = (s32[3]{0:T(128)S(1)}, s32[3]{0:T(128)}, u32[]{:S(2)}) copy-start(s32[3]{0:T(128)} %pad_add_fusion.place.refs_0_) | copy-start | bytes 40
  6.3 13.0 %collective-permute-start = (bf16[384,2048]{1,0:T(8,128)(2,1)}, bf16[384,2048]{1,0:T(8,128)(2,1)S(1)}, u32[]{:S(2)}, u32[]{:S(2)}) collective-permute-start(bf16[384,2048]{1,0:T(8,128)(2,1)} %get-tuple-element.16), channel_id=1, source_target_pairs={{0,1},{1,0},{2,3},{3,2},{4,5},{5,4},{6,7},{7,6},{8,9},{9,8},{10,11... | collective-permute-start | bytes 4718600 | tf_op jit(solution)/shard_map/ppermute | solution.py:43
  6.8 22.9 %collective-permute-start.1 = (bf16[384,2048]{1,0:T(8,128)(2,1)}, bf16[384,2048]{1,0:T(8,128)(2,1)S(1)}, u32[]{:S(2)}, u32[]{:S(2)}) collective-permute-start(bf16[384,2048]{1,0:T(8,128)(2,1)} %get-tuple-element.17), channel_id=1, source_target_pairs={{0,1},{1,0},{2,3},{3,2},{4,5},{5,4},{6,7},{7,6},{8,9},{9,8},{10,11... | collective-permute-start | bytes 4718600 | tf_op jit(solution)/shard_map/ppermute | solution.py:43
  6.8 12.4 %collective-permute-start.2 = (bf16[384,1024]{1,0:T(8,128)(2,1)S(1)}, bf16[384,1024]{1,0:T(8,128)(2,1)S(1)}, u32[]{:S(2)}, u32[]{:S(2)}) collective-permute-start(bf16[384,1024]{1,0:T(8,128)(2,1)S(1)} %copy-done.3), channel_id=1, source_target_pairs={{0,1},{1,0},{2,3},{3,2},{4,5},{5,4},{6,7},{7,6},{8,9},{9,8},{10,11... | collective-permute-start | bytes 2359304 | tf_op jit(solution)/shard_map/ppermute | solution.py:43
  7.3 9.7 %collective-permute-start.3 = (bf16[1024,256]{1,0:T(8,128)(2,1)S(1)}, bf16[1024,256]{1,0:T(8,128)(2,1)S(1)}, u32[]{:S(2)}, u32[]{:S(2)}) collective-permute-start(bf16[1024,256]{1,0:T(8,128)(2,1)S(1)} %copy-done.12), channel_id=1, source_target_pairs={{0,8},{1,17},{2,10},{3,19},{4,12},{5,21},{6,14},{7,23},{8,0},{9,25... | collective-permute-start | bytes 1572872 | tf_op jit(solution)/shard_map/ppermute | solution.py:43
  17.1 25.1 %collective-permute-start.4 = (bf16[2,1024,256]{2,1,0:T(8,128)(2,1)S(1)}, bf16[2,1024,256]{2,1,0:T(8,128)(2,1)S(1)}, u32[]{:S(2)}, u32[]{:S(2)}) collective-permute-start(bf16[2,1024,256]{2,1,0:T(8,128)(2,1)S(1)} %pad_maximum_fusion.refs_6_), channel_id=1, source_target_pairs={{0,2},{1,3},{2,0},{3,1},{4,6},{5,7},{6,4},{7,5},{8,10},{9,11},{10,... | collective-permute-start | bytes 3145736 | tf_op jit(solution)/shard_map/ppermute | solution.py:43
  19.3 2.8 %copy-start = (bf16[384,8192]{1,0:T(8,128)(2,1)S(1)}, bf16[384,8192]{1,0:T(8,128)(2,1)}, u32[]{:S(2)}) copy-start(bf16[384,8192]{1,0:T(8,128)(2,1)} %mine.3) | copy-start | bytes 18874372
  22.1 5.3 %copy-start.1 = (bf16[384,2048]{1,0:T(8,128)(2,1)}, bf16[384,2048]{1,0:T(8,128)(2,1)S(1)}, u32[]{:S(2)}) copy-start(bf16[384,2048]{1,0:T(8,128)(2,1)S(1)} %collective-permute-done.refs_2_.other) | copy-start | bytes 4718596
  27.4 26.1 %collective-permute-start.18 = (bf16[4,2,256,512]{3,2,1,0:T(8,128)(2,1)S(1)}, bf16[4,2,256,512]{3,2,1,0:T(8,128)(2,1)S(1)}, u32[]{:S(2)}, u32[]{:S(2)}) collective-permute-start(bf16[4,2,256,512]{3,2,1,0:T(8,128)(2,1)S(1)} %get-tuple-element.26), channel_id=1, source_target_pairs={{0,16},{1,9},{2,18},{3,11},{4,20},{5,13},{6,22},{7,15},{8,24},{9,1... | collective-permute-start | bytes 6291464 | tf_op jit(solution)/shard_map/ppermute | solution.py:43
  29.0 15.7 %collective-permute-start.6 = (bf16[2,1024,256]{2,1,0:T(8,128)(2,1)S(1)}, bf16[2,1024,256]{2,1,0:T(8,128)(2,1)S(1)}, u32[]{:S(2)}, u32[]{:S(2)}) collective-permute-start(bf16[2,1024,256]{2,1,0:T(8,128)(2,1)S(1)} %pad_maximum_fusion.refs_6_), channel_id=1, source_target_pairs={{2,4},{3,5},{4,2},{5,3},{10,12},{11,13},{12,10},{13,11},{18,20},{1... | collective-permute-start | bytes 3145736 | tf_op jit(solution)/shard_map/ppermute | solution.py:43
  29.7 5.3 %copy-start.2 = (bf16[384,2048]{1,0:T(8,128)(2,1)}, bf16[384,2048]{1,0:T(8,128)(2,1)S(1)}, u32[]{:S(2)}) copy-start(bf16[384,2048]{1,0:T(8,128)(2,1)S(1)} %collective-permute-done.1.refs_3_.other) | copy-start | bytes 4718596
  35.0 65.4 %collective-permute-start.25 = (bf16[4,2,256,512]{3,2,1,0:T(8,128)(2,1)S(1)}, bf16[4,2,256,512]{3,2,1,0:T(8,128)(2,1)S(1)}, u32[]{:S(2)}, u32[]{:S(2)}) collective-permute-start(bf16[4,2,256,512]{3,2,1,0:T(8,128)(2,1)S(1)} %get-tuple-element.28), channel_id=1, source_target_pairs={{0,16},{1,9},{2,18},{3,11},{4,20},{5,13},{6,22},{7,15},{8,24},{9,1... | collective-permute-start | bytes 6291464 | tf_op jit(solution)/shard_map/ppermute | solution.py:43
  42.2 3.2 %collective-permute-start.5 = (bf16[2,1024,256]{2,1,0:T(8,128)(2,1)S(1)}, bf16[2,1024,256]{2,1,0:T(8,128)(2,1)S(1)}, u32[]{:S(2)}, u32[]{:S(2)}) collective-permute-start(bf16[2,1024,256]{2,1,0:T(8,128)(2,1)S(1)} %collective-permute-done.4.refs_8_), channel_id=1, source_target_pairs={{2,4},{3,5},{4,2},{5,3},{10,12},{11,13},{12,10},{13,11},{18,20},{1... | collective-permute-start | bytes 3145736 | tf_op jit(solution)/shard_map/ppermute | solution.py:43
  42.9 44.3 %collective-permute-start.13 = (bf16[2,1024,256]{2,1,0:T(8,128)(2,1)S(1)}, bf16[2,1024,256]{2,1,0:T(8,128)(2,1)S(1)}, u32[]{:S(2)}, u32[]{:S(2)}) collective-permute-start(bf16[2,1024,256]{2,1,0:T(8,128)(2,1)S(1)} %pad_maximum_fusion.refs_6_), channel_id=1, source_target_pairs={{0,16},{1,9},{2,18},{3,11},{4,20},{5,13},{6,22},{7,15},{8,24},{9,1... | collective-permute-start | bytes 3145736 | tf_op jit(solution)/shard_map/ppermute | solution.py:43
  44.7 58.1 %copy-start.9 = (bf16[2,1024,256]{2,1,0:T(8,128)(2,1)}, bf16[2,1024,256]{2,1,0:T(8,128)(2,1)S(1)}, u32[]{:S(2)}) copy-start(bf16[2,1024,256]{2,1,0:T(8,128)(2,1)S(1)} %collective-permute-done.6.refs_10_) | copy-start | bytes 3145732
  44.7 44.5 %collective-permute-start.11 = (bf16[2,1024,256]{2,1,0:T(8,128)(2,1)S(1)}, bf16[2,1024,256]{2,1,0:T(8,128)(2,1)S(1)}, u32[]{:S(2)}, u32[]{:S(2)}) collective-permute-start(bf16[2,1024,256]{2,1,0:T(8,128)(2,1)S(1)} %collective-permute-done.6.refs_10_), channel_id=1, source_target_pairs={{2,18},{3,11},{4,20},{5,13},{10,26},{11,3},{12,28},{13,5},{18,2},{... | collective-permute-start | bytes 3145736 | tf_op jit(solution)/shard_map/ppermute | solution.py:43
  45.4 73.0 %collective-permute-start.7 = (bf16[2,1024,256]{2,1,0:T(8,128)(2,1)S(1)}, bf16[2,1024,256]{2,1,0:T(8,128)(2,1)S(1)}, u32[]{:S(2)}, u32[]{:S(2)}) collective-permute-start(bf16[2,1024,256]{2,1,0:T(8,128)(2,1)S(1)} %collective-permute-done.6.refs_10_), channel_id=1, source_target_pairs={{2,0},{3,1},{4,6},{5,7},{10,8},{11,9},{12,14},{13,15},{18,16},{19,... | collective-permute-start | bytes 3145736 | tf_op jit(solution)/shard_map/ppermute | solution.py:43
  53.5 82.9 %copy-start.8 = (bf16[4,2,256,512]{3,2,1,0:T(8,128)(2,1)}, bf16[4,2,256,512]{3,2,1,0:T(8,128)(2,1)S(1)}, u32[]{:S(2)}) copy-start(bf16[4,2,256,512]{3,2,1,0:T(8,128)(2,1)S(1)} %collective-permute-done.18) | copy-start | bytes 6291460
  53.5 70.8 %collective-permute-start.10 = (bf16[2,1024,256]{2,1,0:T(8,128)(2,1)S(1)}, bf16[2,1024,256]{2,1,0:T(8,128)(2,1)}, u32[]{:S(2)}, u32[]{:S(2)}) collective-permute-start(bf16[2,1024,256]{2,1,0:T(8,128)(2,1)S(1)} %collective-permute-done.5.refs_6_), channel_id=1, source_target_pairs={{2,0},{3,1},{4,6},{5,7},{10,8},{11,9},{12,14},{13,15},{18,16},{19,... | collective-permute-start | bytes 3145736 | tf_op jit(solution)/shard_map/ppermute | solution.py:43
  87.2 15.6 %collective-permute-start.19 = (bf16[2,256,512]{2,1,0:T(8,128)(2,1)S(1)}, bf16[2,256,512]{2,1,0:T(8,128)(2,1)S(1)}, u32[]{:S(2)}, u32[]{:S(2)}) collective-permute-start(bf16[2,256,512]{2,1,0:T(8,128)(2,1)S(1)} %get-tuple-element.34), channel_id=1, source_target_pairs={{0,2},{1,3},{6,4},{7,5},{8,10},{9,11},{14,12},{15,13},{16,18},{17,... | collective-permute-start | bytes 1572872 | tf_op jit(solution)/shard_map/ppermute | solution.py:43
  89.2 29.2 %copy-start.10 = (bf16[2,1024,256]{2,1,0:T(8,128)(2,1)}, bf16[2,1024,256]{2,1,0:T(8,128)(2,1)S(1)}, u32[]{:S(2)}) copy-start(bf16[2,1024,256]{2,1,0:T(8,128)(2,1)S(1)} %collective-permute-done.11.refs_12_) | copy-start | bytes 3145732
  89.2 23.5 %collective-permute-start.21 = (bf16[2,256,512]{2,1,0:T(8,128)(2,1)S(1)}, bf16[2,256,512]{2,1,0:T(8,128)(2,1)S(1)}, u32[]{:S(2)}, u32[]{:S(2)}) collective-permute-start(bf16[2,256,512]{2,1,0:T(8,128)(2,1)S(1)} %get-tuple-element.35), channel_id=1, source_target_pairs={{0,2},{1,3},{6,4},{7,5},{8,10},{9,11},{14,12},{15,13},{16,18},{17,... | collective-permute-start | bytes 1572872 | tf_op jit(solution)/shard_map/ppermute | solution.py:43
  100.4 37.0 %copy-start.7 = (bf16[4,2,256,512]{3,2,1,0:T(8,128)(2,1)}, bf16[4,2,256,512]{3,2,1,0:T(8,128)(2,1)S(1)}, u32[]{:S(2)}) copy-start(bf16[4,2,256,512]{3,2,1,0:T(8,128)(2,1)S(1)} %collective-permute-done.25) | copy-start | bytes 6291460
  100.4 34.4 %collective-permute-start.14 = (bf16[2,1024,256]{2,1,0:T(8,128)(2,1)S(1)}, bf16[2,1024,256]{2,1,0:T(8,128)(2,1)S(1)}, u32[]{:S(2)}, u32[]{:S(2)}) collective-permute-start(bf16[2,1024,256]{2,1,0:T(8,128)(2,1)S(1)} %collective-permute-done.4.refs_8_), channel_id=1, source_target_pairs={{0,16},{1,9},{2,18},{3,11},{4,20},{5,13},{6,22},{7,15},{8,24},{9,1... | collective-permute-start | bytes 3145736 | tf_op jit(solution)/shard_map/ppermute | solution.py:43
  102.7 26.1 %collective-permute-start.26 = (bf16[2,256,512]{2,1,0:T(8,128)(2,1)S(1)}, bf16[2,256,512]{2,1,0:T(8,128)(2,1)S(1)}, u32[]{:S(2)}, u32[]{:S(2)}) collective-permute-start(bf16[2,256,512]{2,1,0:T(8,128)(2,1)S(1)} %get-tuple-element.38), channel_id=1, source_target_pairs={{0,2},{1,3},{6,4},{7,5},{8,10},{9,11},{14,12},{15,13},{16,18},{17,... | collective-permute-start | bytes 1572872 | tf_op jit(solution)/shard_map/ppermute | solution.py:43
  112.7 20.2 %collective-permute-start.28 = (bf16[2,256,512]{2,1,0:T(8,128)(2,1)S(1)}, bf16[2,256,512]{2,1,0:T(8,128)(2,1)S(1)}, u32[]{:S(2)}, u32[]{:S(2)}) collective-permute-start(bf16[2,256,512]{2,1,0:T(8,128)(2,1)S(1)} %get-tuple-element.39), channel_id=1, source_target_pairs={{0,2},{1,3},{6,4},{7,5},{8,10},{9,11},{14,12},{15,13},{16,18},{17,... | collective-permute-start | bytes 1572872 | tf_op jit(solution)/shard_map/ppermute | solution.py:43
  118.4 58.6 %collective-permute-start.8 = (bf16[2,1024,256]{2,1,0:T(8,128)(2,1)S(1)}, bf16[2,1024,256]{2,1,0:T(8,128)(2,1)S(1)}, u32[]{:S(2)}, u32[]{:S(2)}) collective-permute-start(bf16[2,1024,256]{2,1,0:T(8,128)(2,1)S(1)} %collective-permute-done.5.refs_6_), channel_id=1, source_target_pairs={{2,18},{3,11},{4,20},{5,13},{10,26},{11,3},{12,28},{13,5},{18,2},{... | collective-permute-start | bytes 3145736 | tf_op jit(solution)/shard_map/ppermute | solution.py:43
  124.3 52.5 %collective-permute-start.9 = (bf16[2,1024,256]{2,1,0:T(8,128)(2,1)S(1)}, bf16[2,1024,256]{2,1,0:T(8,128)(2,1)S(1)}, u32[]{:S(2)}, u32[]{:S(2)}) collective-permute-start(bf16[2,1024,256]{2,1,0:T(8,128)(2,1)S(1)} %collective-permute-done.7.refs_7_), channel_id=1, source_target_pairs={{0,16},{1,9},{6,22},{7,15},{8,24},{9,1},{14,30},{15,7},{16,0},{17,... | collective-permute-start | bytes 3145736 | tf_op jit(solution)/shard_map/ppermute | solution.py:43
  128.9 49.0 %collective-permute-start.12 = (bf16[2,1024,256]{2,1,0:T(8,128)(2,1)}, bf16[2,1024,256]{2,1,0:T(8,128)(2,1)S(1)}, u32[]{:S(2)}, u32[]{:S(2)}) collective-permute-start(bf16[2,1024,256]{2,1,0:T(8,128)(2,1)} %collective-permute-done.10.refs_11_), channel_id=1, source_target_pairs={{0,16},{1,9},{6,22},{7,15},{8,24},{9,1},{14,30},{15,7},{16,0},{17,... | collective-permute-start | bytes 3145736 | tf_op jit(solution)/shard_map/ppermute | solution.py:43
  132.9 2.6 %collective-permute-start.22 = (bf16[2,256,512]{2,1,0:T(8,128)(2,1)S(1)}, bf16[2,256,512]{2,1,0:T(8,128)(2,1)S(1)}, u32[]{:S(2)}, u32[]{:S(2)}) collective-permute-start(bf16[2,256,512]{2,1,0:T(8,128)(2,1)S(1)} %get-tuple-element.33), channel_id=1, source_target_pairs={{2,4},{3,5},{4,2},{5,3},{10,12},{11,13},{12,10},{13,11},{18,20},{1... | collective-permute-start | bytes 1572872 | tf_op jit(solution)/shard_map/ppermute | solution.py:43
  134.8 2.6 %collective-permute-start.29 = (bf16[2,256,512]{2,1,0:T(8,128)(2,1)S(1)}, bf16[2,256,512]{2,1,0:T(8,128)(2,1)S(1)}, u32[]{:S(2)}, u32[]{:S(2)}) collective-permute-start(bf16[2,256,512]{2,1,0:T(8,128)(2,1)S(1)} %get-tuple-element.37), channel_id=1, source_target_pairs={{2,4},{3,5},{4,2},{5,3},{10,12},{11,13},{12,10},{13,11},{18,20},{1... | collective-permute-start | bytes 1572872 | tf_op jit(solution)/shard_map/ppermute | solution.py:43
  135.5 59.0 %collective-permute-start.20 = (bf16[2,256,512]{2,1,0:T(8,128)(2,1)}, bf16[2,256,512]{2,1,0:T(8,128)(2,1)S(1)}, u32[]{:S(2)}, u32[]{:S(2)}) collective-permute-start(bf16[2,256,512]{2,1,0:T(8,128)(2,1)} %get-tuple-element.32), channel_id=1, source_target_pairs={{2,4},{3,5},{4,2},{5,3},{10,12},{11,13},{12,10},{13,11},{18,20},{1... | collective-permute-start | bytes 1572872 | tf_op jit(solution)/shard_map/ppermute | solution.py:43
  137.4 57.2 %collective-permute-start.23 = (bf16[2,256,512]{2,1,0:T(8,128)(2,1)}, bf16[2,256,512]{2,1,0:T(8,128)(2,1)}, u32[]{:S(2)}, u32[]{:S(2)}) collective-permute-start(bf16[2,256,512]{2,1,0:T(8,128)(2,1)} %fusion.5), channel_id=1, source_target_pairs={{0,2},{1,3},{2,0},{3,1},{4,6},{5,7},{6,4},{7,5},{8,10},{9,11},{10,... | collective-permute-start | bytes 1572872 | tf_op jit(solution)/shard_map/ppermute | solution.py:43
  175.5 1.4 copy-start.13
  176.9 33.4 %collective-permute-start.16 = (bf16[384,2048]{1,0:T(8,128)(2,1)}, bf16[384,2048]{1,0:T(8,128)(2,1)S(1)}, u32[]{:S(2)}, u32[]{:S(2)}) collective-permute-start(bf16[384,2048]{1,0:T(8,128)(2,1)} %get-tuple-element.23), channel_id=1, source_target_pairs={{0,1},{1,0},{2,3},{3,2},{4,5},{5,4},{6,7},{7,6},{8,9},{9,8},{10,11... | collective-permute-start | bytes 4718600 | tf_op jit(solution)/shard_map/ppermute | solution.py:43
  177.0 19.7 %collective-permute-start.27 = (bf16[2,256,512]{2,1,0:T(8,128)(2,1)S(1)}, bf16[2,256,512]{2,1,0:T(8,128)(2,1)S(1)}, u32[]{:S(2)}, u32[]{:S(2)}) collective-permute-start(bf16[2,256,512]{2,1,0:T(8,128)(2,1)S(1)} %copy-done.13), channel_id=1, source_target_pairs={{2,4},{3,5},{4,2},{5,3},{10,12},{11,13},{12,10},{13,11},{18,20},{1... | collective-permute-start | bytes 1572872 | tf_op jit(solution)/shard_map/ppermute | solution.py:43
  177.9 3.3 %copy-start.11 = (bf16[2,1024,256]{2,1,0:T(8,128)(2,1)}, bf16[2,1024,256]{2,1,0:T(8,128)(2,1)S(1)}, u32[]{:S(2)}) copy-start(bf16[2,1024,256]{2,1,0:T(8,128)(2,1)S(1)} %collective-permute-done.12.refs_13_) | copy-start | bytes 3145732
  177.9 20.3 %collective-permute-start.30 = (bf16[2,256,512]{2,1,0:T(8,128)(2,1)S(1)}, bf16[2,256,512]{2,1,0:T(8,128)(2,1)S(1)}, u32[]{:S(2)}, u32[]{:S(2)}) collective-permute-start(bf16[2,256,512]{2,1,0:T(8,128)(2,1)S(1)} %fusion.1), channel_id=1, source_target_pairs={{0,2},{1,3},{2,0},{3,1},{4,6},{5,7},{6,4},{7,5},{8,10},{9,11},{10,... | collective-permute-start | bytes 1572872 | tf_op jit(solution)/shard_map/ppermute | solution.py:43
  194.6 12.6 %collective-permute-start.15 = (f32[384,1024]{1,0:T(8,128)}, f32[384,1024]{1,0:T(8,128)}, u32[]{:S(2)}, u32[]{:S(2)}) collective-permute-start(f32[384,1024]{1,0:T(8,128)} %get-tuple-element.20), channel_id=1, source_target_pairs={{0,1},{1,0},{2,3},{3,2},{4,5},{5,4},{6,7},{7,6},{8,9},{9,8},{10,11... | collective-permute-start | bytes 4718600 | tf_op jit(solution)/shard_map/ppermute | solution.py:43
  194.6 15.6 %collective-permute-start.17 = (bf16[384,2048]{1,0:T(8,128)(2,1)}, bf16[384,2048]{1,0:T(8,128)(2,1)}, u32[]{:S(2)}, u32[]{:S(2)}) collective-permute-start(bf16[384,2048]{1,0:T(8,128)(2,1)} %get-tuple-element.24), channel_id=1, source_target_pairs={{0,1},{1,0},{2,3},{3,2},{4,5},{5,4},{6,7},{7,6},{8,9},{9,8},{10,11... | collective-permute-start | bytes 4718600 | tf_op jit(solution)/shard_map/ppermute | solution.py:43
  196.6 6.4 %collective-permute-start.24 = (bf16[256,512]{1,0:T(8,128)(2,1)S(1)}, bf16[256,512]{1,0:T(8,128)(2,1)S(1)}, u32[]{:S(2)}, u32[]{:S(2)}) collective-permute-start(bf16[256,512]{1,0:T(8,128)(2,1)S(1)} %fusion.12), channel_id=1, source_target_pairs={{0,8},{1,17},{2,10},{3,19},{4,12},{5,21},{6,14},{7,23},{8,0},{9,25... | collective-permute-start | bytes 786440 | tf_op jit(solution)/shard_map/ppermute | solution.py:43
  199.5 6.4 %collective-permute-start.31 = (bf16[256,512]{1,0:T(8,128)(2,1)S(1)}, bf16[256,512]{1,0:T(8,128)(2,1)S(1)}, u32[]{:S(2)}, u32[]{:S(2)}) collective-permute-start(bf16[256,512]{1,0:T(8,128)(2,1)S(1)} %fusion.13), channel_id=1, source_target_pairs={{0,8},{1,17},{2,10},{3,19},{4,12},{5,21},{6,14},{7,23},{8,0},{9,25... | collective-permute-start | bytes 786440 | tf_op jit(solution)/shard_map/ppermute | solution.py:43
  207.1 3.1 %copy-start.4 = (bf16[384,2048]{1,0:T(8,128)(2,1)S(1)}, bf16[384,2048]{1,0:T(8,128)(2,1)}, u32[]{:S(2)}) copy-start(bf16[384,2048]{1,0:T(8,128)(2,1)} %get-tuple-element.21.refs_0_) | copy-start | bytes 4718596
  207.1 3.2 %copy-start.5 = (bf16[384,2048]{1,0:T(8,128)(2,1)S(1)}, bf16[384,2048]{1,0:T(8,128)(2,1)}, u32[]{:S(2)}) copy-start(bf16[384,2048]{1,0:T(8,128)(2,1)} %get-tuple-element.22.refs_1_) | copy-start | bytes 4718596

commit v4 on v1

v4 whole, which is shorter than its diff:
```python
import math

import jax
import jax.numpy as jnp
from jax import lax
from jax.experimental import pallas as pl
from jax.experimental.pallas import tpu as pltpu
from jax.sharding import Mesh, PartitionSpec as P

F32, BF16 = jnp.float32, jnp.bfloat16
AXES = ("blk", "chip", "core")
SHRINK = 1000


def hops(move):
    pairs = []
    for blk in range(4):
        for z in range(4):
            for core in range(2):
                to = move(blk, z, core)
                if to is not None:
                    pairs.append(((blk * 4 + z) * 2 + core, (to[0] * 4 + to[1]) * 2 + to[2]))
    return pairs


def middle(z):
    return z in (1, 2)


SWAP = hops(lambda b, z, c: (b, z, 1 - c))
FLIP_A = hops(lambda b, z, c: (b ^ (1 + c), z, c))
FLIP_B = hops(lambda b, z, c: (b ^ (2 - c), z, c))
PAIR = hops(lambda b, z, c: (b, z ^ 1, c))
MID = hops(lambda b, z, c: (b, z ^ 3, c) if middle(z) else None)
OUT = hops(lambda b, z, c: (b, z ^ 1, c) if middle(z) else None)
IN = hops(lambda b, z, c: (b, z ^ 1, c) if not middle(z) else None)


def after(array, *others):
    return lax.optimization_barrier((array, *others))[0]


def sent(array, pairs):
    return lax.ppermute(array, AXES, pairs)


def column_block(place, a, b):
    core = place[1]
    return place[2] ^ (a * (1 + core)) ^ (b * (2 - core))


def cost(flops, moved):
    return pl.CostEstimate(flops=flops // SHRINK, bytes_accessed=moved // SHRINK, transcendentals=0)


def pack_kernel(place, acts, out):
    out[...] = acts[...]


def packed(place, first, activations, rows):
    tokens = activations.shape[0]
    return pl.pallas_call(
        pack_kernel,
        grid_spec=pltpu.PrefetchScalarGridSpec(
            num_scalar_prefetch=1,
            grid=(2, 2),
            in_specs=[
                pl.BlockSpec(
                    (tokens, rows // 2),
                    lambda k, r, s: (0, 2 * (2 * (s[0] ^ (first + k)) + 1 - s[1]) + r),
                )
            ],
            out_specs=pl.BlockSpec((tokens, rows // 2), lambda k, r, s: (0, 2 * k + r)),
        ),
        out_shape=jax.ShapeDtypeStruct((tokens, 2 * rows), BF16),
        cost_estimate=cost(0, 8 * tokens * rows),
        name="pack",
    )(place, activations)


def term_kernel(place, mine, other, cot_mine, cot_other, *refs):
    tokens, cols = cot_mine.shape[0], cot_mine.shape[1] // 4
    turned = refs[-1]

    @pl.when((pl.program_id(0) == 0) & (pl.program_id(1) == 0))
    def _():
        for b in (0, 1):
            for a in (0, 1):
                at = pl.ds(pl.multiple_of(column_block(place, a, b) * cols, cols), cols)
                to = slice((2 * b + a) * cols, (2 * b + a + 1) * cols)
                turned[to, :tokens] = cot_mine[:, at].T
                turned[to, tokens:] = cot_other[:, at].T

    tall = jnp.concatenate([mine[...], other[...]], 0)
    for b in (0, 1):
        part = jnp.dot(
            turned[2 * b * cols : (2 * b + 2) * cols], tall, preferred_element_type=F32
        ).astype(BF16)
        for k in (0, 1):

            @pl.when(pl.program_id(0) == k)
            def _():
                refs[2 * b + k][...] = part.reshape(2, cols, part.shape[1])


def terms(place, first, activations, other, cot_mine, cot_other, rows):
    tokens, columns = cot_mine.shape
    part, cols = rows // 2, columns // 4
    whole = pl.BlockSpec((tokens, columns), lambda k, r, s: (0, 0))
    pieces = [
        pl.BlockSpec((2, cols, part), lambda k, r, s: (0, 0, jnp.where(k == 0, r, 1))),
        pl.BlockSpec((2, cols, part), lambda k, r, s: (0, 0, jnp.where(k == 0, 0, r))),
    ]
    return pl.pallas_call(
        term_kernel,
        grid_spec=pltpu.PrefetchScalarGridSpec(
            num_scalar_prefetch=1,
            grid=(2, 2),
            in_specs=[
                pl.BlockSpec(
                    (tokens, part),
                    lambda k, r, s: (0, 2 * (2 * (s[0] ^ (first + k)) + s[1]) + r),
                ),
                pl.BlockSpec((tokens, part), lambda k, r, s: (0, 2 * k + r)),
                whole,
                whole,
            ],
            out_specs=pieces * 2,
            scratch_shapes=[pltpu.VMEM((columns, 2 * tokens), BF16)],
        ),
        out_shape=[jax.ShapeDtypeStruct((2, cols, rows), BF16)] * 4,
        compiler_params=pltpu.CompilerParams(vmem_limit_bytes=28 * 2**20),
        cost_estimate=cost(16 * tokens * rows * columns, 8 * tokens * rows + 8 * rows * columns),
        name="terms",
    )(place, activations, other, cot_mine, cot_other)


def project_kernel(place, *refs, first, last):
    acts, other, cot_mine, cot_other, here, there = refs[:6]
    at_out = 6 if first else 8
    near, far, *keys = refs[at_out:-2]
    acc, cots = refs[-2:]
    tokens, cols = cot_mine.shape[0], cot_mine.shape[1] // 4
    tile = pl.program_id(0)
    blocks = [
        (
            slice((2 * b + a) * cols, (2 * b + a + 1) * cols),
            pl.ds(pl.multiple_of(column_block(place, a, b) * cols, cols), cols),
        )
        for b in (0, 1)
        for a in (0, 1)
    ]

    @pl.when(tile == 0)
    def _():
        for to, at in blocks:
            cots[:tokens, to] = cot_mine[:, at]
            cots[tokens:, to] = cot_other[:, at]

    weight = jnp.concatenate([here[0], here[1], there[0], there[1]], 1)
    tall = jnp.concatenate([acts[...], other[...]], 0)
    sums = jnp.dot(tall, weight, preferred_element_type=F32)

    @pl.when(tile == 0)
    def _():
        acc[...] = sums if first else refs[6][...] + sums

    @pl.when(tile > 0)
    def _():
        acc[...] += sums

    total = lax.dot_general(
        cots[...], weight, (((1,), (1,)), ((), ())), preferred_element_type=F32
    ).astype(BF16)
    near[...] = total[:tokens]
    far[...] = total[tokens:]

    @pl.when(tile == pl.num_programs(0) - 1)
    def _():
        if last:
            for to, at in blocks:
                keys[0][:, at] = acc[:tokens, to]
                keys[1][:, at] = acc[tokens:, to]
        else:
            keys[0][...] = acc[...]


def projected(place, k, activations, others, cot_mine, cot_other, here, there, so_far=None):
    tokens, columns = cot_mine.shape
    _, rows, cols = here.shape
    part = rows // 2
    first, last = k == 0, k == 3
    whole = pl.BlockSpec((tokens, columns), lambda r, s: (0, 0))
    both = pl.BlockSpec((2 * tokens, columns), lambda r, s: (0, 0))
    mine = pl.BlockSpec((tokens, part), lambda r, s: (0, 2 * (2 * (s[0] ^ k) + s[1]) + r))
    piece = pl.BlockSpec((2, part, cols), lambda r, s: (0, r, 0))
    one = jax.ShapeDtypeStruct((tokens, columns), F32)
    return pl.pallas_call(
        lambda *refs: project_kernel(*refs, first=first, last=last),
        grid_spec=pltpu.PrefetchScalarGridSpec(
            num_scalar_prefetch=1,
            grid=(2,),
            in_specs=[
                mine,
                pl.BlockSpec((tokens, part), lambda r, s: (0, 2 * (k % 2) + r)),
                whole,
                whole,
                piece,
                piece,
            ]
            + ([] if first else [both, pl.BlockSpec(memory_space=pl.ANY)]),
            out_specs=[mine, pl.BlockSpec((tokens, part), lambda r, s: (0, r))]
            + ([whole, whole] if last else [both]),
            scratch_shapes=[
                pltpu.VMEM((2 * tokens, columns), F32),
                pltpu.VMEM((2 * tokens, columns), BF16),
            ],
        ),
        out_shape=[
            jax.ShapeDtypeStruct(activations.shape, BF16),
            jax.ShapeDtypeStruct((tokens, rows), BF16),
        ]
        + ([one, one] if last else [jax.ShapeDtypeStruct((2 * tokens, columns), F32)]),
        input_output_aliases={} if first else {8: 0},
        compiler_params=pltpu.CompilerParams(vmem_limit_bytes=48 * 2**20),
        cost_estimate=cost(
            8 * tokens * rows * columns, 8 * tokens * rows + 2 * rows * columns + 8 * tokens * columns
        ),
        name="project",
    )(
        place, activations, others, cot_mine, cot_other, here, there,
        *([] if first else [so_far[1], so_far[0]]),
    )


def lay_kernel(place, *refs, count):
    for i in range(count):

        @pl.when(pl.program_id(0) == i)
        def _():
            refs[-1][...] = refs[i][...]


def laid(place, offsets, whole, far):
    tokens, rows = far[0].shape
    count, start = len(offsets), offsets[0]
    return pl.pallas_call(
        lambda *refs: lay_kernel(*refs, count=count),
        grid_spec=pltpu.PrefetchScalarGridSpec(
            num_scalar_prefetch=1,
            grid=(count, 2),
            in_specs=[
                pl.BlockSpec(
                    (tokens, rows // 2),
                    lambda i, r, s, n=n: (0, jnp.clip(2 * (i - n) + r, 0, 1)),
                )
                for n in range(count)
            ]
            + [pl.BlockSpec(memory_space=pl.ANY)],
            out_specs=pl.BlockSpec(
                (tokens, rows // 2),
                lambda i, r, s: (0, 2 * (2 * (s[0] ^ (start + i)) + 1 - s[1]) + r),
            ),
        ),
        out_shape=jax.ShapeDtypeStruct(whole.shape, BF16),
        input_output_aliases={1 + count: 0},
        cost_estimate=cost(0, 4 * count * tokens * rows),
        name="lay",
    )(place, *far, whole)


def added(*arrays):
    total = arrays[0].astype(F32)
    for array in arrays[1:]:
        total = total + array.astype(F32)
    return total


def by_hops(activations, cotangent, kv_weight):
    rows = kv_weight.shape[0]
    tokens = activations.shape[0]
    place = jnp.stack([lax.axis_index(name) for name in ("chip", "core", "blk")]).astype(jnp.int32)

    cot_other = sent(cotangent, SWAP)
    base = jnp.stack([kv_weight, sent(kv_weight, FLIP_A)])
    high = sent(packed(place, 2, after(activations, base), rows), SWAP)
    low = sent(packed(place, 0, after(activations, high), rows), SWAP)
    one, mid = sent(base, PAIR), sent(base, MID)
    base_b = sent(base, FLIP_B)

    shared = (cotangent, cot_other)
    keep2, keep3, send2, send3 = terms(place, 2, activations, high, *shared, rows)
    got3 = sent(after(send3, base), FLIP_B)
    got2 = sent(after(send2, base_b), FLIP_B)
    keep0, keep1, send0, send1 = terms(place, 0, after(activations, keep2), low, *shared, rows)
    so_far = projected(place, 0, after(activations, keep0), low, *shared, base, base_b)
    out0 = sent(so_far[1], SWAP)

    got1 = sent(after(send1, got3), FLIP_B)
    far = sent(after(added(keep3, got3).astype(BF16), one, mid), IN)
    two_mid = sent(one, MID)
    two_end = sent(mid, OUT)
    got0 = sent(after(send0, got2), FLIP_B)
    sum2 = added(keep2, got2)
    two = two_mid + two_end
    near = sent(after(sum2.astype(BF16), far, two), IN)
    mid_far = sent(added(keep2, got2, far).astype(BF16), MID)
    three_end = sent(two_mid, OUT)
    one_b = sent(after(one, got1), FLIP_B)
    two_b = sent(after(two, got0), FLIP_B)

    so_far = projected(place, 1, activations, low, *shared, one, one_b, (so_far[0], so_far[2]))
    out1 = sent(so_far[1], SWAP)
    three = mid + three_end
    sum_mid = sent(after(added(keep3, got3, near).astype(BF16), three), MID)
    sum_one = sent(added(keep1, got1, mid_far).astype(BF16), PAIR)
    three_b = sent(after(three, one_b), FLIP_B)
    so_far = projected(place, 2, activations, high, *shared, two, two_b, (so_far[0], so_far[2]))
    out2 = sent(so_far[1], SWAP)
    last = added(keep0, got0, sum_mid, sum_one)
    final = last[0] + sent(last[1].astype(BF16), FLIP_A).astype(F32)
    grad_weight = (final * (1.0 / math.sqrt(32 * tokens))).astype(BF16).T

    whole = laid(place, (0, 1, 2), so_far[0], (out0, out1, out2))
    whole, out3, keys, keys_far = projected(
        place, 3, activations, high, *shared, three, three_b, (whole, so_far[2])
    )
    grad_input = laid(place, (3,), whole, (sent(out3, SWAP),))
    key_values = (keys + sent(keys_far, SWAP)).astype(BF16)
    return (key_values, grad_input, grad_weight)


def swapped(array):
    return lax.ppermute(array, "core", [(0, 1), (1, 0)])


def by_collectives(activations, cotangent, kv_weight):
    blocks, chips = lax.axis_size("blk"), lax.axis_size("chip")
    core = lax.axis_index("core")
    tokens, features = activations.shape
    rows, cols = kv_weight.shape
    columns = cotangent.shape[1]
    by_core = activations.reshape(tokens, chips, 2, rows)
    mine = lax.dynamic_index_in_dim(by_core, core, 2, keepdims=False)
    other = lax.dynamic_index_in_dim(by_core, 1 - core, 2, keepdims=False)
    acts = jnp.concatenate([mine, swapped(other)], 0)
    cots = jnp.concatenate([cotangent, swapped(cotangent)], 0)
    weight = lax.all_gather(kv_weight, ("blk", "chip"), axis=0, tiled=False)
    weight = weight.reshape(blocks, chips, rows, cols)
    parts = jnp.einsum(
        "tzr,tbc->bzrc", acts, cots.reshape(2 * tokens, blocks, cols), preferred_element_type=F32
    ).astype(BF16).reshape(blocks * chips, rows, cols)
    total = lax.psum_scatter(parts, ("blk", "chip"), scatter_dimension=0, tiled=False)
    count = tokens * blocks * chips * 2
    grad_weight = (total.astype(F32) * (1.0 / math.sqrt(count))).astype(BF16)
    full = weight.transpose(1, 2, 0, 3).reshape(chips * rows, columns)
    keys = jnp.dot(acts.reshape(2 * tokens, chips * rows), full, preferred_element_type=F32)
    key_values = (keys[:tokens] + swapped(keys[tokens:])).astype(BF16)
    inputs = lax.dot_general(
        cots, full, (((1,), (1,)), ((), ())), preferred_element_type=F32
    ).astype(BF16).reshape(2 * tokens, chips, rows)
    near, far = inputs[:tokens], swapped(inputs[tokens:])
    low = jnp.where(core == 0, near, far)
    high = jnp.where(core == 0, far, near)
    grad_input = jnp.stack([low, high], 2).reshape(tokens, features)
    return (key_values, grad_input, grad_weight)


def solution(mesh):
    blocks, shards = mesh.shape["blk"], mesh.shape["shard"]
    split = Mesh(mesh.devices.reshape(blocks, shards // 2, 2), AXES)
    by_token = P(AXES, None)
    by_piece = P(("chip", "core"), "blk")
    return jax.shard_map(
        by_hops if (blocks, shards) == (4, 8) else by_collectives,
        mesh=split,
        in_specs=(by_token, by_token, by_piece),
        out_specs=(by_token, by_token, by_piece),
        check_vma=False,
    )
```

time: 319 us -> 178 us (0.56)
  waiting for transfers between devices: 151 us -> 36.6 us
  local copies, waits for them, and re-layouts: 102 us -> 11.9 us
  Pallas kernels: 0 us -> 68.7 us
  starting transfers between devices: 1.14 us -> 39.5 us
  matrix products: 31.1 us -> 0 us
  between operations: 14.1 us -> 0.91 us
    reduce_scatter x1 -> x0, waiting for transfers between devices: 88.5 us -> none  [local(): lax.psum_scatter(terms, ('blk', 'chip'), scatter_dimension=0, tiled=False)]
    pallas_call x0 -> x10, Pallas kernels: none -> 68.7 us  [the longest x4 37.1 us: projected(): pl.pallas_call(lambda *refs: project_kernel(*refs, first=first, last=last...]
    all_gather x1 -> x0, waiting for transfers between devices: 59.8 us -> none  [local(): weight = lax.all_gather(kv_weight, ('blk', 'chip'), axis=0, tiled=False)]
    ppermute x4 -> x28, starting transfers between devices: 1.07 us -> 39.5 us  [sent(): return lax.ppermute(array, AXES, pairs)]
    reshape x3 -> x0, local copies, waits for them, and re-layouts: 35.6 us -> none  [the longest x1 12.3 us: local(): terms = jnp.einsum('tzr,tbc->bzrc', acts, cots.reshape(2 * tokens, blocks...]
    ppermute x4 -> x28, waiting for transfers between devices: 1.72 us -> 36.6 us  [sent(): return lax.ppermute(array, AXES, pairs)]
    dot_general x3 -> x0, matrix products: 31.1 us -> none  [the longest x1 11.3 us: local(): jnp.einsum('tzr,tbc->bzrc', acts, cots.reshape(2 * tokens, blocks, cols),...]
    slice x4 -> x0, local copies, waits for them, and re-layouts: 14.5 us -> none  [the longest x3 13.2 us: local(): near, far = (inputs[:tokens], swapped(inputs[tokens:]))]
  transfers between devices with their start and end apart: 6 -> 28, of which waited for: 3 -> 9; matrix products, arithmetic and copies ran while one was open for 46% -> 9% of each run, Pallas kernels for 0% -> 36%
where the time goes in v4:
time: 178 us; the launch traced here: 177 us
  Pallas kernels  68.7 us (39%)
  starting transfers between devices  39.5 us (22%)
  waiting for transfers between devices  36.6 us (21%)
  other arithmetic  19.2 us (11%)
  local copies, waits for them, and re-layouts  11.9 us (7%)
    ppermute x28, starting transfers between devices, sent(): return lax.ppermute(array, AXES, pairs)  39.5 us
    pallas_call x4, Pallas kernels, projected(): pl.pallas_call(lambda *refs: project_kernel(*refs, first=first, last=last...  37.1 us
    ppermute x28, waiting for transfers between devices, sent(): return lax.ppermute(array, AXES, pairs)  36.6 us
    pallas_call x2, Pallas kernels, terms(): pl.pallas_call(term_kernel, grid_spec=pltpu.PrefetchScalarGridSpec(num_sc...  14.3 us
    unnamed x47, local copies, waits for them, and re-layouts  11.8 us
    pallas_call x2, Pallas kernels, laid(): pl.pallas_call(lambda *refs: lay_kernel(*refs, count=count), grid_spec=pl...  8.67 us
    pallas_call x2, Pallas kernels, packed(): pl.pallas_call(pack_kernel, grid_spec=pltpu.PrefetchScalarGridSpec(num_sc...  8.62 us
  transfers between devices with their start and end apart: 28, of which 9 were waited for; matrix products, arithmetic and copies ran while one was open for 9% of the time, Pallas kernels for 36%

profile of v4, /device:TPU:0, one launch (start us, length us, event | category | flops | bytes accessed | tf_op | source)
XLA Modules:
  0.0 176.8 jit_solution(10521643703299121374)
XLA Ops:
  0.6 3.0 %collective-permute-start = (bf16[1024,256]{1,0:T(8,128)(2,1)}, bf16[1024,256]{1,0:T(8,128)(2,1)S(1)}, u32[]{:S(2)}, u32[]{:S(2)}) collective-permute-start(bf16[1024,256]{1,0:T(8,128)(2,1)} %param.5), channel_id=1, source_target_pairs={{0,8},{1,17},{2,10},{3,19},{4,12},{5,21},{6,14},{7,23},{8,0},{9,25... | collective-permute-start | bytes 1572872 | tf_op jit(solution)/shard_map/ppermute | solution.py:44
  4.3 6.7 %collective-permute-done = bf16[1024,256]{1,0:T(8,128)(2,1)S(1)} collective-permute-done((bf16[1024,256]{1,0:T(8,128)(2,1)}, bf16[1024,256]{1,0:T(8,128)(2,1)S(1)}, u32[]{:S(2)}, u32[]{:S(2)}) %collective-permute-start) | collective-permute-done | bytes 524320 | tf_op jit(solution)/shard_map/ppermute | solution.py:44
  11.0 2.2 %pad_maximum_fusion.refs_5_ = bf16[2,1024,256]{2,1,0:T(8,128)(2,1)} fusion(bf16[1,1024,256]{2,1,0:T(8,128)(2,1)S(1)} %bitcast.20, bf16[1,1024,256]{2,1,0:T(8,128)(2,1)} %bitcast.19), kind=kLoop, calls=%fused_computation.14 | loop fusion | flops 524288 | bytes 2097152 | tf_op jit(solution)/shard_map/stack | solution.py:285
  13.2 4.4 %pack.2 = bf16[384,2048]{1,0:T(8,128)(2,1)} custom-call(s32[3]{0:T(128)} %pad_add_fusion.place.refs_0_, bf16[384,8192]{1,0:T(8,128)(2,1)} %refs_1_.6), custom_call_target="tpu_custom_call" | custom-call | bytes 3145 | tf_op jit(solution)/shard_map/pack/pallas_call | solution.py:62
  18.1 2.1 %collective-permute-start.4 = (bf16[2,1024,256]{2,1,0:T(8,128)(2,1)}, bf16[2,1024,256]{2,1,0:T(8,128)(2,1)}, u32[]{:S(2)}, u32[]{:S(2)}) collective-permute-start(bf16[2,1024,256]{2,1,0:T(8,128)(2,1)} %pad_maximum_fusion.refs_5_), channel_id=1, source_target_pairs={{0,2},{1,3},{2,0},{3,1},{4,6},{5,7},{6,4},{7,5},{8,10},{9,11},{10,... | collective-permute-start | bytes 3145736 | tf_op jit(solution)/shard_map/ppermute | solution.py:44
  20.2 1.7 collective-permute-start.3
  21.8 1.5 collective-permute-start.13
  23.4 2.8 %copy-done = bf16[384,8192]{1,0:T(8,128)(2,1)S(1)} copy-done((bf16[384,8192]{1,0:T(8,128)(2,1)S(1)}, bf16[384,8192]{1,0:T(8,128)(2,1)}, u32[]{:S(2)}) %copy-start) | copy-done | bytes 6291480
  26.1 7.5 %terms.2 = (bf16[2,256,1024]{2,1,0:T(8,128)(2,1)S(1)}, bf16[2,256,1024]{2,1,0:T(8,128)(2,1)S(1)}, bf16[2,256,1024]{2,1,0:T(8,128)(2,1)S(1)}, bf16[2,256,1024]{2,1,0:T(8,128)(2,1)}) custom-call(s32[3]{0:T(128)S(1)} %copy-done.11, bf16[384,8192]{1,0:T(8,128)(2,1)S(1)} %copy-done, bf16[384,2048]{1,0:T(8,128)(2,1)S(1)} %collective-permute-done.1.other.refs_2_, ...), custom_call_target="tpu_custom_call" | custom-call | flops 6442450 | bytes 11534 | tf_op jit(solution)/shard_map/terms/pallas_call | solution.py:114
  34.6 1.0 copy-done.7
  35.6 1.0 copy-done.14
  36.6 1.0 collective-permute-start.8
  37.6 4.2 %pack.3 = bf16[384,2048]{1,0:T(8,128)(2,1)} custom-call(s32[3]{0:T(128)} %pad_add_fusion.place.refs_0_, bf16[384,8192]{1,0:T(8,128)(2,1)} %refs_1_.6), custom_call_target="tpu_custom_call" | custom-call | bytes 3145 | tf_op jit(solution)/shard_map/pack/pallas_call | solution.py:62
  41.8 2.0 %collective-permute-done.4.refs_5_ = bf16[2,1024,256]{2,1,0:T(8,128)(2,1)} collective-permute-done((bf16[2,1024,256]{2,1,0:T(8,128)(2,1)}, bf16[2,1024,256]{2,1,0:T(8,128)(2,1)}, u32[]{:S(2)}, u32[]{:S(2)}) %collective-permute-start.4) | collective-permute-done | bytes 1048608 | tf_op jit(solution)/shard_map/ppermute | solution.py:44
  44.5 1.3 collective-permute-start.12
  45.8 1.8 collective-permute-start.14
  47.6 4.1 %collective-permute-done.8 = bf16[2,256,1024]{2,1,0:T(8,128)(2,1)} collective-permute-done((bf16[2,256,1024]{2,1,0:T(8,128)(2,1)}, bf16[2,256,1024]{2,1,0:T(8,128)(2,1)}, u32[]{:S(2)}, u32[]{:S(2)}) %collective-permute-start.8) | collective-permute-done | bytes 1048608 | tf_op jit(solution)/shard_map/ppermute | solution.py:44
  51.7 1.9 %fusion = bf16[2,256,1024]{2,1,0:T(8,128)(2,1)S(1)} fusion(bf16[2,256,1024]{2,1,0:T(8,128)(2,1)} %collective-permute-done.8, bf16[2,256,1024]{2,1,0:T(8,128)(2,1)} %copy-done.5), kind=kLoop, calls=%fused_computation.6 | loop fusion | flops 2097152 | bytes 3145728 | tf_op jit(solution)/shard_map/convert_element_type | solution.py:300
  53.6 5.4 %collective-permute-start.22 = (bf16[2,256,1024]{2,1,0:T(8,128)(2,1)S(1)}, bf16[2,256,1024]{2,1,0:T(8,128)(2,1)S(1)}, u32[]{:S(2)}, u32[]{:S(2)}) collective-permute-start(bf16[2,256,1024]{2,1,0:T(8,128)(2,1)S(1)} %fusion), channel_id=1, source_target_pairs={{0,2},{1,3},{6,4},{7,5},{8,10},{9,11},{14,12},{15,13},{16,18},{17,... | collective-permute-start | bytes 3145736 | tf_op jit(solution)/shard_map/ppermute | solution.py:44
  59.1 2.8 %copy-done.1 = bf16[384,8192]{1,0:T(8,128)(2,1)S(1)} copy-done((bf16[384,8192]{1,0:T(8,128)(2,1)S(1)}, bf16[384,8192]{1,0:T(8,128)(2,1)}, u32[]{:S(2)}) %copy-start.1) | copy-done | bytes 6291480
  61.9 6.8 %terms.3 = (bf16[2,256,1024]{2,1,0:T(8,128)(2,1)S(1)}, bf16[2,256,1024]{2,1,0:T(8,128)(2,1)S(1)}, bf16[2,256,1024]{2,1,0:T(8,128)(2,1)S(1)}, bf16[2,256,1024]{2,1,0:T(8,128)(2,1)S(1)}) custom-call(s32[3]{0:T(128)S(1)} %copy-done.12, bf16[384,8192]{1,0:T(8,128)(2,1)S(1)} %copy-done.1, bf16[384,2048]{1,0:T(8,128)(2,1)S(1)} %collective-permute-done.7.other.refs_2_, ...), custom_call_target="tpu_custom_call" | custom-call | flops 6442450 | bytes 11534 | tf_op jit(solution)/shard_map/terms/pallas_call | solution.py:114
  69.3 1.4 collective-permute-start.6
  70.7 2.0 %collective-permute-done.12 = bf16[2,1024,256]{2,1,0:T(8,128)(2,1)S(1)} collective-permute-done((bf16[2,1024,256]{2,1,0:T(8,128)(2,1)}, bf16[2,1024,256]{2,1,0:T(8,128)(2,1)S(1)}, u32[]{:S(2)}, u32[]{:S(2)}) %collective-permute-start.12) | collective-permute-done | bytes 1048608 | tf_op jit(solution)/shard_map/ppermute | solution.py:44
  73.0 1.6 collective-permute-start.15
  74.6 5.3 %collective-permute-done.22 = bf16[2,256,1024]{2,1,0:T(8,128)(2,1)S(1)} collective-permute-done((bf16[2,256,1024]{2,1,0:T(8,128)(2,1)S(1)}, bf16[2,256,1024]{2,1,0:T(8,128)(2,1)S(1)}, u32[]{:S(2)}, u32[]{:S(2)}) %collective-permute-start.22) | collective-permute-done | bytes 1048608 | tf_op jit(solution)/shard_map/ppermute | solution.py:44
  79.9 1.7 fusion.1
  81.6 5.4 %collective-permute-start.23 = (bf16[2,256,1024]{2,1,0:T(8,128)(2,1)}, bf16[2,256,1024]{2,1,0:T(8,128)(2,1)}, u32[]{:S(2)}, u32[]{:S(2)}) collective-permute-start(bf16[2,256,1024]{2,1,0:T(8,128)(2,1)} %get-tuple-element.70), channel_id=1, source_target_pairs={{0,2},{1,3},{6,4},{7,5},{8,10},{9,11},{14,12},{15,13},{16,18},{17,... | collective-permute-start | bytes 3145736 | tf_op jit(solution)/shard_map/ppermute | solution.py:44
  86.9 1.5 collective-permute-start.10
  89.2 5.7 %collective-permute-done.15 = bf16[2,256,1024]{2,1,0:T(8,128)(2,1)S(1)} collective-permute-done((bf16[2,256,1024]{2,1,0:T(8,128)(2,1)S(1)}, bf16[2,256,1024]{2,1,0:T(8,128)(2,1)S(1)}, u32[]{:S(2)}, u32[]{:S(2)}) %collective-permute-start.15) | collective-permute-done | bytes 1048608 | tf_op jit(solution)/shard_map/ppermute | solution.py:44
  95.8 8.4 %project.4 = (bf16[384,8192]{1,0:T(8,128)(2,1)}, bf16[384,1024]{1,0:T(8,128)(2,1)S(1)}, f32[768,1024]{1,0:T(8,128)}) custom-call(s32[3]{0:T(128)S(1)} %copy-done.12, bf16[384,8192]{1,0:T(8,128)(2,1)} %refs_1_.6, bf16[384,2048]{1,0:T(8,128)(2,1)S(1)} %collective-permute-done.7.other.refs_2_, bf16[384,1024]{1,0:T(8,128)(2,1)S(1)} %copy-done.2, ...), custom_call_target="tpu_custom_call" | custom-call | flops 3221225 | bytes 8388 | tf_op jit(solution)/shard_map/project/pallas_call | solution.py:198
  104.3 2.6 %add.41.refs_5_ = bf16[2,1024,256]{2,1,0:T(8,128)(2,1)} add(bf16[2,1024,256]{2,1,0:T(8,128)(2,1)} %collective-permute-done.3, bf16[2,1024,256]{2,1,0:T(8,128)(2,1)S(1)} %collective-permute-done.6) | non-fusion elementwise | flops 524288 | bytes 3145728 | tf_op jit(solution)/shard_map/add | solution.py:314
  106.9 3.2 %add_convert_fusion.2 = bf16[2,256,1024]{2,1,0:T(8,128)(2,1)} fusion(bf16[2,256,1024]{2,1,0:T(8,128)(2,1)} %collective-permute-done.23, bf16[2,256,1024]{2,1,0:T(8,128)(2,1)} %collective-permute-done.8, bf16[2,256,1024]{2,1,0:T(8,128)(2,1)S(1)} %copy-done.6), kind=kLoop, calls=%fused_computation.3 | loop fusion | flops 3145728 | bytes 4194304 | tf_op jit(solution)/shard_map/convert_element_type | solution.py:315
  110.2 1.7 collective-permute-start.24
  111.8 1.7 collective-permute-start.11
  113.6 1.6 add_convert_fusion
  115.2 3.4 %collective-permute-start.26 = (bf16[2,256,1024]{2,1,0:T(8,128)(2,1)}, bf16[2,256,1024]{2,1,0:T(8,128)(2,1)}, u32[]{:S(2)}, u32[]{:S(2)}) collective-permute-start(bf16[2,256,1024]{2,1,0:T(8,128)(2,1)} %add_convert_fusion), channel_id=1, source_target_pairs={{0,2},{1,3},{2,0},{3,1},{4,6},{5,7},{6,4},{7,5},{8,10},{9,11},{10,... | collective-permute-start | bytes 3145736 | tf_op jit(solution)/shard_map/ppermute | solution.py:44
  118.6 9.7 %project.5 = (bf16[384,8192]{1,0:T(8,128)(2,1)}, bf16[384,1024]{1,0:T(8,128)(2,1)S(1)}, f32[768,1024]{1,0:T(8,128)}) custom-call(s32[3]{0:T(128)S(1)} %copy-done.12, bf16[384,8192]{1,0:T(8,128)(2,1)} %refs_1_.6, bf16[384,2048]{1,0:T(8,128)(2,1)S(1)} %collective-permute-done.7.other.refs_2_, ...), custom_call_target="tpu_custom_call", output_to_operand_aliasing={{0}: (8, {})} | custom-call | flops 3221225 | bytes 8388 | tf_op jit(solution)/shard_map/project/pallas_call | solution.py:198
  128.2 9.4 %project.6 = (bf16[384,8192]{1,0:T(8,128)(2,1)}, bf16[384,1024]{1,0:T(8,128)(2,1)S(1)}, f32[768,1024]{1,0:T(8,128)}) custom-call(s32[3]{0:T(128)S(1)} %copy-done.12, bf16[384,8192]{1,0:T(8,128)(2,1)} %refs_1_.6, bf16[384,2048]{1,0:T(8,128)(2,1)S(1)} %collective-permute-done.1.other.refs_2_, ...), custom_call_target="tpu_custom_call", output_to_operand_aliasing={{0}: (8, {})} | custom-call | flops 3221225 | bytes 8388 | tf_op jit(solution)/shard_map/project/pallas_call | solution.py:198
  138.2 1.8 %collective-permute-done.19.refs_3_ = bf16[384,1024]{1,0:T(8,128)(2,1)S(1)} collective-permute-done((bf16[384,1024]{1,0:T(8,128)(2,1)S(1)}, bf16[384,1024]{1,0:T(8,128)(2,1)S(1)}, u32[]{:S(2)}, u32[]{:S(2)}) %collective-permute-start.19) | collective-permute-done | bytes 786464 | tf_op jit(solution)/shard_map/ppermute | solution.py:44
  140.0 1.1 collective-permute-done.18.refs_2_
  142.0 6.1 %lay.2.refs_8_ = bf16[384,8192]{1,0:T(8,128)(2,1)} custom-call(s32[3]{0:T(128)} %pad_add_fusion.place.refs_0_, bf16[384,1024]{1,0:T(8,128)(2,1)} %copy-done.19, bf16[384,1024]{1,0:T(8,128)(2,1)} %copy-done.21, bf16[384,1024]{1,0:T(8,128)(2,1)} %copy-done.20, bf16[384,8192]{1,0:T(8,128)(2,1)} %get-tuple-element.63.refs_4_), custom_call_target="tpu_custom_call", output_to_operand_aliasing={{}: (4, {})} | custom-call | bytes 4718 | tf_op jit(solution)/shard_map/lay/pallas_call | solution.py:247
  148.1 9.7 %project.7 = (bf16[384,8192]{1,0:T(8,128)(2,1)}, bf16[384,1024]{1,0:T(8,128)(2,1)}, f32[384,1024]{1,0:T(8,128)S(1)}, f32[384,1024]{1,0:T(8,128)}) custom-call(s32[3]{0:T(128)S(1)} %copy-done.13, bf16[384,8192]{1,0:T(8,128)(2,1)} %refs_1_.6, bf16[384,2048]{1,0:T(8,128)(2,1)} %copy-done.3, ...), custom_call_target="tpu_custom_call", output_to_operand_aliasing={{0}: (8, {})} | custom-call | flops 3221225 | bytes 8388 | tf_op jit(solution)/shard_map/project/pallas_call | solution.py:198
  158.0 2.4 %convert_add_fusion = f32[2,256,1024]{2,1,0:T(8,128)S(1)} fusion(bf16[2,256,1024]{2,1,0:T(8,128)(2,1)} %collective-permute-done.26, bf16[2,256,1024]{2,1,0:T(8,128)(2,1)} %collective-permute-done.24, bf16[2,256,1024]{2,1,0:T(8,128)(2,1)S(1)} %copy-done.16, bf16[2,256,1024]{2,1,0:T(8,128)(2,1)S(1)} %copy-done.10), kind=kLoop, calls=%fused_computation | loop fusion | flops 3670016 | bytes 6291456 | tf_op jit(solution)/shard_map/add | solution.py:275
  160.4 1.3 collective-permute-start.27
  161.8 7.9 %collective-permute-done.27 = bf16[256,1024]{1,0:T(8,128)(2,1)S(1)} collective-permute-done((bf16[256,1024]{1,0:T(8,128)(2,1)S(1)}, bf16[256,1024]{1,0:T(8,128)(2,1)S(1)}, u32[]{:S(2)}, u32[]{:S(2)}) %collective-permute-start.27) | collective-permute-done | bytes 524320 | tf_op jit(solution)/shard_map/ppermute | solution.py:44
  169.9 1.0 copy.11
  171.7 2.6 %lay.3 = bf16[384,8192]{1,0:T(8,128)(2,1)} custom-call(s32[3]{0:T(128)} %pad_add_fusion.place.refs_0_, bf16[384,1024]{1,0:T(8,128)(2,1)} %copy-done.22, bf16[384,8192]{1,0:T(8,128)(2,1)} %get-tuple-element.67.refs_2_), custom_call_target="tpu_custom_call", output_to_operand_aliasing={{}: (2, {})} | custom-call | bytes 1572 | tf_op jit(solution)/shard_map/lay/pallas_call | solution.py:247
  174.3 2.5 %add_convert_fusion.3 = bf16[384,1024]{1,0:T(8,128)(2,1)} fusion(f32[384,1024]{1,0:T(8,128)S(1)} %get-tuple-element.64, f32[384,1024]{1,0:T(8,128)} %collective-permute-done.20), kind=kLoop, calls=%fused_computation.8 | loop fusion | flops 786432 | bytes 3932160 | tf_op jit(solution)/shard_map/convert_element_type | solution.py:329
  (77 shorter events, 8.3 us)
Async XLA Ops:
  0.6 10.4 %collective-permute-start = (bf16[1024,256]{1,0:T(8,128)(2,1)}, bf16[1024,256]{1,0:T(8,128)(2,1)S(1)}, u32[]{:S(2)}, u32[]{:S(2)}) collective-permute-start(bf16[1024,256]{1,0:T(8,128)(2,1)} %param.5), channel_id=1, source_target_pairs={{0,8},{1,17},{2,10},{3,19},{4,12},{5,21},{6,14},{7,23},{8,0},{9,25... | collective-permute-start | bytes 1572872 | tf_op jit(solution)/shard_map/ppermute | solution.py:44
  13.2 4.4 %copy-start.2 = (bf16[384,1024]{1,0:T(8,128)(2,1)S(1)}, bf16[384,1024]{1,0:T(8,128)(2,1)}, u32[]{:S(2)}) copy-start(bf16[384,1024]{1,0:T(8,128)(2,1)} %refs_3_.7) | copy-start | bytes 2359300
  13.2 10.2 %copy-start.11 = (s32[3]{0:T(128)S(1)}, s32[3]{0:T(128)}, u32[]{:S(2)}) copy-start(s32[3]{0:T(128)} %pad_add_fusion.place.refs_0_) | copy-start | bytes 40
  17.5 5.8 %collective-permute-start.1 = (bf16[384,2048]{1,0:T(8,128)(2,1)}, bf16[384,2048]{1,0:T(8,128)(2,1)S(1)}, u32[]{:S(2)}, u32[]{:S(2)}) collective-permute-start(bf16[384,2048]{1,0:T(8,128)(2,1)} %pack.2), channel_id=1, source_target_pairs={{0,1},{1,0},{2,3},{3,2},{4,5},{5,4},{6,7},{7,6},{8,9},{9,8},{10,11... | collective-permute-start | bytes 4718600 | tf_op jit(solution)/shard_map/ppermute | solution.py:44
  17.5 5.8 %collective-permute-start.2 = (bf16[384,1024]{1,0:T(8,128)(2,1)S(1)}, bf16[384,1024]{1,0:T(8,128)(2,1)S(1)}, u32[]{:S(2)}, u32[]{:S(2)}) collective-permute-start(bf16[384,1024]{1,0:T(8,128)(2,1)S(1)} %copy-done.2), channel_id=1, source_target_pairs={{0,1},{1,0},{2,3},{3,2},{4,5},{5,4},{6,7},{7,6},{8,9},{9,8},{10,11... | collective-permute-start | bytes 2359304 | tf_op jit(solution)/shard_map/ppermute | solution.py:44
  18.1 25.7 %collective-permute-start.4 = (bf16[2,1024,256]{2,1,0:T(8,128)(2,1)}, bf16[2,1024,256]{2,1,0:T(8,128)(2,1)}, u32[]{:S(2)}, u32[]{:S(2)}) collective-permute-start(bf16[2,1024,256]{2,1,0:T(8,128)(2,1)} %pad_maximum_fusion.refs_5_), channel_id=1, source_target_pairs={{0,2},{1,3},{2,0},{3,1},{4,6},{5,7},{6,4},{7,5},{8,10},{9,11},{10,... | collective-permute-start | bytes 3145736 | tf_op jit(solution)/shard_map/ppermute | solution.py:44
  20.2 24.4 %collective-permute-start.3 = (bf16[2,1024,256]{2,1,0:T(8,128)(2,1)}, bf16[2,1024,256]{2,1,0:T(8,128)(2,1)}, u32[]{:S(2)}, u32[]{:S(2)}) collective-permute-start(bf16[2,1024,256]{2,1,0:T(8,128)(2,1)} %pad_maximum_fusion.refs_5_), channel_id=1, source_target_pairs={{2,4},{3,5},{4,2},{5,3},{10,12},{11,13},{12,10},{13,11},{18,20},{1... | collective-permute-start | bytes 3145736 | tf_op jit(solution)/shard_map/ppermute | solution.py:44
  21.8 24.0 %collective-permute-start.13 = (bf16[2,1024,256]{2,1,0:T(8,128)(2,1)}, bf16[2,1024,256]{2,1,0:T(8,128)(2,1)}, u32[]{:S(2)}, u32[]{:S(2)}) collective-permute-start(bf16[2,1024,256]{2,1,0:T(8,128)(2,1)} %pad_maximum_fusion.refs_5_), channel_id=1, source_target_pairs={{0,16},{1,9},{2,18},{3,11},{4,20},{5,13},{6,22},{7,15},{8,24},{9,1... | collective-permute-start | bytes 3145736 | tf_op jit(solution)/shard_map/ppermute | solution.py:44
  23.3 2.8 %copy-start = (bf16[384,8192]{1,0:T(8,128)(2,1)S(1)}, bf16[384,8192]{1,0:T(8,128)(2,1)}, u32[]{:S(2)}) copy-start(bf16[384,8192]{1,0:T(8,128)(2,1)} %refs_1_.6) | copy-start | bytes 18874372
  26.1 102.1 %copy-start.3 = (bf16[384,2048]{1,0:T(8,128)(2,1)}, bf16[384,2048]{1,0:T(8,128)(2,1)S(1)}, u32[]{:S(2)}) copy-start(bf16[384,2048]{1,0:T(8,128)(2,1)S(1)} %collective-permute-done.1.other.refs_2_) | copy-start | bytes 4718596
  34.6 1.0 copy-start.7
  35.6 1.0 copy-start.14
  36.6 15.1 %collective-permute-start.8 = (bf16[2,256,1024]{2,1,0:T(8,128)(2,1)}, bf16[2,256,1024]{2,1,0:T(8,128)(2,1)}, u32[]{:S(2)}, u32[]{:S(2)}) collective-permute-start(bf16[2,256,1024]{2,1,0:T(8,128)(2,1)} %get-tuple-element.44), channel_id=1, source_target_pairs={{0,16},{1,9},{2,18},{3,11},{4,20},{5,13},{6,22},{7,15},{8,24},{9,1... | collective-permute-start | bytes 3145736 | tf_op jit(solution)/shard_map/ppermute | solution.py:44
  41.8 17.3 %copy-start.12 = (s32[3]{0:T(128)S(1)}, s32[3]{0:T(128)}, u32[]{:S(2)}) copy-start(s32[3]{0:T(128)} %pad_add_fusion.place.refs_0_) | copy-start | bytes 40
  41.8 17.3 %collective-permute-start.7 = (bf16[384,2048]{1,0:T(8,128)(2,1)}, bf16[384,2048]{1,0:T(8,128)(2,1)S(1)}, u32[]{:S(2)}, u32[]{:S(2)}) collective-permute-start(bf16[384,2048]{1,0:T(8,128)(2,1)} %pack.3), channel_id=1, source_target_pairs={{0,1},{1,0},{2,3},{3,2},{4,5},{5,4},{6,7},{7,6},{8,9},{9,8},{10,11... | collective-permute-start | bytes 4718600 | tf_op jit(solution)/shard_map/ppermute | solution.py:44
  43.8 25.5 %collective-permute-start.5 = (bf16[2,1024,256]{2,1,0:T(8,128)(2,1)}, bf16[2,1024,256]{2,1,0:T(8,128)(2,1)S(1)}, u32[]{:S(2)}, u32[]{:S(2)}) collective-permute-start(bf16[2,1024,256]{2,1,0:T(8,128)(2,1)} %collective-permute-done.4.refs_5_), channel_id=1, source_target_pairs={{2,4},{3,5},{4,2},{5,3},{10,12},{11,13},{12,10},{13,11},{18,20},{1... | collective-permute-start | bytes 3145736 | tf_op jit(solution)/shard_map/ppermute | solution.py:44
  44.5 28.2 %collective-permute-start.12 = (bf16[2,1024,256]{2,1,0:T(8,128)(2,1)}, bf16[2,1024,256]{2,1,0:T(8,128)(2,1)S(1)}, u32[]{:S(2)}, u32[]{:S(2)}) collective-permute-start(bf16[2,1024,256]{2,1,0:T(8,128)(2,1)} %collective-permute-done.3), channel_id=1, source_target_pairs={{2,0},{3,1},{4,6},{5,7},{10,8},{11,9},{12,14},{13,15},{18,16},{19,... | collective-permute-start | bytes 3145736 | tf_op jit(solution)/shard_map/ppermute | solution.py:44
  45.8 27.1 %collective-permute-start.14 = (bf16[2,256,1024]{2,1,0:T(8,128)(2,1)}, bf16[2,256,1024]{2,1,0:T(8,128)(2,1)S(1)}, u32[]{:S(2)}, u32[]{:S(2)}) collective-permute-start(bf16[2,256,1024]{2,1,0:T(8,128)(2,1)} %copy-done.14), channel_id=1, source_target_pairs={{0,16},{1,9},{2,18},{3,11},{4,20},{5,13},{6,22},{7,15},{8,24},{9,1... | collective-permute-start | bytes 3145736 | tf_op jit(solution)/shard_map/ppermute | solution.py:44
  53.6 26.2 %collective-permute-start.22 = (bf16[2,256,1024]{2,1,0:T(8,128)(2,1)S(1)}, bf16[2,256,1024]{2,1,0:T(8,128)(2,1)S(1)}, u32[]{:S(2)}, u32[]{:S(2)}) collective-permute-start(bf16[2,256,1024]{2,1,0:T(8,128)(2,1)S(1)} %fusion), channel_id=1, source_target_pairs={{0,2},{1,3},{6,4},{7,5},{8,10},{9,11},{14,12},{15,13},{16,18},{17,... | collective-permute-start | bytes 3145736 | tf_op jit(solution)/shard_map/ppermute | solution.py:44
  59.1 2.8 %copy-start.1 = (bf16[384,8192]{1,0:T(8,128)(2,1)S(1)}, bf16[384,8192]{1,0:T(8,128)(2,1)}, u32[]{:S(2)}) copy-start(bf16[384,8192]{1,0:T(8,128)(2,1)} %refs_1_.6) | copy-start | bytes 18874372
  68.7 12.9 %copy-start.9 = (bf16[2,256,1024]{2,1,0:T(8,128)(2,1)}, bf16[2,256,1024]{2,1,0:T(8,128)(2,1)S(1)}, u32[]{:S(2)}) copy-start(bf16[2,256,1024]{2,1,0:T(8,128)(2,1)S(1)} %get-tuple-element.53) | copy-start | bytes 3145732
  68.7 11.1 %copy-start.8 = (bf16[2,256,1024]{2,1,0:T(8,128)(2,1)S(1)}, bf16[2,256,1024]{2,1,0:T(8,128)(2,1)}, u32[]{:S(2)}) copy-start(bf16[2,256,1024]{2,1,0:T(8,128)(2,1)} %copy-done.7) | copy-start | bytes 3145732
  68.7 18.2 %collective-permute-start.9 = (bf16[2,256,1024]{2,1,0:T(8,128)(2,1)S(1)}, bf16[2,256,1024]{2,1,0:T(8,128)(2,1)S(1)}, u32[]{:S(2)}, u32[]{:S(2)}) collective-permute-start(bf16[2,256,1024]{2,1,0:T(8,128)(2,1)S(1)} %get-tuple-element.45), channel_id=1, source_target_pairs={{0,16},{1,9},{2,18},{3,11},{4,20},{5,13},{6,22},{7,15},{8,24},{9,1... | collective-permute-start | bytes 3145736 | tf_op jit(solution)/shard_map/ppermute | solution.py:44
  69.3 34.9 %collective-permute-start.6 = (bf16[2,1024,256]{2,1,0:T(8,128)(2,1)S(1)}, bf16[2,1024,256]{2,1,0:T(8,128)(2,1)S(1)}, u32[]{:S(2)}, u32[]{:S(2)}) collective-permute-start(bf16[2,1024,256]{2,1,0:T(8,128)(2,1)S(1)} %collective-permute-done.5), channel_id=1, source_target_pairs={{2,0},{3,1},{4,6},{5,7},{10,8},{11,9},{12,14},{13,15},{18,16},{19,... | collective-permute-start | bytes 3145736 | tf_op jit(solution)/shard_map/ppermute | solution.py:44
  73.0 22.8 %copy-start.4 = (bf16[2,1024,256]{2,1,0:T(8,128)(2,1)S(1)}, bf16[2,1024,256]{2,1,0:T(8,128)(2,1)}, u32[]{:S(2)}) copy-start(bf16[2,1024,256]{2,1,0:T(8,128)(2,1)} %pad_maximum_fusion.refs_5_) | copy-start | bytes 3145732
  73.0 21.8 %collective-permute-start.15 = (bf16[2,256,1024]{2,1,0:T(8,128)(2,1)S(1)}, bf16[2,256,1024]{2,1,0:T(8,128)(2,1)S(1)}, u32[]{:S(2)}, u32[]{:S(2)}) collective-permute-start(bf16[2,256,1024]{2,1,0:T(8,128)(2,1)S(1)} %get-tuple-element.51), channel_id=1, source_target_pairs={{0,16},{1,9},{2,18},{3,11},{4,20},{5,13},{6,22},{7,15},{8,24},{9,1... | collective-permute-start | bytes 3145736 | tf_op jit(solution)/shard_map/ppermute | solution.py:44
  81.6 25.4 %collective-permute-start.23 = (bf16[2,256,1024]{2,1,0:T(8,128)(2,1)}, bf16[2,256,1024]{2,1,0:T(8,128)(2,1)}, u32[]{:S(2)}, u32[]{:S(2)}) collective-permute-start(bf16[2,256,1024]{2,1,0:T(8,128)(2,1)} %get-tuple-element.70), channel_id=1, source_target_pairs={{0,2},{1,3},{6,4},{7,5},{8,10},{9,11},{14,12},{15,13},{16,18},{17,... | collective-permute-start | bytes 3145736 | tf_op jit(solution)/shard_map/ppermute | solution.py:44
  86.9 8.4 %copy-start.17 = (bf16[2,256,1024]{2,1,0:T(8,128)(2,1)}, bf16[2,256,1024]{2,1,0:T(8,128)(2,1)S(1)}, u32[]{:S(2)}) copy-start(bf16[2,256,1024]{2,1,0:T(8,128)(2,1)S(1)} %collective-permute-done.9) | copy-start | bytes 3145732
  86.9 24.9 %collective-permute-start.10 = (bf16[2,1024,256]{2,1,0:T(8,128)(2,1)}, bf16[2,1024,256]{2,1,0:T(8,128)(2,1)S(1)}, u32[]{:S(2)}, u32[]{:S(2)}) collective-permute-start(bf16[2,1024,256]{2,1,0:T(8,128)(2,1)} %collective-permute-done.4.refs_5_), channel_id=1, source_target_pairs={{0,16},{1,9},{2,18},{3,11},{4,20},{5,13},{6,22},{7,15},{8,24},{9,1... | collective-permute-start | bytes 3145736 | tf_op jit(solution)/shard_map/ppermute | solution.py:44
  88.4 25.1 %collective-permute-start.25 = (bf16[2,256,1024]{2,1,0:T(8,128)(2,1)S(1)}, bf16[2,256,1024]{2,1,0:T(8,128)(2,1)S(1)}, u32[]{:S(2)}, u32[]{:S(2)}) collective-permute-start(bf16[2,256,1024]{2,1,0:T(8,128)(2,1)S(1)} %get-tuple-element.77), channel_id=1, source_target_pairs={{2,4},{3,5},{4,2},{5,3},{10,12},{11,13},{12,10},{13,11},{18,20},{1... | collective-permute-start | bytes 3145736 | tf_op jit(solution)/shard_map/ppermute | solution.py:44
  94.8 1.0 copy-start.15
  94.8 33.4 %collective-permute-start.16 = (bf16[2,1024,256]{2,1,0:T(8,128)(2,1)S(1)}, bf16[2,1024,256]{2,1,0:T(8,128)(2,1)S(1)}, u32[]{:S(2)}, u32[]{:S(2)}) collective-permute-start(bf16[2,1024,256]{2,1,0:T(8,128)(2,1)S(1)} %add.42.refs_5_), channel_id=1, source_target_pairs={{0,16},{1,9},{2,18},{3,11},{4,20},{5,13},{6,22},{7,15},{8,24},{9,1... | collective-permute-start | bytes 3145736 | tf_op jit(solution)/shard_map/ppermute | solution.py:44
  104.2 2.7 %copy-start.6 = (bf16[2,256,1024]{2,1,0:T(8,128)(2,1)S(1)}, bf16[2,256,1024]{2,1,0:T(8,128)(2,1)}, u32[]{:S(2)}) copy-start(bf16[2,256,1024]{2,1,0:T(8,128)(2,1)} %copy-done.5) | copy-start | bytes 3145732
  104.2 33.5 %collective-permute-start.17 = (bf16[384,1024]{1,0:T(8,128)(2,1)S(1)}, bf16[384,1024]{1,0:T(8,128)(2,1)S(1)}, u32[]{:S(2)}, u32[]{:S(2)}) collective-permute-start(bf16[384,1024]{1,0:T(8,128)(2,1)S(1)} %get-tuple-element.60), channel_id=1, source_target_pairs={{0,1},{1,0},{2,3},{3,2},{4,5},{5,4},{6,7},{7,6},{8,9},{9,8},{10,11... | collective-permute-start | bytes 2359304 | tf_op jit(solution)/shard_map/ppermute | solution.py:44
  106.9 6.6 %copy-start.18 = (bf16[2,256,1024]{2,1,0:T(8,128)(2,1)S(1)}, bf16[2,256,1024]{2,1,0:T(8,128)(2,1)}, u32[]{:S(2)}) copy-start(bf16[2,256,1024]{2,1,0:T(8,128)(2,1)} %copy-done.17) | copy-start | bytes 3145732
  110.2 47.8 %collective-permute-start.24 = (bf16[2,256,1024]{2,1,0:T(8,128)(2,1)}, bf16[2,256,1024]{2,1,0:T(8,128)(2,1)}, u32[]{:S(2)}, u32[]{:S(2)}) collective-permute-start(bf16[2,256,1024]{2,1,0:T(8,128)(2,1)} %add_convert_fusion.2), channel_id=1, source_target_pairs={{2,4},{3,5},{4,2},{5,3},{10,12},{11,13},{12,10},{13,11},{18,20},{1... | collective-permute-start | bytes 3145736 | tf_op jit(solution)/shard_map/ppermute | solution.py:44
  111.8 36.2 %collective-permute-start.11 = (bf16[2,1024,256]{2,1,0:T(8,128)(2,1)}, bf16[2,1024,256]{2,1,0:T(8,128)(2,1)}, u32[]{:S(2)}, u32[]{:S(2)}) collective-permute-start(bf16[2,1024,256]{2,1,0:T(8,128)(2,1)} %add.41.refs_5_), channel_id=1, source_target_pairs={{0,16},{1,9},{2,18},{3,11},{4,20},{5,13},{6,22},{7,15},{8,24},{9,1... | collective-permute-start | bytes 3145736 | tf_op jit(solution)/shard_map/ppermute | solution.py:44
  115.2 42.8 %collective-permute-start.26 = (bf16[2,256,1024]{2,1,0:T(8,128)(2,1)}, bf16[2,256,1024]{2,1,0:T(8,128)(2,1)}, u32[]{:S(2)}, u32[]{:S(2)}) collective-permute-start(bf16[2,256,1024]{2,1,0:T(8,128)(2,1)} %add_convert_fusion), channel_id=1, source_target_pairs={{0,2},{1,3},{2,0},{3,1},{4,6},{5,7},{6,4},{7,5},{8,10},{9,11},{10,... | collective-permute-start | bytes 3145736 | tf_op jit(solution)/shard_map/ppermute | solution.py:44
  137.7 2.3 %collective-permute-start.19 = (bf16[384,1024]{1,0:T(8,128)(2,1)S(1)}, bf16[384,1024]{1,0:T(8,128)(2,1)S(1)}, u32[]{:S(2)}, u32[]{:S(2)}) collective-permute-start(bf16[384,1024]{1,0:T(8,128)(2,1)S(1)} %get-tuple-element.62), channel_id=1, source_target_pairs={{0,1},{1,0},{2,3},{3,2},{4,5},{5,4},{6,7},{7,6},{8,9},{9,8},{10,11... | collective-permute-start | bytes 2359304 | tf_op jit(solution)/shard_map/ppermute | solution.py:44
  137.7 3.4 %copy-start.19 = (bf16[384,1024]{1,0:T(8,128)(2,1)}, bf16[384,1024]{1,0:T(8,128)(2,1)S(1)}, u32[]{:S(2)}) copy-start(bf16[384,1024]{1,0:T(8,128)(2,1)S(1)} %collective-permute-done.17.refs_1_) | copy-start | bytes 2359300
  137.7 3.4 %collective-permute-start.18 = (bf16[384,1024]{1,0:T(8,128)(2,1)S(1)}, bf16[384,1024]{1,0:T(8,128)(2,1)S(1)}, u32[]{:S(2)}, u32[]{:S(2)}) collective-permute-start(bf16[384,1024]{1,0:T(8,128)(2,1)S(1)} %get-tuple-element.61), channel_id=1, source_target_pairs={{0,1},{1,0},{2,3},{3,2},{4,5},{5,4},{6,7},{7,6},{8,9},{9,8},{10,11... | collective-permute-start | bytes 2359304 | tf_op jit(solution)/shard_map/ppermute | solution.py:44
  140.0 1.1 copy-start.20
  142.0 6.1 %copy-start.13 = (s32[3]{0:T(128)S(1)}, s32[3]{0:T(128)}, u32[]{:S(2)}) copy-start(s32[3]{0:T(128)} %pad_add_fusion.place.refs_0_) | copy-start | bytes 40
  148.1 9.9 %copy-start.10 = (bf16[2,256,1024]{2,1,0:T(8,128)(2,1)S(1)}, bf16[2,256,1024]{2,1,0:T(8,128)(2,1)}, u32[]{:S(2)}) copy-start(bf16[2,256,1024]{2,1,0:T(8,128)(2,1)} %copy-done.9) | copy-start | bytes 3145732
  148.1 9.9 %copy-start.16 = (bf16[2,256,1024]{2,1,0:T(8,128)(2,1)S(1)}, bf16[2,256,1024]{2,1,0:T(8,128)(2,1)}, u32[]{:S(2)}) copy-start(bf16[2,256,1024]{2,1,0:T(8,128)(2,1)} %copy-done.15) | copy-start | bytes 3145732
  157.8 16.6 %collective-permute-start.20 = (f32[384,1024]{1,0:T(8,128)}, f32[384,1024]{1,0:T(8,128)}, u32[]{:S(2)}, u32[]{:S(2)}) collective-permute-start(f32[384,1024]{1,0:T(8,128)} %get-tuple-element.65), channel_id=1, source_target_pairs={{0,1},{1,0},{2,3},{3,2},{4,5},{5,4},{6,7},{7,6},{8,9},{9,8},{10,11... | collective-permute-start | bytes 4718600 | tf_op jit(solution)/shard_map/ppermute | solution.py:44
  160.4 9.2 %collective-permute-start.27 = (bf16[256,1024]{1,0:T(8,128)(2,1)S(1)}, bf16[256,1024]{1,0:T(8,128)(2,1)S(1)}, u32[]{:S(2)}, u32[]{:S(2)}) collective-permute-start(bf16[256,1024]{1,0:T(8,128)(2,1)S(1)} %fusion.6), channel_id=1, source_target_pairs={{0,8},{1,17},{2,10},{3,19},{4,12},{5,21},{6,14},{7,23},{8,0},{9,25... | collective-permute-start | bytes 1572872 | tf_op jit(solution)/shard_map/ppermute | solution.py:44
  161.8 9.1 %collective-permute-start.21 = (bf16[384,1024]{1,0:T(8,128)(2,1)}, bf16[384,1024]{1,0:T(8,128)(2,1)S(1)}, u32[]{:S(2)}, u32[]{:S(2)}) collective-permute-start(bf16[384,1024]{1,0:T(8,128)(2,1)} %get-tuple-element.66), channel_id=1, source_target_pairs={{0,1},{1,0},{2,3},{3,2},{4,5},{5,4},{6,7},{7,6},{8,9},{9,8},{10,11... | collective-permute-start | bytes 2359304 | tf_op jit(solution)/shard_map/ppermute | solution.py:44
  (3 other events, 2.7 us)

commit v5 on v4

v5 whole, which is shorter than its diff:
```python
import math

import jax
import jax.numpy as jnp
from jax import lax
from jax.experimental import pallas as pl
from jax.experimental.pallas import tpu as pltpu
from jax.sharding import Mesh, PartitionSpec as P

F32, BF16 = jnp.float32, jnp.bfloat16
AXES = ("blk", "chip", "core")
SHRINK = 1000
VMEM = 60 * 2**20


def hops(move):
    pairs = []
    for blk in range(4):
        for z in range(4):
            for core in range(2):
                to = move(blk, z, core)
                if to is not None:
                    pairs.append(((blk * 4 + z) * 2 + core, (to[0] * 4 + to[1]) * 2 + to[2]))
    return pairs


def middle(z):
    return z in (1, 2)


SWAP = hops(lambda b, z, c: (b, z, 1 - c))
FLIP_A = hops(lambda b, z, c: (b ^ (1 + c), z, c))
FLIP_B = hops(lambda b, z, c: (b ^ (2 - c), z, c))
PAIR = hops(lambda b, z, c: (b, z ^ 1, c))
MID = hops(lambda b, z, c: (b, z ^ 3, c) if middle(z) else None)
OUT = hops(lambda b, z, c: (b, z ^ 1, c) if middle(z) else None)
IN = hops(lambda b, z, c: (b, z ^ 1, c) if not middle(z) else None)


def after(array, *others):
    return lax.optimization_barrier((array, *others))[0]


def sent(array, pairs):
    return lax.ppermute(array, AXES, pairs)


def column_block(place, a, b):
    core = place[1]
    return place[2] ^ (a * (1 + core)) ^ (b * (2 - core))


def cost(flops, moved, shrink=SHRINK):
    return pl.CostEstimate(flops=flops // shrink, bytes_accessed=moved // shrink, transcendentals=0)


def term_kernel(place, mine, other, cot_mine, cot_other, *refs):
    tokens, cols = cot_mine.shape[0], cot_mine.shape[1] // 4
    turned = refs[-1]
    step = pl.program_id(0)

    @pl.when((step == 0) & (pl.program_id(1) == 0))
    def _():
        for b in (0, 1):
            for a in (0, 1):
                at = pl.ds(pl.multiple_of(column_block(place, a, b) * cols, cols), cols)
                to = slice((2 * b + a) * cols, (2 * b + a + 1) * cols)
                turned[to, :tokens] = cot_mine[:, at].T
                turned[to, tokens:] = cot_other[:, at].T

    tall = jnp.concatenate([mine[...], other[...]], 0)
    for b in (0, 1):
        part = jnp.dot(
            turned[2 * b * cols : (2 * b + 2) * cols], tall, preferred_element_type=F32
        ).astype(BF16)
        for i in range(3):

            @pl.when((step >= 2) if i == 2 else (step == i))
            def _():
                out = refs[3 * b + i]
                out[...] = part.reshape(out.shape)


def terms(place, activations, other, cot_mine, cot_other, rows):
    tokens, columns = cot_mine.shape
    part, cols = rows // 2, columns // 4
    whole = pl.BlockSpec((tokens, columns), lambda i, r, s: (0, 0))
    mine = pl.BlockSpec((tokens, part), lambda i, r, s: (0, 2 * (2 * (s[0] ^ (3 - i)) + s[1]) + r))
    pieces = [
        pl.BlockSpec((2, cols, part), lambda i, r, s: (0, 0, jnp.where(i == 0, r, 1))),
        pl.BlockSpec(
            (2, cols, part), lambda i, r, s: (0, 0, jnp.where(i == 1, r, jnp.where(i == 0, 0, 1)))
        ),
        pl.BlockSpec(
            (1, 2, cols, part),
            lambda i, r, s: (jnp.where(i == 3, 0, 1), 0, 0, jnp.where(i < 2, 0, r)),
        ),
    ]
    return pl.pallas_call(
        term_kernel,
        grid_spec=pltpu.PrefetchScalarGridSpec(
            num_scalar_prefetch=1,
            grid=(4, 2),
            in_specs=[mine, mine, whole, whole],
            out_specs=pieces * 2,
            scratch_shapes=[pltpu.VMEM((columns, 2 * tokens), BF16)],
        ),
        out_shape=[
            jax.ShapeDtypeStruct((2, cols, rows), BF16),
            jax.ShapeDtypeStruct((2, cols, rows), BF16),
            jax.ShapeDtypeStruct((2, 2, cols, rows), BF16),
        ]
        * 2,
        compiler_params=pltpu.CompilerParams(vmem_limit_bytes=VMEM),
        cost_estimate=cost(16 * tokens * rows * columns, 16 * tokens * rows + 16 * rows * columns),
        name="terms",
    )(place, activations, other, cot_mine, cot_other)


def project_kernel(place, *refs, count, first, last):
    acts, other, cot_mine, cot_other = refs[:4]
    pieces = refs[4 : 4 + 2 * count]
    at_out = 4 + 2 * count + (0 if first else 2)
    near, far, *keys = refs[at_out:-2]
    acc, cots = refs[-2:]
    tokens, cols = cot_mine.shape[0], cot_mine.shape[1] // 4
    group, tile = pl.program_id(0), pl.program_id(1)
    blocks = [
        (
            slice((2 * b + a) * cols, (2 * b + a + 1) * cols),
            pl.ds(pl.multiple_of(column_block(place, a, b) * cols, cols), cols),
        )
        for b in (0, 1)
        for a in (0, 1)
    ]

    @pl.when((group == 0) & (tile == 0))
    def _():
        for to, at in blocks:
            cots[:tokens, to] = cot_mine[:, at]
            cots[tokens:, to] = cot_other[:, at]

    for n in range(count):

        @pl.when(group == n)
        def _():
            here, there = pieces[2 * n], pieces[2 * n + 1]
            weight = jnp.concatenate([here[0], here[1], there[0], there[1]], 1)
            total = lax.dot_general(
                cots[...], weight, (((1,), (1,)), ((), ())), preferred_element_type=F32
            ).astype(BF16)
            near[...] = total[:tokens]
            far[...] = total[tokens:]
            tall = jnp.concatenate([acts[...], other[...]], 0)
            sums = jnp.dot(tall, weight, preferred_element_type=F32)
            if n > 0:
                acc[...] += sums
            else:

                @pl.when(tile == 0)
                def _():
                    acc[...] = sums if first else refs[4 + 2 * count][...] + sums

                @pl.when(tile > 0)
                def _():
                    acc[...] += sums

    @pl.when((group == count - 1) & (tile == pl.num_programs(1) - 1))
    def _():
        if last:
            for to, at in blocks:
                keys[0][:, at] = acc[:tokens, to]
                keys[1][:, at] = acc[tokens:, to]
        else:
            keys[0][...] = acc[...]


def projected(place, start, activations, other, cot_mine, cot_other, pieces, so_far=None):
    tokens, columns = cot_mine.shape
    _, rows, cols = pieces[0].shape
    part, count = rows // 2, len(pieces) // 2
    first, last = so_far is None, start + count == 4
    whole = pl.BlockSpec((tokens, columns), lambda i, r, s: (0, 0))
    both = pl.BlockSpec((2 * tokens, columns), lambda i, r, s: (0, 0))
    mine = pl.BlockSpec(
        (tokens, part), lambda i, r, s: (0, 2 * (2 * (s[0] ^ (start + i)) + s[1]) + r)
    )
    held = [
        pl.BlockSpec((2, part, cols), lambda i, r, s, n=n: (0, jnp.clip(2 * (i - n) + r, 0, 1), 0))
        for n in range(count)
        for _ in range(2)
    ]
    one = jax.ShapeDtypeStruct((tokens, columns), F32)
    return pl.pallas_call(
        lambda *refs: project_kernel(*refs, count=count, first=first, last=last),
        grid_spec=pltpu.PrefetchScalarGridSpec(
            num_scalar_prefetch=1,
            grid=(count, 2),
            in_specs=[mine, mine, whole, whole, *held]
            + ([] if first else [both, pl.BlockSpec(memory_space=pl.ANY)]),
            out_specs=[mine, pl.BlockSpec((tokens, part), lambda i, r, s: (0, 2 * i + r))]
            + ([whole, whole] if last else [both]),
            scratch_shapes=[
                pltpu.VMEM((2 * tokens, columns), F32),
                pltpu.VMEM((2 * tokens, columns), BF16),
            ],
        ),
        out_shape=[
            jax.ShapeDtypeStruct(activations.shape, BF16),
            jax.ShapeDtypeStruct((tokens, count * rows), BF16),
        ]
        + ([one, one] if last else [jax.ShapeDtypeStruct((2 * tokens, columns), F32)]),
        input_output_aliases={} if first else {6 + 2 * count: 0},
        compiler_params=pltpu.CompilerParams(vmem_limit_bytes=VMEM),
        cost_estimate=cost(
            8 * tokens * rows * columns * count,
            (8 * tokens * rows + 2 * rows * columns) * count + 8 * tokens * columns,
            1 if last else SHRINK,
        ),
        name="project",
    )(
        place, activations, other, cot_mine, cot_other, *pieces,
        *([] if first else [so_far[2], so_far[0]]),
    )


def lay_kernel(place, *refs, rows):
    parts, out, sems = refs[:-3], refs[-2], refs[-1]
    copies, k = [], 0
    for part in parts:
        for i in range(part.shape[1] // rows):
            at = pl.multiple_of((2 * (place[0] ^ k) + 1 - place[1]) * rows, rows)
            copies.append(
                pltpu.make_async_copy(
                    part.at[:, i * rows : (i + 1) * rows], out.at[:, pl.ds(at, rows)], sems.at[k]
                )
            )
            k += 1
    for copy in copies:
        copy.start()
    for copy in copies:
        copy.wait()


def laid(place, whole, parts, rows):
    return pl.pallas_call(
        lambda *refs: lay_kernel(*refs, rows=rows),
        in_specs=[pl.BlockSpec(memory_space=pltpu.SMEM)]
        + [pl.BlockSpec(memory_space=pl.ANY)] * (len(parts) + 1),
        out_specs=pl.BlockSpec(memory_space=pl.ANY),
        out_shape=jax.ShapeDtypeStruct(whole.shape, BF16),
        scratch_shapes=[pltpu.SemaphoreType.DMA((4,))],
        input_output_aliases={1 + len(parts): 0},
        compiler_params=pltpu.CompilerParams(vmem_limit_bytes=VMEM),
        cost_estimate=cost(0, 2 * whole.size),
        name="lay",
    )(place, *parts, whole)


def added(*arrays):
    total = arrays[0].astype(F32)
    for array in arrays[1:]:
        total = total + array.astype(F32)
    return total.astype(BF16)


def by_hops(activations, cotangent, kv_weight):
    rows = kv_weight.shape[0]
    tokens = activations.shape[0]
    place = jnp.stack([lax.axis_index(name) for name in ("chip", "core", "blk")]).astype(jnp.int32)

    other = sent(activations, SWAP)
    base = jnp.stack([kv_weight, sent(kv_weight, FLIP_A)])
    cot_other = sent(after(cotangent, base), SWAP)
    shared = (activations, other, cotangent, cot_other)
    one, mid = sent(base, PAIR), sent(base, MID)
    base_b = sent(base, FLIP_B)

    keep3, keep2, keep10, send3, send2, send10 = terms(
        place, after(activations, base), *shared[1:], rows
    )
    got3 = sent(send3, FLIP_B)
    got2 = sent(after(send2, base_b), FLIP_B)
    got10 = sent(after(send10, got3), FLIP_B)
    so_far = projected(place, 0, after(activations, keep10), *shared[1:], (base, base_b))
    out0 = sent(so_far[1], SWAP)

    sum3 = added(after(keep3, so_far[1]), got3)
    far = sent(after(sum3, one, mid), IN)
    two_mid = sent(one, MID)
    two_end = sent(mid, OUT)
    sum2 = added(keep2, got2)
    two = two_mid + two_end
    near = sent(after(sum2, far, two), IN)
    mid_far = sent(added(sum2, far), MID)
    three_end = sent(two_mid, OUT)
    one_b = sent(after(one, got2), FLIP_B)
    two_b = sent(after(two, got10), FLIP_B)

    three = mid + three_end
    three_b = sent(after(three, one_b), FLIP_B)
    sum_mid = sent(added(sum3, after(near, three)), MID)
    sum_one = sent(added(keep10[1], got10[1], mid_far), PAIR)
    so_far = projected(
        place, 1, after(activations, out0), *shared[1:], (one, one_b, two, two_b), so_far
    )
    out12 = sent(so_far[1], SWAP)
    last = [
        keep10[0, a].astype(F32)
        + got10[0, a].astype(F32)
        + sum_mid[a].astype(F32)
        + sum_one[a].astype(F32)
        for a in (0, 1)
    ]
    over = last[1].astype(BF16)
    final = last[0] + sent(over, FLIP_A).astype(F32)
    grad_weight = (final * (1.0 / math.sqrt(32 * tokens))).astype(BF16).T

    whole, out3, keys, keys_far = projected(
        place, 3, after(activations, over), *shared[1:], (three, three_b), so_far
    )
    grad_input = laid(place, whole, (out0, out12, sent(out3, SWAP)), rows)
    key_values = (keys + sent(keys_far, SWAP)).astype(BF16)
    return (key_values, grad_input, grad_weight)


def swapped(array):
    return lax.ppermute(array, "core", [(0, 1), (1, 0)])


def by_collectives(activations, cotangent, kv_weight):
    blocks, chips = lax.axis_size("blk"), lax.axis_size("chip")
    core = lax.axis_index("core")
    tokens, features = activations.shape
    rows, cols = kv_weight.shape
    columns = cotangent.shape[1]
    by_core = activations.reshape(tokens, chips, 2, rows)
    mine = lax.dynamic_index_in_dim(by_core, core, 2, keepdims=False)
    other = lax.dynamic_index_in_dim(by_core, 1 - core, 2, keepdims=False)
    acts = jnp.concatenate([mine, swapped(other)], 0)
    cots = jnp.concatenate([cotangent, swapped(cotangent)], 0)
    weight = lax.all_gather(kv_weight, ("blk", "chip"), axis=0, tiled=False)
    weight = weight.reshape(blocks, chips, rows, cols)
    parts = jnp.einsum(
        "tzr,tbc->bzrc", acts, cots.reshape(2 * tokens, blocks, cols), preferred_element_type=F32
    ).astype(BF16).reshape(blocks * chips, rows, cols)
    total = lax.psum_scatter(parts, ("blk", "chip"), scatter_dimension=0, tiled=False)
    count = tokens * blocks * chips * 2
    grad_weight = (total.astype(F32) * (1.0 / math.sqrt(count))).astype(BF16)
    full = weight.transpose(1, 2, 0, 3).reshape(chips * rows, columns)
    keys = jnp.dot(acts.reshape(2 * tokens, chips * rows), full, preferred_element_type=F32)
    key_values = (keys[:tokens] + swapped(keys[tokens:])).astype(BF16)
    inputs = lax.dot_general(
        cots, full, (((1,), (1,)), ((), ())), preferred_element_type=F32
    ).astype(BF16).reshape(2 * tokens, chips, rows)
    near, far = inputs[:tokens], swapped(inputs[tokens:])
    low = jnp.where(core == 0, near, far)
    high = jnp.where(core == 0, far, near)
    grad_input = jnp.stack([low, high], 2).reshape(tokens, features)
    return (key_values, grad_input, grad_weight)


def solution(mesh):
    blocks, shards = mesh.shape["blk"], mesh.shape["shard"]
    split = Mesh(mesh.devices.reshape(blocks, shards // 2, 2), AXES)
    by_token = P(AXES, None)
    by_piece = P(("chip", "core"), "blk")
    return jax.shard_map(
        by_hops if (blocks, shards) == (4, 8) else by_collectives,
        mesh=split,
        in_specs=(by_token, by_token, by_piece),
        out_specs=(by_token, by_token, by_piece),
        check_vma=False,
    )
```

time: 178 us -> 280 us (1.57)
  Pallas kernels: 68.7 us -> 147 us
  waiting for transfers between devices: 36.6 us -> 67.9 us
  local copies, waits for them, and re-layouts: 11.9 us -> 6.12 us
  other arithmetic: 19.2 us -> 14.5 us
    pallas_call x8 -> x4, Pallas kernels: 54.4 us -> 132 us  [the longest x1 97.1 us: laid(): pl.pallas_call(lambda *refs: lay_kernel(*refs, rows=rows), in_specs=[pl.B...]
    ppermute x28 -> x25, waiting for transfers between devices: 36.6 us -> 67.9 us  [sent(): return lax.ppermute(array, AXES, pairs)]
    unnamed x47 -> x39, local copies, waits for them, and re-layouts: 11.8 us -> 6.12 us
    convert_element_type x4 -> x5, other arithmetic: 8.48 us -> 4.89 us  [the longest x4 3.48 us: added(): return total.astype(BF16)]
    ppermute x28 -> x25, starting transfers between devices: 39.5 us -> 41.4 us  [sent(): return lax.ppermute(array, AXES, pairs)]
    pallas_call x2 -> x1, Pallas kernels: 14.3 us -> 15.4 us  [terms(): pl.pallas_call(term_kernel, grid_spec=pltpu.PrefetchScalarGridSpec(num_sc...]
  transfers between devices with their start and end apart: 28 -> 25, of which waited for: 9 -> 8; matrix products, arithmetic and copies ran while one was open for 9% -> 6% of each run, Pallas kernels for 36% -> 14%
where the time goes in v5:
time: 280 us; the launch traced here: 279 us
  Pallas kernels  147 us (52%)
  waiting for transfers between devices  67.9 us (24%)
  starting transfers between devices  41.4 us (15%)
  other arithmetic  14.5 us (5%)
  local copies, waits for them, and re-layouts  6.12 us (2%)
    pallas_call x1, Pallas kernels, laid(): pl.pallas_call(lambda *refs: lay_kernel(*refs, rows=rows), in_specs=[pl.B...  97.1 us
    ppermute x25, waiting for transfers between devices, sent(): return lax.ppermute(array, AXES, pairs)  67.9 us
    ppermute x25, starting transfers between devices, sent(): return lax.ppermute(array, AXES, pairs)  41.4 us
    pallas_call x3, Pallas kernels, projected(): pl.pallas_call(lambda *refs: project_kernel(*refs, count=count, first=fir...  34.9 us
    pallas_call x1, Pallas kernels, terms(): pl.pallas_call(term_kernel, grid_spec=pltpu.PrefetchScalarGridSpec(num_sc...  15.4 us
    unnamed x39, local copies, waits for them, and re-layouts  6.12 us
  transfers between devices with their start and end apart: 25, of which 8 were waited for; matrix products, arithmetic and copies ran while one was open for 6% of the time, Pallas kernels for 14%

profile of v5, /device:TPU:0, one launch (start us, length us, event | category | flops | bytes accessed | tf_op | source)
XLA Modules:
  0.0 278.6 jit_solution(6579722272570804275)
XLA Ops:
  0.6 0.5 collective-permute-start.1
  1.2 2.6 collective-permute-start
  3.7 7.4 %collective-permute-done = bf16[1024,256]{1,0:T(8,128)(2,1)S(1)} collective-permute-done((bf16[1024,256]{1,0:T(8,128)(2,1)}, bf16[1024,256]{1,0:T(8,128)(2,1)S(1)}, u32[]{:S(2)}, u32[]{:S(2)}) %collective-permute-start) | collective-permute-done | bytes 524320 | tf_op jit(solution)/shard_map/ppermute | solution.py:45
  11.1 1.1 pad_maximum_fusion.refs_5_
  12.3 2.2 collective-permute-start.7
  14.5 1.7 collective-permute-start.8
  16.2 0.6 pad_add_fusion.place.refs_0_
  16.9 1.5 collective-permute-start.5
  18.4 0.9 copy-done.1
  19.3 15.4 %terms.1 = (bf16[2,256,1024]{2,1,0:T(8,128)(2,1)}, bf16[2,256,1024]{2,1,0:T(8,128)(2,1)}, bf16[2,2,256,1024]{3,2,1,0:T(8,128)(2,1)}, bf16[2,256,1024]{2,1,0:T(8,...) custom-call(s32[3]{0:T(128)} %pad_add_fusion.place.refs_0_, bf16[384,8192]{1,0:T(8,128)(2,1)} %refs_1_.2, ...), custom_call_target="tpu_custom_call" | custom-call | flops 6442450 | bytes 23068 | tf_op jit(solution)/shard_map/terms/pallas_call | solution.py:99
  34.7 0.6 collective-permute-start.3
  35.3 3.1 %collective-permute-done.7.refs_5_ = bf16[2,1024,256]{2,1,0:T(8,128)(2,1)} collective-permute-done((bf16[2,1024,256]{2,1,0:T(8,128)(2,1)S(1)}, bf16[2,1024,256]{2,1,0:T(8,128)(2,1)}, u32[]{:S(2)}, u32[]{:S(2)}) %collective-permute-start.7) | collective-permute-done | bytes 1048608 | tf_op jit(solution)/shard_map/ppermute | solution.py:45
  38.4 0.7 collective-permute-start.10
  39.1 1.3 collective-permute-start.11
  40.4 9.3 %project.3 = (bf16[384,8192]{1,0:T(8,128)(2,1)}, bf16[384,1024]{1,0:T(8,128)(2,1)}, f32[768,1024]{1,0:T(8,128)}) custom-call(s32[3]{0:T(128)} %pad_add_fusion.place.refs_0_, bf16[384,8192]{1,0:T(8,128)(2,1)} %refs_1_.2, bf16[384,8192]{1,0:T(8,128)(2,1)} %collective-permute-done.1.other.refs_2_, bf16[384,1024]{1,0:T(8,128)(2,1)} %refs_3_.5, ...), custom_call_target="tpu_custom_call" | custom-call | flops 3221225 | bytes 8388 | tf_op jit(solution)/shard_map/project/pallas_call | solution.py:194
  49.8 1.8 collective-permute-start.6
  51.6 1.6 add_convert_fusion.3
  53.2 7.4 %collective-permute-start.9 = (bf16[2,256,1024]{2,1,0:T(8,128)(2,1)S(1)}, bf16[2,256,1024]{2,1,0:T(8,128)(2,1)S(1)}, u32[]{:S(2)}, u32[]{:S(2)}) collective-permute-start(bf16[2,256,1024]{2,1,0:T(8,128)(2,1)S(1)} %add_convert_fusion.3), channel_id=1, source_target_pairs={{0,2},{1,3},{6,4},{7,5},{8,10},{9,11},{14,12},{15,13},{16,18},{17,... | collective-permute-start | bytes 3145736 | tf_op jit(solution)/shard_map/ppermute | solution.py:45
  60.6 0.6 collective-permute-start.4
  61.2 1.3 collective-permute-start.13
  62.5 5.4 %collective-permute-done.11 = bf16[2,1024,256]{2,1,0:T(8,128)(2,1)} collective-permute-done((bf16[2,1024,256]{2,1,0:T(8,128)(2,1)}, bf16[2,1024,256]{2,1,0:T(8,128)(2,1)}, u32[]{:S(2)}, u32[]{:S(2)}) %collective-permute-start.11) | collective-permute-done | bytes 1048608 | tf_op jit(solution)/shard_map/ppermute | solution.py:45
  67.9 1.5 add.61.refs_7_
  69.4 12.7 %collective-permute-done.9 = bf16[2,256,1024]{2,1,0:T(8,128)(2,1)S(1)} collective-permute-done((bf16[2,256,1024]{2,1,0:T(8,128)(2,1)S(1)}, bf16[2,256,1024]{2,1,0:T(8,128)(2,1)S(1)}, u32[]{:S(2)}, u32[]{:S(2)}) %collective-permute-start.9) | collective-permute-done | bytes 1048608 | tf_op jit(solution)/shard_map/ppermute | solution.py:45
  82.2 0.8 add_convert_fusion
  83.0 4.5 %collective-permute-start.12 = (bf16[2,256,1024]{2,1,0:T(8,128)(2,1)S(1)}, bf16[2,256,1024]{2,1,0:T(8,128)(2,1)S(1)}, u32[]{:S(2)}, u32[]{:S(2)}) collective-permute-start(bf16[2,256,1024]{2,1,0:T(8,128)(2,1)S(1)} %get-tuple-element.47), channel_id=1, source_target_pairs={{0,2},{1,3},{6,4},{7,5},{8,10},{9,11},{14,12},{15,13},{16,18},{17,... | collective-permute-start | bytes 3145736 | tf_op jit(solution)/shard_map/ppermute | solution.py:45
  87.4 0.7 collective-permute-start.15
  88.2 1.6 collective-permute-start.17
  89.7 0.5 collective-permute-done.13
  90.3 1.5 add.62.refs_5_
  91.8 16.2 %collective-permute-done.12 = bf16[2,256,1024]{2,1,0:T(8,128)(2,1)S(1)} collective-permute-done((bf16[2,256,1024]{2,1,0:T(8,128)(2,1)S(1)}, bf16[2,256,1024]{2,1,0:T(8,128)(2,1)S(1)}, u32[]{:S(2)}, u32[]{:S(2)}) %collective-permute-start.12) | collective-permute-done | bytes 1048608 | tf_op jit(solution)/shard_map/ppermute | solution.py:45
  108.5 1.0 collective-permute-start.14
  109.6 0.7 fusion
  110.3 4.9 %collective-permute-start.16 = (bf16[2,256,1024]{2,1,0:T(8,128)(2,1)S(1)}, bf16[2,256,1024]{2,1,0:T(8,128)(2,1)}, u32[]{:S(2)}, u32[]{:S(2)}) collective-permute-start(bf16[2,256,1024]{2,1,0:T(8,128)(2,1)S(1)} %fusion), channel_id=1, source_target_pairs={{0,2},{1,3},{2,0},{3,1},{4,6},{5,7},{6,4},{7,5},{8,10},{9,11},{10,... | collective-permute-start | bytes 3145736 | tf_op jit(solution)/shard_map/ppermute | solution.py:45
  115.2 2.6 collective-permute-start.20
  117.9 1.0 copy-done.15
  118.9 16.6 %collective-permute-done.16 = bf16[2,256,1024]{2,1,0:T(8,128)(2,1)} collective-permute-done((bf16[2,256,1024]{2,1,0:T(8,128)(2,1)S(1)}, bf16[2,256,1024]{2,1,0:T(8,128)(2,1)}, u32[]{:S(2)}, u32[]{:S(2)}) %collective-permute-start.16) | collective-permute-done | bytes 1048608 | tf_op jit(solution)/shard_map/ppermute | solution.py:45
  135.5 1.4 fusion.4
  136.9 1.0 copy-done.12
  138.0 14.8 %project.4 = (bf16[384,8192]{1,0:T(8,128)(2,1)}, bf16[384,2048]{1,0:T(8,128)(2,1)}, f32[768,1024]{1,0:T(8,128)}) custom-call(s32[3]{0:T(128)} %pad_add_fusion.place.refs_0_, bf16[384,8192]{1,0:T(8,128)(2,1)} %refs_1_.2, bf16[384,8192]{1,0:T(8,128)(2,1)} %collective-permute-done.1.other.refs_2_, ...), custom_call_target="tpu_custom_call", output_to_operand_aliasing={{0}: (10, {})} | custom-call | flops 6442450 | bytes 13631 | tf_op jit(solution)/shard_map/project/pallas_call | solution.py:194
  152.8 1.0 copy-done.11
  153.8 10.7 %project.5 = (bf16[384,8192]{1,0:T(8,128)(2,1)}, bf16[384,1024]{1,0:T(8,128)(2,1)}, f32[384,1024]{1,0:T(8,128)}, f32[384,1024]{1,0:T(8,128)}) custom-call(s32[3]{0:T(128)} %pad_add_fusion.place.refs_0_, bf16[384,8192]{1,0:T(8,128)(2,1)} %refs_1_.2, bf16[384,8192]{1,0:T(8,128)(2,1)} %collective-permute-done.1.other.refs_2_, ...), custom_call_target="tpu_custom_call", output_to_operand_aliasing={{0}: (8, {})} | custom-call | flops 3221225472 | bytes 8388608 | tf_op jit(solution)/shard_map/project/pallas_call | solution.py:194
  165.1 3.2 %collective-permute-start.23 = (bf16[384,1024]{1,0:T(8,128)(2,1)}, bf16[384,1024]{1,0:T(8,128)(2,1)}, u32[]{:S(2)}, u32[]{:S(2)}) collective-permute-start(bf16[384,1024]{1,0:T(8,128)(2,1)} %get-tuple-element.61), channel_id=1, source_target_pairs={{0,1},{1,0},{2,3},{3,2},{4,5},{5,4},{6,7},{7,6},{8,9},{9,8},{10,11... | collective-permute-start | bytes 2359304 | tf_op jit(solution)/shard_map/ppermute | solution.py:45
  168.4 5.9 %collective-permute-done.24 = bf16[256,1024]{1,0:T(8,128)(2,1)S(1)} collective-permute-done((bf16[256,1024]{1,0:T(8,128)(2,1)S(1)}, bf16[256,1024]{1,0:T(8,128)(2,1)S(1)}, u32[]{:S(2)}, u32[]{:S(2)}) %collective-permute-start.24) | collective-permute-done | bytes 524320 | tf_op jit(solution)/shard_map/ppermute | solution.py:45
  174.3 1.8 fusion.5
  176.1 1.0 copy.9
  177.1 3.0 %add_convert_fusion.4 = bf16[384,1024]{1,0:T(8,128)(2,1)} fusion(f32[384,1024]{1,0:T(8,128)} %get-tuple-element.58, f32[384,1024]{1,0:T(8,128)} %collective-permute-done.21), kind=kLoop, calls=%fused_computation.6 | loop fusion | flops 786432 | bytes 3932160 | tf_op jit(solution)/shard_map/convert_element_type | solution.py:323
  180.1 1.2 copy-done.7
  181.3 97.1 %lay.1 = bf16[384,8192]{1,0:T(8,128)(2,1)} custom-call(s32[3]{0:T(128)} %pad_add_fusion.place.refs_0_, bf16[384,1024]{1,0:T(8,128)(2,1)} %copy-done.15, bf16[384,2048]{1,0:T(8,128)(2,1)} %copy-done.7, bf16[384,1024]{1,0:T(8,128)(2,1)} %collective-permute-done.23.refs_3_, bf16[384,8192]{1,0:T(8,128)(2,1)} %get-tuple-element.62.refs_4_), custom_call_target="tpu_custom_call", output_to_operand_aliasing={{}: (4, {})} | custom-call | bytes 6291 | tf_op jit(solution)/shard_map/lay/pallas_call | solution.py:246
  (57 shorter events, 1.3 us)
Async XLA Ops:
  0.6 11.6 %copy-start = (bf16[384,1024]{1,0:T(8,128)(2,1)S(1)}, bf16[384,1024]{1,0:T(8,128)(2,1)}, u32[]{:S(2)}) copy-start(bf16[384,1024]{1,0:T(8,128)(2,1)} %refs_3_.5) | copy-start | bytes 2359300
  0.6 17.7 %collective-permute-start.1 = (bf16[384,8192]{1,0:T(8,128)(2,1)}, bf16[384,8192]{1,0:T(8,128)(2,1)}, u32[]{:S(2)}, u32[]{:S(2)}) collective-permute-start(bf16[384,8192]{1,0:T(8,128)(2,1)} %refs_1_.2), channel_id=1, source_target_pairs={{0,1},{1,0},{2,3},{3,2},{4,5},{5,4},{6,7},{7,6},{8,9},{9,8},{10,11... | collective-permute-start | bytes 18874376 | tf_op jit(solution)/shard_map/ppermute | solution.py:45
  1.2 9.9 %collective-permute-start = (bf16[1024,256]{1,0:T(8,128)(2,1)}, bf16[1024,256]{1,0:T(8,128)(2,1)S(1)}, u32[]{:S(2)}, u32[]{:S(2)}) collective-permute-start(bf16[1024,256]{1,0:T(8,128)(2,1)} %param.5), channel_id=1, source_target_pairs={{0,8},{1,17},{2,10},{3,19},{4,12},{5,21},{6,14},{7,23},{8,0},{9,25... | collective-permute-start | bytes 1572872 | tf_op jit(solution)/shard_map/ppermute | solution.py:45
  12.3 22.5 %copy-start.4 = (bf16[2,1024,256]{2,1,0:T(8,128)(2,1)}, bf16[2,1024,256]{2,1,0:T(8,128)(2,1)S(1)}, u32[]{:S(2)}) copy-start(bf16[2,1024,256]{2,1,0:T(8,128)(2,1)S(1)} %pad_maximum_fusion.refs_5_) | copy-start | bytes 3145732
  12.3 6.1 %collective-permute-start.2 = (bf16[384,1024]{1,0:T(8,128)(2,1)S(1)}, bf16[384,1024]{1,0:T(8,128)(2,1)S(1)}, u32[]{:S(2)}, u32[]{:S(2)}) collective-permute-start(bf16[384,1024]{1,0:T(8,128)(2,1)S(1)} %copy-done), channel_id=1, source_target_pairs={{0,1},{1,0},{2,3},{3,2},{4,5},{5,4},{6,7},{7,6},{8,9},{9,8},{10,11... | collective-permute-start | bytes 2359304 | tf_op jit(solution)/shard_map/ppermute | solution.py:45
  12.3 26.0 %collective-permute-start.7 = (bf16[2,1024,256]{2,1,0:T(8,128)(2,1)S(1)}, bf16[2,1024,256]{2,1,0:T(8,128)(2,1)}, u32[]{:S(2)}, u32[]{:S(2)}) collective-permute-start(bf16[2,1024,256]{2,1,0:T(8,128)(2,1)S(1)} %pad_maximum_fusion.refs_5_), channel_id=1, source_target_pairs={{0,2},{1,3},{2,0},{3,1},{4,6},{5,7},{6,4},{7,5},{8,10},{9,11},{10,... | collective-permute-start | bytes 3145736 | tf_op jit(solution)/shard_map/ppermute | solution.py:45
  14.5 24.6 %collective-permute-start.8 = (bf16[2,1024,256]{2,1,0:T(8,128)(2,1)S(1)}, bf16[2,1024,256]{2,1,0:T(8,128)(2,1)}, u32[]{:S(2)}, u32[]{:S(2)}) collective-permute-start(bf16[2,1024,256]{2,1,0:T(8,128)(2,1)S(1)} %pad_maximum_fusion.refs_5_), channel_id=1, source_target_pairs={{2,4},{3,5},{4,2},{5,3},{10,12},{11,13},{12,10},{13,11},{18,20},{1... | collective-permute-start | bytes 3145736 | tf_op jit(solution)/shard_map/ppermute | solution.py:45
  16.9 23.6 %collective-permute-start.5 = (bf16[2,1024,256]{2,1,0:T(8,128)(2,1)S(1)}, bf16[2,1024,256]{2,1,0:T(8,128)(2,1)}, u32[]{:S(2)}, u32[]{:S(2)}) collective-permute-start(bf16[2,1024,256]{2,1,0:T(8,128)(2,1)S(1)} %pad_maximum_fusion.refs_5_), channel_id=1, source_target_pairs={{0,16},{1,9},{2,18},{3,11},{4,20},{5,13},{6,22},{7,15},{8,24},{9,1... | collective-permute-start | bytes 3145736 | tf_op jit(solution)/shard_map/ppermute | solution.py:45
  18.4 0.9 copy-start.1
  34.7 16.8 %collective-permute-start.3 = (bf16[2,256,1024]{2,1,0:T(8,128)(2,1)}, bf16[2,256,1024]{2,1,0:T(8,128)(2,1)}, u32[]{:S(2)}, u32[]{:S(2)}) collective-permute-start(bf16[2,256,1024]{2,1,0:T(8,128)(2,1)} %get-tuple-element.37), channel_id=1, source_target_pairs={{0,16},{1,9},{2,18},{3,11},{4,20},{5,13},{6,22},{7,15},{8,24},{9,1... | collective-permute-start | bytes 3145736 | tf_op jit(solution)/shard_map/ppermute | solution.py:45
  38.4 22.9 %collective-permute-start.10 = (bf16[2,1024,256]{2,1,0:T(8,128)(2,1)}, bf16[2,1024,256]{2,1,0:T(8,128)(2,1)S(1)}, u32[]{:S(2)}, u32[]{:S(2)}) collective-permute-start(bf16[2,1024,256]{2,1,0:T(8,128)(2,1)} %collective-permute-done.7.refs_5_), channel_id=1, source_target_pairs={{2,4},{3,5},{4,2},{5,3},{10,12},{11,13},{12,10},{13,11},{18,20},{1... | collective-permute-start | bytes 3145736 | tf_op jit(solution)/shard_map/ppermute | solution.py:45
  39.1 28.8 %collective-permute-start.11 = (bf16[2,1024,256]{2,1,0:T(8,128)(2,1)}, bf16[2,1024,256]{2,1,0:T(8,128)(2,1)}, u32[]{:S(2)}, u32[]{:S(2)}) collective-permute-start(bf16[2,1024,256]{2,1,0:T(8,128)(2,1)} %collective-permute-done.8), channel_id=1, source_target_pairs={{2,0},{3,1},{4,6},{5,7},{10,8},{11,9},{12,14},{13,15},{18,16},{19,... | collective-permute-start | bytes 3145736 | tf_op jit(solution)/shard_map/ppermute | solution.py:45
  40.4 11.2 %copy-start.10 = (bf16[2,256,1024]{2,1,0:T(8,128)(2,1)S(1)}, bf16[2,256,1024]{2,1,0:T(8,128)(2,1)}, u32[]{:S(2)}) copy-start(bf16[2,256,1024]{2,1,0:T(8,128)(2,1)} %get-tuple-element.42) | copy-start | bytes 3145732
  40.4 9.4 %copy-start.17 = (bf16[2,256,1024]{2,1,0:T(8,128)(2,1)S(1)}, bf16[2,256,1024]{2,1,0:T(8,128)(2,1)}, u32[]{:S(2)}) copy-start(bf16[2,256,1024]{2,1,0:T(8,128)(2,1)} %get-tuple-element.45) | copy-start | bytes 3145732
  49.8 10.8 %copy-start.16 = (bf16[2,2,256,1024]{3,2,1,0:T(8,128)(2,1)S(1)}, bf16[2,2,256,1024]{3,2,1,0:T(8,128)(2,1)}, u32[]{:S(2)}) copy-start(bf16[2,2,256,1024]{3,2,1,0:T(8,128)(2,1)} %get-tuple-element.38) | copy-start | bytes 6291460
  49.8 19.6 %collective-permute-start.6 = (bf16[2,256,1024]{2,1,0:T(8,128)(2,1)S(1)}, bf16[2,256,1024]{2,1,0:T(8,128)(2,1)S(1)}, u32[]{:S(2)}, u32[]{:S(2)}) collective-permute-start(bf16[2,256,1024]{2,1,0:T(8,128)(2,1)S(1)} %copy-done.17), channel_id=1, source_target_pairs={{0,16},{1,9},{2,18},{3,11},{4,20},{5,13},{6,22},{7,15},{8,24},{9,1... | collective-permute-start | bytes 3145736 | tf_op jit(solution)/shard_map/ppermute | solution.py:45
  53.2 29.0 %copy-start.9 = (bf16[2,256,1024]{2,1,0:T(8,128)(2,1)S(1)}, bf16[2,256,1024]{2,1,0:T(8,128)(2,1)}, u32[]{:S(2)}) copy-start(bf16[2,256,1024]{2,1,0:T(8,128)(2,1)} %get-tuple-element.43) | copy-start | bytes 3145732
  53.2 29.0 %collective-permute-start.9 = (bf16[2,256,1024]{2,1,0:T(8,128)(2,1)S(1)}, bf16[2,256,1024]{2,1,0:T(8,128)(2,1)S(1)}, u32[]{:S(2)}, u32[]{:S(2)}) collective-permute-start(bf16[2,256,1024]{2,1,0:T(8,128)(2,1)S(1)} %add_convert_fusion.3), channel_id=1, source_target_pairs={{0,2},{1,3},{6,4},{7,5},{8,10},{9,11},{14,12},{15,13},{16,18},{17,... | collective-permute-start | bytes 3145736 | tf_op jit(solution)/shard_map/ppermute | solution.py:45
  60.6 48.9 %collective-permute-start.4 = (bf16[2,2,256,1024]{3,2,1,0:T(8,128)(2,1)S(1)}, bf16[2,2,256,1024]{3,2,1,0:T(8,128)(2,1)S(1)}, u32[]{:S(2)}, u32[]{:S(2)}) collective-permute-start(bf16[2,2,256,1024]{3,2,1,0:T(8,128)(2,1)S(1)} %copy-done.16), channel_id=1, source_target_pairs={{0,16},{1,9},{2,18},{3,11},{4,20},{5,13},{6,22},{7,15},{8,24},{9,1... | collective-permute-start | bytes 6291464 | tf_op jit(solution)/shard_map/ppermute | solution.py:45
  61.2 29.0 %collective-permute-start.13 = (bf16[2,1024,256]{2,1,0:T(8,128)(2,1)S(1)}, bf16[2,1024,256]{2,1,0:T(8,128)(2,1)S(1)}, u32[]{:S(2)}, u32[]{:S(2)}) collective-permute-start(bf16[2,1024,256]{2,1,0:T(8,128)(2,1)S(1)} %collective-permute-done.10), channel_id=1, source_target_pairs={{2,0},{3,1},{4,6},{5,7},{10,8},{11,9},{12,14},{13,15},{18,16},{19,... | collective-permute-start | bytes 3145736 | tf_op jit(solution)/shard_map/ppermute | solution.py:45
  69.4 45.8 %copy-start.2 = (bf16[2,1024,256]{2,1,0:T(8,128)(2,1)}, bf16[2,1024,256]{2,1,0:T(8,128)(2,1)S(1)}, u32[]{:S(2)}) copy-start(bf16[2,1024,256]{2,1,0:T(8,128)(2,1)S(1)} %add.61.refs_7_) | copy-start | bytes 3145732
  83.0 25.1 %collective-permute-start.12 = (bf16[2,256,1024]{2,1,0:T(8,128)(2,1)S(1)}, bf16[2,256,1024]{2,1,0:T(8,128)(2,1)S(1)}, u32[]{:S(2)}, u32[]{:S(2)}) collective-permute-start(bf16[2,256,1024]{2,1,0:T(8,128)(2,1)S(1)} %get-tuple-element.47), channel_id=1, source_target_pairs={{0,2},{1,3},{6,4},{7,5},{8,10},{9,11},{14,12},{15,13},{16,18},{17,... | collective-permute-start | bytes 3145736 | tf_op jit(solution)/shard_map/ppermute | solution.py:45
  87.4 22.1 %collective-permute-start.15 = (bf16[2,256,1024]{2,1,0:T(8,128)(2,1)S(1)}, bf16[2,256,1024]{2,1,0:T(8,128)(2,1)S(1)}, u32[]{:S(2)}, u32[]{:S(2)}) collective-permute-start(bf16[2,256,1024]{2,1,0:T(8,128)(2,1)S(1)} %get-tuple-element.66), channel_id=1, source_target_pairs={{2,4},{3,5},{4,2},{5,3},{10,12},{11,13},{12,10},{13,11},{18,20},{1... | collective-permute-start | bytes 3145736 | tf_op jit(solution)/shard_map/ppermute | solution.py:45
  88.2 29.6 %collective-permute-start.17 = (bf16[2,1024,256]{2,1,0:T(8,128)(2,1)}, bf16[2,1024,256]{2,1,0:T(8,128)(2,1)S(1)}, u32[]{:S(2)}, u32[]{:S(2)}) collective-permute-start(bf16[2,1024,256]{2,1,0:T(8,128)(2,1)} %collective-permute-done.7.refs_5_), channel_id=1, source_target_pairs={{0,16},{1,9},{2,18},{3,11},{4,20},{5,13},{6,22},{7,15},{8,24},{9,1... | collective-permute-start | bytes 3145736 | tf_op jit(solution)/shard_map/ppermute | solution.py:45
  91.8 26.0 %copy-start.3 = (bf16[2,1024,256]{2,1,0:T(8,128)(2,1)}, bf16[2,1024,256]{2,1,0:T(8,128)(2,1)S(1)}, u32[]{:S(2)}) copy-start(bf16[2,1024,256]{2,1,0:T(8,128)(2,1)S(1)} %add.62.refs_5_) | copy-start | bytes 3145732
  91.8 17.7 %copy-start.5 = (bf16[2,2,256,1024]{3,2,1,0:T(8,128)(2,1)S(1)}, bf16[2,2,256,1024]{3,2,1,0:T(8,128)(2,1)}, u32[]{:S(2)}) copy-start(bf16[2,2,256,1024]{3,2,1,0:T(8,128)(2,1)} %get-tuple-element.35) | copy-start | bytes 6291460
  108.5 6.7 %copy-start.18 = (bf16[384,1024]{1,0:T(8,128)(2,1)S(1)}, bf16[384,1024]{1,0:T(8,128)(2,1)}, u32[]{:S(2)}) copy-start(bf16[384,1024]{1,0:T(8,128)(2,1)} %get-tuple-element.41) | copy-start | bytes 2359300
  108.5 9.4 %collective-permute-start.14 = (bf16[2,256,1024]{2,1,0:T(8,128)(2,1)S(1)}, bf16[2,256,1024]{2,1,0:T(8,128)(2,1)S(1)}, u32[]{:S(2)}, u32[]{:S(2)}) collective-permute-start(bf16[2,256,1024]{2,1,0:T(8,128)(2,1)S(1)} %add_convert_fusion.1), channel_id=1, source_target_pairs={{2,4},{3,5},{4,2},{5,3},{10,12},{11,13},{12,10},{13,11},{18,20},{1... | collective-permute-start | bytes 3145736 | tf_op jit(solution)/shard_map/ppermute | solution.py:45
  109.6 25.9 %copy-start.6 = (bf16[2,2,256,1024]{3,2,1,0:T(8,128)(2,1)}, bf16[2,2,256,1024]{3,2,1,0:T(8,128)(2,1)S(1)}, u32[]{:S(2)}) copy-start(bf16[2,2,256,1024]{3,2,1,0:T(8,128)(2,1)S(1)} %collective-permute-done.4) | copy-start | bytes 6291460
  110.3 25.2 %collective-permute-start.16 = (bf16[2,256,1024]{2,1,0:T(8,128)(2,1)S(1)}, bf16[2,256,1024]{2,1,0:T(8,128)(2,1)}, u32[]{:S(2)}, u32[]{:S(2)}) collective-permute-start(bf16[2,256,1024]{2,1,0:T(8,128)(2,1)S(1)} %fusion), channel_id=1, source_target_pairs={{0,2},{1,3},{2,0},{3,1},{4,6},{5,7},{6,4},{7,5},{8,10},{9,11},{10,... | collective-permute-start | bytes 3145736 | tf_op jit(solution)/shard_map/ppermute | solution.py:45
  115.2 2.8 collective-permute-start.19
  115.2 21.7 %collective-permute-start.20 = (bf16[2,1024,256]{2,1,0:T(8,128)(2,1)S(1)}, bf16[2,1024,256]{2,1,0:T(8,128)(2,1)S(1)}, u32[]{:S(2)}, u32[]{:S(2)}) collective-permute-start(bf16[2,1024,256]{2,1,0:T(8,128)(2,1)S(1)} %add.61.refs_7_), channel_id=1, source_target_pairs={{0,16},{1,9},{2,18},{3,11},{4,20},{5,13},{6,22},{7,15},{8,24},{9,1... | collective-permute-start | bytes 3145736 | tf_op jit(solution)/shard_map/ppermute | solution.py:45
  117.8 20.2 %copy-start.8 = (bf16[2,1024,256]{2,1,0:T(8,128)(2,1)}, bf16[2,1024,256]{2,1,0:T(8,128)(2,1)S(1)}, u32[]{:S(2)}) copy-start(bf16[2,1024,256]{2,1,0:T(8,128)(2,1)S(1)} %collective-permute-done.17.refs_6_) | copy-start | bytes 3145732
  117.8 35.0 %collective-permute-start.18 = (bf16[2,1024,256]{2,1,0:T(8,128)(2,1)S(1)}, bf16[2,1024,256]{2,1,0:T(8,128)(2,1)S(1)}, u32[]{:S(2)}, u32[]{:S(2)}) collective-permute-start(bf16[2,1024,256]{2,1,0:T(8,128)(2,1)S(1)} %add.62.refs_5_), channel_id=1, source_target_pairs={{0,16},{1,9},{2,18},{3,11},{4,20},{5,13},{6,22},{7,15},{8,24},{9,1... | collective-permute-start | bytes 3145736 | tf_op jit(solution)/shard_map/ppermute | solution.py:45
  117.9 1.0 copy-start.15
  118.9 19.1 %copy-start.13 = (bf16[2,256,1024]{2,1,0:T(8,128)(2,1)}, bf16[2,256,1024]{2,1,0:T(8,128)(2,1)S(1)}, u32[]{:S(2)}) copy-start(bf16[2,256,1024]{2,1,0:T(8,128)(2,1)S(1)} %collective-permute-done.14) | copy-start | bytes 3145732
  136.9 1.1 copy-start.12
  152.8 1.0 copy-start.11
  153.8 20.5 %copy-start.14 = (bf16[2,256,1024]{2,1,0:T(8,128)(2,1)S(1)}, bf16[2,256,1024]{2,1,0:T(8,128)(2,1)}, u32[]{:S(2)}) copy-start(bf16[2,256,1024]{2,1,0:T(8,128)(2,1)} %copy-done.13) | copy-start | bytes 3145732
  164.5 12.6 %collective-permute-start.21 = (f32[384,1024]{1,0:T(8,128)}, f32[384,1024]{1,0:T(8,128)}, u32[]{:S(2)}, u32[]{:S(2)}) collective-permute-start(f32[384,1024]{1,0:T(8,128)} %get-tuple-element.59), channel_id=1, source_target_pairs={{0,1},{1,0},{2,3},{3,2},{4,5},{5,4},{6,7},{7,6},{8,9},{9,8},{10,11... | collective-permute-start | bytes 4718600 | tf_op jit(solution)/shard_map/ppermute | solution.py:45
  164.6 15.5 %collective-permute-start.22 = (bf16[384,2048]{1,0:T(8,128)(2,1)}, bf16[384,2048]{1,0:T(8,128)(2,1)S(1)}, u32[]{:S(2)}, u32[]{:S(2)}) collective-permute-start(bf16[384,2048]{1,0:T(8,128)(2,1)} %get-tuple-element.60), channel_id=1, source_target_pairs={{0,1},{1,0},{2,3},{3,2},{4,5},{5,4},{6,7},{7,6},{8,9},{9,8},{10,11... | collective-permute-start | bytes 4718600 | tf_op jit(solution)/shard_map/ppermute | solution.py:45
  165.1 9.2 %collective-permute-start.24 = (bf16[256,1024]{1,0:T(8,128)(2,1)S(1)}, bf16[256,1024]{1,0:T(8,128)(2,1)S(1)}, u32[]{:S(2)}, u32[]{:S(2)}) collective-permute-start(bf16[256,1024]{1,0:T(8,128)(2,1)S(1)} %fusion.4), channel_id=1, source_target_pairs={{0,8},{1,17},{2,10},{3,19},{4,12},{5,21},{6,14},{7,23},{8,0},{9,25... | collective-permute-start | bytes 1572872 | tf_op jit(solution)/shard_map/ppermute | solution.py:45
  165.1 15.0 %collective-permute-start.23 = (bf16[384,1024]{1,0:T(8,128)(2,1)}, bf16[384,1024]{1,0:T(8,128)(2,1)}, u32[]{:S(2)}, u32[]{:S(2)}) collective-permute-start(bf16[384,1024]{1,0:T(8,128)(2,1)} %get-tuple-element.61), channel_id=1, source_target_pairs={{0,1},{1,0},{2,3},{3,2},{4,5},{5,4},{6,7},{7,6},{8,9},{9,8},{10,11... | collective-permute-start | bytes 2359304 | tf_op jit(solution)/shard_map/ppermute | solution.py:45
  180.1 1.2 copy-start.7

commit v6 on v1

v6 whole, which is shorter than its diff:
```python
import math

import jax
import jax.numpy as jnp
from jax import lax
from jax.experimental import pallas as pl
from jax.experimental.pallas import tpu as pltpu
from jax.sharding import Mesh, PartitionSpec as P

F32, BF16 = jnp.float32, jnp.bfloat16
AXES = ("blk", "chip", "core")
SHRINK = 1000
VMEM = 63 * 2**20


def hops(move):
    pairs = []
    for blk in range(4):
        for z in range(4):
            for core in range(2):
                to = move(blk, z, core)
                if to is not None:
                    pairs.append(((blk * 4 + z) * 2 + core, (to[0] * 4 + to[1]) * 2 + to[2]))
    return pairs


def middle(z):
    return z in (1, 2)


SWAP = hops(lambda b, z, c: (b, z, 1 - c))
FLIP_A = hops(lambda b, z, c: (b ^ (1 + c), z, c))
FLIP_B = hops(lambda b, z, c: (b ^ (2 - c), z, c))
PAIR = hops(lambda b, z, c: (b, z ^ 1, c))
MID = hops(lambda b, z, c: (b, z ^ 3, c) if middle(z) else None)
OUT = hops(lambda b, z, c: (b, z ^ 1, c) if middle(z) else None)
IN = hops(lambda b, z, c: (b, z ^ 1, c) if not middle(z) else None)


def after(array, *others):
    return lax.optimization_barrier((array, *others))[0]


def sent(array, pairs):
    return lax.ppermute(array, AXES, pairs)


def column_block(place, a, b):
    core = place[1]
    return place[2] ^ (a * (1 + core)) ^ (b * (2 - core))


def cost(flops, moved, shrink=SHRINK):
    return pl.CostEstimate(flops=flops // shrink, bytes_accessed=moved // shrink, transcendentals=0)


def first_term_kernel(place, mine, other, cot_mine, cot_other, keep, send, cots, turned):
    tokens, cols = cot_mine.shape[0], cot_mine.shape[1] // 4

    @pl.when(pl.program_id(0) == 0)
    def _():
        for b in (0, 1):
            for a in (0, 1):
                at = pl.ds(pl.multiple_of(column_block(place, a, b) * cols, cols), cols)
                to = slice((2 * b + a) * cols, (2 * b + a + 1) * cols)
                for array, half in ((cot_mine, slice(0, tokens)), (cot_other, slice(tokens, None))):
                    piece = array[:, at]
                    cots[half, to] = piece
                    turned[to, half] = piece.T

    tall = jnp.concatenate([mine[...], other[...]], 0)
    for b, out in ((1, send), (0, keep)):
        part = turned[2 * b * cols : (2 * b + 2) * cols]
        out[...] = jnp.dot(part, tall, preferred_element_type=F32).astype(BF16).reshape(out.shape)


def first_terms(place, activations, other, cot_mine, cot_other, rows):
    tokens, columns = cot_mine.shape
    part, cols = rows // 2, columns // 4
    mine = pl.BlockSpec((tokens, part), lambda r, s: (0, 2 * (2 * (s[0] ^ 3) + s[1]) + r))
    piece = pl.BlockSpec((2, cols, part), lambda r, s: (0, 0, r))

    def whole(*shape):
        return pl.BlockSpec(shape, lambda r, s: (0, 0))

    return pl.pallas_call(
        first_term_kernel,
        grid_spec=pltpu.PrefetchScalarGridSpec(
            num_scalar_prefetch=1,
            grid=(2,),
            in_specs=[mine, mine, whole(tokens, columns), whole(tokens, columns)],
            out_specs=[piece, piece, whole(2 * tokens, columns), whole(columns, 2 * tokens)],
        ),
        out_shape=[jax.ShapeDtypeStruct((2, cols, rows), BF16)] * 2
        + [
            jax.ShapeDtypeStruct((2 * tokens, columns), BF16),
            jax.ShapeDtypeStruct((columns, 2 * tokens), BF16),
        ],
        compiler_params=pltpu.CompilerParams(vmem_limit_bytes=VMEM),
        cost_estimate=cost(4 * tokens * rows * columns, 4 * tokens * rows + 4 * rows * columns),
        name="terms",
    )(place, activations, other, cot_mine, cot_other)


def term_kernel(place, mine, other, turned, keep2, keep10, send2, send10):
    rows = turned.shape[0] // 2
    for first in (True, False):

        @pl.when((pl.program_id(0) == 0) == first)
        def _():
            tall = jnp.concatenate([mine[...], other[...]], 0)
            for b, out in ((1, send2 if first else send10), (0, keep2 if first else keep10)):
                part = turned[b * rows : (b + 1) * rows]
                out[...] = (
                    jnp.dot(part, tall, preferred_element_type=F32).astype(BF16).reshape(out.shape)
                )


def terms(place, activations, other, turned, rows):
    columns, tokens = turned.shape[0], activations.shape[0]
    part, cols = rows // 2, columns // 4
    mine = pl.BlockSpec((tokens, part), lambda i, r, s: (0, 2 * (2 * (s[0] ^ (2 - i)) + s[1]) + r))
    pieces = [
        pl.BlockSpec((2, cols, part), lambda i, r, s: (0, 0, jnp.where(i == 0, r, 1))),
        pl.BlockSpec(
            (1, 2, cols, part),
            lambda i, r, s: (jnp.where(i == 2, 0, 1), 0, 0, jnp.where(i == 0, 0, r)),
        ),
    ]
    return pl.pallas_call(
        term_kernel,
        grid_spec=pltpu.PrefetchScalarGridSpec(
            num_scalar_prefetch=1,
            grid=(3, 2),
            in_specs=[mine, mine, pl.BlockSpec(turned.shape, lambda i, r, s: (0, 0))],
            out_specs=pieces * 2,
        ),
        out_shape=[
            jax.ShapeDtypeStruct((2, cols, rows), BF16),
            jax.ShapeDtypeStruct((2, 2, cols, rows), BF16),
        ]
        * 2,
        compiler_params=pltpu.CompilerParams(vmem_limit_bytes=VMEM),
        cost_estimate=cost(12 * tokens * rows * columns, 12 * tokens * rows + 12 * rows * columns),
        name="terms",
    )(place, activations, other, turned)


def project_kernel(place, acts, other, cots, here, there, *refs, first, last):
    near, far, *keys = refs[0 if first else 3 : -1]
    acc = refs[-1]
    tokens, cols = acts.shape[0], here.shape[2]
    step = pl.program_id(0)

    @pl.when(step < 2)
    def _():
        weight = jnp.concatenate([here[0], here[1], there[0], there[1]], 1)
        total = lax.dot_general(
            cots[...], weight, (((1,), (1,)), ((), ())), preferred_element_type=F32
        ).astype(BF16)
        near[...] = total[:tokens]
        far[...] = total[tokens:]
        tall = jnp.concatenate([acts[...], other[...]], 0)
        sums = jnp.dot(tall, weight, preferred_element_type=F32)

        @pl.when(step == 0)
        def _():
            acc[...] = sums if first else refs[0][...] + sums

        @pl.when(step == 1)
        def _():
            if last:
                for b in (0, 1):
                    for a in (0, 1):
                        at = pl.ds(pl.multiple_of(column_block(place, a, b) * cols, cols), cols)
                        to = slice((2 * b + a) * cols, (2 * b + a + 1) * cols)
                        keys[0][:, at] = acc[:tokens, to] + sums[:tokens, to]
                        keys[1][:, at] = acc[tokens:, to] + sums[tokens:, to]
            else:
                keys[0][...] = acc[...] + sums

    if not first:

        @pl.when(step >= 2)
        def _():
            near[...] = refs[1][...]


def projected(place, k, activations, other, cots, here, there, so_far=None, got=None):
    tokens, columns = activations.shape[0], cots.shape[1]
    _, rows, cols = here.shape
    part = rows // 2
    first, last = k == 0, k == 3

    def whole(*shape):
        return pl.BlockSpec(shape, lambda r, s: (0, 0))

    def out_at(r, s):
        own = 2 * (2 * (s[0] ^ k) + s[1]) + r
        received = 2 * (2 * (s[0] ^ (k - 1)) + 1 - s[1]) + r - 2
        return (0, own if first else jnp.where(r < 2, own, received))

    mine = pl.BlockSpec(
        (tokens, part), lambda r, s: (0, 2 * (2 * (s[0] ^ k) + s[1]) + jnp.minimum(r, 1))
    )
    piece = pl.BlockSpec((2, part, cols), lambda r, s: (0, jnp.minimum(r, 1), 0))
    one = jax.ShapeDtypeStruct((tokens, columns), F32)
    return pl.pallas_call(
        lambda *refs: project_kernel(*refs, first=first, last=last),
        grid_spec=pltpu.PrefetchScalarGridSpec(
            num_scalar_prefetch=1,
            grid=(2 if first else 4,),
            in_specs=[mine, mine, whole(2 * tokens, columns), piece, piece]
            + (
                []
                if first
                else [
                    whole(2 * tokens, columns),
                    pl.BlockSpec((tokens, part), lambda r, s: (0, jnp.maximum(r - 2, 0))),
                    pl.BlockSpec(memory_space=pl.ANY),
                ]
            ),
            out_specs=[
                pl.BlockSpec((tokens, part), out_at),
                pl.BlockSpec((tokens, part), lambda r, s: (0, jnp.minimum(r, 1))),
            ]
            + ([whole(tokens, columns)] * 2 if last else [whole(2 * tokens, columns)]),
            scratch_shapes=[pltpu.VMEM((2 * tokens, columns), F32)],
        ),
        out_shape=[
            jax.ShapeDtypeStruct(activations.shape, BF16),
            jax.ShapeDtypeStruct((tokens, rows), BF16),
        ]
        + ([one, one] if last else [jax.ShapeDtypeStruct((2 * tokens, columns), F32)]),
        input_output_aliases={} if first else {8: 0},
        compiler_params=pltpu.CompilerParams(vmem_limit_bytes=VMEM),
        cost_estimate=cost(
            8 * tokens * rows * columns,
            8 * tokens * rows + 2 * rows * columns + 8 * tokens * columns,
            1 if last else SHRINK,
        ),
        name="project",
    )(
        place, activations, other, cots, here, there,
        *([] if first else [so_far[2], got, so_far[0]]),
    )


def finish_kernel(place, got, near, far, whole, out, keys):
    out[...] = got[...]
    keys[...] = (near[...] + far[...]).astype(BF16)


def finished(place, whole, got, keys_near, keys_far):
    tokens, rows = got.shape
    columns = keys_near.shape[1]
    part, some = rows // 2, columns // 2
    wide = pl.BlockSpec((tokens, some), lambda r, s: (0, r))
    return pl.pallas_call(
        finish_kernel,
        grid_spec=pltpu.PrefetchScalarGridSpec(
            num_scalar_prefetch=1,
            grid=(2,),
            in_specs=[
                pl.BlockSpec((tokens, part), lambda r, s: (0, r)),
                wide,
                wide,
                pl.BlockSpec(memory_space=pl.ANY),
            ],
            out_specs=[
                pl.BlockSpec((tokens, part), lambda r, s: (0, 2 * (2 * (s[0] ^ 3) + 1 - s[1]) + r)),
                wide,
            ],
        ),
        out_shape=[
            jax.ShapeDtypeStruct(whole.shape, BF16),
            jax.ShapeDtypeStruct((tokens, columns), BF16),
        ],
        input_output_aliases={4: 0},
        compiler_params=pltpu.CompilerParams(vmem_limit_bytes=VMEM),
        cost_estimate=cost(0, 4 * tokens * rows + 10 * tokens * columns),
        name="finish",
    )(place, got, keys_near, keys_far, whole)


def added(*arrays):
    total = arrays[0].astype(F32)
    for array in arrays[1:]:
        total = total + array.astype(F32)
    return total.astype(BF16)


def by_hops(activations, cotangent, kv_weight):
    rows = kv_weight.shape[0]
    tokens = activations.shape[0]
    place = jnp.stack([lax.axis_index(name) for name in ("chip", "core", "blk")]).astype(jnp.int32)

    other, cot_other = sent(activations, SWAP), sent(cotangent, SWAP)
    base = jnp.stack([kv_weight, sent(kv_weight, FLIP_A)])
    one, mid = sent(base, PAIR), sent(base, MID)
    base_b = sent(base, FLIP_B)

    keep3, send3, cots, turned = first_terms(
        place, after(activations, base), other, cotangent, cot_other, rows
    )
    got3 = sent(send3, FLIP_B)
    keep2, keep10, send2, send10 = terms(place, activations, other, turned, rows)
    got2 = sent(after(send2, got3, base_b), FLIP_B)

    sum3 = added(keep3, got3)
    far = sent(after(sum3, one, mid), IN)
    two_mid = sent(after(one, mid), MID)
    two_end = sent(mid, OUT)
    one_b = sent(after(one, got2), FLIP_B)
    got10 = sent(after(send10, got2), FLIP_B)
    whole, out, keys = projected(
        place, 0, after(activations, keep10), other, cots, base, base_b
    )
    got = sent(out, SWAP)
    sum2 = added(keep2, got2)
    two = two_mid + two_end
    near = sent(after(sum2, far, two, out), IN)
    mid_far = sent(added(sum2, far), MID)
    three_end = sent(two_mid, OUT)
    two_b = sent(after(two, one_b), FLIP_B)
    whole, out, keys = projected(
        place, 1, after(activations, out), other, cots, one, one_b, (whole, None, keys), got
    )
    got = sent(out, SWAP)

    three = mid + three_end
    three_b = sent(after(three, got10), FLIP_B)
    sum_mid = sent(added(sum3, after(near, three, out)), MID)
    sum_one = sent(added(keep10[1], got10[1], mid_far), PAIR)
    whole, out, keys = projected(
        place, 2, after(activations, out), other, cots, two, two_b, (whole, None, keys), got
    )
    got = sent(out, SWAP)
    sum_mid, sum_one = after(sum_mid, out), after(sum_one, out)
    last = [
        keep10[0, a].astype(F32)
        + got10[0, a].astype(F32)
        + sum_mid[a].astype(F32)
        + sum_one[a].astype(F32)
        for a in (0, 1)
    ]
    over = last[1].astype(BF16)
    arrived = sent(over, FLIP_A)
    final = last[0] + arrived.astype(F32)
    grad_weight = (final * (1.0 / math.sqrt(32 * tokens))).astype(BF16).T

    whole, out, keys, keys_far = projected(
        place, 3, after(activations, over), other, cots, three, three_b, (whole, None, keys), got
    )
    grad_input, key_values = finished(
        place, whole, sent(out, SWAP), keys, sent(after(keys_far, arrived), SWAP)
    )
    return (key_values, grad_input, grad_weight)


def swapped(array):
    return lax.ppermute(array, "core", [(0, 1), (1, 0)])


def by_collectives(activations, cotangent, kv_weight):
    blocks, chips = lax.axis_size("blk"), lax.axis_size("chip")
    core = lax.axis_index("core")
    tokens, features = activations.shape
    rows, cols = kv_weight.shape
    columns = cotangent.shape[1]
    by_core = activations.reshape(tokens, chips, 2, rows)
    mine = lax.dynamic_index_in_dim(by_core, core, 2, keepdims=False)
    other = lax.dynamic_index_in_dim(by_core, 1 - core, 2, keepdims=False)
    acts = jnp.concatenate([mine, swapped(other)], 0)
    cots = jnp.concatenate([cotangent, swapped(cotangent)], 0)
    weight = lax.all_gather(kv_weight, ("blk", "chip"), axis=0, tiled=False)
    weight = weight.reshape(blocks, chips, rows, cols)
    parts = jnp.einsum(
        "tzr,tbc->bzrc", acts, cots.reshape(2 * tokens, blocks, cols), preferred_element_type=F32
    ).astype(BF16).reshape(blocks * chips, rows, cols)
    total = lax.psum_scatter(parts, ("blk", "chip"), scatter_dimension=0, tiled=False)
    count = tokens * blocks * chips * 2
    grad_weight = (total.astype(F32) * (1.0 / math.sqrt(count))).astype(BF16)
    full = weight.transpose(1, 2, 0, 3).reshape(chips * rows, columns)
    keys = jnp.dot(acts.reshape(2 * tokens, chips * rows), full, preferred_element_type=F32)
    key_values = (keys[:tokens] + swapped(keys[tokens:])).astype(BF16)
    inputs = lax.dot_general(
        cots, full, (((1,), (1,)), ((), ())), preferred_element_type=F32
    ).astype(BF16).reshape(2 * tokens, chips, rows)
    near, far = inputs[:tokens], swapped(inputs[tokens:])
    low = jnp.where(core == 0, near, far)
    high = jnp.where(core == 0, far, near)
    grad_input = jnp.stack([low, high], 2).reshape(tokens, features)
    return (key_values, grad_input, grad_weight)


def solution(mesh):
    blocks, shards = mesh.shape["blk"], mesh.shape["shard"]
    split = Mesh(mesh.devices.reshape(blocks, shards // 2, 2), AXES)
    by_token = P(AXES, None)
    by_piece = P(("chip", "core"), "blk")
    return jax.shard_map(
        by_hops if (blocks, shards) == (4, 8) else by_collectives,
        mesh=split,
        in_specs=(by_token, by_token, by_piece),
        out_specs=(by_token, by_token, by_piece),
        check_vma=False,
    )
```

time: 319 us -> 184 us (0.58)
  waiting for transfers between devices: 151 us -> 50.5 us
  local copies, waits for them, and re-layouts: 102 us -> 4.92 us
  Pallas kernels: 0 us -> 64.5 us
  starting transfers between devices: 1.14 us -> 36.2 us
  matrix products: 31.1 us -> 0 us
  between operations: 14.1 us -> 0.76 us
  other arithmetic: 19 us -> 26.2 us
    reduce_scatter x1 -> x0, waiting for transfers between devices: 88.5 us -> none  [local(): lax.psum_scatter(terms, ('blk', 'chip'), scatter_dimension=0, tiled=False)]
    pallas_call x0 -> x7, Pallas kernels: none -> 64.5 us  [the longest x4 43.4 us: projected(): pl.pallas_call(lambda *refs: project_kernel(*refs, first=first, last=last...]
    all_gather x1 -> x0, waiting for transfers between devices: 59.8 us -> none  [local(): weight = lax.all_gather(kv_weight, ('blk', 'chip'), axis=0, tiled=False)]
    ppermute x4 -> x26, waiting for transfers between devices: 1.72 us -> 50.5 us  [sent(): return lax.ppermute(array, AXES, pairs)]
    reshape x3 -> x0, local copies, waits for them, and re-layouts: 35.6 us -> none  [the longest x1 12.3 us: local(): terms = jnp.einsum('tzr,tbc->bzrc', acts, cots.reshape(2 * tokens, blocks...]
    ppermute x4 -> x26, starting transfers between devices: 1.07 us -> 36.2 us  [sent(): return lax.ppermute(array, AXES, pairs)]
    dot_general x3 -> x0, matrix products: 31.1 us -> none  [the longest x1 11.3 us: local(): jnp.einsum('tzr,tbc->bzrc', acts, cots.reshape(2 * tokens, blocks, cols),...]
    unnamed x9 -> x15, local copies, waits for them, and re-layouts: 22.3 us -> 4.92 us
  transfers between devices with their start and end apart: 6 -> 26, of which waited for: 3 -> 9; matrix products, arithmetic and copies ran while one was open for 46% -> 15% of each run, Pallas kernels for 0% -> 33%
where the time goes in v6:
time: 184 us; the launch traced here: 183 us
  Pallas kernels  64.5 us (35%)
  waiting for transfers between devices  50.5 us (27%)
  starting transfers between devices  36.2 us (20%)
  other arithmetic  26.2 us (14%)
  local copies, waits for them, and re-layouts  4.92 us (3%)
    ppermute x26, waiting for transfers between devices, sent(): return lax.ppermute(array, AXES, pairs)  50.5 us
    pallas_call x4, Pallas kernels, projected(): pl.pallas_call(lambda *refs: project_kernel(*refs, first=first, last=last...  43.4 us
    ppermute x26, starting transfers between devices, sent(): return lax.ppermute(array, AXES, pairs)  36.2 us
    convert_element_type x4, other arithmetic, added(): return total.astype(BF16)  13.3 us
    pallas_call x1, Pallas kernels, terms(): pl.pallas_call(term_kernel, grid_spec=pltpu.PrefetchScalarGridSpec(num_sc...  10.9 us
    pallas_call x1, Pallas kernels, first_terms(): pl.pallas_call(first_term_kernel, grid_spec=pltpu.PrefetchScalarGridSpec(...  6.49 us
    unnamed x15, local copies, waits for them, and re-layouts  4.92 us
    pallas_call x1, Pallas kernels, finished(): pl.pallas_call(finish_kernel, grid_spec=pltpu.PrefetchScalarGridSpec(num_...  3.74 us
  transfers between devices with their start and end apart: 26, of which 9 were waited for; matrix products, arithmetic and copies ran while one was open for 15% of the time, Pallas kernels for 33%

profile of v6, /device:TPU:0, one launch (start us, length us, event | category | flops | bytes accessed | tf_op | source)
XLA Modules:
  0.0 183.1 jit_solution(15915797169612264942)
XLA Ops:
  0.6 0.5 collective-permute-start
  1.2 2.9 %collective-permute-start.1 = (bf16[1024,256]{1,0:T(8,128)(2,1)}, bf16[1024,256]{1,0:T(8,128)(2,1)S(1)}, u32[]{:S(2)}, u32[]{:S(2)}) collective-permute-start(bf16[1024,256]{1,0:T(8,128)(2,1)} %param.5), channel_id=1, source_target_pairs={{0,8},{1,17},{2,10},{3,19},{4,12},{5,21},{6,14},{7,23},{8,0},{9,25... | collective-permute-start | bytes 1572872 | tf_op jit(solution)/shard_map/ppermute | solution.py:45
  4.1 7.4 %collective-permute-done.1 = bf16[1024,256]{1,0:T(8,128)(2,1)S(1)} collective-permute-done((bf16[1024,256]{1,0:T(8,128)(2,1)}, bf16[1024,256]{1,0:T(8,128)(2,1)S(1)}, u32[]{:S(2)}, u32[]{:S(2)}) %collective-permute-start.1) | collective-permute-done | bytes 524320 | tf_op jit(solution)/shard_map/ppermute | solution.py:45
  11.5 2.1 %pad_maximum_fusion.refs_4_ = bf16[2,1024,256]{2,1,0:T(8,128)(2,1)} fusion(bf16[1,1024,256]{2,1,0:T(8,128)(2,1)S(1)} %bitcast.30, bf16[1,1024,256]{2,1,0:T(8,128)(2,1)} %bitcast.29), kind=kLoop, calls=%fused_computation.6 | loop fusion | flops 524288 | bytes 2097152 | tf_op jit(solution)/shard_map/stack | solution.py:299
  13.6 1.6 collective-permute-start.8
  15.3 4.0 %collective-permute-start.7 = (bf16[2,1024,256]{2,1,0:T(8,128)(2,1)}, bf16[2,1024,256]{2,1,0:T(8,128)(2,1)}, u32[]{:S(2)}, u32[]{:S(2)}) collective-permute-start(bf16[2,1024,256]{2,1,0:T(8,128)(2,1)} %pad_maximum_fusion.refs_4_), channel_id=1, source_target_pairs={{0,2},{1,3},{2,0},{3,1},{4,6},{5,7},{6,4},{7,5},{8,10},{9,11},{10,... | collective-permute-start | bytes 3145736 | tf_op jit(solution)/shard_map/ppermute | solution.py:45
  19.3 0.6 pad_add_fusion.place.refs_0_
  19.9 1.5 collective-permute-start.4
  21.5 0.9 copy-done.4
  22.3 6.5 %terms.2 = (bf16[2,256,1024]{2,1,0:T(8,128)(2,1)}, bf16[2,256,1024]{2,1,0:T(8,128)(2,1)}, bf16[768,1024]{1,0:T(8,128)(2,1)}, bf16[1024,768]{1,0:T(8,128)(2,1)}) custom-call(s32[3]{0:T(128)} %pad_add_fusion.place.refs_0_, bf16[384,8192]{1,0:T(8,128)(2,1)} %refs_1_.3, bf16[384,8192]{1,0:T(8,128)(2,1)} %collective-permute-done.other.refs_2_, ...), custom_call_target="tpu_custom_call" | custom-call | flops 1610612 | bytes 5767 | tf_op jit(solution)/shard_map/terms/pallas_call | solution.py:86
  29.3 12.6 %collective-permute-done.7.refs_4_ = bf16[2,1024,256]{2,1,0:T(8,128)(2,1)} collective-permute-done((bf16[2,1024,256]{2,1,0:T(8,128)(2,1)}, bf16[2,1024,256]{2,1,0:T(8,128)(2,1)}, u32[]{:S(2)}, u32[]{:S(2)}) %collective-permute-start.7) | collective-permute-done | bytes 1048608 | tf_op jit(solution)/shard_map/ppermute | solution.py:45
  41.9 1.7 collective-permute-start.10
  43.5 10.9 %terms.3 = (bf16[2,256,1024]{2,1,0:T(8,128)(2,1)}, bf16[2,2,256,1024]{3,2,1,0:T(8,128)(2,1)}, bf16[2,256,1024]{2,1,0:T(8,128)(2,1)}, bf16[2,2,256,1024]{3,2,1,0:T(8,128)(2,1)}) custom-call(s32[3]{0:T(128)} %pad_add_fusion.place.refs_0_, bf16[384,8192]{1,0:T(8,128)(2,1)} %refs_1_.3, bf16[384,8192]{1,0:T(8,128)(2,1)} %collective-permute-done.other.refs_2_, ...), custom_call_target="tpu_custom_call" | custom-call | flops 4831838 | bytes 17301 | tf_op jit(solution)/shard_map/terms/pallas_call | solution.py:130
  54.4 1.6 collective-permute-start.5
  56.0 1.3 collective-permute-start.11
  57.3 3.0 %add_convert_fusion.3 = bf16[2,256,1024]{2,1,0:T(8,128)(2,1)} fusion(bf16[2,256,1024]{2,1,0:T(8,128)(2,1)} %collective-permute-done.3, bf16[2,256,1024]{2,1,0:T(8,128)(2,1)} %get-tuple-element.51), kind=kLoop, calls=%fused_computation.5 | loop fusion | flops 2097152 | bytes 3145728 | tf_op jit(solution)/shard_map/convert_element_type | solution.py:290
  60.3 5.6 %collective-permute-start.9 = (bf16[2,256,1024]{2,1,0:T(8,128)(2,1)}, bf16[2,256,1024]{2,1,0:T(8,128)(2,1)}, u32[]{:S(2)}, u32[]{:S(2)}) collective-permute-start(bf16[2,256,1024]{2,1,0:T(8,128)(2,1)} %add_convert_fusion.3), channel_id=1, source_target_pairs={{0,2},{1,3},{6,4},{7,5},{8,10},{9,11},{14,12},{15,13},{16,18},{17,... | collective-permute-start | bytes 3145736 | tf_op jit(solution)/shard_map/ppermute | solution.py:45
  65.9 1.3 collective-permute-start.13
  67.2 2.4 %collective-permute-done.5 = bf16[2,256,1024]{2,1,0:T(8,128)(2,1)} collective-permute-done((bf16[2,256,1024]{2,1,0:T(8,128)(2,1)}, bf16[2,256,1024]{2,1,0:T(8,128)(2,1)}, u32[]{:S(2)}, u32[]{:S(2)}) %collective-permute-start.5) | collective-permute-done | bytes 1048608 | tf_op jit(solution)/shard_map/ppermute | solution.py:45
  69.6 1.5 collective-permute-start.6
  71.1 13.1 %collective-permute-done.11 = bf16[2,1024,256]{2,1,0:T(8,128)(2,1)S(1)} collective-permute-done((bf16[2,1024,256]{2,1,0:T(8,128)(2,1)}, bf16[2,1024,256]{2,1,0:T(8,128)(2,1)S(1)}, u32[]{:S(2)}, u32[]{:S(2)}) %collective-permute-start.11) | collective-permute-done | bytes 1048608 | tf_op jit(solution)/shard_map/ppermute | solution.py:45
  84.2 2.6 %add.58.refs_4_ = bf16[2,1024,256]{2,1,0:T(8,128)(2,1)} add(bf16[2,1024,256]{2,1,0:T(8,128)(2,1)} %collective-permute-done.10, bf16[2,1024,256]{2,1,0:T(8,128)(2,1)S(1)} %collective-permute-done.11) | non-fusion elementwise | flops 524288 | bytes 3145728 | tf_op jit(solution)/shard_map/add | solution.py:321
  86.8 8.8 %project.4 = (bf16[384,8192]{1,0:T(8,128)(2,1)}, bf16[384,1024]{1,0:T(8,128)(2,1)}, f32[768,1024]{1,0:T(8,128)}) custom-call(s32[3]{0:T(128)} %pad_add_fusion.place.refs_0_, bf16[384,8192]{1,0:T(8,128)(2,1)} %refs_1_.3, bf16[384,8192]{1,0:T(8,128)(2,1)} %collective-permute-done.other.refs_2_, bf16[768,1024]{1,0:T(8,128)(2,1)} %get-tuple-element.56.refs_3_, ...), custom_call_target="tpu_custom_call" | custom-call | flops 3221225 | bytes 8388 | tf_op jit(solution)/shard_map/project/pallas_call | solution.py:208
  95.5 0.5 collective-permute-start.14
  96.0 4.0 %add_convert_fusion = (bf16[2,256,1024]{2,1,0:T(8,128)(2,1)}, bf16[2,256,1024]{2,1,0:T(8,128)(2,1)}) fusion(bf16[2,256,1024]{2,1,0:T(8,128)(2,1)} %collective-permute-done.9, bf16[2,256,1024]{2,1,0:T(8,128)(2,1)} %collective-permute-done.5, bf16[2,256,1024]{2,1,0:T(8,128)(2,1)} %get-tuple-element.52), kind=kLoop, calls=%fused_computation.2 | loop fusion | flops 4194304 | bytes 5242880 | tf_op jit(solution)/shard_map/convert_element_type | solution.py:290
  100.1 2.5 %collective-permute-start.12 = (bf16[2,256,1024]{2,1,0:T(8,128)(2,1)}, bf16[2,256,1024]{2,1,0:T(8,128)(2,1)}, u32[]{:S(2)}, u32[]{:S(2)}) collective-permute-start(bf16[2,256,1024]{2,1,0:T(8,128)(2,1)} %get-tuple-element.58), channel_id=1, source_target_pairs={{0,2},{1,3},{6,4},{7,5},{8,10},{9,11},{14,12},{15,13},{16,18},{17,... | collective-permute-start | bytes 3145736 | tf_op jit(solution)/shard_map/ppermute | solution.py:45
  102.6 1.1 collective-permute-done.13
  103.8 1.7 collective-permute-start.19
  105.4 2.8 %add.59.refs_4_ = bf16[2,1024,256]{2,1,0:T(8,128)(2,1)} add(bf16[2,1024,256]{2,1,0:T(8,128)(2,1)} %collective-permute-done.8, bf16[2,1024,256]{2,1,0:T(8,128)(2,1)} %collective-permute-done.13) | non-fusion elementwise | flops 524288 | bytes 3145728 | tf_op jit(solution)/shard_map/add | solution.py:331
  108.2 2.5 %collective-permute-done.14.refs_5_ = bf16[2,1024,256]{2,1,0:T(8,128)(2,1)} collective-permute-done((bf16[2,1024,256]{2,1,0:T(8,128)(2,1)}, bf16[2,1024,256]{2,1,0:T(8,128)(2,1)}, u32[]{:S(2)}, u32[]{:S(2)}) %collective-permute-start.14) | collective-permute-done | bytes 1048608 | tf_op jit(solution)/shard_map/ppermute | solution.py:45
  111.2 0.9 copy-done.2
  112.0 11.5 %project.5 = (bf16[384,8192]{1,0:T(8,128)(2,1)}, bf16[384,1024]{1,0:T(8,128)(2,1)}, f32[768,1024]{1,0:T(8,128)}) custom-call(s32[3]{0:T(128)} %pad_add_fusion.place.refs_0_, bf16[384,8192]{1,0:T(8,128)(2,1)} %refs_1_.3, bf16[384,8192]{1,0:T(8,128)(2,1)} %collective-permute-done.other.refs_2_, ...), custom_call_target="tpu_custom_call", output_to_operand_aliasing={{0}: (8, {})} | custom-call | flops 3221225 | bytes 8388 | tf_op jit(solution)/shard_map/project/pallas_call | solution.py:208
  123.6 3.1 %add_convert_fusion.1 = bf16[2,256,1024]{2,1,0:T(8,128)(2,1)} fusion(bf16[2,256,1024]{2,1,0:T(8,128)(2,1)} %collective-permute-done.12, bf16[2,256,1024]{2,1,0:T(8,128)(2,1)} %add_convert_fusion.3), kind=kLoop, calls=%fused_computation.3 | loop fusion | flops 2097152 | bytes 3145728 | tf_op jit(solution)/shard_map/convert_element_type | solution.py:290
  126.7 1.6 collective-permute-start.16
  128.4 3.1 %fusion = bf16[2,256,1024]{2,1,0:T(8,128)(2,1)} fusion(bf16[2,256,1024]{2,1,0:T(8,128)(2,1)} %collective-permute-done.19, bf16[2,2,256,1024]{3,2,1,0:T(8,128)(2,1)} %collective-permute-done.6, bf16[2,2,256,1024]{3,2,1,0:T(8,128)(2,1)S(1)} %copy-done), kind=kLoop, calls=%fused_computation.1 | loop fusion | flops 3145728 | bytes 4194304 | tf_op jit(solution)/shard_map/convert_element_type | solution.py:290
  131.5 2.1 %collective-permute-start.20 = (bf16[2,256,1024]{2,1,0:T(8,128)(2,1)}, bf16[2,256,1024]{2,1,0:T(8,128)(2,1)}, u32[]{:S(2)}, u32[]{:S(2)}) collective-permute-start(bf16[2,256,1024]{2,1,0:T(8,128)(2,1)} %fusion), channel_id=1, source_target_pairs={{0,2},{1,3},{2,0},{3,1},{4,6},{5,7},{6,4},{7,5},{8,10},{9,11},{10,... | collective-permute-start | bytes 3145736 | tf_op jit(solution)/shard_map/ppermute | solution.py:45
  133.6 1.0 collective-permute-start.21
  134.6 0.9 copy-done.1
  135.4 11.5 %project.6 = (bf16[384,8192]{1,0:T(8,128)(2,1)}, bf16[384,1024]{1,0:T(8,128)(2,1)}, f32[768,1024]{1,0:T(8,128)}) custom-call(s32[3]{0:T(128)} %pad_add_fusion.place.refs_0_, bf16[384,8192]{1,0:T(8,128)(2,1)} %refs_1_.3, bf16[384,8192]{1,0:T(8,128)(2,1)} %collective-permute-done.other.refs_2_, ...), custom_call_target="tpu_custom_call", output_to_operand_aliasing={{0}: (8, {})} | custom-call | flops 3221225 | bytes 8388 | tf_op jit(solution)/shard_map/project/pallas_call | solution.py:208
  147.1 10.2 %collective-permute-done.20 = bf16[2,256,1024]{2,1,0:T(8,128)(2,1)} collective-permute-done((bf16[2,256,1024]{2,1,0:T(8,128)(2,1)}, bf16[2,256,1024]{2,1,0:T(8,128)(2,1)}, u32[]{:S(2)}, u32[]{:S(2)}) %collective-permute-start.20) | collective-permute-done | bytes 1048608 | tf_op jit(solution)/shard_map/ppermute | solution.py:45
  157.3 2.7 %fusion.4 = bf16[256,1024]{1,0:T(8,128)(2,1)} fusion(bf16[2,2,256,1024]{3,2,1,0:T(8,128)(2,1)} %collective-permute-done.6, bf16[2,256,1024]{2,1,0:T(8,128)(2,1)} %collective-permute-done.20, bf16[2,256,1024]{2,1,0:T(8,128)(2,1)} %collective-permute-done.16, bf16[2,2,256,1024]{3,2,1,0:T(8,128)(2,1)} %get-tuple-element.45), kind=kLoop, calls=%fused_computation.13 | loop fusion | flops 2097152 | bytes 2621440 | tf_op jit(solution)/shard_map/convert_element_type | solution.py:347
  160.0 1.5 collective-permute-start.24
  161.5 0.9 copy-done.3
  162.3 11.6 %project.7 = (bf16[384,8192]{1,0:T(8,128)(2,1)}, bf16[384,1024]{1,0:T(8,128)(2,1)}, f32[384,1024]{1,0:T(8,128)}, f32[384,1024]{1,0:T(8,128)}) custom-call(s32[3]{0:T(128)} %pad_add_fusion.place.refs_0_, bf16[384,8192]{1,0:T(8,128)(2,1)} %refs_1_.3, bf16[384,8192]{1,0:T(8,128)(2,1)} %collective-permute-done.other.refs_2_, ...), custom_call_target="tpu_custom_call", output_to_operand_aliasing={{0}: (8, {})} | custom-call | flops 3221225472 | bytes 8388608 | tf_op jit(solution)/shard_map/project/pallas_call | solution.py:208
  174.6 2.1 %fusion.5 = bf16[1024,256]{0,1:T(8,128)(2,1)S(1)} fusion(bf16[256,1024]{1,0:T(8,128)(2,1)} %collective-permute-done.24, bf16[2,2,256,1024]{3,2,1,0:T(8,128)(2,1)} %collective-permute-done.6, bf16[2,256,1024]{2,1,0:T(8,128)(2,1)} %collective-permute-done.20, bf16[2,256,1024]{2,1,0:T(8,128)(2,1)} %collective-permute-done.16, ...), kind=kLoop, calls=%fused_computation.15 | loop fusion | flops 2883584 | bytes 3145728 | tf_op jit(solution)/shard_map/transpose | solution.py:350
  176.7 1.0 copy.10
  177.7 0.8 collective-permute-done.23.got
  179.3 3.7 %finish.1 = (bf16[384,8192]{1,0:T(8,128)(2,1)}, bf16[384,1024]{1,0:T(8,128)(2,1)}) custom-call(s32[3]{0:T(128)} %pad_add_fusion.place.refs_0_, bf16[384,1024]{1,0:T(8,128)(2,1)} %copy-done.5, f32[384,1024]{1,0:T(8,128)} %get-tuple-element.77.near, f32[384,1024]{1,0:T(8,128)} %collective-permute-done.25.far, ...), custom_call_target="tpu_custom_call", output_to_operand_aliasing={{0}: (4, {})} | custom-call | bytes 5505 | tf_op jit(solution)/shard_map/finish/pallas_call | solution.py:259
  (36 shorter events, 2.7 us)
Async XLA Ops:
  0.6 20.8 %collective-permute-start = (bf16[384,8192]{1,0:T(8,128)(2,1)}, bf16[384,8192]{1,0:T(8,128)(2,1)}, u32[]{:S(2)}, u32[]{:S(2)}) collective-permute-start(bf16[384,8192]{1,0:T(8,128)(2,1)} %refs_1_.3), channel_id=1, source_target_pairs={{0,1},{1,0},{2,3},{3,2},{4,5},{5,4},{6,7},{7,6},{8,9},{9,8},{10,11... | collective-permute-start | bytes 18874376 | tf_op jit(solution)/shard_map/ppermute | solution.py:45
  1.1 20.3 %collective-permute-start.2 = (bf16[384,1024]{1,0:T(8,128)(2,1)}, bf16[384,1024]{1,0:T(8,128)(2,1)S(1)}, u32[]{:S(2)}, u32[]{:S(2)}) collective-permute-start(bf16[384,1024]{1,0:T(8,128)(2,1)} %cot_mine.1), channel_id=1, source_target_pairs={{0,1},{1,0},{2,3},{3,2},{4,5},{5,4},{6,7},{7,6},{8,9},{9,8},{10,11... | collective-permute-start | bytes 2359304 | tf_op jit(solution)/shard_map/ppermute | solution.py:45
  1.2 10.3 %collective-permute-start.1 = (bf16[1024,256]{1,0:T(8,128)(2,1)}, bf16[1024,256]{1,0:T(8,128)(2,1)S(1)}, u32[]{:S(2)}, u32[]{:S(2)}) collective-permute-start(bf16[1024,256]{1,0:T(8,128)(2,1)} %param.5), channel_id=1, source_target_pairs={{0,8},{1,17},{2,10},{3,19},{4,12},{5,21},{6,14},{7,23},{8,0},{9,25... | collective-permute-start | bytes 1572872 | tf_op jit(solution)/shard_map/ppermute | solution.py:45
  13.6 15.7 %collective-permute-start.8 = (bf16[2,1024,256]{2,1,0:T(8,128)(2,1)}, bf16[2,1024,256]{2,1,0:T(8,128)(2,1)}, u32[]{:S(2)}, u32[]{:S(2)}) collective-permute-start(bf16[2,1024,256]{2,1,0:T(8,128)(2,1)} %pad_maximum_fusion.refs_4_), channel_id=1, source_target_pairs={{2,4},{3,5},{4,2},{5,3},{10,12},{11,13},{12,10},{13,11},{18,20},{1... | collective-permute-start | bytes 3145736 | tf_op jit(solution)/shard_map/ppermute | solution.py:45
  15.3 26.6 %collective-permute-start.7 = (bf16[2,1024,256]{2,1,0:T(8,128)(2,1)}, bf16[2,1024,256]{2,1,0:T(8,128)(2,1)}, u32[]{:S(2)}, u32[]{:S(2)}) collective-permute-start(bf16[2,1024,256]{2,1,0:T(8,128)(2,1)} %pad_maximum_fusion.refs_4_), channel_id=1, source_target_pairs={{0,2},{1,3},{2,0},{3,1},{4,6},{5,7},{6,4},{7,5},{8,10},{9,11},{10,... | collective-permute-start | bytes 3145736 | tf_op jit(solution)/shard_map/ppermute | solution.py:45
  19.9 34.5 %collective-permute-start.4 = (bf16[2,1024,256]{2,1,0:T(8,128)(2,1)}, bf16[2,1024,256]{2,1,0:T(8,128)(2,1)}, u32[]{:S(2)}, u32[]{:S(2)}) collective-permute-start(bf16[2,1024,256]{2,1,0:T(8,128)(2,1)} %pad_maximum_fusion.refs_4_), channel_id=1, source_target_pairs={{0,16},{1,9},{2,18},{3,11},{4,20},{5,13},{6,22},{7,15},{8,24},{9,1... | collective-permute-start | bytes 3145736 | tf_op jit(solution)/shard_map/ppermute | solution.py:45
  21.4 0.9 copy-start.4
  28.8 25.6 %collective-permute-start.3 = (bf16[2,256,1024]{2,1,0:T(8,128)(2,1)}, bf16[2,256,1024]{2,1,0:T(8,128)(2,1)}, u32[]{:S(2)}, u32[]{:S(2)}) collective-permute-start(bf16[2,256,1024]{2,1,0:T(8,128)(2,1)} %get-tuple-element.48), channel_id=1, source_target_pairs={{0,16},{1,9},{2,18},{3,11},{4,20},{5,13},{6,22},{7,15},{8,24},{9,1... | collective-permute-start | bytes 3145736 | tf_op jit(solution)/shard_map/ppermute | solution.py:45
  41.9 24.0 %collective-permute-start.10 = (bf16[2,1024,256]{2,1,0:T(8,128)(2,1)}, bf16[2,1024,256]{2,1,0:T(8,128)(2,1)}, u32[]{:S(2)}, u32[]{:S(2)}) collective-permute-start(bf16[2,1024,256]{2,1,0:T(8,128)(2,1)} %collective-permute-done.7.refs_4_), channel_id=1, source_target_pairs={{2,4},{3,5},{4,2},{5,3},{10,12},{11,13},{12,10},{13,11},{18,20},{1... | collective-permute-start | bytes 3145736 | tf_op jit(solution)/shard_map/ppermute | solution.py:45
  54.4 15.2 %collective-permute-start.5 = (bf16[2,256,1024]{2,1,0:T(8,128)(2,1)}, bf16[2,256,1024]{2,1,0:T(8,128)(2,1)}, u32[]{:S(2)}, u32[]{:S(2)}) collective-permute-start(bf16[2,256,1024]{2,1,0:T(8,128)(2,1)} %get-tuple-element.49), channel_id=1, source_target_pairs={{0,16},{1,9},{2,18},{3,11},{4,20},{5,13},{6,22},{7,15},{8,24},{9,1... | collective-permute-start | bytes 3145736 | tf_op jit(solution)/shard_map/ppermute | solution.py:45
  56.0 28.2 %collective-permute-start.11 = (bf16[2,1024,256]{2,1,0:T(8,128)(2,1)}, bf16[2,1024,256]{2,1,0:T(8,128)(2,1)S(1)}, u32[]{:S(2)}, u32[]{:S(2)}) collective-permute-start(bf16[2,1024,256]{2,1,0:T(8,128)(2,1)} %collective-permute-done.8), channel_id=1, source_target_pairs={{2,0},{3,1},{4,6},{5,7},{10,8},{11,9},{12,14},{13,15},{18,16},{19,... | collective-permute-start | bytes 3145736 | tf_op jit(solution)/shard_map/ppermute | solution.py:45
  60.3 35.7 %collective-permute-start.9 = (bf16[2,256,1024]{2,1,0:T(8,128)(2,1)}, bf16[2,256,1024]{2,1,0:T(8,128)(2,1)}, u32[]{:S(2)}, u32[]{:S(2)}) collective-permute-start(bf16[2,256,1024]{2,1,0:T(8,128)(2,1)} %add_convert_fusion.3), channel_id=1, source_target_pairs={{0,2},{1,3},{6,4},{7,5},{8,10},{9,11},{14,12},{15,13},{16,18},{17,... | collective-permute-start | bytes 3145736 | tf_op jit(solution)/shard_map/ppermute | solution.py:45
  65.9 37.9 %collective-permute-start.13 = (bf16[2,1024,256]{2,1,0:T(8,128)(2,1)}, bf16[2,1024,256]{2,1,0:T(8,128)(2,1)}, u32[]{:S(2)}, u32[]{:S(2)}) collective-permute-start(bf16[2,1024,256]{2,1,0:T(8,128)(2,1)} %collective-permute-done.10), channel_id=1, source_target_pairs={{2,0},{3,1},{4,6},{5,7},{10,8},{11,9},{12,14},{13,15},{18,16},{19,... | collective-permute-start | bytes 3145736 | tf_op jit(solution)/shard_map/ppermute | solution.py:45
  69.6 58.7 %collective-permute-start.6 = (bf16[2,2,256,1024]{3,2,1,0:T(8,128)(2,1)}, bf16[2,2,256,1024]{3,2,1,0:T(8,128)(2,1)}, u32[]{:S(2)}, u32[]{:S(2)}) collective-permute-start(bf16[2,2,256,1024]{3,2,1,0:T(8,128)(2,1)} %get-tuple-element.50), channel_id=1, source_target_pairs={{0,16},{1,9},{2,18},{3,11},{4,20},{5,13},{6,22},{7,15},{8,24},{9,1... | collective-permute-start | bytes 6291464 | tf_op jit(solution)/shard_map/ppermute | solution.py:45
  95.5 15.1 %collective-permute-start.14 = (bf16[2,1024,256]{2,1,0:T(8,128)(2,1)}, bf16[2,1024,256]{2,1,0:T(8,128)(2,1)}, u32[]{:S(2)}, u32[]{:S(2)}) collective-permute-start(bf16[2,1024,256]{2,1,0:T(8,128)(2,1)} %collective-permute-done.7.refs_4_), channel_id=1, source_target_pairs={{0,16},{1,9},{2,18},{3,11},{4,20},{5,13},{6,22},{7,15},{8,24},{9,1... | collective-permute-start | bytes 3145736 | tf_op jit(solution)/shard_map/ppermute | solution.py:45
  96.0 6.6 %copy-start.6 = (bf16[384,1024]{1,0:T(8,128)(2,1)S(1)}, bf16[384,1024]{1,0:T(8,128)(2,1)}, u32[]{:S(2)}) copy-start(bf16[384,1024]{1,0:T(8,128)(2,1)} %get-tuple-element.57) | copy-start | bytes 2359300
  100.1 23.5 %collective-permute-start.12 = (bf16[2,256,1024]{2,1,0:T(8,128)(2,1)}, bf16[2,256,1024]{2,1,0:T(8,128)(2,1)}, u32[]{:S(2)}, u32[]{:S(2)}) collective-permute-start(bf16[2,256,1024]{2,1,0:T(8,128)(2,1)} %get-tuple-element.58), channel_id=1, source_target_pairs={{0,2},{1,3},{6,4},{7,5},{8,10},{9,11},{14,12},{15,13},{16,18},{17,... | collective-permute-start | bytes 3145736 | tf_op jit(solution)/shard_map/ppermute | solution.py:45
  102.6 8.6 %collective-permute-start.15 = (bf16[384,1024]{1,0:T(8,128)(2,1)S(1)}, bf16[384,1024]{1,0:T(8,128)(2,1)S(1)}, u32[]{:S(2)}, u32[]{:S(2)}) collective-permute-start(bf16[384,1024]{1,0:T(8,128)(2,1)S(1)} %copy-done.6), channel_id=1, source_target_pairs={{0,1},{1,0},{2,3},{3,2},{4,5},{5,4},{6,7},{7,6},{8,9},{9,8},{10,11... | collective-permute-start | bytes 2359304 | tf_op jit(solution)/shard_map/ppermute | solution.py:45
  103.8 24.6 %collective-permute-start.19 = (bf16[2,256,1024]{2,1,0:T(8,128)(2,1)}, bf16[2,256,1024]{2,1,0:T(8,128)(2,1)}, u32[]{:S(2)}, u32[]{:S(2)}) collective-permute-start(bf16[2,256,1024]{2,1,0:T(8,128)(2,1)} %get-tuple-element.86), channel_id=1, source_target_pairs={{2,4},{3,5},{4,2},{5,3},{10,12},{11,13},{12,10},{13,11},{18,20},{1... | collective-permute-start | bytes 3145736 | tf_op jit(solution)/shard_map/ppermute | solution.py:45
  110.7 23.9 %collective-permute-start.17 = (bf16[2,1024,256]{2,1,0:T(8,128)(2,1)}, bf16[2,1024,256]{2,1,0:T(8,128)(2,1)}, u32[]{:S(2)}, u32[]{:S(2)}) collective-permute-start(bf16[2,1024,256]{2,1,0:T(8,128)(2,1)} %add.58.refs_4_), channel_id=1, source_target_pairs={{0,16},{1,9},{2,18},{3,11},{4,20},{5,13},{6,22},{7,15},{8,24},{9,1... | collective-permute-start | bytes 3145736 | tf_op jit(solution)/shard_map/ppermute | solution.py:45
  111.2 0.9 copy-start.2
  123.5 4.9 %copy-start = (bf16[2,2,256,1024]{3,2,1,0:T(8,128)(2,1)S(1)}, bf16[2,2,256,1024]{3,2,1,0:T(8,128)(2,1)}, u32[]{:S(2)}) copy-start(bf16[2,2,256,1024]{3,2,1,0:T(8,128)(2,1)} %get-tuple-element.45) | copy-start | bytes 6291460
  123.5 11.0 %collective-permute-start.18 = (bf16[384,1024]{1,0:T(8,128)(2,1)}, bf16[384,1024]{1,0:T(8,128)(2,1)S(1)}, u32[]{:S(2)}, u32[]{:S(2)}) collective-permute-start(bf16[384,1024]{1,0:T(8,128)(2,1)} %get-tuple-element.63), channel_id=1, source_target_pairs={{0,1},{1,0},{2,3},{3,2},{4,5},{5,4},{6,7},{7,6},{8,9},{9,8},{10,11... | collective-permute-start | bytes 2359304 | tf_op jit(solution)/shard_map/ppermute | solution.py:45
  126.7 20.3 %collective-permute-start.16 = (bf16[2,256,1024]{2,1,0:T(8,128)(2,1)}, bf16[2,256,1024]{2,1,0:T(8,128)(2,1)}, u32[]{:S(2)}, u32[]{:S(2)}) collective-permute-start(bf16[2,256,1024]{2,1,0:T(8,128)(2,1)} %add_convert_fusion.1), channel_id=1, source_target_pairs={{2,4},{3,5},{4,2},{5,3},{10,12},{11,13},{12,10},{13,11},{18,20},{1... | collective-permute-start | bytes 3145736 | tf_op jit(solution)/shard_map/ppermute | solution.py:45
  131.5 25.8 %collective-permute-start.20 = (bf16[2,256,1024]{2,1,0:T(8,128)(2,1)}, bf16[2,256,1024]{2,1,0:T(8,128)(2,1)}, u32[]{:S(2)}, u32[]{:S(2)}) collective-permute-start(bf16[2,256,1024]{2,1,0:T(8,128)(2,1)} %fusion), channel_id=1, source_target_pairs={{0,2},{1,3},{2,0},{3,1},{4,6},{5,7},{6,4},{7,5},{8,10},{9,11},{10,... | collective-permute-start | bytes 3145736 | tf_op jit(solution)/shard_map/ppermute | solution.py:45
  133.6 27.9 %collective-permute-start.21 = (bf16[2,1024,256]{2,1,0:T(8,128)(2,1)}, bf16[2,1024,256]{2,1,0:T(8,128)(2,1)}, u32[]{:S(2)}, u32[]{:S(2)}) collective-permute-start(bf16[2,1024,256]{2,1,0:T(8,128)(2,1)} %add.59.refs_4_), channel_id=1, source_target_pairs={{0,16},{1,9},{2,18},{3,11},{4,20},{5,13},{6,22},{7,15},{8,24},{9,1... | collective-permute-start | bytes 3145736 | tf_op jit(solution)/shard_map/ppermute | solution.py:45
  134.6 0.9 copy-start.1
  147.0 14.5 %collective-permute-start.22 = (bf16[384,1024]{1,0:T(8,128)(2,1)}, bf16[384,1024]{1,0:T(8,128)(2,1)S(1)}, u32[]{:S(2)}, u32[]{:S(2)}) collective-permute-start(bf16[384,1024]{1,0:T(8,128)(2,1)} %get-tuple-element.69), channel_id=1, source_target_pairs={{0,1},{1,0},{2,3},{3,2},{4,5},{5,4},{6,7},{7,6},{8,9},{9,8},{10,11... | collective-permute-start | bytes 2359304 | tf_op jit(solution)/shard_map/ppermute | solution.py:45
  160.0 14.0 %collective-permute-start.24 = (bf16[256,1024]{1,0:T(8,128)(2,1)}, bf16[256,1024]{1,0:T(8,128)(2,1)}, u32[]{:S(2)}, u32[]{:S(2)}) collective-permute-start(bf16[256,1024]{1,0:T(8,128)(2,1)} %fusion.4), channel_id=1, source_target_pairs={{0,8},{1,17},{2,10},{3,19},{4,12},{5,21},{6,14},{7,23},{8,0},{9,25... | collective-permute-start | bytes 1572872 | tf_op jit(solution)/shard_map/ppermute | solution.py:45
  161.4 0.9 copy-start.3
  174.0 4.9 %collective-permute-start.25 = (f32[384,1024]{1,0:T(8,128)}, f32[384,1024]{1,0:T(8,128)}, u32[]{:S(2)}, u32[]{:S(2)}) collective-permute-start(f32[384,1024]{1,0:T(8,128)} %get-tuple-element.79), channel_id=1, source_target_pairs={{0,1},{1,0},{2,3},{3,2},{4,5},{5,4},{6,7},{7,6},{8,9},{9,8},{10,11... | collective-permute-start | bytes 4718600 | tf_op jit(solution)/shard_map/ppermute | solution.py:45
  174.1 4.4 %collective-permute-start.23 = (bf16[384,1024]{1,0:T(8,128)(2,1)}, bf16[384,1024]{1,0:T(8,128)(2,1)S(1)}, u32[]{:S(2)}, u32[]{:S(2)}) collective-permute-start(bf16[384,1024]{1,0:T(8,128)(2,1)} %get-tuple-element.76), channel_id=1, source_target_pairs={{0,1},{1,0},{2,3},{3,2},{4,5},{5,4},{6,7},{7,6},{8,9},{9,8},{10,11... | collective-permute-start | bytes 2359304 | tf_op jit(solution)/shard_map/ppermute | solution.py:45
  178.5 0.9 copy-start.5

commit v7 on v6

--- a/solution.py
+++ b/solution.py
@@ -10,7 +10,8 @@
 F32, BF16 = jnp.float32, jnp.bfloat16
 AXES = ("blk", "chip", "core")
 SHRINK = 1000
-VMEM = 63 * 2**20
+MIB = 2**20
+ONCE = pl.Buffered(1)
 
 
 def hops(move):
@@ -80,6 +81,8 @@
     mine = pl.BlockSpec((tokens, part), lambda r, s: (0, 2 * (2 * (s[0] ^ 3) + s[1]) + r))
     piece = pl.BlockSpec((2, cols, part), lambda r, s: (0, 0, r))
 
+    held = pl.BlockSpec((tokens, columns), lambda r, s: (0, 0), pipeline_mode=ONCE)
+
     def whole(*shape):
         return pl.BlockSpec(shape, lambda r, s: (0, 0))
 
@@ -88,7 +91,7 @@
         grid_spec=pltpu.PrefetchScalarGridSpec(
             num_scalar_prefetch=1,
             grid=(2,),
-            in_specs=[mine, mine, whole(tokens, columns), whole(tokens, columns)],
+            in_specs=[mine, mine, held, held],
             out_specs=[piece, piece, whole(2 * tokens, columns), whole(columns, 2 * tokens)],
         ),
         out_shape=[jax.ShapeDtypeStruct((2, cols, rows), BF16)] * 2
@@ -96,7 +99,7 @@
             jax.ShapeDtypeStruct((2 * tokens, columns), BF16),
             jax.ShapeDtypeStruct((columns, 2 * tokens), BF16),
         ],
-        compiler_params=pltpu.CompilerParams(vmem_limit_bytes=VMEM),
+        compiler_params=pltpu.CompilerParams(vmem_limit_bytes=22 * MIB),
         cost_estimate=cost(4 * tokens * rows * columns, 4 * tokens * rows + 4 * rows * columns),
         name="terms",
     )(place, activations, other, cot_mine, cot_other)
@@ -132,7 +135,7 @@
         grid_spec=pltpu.PrefetchScalarGridSpec(
             num_scalar_prefetch=1,
             grid=(3, 2),
-            in_specs=[mine, mine, pl.BlockSpec(turned.shape, lambda i, r, s: (0, 0))],
+            in_specs=[mine, mine, pl.BlockSpec(turned.shape, lambda i, r, s: (0, 0), pipeline_mode=ONCE)],
             out_specs=pieces * 2,
         ),
         out_shape=[
@@ -140,7 +143,7 @@
             jax.ShapeDtypeStruct((2, 2, cols, rows), BF16),
         ]
         * 2,
-        compiler_params=pltpu.CompilerParams(vmem_limit_bytes=VMEM),
+        compiler_params=pltpu.CompilerParams(vmem_limit_bytes=16 * MIB),
         cost_estimate=cost(12 * tokens * rows * columns, 12 * tokens * rows + 12 * rows * columns),
         name="terms",
     )(place, activations, other, turned)
@@ -195,6 +198,8 @@
     def whole(*shape):
         return pl.BlockSpec(shape, lambda r, s: (0, 0))
 
+    held = pl.BlockSpec((2 * tokens, columns), lambda r, s: (0, 0), pipeline_mode=ONCE)
+
     def out_at(r, s):
         own = 2 * (2 * (s[0] ^ k) + s[1]) + r
         received = 2 * (2 * (s[0] ^ (k - 1)) + 1 - s[1]) + r - 2
@@ -210,12 +215,12 @@
         grid_spec=pltpu.PrefetchScalarGridSpec(
             num_scalar_prefetch=1,
             grid=(2 if first else 4,),
-            in_specs=[mine, mine, whole(2 * tokens, columns), piece, piece]
+            in_specs=[mine, mine, held, piece, piece]
             + (
                 []
                 if first
                 else [
-                    whole(2 * tokens, columns),
+                    held,
                     pl.BlockSpec((tokens, part), lambda r, s: (0, jnp.maximum(r - 2, 0))),
                     pl.BlockSpec(memory_space=pl.ANY),
                 ]
@@ -233,7 +238,7 @@
         ]
         + ([one, one] if last else [jax.ShapeDtypeStruct((2 * tokens, columns), F32)]),
         input_output_aliases={} if first else {8: 0},
-        compiler_params=pltpu.CompilerParams(vmem_limit_bytes=VMEM),
+        compiler_params=pltpu.CompilerParams(vmem_limit_bytes=28 * MIB),
         cost_estimate=cost(
             8 * tokens * rows * columns,
             8 * tokens * rows + 2 * rows * columns + 8 * tokens * columns,
@@ -277,7 +282,7 @@
             jax.ShapeDtypeStruct((tokens, columns), BF16),
         ],
         input_output_aliases={4: 0},
-        compiler_params=pltpu.CompilerParams(vmem_limit_bytes=VMEM),
+        compiler_params=pltpu.CompilerParams(vmem_limit_bytes=10 * MIB),
         cost_estimate=cost(0, 4 * tokens * rows + 10 * tokens * columns),
         name="finish",
     )(place, got, keys_near, keys_far, whole)
@@ -301,7 +306,7 @@
     base_b = sent(base, FLIP_B)
 
     keep3, send3, cots, turned = first_terms(
-        place, after(activations, base), other, cotangent, cot_other, rows
+        place, activations, other, cotangent, cot_other, rows
     )
     got3 = sent(send3, FLIP_B)
     keep2, keep10, send2, send10 = terms(place, activations, other, turned, rows)

time: 184 us -> 166 us (0.902)
  Pallas kernels: 64.5 us -> 45.6 us
  other arithmetic: 26.2 us -> 13.7 us
  starting transfers between devices: 36.2 us -> 47.9 us
  waiting for transfers between devices: 50.5 us -> 52.4 us
    pallas_call x4, Pallas kernels: 43.4 us -> 29.9 us  [projected(): pl.pallas_call(lambda *refs: project_kernel(*refs, first=first, last=last...]
    ppermute x26, starting transfers between devices: 36.2 us -> 47.9 us  [sent(): return lax.ppermute(array, AXES, pairs)]
    convert_element_type x4, other arithmetic: 13.3 us -> 7.88 us  [added(): return total.astype(BF16)]
    add x1, other arithmetic: 2.78 us -> 0.27 us  [by_hops(): three = mid + three_end]
    pallas_call x1, Pallas kernels: 10.9 us -> 8.49 us  [terms(): pl.pallas_call(term_kernel, grid_spec=pltpu.PrefetchScalarGridSpec(num_sc...]
    add x1, other arithmetic: 2.56 us -> 0.27 us  [by_hops(): two = two_mid + two_end]
    pallas_call x1, Pallas kernels: 6.49 us -> 4.49 us  [first_terms(): pl.pallas_call(first_term_kernel, grid_spec=pltpu.PrefetchScalarGridSpec(...]
    ppermute x26, waiting for transfers between devices: 50.5 us -> 52.4 us  [sent(): return lax.ppermute(array, AXES, pairs)]
  transfers between devices with their start and end apart: 26 -> 26, of which waited for: 9 -> 7; matrix products, arithmetic and copies ran while one was open for 15% -> 10% of each run, Pallas kernels for 33% -> 26%
where the time goes in v7:
time: 166 us; the launch traced here: 165 us
  waiting for transfers between devices  52.4 us (32%)
  starting transfers between devices  47.9 us (29%)
  Pallas kernels  45.6 us (27%)
  other arithmetic  13.7 us (8%)
  local copies, waits for them, and re-layouts  4.84 us (3%)
    ppermute x26, waiting for transfers between devices, sent(): return lax.ppermute(array, AXES, pairs)  52.4 us
    ppermute x26, starting transfers between devices, sent(): return lax.ppermute(array, AXES, pairs)  47.9 us
    pallas_call x4, Pallas kernels, projected(): pl.pallas_call(lambda *refs: project_kernel(*refs, first=first, last=last...  29.9 us
    pallas_call x1, Pallas kernels, terms(): pl.pallas_call(term_kernel, grid_spec=pltpu.PrefetchScalarGridSpec(num_sc...  8.49 us
    convert_element_type x4, other arithmetic, added(): return total.astype(BF16)  7.88 us
    unnamed x15, local copies, waits for them, and re-layouts  4.84 us
    pallas_call x1, Pallas kernels, first_terms(): pl.pallas_call(first_term_kernel, grid_spec=pltpu.PrefetchScalarGridSpec(...  4.49 us
  transfers between devices with their start and end apart: 26, of which 7 were waited for; matrix products, arithmetic and copies ran while one was open for 10% of the time, Pallas kernels for 26%

profile of v7, /device:TPU:0, one launch (start us, length us, event | category | flops | bytes accessed | tf_op | source)
XLA Modules:
  0.0 165.4 jit_solution(15380438988308000793)
XLA Ops:
  0.6 0.5 collective-permute-start
  1.2 0.1 collective-permute-start.1
  1.2 2.9 %collective-permute-start.3 = (bf16[1024,256]{1,0:T(8,128)(2,1)}, bf16[1024,256]{1,0:T(8,128)(2,1)S(1)}, u32[]{:S(2)}, u32[]{:S(2)}) collective-permute-start(bf16[1024,256]{1,0:T(8,128)(2,1)} %param.5), channel_id=1, source_target_pairs={{0,8},{1,17},{2,10},{3,19},{4,12},{5,21},{6,14},{7,23},{8,0},{9,25... | collective-permute-start | bytes 1572872 | tf_op jit(solution)/shard_map/ppermute | solution.py:46
  4.2 7.4 %collective-permute-done.3 = bf16[1024,256]{1,0:T(8,128)(2,1)S(1)} collective-permute-done((bf16[1024,256]{1,0:T(8,128)(2,1)}, bf16[1024,256]{1,0:T(8,128)(2,1)S(1)}, u32[]{:S(2)}, u32[]{:S(2)}) %collective-permute-start.3) | collective-permute-done | bytes 524320 | tf_op jit(solution)/shard_map/ppermute | solution.py:46
  11.5 1.1 pad_maximum_fusion.refs_4_
  12.7 0.7 collective-permute-start.8
  13.4 4.9 %collective-permute-start.7 = (bf16[2,1024,256]{2,1,0:T(8,128)(2,1)S(1)}, bf16[2,1024,256]{2,1,0:T(8,128)(2,1)S(1)}, u32[]{:S(2)}, u32[]{:S(2)}) collective-permute-start(bf16[2,1024,256]{2,1,0:T(8,128)(2,1)S(1)} %pad_maximum_fusion.refs_4_), channel_id=1, source_target_pairs={{0,2},{1,3},{2,0},{3,1},{4,6},{5,7},{6,4},{7,5},{8,10},{9,11},{10,... | collective-permute-start | bytes 3145736 | tf_op jit(solution)/shard_map/ppermute | solution.py:46
  18.3 0.1 pad_add_fusion.place.refs_0_
  18.4 1.5 collective-permute-start.4
  20.0 2.8 %copy-done = bf16[384,8192]{1,0:T(8,128)(2,1)S(1)} copy-done((bf16[384,8192]{1,0:T(8,128)(2,1)S(1)}, bf16[384,8192]{1,0:T(8,128)(2,1)}, u32[]{:S(2)}) %copy-start) | copy-done | bytes 6291480
  22.7 4.5 %terms.2 = (bf16[2,256,1024]{2,1,0:T(8,128)(2,1)S(1)}, bf16[2,256,1024]{2,1,0:T(8,128)(2,1)S(1)}, bf16[768,1024]{1,0:T(8,128)(2,1)S(1)}, bf16[1024,768]{1,0:T(8,128)(2,1)S(1)}) custom-call(s32[3]{0:T(128)S(1)} %pad_add_fusion.place.refs_0_, bf16[384,8192]{1,0:T(8,128)(2,1)S(1)} %copy-done, bf16[384,8192]{1,0:T(8,128)(2,1)} %collective-permute-done.other.refs_2_, ...), custom_call_target="tpu_custom_call" | custom-call | flops 1610612 | bytes 5767 | tf_op jit(solution)/shard_map/terms/pallas_call | solution.py:89
  27.2 0.6 collective-permute-start.2
  27.8 12.8 %collective-permute-done.7.refs_4_ = bf16[2,1024,256]{2,1,0:T(8,128)(2,1)S(1)} collective-permute-done((bf16[2,1024,256]{2,1,0:T(8,128)(2,1)S(1)}, bf16[2,1024,256]{2,1,0:T(8,128)(2,1)S(1)}, u32[]{:S(2)}, u32[]{:S(2)}) %collective-permute-start.7) | collective-permute-done | bytes 1048608 | tf_op jit(solution)/shard_map/ppermute | solution.py:46
  40.6 0.7 collective-permute-start.10
  41.3 8.5 %terms.3 = (bf16[2,256,1024]{2,1,0:T(8,128)(2,1)S(1)}, bf16[2,2,256,1024]{3,2,1,0:T(8,128)(2,1)S(1)}, bf16[2,256,1024]{2,1,0:T(8,128)(2,1)S(1)}, bf16[2,2,256,1024]{3,2,1,0:T(8,128)(2,1)S(1)}) custom-call(s32[3]{0:T(128)S(1)} %pad_add_fusion.place.refs_0_, bf16[384,8192]{1,0:T(8,128)(2,1)S(1)} %copy-done.1, ...), custom_call_target="tpu_custom_call" | custom-call | flops 4831838 | bytes 17301 | tf_op jit(solution)/shard_map/terms/pallas_call | solution.py:133
  49.9 1.6 collective-permute-start.5
  51.4 1.3 collective-permute-start.11
  52.7 0.4 add_convert_fusion.3
  53.1 6.4 %collective-permute-start.9 = (bf16[2,256,1024]{2,1,0:T(8,128)(2,1)S(1)}, bf16[2,256,1024]{2,1,0:T(8,128)(2,1)}, u32[]{:S(2)}, u32[]{:S(2)}) collective-permute-start(bf16[2,256,1024]{2,1,0:T(8,128)(2,1)S(1)} %add_convert_fusion.3), channel_id=1, source_target_pairs={{0,2},{1,3},{6,4},{7,5},{8,10},{9,11},{14,12},{15,13},{16,18},{17,... | collective-permute-start | bytes 3145736 | tf_op jit(solution)/shard_map/ppermute | solution.py:46
  59.6 1.3 collective-permute-start.13
  60.9 3.9 %collective-permute-done.5 = bf16[2,256,1024]{2,1,0:T(8,128)(2,1)S(1)} collective-permute-done((bf16[2,256,1024]{2,1,0:T(8,128)(2,1)S(1)}, bf16[2,256,1024]{2,1,0:T(8,128)(2,1)S(1)}, u32[]{:S(2)}, u32[]{:S(2)}) %collective-permute-start.5) | collective-permute-done | bytes 1048608 | tf_op jit(solution)/shard_map/ppermute | solution.py:46
  64.7 1.5 collective-permute-start.6
  66.2 13.9 %collective-permute-done.11 = bf16[2,1024,256]{2,1,0:T(8,128)(2,1)S(1)} collective-permute-done((bf16[2,1024,256]{2,1,0:T(8,128)(2,1)S(1)}, bf16[2,1024,256]{2,1,0:T(8,128)(2,1)S(1)}, u32[]{:S(2)}, u32[]{:S(2)}) %collective-permute-start.11) | collective-permute-done | bytes 1048608 | tf_op jit(solution)/shard_map/ppermute | solution.py:46
  80.1 0.3 add.58.refs_4_
  80.4 6.5 %project.4 = (bf16[384,8192]{1,0:T(8,128)(2,1)}, bf16[384,1024]{1,0:T(8,128)(2,1)S(1)}, f32[768,1024]{1,0:T(8,128)S(1)}) custom-call(s32[3]{0:T(128)S(1)} %pad_add_fusion.place.refs_0_, bf16[384,8192]{1,0:T(8,128)(2,1)S(1)} %copy-done.1, bf16[384,8192]{1,0:T(8,128)(2,1)} %collective-permute-done.other.refs_2_, ...), custom_call_target="tpu_custom_call" | custom-call | flops 3221225 | bytes 8388 | tf_op jit(solution)/shard_map/project/pallas_call | solution.py:213
  86.9 0.5 collective-permute-start.14
  87.4 3.2 %add_convert_fusion = (bf16[2,256,1024]{2,1,0:T(8,128)(2,1)S(1)}, bf16[2,256,1024]{2,1,0:T(8,128)(2,1)}) fusion(bf16[2,256,1024]{2,1,0:T(8,128)(2,1)} %collective-permute-done.9, bf16[2,256,1024]{2,1,0:T(8,128)(2,1)} %copy-done.4, bf16[2,256,1024]{2,1,0:T(8,128)(2,1)S(1)} %get-tuple-element.50), kind=kLoop, calls=%fused_computation.2 | loop fusion | flops 4194304 | bytes 5242880 | tf_op jit(solution)/shard_map/convert_element_type | solution.py:295
  90.7 2.5 %collective-permute-start.12 = (bf16[2,256,1024]{2,1,0:T(8,128)(2,1)}, bf16[2,256,1024]{2,1,0:T(8,128)(2,1)}, u32[]{:S(2)}, u32[]{:S(2)}) collective-permute-start(bf16[2,256,1024]{2,1,0:T(8,128)(2,1)} %get-tuple-element.56), channel_id=1, source_target_pairs={{0,2},{1,3},{6,4},{7,5},{8,10},{9,11},{14,12},{15,13},{16,18},{17,... | collective-permute-start | bytes 3145736 | tf_op jit(solution)/shard_map/ppermute | solution.py:46
  93.2 6.1 %collective-permute-done.13 = bf16[2,1024,256]{2,1,0:T(8,128)(2,1)S(1)} collective-permute-done((bf16[2,1024,256]{2,1,0:T(8,128)(2,1)S(1)}, bf16[2,1024,256]{2,1,0:T(8,128)(2,1)S(1)}, u32[]{:S(2)}, u32[]{:S(2)}) %collective-permute-start.13) | collective-permute-done | bytes 1048608 | tf_op jit(solution)/shard_map/ppermute | solution.py:46
  99.3 1.7 collective-permute-start.19
  101.0 0.3 add.59.refs_4_
  101.3 0.7 collective-permute-done.14.refs_5_
  102.0 1.5 collective-permute-start.17
  103.5 7.5 %project.5 = (bf16[384,8192]{1,0:T(8,128)(2,1)}, bf16[384,1024]{1,0:T(8,128)(2,1)S(1)}, f32[768,1024]{1,0:T(8,128)S(1)}) custom-call(s32[3]{0:T(128)S(1)} %pad_add_fusion.place.refs_0_, bf16[384,8192]{1,0:T(8,128)(2,1)S(1)} %copy-done.1, bf16[384,8192]{1,0:T(8,128)(2,1)} %collective-permute-done.other.refs_2_, ...), custom_call_target="tpu_custom_call", output_to_operand_aliasing={{0}: (8, {})} | custom-call | flops 3221225 | bytes 8388 | tf_op jit(solution)/shard_map/project/pallas_call | solution.py:213
  111.0 1.6 add_convert_fusion.1
  112.7 0.9 collective-permute-start.16
  113.6 2.6 %fusion = bf16[2,256,1024]{2,1,0:T(8,128)(2,1)S(1)} fusion(bf16[2,256,1024]{2,1,0:T(8,128)(2,1)} %collective-permute-done.19, bf16[2,2,256,1024]{3,2,1,0:T(8,128)(2,1)S(1)} %collective-permute-done.6, bf16[2,2,256,1024]{3,2,1,0:T(8,128)(2,1)S(1)} %get-tuple-element.43), kind=kLoop, calls=%fused_computation.1 | loop fusion | flops 3145728 | bytes 4194304 | tf_op jit(solution)/shard_map/convert_element_type | solution.py:295
  116.2 10.1 %collective-permute-start.20 = (bf16[2,256,1024]{2,1,0:T(8,128)(2,1)S(1)}, bf16[2,256,1024]{2,1,0:T(8,128)(2,1)S(1)}, u32[]{:S(2)}, u32[]{:S(2)}) collective-permute-start(bf16[2,256,1024]{2,1,0:T(8,128)(2,1)S(1)} %fusion), channel_id=1, source_target_pairs={{0,2},{1,3},{2,0},{3,1},{4,6},{5,7},{6,4},{7,5},{8,10},{9,11},{10,... | collective-permute-start | bytes 3145736 | tf_op jit(solution)/shard_map/ppermute | solution.py:46
  126.3 4.6 %collective-permute-start.21 = (bf16[2,1024,256]{2,1,0:T(8,128)(2,1)S(1)}, bf16[2,1024,256]{2,1,0:T(8,128)(2,1)S(1)}, u32[]{:S(2)}, u32[]{:S(2)}) collective-permute-start(bf16[2,1024,256]{2,1,0:T(8,128)(2,1)S(1)} %add.59.refs_4_), channel_id=1, source_target_pairs={{0,16},{1,9},{2,18},{3,11},{4,20},{5,13},{6,22},{7,15},{8,24},{9,1... | collective-permute-start | bytes 3145736 | tf_op jit(solution)/shard_map/ppermute | solution.py:46
  130.9 7.5 %project.6 = (bf16[384,8192]{1,0:T(8,128)(2,1)}, bf16[384,1024]{1,0:T(8,128)(2,1)S(1)}, f32[768,1024]{1,0:T(8,128)S(1)}) custom-call(s32[3]{0:T(128)S(1)} %pad_add_fusion.place.refs_0_, bf16[384,8192]{1,0:T(8,128)(2,1)S(1)} %copy-done.1, bf16[384,8192]{1,0:T(8,128)(2,1)} %collective-permute-done.other.refs_2_, ...), custom_call_target="tpu_custom_call", output_to_operand_aliasing={{0}: (8, {})} | custom-call | flops 3221225 | bytes 8388 | tf_op jit(solution)/shard_map/project/pallas_call | solution.py:213
  138.4 7.6 %collective-permute-done.20 = bf16[2,256,1024]{2,1,0:T(8,128)(2,1)S(1)} collective-permute-done((bf16[2,256,1024]{2,1,0:T(8,128)(2,1)S(1)}, bf16[2,256,1024]{2,1,0:T(8,128)(2,1)S(1)}, u32[]{:S(2)}, u32[]{:S(2)}) %collective-permute-start.20) | collective-permute-done | bytes 1048608 | tf_op jit(solution)/shard_map/ppermute | solution.py:46
  146.0 1.8 %fusion.4 = bf16[256,1024]{1,0:T(8,128)(2,1)S(1)} fusion(bf16[2,2,256,1024]{3,2,1,0:T(8,128)(2,1)} %copy-done.3, bf16[2,256,1024]{2,1,0:T(8,128)(2,1)S(1)} %collective-permute-done.20, bf16[2,256,1024]{2,1,0:T(8,128)(2,1)S(1)} %collective-permute-done.16, bf16[2,2,256,1024]{3,2,1,0:T(8,128)(2,1)S(1)} %get-tuple-element.43), kind=kLoop, calls=%fused_computation.13 | loop fusion | flops 2097152 | bytes 2621440 | tf_op jit(solution)/shard_map/convert_element_type | solution.py:352
  147.8 1.6 collective-permute-start.24
  149.3 8.3 %project.7 = (bf16[384,8192]{1,0:T(8,128)(2,1)}, bf16[384,1024]{1,0:T(8,128)(2,1)}, f32[384,1024]{1,0:T(8,128)S(1)}, f32[384,1024]{1,0:T(8,128)}) custom-call(s32[3]{0:T(128)S(1)} %pad_add_fusion.place.refs_0_, bf16[384,8192]{1,0:T(8,128)(2,1)S(1)} %copy-done.1, ...), custom_call_target="tpu_custom_call", output_to_operand_aliasing={{0}: (8, {})} | custom-call | flops 3221225472 | bytes 8388608 | tf_op jit(solution)/shard_map/project/pallas_call | solution.py:213
  157.8 0.5 collective-permute-start.23
  158.3 2.3 %fusion.5 = bf16[1024,256]{0,1:T(8,128)(2,1)} fusion(bf16[256,1024]{1,0:T(8,128)(2,1)S(1)} %collective-permute-done.24, bf16[2,2,256,1024]{3,2,1,0:T(8,128)(2,1)} %copy-done.3, bf16[2,256,1024]{2,1,0:T(8,128)(2,1)S(1)} %copy-done.6, bf16[2,256,1024]{2,1,0:T(8,128)(2,1)S(1)} %collective-permute-done.16, bf16[2,2,256,1024]{3,2,1,0:T(8,128)(2,1)S(1)} %get-tuple-element.43), kind=kLoop, calls=%fused_computation.15 | loop fusion | flops 2883584 | bytes 3145728 | tf_op jit(solution)/shard_map/transpose | solution.py:355
  160.6 2.0 %copy.10 = bf16[1024,256]{1,0:T(8,128)(2,1)} copy(bf16[1024,256]{0,1:T(8,128)(2,1)} %fusion.5) | data formatting | bytes 1048576
  162.6 2.8 %finish.1 = (bf16[384,8192]{1,0:T(8,128)(2,1)}, bf16[384,1024]{1,0:T(8,128)(2,1)}) custom-call(s32[3]{0:T(128)S(1)} %pad_add_fusion.place.refs_0_, bf16[384,1024]{1,0:T(8,128)(2,1)} %collective-permute-done.23.got, f32[384,1024]{1,0:T(8,128)S(1)} %get-tuple-element.75.near, ...), custom_call_target="tpu_custom_call", output_to_operand_aliasing={{0}: (4, {})} | custom-call | bytes 5505 | tf_op jit(solution)/shard_map/finish/pallas_call | solution.py:264
  (36 shorter events, 0.2 us)
Async XLA Ops:
  0.6 19.3 %copy-start.2 = (bf16[384,1024]{1,0:T(8,128)(2,1)S(1)}, bf16[384,1024]{1,0:T(8,128)(2,1)}, u32[]{:S(2)}) copy-start(bf16[384,1024]{1,0:T(8,128)(2,1)} %cot_mine.1) | copy-start | bytes 2359300
  0.6 19.3 %collective-permute-start = (bf16[384,8192]{1,0:T(8,128)(2,1)}, bf16[384,8192]{1,0:T(8,128)(2,1)}, u32[]{:S(2)}, u32[]{:S(2)}) collective-permute-start(bf16[384,8192]{1,0:T(8,128)(2,1)} %refs_1_.3), channel_id=1, source_target_pairs={{0,1},{1,0},{2,3},{3,2},{4,5},{5,4},{6,7},{7,6},{8,9},{9,8},{10,11... | collective-permute-start | bytes 18874376 | tf_op jit(solution)/shard_map/ppermute | solution.py:46
  1.2 18.8 %collective-permute-start.1 = (bf16[384,1024]{1,0:T(8,128)(2,1)}, bf16[384,1024]{1,0:T(8,128)(2,1)S(1)}, u32[]{:S(2)}, u32[]{:S(2)}) collective-permute-start(bf16[384,1024]{1,0:T(8,128)(2,1)} %cot_mine.1), channel_id=1, source_target_pairs={{0,1},{1,0},{2,3},{3,2},{4,5},{5,4},{6,7},{7,6},{8,9},{9,8},{10,11... | collective-permute-start | bytes 2359304 | tf_op jit(solution)/shard_map/ppermute | solution.py:46
  1.2 10.3 %collective-permute-start.3 = (bf16[1024,256]{1,0:T(8,128)(2,1)}, bf16[1024,256]{1,0:T(8,128)(2,1)S(1)}, u32[]{:S(2)}, u32[]{:S(2)}) collective-permute-start(bf16[1024,256]{1,0:T(8,128)(2,1)} %param.5), channel_id=1, source_target_pairs={{0,8},{1,17},{2,10},{3,19},{4,12},{5,21},{6,14},{7,23},{8,0},{9,25... | collective-permute-start | bytes 1572872 | tf_op jit(solution)/shard_map/ppermute | solution.py:46
  12.7 15.1 %collective-permute-start.8 = (bf16[2,1024,256]{2,1,0:T(8,128)(2,1)S(1)}, bf16[2,1024,256]{2,1,0:T(8,128)(2,1)S(1)}, u32[]{:S(2)}, u32[]{:S(2)}) collective-permute-start(bf16[2,1024,256]{2,1,0:T(8,128)(2,1)S(1)} %pad_maximum_fusion.refs_4_), channel_id=1, source_target_pairs={{2,4},{3,5},{4,2},{5,3},{10,12},{11,13},{12,10},{13,11},{18,20},{1... | collective-permute-start | bytes 3145736 | tf_op jit(solution)/shard_map/ppermute | solution.py:46
  13.4 27.2 %collective-permute-start.7 = (bf16[2,1024,256]{2,1,0:T(8,128)(2,1)S(1)}, bf16[2,1024,256]{2,1,0:T(8,128)(2,1)S(1)}, u32[]{:S(2)}, u32[]{:S(2)}) collective-permute-start(bf16[2,1024,256]{2,1,0:T(8,128)(2,1)S(1)} %pad_maximum_fusion.refs_4_), channel_id=1, source_target_pairs={{0,2},{1,3},{2,0},{3,1},{4,6},{5,7},{6,4},{7,5},{8,10},{9,11},{10,... | collective-permute-start | bytes 3145736 | tf_op jit(solution)/shard_map/ppermute | solution.py:46
  18.4 31.4 %collective-permute-start.4 = (bf16[2,1024,256]{2,1,0:T(8,128)(2,1)S(1)}, bf16[2,1024,256]{2,1,0:T(8,128)(2,1)S(1)}, u32[]{:S(2)}, u32[]{:S(2)}) collective-permute-start(bf16[2,1024,256]{2,1,0:T(8,128)(2,1)S(1)} %pad_maximum_fusion.refs_4_), channel_id=1, source_target_pairs={{0,16},{1,9},{2,18},{3,11},{4,20},{5,13},{6,22},{7,15},{8,24},{9,1... | collective-permute-start | bytes 3145736 | tf_op jit(solution)/shard_map/ppermute | solution.py:46
  19.9 2.8 %copy-start = (bf16[384,8192]{1,0:T(8,128)(2,1)S(1)}, bf16[384,8192]{1,0:T(8,128)(2,1)}, u32[]{:S(2)}) copy-start(bf16[384,8192]{1,0:T(8,128)(2,1)} %refs_1_.3) | copy-start | bytes 18874372
  22.7 18.6 %copy-start.1 = (bf16[384,8192]{1,0:T(8,128)(2,1)S(1)}, bf16[384,8192]{1,0:T(8,128)(2,1)}, u32[]{:S(2)}) copy-start(bf16[384,8192]{1,0:T(8,128)(2,1)} %refs_1_.3) | copy-start | bytes 18874372
  27.2 22.6 %collective-permute-start.2 = (bf16[2,256,1024]{2,1,0:T(8,128)(2,1)S(1)}, bf16[2,256,1024]{2,1,0:T(8,128)(2,1)S(1)}, u32[]{:S(2)}, u32[]{:S(2)}) collective-permute-start(bf16[2,256,1024]{2,1,0:T(8,128)(2,1)S(1)} %get-tuple-element.46), channel_id=1, source_target_pairs={{0,16},{1,9},{2,18},{3,11},{4,20},{5,13},{6,22},{7,15},{8,24},{9,1... | collective-permute-start | bytes 3145736 | tf_op jit(solution)/shard_map/ppermute | solution.py:46
  40.6 19.0 %collective-permute-start.10 = (bf16[2,1024,256]{2,1,0:T(8,128)(2,1)S(1)}, bf16[2,1024,256]{2,1,0:T(8,128)(2,1)S(1)}, u32[]{:S(2)}, u32[]{:S(2)}) collective-permute-start(bf16[2,1024,256]{2,1,0:T(8,128)(2,1)S(1)} %collective-permute-done.7.refs_4_), channel_id=1, source_target_pairs={{2,4},{3,5},{4,2},{5,3},{10,12},{11,13},{12,10},{13,11},{18,20},{1... | collective-permute-start | bytes 3145736 | tf_op jit(solution)/shard_map/ppermute | solution.py:46
  49.9 14.9 %collective-permute-start.5 = (bf16[2,256,1024]{2,1,0:T(8,128)(2,1)S(1)}, bf16[2,256,1024]{2,1,0:T(8,128)(2,1)S(1)}, u32[]{:S(2)}, u32[]{:S(2)}) collective-permute-start(bf16[2,256,1024]{2,1,0:T(8,128)(2,1)S(1)} %get-tuple-element.47), channel_id=1, source_target_pairs={{0,16},{1,9},{2,18},{3,11},{4,20},{5,13},{6,22},{7,15},{8,24},{9,1... | collective-permute-start | bytes 3145736 | tf_op jit(solution)/shard_map/ppermute | solution.py:46
  51.4 28.7 %collective-permute-start.11 = (bf16[2,1024,256]{2,1,0:T(8,128)(2,1)S(1)}, bf16[2,1024,256]{2,1,0:T(8,128)(2,1)S(1)}, u32[]{:S(2)}, u32[]{:S(2)}) collective-permute-start(bf16[2,1024,256]{2,1,0:T(8,128)(2,1)S(1)} %collective-permute-done.8), channel_id=1, source_target_pairs={{2,0},{3,1},{4,6},{5,7},{10,8},{11,9},{12,14},{13,15},{18,16},{19,... | collective-permute-start | bytes 3145736 | tf_op jit(solution)/shard_map/ppermute | solution.py:46
  53.1 34.3 %collective-permute-start.9 = (bf16[2,256,1024]{2,1,0:T(8,128)(2,1)S(1)}, bf16[2,256,1024]{2,1,0:T(8,128)(2,1)}, u32[]{:S(2)}, u32[]{:S(2)}) collective-permute-start(bf16[2,256,1024]{2,1,0:T(8,128)(2,1)S(1)} %add_convert_fusion.3), channel_id=1, source_target_pairs={{0,2},{1,3},{6,4},{7,5},{8,10},{9,11},{14,12},{15,13},{16,18},{17,... | collective-permute-start | bytes 3145736 | tf_op jit(solution)/shard_map/ppermute | solution.py:46
  59.6 39.8 %collective-permute-start.13 = (bf16[2,1024,256]{2,1,0:T(8,128)(2,1)S(1)}, bf16[2,1024,256]{2,1,0:T(8,128)(2,1)S(1)}, u32[]{:S(2)}, u32[]{:S(2)}) collective-permute-start(bf16[2,1024,256]{2,1,0:T(8,128)(2,1)S(1)} %collective-permute-done.10), channel_id=1, source_target_pairs={{2,0},{3,1},{4,6},{5,7},{10,8},{11,9},{12,14},{13,15},{18,16},{19,... | collective-permute-start | bytes 3145736 | tf_op jit(solution)/shard_map/ppermute | solution.py:46
  64.7 15.7 %copy-start.4 = (bf16[2,256,1024]{2,1,0:T(8,128)(2,1)}, bf16[2,256,1024]{2,1,0:T(8,128)(2,1)S(1)}, u32[]{:S(2)}) copy-start(bf16[2,256,1024]{2,1,0:T(8,128)(2,1)S(1)} %collective-permute-done.5) | copy-start | bytes 3145732
  64.7 48.9 %collective-permute-start.6 = (bf16[2,2,256,1024]{3,2,1,0:T(8,128)(2,1)S(1)}, bf16[2,2,256,1024]{3,2,1,0:T(8,128)(2,1)S(1)}, u32[]{:S(2)}, u32[]{:S(2)}) collective-permute-start(bf16[2,2,256,1024]{3,2,1,0:T(8,128)(2,1)S(1)} %get-tuple-element.48), channel_id=1, source_target_pairs={{0,16},{1,9},{2,18},{3,11},{4,20},{5,13},{6,22},{7,15},{8,24},{9,1... | collective-permute-start | bytes 6291464 | tf_op jit(solution)/shard_map/ppermute | solution.py:46
  86.9 15.1 %collective-permute-start.14 = (bf16[2,1024,256]{2,1,0:T(8,128)(2,1)S(1)}, bf16[2,1024,256]{2,1,0:T(8,128)(2,1)S(1)}, u32[]{:S(2)}, u32[]{:S(2)}) collective-permute-start(bf16[2,1024,256]{2,1,0:T(8,128)(2,1)S(1)} %collective-permute-done.7.refs_4_), channel_id=1, source_target_pairs={{0,16},{1,9},{2,18},{3,11},{4,20},{5,13},{6,22},{7,15},{8,24},{9,1... | collective-permute-start | bytes 3145736 | tf_op jit(solution)/shard_map/ppermute | solution.py:46
  90.7 20.4 %collective-permute-start.12 = (bf16[2,256,1024]{2,1,0:T(8,128)(2,1)}, bf16[2,256,1024]{2,1,0:T(8,128)(2,1)}, u32[]{:S(2)}, u32[]{:S(2)}) collective-permute-start(bf16[2,256,1024]{2,1,0:T(8,128)(2,1)} %get-tuple-element.56), channel_id=1, source_target_pairs={{0,2},{1,3},{6,4},{7,5},{8,10},{9,11},{14,12},{15,13},{16,18},{17,... | collective-permute-start | bytes 3145736 | tf_op jit(solution)/shard_map/ppermute | solution.py:46
  93.2 10.3 %collective-permute-start.15 = (bf16[384,1024]{1,0:T(8,128)(2,1)S(1)}, bf16[384,1024]{1,0:T(8,128)(2,1)S(1)}, u32[]{:S(2)}, u32[]{:S(2)}) collective-permute-start(bf16[384,1024]{1,0:T(8,128)(2,1)S(1)} %get-tuple-element.55), channel_id=1, source_target_pairs={{0,1},{1,0},{2,3},{3,2},{4,5},{5,4},{6,7},{7,6},{8,9},{9,8},{10,11... | collective-permute-start | bytes 2359304 | tf_op jit(solution)/shard_map/ppermute | solution.py:46
  99.3 14.3 %collective-permute-start.19 = (bf16[2,256,1024]{2,1,0:T(8,128)(2,1)S(1)}, bf16[2,256,1024]{2,1,0:T(8,128)(2,1)}, u32[]{:S(2)}, u32[]{:S(2)}) collective-permute-start(bf16[2,256,1024]{2,1,0:T(8,128)(2,1)S(1)} %get-tuple-element.84), channel_id=1, source_target_pairs={{2,4},{3,5},{4,2},{5,3},{10,12},{11,13},{12,10},{13,11},{18,20},{1... | collective-permute-start | bytes 3145736 | tf_op jit(solution)/shard_map/ppermute | solution.py:46
  102.0 28.9 %collective-permute-start.17 = (bf16[2,1024,256]{2,1,0:T(8,128)(2,1)S(1)}, bf16[2,1024,256]{2,1,0:T(8,128)(2,1)S(1)}, u32[]{:S(2)}, u32[]{:S(2)}) collective-permute-start(bf16[2,1024,256]{2,1,0:T(8,128)(2,1)S(1)} %add.58.refs_4_), channel_id=1, source_target_pairs={{0,16},{1,9},{2,18},{3,11},{4,20},{5,13},{6,22},{7,15},{8,24},{9,1... | collective-permute-start | bytes 3145736 | tf_op jit(solution)/shard_map/ppermute | solution.py:46
  111.0 19.9 %collective-permute-start.18 = (bf16[384,1024]{1,0:T(8,128)(2,1)S(1)}, bf16[384,1024]{1,0:T(8,128)(2,1)S(1)}, u32[]{:S(2)}, u32[]{:S(2)}) collective-permute-start(bf16[384,1024]{1,0:T(8,128)(2,1)S(1)} %get-tuple-element.61), channel_id=1, source_target_pairs={{0,1},{1,0},{2,3},{3,2},{4,5},{5,4},{6,7},{7,6},{8,9},{9,8},{10,11... | collective-permute-start | bytes 2359304 | tf_op jit(solution)/shard_map/ppermute | solution.py:46
  112.7 25.8 %collective-permute-start.16 = (bf16[2,256,1024]{2,1,0:T(8,128)(2,1)S(1)}, bf16[2,256,1024]{2,1,0:T(8,128)(2,1)S(1)}, u32[]{:S(2)}, u32[]{:S(2)}) collective-permute-start(bf16[2,256,1024]{2,1,0:T(8,128)(2,1)S(1)} %add_convert_fusion.1), channel_id=1, source_target_pairs={{2,4},{3,5},{4,2},{5,3},{10,12},{11,13},{12,10},{13,11},{18,20},{1... | collective-permute-start | bytes 3145736 | tf_op jit(solution)/shard_map/ppermute | solution.py:46
  113.6 2.6 %copy-start.3 = (bf16[2,2,256,1024]{3,2,1,0:T(8,128)(2,1)}, bf16[2,2,256,1024]{3,2,1,0:T(8,128)(2,1)S(1)}, u32[]{:S(2)}) copy-start(bf16[2,2,256,1024]{3,2,1,0:T(8,128)(2,1)S(1)} %collective-permute-done.6) | copy-start | bytes 6291460
  116.2 29.7 %collective-permute-start.20 = (bf16[2,256,1024]{2,1,0:T(8,128)(2,1)S(1)}, bf16[2,256,1024]{2,1,0:T(8,128)(2,1)S(1)}, u32[]{:S(2)}, u32[]{:S(2)}) collective-permute-start(bf16[2,256,1024]{2,1,0:T(8,128)(2,1)S(1)} %fusion), channel_id=1, source_target_pairs={{0,2},{1,3},{2,0},{3,1},{4,6},{5,7},{6,4},{7,5},{8,10},{9,11},{10,... | collective-permute-start | bytes 3145736 | tf_op jit(solution)/shard_map/ppermute | solution.py:46
  126.3 23.0 %collective-permute-start.21 = (bf16[2,1024,256]{2,1,0:T(8,128)(2,1)S(1)}, bf16[2,1024,256]{2,1,0:T(8,128)(2,1)S(1)}, u32[]{:S(2)}, u32[]{:S(2)}) collective-permute-start(bf16[2,1024,256]{2,1,0:T(8,128)(2,1)S(1)} %add.59.refs_4_), channel_id=1, source_target_pairs={{0,16},{1,9},{2,18},{3,11},{4,20},{5,13},{6,22},{7,15},{8,24},{9,1... | collective-permute-start | bytes 3145736 | tf_op jit(solution)/shard_map/ppermute | solution.py:46
  138.4 10.9 %collective-permute-start.22 = (bf16[384,1024]{1,0:T(8,128)(2,1)S(1)}, bf16[384,1024]{1,0:T(8,128)(2,1)S(1)}, u32[]{:S(2)}, u32[]{:S(2)}) collective-permute-start(bf16[384,1024]{1,0:T(8,128)(2,1)S(1)} %get-tuple-element.67), channel_id=1, source_target_pairs={{0,1},{1,0},{2,3},{3,2},{4,5},{5,4},{6,7},{7,6},{8,9},{9,8},{10,11... | collective-permute-start | bytes 2359304 | tf_op jit(solution)/shard_map/ppermute | solution.py:46
  146.0 3.3 %copy-start.5 = (bf16[2,256,1024]{2,1,0:T(8,128)(2,1)}, bf16[2,256,1024]{2,1,0:T(8,128)(2,1)S(1)}, u32[]{:S(2)}) copy-start(bf16[2,256,1024]{2,1,0:T(8,128)(2,1)S(1)} %collective-permute-done.20) | copy-start | bytes 3145732
  147.8 9.9 %collective-permute-start.24 = (bf16[256,1024]{1,0:T(8,128)(2,1)S(1)}, bf16[256,1024]{1,0:T(8,128)(2,1)S(1)}, u32[]{:S(2)}, u32[]{:S(2)}) collective-permute-start(bf16[256,1024]{1,0:T(8,128)(2,1)S(1)} %fusion.4), channel_id=1, source_target_pairs={{0,8},{1,17},{2,10},{3,19},{4,12},{5,21},{6,14},{7,23},{8,0},{9,25... | collective-permute-start | bytes 1572872 | tf_op jit(solution)/shard_map/ppermute | solution.py:46
  149.3 8.9 %copy-start.6 = (bf16[2,256,1024]{2,1,0:T(8,128)(2,1)S(1)}, bf16[2,256,1024]{2,1,0:T(8,128)(2,1)}, u32[]{:S(2)}) copy-start(bf16[2,256,1024]{2,1,0:T(8,128)(2,1)} %copy-done.5) | copy-start | bytes 3145732
  157.7 4.9 %collective-permute-start.25 = (f32[384,1024]{1,0:T(8,128)}, f32[384,1024]{1,0:T(8,128)S(1)}, u32[]{:S(2)}, u32[]{:S(2)}) collective-permute-start(f32[384,1024]{1,0:T(8,128)} %get-tuple-element.77), channel_id=1, source_target_pairs={{0,1},{1,0},{2,3},{3,2},{4,5},{5,4},{6,7},{7,6},{8,9},{9,8},{10,11... | collective-permute-start | bytes 4718600 | tf_op jit(solution)/shard_map/ppermute | solution.py:46
  157.8 4.9 %collective-permute-start.23 = (bf16[384,1024]{1,0:T(8,128)(2,1)}, bf16[384,1024]{1,0:T(8,128)(2,1)}, u32[]{:S(2)}, u32[]{:S(2)}) collective-permute-start(bf16[384,1024]{1,0:T(8,128)(2,1)} %get-tuple-element.74), channel_id=1, source_target_pairs={{0,1},{1,0},{2,3},{3,2},{4,5},{5,4},{6,7},{7,6},{8,9},{9,8},{10,11... | collective-permute-start | bytes 2359304 | tf_op jit(solution)/shard_map/ppermute | solution.py:46

commit v8 on v7

--- a/solution.py
+++ b/solution.py
@@ -11,6 +11,7 @@
 AXES = ("blk", "chip", "core")
 SHRINK = 1000
 MIB = 2**20
+GATE = 10**7
 ONCE = pl.Buffered(1)
 
 
@@ -53,6 +54,23 @@
 
 def cost(flops, moved, shrink=SHRINK):
     return pl.CostEstimate(flops=flops // shrink, bytes_accessed=moved // shrink, transcendentals=0)
+
+
+def gate(place, *arrays):
+    def kernel(*refs):
+        for i in range(3):
+            refs[-1][i] = refs[0][i]
+
+    return pl.pallas_call(
+        kernel,
+        in_specs=[pl.BlockSpec(memory_space=pltpu.SMEM)]
+        + [pl.BlockSpec(memory_space=pl.ANY)] * len(arrays),
+        out_specs=pl.BlockSpec(memory_space=pltpu.SMEM),
+        out_shape=jax.ShapeDtypeStruct(place.shape, place.dtype),
+        compiler_params=pltpu.CompilerParams(vmem_limit_bytes=MIB),
+        cost_estimate=cost(0, GATE, 1),
+        name="gate",
+    )(place, *arrays)
 
 
 def first_term_kernel(place, mine, other, cot_mine, cot_other, keep, send, cots, turned):
@@ -251,18 +269,20 @@
     )
 
 
-def finish_kernel(place, got, near, far, whole, out, keys):
+def finish_kernel(place, got, near, far, last, arrived, whole, out, keys, weight, *, scale):
     out[...] = got[...]
     keys[...] = (near[...] + far[...]).astype(BF16)
-
-
-def finished(place, whole, got, keys_near, keys_far):
+    weight[...] = ((last[...] + arrived[...].astype(F32)) * scale).T.astype(BF16)
+
+
+def finished(place, whole, got, keys_near, keys_far, last, arrived, scale):
     tokens, rows = got.shape
-    columns = keys_near.shape[1]
+    cols, columns = last.shape[0], keys_near.shape[1]
     part, some = rows // 2, columns // 2
     wide = pl.BlockSpec((tokens, some), lambda r, s: (0, r))
+    flat = pl.BlockSpec((cols, part), lambda r, s: (0, r))
     return pl.pallas_call(
-        finish_kernel,
+        lambda *refs: finish_kernel(*refs, scale=scale),
         grid_spec=pltpu.PrefetchScalarGridSpec(
             num_scalar_prefetch=1,
             grid=(2,),
@@ -270,22 +290,26 @@
                 pl.BlockSpec((tokens, part), lambda r, s: (0, r)),
                 wide,
                 wide,
+                flat,
+                flat,
                 pl.BlockSpec(memory_space=pl.ANY),
             ],
             out_specs=[
                 pl.BlockSpec((tokens, part), lambda r, s: (0, 2 * (2 * (s[0] ^ 3) + 1 - s[1]) + r)),
                 wide,
+                pl.BlockSpec((part, cols), lambda r, s: (r, 0)),
             ],
         ),
         out_shape=[
             jax.ShapeDtypeStruct(whole.shape, BF16),
             jax.ShapeDtypeStruct((tokens, columns), BF16),
+            jax.ShapeDtypeStruct((rows, cols), BF16),
         ],
-        input_output_aliases={4: 0},
-        compiler_params=pltpu.CompilerParams(vmem_limit_bytes=10 * MIB),
+        input_output_aliases={6: 0},
+        compiler_params=pltpu.CompilerParams(vmem_limit_bytes=12 * MIB),
         cost_estimate=cost(0, 4 * tokens * rows + 10 * tokens * columns),
         name="finish",
-    )(place, got, keys_near, keys_far, whole)
+    )(place, got, keys_near, keys_far, last, arrived, whole)
 
 
 def added(*arrays):
@@ -310,31 +334,32 @@
     )
     got3 = sent(send3, FLIP_B)
     keep2, keep10, send2, send10 = terms(place, activations, other, turned, rows)
-    got2 = sent(after(send2, got3, base_b), FLIP_B)
-
-    sum3 = added(keep3, got3)
-    far = sent(after(sum3, one, mid), IN)
-    two_mid = sent(after(one, mid), MID)
+    first = gate(place, after(one, keep10), mid, base_b)
+    got2 = sent(after(send2, first, got3), FLIP_B)
+
+    sum3 = added(after(keep3, first), got3)
+    far = sent(sum3, IN)
+    two_mid = sent(after(one, first, keep10), MID)
     two_end = sent(mid, OUT)
-    one_b = sent(after(one, got2), FLIP_B)
-    got10 = sent(after(send10, got2), FLIP_B)
+    one_b = sent(after(one, got3), FLIP_B)
     whole, out, keys = projected(
-        place, 0, after(activations, keep10), other, cots, base, base_b
-    )
+        first, 0, after(activations, keep10), other, cots, base, base_b
+    )
+    got10 = sent(after(send10, got2, out), FLIP_B)
     got = sent(out, SWAP)
     sum2 = added(keep2, got2)
     two = two_mid + two_end
-    near = sent(after(sum2, far, two, out), IN)
+    near = sent(after(sum2, far, two, out, one_b), IN)
     mid_far = sent(added(sum2, far), MID)
-    three_end = sent(two_mid, OUT)
-    two_b = sent(after(two, one_b), FLIP_B)
+    three_end = sent(after(two_mid, out), OUT)
+    two_b = sent(after(two, got10), FLIP_B)
     whole, out, keys = projected(
         place, 1, after(activations, out), other, cots, one, one_b, (whole, None, keys), got
     )
     got = sent(out, SWAP)
 
     three = mid + three_end
-    three_b = sent(after(three, got10), FLIP_B)
+    three_b = sent(after(three, two_b), FLIP_B)
     sum_mid = sent(added(sum3, after(near, three, out)), MID)
     sum_one = sent(added(keep10[1], got10[1], mid_far), PAIR)
     whole, out, keys = projected(
@@ -351,14 +376,19 @@
     ]
     over = last[1].astype(BF16)
     arrived = sent(over, FLIP_A)
-    final = last[0] + arrived.astype(F32)
-    grad_weight = (final * (1.0 / math.sqrt(32 * tokens))).astype(BF16).T
 
     whole, out, keys, keys_far = projected(
         place, 3, after(activations, over), other, cots, three, three_b, (whole, None, keys), got
     )
-    grad_input, key_values = finished(
-        place, whole, sent(out, SWAP), keys, sent(after(keys_far, arrived), SWAP)
+    grad_input, key_values, grad_weight = finished(
+        place,
+        whole,
+        sent(out, SWAP),
+        keys,
+        sent(after(keys_far, arrived), SWAP),
+        last[0],
+        arrived,
+        1.0 / math.sqrt(32 * tokens),
     )
     return (key_values, grad_input, grad_weight)
 

time: 166 us -> 151 us (0.910)
  waiting for transfers between devices: 52.4 us -> 42.5 us
  other arithmetic: 13.7 us -> 11.1 us
  local copies, waits for them, and re-layouts: 4.84 us -> 2.79 us
    ppermute x26, waiting for transfers between devices: 52.4 us -> 42.5 us  [sent(): return lax.ppermute(array, AXES, pairs)]
    transpose x1 -> x0, other arithmetic: 2.32 us -> none  [by_hops(): grad_weight = (final * (1.0 / math.sqrt(32 * tokens))).astype(BF16).T]
    unnamed x15 -> x6, local copies, waits for them, and re-layouts: 4.84 us -> 2.79 us
    convert_element_type x1 -> x0, other arithmetic: 1.76 us -> none  [by_hops(): over = last[1].astype(BF16)]
    pallas_call x1 -> x2, Pallas kernels: 2.78 us -> 3.63 us  [the longest x1 2.49 us: finished(): pl.pallas_call(lambda *refs: finish_kernel(*refs, scale=scale), grid_spec...]
  transfers between devices with their start and end apart: 26 -> 26, of which waited for: 7 -> 8; matrix products, arithmetic and copies ran while one was open for 10% -> 7% of each run, Pallas kernels for 26% -> 29%
where the time goes in v8:
time: 151 us; the launch traced here: 150 us
  starting transfers between devices  47.3 us (31%)
  Pallas kernels  45.8 us (30%)
  waiting for transfers between devices  42.5 us (28%)
  other arithmetic  11.1 us (7%)
  local copies, waits for them, and re-layouts  2.79 us (2%)
    ppermute x26, starting transfers between devices, sent(): return lax.ppermute(array, AXES, pairs)  47.3 us
    ppermute x26, waiting for transfers between devices, sent(): return lax.ppermute(array, AXES, pairs)  42.5 us
    pallas_call x4, Pallas kernels, projected(): pl.pallas_call(lambda *refs: project_kernel(*refs, first=first, last=last...  29.2 us
    pallas_call x1, Pallas kernels, terms(): pl.pallas_call(term_kernel, grid_spec=pltpu.PrefetchScalarGridSpec(num_sc...  8.48 us
    convert_element_type x4, other arithmetic, added(): return total.astype(BF16)  7.18 us
    pallas_call x1, Pallas kernels, first_terms(): pl.pallas_call(first_term_kernel, grid_spec=pltpu.PrefetchScalarGridSpec(...  4.49 us
  transfers between devices with their start and end apart: 26, of which 8 were waited for; matrix products, arithmetic and copies ran while one was open for 7% of the time, Pallas kernels for 29%

profile of v8, /device:TPU:0, one launch (start us, length us, event | category | flops | bytes accessed | tf_op | source)
XLA Modules:
  0.0 150.3 jit_solution(16899731159291546066)
XLA Ops:
  0.6 0.5 collective-permute-start
  1.2 0.1 collective-permute-start.1
  1.2 2.9 %collective-permute-start.2 = (bf16[1024,256]{1,0:T(8,128)(2,1)}, bf16[1024,256]{1,0:T(8,128)(2,1)S(1)}, u32[]{:S(2)}, u32[]{:S(2)}) collective-permute-start(bf16[1024,256]{1,0:T(8,128)(2,1)} %param.5), channel_id=1, source_target_pairs={{0,8},{1,17},{2,10},{3,19},{4,12},{5,21},{6,14},{7,23},{8,0},{9,25... | collective-permute-start | bytes 1572872 | tf_op jit(solution)/shard_map/ppermute | solution.py:47
  4.2 0.1 pad_add_fusion.place.refs_0_
  4.2 7.3 %collective-permute-done.2 = bf16[1024,256]{1,0:T(8,128)(2,1)S(1)} collective-permute-done((bf16[1024,256]{1,0:T(8,128)(2,1)}, bf16[1024,256]{1,0:T(8,128)(2,1)S(1)}, u32[]{:S(2)}, u32[]{:S(2)}) %collective-permute-start.2) | collective-permute-done | bytes 524320 | tf_op jit(solution)/shard_map/ppermute | solution.py:47
  11.5 1.1 pad_maximum_fusion.refs_4_
  12.7 2.1 %collective-permute-start.5 = (bf16[2,1024,256]{2,1,0:T(8,128)(2,1)S(1)}, bf16[2,1024,256]{2,1,0:T(8,128)(2,1)S(1)}, u32[]{:S(2)}, u32[]{:S(2)}) collective-permute-start(bf16[2,1024,256]{2,1,0:T(8,128)(2,1)S(1)} %pad_maximum_fusion.refs_4_), channel_id=1, source_target_pairs={{0,16},{1,9},{2,18},{3,11},{4,20},{5,13},{6,22},{7,15},{8,24},{9,1... | collective-permute-start | bytes 3145736 | tf_op jit(solution)/shard_map/ppermute | solution.py:47
  14.8 1.6 %collective-permute-start.3 = (bf16[2,1024,256]{2,1,0:T(8,128)(2,1)S(1)}, bf16[2,1024,256]{2,1,0:T(8,128)(2,1)S(1)}, u32[]{:S(2)}, u32[]{:S(2)}) collective-permute-start(bf16[2,1024,256]{2,1,0:T(8,128)(2,1)S(1)} %pad_maximum_fusion.refs_4_), channel_id=1, source_target_pairs={{0,2},{1,3},{2,0},{3,1},{4,6},{5,7},{6,4},{7,5},{8,10},{9,11},{10,... | collective-permute-start | bytes 3145736 | tf_op jit(solution)/shard_map/ppermute | solution.py:47
  16.4 0.7 collective-permute-start.4
  17.1 2.8 %copy-done = bf16[384,8192]{1,0:T(8,128)(2,1)S(1)} copy-done((bf16[384,8192]{1,0:T(8,128)(2,1)S(1)}, bf16[384,8192]{1,0:T(8,128)(2,1)}, u32[]{:S(2)}) %copy-start) | copy-done | bytes 6291480
  19.9 4.5 %terms.2 = (bf16[2,256,1024]{2,1,0:T(8,128)(2,1)S(1)}, bf16[2,256,1024]{2,1,0:T(8,128)(2,1)S(1)}, bf16[768,1024]{1,0:T(8,128)(2,1)S(1)}, bf16[1024,768]{1,0:T(8,128)(2,1)S(1)}) custom-call(s32[3]{0:T(128)S(1)} %pad_add_fusion.place.refs_0_, bf16[384,8192]{1,0:T(8,128)(2,1)S(1)} %copy-done, bf16[384,8192]{1,0:T(8,128)(2,1)} %collective-permute-done.other.refs_2_, ...), custom_call_target="tpu_custom_call" | custom-call | flops 1610612 | bytes 5767 | tf_op jit(solution)/shard_map/terms/pallas_call | solution.py:107
  24.4 0.6 collective-permute-start.6
  25.0 8.5 %terms.3 = (bf16[2,256,1024]{2,1,0:T(8,128)(2,1)S(1)}, bf16[2,2,256,1024]{3,2,1,0:T(8,128)(2,1)S(1)}, bf16[2,256,1024]{2,1,0:T(8,128)(2,1)S(1)}, bf16[2,2,256,1024]{3,2,1,0:T(8,128)(2,1)S(1)}) custom-call(s32[3]{0:T(128)S(1)} %pad_add_fusion.place.refs_0_, bf16[384,8192]{1,0:T(8,128)(2,1)S(1)} %copy-done.1, ...), custom_call_target="tpu_custom_call" | custom-call | flops 4831838 | bytes 17301 | tf_op jit(solution)/shard_map/terms/pallas_call | solution.py:151
  33.5 5.3 %collective-permute-done.3.refs_1_.refs_4_ = bf16[2,1024,256]{2,1,0:T(8,128)(2,1)S(1)} collective-permute-done((bf16[2,1024,256]{2,1,0:T(8,128)(2,1)S(1)}, bf16[2,1024,256]{2,1,0:T(8,128)(2,1)S(1)}, u32[]{:S(2)}, u32[]{:S(2)}) %collective-permute-start.3) | collective-permute-done | bytes 1048608 | tf_op jit(solution)/shard_map/ppermute | solution.py:47
  38.8 1.1 gate.1.refs_0_
  39.9 1.6 %collective-permute-start.7 = (bf16[2,256,1024]{2,1,0:T(8,128)(2,1)S(1)}, bf16[2,256,1024]{2,1,0:T(8,128)(2,1)S(1)}, u32[]{:S(2)}, u32[]{:S(2)}) collective-permute-start(bf16[2,256,1024]{2,1,0:T(8,128)(2,1)S(1)} %get-tuple-element.51), channel_id=1, source_target_pairs={{0,16},{1,9},{2,18},{3,11},{4,20},{5,13},{6,22},{7,15},{8,24},{9,1... | collective-permute-start | bytes 3145736 | tf_op jit(solution)/shard_map/ppermute | solution.py:47
  41.5 1.3 collective-permute-start.11
  42.8 0.7 collective-permute-start.10
  43.5 0.4 add_convert_fusion.3
  44.0 11.4 %collective-permute-start.9 = (bf16[2,256,1024]{2,1,0:T(8,128)(2,1)S(1)}, bf16[2,256,1024]{2,1,0:T(8,128)(2,1)}, u32[]{:S(2)}, u32[]{:S(2)}) collective-permute-start(bf16[2,256,1024]{2,1,0:T(8,128)(2,1)S(1)} %add_convert_fusion.3), channel_id=1, source_target_pairs={{0,2},{1,3},{6,4},{7,5},{8,10},{9,11},{14,12},{15,13},{16,18},{17,... | collective-permute-start | bytes 3145736 | tf_op jit(solution)/shard_map/ppermute | solution.py:47
  55.3 0.5 collective-permute-start.12
  55.8 6.5 %project.4 = (bf16[384,8192]{1,0:T(8,128)(2,1)}, bf16[384,1024]{1,0:T(8,128)(2,1)S(1)}, f32[768,1024]{1,0:T(8,128)S(1)}) custom-call(s32[3]{0:T(128)S(1)} %gate.1.refs_0_, bf16[384,8192]{1,0:T(8,128)(2,1)S(1)} %copy-done.1, bf16[384,8192]{1,0:T(8,128)(2,1)} %collective-permute-done.other.refs_2_, bf16[768,1024]{1,0:T(8,128)(2,1)S(1)} %get-tuple-element.53.refs_3_, ...), custom_call_target="tpu_custom_call" | custom-call | flops 3221225 | bytes 8388 | tf_op jit(solution)/shard_map/project/pallas_call | solution.py:231
  62.3 1.5 %collective-permute-start.8 = (bf16[2,2,256,1024]{3,2,1,0:T(8,128)(2,1)S(1)}, bf16[2,2,256,1024]{3,2,1,0:T(8,128)(2,1)S(1)}, u32[]{:S(2)}, u32[]{:S(2)}) collective-permute-start(bf16[2,2,256,1024]{3,2,1,0:T(8,128)(2,1)S(1)} %get-tuple-element.55), channel_id=1, source_target_pairs={{0,16},{1,9},{2,18},{3,11},{4,20},{5,13},{6,22},{7,15},{8,24},{9,1... | collective-permute-start | bytes 6291464 | tf_op jit(solution)/shard_map/ppermute | solution.py:47
  63.8 1.3 collective-permute-start.14
  65.1 2.2 %collective-permute-done.11 = bf16[2,1024,256]{2,1,0:T(8,128)(2,1)} collective-permute-done((bf16[2,1024,256]{2,1,0:T(8,128)(2,1)S(1)}, bf16[2,1024,256]{2,1,0:T(8,128)(2,1)}, u32[]{:S(2)}, u32[]{:S(2)}) %collective-permute-start.11) | collective-permute-done | bytes 1048608 | tf_op jit(solution)/shard_map/ppermute | solution.py:47
  67.3 1.5 %add.55.refs_4_ = bf16[2,1024,256]{2,1,0:T(8,128)(2,1)S(1)} add(bf16[2,1024,256]{2,1,0:T(8,128)(2,1)S(1)} %collective-permute-done.10, bf16[2,1024,256]{2,1,0:T(8,128)(2,1)} %collective-permute-done.11) | non-fusion elementwise | flops 524288 | bytes 3145728 | tf_op jit(solution)/shard_map/add | solution.py:351
  68.8 4.0 %collective-permute-done.9 = bf16[2,256,1024]{2,1,0:T(8,128)(2,1)} collective-permute-done((bf16[2,256,1024]{2,1,0:T(8,128)(2,1)S(1)}, bf16[2,256,1024]{2,1,0:T(8,128)(2,1)}, u32[]{:S(2)}, u32[]{:S(2)}) %collective-permute-start.9) | collective-permute-done | bytes 1048608 | tf_op jit(solution)/shard_map/ppermute | solution.py:47
  72.8 3.3 %add_convert_fusion = (bf16[2,256,1024]{2,1,0:T(8,128)(2,1)}, bf16[2,256,1024]{2,1,0:T(8,128)(2,1)}) fusion(bf16[2,256,1024]{2,1,0:T(8,128)(2,1)} %collective-permute-done.9, bf16[2,256,1024]{2,1,0:T(8,128)(2,1)S(1)} %collective-permute-done.7, bf16[2,256,1024]{2,1,0:T(8,128)(2,1)S(1)} %get-tuple-element.58), kind=kLoop, calls=%fused_computation.2 | loop fusion | flops 4194304 | bytes 5242880 | tf_op jit(solution)/shard_map/convert_element_type | solution.py:319
  76.1 5.5 %collective-permute-start.13 = (bf16[2,256,1024]{2,1,0:T(8,128)(2,1)}, bf16[2,256,1024]{2,1,0:T(8,128)(2,1)}, u32[]{:S(2)}, u32[]{:S(2)}) collective-permute-start(bf16[2,256,1024]{2,1,0:T(8,128)(2,1)} %get-tuple-element.61), channel_id=1, source_target_pairs={{0,2},{1,3},{6,4},{7,5},{8,10},{9,11},{14,12},{15,13},{16,18},{17,... | collective-permute-start | bytes 3145736 | tf_op jit(solution)/shard_map/ppermute | solution.py:47
  81.6 1.7 %collective-permute-start.19 = (bf16[2,256,1024]{2,1,0:T(8,128)(2,1)}, bf16[2,256,1024]{2,1,0:T(8,128)(2,1)}, u32[]{:S(2)}, u32[]{:S(2)}) collective-permute-start(bf16[2,256,1024]{2,1,0:T(8,128)(2,1)} %get-tuple-element.87), channel_id=1, source_target_pairs={{2,4},{3,5},{4,2},{5,3},{10,12},{11,13},{12,10},{13,11},{18,20},{1... | collective-permute-start | bytes 3145736 | tf_op jit(solution)/shard_map/ppermute | solution.py:47
  83.3 8.8 %collective-permute-done.14 = bf16[2,1024,256]{2,1,0:T(8,128)(2,1)S(1)} collective-permute-done((bf16[2,1024,256]{2,1,0:T(8,128)(2,1)S(1)}, bf16[2,1024,256]{2,1,0:T(8,128)(2,1)S(1)}, u32[]{:S(2)}, u32[]{:S(2)}) %collective-permute-start.14) | collective-permute-done | bytes 1048608 | tf_op jit(solution)/shard_map/ppermute | solution.py:47
  92.1 0.3 add.56.refs_4_
  92.4 7.5 %project.5 = (bf16[384,8192]{1,0:T(8,128)(2,1)}, bf16[384,1024]{1,0:T(8,128)(2,1)S(1)}, f32[768,1024]{1,0:T(8,128)S(1)}) custom-call(s32[3]{0:T(128)S(1)} %pad_add_fusion.place.refs_0_, bf16[384,8192]{1,0:T(8,128)(2,1)S(1)} %copy-done.1, bf16[384,8192]{1,0:T(8,128)(2,1)} %collective-permute-done.other.refs_2_, ...), custom_call_target="tpu_custom_call", output_to_operand_aliasing={{0}: (8, {})} | custom-call | flops 3221225 | bytes 8388 | tf_op jit(solution)/shard_map/project/pallas_call | solution.py:231
  99.9 4.7 %collective-permute-start.17 = (bf16[2,1024,256]{2,1,0:T(8,128)(2,1)S(1)}, bf16[2,1024,256]{2,1,0:T(8,128)(2,1)S(1)}, u32[]{:S(2)}, u32[]{:S(2)}) collective-permute-start(bf16[2,1024,256]{2,1,0:T(8,128)(2,1)S(1)} %add.55.refs_4_), channel_id=1, source_target_pairs={{0,16},{1,9},{2,18},{3,11},{4,20},{5,13},{6,22},{7,15},{8,24},{9,1... | collective-permute-start | bytes 3145736 | tf_op jit(solution)/shard_map/ppermute | solution.py:47
  104.6 1.6 %add_convert_fusion.1 = bf16[2,256,1024]{2,1,0:T(8,128)(2,1)S(1)} fusion(bf16[2,256,1024]{2,1,0:T(8,128)(2,1)} %collective-permute-done.13, bf16[2,256,1024]{2,1,0:T(8,128)(2,1)S(1)} %add_convert_fusion.3), kind=kLoop, calls=%fused_computation.3 | loop fusion | flops 2097152 | bytes 3145728 | tf_op jit(solution)/shard_map/convert_element_type | solution.py:319
  106.3 0.9 collective-permute-start.16
  107.2 1.9 %fusion = bf16[2,256,1024]{2,1,0:T(8,128)(2,1)S(1)} fusion(bf16[2,256,1024]{2,1,0:T(8,128)(2,1)} %collective-permute-done.19, bf16[2,2,256,1024]{3,2,1,0:T(8,128)(2,1)S(1)} %collective-permute-done.8, bf16[2,2,256,1024]{3,2,1,0:T(8,128)(2,1)S(1)} %get-tuple-element.46), kind=kLoop, calls=%fused_computation.1 | loop fusion | flops 3145728 | bytes 4194304 | tf_op jit(solution)/shard_map/convert_element_type | solution.py:319
  109.0 3.4 %collective-permute-start.20 = (bf16[2,256,1024]{2,1,0:T(8,128)(2,1)S(1)}, bf16[2,256,1024]{2,1,0:T(8,128)(2,1)S(1)}, u32[]{:S(2)}, u32[]{:S(2)}) collective-permute-start(bf16[2,256,1024]{2,1,0:T(8,128)(2,1)S(1)} %fusion), channel_id=1, source_target_pairs={{0,2},{1,3},{2,0},{3,1},{4,6},{5,7},{6,4},{7,5},{8,10},{9,11},{10,... | collective-permute-start | bytes 3145736 | tf_op jit(solution)/shard_map/ppermute | solution.py:47
  112.4 5.0 %collective-permute-done.17.refs_5_ = bf16[2,1024,256]{2,1,0:T(8,128)(2,1)S(1)} collective-permute-done((bf16[2,1024,256]{2,1,0:T(8,128)(2,1)S(1)}, bf16[2,1024,256]{2,1,0:T(8,128)(2,1)S(1)}, u32[]{:S(2)}, u32[]{:S(2)}) %collective-permute-start.17) | collective-permute-done | bytes 1048608 | tf_op jit(solution)/shard_map/ppermute | solution.py:47
  117.4 2.0 %collective-permute-start.21 = (bf16[2,1024,256]{2,1,0:T(8,128)(2,1)S(1)}, bf16[2,1024,256]{2,1,0:T(8,128)(2,1)S(1)}, u32[]{:S(2)}, u32[]{:S(2)}) collective-permute-start(bf16[2,1024,256]{2,1,0:T(8,128)(2,1)S(1)} %add.56.refs_4_), channel_id=1, source_target_pairs={{0,16},{1,9},{2,18},{3,11},{4,20},{5,13},{6,22},{7,15},{8,24},{9,1... | collective-permute-start | bytes 3145736 | tf_op jit(solution)/shard_map/ppermute | solution.py:47
  119.4 7.5 %project.6 = (bf16[384,8192]{1,0:T(8,128)(2,1)}, bf16[384,1024]{1,0:T(8,128)(2,1)S(1)}, f32[768,1024]{1,0:T(8,128)S(1)}) custom-call(s32[3]{0:T(128)S(1)} %pad_add_fusion.place.refs_0_, bf16[384,8192]{1,0:T(8,128)(2,1)S(1)} %copy-done.1, bf16[384,8192]{1,0:T(8,128)(2,1)} %collective-permute-done.other.refs_2_, ...), custom_call_target="tpu_custom_call", output_to_operand_aliasing={{0}: (8, {})} | custom-call | flops 3221225 | bytes 8388 | tf_op jit(solution)/shard_map/project/pallas_call | solution.py:231
  127.0 5.8 %collective-permute-done.20 = bf16[2,256,1024]{2,1,0:T(8,128)(2,1)S(1)} collective-permute-done((bf16[2,256,1024]{2,1,0:T(8,128)(2,1)S(1)}, bf16[2,256,1024]{2,1,0:T(8,128)(2,1)S(1)}, u32[]{:S(2)}, u32[]{:S(2)}) %collective-permute-start.20) | collective-permute-done | bytes 1048608 | tf_op jit(solution)/shard_map/ppermute | solution.py:47
  132.8 0.9 convert_add_fusion
  133.7 1.8 %collective-permute-start.24 = (bf16[256,1024]{1,0:T(8,128)(2,1)S(1)}, bf16[256,1024]{1,0:T(8,128)(2,1)S(1)}, u32[]{:S(2)}, u32[]{:S(2)}) collective-permute-start(bf16[256,1024]{1,0:T(8,128)(2,1)S(1)} %get-tuple-element.90), channel_id=1, source_target_pairs={{0,8},{1,17},{2,10},{3,19},{4,12},{5,21},{6,14},{7,23},{8,0},{9,25... | collective-permute-start | bytes 1572872 | tf_op jit(solution)/shard_map/ppermute | solution.py:47
  135.5 7.7 %project.7 = (bf16[384,8192]{1,0:T(8,128)(2,1)}, bf16[384,1024]{1,0:T(8,128)(2,1)S(1)}, f32[384,1024]{1,0:T(8,128)S(1)}, f32[384,1024]{1,0:T(8,128)S(1)}) custom-call(s32[3]{0:T(128)S(1)} %pad_add_fusion.place.refs_0_, bf16[384,8192]{1,0:T(8,128)(2,1)S(1)} %copy-done.1, ...), custom_call_target="tpu_custom_call", output_to_operand_aliasing={{0}: (8, {})} | custom-call | flops 3221225472 | bytes 8388608 | tf_op jit(solution)/shard_map/project/pallas_call | solution.py:231
  143.1 0.5 collective-permute-start.25
  143.7 4.1 %collective-permute-done.23.refs_1_ = bf16[384,1024]{1,0:T(8,128)(2,1)S(1)} collective-permute-done((bf16[384,1024]{1,0:T(8,128)(2,1)S(1)}, bf16[384,1024]{1,0:T(8,128)(2,1)S(1)}, u32[]{:S(2)}, u32[]{:S(2)}) %collective-permute-start.23) | collective-permute-done | bytes 786464 | tf_op jit(solution)/shard_map/ppermute | solution.py:47
  147.8 2.5 %finish.1 = (bf16[384,8192]{1,0:T(8,128)(2,1)}, bf16[384,1024]{1,0:T(8,128)(2,1)}, bf16[1024,256]{1,0:T(8,128)(2,1)}) custom-call(s32[3]{0:T(128)S(1)} %pad_add_fusion.place.refs_0_, bf16[384,1024]{1,0:T(8,128)(2,1)S(1)} %collective-permute-done.23.refs_1_, f32[384,1024]{1,0:T(8,128)S(1)} %get-tuple-element.80.refs_2_, ...), custom_call_target="tpu_custom_call", output_to_operand_aliasing={{0}: (6, {})} | custom-call | bytes 5505 | tf_op jit(solution)/shard_map/finish/pallas_call | solution.py:284
  (27 shorter events, 0.1 us)
Async XLA Ops:
  0.6 16.5 %copy-start.2 = (bf16[384,1024]{1,0:T(8,128)(2,1)S(1)}, bf16[384,1024]{1,0:T(8,128)(2,1)}, u32[]{:S(2)}) copy-start(bf16[384,1024]{1,0:T(8,128)(2,1)} %cot_mine.1) | copy-start | bytes 2359300
  0.6 16.5 %collective-permute-start = (bf16[384,8192]{1,0:T(8,128)(2,1)}, bf16[384,8192]{1,0:T(8,128)(2,1)}, u32[]{:S(2)}, u32[]{:S(2)}) collective-permute-start(bf16[384,8192]{1,0:T(8,128)(2,1)} %refs_1_.3), channel_id=1, source_target_pairs={{0,1},{1,0},{2,3},{3,2},{4,5},{5,4},{6,7},{7,6},{8,9},{9,8},{10,11... | collective-permute-start | bytes 18874376 | tf_op jit(solution)/shard_map/ppermute | solution.py:47
  1.2 15.9 %collective-permute-start.1 = (bf16[384,1024]{1,0:T(8,128)(2,1)}, bf16[384,1024]{1,0:T(8,128)(2,1)S(1)}, u32[]{:S(2)}, u32[]{:S(2)}) collective-permute-start(bf16[384,1024]{1,0:T(8,128)(2,1)} %cot_mine.1), channel_id=1, source_target_pairs={{0,1},{1,0},{2,3},{3,2},{4,5},{5,4},{6,7},{7,6},{8,9},{9,8},{10,11... | collective-permute-start | bytes 2359304 | tf_op jit(solution)/shard_map/ppermute | solution.py:47
  1.2 10.3 %collective-permute-start.2 = (bf16[1024,256]{1,0:T(8,128)(2,1)}, bf16[1024,256]{1,0:T(8,128)(2,1)S(1)}, u32[]{:S(2)}, u32[]{:S(2)}) collective-permute-start(bf16[1024,256]{1,0:T(8,128)(2,1)} %param.5), channel_id=1, source_target_pairs={{0,8},{1,17},{2,10},{3,19},{4,12},{5,21},{6,14},{7,23},{8,0},{9,25... | collective-permute-start | bytes 1572872 | tf_op jit(solution)/shard_map/ppermute | solution.py:47
  12.7 26.1 %collective-permute-start.5 = (bf16[2,1024,256]{2,1,0:T(8,128)(2,1)S(1)}, bf16[2,1024,256]{2,1,0:T(8,128)(2,1)S(1)}, u32[]{:S(2)}, u32[]{:S(2)}) collective-permute-start(bf16[2,1024,256]{2,1,0:T(8,128)(2,1)S(1)} %pad_maximum_fusion.refs_4_), channel_id=1, source_target_pairs={{0,16},{1,9},{2,18},{3,11},{4,20},{5,13},{6,22},{7,15},{8,24},{9,1... | collective-permute-start | bytes 3145736 | tf_op jit(solution)/shard_map/ppermute | solution.py:47
  14.8 24.0 %collective-permute-start.3 = (bf16[2,1024,256]{2,1,0:T(8,128)(2,1)S(1)}, bf16[2,1024,256]{2,1,0:T(8,128)(2,1)S(1)}, u32[]{:S(2)}, u32[]{:S(2)}) collective-permute-start(bf16[2,1024,256]{2,1,0:T(8,128)(2,1)S(1)} %pad_maximum_fusion.refs_4_), channel_id=1, source_target_pairs={{0,2},{1,3},{2,0},{3,1},{4,6},{5,7},{6,4},{7,5},{8,10},{9,11},{10,... | collective-permute-start | bytes 3145736 | tf_op jit(solution)/shard_map/ppermute | solution.py:47
  16.4 22.4 %collective-permute-start.4 = (bf16[2,1024,256]{2,1,0:T(8,128)(2,1)S(1)}, bf16[2,1024,256]{2,1,0:T(8,128)(2,1)S(1)}, u32[]{:S(2)}, u32[]{:S(2)}) collective-permute-start(bf16[2,1024,256]{2,1,0:T(8,128)(2,1)S(1)} %pad_maximum_fusion.refs_4_), channel_id=1, source_target_pairs={{2,4},{3,5},{4,2},{5,3},{10,12},{11,13},{12,10},{13,11},{18,20},{1... | collective-permute-start | bytes 3145736 | tf_op jit(solution)/shard_map/ppermute | solution.py:47
  17.1 2.8 %copy-start = (bf16[384,8192]{1,0:T(8,128)(2,1)S(1)}, bf16[384,8192]{1,0:T(8,128)(2,1)}, u32[]{:S(2)}) copy-start(bf16[384,8192]{1,0:T(8,128)(2,1)} %refs_1_.3) | copy-start | bytes 18874372
  19.9 5.1 %copy-start.1 = (bf16[384,8192]{1,0:T(8,128)(2,1)S(1)}, bf16[384,8192]{1,0:T(8,128)(2,1)}, u32[]{:S(2)}) copy-start(bf16[384,8192]{1,0:T(8,128)(2,1)} %refs_1_.3) | copy-start | bytes 18874372
  24.4 15.5 %collective-permute-start.6 = (bf16[2,256,1024]{2,1,0:T(8,128)(2,1)S(1)}, bf16[2,256,1024]{2,1,0:T(8,128)(2,1)S(1)}, u32[]{:S(2)}, u32[]{:S(2)}) collective-permute-start(bf16[2,256,1024]{2,1,0:T(8,128)(2,1)S(1)} %get-tuple-element.50), channel_id=1, source_target_pairs={{0,16},{1,9},{2,18},{3,11},{4,20},{5,13},{6,22},{7,15},{8,24},{9,1... | collective-permute-start | bytes 3145736 | tf_op jit(solution)/shard_map/ppermute | solution.py:47
  39.9 22.4 %collective-permute-start.7 = (bf16[2,256,1024]{2,1,0:T(8,128)(2,1)S(1)}, bf16[2,256,1024]{2,1,0:T(8,128)(2,1)S(1)}, u32[]{:S(2)}, u32[]{:S(2)}) collective-permute-start(bf16[2,256,1024]{2,1,0:T(8,128)(2,1)S(1)} %get-tuple-element.51), channel_id=1, source_target_pairs={{0,16},{1,9},{2,18},{3,11},{4,20},{5,13},{6,22},{7,15},{8,24},{9,1... | collective-permute-start | bytes 3145736 | tf_op jit(solution)/shard_map/ppermute | solution.py:47
  41.5 25.8 %collective-permute-start.11 = (bf16[2,1024,256]{2,1,0:T(8,128)(2,1)S(1)}, bf16[2,1024,256]{2,1,0:T(8,128)(2,1)}, u32[]{:S(2)}, u32[]{:S(2)}) collective-permute-start(bf16[2,1024,256]{2,1,0:T(8,128)(2,1)S(1)} %collective-permute-done.4.refs_2_), channel_id=1, source_target_pairs={{2,0},{3,1},{4,6},{5,7},{10,8},{11,9},{12,14},{13,15},{18,16},{19,... | collective-permute-start | bytes 3145736 | tf_op jit(solution)/shard_map/ppermute | solution.py:47
  42.8 21.0 %collective-permute-start.10 = (bf16[2,1024,256]{2,1,0:T(8,128)(2,1)S(1)}, bf16[2,1024,256]{2,1,0:T(8,128)(2,1)S(1)}, u32[]{:S(2)}, u32[]{:S(2)}) collective-permute-start(bf16[2,1024,256]{2,1,0:T(8,128)(2,1)S(1)} %collective-permute-done.3.refs_1_.refs_4_), channel_id=1, source_target_pairs={{2,4},{3,5},{4,2},{5,3},{10,12},{11,13},{12,10},{13,11},{18,20},{1... | collective-permute-start | bytes 3145736 | tf_op jit(solution)/shard_map/ppermute | solution.py:47
  44.0 28.9 %collective-permute-start.9 = (bf16[2,256,1024]{2,1,0:T(8,128)(2,1)S(1)}, bf16[2,256,1024]{2,1,0:T(8,128)(2,1)}, u32[]{:S(2)}, u32[]{:S(2)}) collective-permute-start(bf16[2,256,1024]{2,1,0:T(8,128)(2,1)S(1)} %add_convert_fusion.3), channel_id=1, source_target_pairs={{0,2},{1,3},{6,4},{7,5},{8,10},{9,11},{14,12},{15,13},{16,18},{17,... | collective-permute-start | bytes 3145736 | tf_op jit(solution)/shard_map/ppermute | solution.py:47
  55.3 20.8 %collective-permute-start.12 = (bf16[2,1024,256]{2,1,0:T(8,128)(2,1)S(1)}, bf16[2,1024,256]{2,1,0:T(8,128)(2,1)S(1)}, u32[]{:S(2)}, u32[]{:S(2)}) collective-permute-start(bf16[2,1024,256]{2,1,0:T(8,128)(2,1)S(1)} %collective-permute-done.3.refs_1_.refs_4_), channel_id=1, source_target_pairs={{0,16},{1,9},{2,18},{3,11},{4,20},{5,13},{6,22},{7,15},{8,24},{9,1... | collective-permute-start | bytes 3145736 | tf_op jit(solution)/shard_map/ppermute | solution.py:47
  62.3 37.6 %collective-permute-start.8 = (bf16[2,2,256,1024]{3,2,1,0:T(8,128)(2,1)S(1)}, bf16[2,2,256,1024]{3,2,1,0:T(8,128)(2,1)S(1)}, u32[]{:S(2)}, u32[]{:S(2)}) collective-permute-start(bf16[2,2,256,1024]{3,2,1,0:T(8,128)(2,1)S(1)} %get-tuple-element.55), channel_id=1, source_target_pairs={{0,16},{1,9},{2,18},{3,11},{4,20},{5,13},{6,22},{7,15},{8,24},{9,1... | collective-permute-start | bytes 6291464 | tf_op jit(solution)/shard_map/ppermute | solution.py:47
  63.8 28.2 %collective-permute-start.14 = (bf16[2,1024,256]{2,1,0:T(8,128)(2,1)S(1)}, bf16[2,1024,256]{2,1,0:T(8,128)(2,1)S(1)}, u32[]{:S(2)}, u32[]{:S(2)}) collective-permute-start(bf16[2,1024,256]{2,1,0:T(8,128)(2,1)S(1)} %collective-permute-done.10), channel_id=1, source_target_pairs={{2,0},{3,1},{4,6},{5,7},{10,8},{11,9},{12,14},{13,15},{18,16},{19,... | collective-permute-start | bytes 3145736 | tf_op jit(solution)/shard_map/ppermute | solution.py:47
  76.1 23.8 %collective-permute-start.13 = (bf16[2,256,1024]{2,1,0:T(8,128)(2,1)}, bf16[2,256,1024]{2,1,0:T(8,128)(2,1)}, u32[]{:S(2)}, u32[]{:S(2)}) collective-permute-start(bf16[2,256,1024]{2,1,0:T(8,128)(2,1)} %get-tuple-element.61), channel_id=1, source_target_pairs={{0,2},{1,3},{6,4},{7,5},{8,10},{9,11},{14,12},{15,13},{16,18},{17,... | collective-permute-start | bytes 3145736 | tf_op jit(solution)/shard_map/ppermute | solution.py:47
  81.6 10.8 %collective-permute-start.15 = (bf16[384,1024]{1,0:T(8,128)(2,1)S(1)}, bf16[384,1024]{1,0:T(8,128)(2,1)S(1)}, u32[]{:S(2)}, u32[]{:S(2)}) collective-permute-start(bf16[384,1024]{1,0:T(8,128)(2,1)S(1)} %get-tuple-element.54), channel_id=1, source_target_pairs={{0,1},{1,0},{2,3},{3,2},{4,5},{5,4},{6,7},{7,6},{8,9},{9,8},{10,11... | collective-permute-start | bytes 2359304 | tf_op jit(solution)/shard_map/ppermute | solution.py:47
  81.6 25.6 %collective-permute-start.19 = (bf16[2,256,1024]{2,1,0:T(8,128)(2,1)}, bf16[2,256,1024]{2,1,0:T(8,128)(2,1)}, u32[]{:S(2)}, u32[]{:S(2)}) collective-permute-start(bf16[2,256,1024]{2,1,0:T(8,128)(2,1)} %get-tuple-element.87), channel_id=1, source_target_pairs={{2,4},{3,5},{4,2},{5,3},{10,12},{11,13},{12,10},{13,11},{18,20},{1... | collective-permute-start | bytes 3145736 | tf_op jit(solution)/shard_map/ppermute | solution.py:47
  99.9 17.5 %collective-permute-start.17 = (bf16[2,1024,256]{2,1,0:T(8,128)(2,1)S(1)}, bf16[2,1024,256]{2,1,0:T(8,128)(2,1)S(1)}, u32[]{:S(2)}, u32[]{:S(2)}) collective-permute-start(bf16[2,1024,256]{2,1,0:T(8,128)(2,1)S(1)} %add.55.refs_4_), channel_id=1, source_target_pairs={{0,16},{1,9},{2,18},{3,11},{4,20},{5,13},{6,22},{7,15},{8,24},{9,1... | collective-permute-start | bytes 3145736 | tf_op jit(solution)/shard_map/ppermute | solution.py:47
  106.3 20.7 %collective-permute-start.16 = (bf16[2,256,1024]{2,1,0:T(8,128)(2,1)S(1)}, bf16[2,256,1024]{2,1,0:T(8,128)(2,1)S(1)}, u32[]{:S(2)}, u32[]{:S(2)}) collective-permute-start(bf16[2,256,1024]{2,1,0:T(8,128)(2,1)S(1)} %add_convert_fusion.1), channel_id=1, source_target_pairs={{2,4},{3,5},{4,2},{5,3},{10,12},{11,13},{12,10},{13,11},{18,20},{1... | collective-permute-start | bytes 3145736 | tf_op jit(solution)/shard_map/ppermute | solution.py:47
  109.0 23.7 %collective-permute-start.20 = (bf16[2,256,1024]{2,1,0:T(8,128)(2,1)S(1)}, bf16[2,256,1024]{2,1,0:T(8,128)(2,1)S(1)}, u32[]{:S(2)}, u32[]{:S(2)}) collective-permute-start(bf16[2,256,1024]{2,1,0:T(8,128)(2,1)S(1)} %fusion), channel_id=1, source_target_pairs={{0,2},{1,3},{2,0},{3,1},{4,6},{5,7},{6,4},{7,5},{8,10},{9,11},{10,... | collective-permute-start | bytes 3145736 | tf_op jit(solution)/shard_map/ppermute | solution.py:47
  112.4 7.0 %collective-permute-start.18 = (bf16[384,1024]{1,0:T(8,128)(2,1)S(1)}, bf16[384,1024]{1,0:T(8,128)(2,1)S(1)}, u32[]{:S(2)}, u32[]{:S(2)}) collective-permute-start(bf16[384,1024]{1,0:T(8,128)(2,1)S(1)} %get-tuple-element.66), channel_id=1, source_target_pairs={{0,1},{1,0},{2,3},{3,2},{4,5},{5,4},{6,7},{7,6},{8,9},{9,8},{10,11... | collective-permute-start | bytes 2359304 | tf_op jit(solution)/shard_map/ppermute | solution.py:47
  117.4 18.1 %collective-permute-start.21 = (bf16[2,1024,256]{2,1,0:T(8,128)(2,1)S(1)}, bf16[2,1024,256]{2,1,0:T(8,128)(2,1)S(1)}, u32[]{:S(2)}, u32[]{:S(2)}) collective-permute-start(bf16[2,1024,256]{2,1,0:T(8,128)(2,1)S(1)} %add.56.refs_4_), channel_id=1, source_target_pairs={{0,16},{1,9},{2,18},{3,11},{4,20},{5,13},{6,22},{7,15},{8,24},{9,1... | collective-permute-start | bytes 3145736 | tf_op jit(solution)/shard_map/ppermute | solution.py:47
  127.0 8.5 %collective-permute-start.22 = (bf16[384,1024]{1,0:T(8,128)(2,1)S(1)}, bf16[384,1024]{1,0:T(8,128)(2,1)S(1)}, u32[]{:S(2)}, u32[]{:S(2)}) collective-permute-start(bf16[384,1024]{1,0:T(8,128)(2,1)S(1)} %get-tuple-element.72), channel_id=1, source_target_pairs={{0,1},{1,0},{2,3},{3,2},{4,5},{5,4},{6,7},{7,6},{8,9},{9,8},{10,11... | collective-permute-start | bytes 2359304 | tf_op jit(solution)/shard_map/ppermute | solution.py:47
  133.7 9.5 %collective-permute-start.24 = (bf16[256,1024]{1,0:T(8,128)(2,1)S(1)}, bf16[256,1024]{1,0:T(8,128)(2,1)S(1)}, u32[]{:S(2)}, u32[]{:S(2)}) collective-permute-start(bf16[256,1024]{1,0:T(8,128)(2,1)S(1)} %get-tuple-element.90), channel_id=1, source_target_pairs={{0,8},{1,17},{2,10},{3,19},{4,12},{5,21},{6,14},{7,23},{8,0},{9,25... | collective-permute-start | bytes 1572872 | tf_op jit(solution)/shard_map/ppermute | solution.py:47
  143.1 4.7 %collective-permute-start.25 = (f32[384,1024]{1,0:T(8,128)S(1)}, f32[384,1024]{1,0:T(8,128)S(1)}, u32[]{:S(2)}, u32[]{:S(2)}) collective-permute-start(f32[384,1024]{1,0:T(8,128)S(1)} %get-tuple-element.82), channel_id=1, source_target_pairs={{0,1},{1,0},{2,3},{3,2},{4,5},{5,4},{6,7},{7,6},{8,9},{9,8},{10,11... | collective-permute-start | bytes 4718600 | tf_op jit(solution)/shard_map/ppermute | solution.py:47
  143.6 4.2 %collective-permute-start.23 = (bf16[384,1024]{1,0:T(8,128)(2,1)S(1)}, bf16[384,1024]{1,0:T(8,128)(2,1)S(1)}, u32[]{:S(2)}, u32[]{:S(2)}) collective-permute-start(bf16[384,1024]{1,0:T(8,128)(2,1)S(1)} %get-tuple-element.79), channel_id=1, source_target_pairs={{0,1},{1,0},{2,3},{3,2},{4,5},{5,4},{6,7},{7,6},{8,9},{9,8},{10,11... | collective-permute-start | bytes 2359304 | tf_op jit(solution)/shard_map/ppermute | solution.py:47

commit v9 on v8

--- a/solution.py
+++ b/solution.py
@@ -167,8 +167,8 @@
     )(place, activations, other, turned)
 
 
-def project_kernel(place, acts, other, cots, here, there, *refs, first, last):
-    near, far, *keys = refs[0 if first else 3 : -1]
+def project_kernel(place, acts, other, cots, here, there, *refs, first, last, lays):
+    near, far, *keys = refs[0 if first else 2 + lays : -1]
     acc = refs[-1]
     tokens, cols = acts.shape[0], here.shape[2]
     step = pl.program_id(0)
@@ -200,7 +200,7 @@
             else:
                 keys[0][...] = acc[...] + sums
 
-    if not first:
+    if lays:
 
         @pl.when(step >= 2)
         def _():
@@ -211,7 +211,7 @@
     tokens, columns = activations.shape[0], cots.shape[1]
     _, rows, cols = here.shape
     part = rows // 2
-    first, last = k == 0, k == 3
+    first, last, lays = k == 0, k == 3, got is not None
 
     def whole(*shape):
         return pl.BlockSpec(shape, lambda r, s: (0, 0))
@@ -220,8 +220,8 @@
 
     def out_at(r, s):
         own = 2 * (2 * (s[0] ^ k) + s[1]) + r
-        received = 2 * (2 * (s[0] ^ (k - 1)) + 1 - s[1]) + r - 2
-        return (0, own if first else jnp.where(r < 2, own, received))
+        received = 2 * (2 * (s[0] ^ (k - 2)) + 1 - s[1]) + r - 2
+        return (0, jnp.where(r < 2, own, received) if lays else own)
 
     mine = pl.BlockSpec(
         (tokens, part), lambda r, s: (0, 2 * (2 * (s[0] ^ k) + s[1]) + jnp.minimum(r, 1))
@@ -229,20 +229,14 @@
     piece = pl.BlockSpec((2, part, cols), lambda r, s: (0, jnp.minimum(r, 1), 0))
     one = jax.ShapeDtypeStruct((tokens, columns), F32)
     return pl.pallas_call(
-        lambda *refs: project_kernel(*refs, first=first, last=last),
+        lambda *refs: project_kernel(*refs, first=first, last=last, lays=lays),
         grid_spec=pltpu.PrefetchScalarGridSpec(
             num_scalar_prefetch=1,
-            grid=(2 if first else 4,),
+            grid=(4 if lays else 2,),
             in_specs=[mine, mine, held, piece, piece]
-            + (
-                []
-                if first
-                else [
-                    held,
-                    pl.BlockSpec((tokens, part), lambda r, s: (0, jnp.maximum(r - 2, 0))),
-                    pl.BlockSpec(memory_space=pl.ANY),
-                ]
-            ),
+            + ([] if first else [held])
+            + ([pl.BlockSpec((tokens, part), lambda r, s: (0, jnp.maximum(r - 2, 0)))] * lays)
+            + ([] if first else [pl.BlockSpec(memory_space=pl.ANY)]),
             out_specs=[
                 pl.BlockSpec((tokens, part), out_at),
                 pl.BlockSpec((tokens, part), lambda r, s: (0, jnp.minimum(r, 1))),
@@ -255,39 +249,48 @@
             jax.ShapeDtypeStruct((tokens, rows), BF16),
         ]
         + ([one, one] if last else [jax.ShapeDtypeStruct((2 * tokens, columns), F32)]),
-        input_output_aliases={} if first else {8: 0},
+        input_output_aliases={} if first else {7 + lays: 0},
         compiler_params=pltpu.CompilerParams(vmem_limit_bytes=28 * MIB),
         cost_estimate=cost(
             8 * tokens * rows * columns,
             8 * tokens * rows + 2 * rows * columns + 8 * tokens * columns,
-            1 if last else SHRINK,
         ),
         name="project",
     )(
         place, activations, other, cots, here, there,
-        *([] if first else [so_far[2], got, so_far[0]]),
-    )
-
-
-def finish_kernel(place, got, near, far, last, arrived, whole, out, keys, weight, *, scale):
-    out[...] = got[...]
+        *([] if first else [so_far[2], *([got] * lays), so_far[0]]),
+    )
+
+
+def finish_kernel(place, got2, got3, near, far, last, arrived, whole, out, keys, weight, *, scale):
+    for k, got in ((0, got2), (1, got3)):
+
+        @pl.when(lax.div(pl.program_id(0), 2) == k)
+        def _():
+            out[...] = got[...]
+
     keys[...] = (near[...] + far[...]).astype(BF16)
     weight[...] = ((last[...] + arrived[...].astype(F32)) * scale).T.astype(BF16)
 
 
-def finished(place, whole, got, keys_near, keys_far, last, arrived, scale):
-    tokens, rows = got.shape
+def finished(place, whole, got2, got3, keys_near, keys_far, last, arrived, scale):
+    tokens, rows = got3.shape
     cols, columns = last.shape[0], keys_near.shape[1]
-    part, some = rows // 2, columns // 2
-    wide = pl.BlockSpec((tokens, some), lambda r, s: (0, r))
-    flat = pl.BlockSpec((cols, part), lambda r, s: (0, r))
+    part = rows // 2
+    wide = pl.BlockSpec((tokens, columns // 4), lambda r, s: (0, r))
+    flat = pl.BlockSpec((cols, rows // 4), lambda r, s: (0, r))
+
+    def laid_at(r, s):
+        return (0, 2 * (2 * (s[0] ^ (2 + lax.div(r, 2))) + 1 - s[1]) + lax.rem(r, 2))
+
     return pl.pallas_call(
         lambda *refs: finish_kernel(*refs, scale=scale),
         grid_spec=pltpu.PrefetchScalarGridSpec(
             num_scalar_prefetch=1,
-            grid=(2,),
+            grid=(4,),
             in_specs=[
-                pl.BlockSpec((tokens, part), lambda r, s: (0, r)),
+                pl.BlockSpec((tokens, part), lambda r, s: (0, jnp.minimum(r, 1))),
+                pl.BlockSpec((tokens, part), lambda r, s: (0, jnp.maximum(r - 2, 0))),
                 wide,
                 wide,
                 flat,
@@ -295,9 +298,9 @@
                 pl.BlockSpec(memory_space=pl.ANY),
             ],
             out_specs=[
-                pl.BlockSpec((tokens, part), lambda r, s: (0, 2 * (2 * (s[0] ^ 3) + 1 - s[1]) + r)),
+                pl.BlockSpec((tokens, part), laid_at),
                 wide,
-                pl.BlockSpec((part, cols), lambda r, s: (r, 0)),
+                pl.BlockSpec((rows // 4, cols), lambda r, s: (r, 0)),
             ],
         ),
         out_shape=[
@@ -305,11 +308,11 @@
             jax.ShapeDtypeStruct((tokens, columns), BF16),
             jax.ShapeDtypeStruct((rows, cols), BF16),
         ],
-        input_output_aliases={6: 0},
+        input_output_aliases={7: 0},
         compiler_params=pltpu.CompilerParams(vmem_limit_bytes=12 * MIB),
-        cost_estimate=cost(0, 4 * tokens * rows + 10 * tokens * columns),
+        cost_estimate=cost(0, 8 * tokens * rows + 10 * tokens * columns),
         name="finish",
-    )(place, got, keys_near, keys_far, last, arrived, whole)
+    )(place, got2, got3, keys_near, keys_far, last, arrived, whole)
 
 
 def added(*arrays):
@@ -339,34 +342,41 @@
 
     sum3 = added(after(keep3, first), got3)
     far = sent(sum3, IN)
-    two_mid = sent(after(one, first, keep10), MID)
-    two_end = sent(mid, OUT)
+    two_mid = sent(after(one, first, sum3), MID)
+    two_end = sent(after(mid, sum3), OUT)
     one_b = sent(after(one, got3), FLIP_B)
-    whole, out, keys = projected(
-        first, 0, after(activations, keep10), other, cots, base, base_b
-    )
-    got10 = sent(after(send10, got2, out), FLIP_B)
-    got = sent(out, SWAP)
-    sum2 = added(keep2, got2)
-    two = two_mid + two_end
-    near = sent(after(sum2, far, two, out, one_b), IN)
-    mid_far = sent(added(sum2, far), MID)
-    three_end = sent(after(two_mid, out), OUT)
-    two_b = sent(after(two, got10), FLIP_B)
-    whole, out, keys = projected(
-        place, 1, after(activations, out), other, cots, one, one_b, (whole, None, keys), got
-    )
-    got = sent(out, SWAP)
-
-    three = mid + three_end
-    three_b = sent(after(three, two_b), FLIP_B)
-    sum_mid = sent(added(sum3, after(near, three, out)), MID)
-    sum_one = sent(added(keep10[1], got10[1], mid_far), PAIR)
-    whole, out, keys = projected(
-        place, 2, after(activations, out), other, cots, two, two_b, (whole, None, keys), got
-    )
-    got = sent(out, SWAP)
-    sum_mid, sum_one = after(sum_mid, out), after(sum_one, out)
+    whole, out0, keys = projected(
+        first, 0, after(activations, keep10, sum3), other, cots, base, base_b
+    )
+    got0 = sent(out0, SWAP)
+    second = gate(place, after(far, out0), two_mid, two_end, got2, one_b)
+
+    sum2_far = added(after(keep2, second), got2, far)
+    mid_far = sent(sum2_far, MID)
+    near = sent(after(added(keep2, got2), sum2_far), IN)
+    three_end = sent(after(two_mid, second), OUT)
+    got10 = sent(after(send10, second), FLIP_B)
+    two = after(two_mid, second) + two_end
+    whole, out1, keys = projected(
+        second, 1, after(activations, sum2_far), other, cots, one, one_b, (whole, None, keys)
+    )
+    got1 = sent(out1, SWAP)
+    third = gate(place, after(near, out1), mid_far, three_end, got10)
+
+    sum1 = added(after(keep10[1], third), got10[1], mid_far)
+    sum_one = sent(sum1, PAIR)
+    sum3_near = added(sum3, after(near, third))
+    sum_mid = sent(sum3_near, MID)
+    two_b = sent(after(two, third), FLIP_B)
+    three = after(mid, third) + three_end
+    three_b = sent(three, FLIP_B)
+    whole, out2, keys = projected(
+        third, 2, after(activations, sum3_near), other, cots, two, two_b, (whole, None, keys), got0
+    )
+    whole, out3, keys, keys_far = projected(
+        place, 3, after(activations, out2), other, cots, three, three_b, (whole, None, keys), got1
+    )
+    sum_mid, sum_one = after(sum_mid, out3), after(sum_one, out3)
     last = [
         keep10[0, a].astype(F32)
         + got10[0, a].astype(F32)
@@ -374,20 +384,15 @@
         + sum_one[a].astype(F32)
         for a in (0, 1)
     ]
-    over = last[1].astype(BF16)
-    arrived = sent(over, FLIP_A)
-
-    whole, out, keys, keys_far = projected(
-        place, 3, after(activations, over), other, cots, three, three_b, (whole, None, keys), got
-    )
     grad_input, key_values, grad_weight = finished(
         place,
         whole,
-        sent(out, SWAP),
+        sent(out2, SWAP),
+        sent(out3, SWAP),
         keys,
-        sent(after(keys_far, arrived), SWAP),
+        sent(keys_far, SWAP),
         last[0],
-        arrived,
+        sent(last[1].astype(BF16), FLIP_A),
         1.0 / math.sqrt(32 * tokens),
     )
     return (key_values, grad_input, grad_weight)

time: 151 us -> 155 us (1.026)
  waiting for transfers between devices: 42.5 us -> 62.7 us
  starting transfers between devices: 47.3 us -> 31.5 us
  other arithmetic: 11.1 us -> 7.35 us
  Pallas kernels: 45.8 us -> 48.7 us
    ppermute x26, waiting for transfers between devices: 42.5 us -> 62.7 us  [sent(): return lax.ppermute(array, AXES, pairs)]
    ppermute x26, starting transfers between devices: 47.3 us -> 31.5 us  [sent(): return lax.ppermute(array, AXES, pairs)]
    convert_element_type x4, other arithmetic: 7.18 us -> 3.51 us  [added(): return total.astype(BF16)]
    pallas_call x1 -> x3, Pallas kernels: 1.14 us -> 3.41 us  [gate(): pl.pallas_call(kernel, in_specs=[pl.BlockSpec(memory_space=pltpu.SMEM)] +...]
    add x3 -> x2, other arithmetic: 2.69 us -> 0.55 us  [the longest x1 0.28 us: by_hops(): two = after(two_mid, second) + two_end]
    convert_element_type x0 -> x1, other arithmetic: none -> 2.07 us  [by_hops(): last[1].astype(BF16)]
    unnamed x6 -> x18, local copies, waits for them, and re-layouts: 2.79 us -> 3.19 us
  transfers between devices with their start and end apart: 26 -> 26, of which waited for: 8 -> 10; matrix products, arithmetic and copies ran while one was open for 7% -> 5% of each run, Pallas kernels for 29% -> 29%
where the time goes in v9:
time: 155 us; the launch traced here: 154 us
  waiting for transfers between devices  62.7 us (40%)
  Pallas kernels  48.7 us (31%)
  starting transfers between devices  31.5 us (20%)
  other arithmetic  7.35 us (5%)
  local copies, waits for them, and re-layouts  3.26 us (2%)
    ppermute x26, waiting for transfers between devices, sent(): return lax.ppermute(array, AXES, pairs)  62.7 us
    ppermute x26, starting transfers between devices, sent(): return lax.ppermute(array, AXES, pairs)  31.5 us
    pallas_call x4, Pallas kernels, projected(): pl.pallas_call(lambda *refs: project_kernel(*refs, first=first, last=last...  28.4 us
    pallas_call x1, Pallas kernels, terms(): pl.pallas_call(term_kernel, grid_spec=pltpu.PrefetchScalarGridSpec(num_sc...  9.18 us
    pallas_call x1, Pallas kernels, first_terms(): pl.pallas_call(first_term_kernel, grid_spec=pltpu.PrefetchScalarGridSpec(...  4.49 us
    convert_element_type x4, other arithmetic, added(): return total.astype(BF16)  3.51 us
    pallas_call x3, Pallas kernels, gate(): pl.pallas_call(kernel, in_specs=[pl.BlockSpec(memory_space=pltpu.SMEM)] +...  3.41 us
    pallas_call x1, Pallas kernels, finished(): pl.pallas_call(lambda *refs: finish_kernel(*refs, scale=scale), grid_spec...  3.2 us
  transfers between devices with their start and end apart: 26, of which 10 were waited for; matrix products, arithmetic and copies ran while one was open for 5% of the time, Pallas kernels for 29%

profile of v9, /device:TPU:0, one launch (start us, length us, event | category | flops | bytes accessed | tf_op | source)
XLA Modules:
  0.0 154.3 jit_solution(7286831902262028930)
XLA Ops:
  0.6 0.5 collective-permute-start
  1.2 2.9 %collective-permute-start.2 = (bf16[1024,256]{1,0:T(8,128)(2,1)}, bf16[1024,256]{1,0:T(8,128)(2,1)S(1)}, u32[]{:S(2)}, u32[]{:S(2)}) collective-permute-start(bf16[1024,256]{1,0:T(8,128)(2,1)} %param.5), channel_id=1, source_target_pairs={{0,8},{1,17},{2,10},{3,19},{4,12},{5,21},{6,14},{7,23},{8,0},{9,25... | collective-permute-start | bytes 1572872 | tf_op jit(solution)/shard_map/ppermute | solution.py:47
  4.2 7.4 %collective-permute-done.2 = bf16[1024,256]{1,0:T(8,128)(2,1)S(1)} collective-permute-done((bf16[1024,256]{1,0:T(8,128)(2,1)}, bf16[1024,256]{1,0:T(8,128)(2,1)S(1)}, u32[]{:S(2)}, u32[]{:S(2)}) %collective-permute-start.2) | collective-permute-done | bytes 524320 | tf_op jit(solution)/shard_map/ppermute | solution.py:47
  11.5 1.1 pad_maximum_fusion.refs_4_
  12.7 2.2 %collective-permute-start.3 = (bf16[2,1024,256]{2,1,0:T(8,128)(2,1)S(1)}, bf16[2,1024,256]{2,1,0:T(8,128)(2,1)S(1)}, u32[]{:S(2)}, u32[]{:S(2)}) collective-permute-start(bf16[2,1024,256]{2,1,0:T(8,128)(2,1)S(1)} %pad_maximum_fusion.refs_4_), channel_id=1, source_target_pairs={{0,2},{1,3},{2,0},{3,1},{4,6},{5,7},{6,4},{7,5},{8,10},{9,11},{10,... | collective-permute-start | bytes 3145736 | tf_op jit(solution)/shard_map/ppermute | solution.py:47
  14.9 0.7 collective-permute-start.4
  15.6 1.6 %collective-permute-start.5 = (bf16[2,1024,256]{2,1,0:T(8,128)(2,1)S(1)}, bf16[2,1024,256]{2,1,0:T(8,128)(2,1)S(1)}, u32[]{:S(2)}, u32[]{:S(2)}) collective-permute-start(bf16[2,1024,256]{2,1,0:T(8,128)(2,1)S(1)} %pad_maximum_fusion.refs_4_), channel_id=1, source_target_pairs={{0,16},{1,9},{2,18},{3,11},{4,20},{5,13},{6,22},{7,15},{8,24},{9,1... | collective-permute-start | bytes 3145736 | tf_op jit(solution)/shard_map/ppermute | solution.py:47
  17.2 2.8 %copy-done = bf16[384,8192]{1,0:T(8,128)(2,1)S(1)} copy-done((bf16[384,8192]{1,0:T(8,128)(2,1)S(1)}, bf16[384,8192]{1,0:T(8,128)(2,1)}, u32[]{:S(2)}) %copy-start) | copy-done | bytes 6291480
  20.0 4.5 %terms.2 = (bf16[2,256,1024]{2,1,0:T(8,128)(2,1)S(1)}, bf16[2,256,1024]{2,1,0:T(8,128)(2,1)S(1)}, bf16[768,1024]{1,0:T(8,128)(2,1)S(1)}, bf16[1024,768]{1,0:T(8,128)(2,1)S(1)}) custom-call(s32[3]{0:T(128)S(1)} %pad_add_fusion.place.refs_0_, bf16[384,8192]{1,0:T(8,128)(2,1)S(1)} %copy-done, bf16[384,8192]{1,0:T(8,128)(2,1)} %collective-permute-done.other.refs_2_, ...), custom_call_target="tpu_custom_call" | custom-call | flops 1610612 | bytes 5767 | tf_op jit(solution)/shard_map/terms/pallas_call | solution.py:107
  24.5 0.6 collective-permute-start.6
  25.1 9.2 %terms.3 = (bf16[2,256,1024]{2,1,0:T(8,128)(2,1)S(1)}, bf16[2,2,256,1024]{3,2,1,0:T(8,128)(2,1)S(1)}, bf16[2,256,1024]{2,1,0:T(8,128)(2,1)S(1)}, bf16[2,2,256,1024]{3,2,1,0:T(8,128)(2,1)}) custom-call(s32[3]{0:T(128)S(1)} %pad_add_fusion.place.refs_0_, bf16[384,8192]{1,0:T(8,128)(2,1)S(1)} %copy-done.1, ...), custom_call_target="tpu_custom_call" | custom-call | flops 4831838 | bytes 17301 | tf_op jit(solution)/shard_map/terms/pallas_call | solution.py:151
  34.3 3.1 %collective-permute-done.3.refs_1_.refs_4_ = bf16[2,1024,256]{2,1,0:T(8,128)(2,1)S(1)} collective-permute-done((bf16[2,1024,256]{2,1,0:T(8,128)(2,1)S(1)}, bf16[2,1024,256]{2,1,0:T(8,128)(2,1)S(1)}, u32[]{:S(2)}, u32[]{:S(2)}) %collective-permute-start.3) | collective-permute-done | bytes 1048608 | tf_op jit(solution)/shard_map/ppermute | solution.py:47
  37.4 1.1 gate.3.refs_0_
  38.5 3.2 %collective-permute-done.6 = bf16[2,256,1024]{2,1,0:T(8,128)(2,1)S(1)} collective-permute-done((bf16[2,256,1024]{2,1,0:T(8,128)(2,1)S(1)}, bf16[2,256,1024]{2,1,0:T(8,128)(2,1)S(1)}, u32[]{:S(2)}, u32[]{:S(2)}) %collective-permute-start.6) | collective-permute-done | bytes 1048608 | tf_op jit(solution)/shard_map/ppermute | solution.py:47
  41.7 1.5 collective-permute-start.7
  43.3 0.4 add_convert_fusion.1
  43.7 6.3 %collective-permute-start.8 = (bf16[2,256,1024]{2,1,0:T(8,128)(2,1)S(1)}, bf16[2,256,1024]{2,1,0:T(8,128)(2,1)S(1)}, u32[]{:S(2)}, u32[]{:S(2)}) collective-permute-start(bf16[2,256,1024]{2,1,0:T(8,128)(2,1)S(1)} %add_convert_fusion.1), channel_id=1, source_target_pairs={{0,2},{1,3},{6,4},{7,5},{8,10},{9,11},{14,12},{15,13},{16,18},{17,... | collective-permute-start | bytes 3145736 | tf_op jit(solution)/shard_map/ppermute | solution.py:47
  50.0 0.7 collective-permute-start.9
  50.7 1.3 collective-permute-start.10
  52.0 0.6 collective-permute-start.11
  52.6 6.5 %project.4 = (bf16[384,8192]{1,0:T(8,128)(2,1)}, bf16[384,1024]{1,0:T(8,128)(2,1)S(1)}, f32[768,1024]{1,0:T(8,128)S(1)}) custom-call(s32[3]{0:T(128)S(1)} %gate.3.refs_0_, bf16[384,8192]{1,0:T(8,128)(2,1)S(1)} %copy-done.1, bf16[384,8192]{1,0:T(8,128)(2,1)} %collective-permute-done.other.refs_2_, bf16[768,1024]{1,0:T(8,128)(2,1)S(1)} %get-tuple-element.59.refs_3_, ...), custom_call_target="tpu_custom_call" | custom-call | flops 3221225 | bytes 8388 | tf_op jit(solution)/shard_map/project/pallas_call | solution.py:231
  59.1 10.9 %collective-permute-done.8.refs_1_ = bf16[2,256,1024]{2,1,0:T(8,128)(2,1)S(1)} collective-permute-done((bf16[2,256,1024]{2,1,0:T(8,128)(2,1)S(1)}, bf16[2,256,1024]{2,1,0:T(8,128)(2,1)S(1)}, u32[]{:S(2)}, u32[]{:S(2)}) %collective-permute-start.8) | collective-permute-done | bytes 1048608 | tf_op jit(solution)/shard_map/ppermute | solution.py:47
  70.0 4.9 %collective-permute-done.10.refs_3_ = bf16[2,1024,256]{2,1,0:T(8,128)(2,1)S(1)} collective-permute-done((bf16[2,1024,256]{2,1,0:T(8,128)(2,1)S(1)}, bf16[2,1024,256]{2,1,0:T(8,128)(2,1)S(1)}, u32[]{:S(2)}, u32[]{:S(2)}) %collective-permute-start.10) | collective-permute-done | bytes 1048608 | tf_op jit(solution)/shard_map/ppermute | solution.py:47
  74.9 1.1 gate.4.refs_0_
  76.1 1.6 %collective-permute-start.15 = (bf16[2,2,256,1024]{3,2,1,0:T(8,128)(2,1)}, bf16[2,2,256,1024]{3,2,1,0:T(8,128)(2,1)S(1)}, u32[]{:S(2)}, u32[]{:S(2)}) collective-permute-start(bf16[2,2,256,1024]{3,2,1,0:T(8,128)(2,1)} %get-tuple-element.74), channel_id=1, source_target_pairs={{0,16},{1,9},{2,18},{3,11},{4,20},{5,13},{6,22},{7,15},{8,24},{9,1... | collective-permute-start | bytes 6291464 | tf_op jit(solution)/shard_map/ppermute | solution.py:47
  77.7 2.0 %fusion.2 = (bf16[2,256,1024]{2,1,0:T(8,128)(2,1)}, bf16[2,256,1024]{2,1,0:T(8,128)(2,1)}) fusion(bf16[2,256,1024]{2,1,0:T(8,128)(2,1)S(1)} %collective-permute-done.7.refs_4_, bf16[2,256,1024]{2,1,0:T(8,128)(2,1)S(1)} %collective-permute-done.8.refs_1_, bf16[2,256,1024]{2,1,0:T(8,128)(2,1)S(1)} %get-tuple-element.65), kind=kLoop, calls=%fused_computation.4 | loop fusion | flops 4718592 | bytes 5242880 | tf_op jit(solution)/shard_map/convert_element_type | solution.py:322
  79.7 1.8 %collective-permute-start.12 = (bf16[2,256,1024]{2,1,0:T(8,128)(2,1)}, bf16[2,256,1024]{2,1,0:T(8,128)(2,1)S(1)}, u32[]{:S(2)}, u32[]{:S(2)}) collective-permute-start(bf16[2,256,1024]{2,1,0:T(8,128)(2,1)} %get-tuple-element.66), channel_id=1, source_target_pairs={{0,2},{1,3},{6,4},{7,5},{8,10},{9,11},{14,12},{15,13},{16,18},{17,... | collective-permute-start | bytes 3145736 | tf_op jit(solution)/shard_map/ppermute | solution.py:47
  81.5 0.7 collective-permute-start.13
  82.2 1.5 collective-permute-start.14
  83.8 0.3 add.56.refs_4_
  84.1 6.7 %project.5 = (bf16[384,8192]{1,0:T(8,128)(2,1)}, bf16[384,1024]{1,0:T(8,128)(2,1)S(1)}, f32[768,1024]{1,0:T(8,128)S(1)}) custom-call(s32[3]{0:T(128)S(1)} %gate.4.refs_0_, bf16[384,8192]{1,0:T(8,128)(2,1)S(1)} %copy-done.1, bf16[384,8192]{1,0:T(8,128)(2,1)} %collective-permute-done.other.refs_2_, ...), custom_call_target="tpu_custom_call", output_to_operand_aliasing={{0}: (7, {})} | custom-call | flops 3221225 | bytes 8388 | tf_op jit(solution)/shard_map/project/pallas_call | solution.py:231
  90.8 8.4 %collective-permute-done.12.refs_1_ = bf16[2,256,1024]{2,1,0:T(8,128)(2,1)S(1)} collective-permute-done((bf16[2,256,1024]{2,1,0:T(8,128)(2,1)}, bf16[2,256,1024]{2,1,0:T(8,128)(2,1)S(1)}, u32[]{:S(2)}, u32[]{:S(2)}) %collective-permute-start.12) | collective-permute-done | bytes 1048608 | tf_op jit(solution)/shard_map/ppermute | solution.py:47
  99.2 4.6 %collective-permute-done.14.refs_3_ = bf16[2,1024,256]{2,1,0:T(8,128)(2,1)S(1)} collective-permute-done((bf16[2,1024,256]{2,1,0:T(8,128)(2,1)S(1)}, bf16[2,1024,256]{2,1,0:T(8,128)(2,1)S(1)}, u32[]{:S(2)}, u32[]{:S(2)}) %collective-permute-start.14) | collective-permute-done | bytes 1048608 | tf_op jit(solution)/shard_map/ppermute | solution.py:47
  103.8 1.1 gate.5.refs_0_
  105.0 2.6 %collective-permute-start.16 = (bf16[2,1024,256]{2,1,0:T(8,128)(2,1)S(1)}, bf16[2,1024,256]{2,1,0:T(8,128)(2,1)S(1)}, u32[]{:S(2)}, u32[]{:S(2)}) collective-permute-start(bf16[2,1024,256]{2,1,0:T(8,128)(2,1)S(1)} %add.56.refs_4_), channel_id=1, source_target_pairs={{0,16},{1,9},{2,18},{3,11},{4,20},{5,13},{6,22},{7,15},{8,24},{9,1... | collective-permute-start | bytes 3145736 | tf_op jit(solution)/shard_map/ppermute | solution.py:47
  108.1 0.7 fusion.4
  108.8 0.4 copy-done.8
  109.2 0.4 add_convert_fusion
  109.7 1.8 %collective-permute-start.23 = (bf16[2,256,1024]{2,1,0:T(8,128)(2,1)S(1)}, bf16[2,256,1024]{2,1,0:T(8,128)(2,1)}, u32[]{:S(2)}, u32[]{:S(2)}) collective-permute-start(bf16[2,256,1024]{2,1,0:T(8,128)(2,1)S(1)} %add_convert_fusion), channel_id=1, source_target_pairs={{2,4},{3,5},{4,2},{5,3},{10,12},{11,13},{12,10},{13,11},{18,20},{1... | collective-permute-start | bytes 3145736 | tf_op jit(solution)/shard_map/ppermute | solution.py:47
  111.4 8.9 %collective-permute-done.16.refs_5_ = bf16[2,1024,256]{2,1,0:T(8,128)(2,1)S(1)} collective-permute-done((bf16[2,1024,256]{2,1,0:T(8,128)(2,1)S(1)}, bf16[2,1024,256]{2,1,0:T(8,128)(2,1)S(1)}, u32[]{:S(2)}, u32[]{:S(2)}) %collective-permute-start.16) | collective-permute-done | bytes 1048608 | tf_op jit(solution)/shard_map/ppermute | solution.py:47
  120.4 7.5 %project.6 = (bf16[384,8192]{1,0:T(8,128)(2,1)}, bf16[384,1024]{1,0:T(8,128)(2,1)S(1)}, f32[768,1024]{1,0:T(8,128)S(1)}) custom-call(s32[3]{0:T(128)S(1)} %gate.5.refs_0_, bf16[384,8192]{1,0:T(8,128)(2,1)S(1)} %copy-done.1, bf16[384,8192]{1,0:T(8,128)(2,1)} %collective-permute-done.other.refs_2_, ...), custom_call_target="tpu_custom_call", output_to_operand_aliasing={{0}: (8, {})} | custom-call | flops 3221225 | bytes 8388 | tf_op jit(solution)/shard_map/project/pallas_call | solution.py:231
  127.9 3.7 %collective-permute-done.19.refs_5_ = bf16[2,1024,256]{2,1,0:T(8,128)(2,1)S(1)} collective-permute-done((bf16[2,1024,256]{2,1,0:T(8,128)(2,1)S(1)}, bf16[2,1024,256]{2,1,0:T(8,128)(2,1)S(1)}, u32[]{:S(2)}, u32[]{:S(2)}) %collective-permute-start.19) | collective-permute-done | bytes 1048608 | tf_op jit(solution)/shard_map/ppermute | solution.py:47
  131.6 7.7 %project.7 = (bf16[384,8192]{1,0:T(8,128)(2,1)}, bf16[384,1024]{1,0:T(8,128)(2,1)S(1)}, f32[384,1024]{1,0:T(8,128)S(1)}, f32[384,1024]{1,0:T(8,128)S(1)}) custom-call(s32[3]{0:T(128)S(1)} %pad_add_fusion.place.refs_0_, bf16[384,8192]{1,0:T(8,128)(2,1)S(1)} %copy-done.1, ...), custom_call_target="tpu_custom_call", output_to_operand_aliasing={{0}: (8, {})} | custom-call | flops 3221225 | bytes 8388 | tf_op jit(solution)/shard_map/project/pallas_call | solution.py:231
  139.3 0.5 collective-permute-start.18
  139.8 2.1 %fusion.5 = (bf16[256,1024]{1,0:T(8,128)(2,1)S(1)}, f32[256,1024]{1,0:T(8,128)S(1)}) fusion(bf16[2,2,256,1024]{3,2,1,0:T(8,128)(2,1)S(1)} %collective-permute-done.15.refs_4_, bf16[2,256,1024]{2,1,0:T(8,128)(2,1)S(1)} %collective-permute-done.24, bf16[2,256,1024]{2,1,0:T(8,128)(2,1)} %collective-permute-done.23, ...), kind=kLoop, calls=%fused_computation.13 | loop fusion | flops 3932160 | bytes 5767168 | tf_op jit(solution)/shard_map/convert_element_type | solution.py:395
  141.9 1.8 %collective-permute-start.25 = (bf16[256,1024]{1,0:T(8,128)(2,1)S(1)}, bf16[256,1024]{1,0:T(8,128)(2,1)S(1)}, u32[]{:S(2)}, u32[]{:S(2)}) collective-permute-start(bf16[256,1024]{1,0:T(8,128)(2,1)S(1)} %get-tuple-element.95), channel_id=1, source_target_pairs={{0,8},{1,17},{2,10},{3,19},{4,12},{5,21},{6,14},{7,23},{8,0},{9,25... | collective-permute-start | bytes 1572872 | tf_op jit(solution)/shard_map/ppermute | solution.py:47
  143.6 7.5 %collective-permute-done.25.refs_6_ = bf16[256,1024]{1,0:T(8,128)(2,1)S(1)} collective-permute-done((bf16[256,1024]{1,0:T(8,128)(2,1)S(1)}, bf16[256,1024]{1,0:T(8,128)(2,1)S(1)}, u32[]{:S(2)}, u32[]{:S(2)}) %collective-permute-start.25) | collective-permute-done | bytes 524320 | tf_op jit(solution)/shard_map/ppermute | solution.py:47
  151.1 3.2 %finish.1 = (bf16[384,8192]{1,0:T(8,128)(2,1)}, bf16[384,1024]{1,0:T(8,128)(2,1)}, bf16[1024,256]{1,0:T(8,128)(2,1)}) custom-call(s32[3]{0:T(128)S(1)} %pad_add_fusion.place.refs_0_, bf16[384,1024]{1,0:T(8,128)(2,1)S(1)} %collective-permute-done.18.refs_1_, bf16[384,1024]{1,0:T(8,128)(2,1)S(1)} %collective-permute-done.21.refs_2_, ...), custom_call_target="tpu_custom_call", output_to_operand_aliasing={{0}: (7, {})} | custom-call | bytes 7077 | tf_op jit(solution)/shard_map/finish/pallas_call | solution.py:286
  (42 shorter events, 0.9 us)
Async XLA Ops:
  0.6 16.6 %copy-start.6 = (bf16[384,1024]{1,0:T(8,128)(2,1)S(1)}, bf16[384,1024]{1,0:T(8,128)(2,1)}, u32[]{:S(2)}) copy-start(bf16[384,1024]{1,0:T(8,128)(2,1)} %cot_mine.1) | copy-start | bytes 2359300
  0.6 16.6 %collective-permute-start = (bf16[384,8192]{1,0:T(8,128)(2,1)}, bf16[384,8192]{1,0:T(8,128)(2,1)}, u32[]{:S(2)}, u32[]{:S(2)}) collective-permute-start(bf16[384,8192]{1,0:T(8,128)(2,1)} %refs_1_.3), channel_id=1, source_target_pairs={{0,1},{1,0},{2,3},{3,2},{4,5},{5,4},{6,7},{7,6},{8,9},{9,8},{10,11... | collective-permute-start | bytes 18874376 | tf_op jit(solution)/shard_map/ppermute | solution.py:47
  1.2 16.1 %collective-permute-start.1 = (bf16[384,1024]{1,0:T(8,128)(2,1)}, bf16[384,1024]{1,0:T(8,128)(2,1)S(1)}, u32[]{:S(2)}, u32[]{:S(2)}) collective-permute-start(bf16[384,1024]{1,0:T(8,128)(2,1)} %cot_mine.1), channel_id=1, source_target_pairs={{0,1},{1,0},{2,3},{3,2},{4,5},{5,4},{6,7},{7,6},{8,9},{9,8},{10,11... | collective-permute-start | bytes 2359304 | tf_op jit(solution)/shard_map/ppermute | solution.py:47
  1.2 10.3 %collective-permute-start.2 = (bf16[1024,256]{1,0:T(8,128)(2,1)}, bf16[1024,256]{1,0:T(8,128)(2,1)S(1)}, u32[]{:S(2)}, u32[]{:S(2)}) collective-permute-start(bf16[1024,256]{1,0:T(8,128)(2,1)} %param.5), channel_id=1, source_target_pairs={{0,8},{1,17},{2,10},{3,19},{4,12},{5,21},{6,14},{7,23},{8,0},{9,25... | collective-permute-start | bytes 1572872 | tf_op jit(solution)/shard_map/ppermute | solution.py:47
  12.7 24.7 %collective-permute-start.3 = (bf16[2,1024,256]{2,1,0:T(8,128)(2,1)S(1)}, bf16[2,1024,256]{2,1,0:T(8,128)(2,1)S(1)}, u32[]{:S(2)}, u32[]{:S(2)}) collective-permute-start(bf16[2,1024,256]{2,1,0:T(8,128)(2,1)S(1)} %pad_maximum_fusion.refs_4_), channel_id=1, source_target_pairs={{0,2},{1,3},{2,0},{3,1},{4,6},{5,7},{6,4},{7,5},{8,10},{9,11},{10,... | collective-permute-start | bytes 3145736 | tf_op jit(solution)/shard_map/ppermute | solution.py:47
  14.9 22.5 %collective-permute-start.4 = (bf16[2,1024,256]{2,1,0:T(8,128)(2,1)S(1)}, bf16[2,1024,256]{2,1,0:T(8,128)(2,1)S(1)}, u32[]{:S(2)}, u32[]{:S(2)}) collective-permute-start(bf16[2,1024,256]{2,1,0:T(8,128)(2,1)S(1)} %pad_maximum_fusion.refs_4_), channel_id=1, source_target_pairs={{2,4},{3,5},{4,2},{5,3},{10,12},{11,13},{12,10},{13,11},{18,20},{1... | collective-permute-start | bytes 3145736 | tf_op jit(solution)/shard_map/ppermute | solution.py:47
  15.6 21.8 %collective-permute-start.5 = (bf16[2,1024,256]{2,1,0:T(8,128)(2,1)S(1)}, bf16[2,1024,256]{2,1,0:T(8,128)(2,1)S(1)}, u32[]{:S(2)}, u32[]{:S(2)}) collective-permute-start(bf16[2,1024,256]{2,1,0:T(8,128)(2,1)S(1)} %pad_maximum_fusion.refs_4_), channel_id=1, source_target_pairs={{0,16},{1,9},{2,18},{3,11},{4,20},{5,13},{6,22},{7,15},{8,24},{9,1... | collective-permute-start | bytes 3145736 | tf_op jit(solution)/shard_map/ppermute | solution.py:47
  17.2 2.8 %copy-start = (bf16[384,8192]{1,0:T(8,128)(2,1)S(1)}, bf16[384,8192]{1,0:T(8,128)(2,1)}, u32[]{:S(2)}) copy-start(bf16[384,8192]{1,0:T(8,128)(2,1)} %refs_1_.3) | copy-start | bytes 18874372
  20.0 5.1 %copy-start.1 = (bf16[384,8192]{1,0:T(8,128)(2,1)S(1)}, bf16[384,8192]{1,0:T(8,128)(2,1)}, u32[]{:S(2)}) copy-start(bf16[384,8192]{1,0:T(8,128)(2,1)} %refs_1_.3) | copy-start | bytes 18874372
  24.5 17.2 %collective-permute-start.6 = (bf16[2,256,1024]{2,1,0:T(8,128)(2,1)S(1)}, bf16[2,256,1024]{2,1,0:T(8,128)(2,1)S(1)}, u32[]{:S(2)}, u32[]{:S(2)}) collective-permute-start(bf16[2,256,1024]{2,1,0:T(8,128)(2,1)S(1)} %get-tuple-element.54), channel_id=1, source_target_pairs={{0,16},{1,9},{2,18},{3,11},{4,20},{5,13},{6,22},{7,15},{8,24},{9,1... | collective-permute-start | bytes 3145736 | tf_op jit(solution)/shard_map/ppermute | solution.py:47
  41.7 28.3 %collective-permute-start.7 = (bf16[2,256,1024]{2,1,0:T(8,128)(2,1)S(1)}, bf16[2,256,1024]{2,1,0:T(8,128)(2,1)S(1)}, u32[]{:S(2)}, u32[]{:S(2)}) collective-permute-start(bf16[2,256,1024]{2,1,0:T(8,128)(2,1)S(1)} %get-tuple-element.55), channel_id=1, source_target_pairs={{0,16},{1,9},{2,18},{3,11},{4,20},{5,13},{6,22},{7,15},{8,24},{9,1... | collective-permute-start | bytes 3145736 | tf_op jit(solution)/shard_map/ppermute | solution.py:47
  43.7 15.4 %copy-start.7 = (bf16[2,256,1024]{2,1,0:T(8,128)(2,1)}, bf16[2,256,1024]{2,1,0:T(8,128)(2,1)S(1)}, u32[]{:S(2)}) copy-start(bf16[2,256,1024]{2,1,0:T(8,128)(2,1)S(1)} %add_convert_fusion.1) | copy-start | bytes 3145732
  43.7 26.3 %collective-permute-start.8 = (bf16[2,256,1024]{2,1,0:T(8,128)(2,1)S(1)}, bf16[2,256,1024]{2,1,0:T(8,128)(2,1)S(1)}, u32[]{:S(2)}, u32[]{:S(2)}) collective-permute-start(bf16[2,256,1024]{2,1,0:T(8,128)(2,1)S(1)} %add_convert_fusion.1), channel_id=1, source_target_pairs={{0,2},{1,3},{6,4},{7,5},{8,10},{9,11},{14,12},{15,13},{16,18},{17,... | collective-permute-start | bytes 3145736 | tf_op jit(solution)/shard_map/ppermute | solution.py:47
  50.0 20.0 %collective-permute-start.9 = (bf16[2,1024,256]{2,1,0:T(8,128)(2,1)S(1)}, bf16[2,1024,256]{2,1,0:T(8,128)(2,1)S(1)}, u32[]{:S(2)}, u32[]{:S(2)}) collective-permute-start(bf16[2,1024,256]{2,1,0:T(8,128)(2,1)S(1)} %collective-permute-done.3.refs_1_.refs_4_), channel_id=1, source_target_pairs={{2,4},{3,5},{4,2},{5,3},{10,12},{11,13},{12,10},{13,11},{18,20},{1... | collective-permute-start | bytes 3145736 | tf_op jit(solution)/shard_map/ppermute | solution.py:47
  50.7 24.2 %collective-permute-start.10 = (bf16[2,1024,256]{2,1,0:T(8,128)(2,1)S(1)}, bf16[2,1024,256]{2,1,0:T(8,128)(2,1)S(1)}, u32[]{:S(2)}, u32[]{:S(2)}) collective-permute-start(bf16[2,1024,256]{2,1,0:T(8,128)(2,1)S(1)} %collective-permute-done.4.refs_2_), channel_id=1, source_target_pairs={{2,0},{3,1},{4,6},{5,7},{10,8},{11,9},{12,14},{13,15},{18,16},{19,... | collective-permute-start | bytes 3145736 | tf_op jit(solution)/shard_map/ppermute | solution.py:47
  52.0 22.9 %collective-permute-start.11 = (bf16[2,1024,256]{2,1,0:T(8,128)(2,1)S(1)}, bf16[2,1024,256]{2,1,0:T(8,128)(2,1)S(1)}, u32[]{:S(2)}, u32[]{:S(2)}) collective-permute-start(bf16[2,1024,256]{2,1,0:T(8,128)(2,1)S(1)} %collective-permute-done.3.refs_1_.refs_4_), channel_id=1, source_target_pairs={{0,16},{1,9},{2,18},{3,11},{4,20},{5,13},{6,22},{7,15},{8,24},{9,1... | collective-permute-start | bytes 3145736 | tf_op jit(solution)/shard_map/ppermute | solution.py:47
  59.1 17.0 %copy-start.4 = (f32[768,1024]{1,0:T(8,128)}, f32[768,1024]{1,0:T(8,128)S(1)}, u32[]{:S(2)}) copy-start(f32[768,1024]{1,0:T(8,128)S(1)} %get-tuple-element.68.refs_6_) | copy-start | bytes 9437188
  76.1 27.8 %collective-permute-start.15 = (bf16[2,2,256,1024]{3,2,1,0:T(8,128)(2,1)}, bf16[2,2,256,1024]{3,2,1,0:T(8,128)(2,1)S(1)}, u32[]{:S(2)}, u32[]{:S(2)}) collective-permute-start(bf16[2,2,256,1024]{3,2,1,0:T(8,128)(2,1)} %get-tuple-element.74), channel_id=1, source_target_pairs={{0,16},{1,9},{2,18},{3,11},{4,20},{5,13},{6,22},{7,15},{8,24},{9,1... | collective-permute-start | bytes 6291464 | tf_op jit(solution)/shard_map/ppermute | solution.py:47
  79.7 4.4 %copy-start.5 = (f32[768,1024]{1,0:T(8,128)S(1)}, f32[768,1024]{1,0:T(8,128)}, u32[]{:S(2)}) copy-start(f32[768,1024]{1,0:T(8,128)} %copy-done.4) | copy-start | bytes 9437188
  79.7 19.5 %collective-permute-start.12 = (bf16[2,256,1024]{2,1,0:T(8,128)(2,1)}, bf16[2,256,1024]{2,1,0:T(8,128)(2,1)S(1)}, u32[]{:S(2)}, u32[]{:S(2)}) collective-permute-start(bf16[2,256,1024]{2,1,0:T(8,128)(2,1)} %get-tuple-element.66), channel_id=1, source_target_pairs={{0,2},{1,3},{6,4},{7,5},{8,10},{9,11},{14,12},{15,13},{16,18},{17,... | collective-permute-start | bytes 3145736 | tf_op jit(solution)/shard_map/ppermute | solution.py:47
  81.5 17.7 %collective-permute-start.13 = (bf16[2,256,1024]{2,1,0:T(8,128)(2,1)}, bf16[2,256,1024]{2,1,0:T(8,128)(2,1)S(1)}, u32[]{:S(2)}, u32[]{:S(2)}) collective-permute-start(bf16[2,256,1024]{2,1,0:T(8,128)(2,1)} %get-tuple-element.97), channel_id=1, source_target_pairs={{2,4},{3,5},{4,2},{5,3},{10,12},{11,13},{12,10},{13,11},{18,20},{1... | collective-permute-start | bytes 3145736 | tf_op jit(solution)/shard_map/ppermute | solution.py:47
  82.2 21.6 %collective-permute-start.14 = (bf16[2,1024,256]{2,1,0:T(8,128)(2,1)S(1)}, bf16[2,1024,256]{2,1,0:T(8,128)(2,1)S(1)}, u32[]{:S(2)}, u32[]{:S(2)}) collective-permute-start(bf16[2,1024,256]{2,1,0:T(8,128)(2,1)S(1)} %collective-permute-done.9.refs_2_), channel_id=1, source_target_pairs={{2,0},{3,1},{4,6},{5,7},{10,8},{11,9},{12,14},{13,15},{18,16},{19,... | collective-permute-start | bytes 3145736 | tf_op jit(solution)/shard_map/ppermute | solution.py:47
  83.7 26.0 %collective-permute-start.17 = (bf16[384,1024]{1,0:T(8,128)(2,1)S(1)}, bf16[384,1024]{1,0:T(8,128)(2,1)S(1)}, u32[]{:S(2)}, u32[]{:S(2)}) collective-permute-start(bf16[384,1024]{1,0:T(8,128)(2,1)S(1)} %get-tuple-element.60), channel_id=1, source_target_pairs={{0,1},{1,0},{2,3},{3,2},{4,5},{5,4},{6,7},{7,6},{8,9},{9,8},{10,11... | collective-permute-start | bytes 2359304 | tf_op jit(solution)/shard_map/ppermute | solution.py:47
  90.8 14.2 %copy-start.2 = (f32[768,1024]{1,0:T(8,128)}, f32[768,1024]{1,0:T(8,128)S(1)}, u32[]{:S(2)}) copy-start(f32[768,1024]{1,0:T(8,128)S(1)} %get-tuple-element.78.refs_6_) | copy-start | bytes 9437188
  105.0 15.4 %collective-permute-start.16 = (bf16[2,1024,256]{2,1,0:T(8,128)(2,1)S(1)}, bf16[2,1024,256]{2,1,0:T(8,128)(2,1)S(1)}, u32[]{:S(2)}, u32[]{:S(2)}) collective-permute-start(bf16[2,1024,256]{2,1,0:T(8,128)(2,1)S(1)} %add.56.refs_4_), channel_id=1, source_target_pairs={{0,16},{1,9},{2,18},{3,11},{4,20},{5,13},{6,22},{7,15},{8,24},{9,1... | collective-permute-start | bytes 3145736 | tf_op jit(solution)/shard_map/ppermute | solution.py:47
  107.8 23.7 %collective-permute-start.19 = (bf16[2,1024,256]{2,1,0:T(8,128)(2,1)S(1)}, bf16[2,1024,256]{2,1,0:T(8,128)(2,1)S(1)}, u32[]{:S(2)}, u32[]{:S(2)}) collective-permute-start(bf16[2,1024,256]{2,1,0:T(8,128)(2,1)S(1)} %add.57.refs_4_), channel_id=1, source_target_pairs={{0,16},{1,9},{2,18},{3,11},{4,20},{5,13},{6,22},{7,15},{8,24},{9,1... | collective-permute-start | bytes 3145736 | tf_op jit(solution)/shard_map/ppermute | solution.py:47
  108.0 1.2 copy-start.8
  108.0 19.9 %collective-permute-start.20 = (bf16[384,1024]{1,0:T(8,128)(2,1)S(1)}, bf16[384,1024]{1,0:T(8,128)(2,1)S(1)}, u32[]{:S(2)}, u32[]{:S(2)}) collective-permute-start(bf16[384,1024]{1,0:T(8,128)(2,1)S(1)} %get-tuple-element.70), channel_id=1, source_target_pairs={{0,1},{1,0},{2,3},{3,2},{4,5},{5,4},{6,7},{7,6},{8,9},{9,8},{10,11... | collective-permute-start | bytes 2359304 | tf_op jit(solution)/shard_map/ppermute | solution.py:47
  108.8 11.6 %copy-start.3 = (f32[768,1024]{1,0:T(8,128)S(1)}, f32[768,1024]{1,0:T(8,128)}, u32[]{:S(2)}) copy-start(f32[768,1024]{1,0:T(8,128)} %copy-done.2) | copy-start | bytes 9437188
  108.8 31.0 %collective-permute-start.24 = (bf16[2,256,1024]{2,1,0:T(8,128)(2,1)S(1)}, bf16[2,256,1024]{2,1,0:T(8,128)(2,1)S(1)}, u32[]{:S(2)}, u32[]{:S(2)}) collective-permute-start(bf16[2,256,1024]{2,1,0:T(8,128)(2,1)S(1)} %fusion.4), channel_id=1, source_target_pairs={{0,2},{1,3},{2,0},{3,1},{4,6},{5,7},{6,4},{7,5},{8,10},{9,11},{10,... | collective-permute-start | bytes 3145736 | tf_op jit(solution)/shard_map/ppermute | solution.py:47
  109.7 30.1 %collective-permute-start.23 = (bf16[2,256,1024]{2,1,0:T(8,128)(2,1)S(1)}, bf16[2,256,1024]{2,1,0:T(8,128)(2,1)}, u32[]{:S(2)}, u32[]{:S(2)}) collective-permute-start(bf16[2,256,1024]{2,1,0:T(8,128)(2,1)S(1)} %add_convert_fusion), channel_id=1, source_target_pairs={{2,4},{3,5},{4,2},{5,3},{10,12},{11,13},{12,10},{13,11},{18,20},{1... | collective-permute-start | bytes 3145736 | tf_op jit(solution)/shard_map/ppermute | solution.py:47
  139.3 11.9 %collective-permute-start.22 = (f32[384,1024]{1,0:T(8,128)S(1)}, f32[384,1024]{1,0:T(8,128)S(1)}, u32[]{:S(2)}, u32[]{:S(2)}) collective-permute-start(f32[384,1024]{1,0:T(8,128)S(1)} %get-tuple-element.87), channel_id=1, source_target_pairs={{0,1},{1,0},{2,3},{3,2},{4,5},{5,4},{6,7},{7,6},{8,9},{9,8},{10,11... | collective-permute-start | bytes 4718600 | tf_op jit(solution)/shard_map/ppermute | solution.py:47
  139.3 11.8 %collective-permute-start.18 = (bf16[384,1024]{1,0:T(8,128)(2,1)S(1)}, bf16[384,1024]{1,0:T(8,128)(2,1)S(1)}, u32[]{:S(2)}, u32[]{:S(2)}) collective-permute-start(bf16[384,1024]{1,0:T(8,128)(2,1)S(1)} %get-tuple-element.80), channel_id=1, source_target_pairs={{0,1},{1,0},{2,3},{3,2},{4,5},{5,4},{6,7},{7,6},{8,9},{9,8},{10,11... | collective-permute-start | bytes 2359304 | tf_op jit(solution)/shard_map/ppermute | solution.py:47
  139.8 11.3 %collective-permute-start.21 = (bf16[384,1024]{1,0:T(8,128)(2,1)S(1)}, bf16[384,1024]{1,0:T(8,128)(2,1)S(1)}, u32[]{:S(2)}, u32[]{:S(2)}) collective-permute-start(bf16[384,1024]{1,0:T(8,128)(2,1)S(1)} %get-tuple-element.85), channel_id=1, source_target_pairs={{0,1},{1,0},{2,3},{3,2},{4,5},{5,4},{6,7},{7,6},{8,9},{9,8},{10,11... | collective-permute-start | bytes 2359304 | tf_op jit(solution)/shard_map/ppermute | solution.py:47
  141.9 9.2 %collective-permute-start.25 = (bf16[256,1024]{1,0:T(8,128)(2,1)S(1)}, bf16[256,1024]{1,0:T(8,128)(2,1)S(1)}, u32[]{:S(2)}, u32[]{:S(2)}) collective-permute-start(bf16[256,1024]{1,0:T(8,128)(2,1)S(1)} %get-tuple-element.95), channel_id=1, source_target_pairs={{0,8},{1,17},{2,10},{3,19},{4,12},{5,21},{6,14},{7,23},{8,0},{9,25... | collective-permute-start | bytes 1572872 | tf_op jit(solution)/shard_map/ppermute | solution.py:47

commit v10 on v9

--- a/solution.py
+++ b/solution.py
@@ -123,14 +123,15 @@
     )(place, activations, other, cot_mine, cot_other)
 
 
-def term_kernel(place, mine, other, turned, keep2, keep10, send2, send10):
+def term_kernel(place, mine, other, turned, *outs):
     rows = turned.shape[0] // 2
-    for first in (True, False):
-
-        @pl.when((pl.program_id(0) == 0) == first)
+    for i in range(3):
+
+        @pl.when(pl.program_id(0) == i)
         def _():
             tall = jnp.concatenate([mine[...], other[...]], 0)
-            for b, out in ((1, send2 if first else send10), (0, keep2 if first else keep10)):
+            for b in (1, 0):
+                out = outs[3 * b + i]
                 part = turned[b * rows : (b + 1) * rows]
                 out[...] = (
                     jnp.dot(part, tall, preferred_element_type=F32).astype(BF16).reshape(out.shape)
@@ -142,26 +143,23 @@
     part, cols = rows // 2, columns // 4
     mine = pl.BlockSpec((tokens, part), lambda i, r, s: (0, 2 * (2 * (s[0] ^ (2 - i)) + s[1]) + r))
     pieces = [
-        pl.BlockSpec((2, cols, part), lambda i, r, s: (0, 0, jnp.where(i == 0, r, 1))),
-        pl.BlockSpec(
-            (1, 2, cols, part),
-            lambda i, r, s: (jnp.where(i == 2, 0, 1), 0, 0, jnp.where(i == 0, 0, r)),
-        ),
+        pl.BlockSpec((2, cols, part), lambda i, r, s, n=n: (0, 0, jnp.clip(2 * (i - n) + r, 0, 1)))
+        for n in range(3)
     ]
     return pl.pallas_call(
         term_kernel,
         grid_spec=pltpu.PrefetchScalarGridSpec(
             num_scalar_prefetch=1,
             grid=(3, 2),
-            in_specs=[mine, mine, pl.BlockSpec(turned.shape, lambda i, r, s: (0, 0), pipeline_mode=ONCE)],
+            in_specs=[
+                mine,
+                mine,
+                pl.BlockSpec(turned.shape, lambda i, r, s: (0, 0), pipeline_mode=ONCE),
+            ],
             out_specs=pieces * 2,
         ),
-        out_shape=[
-            jax.ShapeDtypeStruct((2, cols, rows), BF16),
-            jax.ShapeDtypeStruct((2, 2, cols, rows), BF16),
-        ]
-        * 2,
-        compiler_params=pltpu.CompilerParams(vmem_limit_bytes=16 * MIB),
+        out_shape=[jax.ShapeDtypeStruct((2, cols, rows), BF16)] * 6,
+        compiler_params=pltpu.CompilerParams(vmem_limit_bytes=18 * MIB),
         cost_estimate=cost(12 * tokens * rows * columns, 12 * tokens * rows + 12 * rows * columns),
         name="terms",
     )(place, activations, other, turned)
@@ -336,50 +334,57 @@
         place, activations, other, cotangent, cot_other, rows
     )
     got3 = sent(send3, FLIP_B)
-    keep2, keep10, send2, send10 = terms(place, activations, other, turned, rows)
-    first = gate(place, after(one, keep10), mid, base_b)
-    got2 = sent(after(send2, first, got3), FLIP_B)
+    keep2, keep1, keep0, send2, send1, send0 = terms(place, activations, other, turned, rows)
+    first = gate(place, after(one, keep0), mid, base_b)
 
     sum3 = added(after(keep3, first), got3)
     far = sent(sum3, IN)
     two_mid = sent(after(one, first, sum3), MID)
     two_end = sent(after(mid, sum3), OUT)
-    one_b = sent(after(one, got3), FLIP_B)
+    got2 = sent(after(send2, sum3), FLIP_B)
+    one_b = sent(after(one, sum3), FLIP_B)
     whole, out0, keys = projected(
-        first, 0, after(activations, keep10, sum3), other, cots, base, base_b
-    )
-    got0 = sent(out0, SWAP)
-    second = gate(place, after(far, out0), two_mid, two_end, got2, one_b)
-
-    sum2_far = added(after(keep2, second), got2, far)
+        first, 0, after(activations, keep0, sum3), other, cots, base, base_b
+    )
+    got_out0 = sent(out0, SWAP)
+
+    sum2_far = added(after(far, two_mid, two_end, one_b, out0), keep2, got2)
     mid_far = sent(sum2_far, MID)
     near = sent(after(added(keep2, got2), sum2_far), IN)
-    three_end = sent(after(two_mid, second), OUT)
-    got10 = sent(after(send10, second), FLIP_B)
-    two = after(two_mid, second) + two_end
+    three_end = sent(after(two_mid, sum2_far), OUT)
+    got1 = sent(after(send1, sum2_far), FLIP_B)
+    two = after(two_mid, sum2_far) + two_end
+    two_b = sent(two, FLIP_B)
     whole, out1, keys = projected(
-        second, 1, after(activations, sum2_far), other, cots, one, one_b, (whole, None, keys)
-    )
-    got1 = sent(out1, SWAP)
-    third = gate(place, after(near, out1), mid_far, three_end, got10)
-
-    sum1 = added(after(keep10[1], third), got10[1], mid_far)
+        place, 1, after(activations, sum2_far), other, cots, one, one_b, (whole, None, keys)
+    )
+    got_out1 = sent(out1, SWAP)
+
+    sum1 = added(after(mid_far, near, three_end, two_b, out1), keep1, got1)
     sum_one = sent(sum1, PAIR)
-    sum3_near = added(sum3, after(near, third))
+    sum3_near = added(sum3, after(near, sum1))
     sum_mid = sent(sum3_near, MID)
-    two_b = sent(after(two, third), FLIP_B)
-    three = after(mid, third) + three_end
+    three = after(mid, sum1) + three_end
     three_b = sent(three, FLIP_B)
+    got0 = sent(after(send0, three_b), FLIP_B)
     whole, out2, keys = projected(
-        third, 2, after(activations, sum3_near), other, cots, two, two_b, (whole, None, keys), got0
+        place,
+        2,
+        after(activations, sum3_near),
+        other,
+        cots,
+        two,
+        two_b,
+        (whole, None, keys),
+        got_out0,
     )
     whole, out3, keys, keys_far = projected(
-        place, 3, after(activations, out2), other, cots, three, three_b, (whole, None, keys), got1
+        place, 3, after(activations, out2), other, cots, three, three_b, (whole, None, keys), got_out1
     )
     sum_mid, sum_one = after(sum_mid, out3), after(sum_one, out3)
     last = [
-        keep10[0, a].astype(F32)
-        + got10[0, a].astype(F32)
+        keep0[a].astype(F32)
+        + got0[a].astype(F32)
         + sum_mid[a].astype(F32)
         + sum_one[a].astype(F32)
         for a in (0, 1)

time: 155 us -> 159 us (1.026)
  starting transfers between devices: 31.5 us -> 45 us
  waiting for transfers between devices: 62.7 us -> 53.8 us
  Pallas kernels: 48.7 us -> 45.9 us
    ppermute x26 -> x27, starting transfers between devices: 31.5 us -> 45 us  [sent(): return lax.ppermute(array, AXES, pairs)]
    ppermute x26 -> x27, waiting for transfers between devices: 62.7 us -> 53.8 us  [sent(): return lax.ppermute(array, AXES, pairs)]
    add x2 -> x3, other arithmetic: 0.55 us -> 4.19 us  [the longest x1 2.38 us: by_hops(): keep0[a].astype(F32) + got0[a].astype(F32) + sum_mid[a].astype(F32)]
    pallas_call x3 -> x1, Pallas kernels: 3.41 us -> 1.14 us  [gate(): pl.pallas_call(kernel, in_specs=[pl.BlockSpec(memory_space=pltpu.SMEM)] +...]
    convert_element_type x1 -> x0, other arithmetic: 2.07 us -> none  [by_hops(): last[1].astype(BF16)]
    unnamed x18 -> x14, local copies, waits for them, and re-layouts: 3.19 us -> 2.8 us
  transfers between devices with their start and end apart: 26 -> 27, of which waited for: 10 -> 11; matrix products, arithmetic and copies ran while one was open for 5% -> 4% of each run, Pallas kernels for 29% -> 27%
where the time goes in v10:
time: 159 us; the launch traced here: 157 us
  waiting for transfers between devices  53.8 us (34%)
  Pallas kernels  45.9 us (29%)
  starting transfers between devices  45 us (28%)
  other arithmetic  8.89 us (6%)
  local copies, waits for them, and re-layouts  2.8 us (2%)
    ppermute x27, waiting for transfers between devices, sent(): return lax.ppermute(array, AXES, pairs)  53.8 us
    ppermute x27, starting transfers between devices, sent(): return lax.ppermute(array, AXES, pairs)  45 us
    pallas_call x4, Pallas kernels, projected(): pl.pallas_call(lambda *refs: project_kernel(*refs, first=first, last=last...  28.4 us
    pallas_call x1, Pallas kernels, terms(): pl.pallas_call(term_kernel, grid_spec=pltpu.PrefetchScalarGridSpec(num_sc...  8.66 us
    pallas_call x1, Pallas kernels, first_terms(): pl.pallas_call(first_term_kernel, grid_spec=pltpu.PrefetchScalarGridSpec(...  4.49 us
    convert_element_type x4, other arithmetic, added(): return total.astype(BF16)  3.48 us
    pallas_call x1, Pallas kernels, finished(): pl.pallas_call(lambda *refs: finish_kernel(*refs, scale=scale), grid_spec...  3.19 us
  transfers between devices with their start and end apart: 27, of which 11 were waited for; matrix products, arithmetic and copies ran while one was open for 4% of the time, Pallas kernels for 27%

profile of v10, /device:TPU:0, one launch (start us, length us, event | category | flops | bytes accessed | tf_op | source)
XLA Modules:
  0.0 157.2 jit_solution(2959806487865928779)
XLA Ops:
  0.6 0.5 collective-permute-start
  1.2 2.9 %collective-permute-start.2 = (bf16[1024,256]{1,0:T(8,128)(2,1)}, bf16[1024,256]{1,0:T(8,128)(2,1)S(1)}, u32[]{:S(2)}, u32[]{:S(2)}) collective-permute-start(bf16[1024,256]{1,0:T(8,128)(2,1)} %param.5), channel_id=1, source_target_pairs={{0,8},{1,17},{2,10},{3,19},{4,12},{5,21},{6,14},{7,23},{8,0},{9,25... | collective-permute-start | bytes 1572872 | tf_op jit(solution)/shard_map/ppermute | solution.py:47
  4.2 7.4 %collective-permute-done.2 = bf16[1024,256]{1,0:T(8,128)(2,1)S(1)} collective-permute-done((bf16[1024,256]{1,0:T(8,128)(2,1)}, bf16[1024,256]{1,0:T(8,128)(2,1)S(1)}, u32[]{:S(2)}, u32[]{:S(2)}) %collective-permute-start.2) | collective-permute-done | bytes 524320 | tf_op jit(solution)/shard_map/ppermute | solution.py:47
  11.5 1.1 pad_maximum_fusion.refs_4_
  12.7 2.2 %collective-permute-start.3 = (bf16[2,1024,256]{2,1,0:T(8,128)(2,1)S(1)}, bf16[2,1024,256]{2,1,0:T(8,128)(2,1)S(1)}, u32[]{:S(2)}, u32[]{:S(2)}) collective-permute-start(bf16[2,1024,256]{2,1,0:T(8,128)(2,1)S(1)} %pad_maximum_fusion.refs_4_), channel_id=1, source_target_pairs={{0,2},{1,3},{2,0},{3,1},{4,6},{5,7},{6,4},{7,5},{8,10},{9,11},{10,... | collective-permute-start | bytes 3145736 | tf_op jit(solution)/shard_map/ppermute | solution.py:47
  14.9 1.5 collective-permute-start.5
  16.4 0.7 collective-permute-start.4
  17.2 2.8 %copy-done = bf16[384,8192]{1,0:T(8,128)(2,1)S(1)} copy-done((bf16[384,8192]{1,0:T(8,128)(2,1)S(1)}, bf16[384,8192]{1,0:T(8,128)(2,1)}, u32[]{:S(2)}) %copy-start) | copy-done | bytes 6291480
  20.0 4.5 %terms.2 = (bf16[2,256,1024]{2,1,0:T(8,128)(2,1)S(1)}, bf16[2,256,1024]{2,1,0:T(8,128)(2,1)S(1)}, bf16[768,1024]{1,0:T(8,128)(2,1)S(1)}, bf16[1024,768]{1,0:T(8,128)(2,1)S(1)}) custom-call(s32[3]{0:T(128)S(1)} %pad_add_fusion.place.refs_0_, bf16[384,8192]{1,0:T(8,128)(2,1)S(1)} %copy-done, bf16[384,8192]{1,0:T(8,128)(2,1)} %collective-permute-done.other.refs_2_, ...), custom_call_target="tpu_custom_call" | custom-call | flops 1610612 | bytes 5767 | tf_op jit(solution)/shard_map/terms/pallas_call | solution.py:107
  24.5 0.6 collective-permute-start.6
  25.1 8.7 %terms.3 = (bf16[2,256,1024]{2,1,0:T(8,128)(2,1)S(1)}, bf16[2,256,1024]{2,1,0:T(8,128)(2,1)S(1)}, bf16[2,256,1024]{2,1,0:T(8,128)(2,1)S(1)}, bf16[2,256,1024]{2,...) custom-call(s32[3]{0:T(128)S(1)} %pad_add_fusion.place.refs_0_, ...), custom_call_target="tpu_custom_call" | custom-call | flops 4831838 | bytes 17301 | tf_op jit(solution)/shard_map/terms/pallas_call | solution.py:149
  33.7 3.7 %collective-permute-done.3.refs_1_.refs_4_ = bf16[2,1024,256]{2,1,0:T(8,128)(2,1)S(1)} collective-permute-done((bf16[2,1024,256]{2,1,0:T(8,128)(2,1)S(1)}, bf16[2,1024,256]{2,1,0:T(8,128)(2,1)S(1)}, u32[]{:S(2)}, u32[]{:S(2)}) %collective-permute-start.3) | collective-permute-done | bytes 1048608 | tf_op jit(solution)/shard_map/ppermute | solution.py:47
  37.4 1.1 gate.1.refs_0_
  38.5 2.4 %collective-permute-done.6 = bf16[2,256,1024]{2,1,0:T(8,128)(2,1)S(1)} collective-permute-done((bf16[2,256,1024]{2,1,0:T(8,128)(2,1)S(1)}, bf16[2,256,1024]{2,1,0:T(8,128)(2,1)S(1)}, u32[]{:S(2)}, u32[]{:S(2)}) %collective-permute-start.6) | collective-permute-done | bytes 1048608 | tf_op jit(solution)/shard_map/ppermute | solution.py:47
  41.4 5.6 %collective-permute-start.8 = (bf16[2,256,1024]{2,1,0:T(8,128)(2,1)S(1)}, bf16[2,256,1024]{2,1,0:T(8,128)(2,1)S(1)}, u32[]{:S(2)}, u32[]{:S(2)}) collective-permute-start(bf16[2,256,1024]{2,1,0:T(8,128)(2,1)S(1)} %add_convert_fusion.2), channel_id=1, source_target_pairs={{0,2},{1,3},{6,4},{7,5},{8,10},{9,11},{14,12},{15,13},{16,18},{17,... | collective-permute-start | bytes 3145736 | tf_op jit(solution)/shard_map/ppermute | solution.py:47
  47.0 1.6 %collective-permute-start.9 = (bf16[2,1024,256]{2,1,0:T(8,128)(2,1)S(1)}, bf16[2,1024,256]{2,1,0:T(8,128)(2,1)}, u32[]{:S(2)}, u32[]{:S(2)}) collective-permute-start(bf16[2,1024,256]{2,1,0:T(8,128)(2,1)S(1)} %collective-permute-done.3.refs_1_.refs_4_), channel_id=1, source_target_pairs={{2,4},{3,5},{4,2},{5,3},{10,12},{11,13},{12,10},{13,11},{18,20},{1... | collective-permute-start | bytes 3145736 | tf_op jit(solution)/shard_map/ppermute | solution.py:47
  48.7 1.3 collective-permute-start.10
  49.9 1.6 %collective-permute-start.11 = (bf16[2,1024,256]{2,1,0:T(8,128)(2,1)S(1)}, bf16[2,1024,256]{2,1,0:T(8,128)(2,1)S(1)}, u32[]{:S(2)}, u32[]{:S(2)}) collective-permute-start(bf16[2,1024,256]{2,1,0:T(8,128)(2,1)S(1)} %collective-permute-done.3.refs_1_.refs_4_), channel_id=1, source_target_pairs={{0,16},{1,9},{2,18},{3,11},{4,20},{5,13},{6,22},{7,15},{8,24},{9,1... | collective-permute-start | bytes 3145736 | tf_op jit(solution)/shard_map/ppermute | solution.py:47
  51.5 0.5 collective-permute-start.7
  52.0 6.5 %project.4 = (bf16[384,8192]{1,0:T(8,128)(2,1)}, bf16[384,1024]{1,0:T(8,128)(2,1)S(1)}, f32[768,1024]{1,0:T(8,128)S(1)}) custom-call(s32[3]{0:T(128)S(1)} %gate.1.refs_0_, bf16[384,8192]{1,0:T(8,128)(2,1)S(1)} %copy-done.1, bf16[384,8192]{1,0:T(8,128)(2,1)} %collective-permute-done.other.refs_2_, bf16[768,1024]{1,0:T(8,128)(2,1)S(1)} %get-tuple-element.62.refs_3_, ...), custom_call_target="tpu_custom_call" | custom-call | flops 3221225 | bytes 8388 | tf_op jit(solution)/shard_map/project/pallas_call | solution.py:229
  58.5 14.8 %collective-permute-done.10 = bf16[2,1024,256]{2,1,0:T(8,128)(2,1)S(1)} collective-permute-done((bf16[2,1024,256]{2,1,0:T(8,128)(2,1)S(1)}, bf16[2,1024,256]{2,1,0:T(8,128)(2,1)S(1)}, u32[]{:S(2)}, u32[]{:S(2)}) %collective-permute-start.10) | collective-permute-done | bytes 1048608 | tf_op jit(solution)/shard_map/ppermute | solution.py:47
  73.3 2.7 %collective-permute-done.7 = bf16[2,256,1024]{2,1,0:T(8,128)(2,1)S(1)} collective-permute-done((bf16[2,256,1024]{2,1,0:T(8,128)(2,1)S(1)}, bf16[2,256,1024]{2,1,0:T(8,128)(2,1)S(1)}, u32[]{:S(2)}, u32[]{:S(2)}) %collective-permute-start.7) | collective-permute-done | bytes 1048608 | tf_op jit(solution)/shard_map/ppermute | solution.py:47
  76.0 0.8 fusion.1
  76.9 0.7 collective-permute-start.13
  77.6 1.3 collective-permute-start.14
  78.9 1.5 add.58.refs_4_
  80.4 1.6 %collective-permute-start.15 = (bf16[2,1024,256]{2,1,0:T(8,128)(2,1)S(1)}, bf16[2,1024,256]{2,1,0:T(8,128)(2,1)S(1)}, u32[]{:S(2)}, u32[]{:S(2)}) collective-permute-start(bf16[2,1024,256]{2,1,0:T(8,128)(2,1)S(1)} %add.58.refs_4_), channel_id=1, source_target_pairs={{0,16},{1,9},{2,18},{3,11},{4,20},{5,13},{6,22},{7,15},{8,24},{9,1... | collective-permute-start | bytes 3145736 | tf_op jit(solution)/shard_map/ppermute | solution.py:47
  82.0 7.8 %collective-permute-start.12 = (bf16[2,256,1024]{2,1,0:T(8,128)(2,1)S(1)}, bf16[2,256,1024]{2,1,0:T(8,128)(2,1)S(1)}, u32[]{:S(2)}, u32[]{:S(2)}) collective-permute-start(bf16[2,256,1024]{2,1,0:T(8,128)(2,1)S(1)} %get-tuple-element.65), channel_id=1, source_target_pairs={{0,2},{1,3},{6,4},{7,5},{8,10},{9,11},{14,12},{15,13},{16,18},{17,... | collective-permute-start | bytes 3145736 | tf_op jit(solution)/shard_map/ppermute | solution.py:47
  89.8 0.6 collective-permute-start.16
  90.4 6.7 %project.5 = (bf16[384,8192]{1,0:T(8,128)(2,1)}, bf16[384,1024]{1,0:T(8,128)(2,1)S(1)}, f32[768,1024]{1,0:T(8,128)S(1)}) custom-call(s32[3]{0:T(128)S(1)} %pad_add_fusion.place.refs_0_, bf16[384,8192]{1,0:T(8,128)(2,1)S(1)} %copy-done.1, bf16[384,8192]{1,0:T(8,128)(2,1)} %collective-permute-done.other.refs_2_, ...), custom_call_target="tpu_custom_call", output_to_operand_aliasing={{0}: (7, {})} | custom-call | flops 3221225 | bytes 8388 | tf_op jit(solution)/shard_map/project/pallas_call | solution.py:229
  97.1 6.9 %collective-permute-done.14 = bf16[2,1024,256]{2,1,0:T(8,128)(2,1)S(1)} collective-permute-done((bf16[2,1024,256]{2,1,0:T(8,128)(2,1)}, bf16[2,1024,256]{2,1,0:T(8,128)(2,1)S(1)}, u32[]{:S(2)}, u32[]{:S(2)}) %collective-permute-start.14) | collective-permute-done | bytes 1048608 | tf_op jit(solution)/shard_map/ppermute | solution.py:47
  104.0 2.6 %collective-permute-done.12 = bf16[2,256,1024]{2,1,0:T(8,128)(2,1)S(1)} collective-permute-done((bf16[2,256,1024]{2,1,0:T(8,128)(2,1)S(1)}, bf16[2,256,1024]{2,1,0:T(8,128)(2,1)S(1)}, u32[]{:S(2)}, u32[]{:S(2)}) %collective-permute-start.12) | collective-permute-done | bytes 1048608 | tf_op jit(solution)/shard_map/ppermute | solution.py:47
  106.7 1.9 %add_convert_fusion.1 = bf16[2,256,1024]{2,1,0:T(8,128)(2,1)S(1)} fusion(bf16[2,256,1024]{2,1,0:T(8,128)(2,1)} %collective-permute-done.16, bf16[2,256,1024]{2,1,0:T(8,128)(2,1)S(1)} %get-tuple-element.72, bf16[2,256,1024]{2,1,0:T(8,128)(2,1)S(1)} %collective-permute-done.13), kind=kLoop, calls=%fused_computation.6 | loop fusion | flops 3145728 | bytes 4194304 | tf_op jit(solution)/shard_map/convert_element_type | solution.py:320
  108.9 2.6 %collective-permute-start.19 = (bf16[2,1024,256]{2,1,0:T(8,128)(2,1)S(1)}, bf16[2,1024,256]{2,1,0:T(8,128)(2,1)S(1)}, u32[]{:S(2)}, u32[]{:S(2)}) collective-permute-start(bf16[2,1024,256]{2,1,0:T(8,128)(2,1)S(1)} %add.62.refs_4_), channel_id=1, source_target_pairs={{0,16},{1,9},{2,18},{3,11},{4,20},{5,13},{6,22},{7,15},{8,24},{9,1... | collective-permute-start | bytes 3145736 | tf_op jit(solution)/shard_map/ppermute | solution.py:47
  111.5 0.5 collective-permute-start.20
  112.4 0.7 collective-permute-start.24
  113.1 6.1 %collective-permute-start.25 = (bf16[2,256,1024]{2,1,0:T(8,128)(2,1)S(1)}, bf16[2,256,1024]{2,1,0:T(8,128)(2,1)}, u32[]{:S(2)}, u32[]{:S(2)}) collective-permute-start(bf16[2,256,1024]{2,1,0:T(8,128)(2,1)S(1)} %add_convert_fusion.1), channel_id=1, source_target_pairs={{0,2},{1,3},{2,0},{3,1},{4,6},{5,7},{6,4},{7,5},{8,10},{9,11},{10,... | collective-permute-start | bytes 3145736 | tf_op jit(solution)/shard_map/ppermute | solution.py:47
  119.3 5.0 %collective-permute-done.19.refs_5_ = bf16[2,1024,256]{2,1,0:T(8,128)(2,1)S(1)} collective-permute-done((bf16[2,1024,256]{2,1,0:T(8,128)(2,1)S(1)}, bf16[2,1024,256]{2,1,0:T(8,128)(2,1)S(1)}, u32[]{:S(2)}, u32[]{:S(2)}) %collective-permute-start.19) | collective-permute-done | bytes 1048608 | tf_op jit(solution)/shard_map/ppermute | solution.py:47
  124.3 2.0 %collective-permute-start.23 = (bf16[2,256,1024]{2,1,0:T(8,128)(2,1)S(1)}, bf16[2,256,1024]{2,1,0:T(8,128)(2,1)}, u32[]{:S(2)}, u32[]{:S(2)}) collective-permute-start(bf16[2,256,1024]{2,1,0:T(8,128)(2,1)S(1)} %copy-done.4), channel_id=1, source_target_pairs={{0,16},{1,9},{2,18},{3,11},{4,20},{5,13},{6,22},{7,15},{8,24},{9,1... | collective-permute-start | bytes 3145736 | tf_op jit(solution)/shard_map/ppermute | solution.py:47
  126.3 7.5 %project.6 = (bf16[384,8192]{1,0:T(8,128)(2,1)}, bf16[384,1024]{1,0:T(8,128)(2,1)S(1)}, f32[768,1024]{1,0:T(8,128)S(1)}) custom-call(s32[3]{0:T(128)S(1)} %pad_add_fusion.place.refs_0_, bf16[384,8192]{1,0:T(8,128)(2,1)S(1)} %copy-done.1, bf16[384,8192]{1,0:T(8,128)(2,1)} %collective-permute-done.other.refs_2_, ...), custom_call_target="tpu_custom_call", output_to_operand_aliasing={{0}: (8, {})} | custom-call | flops 3221225 | bytes 8388 | tf_op jit(solution)/shard_map/project/pallas_call | solution.py:229
  133.8 7.7 %project.7 = (bf16[384,8192]{1,0:T(8,128)(2,1)}, bf16[384,1024]{1,0:T(8,128)(2,1)S(1)}, f32[384,1024]{1,0:T(8,128)S(1)}, f32[384,1024]{1,0:T(8,128)S(1)}) custom-call(s32[3]{0:T(128)S(1)} %pad_add_fusion.place.refs_0_, bf16[384,8192]{1,0:T(8,128)(2,1)S(1)} %copy-done.1, ...), custom_call_target="tpu_custom_call", output_to_operand_aliasing={{0}: (8, {})} | custom-call | flops 3221225 | bytes 8388 | tf_op jit(solution)/shard_map/project/pallas_call | solution.py:229
  141.5 0.5 collective-permute-start.18
  142.0 0.4 collective-permute-done.25
  142.4 2.4 %fusion.2 = (bf16[256,1024]{1,0:T(8,128)(2,1)S(1)}, f32[256,1024]{1,0:T(8,128)S(1)}) fusion(bf16[2,256,1024]{2,1,0:T(8,128)(2,1)} %collective-permute-done.23, bf16[2,256,1024]{2,1,0:T(8,128)(2,1)} %collective-permute-done.25, bf16[2,256,1024]{2,1,0:T(8,128)(2,1)S(1)} %collective-permute-done.24, bf16[2,256,1024]{2,1,0:T(8,128)(2,1)S(1)} %get-tuple-element.51), kind=kLoop, calls=%fused_computation.11 | loop fusion | flops 3932160 | bytes 5767168 | tf_op jit(solution)/shard_map/add | solution.py:386
  144.8 1.4 collective-permute-start.26
  146.2 1.0 collective-permute-done.21.refs_2_
  147.1 6.9 %collective-permute-done.26.refs_6_ = bf16[256,1024]{1,0:T(8,128)(2,1)S(1)} collective-permute-done((bf16[256,1024]{1,0:T(8,128)(2,1)S(1)}, bf16[256,1024]{1,0:T(8,128)(2,1)S(1)}, u32[]{:S(2)}, u32[]{:S(2)}) %collective-permute-start.26) | collective-permute-done | bytes 524320 | tf_op jit(solution)/shard_map/ppermute | solution.py:47
  154.1 3.2 %finish.1 = (bf16[384,8192]{1,0:T(8,128)(2,1)}, bf16[384,1024]{1,0:T(8,128)(2,1)}, bf16[1024,256]{1,0:T(8,128)(2,1)}) custom-call(s32[3]{0:T(128)S(1)} %pad_add_fusion.place.refs_0_, bf16[384,1024]{1,0:T(8,128)(2,1)S(1)} %collective-permute-done.18.refs_1_, bf16[384,1024]{1,0:T(8,128)(2,1)S(1)} %collective-permute-done.21.refs_2_, ...), custom_call_target="tpu_custom_call", output_to_operand_aliasing={{0}: (7, {})} | custom-call | bytes 7077 | tf_op jit(solution)/shard_map/finish/pallas_call | solution.py:284
  (37 shorter events, 1.3 us)
Async XLA Ops:
  0.6 16.6 %copy-start.2 = (bf16[384,1024]{1,0:T(8,128)(2,1)S(1)}, bf16[384,1024]{1,0:T(8,128)(2,1)}, u32[]{:S(2)}) copy-start(bf16[384,1024]{1,0:T(8,128)(2,1)} %cot_mine.1) | copy-start | bytes 2359300
  0.6 16.5 %collective-permute-start = (bf16[384,8192]{1,0:T(8,128)(2,1)}, bf16[384,8192]{1,0:T(8,128)(2,1)}, u32[]{:S(2)}, u32[]{:S(2)}) collective-permute-start(bf16[384,8192]{1,0:T(8,128)(2,1)} %refs_1_.3), channel_id=1, source_target_pairs={{0,1},{1,0},{2,3},{3,2},{4,5},{5,4},{6,7},{7,6},{8,9},{9,8},{10,11... | collective-permute-start | bytes 18874376 | tf_op jit(solution)/shard_map/ppermute | solution.py:47
  1.2 16.0 %collective-permute-start.1 = (bf16[384,1024]{1,0:T(8,128)(2,1)}, bf16[384,1024]{1,0:T(8,128)(2,1)S(1)}, u32[]{:S(2)}, u32[]{:S(2)}) collective-permute-start(bf16[384,1024]{1,0:T(8,128)(2,1)} %cot_mine.1), channel_id=1, source_target_pairs={{0,1},{1,0},{2,3},{3,2},{4,5},{5,4},{6,7},{7,6},{8,9},{9,8},{10,11... | collective-permute-start | bytes 2359304 | tf_op jit(solution)/shard_map/ppermute | solution.py:47
  1.2 10.3 %collective-permute-start.2 = (bf16[1024,256]{1,0:T(8,128)(2,1)}, bf16[1024,256]{1,0:T(8,128)(2,1)S(1)}, u32[]{:S(2)}, u32[]{:S(2)}) collective-permute-start(bf16[1024,256]{1,0:T(8,128)(2,1)} %param.5), channel_id=1, source_target_pairs={{0,8},{1,17},{2,10},{3,19},{4,12},{5,21},{6,14},{7,23},{8,0},{9,25... | collective-permute-start | bytes 1572872 | tf_op jit(solution)/shard_map/ppermute | solution.py:47
  12.7 24.7 %collective-permute-start.3 = (bf16[2,1024,256]{2,1,0:T(8,128)(2,1)S(1)}, bf16[2,1024,256]{2,1,0:T(8,128)(2,1)S(1)}, u32[]{:S(2)}, u32[]{:S(2)}) collective-permute-start(bf16[2,1024,256]{2,1,0:T(8,128)(2,1)S(1)} %pad_maximum_fusion.refs_4_), channel_id=1, source_target_pairs={{0,2},{1,3},{2,0},{3,1},{4,6},{5,7},{6,4},{7,5},{8,10},{9,11},{10,... | collective-permute-start | bytes 3145736 | tf_op jit(solution)/shard_map/ppermute | solution.py:47
  14.9 22.5 %collective-permute-start.5 = (bf16[2,1024,256]{2,1,0:T(8,128)(2,1)S(1)}, bf16[2,1024,256]{2,1,0:T(8,128)(2,1)S(1)}, u32[]{:S(2)}, u32[]{:S(2)}) collective-permute-start(bf16[2,1024,256]{2,1,0:T(8,128)(2,1)S(1)} %pad_maximum_fusion.refs_4_), channel_id=1, source_target_pairs={{0,16},{1,9},{2,18},{3,11},{4,20},{5,13},{6,22},{7,15},{8,24},{9,1... | collective-permute-start | bytes 3145736 | tf_op jit(solution)/shard_map/ppermute | solution.py:47
  16.4 21.0 %collective-permute-start.4 = (bf16[2,1024,256]{2,1,0:T(8,128)(2,1)S(1)}, bf16[2,1024,256]{2,1,0:T(8,128)(2,1)S(1)}, u32[]{:S(2)}, u32[]{:S(2)}) collective-permute-start(bf16[2,1024,256]{2,1,0:T(8,128)(2,1)S(1)} %pad_maximum_fusion.refs_4_), channel_id=1, source_target_pairs={{2,4},{3,5},{4,2},{5,3},{10,12},{11,13},{12,10},{13,11},{18,20},{1... | collective-permute-start | bytes 3145736 | tf_op jit(solution)/shard_map/ppermute | solution.py:47
  17.2 2.8 %copy-start = (bf16[384,8192]{1,0:T(8,128)(2,1)S(1)}, bf16[384,8192]{1,0:T(8,128)(2,1)}, u32[]{:S(2)}) copy-start(bf16[384,8192]{1,0:T(8,128)(2,1)} %refs_1_.3) | copy-start | bytes 18874372
  20.0 5.1 %copy-start.1 = (bf16[384,8192]{1,0:T(8,128)(2,1)S(1)}, bf16[384,8192]{1,0:T(8,128)(2,1)}, u32[]{:S(2)}) copy-start(bf16[384,8192]{1,0:T(8,128)(2,1)} %refs_1_.3) | copy-start | bytes 18874372
  24.5 16.5 %collective-permute-start.6 = (bf16[2,256,1024]{2,1,0:T(8,128)(2,1)S(1)}, bf16[2,256,1024]{2,1,0:T(8,128)(2,1)S(1)}, u32[]{:S(2)}, u32[]{:S(2)}) collective-permute-start(bf16[2,256,1024]{2,1,0:T(8,128)(2,1)S(1)} %get-tuple-element.54), channel_id=1, source_target_pairs={{0,16},{1,9},{2,18},{3,11},{4,20},{5,13},{6,22},{7,15},{8,24},{9,1... | collective-permute-start | bytes 3145736 | tf_op jit(solution)/shard_map/ppermute | solution.py:47
  33.7 7.6 %copy-start.3 = (bf16[2,256,1024]{2,1,0:T(8,128)(2,1)}, bf16[2,256,1024]{2,1,0:T(8,128)(2,1)S(1)}, u32[]{:S(2)}) copy-start(bf16[2,256,1024]{2,1,0:T(8,128)(2,1)S(1)} %get-tuple-element.88) | copy-start | bytes 3145732
  41.4 17.1 %copy-start.5 = (bf16[2,256,1024]{2,1,0:T(8,128)(2,1)}, bf16[2,256,1024]{2,1,0:T(8,128)(2,1)S(1)}, u32[]{:S(2)}) copy-start(bf16[2,256,1024]{2,1,0:T(8,128)(2,1)S(1)} %add_convert_fusion.2) | copy-start | bytes 3145732
  41.4 31.9 %collective-permute-start.8 = (bf16[2,256,1024]{2,1,0:T(8,128)(2,1)S(1)}, bf16[2,256,1024]{2,1,0:T(8,128)(2,1)S(1)}, u32[]{:S(2)}, u32[]{:S(2)}) collective-permute-start(bf16[2,256,1024]{2,1,0:T(8,128)(2,1)S(1)} %add_convert_fusion.2), channel_id=1, source_target_pairs={{0,2},{1,3},{6,4},{7,5},{8,10},{9,11},{14,12},{15,13},{16,18},{17,... | collective-permute-start | bytes 3145736 | tf_op jit(solution)/shard_map/ppermute | solution.py:47
  47.0 11.5 %collective-permute-start.9 = (bf16[2,1024,256]{2,1,0:T(8,128)(2,1)S(1)}, bf16[2,1024,256]{2,1,0:T(8,128)(2,1)}, u32[]{:S(2)}, u32[]{:S(2)}) collective-permute-start(bf16[2,1024,256]{2,1,0:T(8,128)(2,1)S(1)} %collective-permute-done.3.refs_1_.refs_4_), channel_id=1, source_target_pairs={{2,4},{3,5},{4,2},{5,3},{10,12},{11,13},{12,10},{13,11},{18,20},{1... | collective-permute-start | bytes 3145736 | tf_op jit(solution)/shard_map/ppermute | solution.py:47
  48.7 24.7 %collective-permute-start.10 = (bf16[2,1024,256]{2,1,0:T(8,128)(2,1)S(1)}, bf16[2,1024,256]{2,1,0:T(8,128)(2,1)S(1)}, u32[]{:S(2)}, u32[]{:S(2)}) collective-permute-start(bf16[2,1024,256]{2,1,0:T(8,128)(2,1)S(1)} %collective-permute-done.4.refs_2_), channel_id=1, source_target_pairs={{2,0},{3,1},{4,6},{5,7},{10,8},{11,9},{12,14},{13,15},{18,16},{19,... | collective-permute-start | bytes 3145736 | tf_op jit(solution)/shard_map/ppermute | solution.py:47
  49.9 23.4 %collective-permute-start.11 = (bf16[2,1024,256]{2,1,0:T(8,128)(2,1)S(1)}, bf16[2,1024,256]{2,1,0:T(8,128)(2,1)S(1)}, u32[]{:S(2)}, u32[]{:S(2)}) collective-permute-start(bf16[2,1024,256]{2,1,0:T(8,128)(2,1)S(1)} %collective-permute-done.3.refs_1_.refs_4_), channel_id=1, source_target_pairs={{0,16},{1,9},{2,18},{3,11},{4,20},{5,13},{6,22},{7,15},{8,24},{9,1... | collective-permute-start | bytes 3145736 | tf_op jit(solution)/shard_map/ppermute | solution.py:47
  51.5 24.5 %collective-permute-start.7 = (bf16[2,256,1024]{2,1,0:T(8,128)(2,1)S(1)}, bf16[2,256,1024]{2,1,0:T(8,128)(2,1)S(1)}, u32[]{:S(2)}, u32[]{:S(2)}) collective-permute-start(bf16[2,256,1024]{2,1,0:T(8,128)(2,1)S(1)} %get-tuple-element.57), channel_id=1, source_target_pairs={{0,16},{1,9},{2,18},{3,11},{4,20},{5,13},{6,22},{7,15},{8,24},{9,1... | collective-permute-start | bytes 3145736 | tf_op jit(solution)/shard_map/ppermute | solution.py:47
  76.9 29.8 %collective-permute-start.13 = (bf16[2,256,1024]{2,1,0:T(8,128)(2,1)S(1)}, bf16[2,256,1024]{2,1,0:T(8,128)(2,1)S(1)}, u32[]{:S(2)}, u32[]{:S(2)}) collective-permute-start(bf16[2,256,1024]{2,1,0:T(8,128)(2,1)S(1)} %get-tuple-element.97), channel_id=1, source_target_pairs={{2,4},{3,5},{4,2},{5,3},{10,12},{11,13},{12,10},{13,11},{18,20},{1... | collective-permute-start | bytes 3145736 | tf_op jit(solution)/shard_map/ppermute | solution.py:47
  77.6 26.4 %collective-permute-start.14 = (bf16[2,1024,256]{2,1,0:T(8,128)(2,1)}, bf16[2,1024,256]{2,1,0:T(8,128)(2,1)S(1)}, u32[]{:S(2)}, u32[]{:S(2)}) collective-permute-start(bf16[2,1024,256]{2,1,0:T(8,128)(2,1)} %collective-permute-done.9), channel_id=1, source_target_pairs={{2,0},{3,1},{4,6},{5,7},{10,8},{11,9},{12,14},{13,15},{18,16},{19,... | collective-permute-start | bytes 3145736 | tf_op jit(solution)/shard_map/ppermute | solution.py:47
  80.4 16.7 %collective-permute-start.15 = (bf16[2,1024,256]{2,1,0:T(8,128)(2,1)S(1)}, bf16[2,1024,256]{2,1,0:T(8,128)(2,1)S(1)}, u32[]{:S(2)}, u32[]{:S(2)}) collective-permute-start(bf16[2,1024,256]{2,1,0:T(8,128)(2,1)S(1)} %add.58.refs_4_), channel_id=1, source_target_pairs={{0,16},{1,9},{2,18},{3,11},{4,20},{5,13},{6,22},{7,15},{8,24},{9,1... | collective-permute-start | bytes 3145736 | tf_op jit(solution)/shard_map/ppermute | solution.py:47
  82.0 24.7 %collective-permute-start.12 = (bf16[2,256,1024]{2,1,0:T(8,128)(2,1)S(1)}, bf16[2,256,1024]{2,1,0:T(8,128)(2,1)S(1)}, u32[]{:S(2)}, u32[]{:S(2)}) collective-permute-start(bf16[2,256,1024]{2,1,0:T(8,128)(2,1)S(1)} %get-tuple-element.65), channel_id=1, source_target_pairs={{0,2},{1,3},{6,4},{7,5},{8,10},{9,11},{14,12},{15,13},{16,18},{17,... | collective-permute-start | bytes 3145736 | tf_op jit(solution)/shard_map/ppermute | solution.py:47
  89.8 16.8 %collective-permute-start.16 = (bf16[2,256,1024]{2,1,0:T(8,128)(2,1)S(1)}, bf16[2,256,1024]{2,1,0:T(8,128)(2,1)}, u32[]{:S(2)}, u32[]{:S(2)}) collective-permute-start(bf16[2,256,1024]{2,1,0:T(8,128)(2,1)S(1)} %get-tuple-element.74), channel_id=1, source_target_pairs={{0,16},{1,9},{2,18},{3,11},{4,20},{5,13},{6,22},{7,15},{8,24},{9,1... | collective-permute-start | bytes 3145736 | tf_op jit(solution)/shard_map/ppermute | solution.py:47
  108.6 3.4 %copy-start.6 = (bf16[2,256,1024]{2,1,0:T(8,128)(2,1)S(1)}, bf16[2,256,1024]{2,1,0:T(8,128)(2,1)}, u32[]{:S(2)}) copy-start(bf16[2,256,1024]{2,1,0:T(8,128)(2,1)} %copy-done.5) | copy-start | bytes 3145732
  108.8 15.4 %copy-start.4 = (bf16[2,256,1024]{2,1,0:T(8,128)(2,1)S(1)}, bf16[2,256,1024]{2,1,0:T(8,128)(2,1)}, u32[]{:S(2)}) copy-start(bf16[2,256,1024]{2,1,0:T(8,128)(2,1)} %copy-done.3) | copy-start | bytes 3145732
  108.9 15.4 %collective-permute-start.19 = (bf16[2,1024,256]{2,1,0:T(8,128)(2,1)S(1)}, bf16[2,1024,256]{2,1,0:T(8,128)(2,1)S(1)}, u32[]{:S(2)}, u32[]{:S(2)}) collective-permute-start(bf16[2,1024,256]{2,1,0:T(8,128)(2,1)S(1)} %add.62.refs_4_), channel_id=1, source_target_pairs={{0,16},{1,9},{2,18},{3,11},{4,20},{5,13},{6,22},{7,15},{8,24},{9,1... | collective-permute-start | bytes 3145736 | tf_op jit(solution)/shard_map/ppermute | solution.py:47
  111.5 14.8 %collective-permute-start.17 = (bf16[384,1024]{1,0:T(8,128)(2,1)S(1)}, bf16[384,1024]{1,0:T(8,128)(2,1)S(1)}, u32[]{:S(2)}, u32[]{:S(2)}) collective-permute-start(bf16[384,1024]{1,0:T(8,128)(2,1)S(1)} %get-tuple-element.63), channel_id=1, source_target_pairs={{0,1},{1,0},{2,3},{3,2},{4,5},{5,4},{6,7},{7,6},{8,9},{9,8},{10,11... | collective-permute-start | bytes 2359304 | tf_op jit(solution)/shard_map/ppermute | solution.py:47
  111.5 22.3 %collective-permute-start.20 = (bf16[384,1024]{1,0:T(8,128)(2,1)S(1)}, bf16[384,1024]{1,0:T(8,128)(2,1)S(1)}, u32[]{:S(2)}, u32[]{:S(2)}) collective-permute-start(bf16[384,1024]{1,0:T(8,128)(2,1)S(1)} %get-tuple-element.70), channel_id=1, source_target_pairs={{0,1},{1,0},{2,3},{3,2},{4,5},{5,4},{6,7},{7,6},{8,9},{9,8},{10,11... | collective-permute-start | bytes 2359304 | tf_op jit(solution)/shard_map/ppermute | solution.py:47
  112.4 29.6 %collective-permute-start.24 = (bf16[2,256,1024]{2,1,0:T(8,128)(2,1)S(1)}, bf16[2,256,1024]{2,1,0:T(8,128)(2,1)S(1)}, u32[]{:S(2)}, u32[]{:S(2)}) collective-permute-start(bf16[2,256,1024]{2,1,0:T(8,128)(2,1)S(1)} %add_convert_fusion), channel_id=1, source_target_pairs={{2,4},{3,5},{4,2},{5,3},{10,12},{11,13},{12,10},{13,11},{18,20},{1... | collective-permute-start | bytes 3145736 | tf_op jit(solution)/shard_map/ppermute | solution.py:47
  113.1 29.3 %collective-permute-start.25 = (bf16[2,256,1024]{2,1,0:T(8,128)(2,1)S(1)}, bf16[2,256,1024]{2,1,0:T(8,128)(2,1)}, u32[]{:S(2)}, u32[]{:S(2)}) collective-permute-start(bf16[2,256,1024]{2,1,0:T(8,128)(2,1)S(1)} %add_convert_fusion.1), channel_id=1, source_target_pairs={{0,2},{1,3},{2,0},{3,1},{4,6},{5,7},{6,4},{7,5},{8,10},{9,11},{10,... | collective-permute-start | bytes 3145736 | tf_op jit(solution)/shard_map/ppermute | solution.py:47
  124.3 18.2 %collective-permute-start.23 = (bf16[2,256,1024]{2,1,0:T(8,128)(2,1)S(1)}, bf16[2,256,1024]{2,1,0:T(8,128)(2,1)}, u32[]{:S(2)}, u32[]{:S(2)}) collective-permute-start(bf16[2,256,1024]{2,1,0:T(8,128)(2,1)S(1)} %copy-done.4), channel_id=1, source_target_pairs={{0,16},{1,9},{2,18},{3,11},{4,20},{5,13},{6,22},{7,15},{8,24},{9,1... | collective-permute-start | bytes 3145736 | tf_op jit(solution)/shard_map/ppermute | solution.py:47
  141.5 12.6 %collective-permute-start.22 = (f32[384,1024]{1,0:T(8,128)S(1)}, f32[384,1024]{1,0:T(8,128)S(1)}, u32[]{:S(2)}, u32[]{:S(2)}) collective-permute-start(f32[384,1024]{1,0:T(8,128)S(1)} %get-tuple-element.86), channel_id=1, source_target_pairs={{0,1},{1,0},{2,3},{3,2},{4,5},{5,4},{6,7},{7,6},{8,9},{9,8},{10,11... | collective-permute-start | bytes 4718600 | tf_op jit(solution)/shard_map/ppermute | solution.py:47
  141.5 4.7 %collective-permute-start.18 = (bf16[384,1024]{1,0:T(8,128)(2,1)S(1)}, bf16[384,1024]{1,0:T(8,128)(2,1)S(1)}, u32[]{:S(2)}, u32[]{:S(2)}) collective-permute-start(bf16[384,1024]{1,0:T(8,128)(2,1)S(1)} %get-tuple-element.79), channel_id=1, source_target_pairs={{0,1},{1,0},{2,3},{3,2},{4,5},{5,4},{6,7},{7,6},{8,9},{9,8},{10,11... | collective-permute-start | bytes 2359304 | tf_op jit(solution)/shard_map/ppermute | solution.py:47
  142.0 5.1 %collective-permute-start.21 = (bf16[384,1024]{1,0:T(8,128)(2,1)S(1)}, bf16[384,1024]{1,0:T(8,128)(2,1)S(1)}, u32[]{:S(2)}, u32[]{:S(2)}) collective-permute-start(bf16[384,1024]{1,0:T(8,128)(2,1)S(1)} %get-tuple-element.84), channel_id=1, source_target_pairs={{0,1},{1,0},{2,3},{3,2},{4,5},{5,4},{6,7},{7,6},{8,9},{9,8},{10,11... | collective-permute-start | bytes 2359304 | tf_op jit(solution)/shard_map/ppermute | solution.py:47
  144.8 9.2 %collective-permute-start.26 = (bf16[256,1024]{1,0:T(8,128)(2,1)S(1)}, bf16[256,1024]{1,0:T(8,128)(2,1)S(1)}, u32[]{:S(2)}, u32[]{:S(2)}) collective-permute-start(bf16[256,1024]{1,0:T(8,128)(2,1)S(1)} %get-tuple-element.95), channel_id=1, source_target_pairs={{0,8},{1,17},{2,10},{3,19},{4,12},{5,21},{6,14},{7,23},{8,0},{9,25... | collective-permute-start | bytes 1572872 | tf_op jit(solution)/shard_map/ppermute | solution.py:47

commit v11 on v10

--- a/solution.py
+++ b/solution.py
@@ -165,80 +165,62 @@
     )(place, activations, other, turned)
 
 
-def project_kernel(place, acts, other, cots, here, there, *refs, first, last, lays):
-    near, far, *keys = refs[0 if first else 2 + lays : -1]
+def project_kernel(place, acts, other, cots, here, there, *refs, first, last):
+    near, far, *keys = refs[0 if first else 2 : -1]
     acc = refs[-1]
     tokens, cols = acts.shape[0], here.shape[2]
     step = pl.program_id(0)
 
-    @pl.when(step < 2)
+    weight = jnp.concatenate([here[0], here[1], there[0], there[1]], 1)
+    total = lax.dot_general(
+        cots[...], weight, (((1,), (1,)), ((), ())), preferred_element_type=F32
+    ).astype(BF16)
+    near[...] = total[:tokens]
+    far[...] = total[tokens:]
+    tall = jnp.concatenate([acts[...], other[...]], 0)
+    sums = jnp.dot(tall, weight, preferred_element_type=F32)
+
+    @pl.when(step == 0)
     def _():
-        weight = jnp.concatenate([here[0], here[1], there[0], there[1]], 1)
-        total = lax.dot_general(
-            cots[...], weight, (((1,), (1,)), ((), ())), preferred_element_type=F32
-        ).astype(BF16)
-        near[...] = total[:tokens]
-        far[...] = total[tokens:]
-        tall = jnp.concatenate([acts[...], other[...]], 0)
-        sums = jnp.dot(tall, weight, preferred_element_type=F32)
-
-        @pl.when(step == 0)
-        def _():
-            acc[...] = sums if first else refs[0][...] + sums
-
-        @pl.when(step == 1)
-        def _():
-            if last:
-                for b in (0, 1):
-                    for a in (0, 1):
-                        at = pl.ds(pl.multiple_of(column_block(place, a, b) * cols, cols), cols)
-                        to = slice((2 * b + a) * cols, (2 * b + a + 1) * cols)
-                        keys[0][:, at] = acc[:tokens, to] + sums[:tokens, to]
-                        keys[1][:, at] = acc[tokens:, to] + sums[tokens:, to]
-            else:
-                keys[0][...] = acc[...] + sums
-
-    if lays:
-
-        @pl.when(step >= 2)
-        def _():
-            near[...] = refs[1][...]
-
-
-def projected(place, k, activations, other, cots, here, there, so_far=None, got=None):
+        acc[...] = sums if first else refs[0][...] + sums
+
+    @pl.when(step == 1)
+    def _():
+        if last:
+            for b in (0, 1):
+                for a in (0, 1):
+                    at = pl.ds(pl.multiple_of(column_block(place, a, b) * cols, cols), cols)
+                    to = slice((2 * b + a) * cols, (2 * b + a + 1) * cols)
+                    keys[0][:, at] = acc[:tokens, to] + sums[:tokens, to]
+                    keys[1][:, at] = acc[tokens:, to] + sums[tokens:, to]
+        else:
+            keys[0][...] = acc[...] + sums
+
+
+def projected(place, k, activations, other, cots, here, there, so_far=None):
     tokens, columns = activations.shape[0], cots.shape[1]
     _, rows, cols = here.shape
     part = rows // 2
-    first, last, lays = k == 0, k == 3, got is not None
+    first, last = k == 0, k == 3
 
     def whole(*shape):
         return pl.BlockSpec(shape, lambda r, s: (0, 0))
 
     held = pl.BlockSpec((2 * tokens, columns), lambda r, s: (0, 0), pipeline_mode=ONCE)
 
-    def out_at(r, s):
-        own = 2 * (2 * (s[0] ^ k) + s[1]) + r
-        received = 2 * (2 * (s[0] ^ (k - 2)) + 1 - s[1]) + r - 2
-        return (0, jnp.where(r < 2, own, received) if lays else own)
-
     mine = pl.BlockSpec(
-        (tokens, part), lambda r, s: (0, 2 * (2 * (s[0] ^ k) + s[1]) + jnp.minimum(r, 1))
-    )
-    piece = pl.BlockSpec((2, part, cols), lambda r, s: (0, jnp.minimum(r, 1), 0))
+        (tokens, part), lambda r, s: (0, 2 * (2 * (s[0] ^ k) + s[1]) + r)
+    )
+    piece = pl.BlockSpec((2, part, cols), lambda r, s: (0, r, 0))
     one = jax.ShapeDtypeStruct((tokens, columns), F32)
     return pl.pallas_call(
-        lambda *refs: project_kernel(*refs, first=first, last=last, lays=lays),
+        lambda *refs: project_kernel(*refs, first=first, last=last),
         grid_spec=pltpu.PrefetchScalarGridSpec(
             num_scalar_prefetch=1,
-            grid=(4 if lays else 2,),
+            grid=(2,),
             in_specs=[mine, mine, held, piece, piece]
-            + ([] if first else [held])
-            + ([pl.BlockSpec((tokens, part), lambda r, s: (0, jnp.maximum(r - 2, 0)))] * lays)
-            + ([] if first else [pl.BlockSpec(memory_space=pl.ANY)]),
-            out_specs=[
-                pl.BlockSpec((tokens, part), out_at),
-                pl.BlockSpec((tokens, part), lambda r, s: (0, jnp.minimum(r, 1))),
-            ]
+            + ([] if first else [held, pl.BlockSpec(memory_space=pl.ANY)]),
+            out_specs=[mine, pl.BlockSpec((tokens, part), lambda r, s: (0, r))]
             + ([whole(tokens, columns)] * 2 if last else [whole(2 * tokens, columns)]),
             scratch_shapes=[pltpu.VMEM((2 * tokens, columns), F32)],
         ),
@@ -247,7 +229,7 @@
             jax.ShapeDtypeStruct((tokens, rows), BF16),
         ]
         + ([one, one] if last else [jax.ShapeDtypeStruct((2 * tokens, columns), F32)]),
-        input_output_aliases={} if first else {7 + lays: 0},
+        input_output_aliases={} if first else {7: 0},
         compiler_params=pltpu.CompilerParams(vmem_limit_bytes=28 * MIB),
         cost_estimate=cost(
             8 * tokens * rows * columns,
@@ -256,39 +238,56 @@
         name="project",
     )(
         place, activations, other, cots, here, there,
-        *([] if first else [so_far[2], *([got] * lays), so_far[0]]),
-    )
-
-
-def finish_kernel(place, got2, got3, near, far, last, arrived, whole, out, keys, weight, *, scale):
-    for k, got in ((0, got2), (1, got3)):
-
-        @pl.when(lax.div(pl.program_id(0), 2) == k)
+        *([] if first else [so_far[2], so_far[0]]),
+    )
+
+
+def lay_kernel(place, *refs):
+    for k in range(3):
+
+        @pl.when(pl.program_id(0) == k)
         def _():
-            out[...] = got[...]
-
+            refs[-1][...] = refs[k][...]
+
+
+def laid(place, whole, parts):
+    tokens, rows = parts[0].shape
+    return pl.pallas_call(
+        lay_kernel,
+        grid_spec=pltpu.PrefetchScalarGridSpec(
+            num_scalar_prefetch=1,
+            grid=(3,),
+            in_specs=[pl.BlockSpec((tokens, rows), lambda i, s: (0, 0), pipeline_mode=ONCE)] * 3
+            + [pl.BlockSpec(memory_space=pl.ANY)],
+            out_specs=pl.BlockSpec((tokens, rows), lambda i, s: (0, 2 * (s[0] ^ i) + 1 - s[1])),
+        ),
+        out_shape=jax.ShapeDtypeStruct(whole.shape, BF16),
+        input_output_aliases={4: 0},
+        compiler_params=pltpu.CompilerParams(vmem_limit_bytes=8 * MIB),
+        cost_estimate=cost(0, 12 * tokens * rows),
+        name="lay",
+    )(place, *parts, whole)
+
+
+def finish_kernel(place, got, near, far, last, arrived, whole, out, keys, weight, *, scale):
+    out[...] = got[...]
     keys[...] = (near[...] + far[...]).astype(BF16)
     weight[...] = ((last[...] + arrived[...].astype(F32)) * scale).T.astype(BF16)
 
 
-def finished(place, whole, got2, got3, keys_near, keys_far, last, arrived, scale):
-    tokens, rows = got3.shape
+def finished(place, whole, got, keys_near, keys_far, last, arrived, scale):
+    tokens, rows = got.shape
     cols, columns = last.shape[0], keys_near.shape[1]
-    part = rows // 2
-    wide = pl.BlockSpec((tokens, columns // 4), lambda r, s: (0, r))
-    flat = pl.BlockSpec((cols, rows // 4), lambda r, s: (0, r))
-
-    def laid_at(r, s):
-        return (0, 2 * (2 * (s[0] ^ (2 + lax.div(r, 2))) + 1 - s[1]) + lax.rem(r, 2))
-
+    part, some = rows // 2, columns // 2
+    wide = pl.BlockSpec((tokens, some), lambda r, s: (0, r))
+    flat = pl.BlockSpec((cols, part), lambda r, s: (0, r))
     return pl.pallas_call(
         lambda *refs: finish_kernel(*refs, scale=scale),
         grid_spec=pltpu.PrefetchScalarGridSpec(
             num_scalar_prefetch=1,
-            grid=(4,),
+            grid=(2,),
             in_specs=[
-                pl.BlockSpec((tokens, part), lambda r, s: (0, jnp.minimum(r, 1))),
-                pl.BlockSpec((tokens, part), lambda r, s: (0, jnp.maximum(r - 2, 0))),
+                pl.BlockSpec((tokens, part), lambda r, s: (0, r)),
                 wide,
                 wide,
                 flat,
@@ -296,9 +295,9 @@
                 pl.BlockSpec(memory_space=pl.ANY),
             ],
             out_specs=[
-                pl.BlockSpec((tokens, part), laid_at),
+                pl.BlockSpec((tokens, part), lambda r, s: (0, 2 * (2 * (s[0] ^ 3) + 1 - s[1]) + r)),
                 wide,
-                pl.BlockSpec((rows // 4, cols), lambda r, s: (r, 0)),
+                pl.BlockSpec((part, cols), lambda r, s: (r, 0)),
             ],
         ),
         out_shape=[
@@ -306,11 +305,11 @@
             jax.ShapeDtypeStruct((tokens, columns), BF16),
             jax.ShapeDtypeStruct((rows, cols), BF16),
         ],
-        input_output_aliases={7: 0},
+        input_output_aliases={6: 0},
         compiler_params=pltpu.CompilerParams(vmem_limit_bytes=12 * MIB),
-        cost_estimate=cost(0, 8 * tokens * rows + 10 * tokens * columns),
+        cost_estimate=cost(0, 4 * tokens * rows + 10 * tokens * columns),
         name="finish",
-    )(place, got2, got3, keys_near, keys_far, last, arrived, whole)
+    )(place, got, keys_near, keys_far, last, arrived, whole)
 
 
 def added(*arrays):
@@ -346,7 +345,6 @@
     whole, out0, keys = projected(
         first, 0, after(activations, keep0, sum3), other, cots, base, base_b
     )
-    got_out0 = sent(out0, SWAP)
 
     sum2_far = added(after(far, two_mid, two_end, one_b, out0), keep2, got2)
     mid_far = sent(sum2_far, MID)
@@ -358,46 +356,38 @@
     whole, out1, keys = projected(
         place, 1, after(activations, sum2_far), other, cots, one, one_b, (whole, None, keys)
     )
-    got_out1 = sent(out1, SWAP)
-
-    sum1 = added(after(mid_far, near, three_end, two_b, out1), keep1, got1)
+
+    sum3_near = added(sum3, near)
+    sum_mid = sent(sum3_near, MID)
+    part1 = added(after(keep1, sum3_near), mid_far)
+    sum1 = added(after(part1, three_end, two_b, out1), got1)
     sum_one = sent(sum1, PAIR)
-    sum3_near = added(sum3, after(near, sum1))
-    sum_mid = sent(sum3_near, MID)
     three = after(mid, sum1) + three_end
     three_b = sent(three, FLIP_B)
-    got0 = sent(after(send0, three_b), FLIP_B)
     whole, out2, keys = projected(
+        place, 2, after(activations, sum1), other, cots, two, two_b, (whole, None, keys)
+    )
+    got0 = sent(after(send0, three_b, out2), FLIP_B)
+    part0 = [keep0[a].astype(F32) + sum_mid[a].astype(F32) for a in (0, 1)]
+    whole, out3, keys, keys_far = projected(
+        place, 3, after(activations, out2, *part0), other, cots, three, three_b, (whole, None, keys)
+    )
+    sum_one = after(sum_one, out3)
+    last = [part0[a] + got0[a].astype(F32) + sum_one[a].astype(F32) for a in (0, 1)]
+    over = last[1].astype(BF16)
+    whole = laid(
         place,
-        2,
-        after(activations, sum3_near),
-        other,
-        cots,
-        two,
-        two_b,
-        (whole, None, keys),
-        got_out0,
-    )
-    whole, out3, keys, keys_far = projected(
-        place, 3, after(activations, out2), other, cots, three, three_b, (whole, None, keys), got_out1
-    )
-    sum_mid, sum_one = after(sum_mid, out3), after(sum_one, out3)
-    last = [
-        keep0[a].astype(F32)
-        + got0[a].astype(F32)
-        + sum_mid[a].astype(F32)
-        + sum_one[a].astype(F32)
-        for a in (0, 1)
-    ]
+        whole,
+        (sent(out0, SWAP), sent(out1, SWAP), sent(out2, SWAP)),
+    )
     grad_input, key_values, grad_weight = finished(
         place,
         whole,
-        sent(out2, SWAP),
         sent(out3, SWAP),
         keys,
         sent(keys_far, SWAP),
         last[0],
-        sent(last[1].astype(BF16), FLIP_A),
+        sent(over, FLIP_A),
         1.0 / math.sqrt(32 * tokens),
     )
     return (key_values, grad_input, grad_weight)

time: 159 us -> 157 us (0.987)
  starting transfers between devices: 45 us -> 39 us
  waiting for transfers between devices: 53.8 us -> 58.6 us
    ppermute x27, starting transfers between devices: 45 us -> 39 us  [sent(): return lax.ppermute(array, AXES, pairs)]
    ppermute x27, waiting for transfers between devices: 53.8 us -> 58.6 us  [sent(): return lax.ppermute(array, AXES, pairs)]
    convert_element_type x4 -> x5, other arithmetic: 3.48 us -> 6.81 us  [added(): return total.astype(BF16)]
    pallas_call x0 -> x1, Pallas kernels: none -> 2.45 us  [laid(): pl.pallas_call(lay_kernel, grid_spec=pltpu.PrefetchScalarGridSpec(num_sca...]
    add x1 -> x0, other arithmetic: 2.38 us -> none  [by_hops(): keep0[a].astype(F32) + got0[a].astype(F32) + sum_mid[a].astype(F32)]
    pallas_call x4, Pallas kernels: 28.4 us -> 26.7 us  [projected(): pl.pallas_call(lambda *refs: project_kernel(*refs, first=first, last=last...]
  transfers between devices with their start and end apart: 27 -> 27, of which waited for: 11 -> 12; matrix products, arithmetic and copies ran while one was open for 4% -> 4% of each run, Pallas kernels for 27% -> 28%
where the time goes in v11:
time: 157 us
  waiting for transfers between devices  58.6 us (37%)
  Pallas kernels  45.9 us (29%)
  starting transfers between devices  39 us (25%)
  other arithmetic  9.46 us (6%)
  local copies, waits for them, and re-layouts  2.8 us (2%)
    ppermute x27, waiting for transfers between devices, sent(): return lax.ppermute(array, AXES, pairs)  58.6 us
    ppermute x27, starting transfers between devices, sent(): return lax.ppermute(array, AXES, pairs)  39 us
    pallas_call x4, Pallas kernels, projected(): pl.pallas_call(lambda *refs: project_kernel(*refs, first=first, last=last...  26.7 us
    pallas_call x1, Pallas kernels, terms(): pl.pallas_call(term_kernel, grid_spec=pltpu.PrefetchScalarGridSpec(num_sc...  8.66 us
    convert_element_type x5, other arithmetic, added(): return total.astype(BF16)  6.81 us
    pallas_call x1, Pallas kernels, first_terms(): pl.pallas_call(first_term_kernel, grid_spec=pltpu.PrefetchScalarGridSpec(...  4.49 us
  transfers between devices with their start and end apart: 27, of which 12 were waited for; matrix products, arithmetic and copies ran while one was open for 4% of the time, Pallas kernels for 28%

profile of v11, /device:TPU:0, one launch (start us, length us, event | category | flops | bytes accessed | tf_op | source)
XLA Modules:
  0.0 156.5 jit_solution(891878040727019838)
XLA Ops:
  0.6 0.5 collective-permute-start
  1.2 2.9 %collective-permute-start.2 = (bf16[1024,256]{1,0:T(8,128)(2,1)}, bf16[1024,256]{1,0:T(8,128)(2,1)S(1)}, u32[]{:S(2)}, u32[]{:S(2)}) collective-permute-start(bf16[1024,256]{1,0:T(8,128)(2,1)} %param.5), channel_id=1, source_target_pairs={{0,8},{1,17},{2,10},{3,19},{4,12},{5,21},{6,14},{7,23},{8,0},{9,25... | collective-permute-start | bytes 1572872 | tf_op jit(solution)/shard_map/ppermute | solution.py:47
  4.2 7.4 %collective-permute-done.2 = bf16[1024,256]{1,0:T(8,128)(2,1)S(1)} collective-permute-done((bf16[1024,256]{1,0:T(8,128)(2,1)}, bf16[1024,256]{1,0:T(8,128)(2,1)S(1)}, u32[]{:S(2)}, u32[]{:S(2)}) %collective-permute-start.2) | collective-permute-done | bytes 524320 | tf_op jit(solution)/shard_map/ppermute | solution.py:47
  11.5 1.1 pad_maximum_fusion.refs_4_
  12.7 2.2 %collective-permute-start.3 = (bf16[2,1024,256]{2,1,0:T(8,128)(2,1)S(1)}, bf16[2,1024,256]{2,1,0:T(8,128)(2,1)S(1)}, u32[]{:S(2)}, u32[]{:S(2)}) collective-permute-start(bf16[2,1024,256]{2,1,0:T(8,128)(2,1)S(1)} %pad_maximum_fusion.refs_4_), channel_id=1, source_target_pairs={{0,2},{1,3},{2,0},{3,1},{4,6},{5,7},{6,4},{7,5},{8,10},{9,11},{10,... | collective-permute-start | bytes 3145736 | tf_op jit(solution)/shard_map/ppermute | solution.py:47
  14.9 0.7 collective-permute-start.4
  15.6 1.6 %collective-permute-start.5 = (bf16[2,1024,256]{2,1,0:T(8,128)(2,1)S(1)}, bf16[2,1024,256]{2,1,0:T(8,128)(2,1)S(1)}, u32[]{:S(2)}, u32[]{:S(2)}) collective-permute-start(bf16[2,1024,256]{2,1,0:T(8,128)(2,1)S(1)} %pad_maximum_fusion.refs_4_), channel_id=1, source_target_pairs={{0,16},{1,9},{2,18},{3,11},{4,20},{5,13},{6,22},{7,15},{8,24},{9,1... | collective-permute-start | bytes 3145736 | tf_op jit(solution)/shard_map/ppermute | solution.py:47
  17.2 2.8 %copy-done = bf16[384,8192]{1,0:T(8,128)(2,1)S(1)} copy-done((bf16[384,8192]{1,0:T(8,128)(2,1)S(1)}, bf16[384,8192]{1,0:T(8,128)(2,1)}, u32[]{:S(2)}) %copy-start) | copy-done | bytes 6291480
  20.0 4.5 %terms.2 = (bf16[2,256,1024]{2,1,0:T(8,128)(2,1)S(1)}, bf16[2,256,1024]{2,1,0:T(8,128)(2,1)S(1)}, bf16[768,1024]{1,0:T(8,128)(2,1)S(1)}, bf16[1024,768]{1,0:T(8,128)(2,1)S(1)}) custom-call(s32[3]{0:T(128)S(1)} %pad_add_fusion.place.refs_0_, bf16[384,8192]{1,0:T(8,128)(2,1)S(1)} %copy-done, bf16[384,8192]{1,0:T(8,128)(2,1)} %collective-permute-done.other.refs_2_, ...), custom_call_target="tpu_custom_call" | custom-call | flops 1610612 | bytes 5767 | tf_op jit(solution)/shard_map/terms/pallas_call | solution.py:107
  24.5 0.6 collective-permute-start.6
  25.1 8.7 %terms.3 = (bf16[2,256,1024]{2,1,0:T(8,128)(2,1)S(1)}, bf16[2,256,1024]{2,1,0:T(8,128)(2,1)S(1)}, bf16[2,256,1024]{2,1,0:T(8,128)(2,1)S(1)}, bf16[2,256,1024]{2,...) custom-call(s32[3]{0:T(128)S(1)} %pad_add_fusion.place.refs_0_, ...), custom_call_target="tpu_custom_call" | custom-call | flops 4831838 | bytes 17301 | tf_op jit(solution)/shard_map/terms/pallas_call | solution.py:149
  33.8 3.6 %collective-permute-done.3.refs_1_.refs_4_ = bf16[2,1024,256]{2,1,0:T(8,128)(2,1)S(1)} collective-permute-done((bf16[2,1024,256]{2,1,0:T(8,128)(2,1)S(1)}, bf16[2,1024,256]{2,1,0:T(8,128)(2,1)S(1)}, u32[]{:S(2)}, u32[]{:S(2)}) %collective-permute-start.3) | collective-permute-done | bytes 1048608 | tf_op jit(solution)/shard_map/ppermute | solution.py:47
  37.4 1.1 gate.1.refs_0_
  38.5 3.2 %collective-permute-done.6 = bf16[2,256,1024]{2,1,0:T(8,128)(2,1)S(1)} collective-permute-done((bf16[2,256,1024]{2,1,0:T(8,128)(2,1)S(1)}, bf16[2,256,1024]{2,1,0:T(8,128)(2,1)S(1)}, u32[]{:S(2)}, u32[]{:S(2)}) %collective-permute-start.6) | collective-permute-done | bytes 1048608 | tf_op jit(solution)/shard_map/ppermute | solution.py:47
  42.2 6.3 %collective-permute-start.8 = (bf16[2,256,1024]{2,1,0:T(8,128)(2,1)S(1)}, bf16[2,256,1024]{2,1,0:T(8,128)(2,1)S(1)}, u32[]{:S(2)}, u32[]{:S(2)}) collective-permute-start(bf16[2,256,1024]{2,1,0:T(8,128)(2,1)S(1)} %add_convert_fusion.3), channel_id=1, source_target_pairs={{0,2},{1,3},{6,4},{7,5},{8,10},{9,11},{14,12},{15,13},{16,18},{17,... | collective-permute-start | bytes 3145736 | tf_op jit(solution)/shard_map/ppermute | solution.py:47
  48.5 0.7 collective-permute-start.9
  49.2 1.3 collective-permute-start.10
  50.5 1.6 %collective-permute-start.11 = (bf16[2,1024,256]{2,1,0:T(8,128)(2,1)S(1)}, bf16[2,1024,256]{2,1,0:T(8,128)(2,1)S(1)}, u32[]{:S(2)}, u32[]{:S(2)}) collective-permute-start(bf16[2,1024,256]{2,1,0:T(8,128)(2,1)S(1)} %collective-permute-done.3.refs_1_.refs_4_), channel_id=1, source_target_pairs={{0,16},{1,9},{2,18},{3,11},{4,20},{5,13},{6,22},{7,15},{8,24},{9,1... | collective-permute-start | bytes 3145736 | tf_op jit(solution)/shard_map/ppermute | solution.py:47
  52.1 0.5 collective-permute-start.7
  52.6 6.5 %project.4 = (bf16[384,8192]{1,0:T(8,128)(2,1)}, bf16[384,1024]{1,0:T(8,128)(2,1)S(1)}, f32[768,1024]{1,0:T(8,128)S(1)}) custom-call(s32[3]{0:T(128)S(1)} %gate.1.refs_0_, bf16[384,8192]{1,0:T(8,128)(2,1)S(1)} %copy-done.1, bf16[384,8192]{1,0:T(8,128)(2,1)} %collective-permute-done.other.refs_2_, bf16[768,1024]{1,0:T(8,128)(2,1)S(1)} %get-tuple-element.62.refs_3_, ...), custom_call_target="tpu_custom_call" | custom-call | flops 3221225 | bytes 8388 | tf_op jit(solution)/shard_map/project/pallas_call | solution.py:216
  59.1 9.7 %collective-permute-done.8 = bf16[2,256,1024]{2,1,0:T(8,128)(2,1)S(1)} collective-permute-done((bf16[2,256,1024]{2,1,0:T(8,128)(2,1)S(1)}, bf16[2,256,1024]{2,1,0:T(8,128)(2,1)S(1)}, u32[]{:S(2)}, u32[]{:S(2)}) %collective-permute-start.8) | collective-permute-done | bytes 1048608 | tf_op jit(solution)/shard_map/ppermute | solution.py:47
  68.8 4.9 %collective-permute-done.10 = bf16[2,1024,256]{2,1,0:T(8,128)(2,1)S(1)} collective-permute-done((bf16[2,1024,256]{2,1,0:T(8,128)(2,1)S(1)}, bf16[2,1024,256]{2,1,0:T(8,128)(2,1)S(1)}, u32[]{:S(2)}, u32[]{:S(2)}) %collective-permute-start.10) | collective-permute-done | bytes 1048608 | tf_op jit(solution)/shard_map/ppermute | solution.py:47
  73.7 2.9 %collective-permute-done.7 = bf16[2,256,1024]{2,1,0:T(8,128)(2,1)S(1)} collective-permute-done((bf16[2,256,1024]{2,1,0:T(8,128)(2,1)S(1)}, bf16[2,256,1024]{2,1,0:T(8,128)(2,1)S(1)}, u32[]{:S(2)}, u32[]{:S(2)}) %collective-permute-start.7) | collective-permute-done | bytes 1048608 | tf_op jit(solution)/shard_map/ppermute | solution.py:47
  76.6 1.7 %fusion = (bf16[2,256,1024]{2,1,0:T(8,128)(2,1)}, bf16[2,256,1024]{2,1,0:T(8,128)(2,1)S(1)}) fusion(bf16[2,256,1024]{2,1,0:T(8,128)(2,1)S(1)} %collective-permute-done.7, bf16[2,256,1024]{2,1,0:T(8,128)(2,1)S(1)} %get-tuple-element.55, bf16[2,256,1024]{2,1,0:T(8,128)(2,1)S(1)} %collective-permute-done.8), kind=kLoop, calls=%fused_computation.3 | loop fusion | flops 4194304 | bytes 5242880 | tf_op jit(solution)/shard_map/convert_element_type | solution.py:319
  78.3 5.7 %collective-permute-start.12 = (bf16[2,256,1024]{2,1,0:T(8,128)(2,1)}, bf16[2,256,1024]{2,1,0:T(8,128)(2,1)}, u32[]{:S(2)}, u32[]{:S(2)}) collective-permute-start(bf16[2,256,1024]{2,1,0:T(8,128)(2,1)} %get-tuple-element.65), channel_id=1, source_target_pairs={{0,2},{1,3},{6,4},{7,5},{8,10},{9,11},{14,12},{15,13},{16,18},{17,... | collective-permute-start | bytes 3145736 | tf_op jit(solution)/shard_map/ppermute | solution.py:47
  84.0 1.6 %collective-permute-start.13 = (bf16[2,256,1024]{2,1,0:T(8,128)(2,1)S(1)}, bf16[2,256,1024]{2,1,0:T(8,128)(2,1)}, u32[]{:S(2)}, u32[]{:S(2)}) collective-permute-start(bf16[2,256,1024]{2,1,0:T(8,128)(2,1)S(1)} %get-tuple-element.96), channel_id=1, source_target_pairs={{2,4},{3,5},{4,2},{5,3},{10,12},{11,13},{12,10},{13,11},{18,20},{1... | collective-permute-start | bytes 3145736 | tf_op jit(solution)/shard_map/ppermute | solution.py:47
  85.7 1.5 collective-permute-start.14
  87.4 1.6 %collective-permute-start.15 = (bf16[2,1024,256]{2,1,0:T(8,128)(2,1)S(1)}, bf16[2,1024,256]{2,1,0:T(8,128)(2,1)S(1)}, u32[]{:S(2)}, u32[]{:S(2)}) collective-permute-start(bf16[2,1024,256]{2,1,0:T(8,128)(2,1)S(1)} %add.57.refs_4_), channel_id=1, source_target_pairs={{0,16},{1,9},{2,18},{3,11},{4,20},{5,13},{6,22},{7,15},{8,24},{9,1... | collective-permute-start | bytes 3145736 | tf_op jit(solution)/shard_map/ppermute | solution.py:47
  89.5 6.7 %project.5 = (bf16[384,8192]{1,0:T(8,128)(2,1)}, bf16[384,1024]{1,0:T(8,128)(2,1)S(1)}, f32[768,1024]{1,0:T(8,128)S(1)}) custom-call(s32[3]{0:T(128)S(1)} %pad_add_fusion.place.refs_0_, bf16[384,8192]{1,0:T(8,128)(2,1)S(1)} %copy-done.1, bf16[384,8192]{1,0:T(8,128)(2,1)} %collective-permute-done.other.refs_2_, ...), custom_call_target="tpu_custom_call", output_to_operand_aliasing={{0}: (7, {})} | custom-call | flops 3221225 | bytes 8388 | tf_op jit(solution)/shard_map/project/pallas_call | solution.py:216
  96.2 6.0 %collective-permute-done.12 = bf16[2,256,1024]{2,1,0:T(8,128)(2,1)} collective-permute-done((bf16[2,256,1024]{2,1,0:T(8,128)(2,1)}, bf16[2,256,1024]{2,1,0:T(8,128)(2,1)}, u32[]{:S(2)}, u32[]{:S(2)}) %collective-permute-start.12) | collective-permute-done | bytes 1048608 | tf_op jit(solution)/shard_map/ppermute | solution.py:47
  102.2 2.6 %add_convert_fusion.2 = bf16[2,256,1024]{2,1,0:T(8,128)(2,1)} fusion(bf16[2,256,1024]{2,1,0:T(8,128)(2,1)} %collective-permute-done.12, bf16[2,256,1024]{2,1,0:T(8,128)(2,1)S(1)} %add_convert_fusion.3), kind=kLoop, calls=%fused_computation.7 | loop fusion | flops 2097152 | bytes 3145728 | tf_op jit(solution)/shard_map/convert_element_type | solution.py:319
  104.9 1.6 %add_convert_fusion.1 = bf16[2,256,1024]{2,1,0:T(8,128)(2,1)S(1)} fusion(bf16[2,256,1024]{2,1,0:T(8,128)(2,1)} %collective-permute-done.13, bf16[2,256,1024]{2,1,0:T(8,128)(2,1)S(1)} %get-tuple-element.66), kind=kLoop, calls=%fused_computation.6 | loop fusion | flops 2097152 | bytes 3145728 | tf_op jit(solution)/shard_map/convert_element_type | solution.py:319
  106.5 2.2 %collective-permute-done.14 = bf16[2,1024,256]{2,1,0:T(8,128)(2,1)S(1)} collective-permute-done((bf16[2,1024,256]{2,1,0:T(8,128)(2,1)S(1)}, bf16[2,1024,256]{2,1,0:T(8,128)(2,1)S(1)}, u32[]{:S(2)}, u32[]{:S(2)}) %collective-permute-start.14) | collective-permute-done | bytes 1048608 | tf_op jit(solution)/shard_map/ppermute | solution.py:47
  108.7 4.8 %collective-permute-done.16 = bf16[2,256,1024]{2,1,0:T(8,128)(2,1)S(1)} collective-permute-done((bf16[2,256,1024]{2,1,0:T(8,128)(2,1)S(1)}, bf16[2,256,1024]{2,1,0:T(8,128)(2,1)S(1)}, u32[]{:S(2)}, u32[]{:S(2)}) %collective-permute-start.16) | collective-permute-done | bytes 1048608 | tf_op jit(solution)/shard_map/ppermute | solution.py:47
  114.2 1.6 %collective-permute-start.18 = (bf16[2,1024,256]{2,1,0:T(8,128)(2,1)S(1)}, bf16[2,1024,256]{2,1,0:T(8,128)(2,1)S(1)}, u32[]{:S(2)}, u32[]{:S(2)}) collective-permute-start(bf16[2,1024,256]{2,1,0:T(8,128)(2,1)S(1)} %add.63.refs_4_), channel_id=1, source_target_pairs={{0,16},{1,9},{2,18},{3,11},{4,20},{5,13},{6,22},{7,15},{8,24},{9,1... | collective-permute-start | bytes 3145736 | tf_op jit(solution)/shard_map/ppermute | solution.py:47
  115.8 2.7 %collective-permute-start.22 = (bf16[2,256,1024]{2,1,0:T(8,128)(2,1)S(1)}, bf16[2,256,1024]{2,1,0:T(8,128)(2,1)S(1)}, u32[]{:S(2)}, u32[]{:S(2)}) collective-permute-start(bf16[2,256,1024]{2,1,0:T(8,128)(2,1)S(1)} %add_convert_fusion), channel_id=1, source_target_pairs={{0,2},{1,3},{2,0},{3,1},{4,6},{5,7},{6,4},{7,5},{8,10},{9,11},{10,... | collective-permute-start | bytes 3145736 | tf_op jit(solution)/shard_map/ppermute | solution.py:47
  118.5 0.7 collective-permute-start.17
  119.2 6.7 %project.6 = (bf16[384,8192]{1,0:T(8,128)(2,1)}, bf16[384,1024]{1,0:T(8,128)(2,1)S(1)}, f32[768,1024]{1,0:T(8,128)S(1)}) custom-call(s32[3]{0:T(128)S(1)} %pad_add_fusion.place.refs_0_, bf16[384,8192]{1,0:T(8,128)(2,1)S(1)} %copy-done.1, bf16[384,8192]{1,0:T(8,128)(2,1)} %collective-permute-done.other.refs_2_, ...), custom_call_target="tpu_custom_call", output_to_operand_aliasing={{0}: (7, {})} | custom-call | flops 3221225 | bytes 8388 | tf_op jit(solution)/shard_map/project/pallas_call | solution.py:216
  125.9 3.2 %collective-permute-done.18.refs_5_ = bf16[2,1024,256]{2,1,0:T(8,128)(2,1)S(1)} collective-permute-done((bf16[2,1024,256]{2,1,0:T(8,128)(2,1)S(1)}, bf16[2,1024,256]{2,1,0:T(8,128)(2,1)S(1)}, u32[]{:S(2)}, u32[]{:S(2)}) %collective-permute-start.18) | collective-permute-done | bytes 1048608 | tf_op jit(solution)/shard_map/ppermute | solution.py:47
  129.1 1.5 collective-permute-start.21
  130.6 6.8 %project.7 = (bf16[384,8192]{1,0:T(8,128)(2,1)}, bf16[384,1024]{1,0:T(8,128)(2,1)S(1)}, f32[384,1024]{1,0:T(8,128)S(1)}, f32[384,1024]{1,0:T(8,128)S(1)}) custom-call(s32[3]{0:T(128)S(1)} %pad_add_fusion.place.refs_0_, bf16[384,8192]{1,0:T(8,128)(2,1)S(1)} %copy-done.1, ...), custom_call_target="tpu_custom_call", output_to_operand_aliasing={{0}: (7, {})} | custom-call | flops 3221225 | bytes 8388 | tf_op jit(solution)/shard_map/project/pallas_call | solution.py:216
  137.4 0.5 collective-permute-start.24
  138.5 5.4 %collective-permute-done.21 = bf16[2,256,1024]{2,1,0:T(8,128)(2,1)S(1)} collective-permute-done((bf16[2,256,1024]{2,1,0:T(8,128)(2,1)S(1)}, bf16[2,256,1024]{2,1,0:T(8,128)(2,1)S(1)}, u32[]{:S(2)}, u32[]{:S(2)}) %collective-permute-start.21) | collective-permute-done | bytes 1048608 | tf_op jit(solution)/shard_map/ppermute | solution.py:47
  143.9 0.9 fusion.2
  144.8 1.6 collective-permute-start.23
  146.3 2.4 %lay.1.refs_6_ = bf16[384,8192]{1,0:T(8,128)(2,1)} custom-call(s32[3]{0:T(128)S(1)} %pad_add_fusion.place.refs_0_, bf16[384,1024]{1,0:T(8,128)(2,1)S(1)} %collective-permute-done.24.refs_0_, bf16[384,1024]{1,0:T(8,128)(2,1)S(1)} %collective-permute-done.25.refs_1_, ...), custom_call_target="tpu_custom_call", output_to_operand_aliasing={{}: (4, {})} | custom-call | bytes 4718 | tf_op jit(solution)/shard_map/lay/pallas_call | solution.py:255
  148.8 5.2 %collective-permute-done.23.refs_5_ = bf16[256,1024]{1,0:T(8,128)(2,1)S(1)} collective-permute-done((bf16[256,1024]{1,0:T(8,128)(2,1)S(1)}, bf16[256,1024]{1,0:T(8,128)(2,1)S(1)}, u32[]{:S(2)}, u32[]{:S(2)}) %collective-permute-start.23) | collective-permute-done | bytes 524320 | tf_op jit(solution)/shard_map/ppermute | solution.py:47
  154.0 2.5 %finish.1 = (bf16[384,8192]{1,0:T(8,128)(2,1)}, bf16[384,1024]{1,0:T(8,128)(2,1)}, bf16[1024,256]{1,0:T(8,128)(2,1)}) custom-call(s32[3]{0:T(128)S(1)} %pad_add_fusion.place.refs_0_, bf16[384,1024]{1,0:T(8,128)(2,1)S(1)} %collective-permute-done.19.refs_1_, f32[384,1024]{1,0:T(8,128)S(1)} %get-tuple-element.84.refs_2_, ...), custom_call_target="tpu_custom_call", output_to_operand_aliasing={{0}: (6, {})} | custom-call | bytes 5505 | tf_op jit(solution)/shard_map/finish/pallas_call | solution.py:284
  (35 shorter events, 2.6 us)
Async XLA Ops:
  0.6 16.6 %copy-start.2 = (bf16[384,1024]{1,0:T(8,128)(2,1)S(1)}, bf16[384,1024]{1,0:T(8,128)(2,1)}, u32[]{:S(2)}) copy-start(bf16[384,1024]{1,0:T(8,128)(2,1)} %cot_mine.1) | copy-start | bytes 2359300
  0.6 16.6 %collective-permute-start = (bf16[384,8192]{1,0:T(8,128)(2,1)}, bf16[384,8192]{1,0:T(8,128)(2,1)}, u32[]{:S(2)}, u32[]{:S(2)}) collective-permute-start(bf16[384,8192]{1,0:T(8,128)(2,1)} %refs_1_.3), channel_id=1, source_target_pairs={{0,1},{1,0},{2,3},{3,2},{4,5},{5,4},{6,7},{7,6},{8,9},{9,8},{10,11... | collective-permute-start | bytes 18874376 | tf_op jit(solution)/shard_map/ppermute | solution.py:47
  1.2 16.1 %collective-permute-start.1 = (bf16[384,1024]{1,0:T(8,128)(2,1)}, bf16[384,1024]{1,0:T(8,128)(2,1)S(1)}, u32[]{:S(2)}, u32[]{:S(2)}) collective-permute-start(bf16[384,1024]{1,0:T(8,128)(2,1)} %cot_mine.1), channel_id=1, source_target_pairs={{0,1},{1,0},{2,3},{3,2},{4,5},{5,4},{6,7},{7,6},{8,9},{9,8},{10,11... | collective-permute-start | bytes 2359304 | tf_op jit(solution)/shard_map/ppermute | solution.py:47
  1.2 10.3 %collective-permute-start.2 = (bf16[1024,256]{1,0:T(8,128)(2,1)}, bf16[1024,256]{1,0:T(8,128)(2,1)S(1)}, u32[]{:S(2)}, u32[]{:S(2)}) collective-permute-start(bf16[1024,256]{1,0:T(8,128)(2,1)} %param.5), channel_id=1, source_target_pairs={{0,8},{1,17},{2,10},{3,19},{4,12},{5,21},{6,14},{7,23},{8,0},{9,25... | collective-permute-start | bytes 1572872 | tf_op jit(solution)/shard_map/ppermute | solution.py:47
  12.7 24.7 %collective-permute-start.3 = (bf16[2,1024,256]{2,1,0:T(8,128)(2,1)S(1)}, bf16[2,1024,256]{2,1,0:T(8,128)(2,1)S(1)}, u32[]{:S(2)}, u32[]{:S(2)}) collective-permute-start(bf16[2,1024,256]{2,1,0:T(8,128)(2,1)S(1)} %pad_maximum_fusion.refs_4_), channel_id=1, source_target_pairs={{0,2},{1,3},{2,0},{3,1},{4,6},{5,7},{6,4},{7,5},{8,10},{9,11},{10,... | collective-permute-start | bytes 3145736 | tf_op jit(solution)/shard_map/ppermute | solution.py:47
  14.9 22.5 %collective-permute-start.4 = (bf16[2,1024,256]{2,1,0:T(8,128)(2,1)S(1)}, bf16[2,1024,256]{2,1,0:T(8,128)(2,1)S(1)}, u32[]{:S(2)}, u32[]{:S(2)}) collective-permute-start(bf16[2,1024,256]{2,1,0:T(8,128)(2,1)S(1)} %pad_maximum_fusion.refs_4_), channel_id=1, source_target_pairs={{2,4},{3,5},{4,2},{5,3},{10,12},{11,13},{12,10},{13,11},{18,20},{1... | collective-permute-start | bytes 3145736 | tf_op jit(solution)/shard_map/ppermute | solution.py:47
  15.6 21.8 %collective-permute-start.5 = (bf16[2,1024,256]{2,1,0:T(8,128)(2,1)S(1)}, bf16[2,1024,256]{2,1,0:T(8,128)(2,1)S(1)}, u32[]{:S(2)}, u32[]{:S(2)}) collective-permute-start(bf16[2,1024,256]{2,1,0:T(8,128)(2,1)S(1)} %pad_maximum_fusion.refs_4_), channel_id=1, source_target_pairs={{0,16},{1,9},{2,18},{3,11},{4,20},{5,13},{6,22},{7,15},{8,24},{9,1... | collective-permute-start | bytes 3145736 | tf_op jit(solution)/shard_map/ppermute | solution.py:47
  17.2 2.8 %copy-start = (bf16[384,8192]{1,0:T(8,128)(2,1)S(1)}, bf16[384,8192]{1,0:T(8,128)(2,1)}, u32[]{:S(2)}) copy-start(bf16[384,8192]{1,0:T(8,128)(2,1)} %refs_1_.3) | copy-start | bytes 18874372
  20.0 5.1 %copy-start.1 = (bf16[384,8192]{1,0:T(8,128)(2,1)S(1)}, bf16[384,8192]{1,0:T(8,128)(2,1)}, u32[]{:S(2)}) copy-start(bf16[384,8192]{1,0:T(8,128)(2,1)} %refs_1_.3) | copy-start | bytes 18874372
  24.5 17.2 %collective-permute-start.6 = (bf16[2,256,1024]{2,1,0:T(8,128)(2,1)S(1)}, bf16[2,256,1024]{2,1,0:T(8,128)(2,1)S(1)}, u32[]{:S(2)}, u32[]{:S(2)}) collective-permute-start(bf16[2,256,1024]{2,1,0:T(8,128)(2,1)S(1)} %get-tuple-element.54), channel_id=1, source_target_pairs={{0,16},{1,9},{2,18},{3,11},{4,20},{5,13},{6,22},{7,15},{8,24},{9,1... | collective-permute-start | bytes 3145736 | tf_op jit(solution)/shard_map/ppermute | solution.py:47
  42.2 26.6 %collective-permute-start.8 = (bf16[2,256,1024]{2,1,0:T(8,128)(2,1)S(1)}, bf16[2,256,1024]{2,1,0:T(8,128)(2,1)S(1)}, u32[]{:S(2)}, u32[]{:S(2)}) collective-permute-start(bf16[2,256,1024]{2,1,0:T(8,128)(2,1)S(1)} %add_convert_fusion.3), channel_id=1, source_target_pairs={{0,2},{1,3},{6,4},{7,5},{8,10},{9,11},{14,12},{15,13},{16,18},{17,... | collective-permute-start | bytes 3145736 | tf_op jit(solution)/shard_map/ppermute | solution.py:47
  48.5 20.3 %collective-permute-start.9 = (bf16[2,1024,256]{2,1,0:T(8,128)(2,1)S(1)}, bf16[2,1024,256]{2,1,0:T(8,128)(2,1)S(1)}, u32[]{:S(2)}, u32[]{:S(2)}) collective-permute-start(bf16[2,1024,256]{2,1,0:T(8,128)(2,1)S(1)} %collective-permute-done.3.refs_1_.refs_4_), channel_id=1, source_target_pairs={{2,4},{3,5},{4,2},{5,3},{10,12},{11,13},{12,10},{13,11},{18,20},{1... | collective-permute-start | bytes 3145736 | tf_op jit(solution)/shard_map/ppermute | solution.py:47
  49.2 24.5 %collective-permute-start.10 = (bf16[2,1024,256]{2,1,0:T(8,128)(2,1)S(1)}, bf16[2,1024,256]{2,1,0:T(8,128)(2,1)S(1)}, u32[]{:S(2)}, u32[]{:S(2)}) collective-permute-start(bf16[2,1024,256]{2,1,0:T(8,128)(2,1)S(1)} %collective-permute-done.4.refs_2_), channel_id=1, source_target_pairs={{2,0},{3,1},{4,6},{5,7},{10,8},{11,9},{12,14},{13,15},{18,16},{19,... | collective-permute-start | bytes 3145736 | tf_op jit(solution)/shard_map/ppermute | solution.py:47
  50.5 23.2 %collective-permute-start.11 = (bf16[2,1024,256]{2,1,0:T(8,128)(2,1)S(1)}, bf16[2,1024,256]{2,1,0:T(8,128)(2,1)S(1)}, u32[]{:S(2)}, u32[]{:S(2)}) collective-permute-start(bf16[2,1024,256]{2,1,0:T(8,128)(2,1)S(1)} %collective-permute-done.3.refs_1_.refs_4_), channel_id=1, source_target_pairs={{0,16},{1,9},{2,18},{3,11},{4,20},{5,13},{6,22},{7,15},{8,24},{9,1... | collective-permute-start | bytes 3145736 | tf_op jit(solution)/shard_map/ppermute | solution.py:47
  52.1 24.5 %collective-permute-start.7 = (bf16[2,256,1024]{2,1,0:T(8,128)(2,1)S(1)}, bf16[2,256,1024]{2,1,0:T(8,128)(2,1)S(1)}, u32[]{:S(2)}, u32[]{:S(2)}) collective-permute-start(bf16[2,256,1024]{2,1,0:T(8,128)(2,1)S(1)} %get-tuple-element.57), channel_id=1, source_target_pairs={{0,16},{1,9},{2,18},{3,11},{4,20},{5,13},{6,22},{7,15},{8,24},{9,1... | collective-permute-start | bytes 3145736 | tf_op jit(solution)/shard_map/ppermute | solution.py:47
  78.3 23.9 %collective-permute-start.12 = (bf16[2,256,1024]{2,1,0:T(8,128)(2,1)}, bf16[2,256,1024]{2,1,0:T(8,128)(2,1)}, u32[]{:S(2)}, u32[]{:S(2)}) collective-permute-start(bf16[2,256,1024]{2,1,0:T(8,128)(2,1)} %get-tuple-element.65), channel_id=1, source_target_pairs={{0,2},{1,3},{6,4},{7,5},{8,10},{9,11},{14,12},{15,13},{16,18},{17,... | collective-permute-start | bytes 3145736 | tf_op jit(solution)/shard_map/ppermute | solution.py:47
  84.0 20.8 %collective-permute-start.13 = (bf16[2,256,1024]{2,1,0:T(8,128)(2,1)S(1)}, bf16[2,256,1024]{2,1,0:T(8,128)(2,1)}, u32[]{:S(2)}, u32[]{:S(2)}) collective-permute-start(bf16[2,256,1024]{2,1,0:T(8,128)(2,1)S(1)} %get-tuple-element.96), channel_id=1, source_target_pairs={{2,4},{3,5},{4,2},{5,3},{10,12},{11,13},{12,10},{13,11},{18,20},{1... | collective-permute-start | bytes 3145736 | tf_op jit(solution)/shard_map/ppermute | solution.py:47
  85.7 23.1 %collective-permute-start.14 = (bf16[2,1024,256]{2,1,0:T(8,128)(2,1)S(1)}, bf16[2,1024,256]{2,1,0:T(8,128)(2,1)S(1)}, u32[]{:S(2)}, u32[]{:S(2)}) collective-permute-start(bf16[2,1024,256]{2,1,0:T(8,128)(2,1)S(1)} %collective-permute-done.9), channel_id=1, source_target_pairs={{2,0},{3,1},{4,6},{5,7},{10,8},{11,9},{12,14},{13,15},{18,16},{19,... | collective-permute-start | bytes 3145736 | tf_op jit(solution)/shard_map/ppermute | solution.py:47
  87.4 21.3 %collective-permute-start.15 = (bf16[2,1024,256]{2,1,0:T(8,128)(2,1)S(1)}, bf16[2,1024,256]{2,1,0:T(8,128)(2,1)S(1)}, u32[]{:S(2)}, u32[]{:S(2)}) collective-permute-start(bf16[2,1024,256]{2,1,0:T(8,128)(2,1)S(1)} %add.57.refs_4_), channel_id=1, source_target_pairs={{0,16},{1,9},{2,18},{3,11},{4,20},{5,13},{6,22},{7,15},{8,24},{9,1... | collective-permute-start | bytes 3145736 | tf_op jit(solution)/shard_map/ppermute | solution.py:47
  89.0 24.5 %collective-permute-start.16 = (bf16[2,256,1024]{2,1,0:T(8,128)(2,1)S(1)}, bf16[2,256,1024]{2,1,0:T(8,128)(2,1)S(1)}, u32[]{:S(2)}, u32[]{:S(2)}) collective-permute-start(bf16[2,256,1024]{2,1,0:T(8,128)(2,1)S(1)} %get-tuple-element.74), channel_id=1, source_target_pairs={{0,16},{1,9},{2,18},{3,11},{4,20},{5,13},{6,22},{7,15},{8,24},{9,1... | collective-permute-start | bytes 3145736 | tf_op jit(solution)/shard_map/ppermute | solution.py:47
  96.2 10.3 %copy-start.3 = (bf16[384,1024]{1,0:T(8,128)(2,1)}, bf16[384,1024]{1,0:T(8,128)(2,1)S(1)}, u32[]{:S(2)}) copy-start(bf16[384,1024]{1,0:T(8,128)(2,1)S(1)} %get-tuple-element.71) | copy-start | bytes 2359300
  114.2 14.9 %collective-permute-start.18 = (bf16[2,1024,256]{2,1,0:T(8,128)(2,1)S(1)}, bf16[2,1024,256]{2,1,0:T(8,128)(2,1)S(1)}, u32[]{:S(2)}, u32[]{:S(2)}) collective-permute-start(bf16[2,1024,256]{2,1,0:T(8,128)(2,1)S(1)} %add.63.refs_4_), channel_id=1, source_target_pairs={{0,16},{1,9},{2,18},{3,11},{4,20},{5,13},{6,22},{7,15},{8,24},{9,1... | collective-permute-start | bytes 3145736 | tf_op jit(solution)/shard_map/ppermute | solution.py:47
  115.8 22.2 %collective-permute-start.22 = (bf16[2,256,1024]{2,1,0:T(8,128)(2,1)S(1)}, bf16[2,256,1024]{2,1,0:T(8,128)(2,1)S(1)}, u32[]{:S(2)}, u32[]{:S(2)}) collective-permute-start(bf16[2,256,1024]{2,1,0:T(8,128)(2,1)S(1)} %add_convert_fusion), channel_id=1, source_target_pairs={{0,2},{1,3},{2,0},{3,1},{4,6},{5,7},{6,4},{7,5},{8,10},{9,11},{10,... | collective-permute-start | bytes 3145736 | tf_op jit(solution)/shard_map/ppermute | solution.py:47
  118.5 19.5 %collective-permute-start.17 = (bf16[2,256,1024]{2,1,0:T(8,128)(2,1)}, bf16[2,256,1024]{2,1,0:T(8,128)(2,1)S(1)}, u32[]{:S(2)}, u32[]{:S(2)}) collective-permute-start(bf16[2,256,1024]{2,1,0:T(8,128)(2,1)} %add_convert_fusion.2), channel_id=1, source_target_pairs={{2,4},{3,5},{4,2},{5,3},{10,12},{11,13},{12,10},{13,11},{18,20},{1... | collective-permute-start | bytes 3145736 | tf_op jit(solution)/shard_map/ppermute | solution.py:47
  129.1 14.8 %collective-permute-start.21 = (bf16[2,256,1024]{2,1,0:T(8,128)(2,1)S(1)}, bf16[2,256,1024]{2,1,0:T(8,128)(2,1)S(1)}, u32[]{:S(2)}, u32[]{:S(2)}) collective-permute-start(bf16[2,256,1024]{2,1,0:T(8,128)(2,1)S(1)} %get-tuple-element.87), channel_id=1, source_target_pairs={{0,16},{1,9},{2,18},{3,11},{4,20},{5,13},{6,22},{7,15},{8,24},{9,1... | collective-permute-start | bytes 3145736 | tf_op jit(solution)/shard_map/ppermute | solution.py:47
  130.6 7.4 %copy-start.4 = (bf16[384,1024]{1,0:T(8,128)(2,1)S(1)}, bf16[384,1024]{1,0:T(8,128)(2,1)}, u32[]{:S(2)}) copy-start(bf16[384,1024]{1,0:T(8,128)(2,1)} %copy-done.3) | copy-start | bytes 2359300
  137.4 11.4 %collective-permute-start.20 = (f32[384,1024]{1,0:T(8,128)S(1)}, f32[384,1024]{1,0:T(8,128)S(1)}, u32[]{:S(2)}, u32[]{:S(2)}) collective-permute-start(f32[384,1024]{1,0:T(8,128)S(1)} %get-tuple-element.85), channel_id=1, source_target_pairs={{0,1},{1,0},{2,3},{3,2},{4,5},{5,4},{6,7},{7,6},{8,9},{9,8},{10,11... | collective-permute-start | bytes 4718600 | tf_op jit(solution)/shard_map/ppermute | solution.py:47
  137.4 7.3 %collective-permute-start.24 = (bf16[384,1024]{1,0:T(8,128)(2,1)S(1)}, bf16[384,1024]{1,0:T(8,128)(2,1)S(1)}, u32[]{:S(2)}, u32[]{:S(2)}) collective-permute-start(bf16[384,1024]{1,0:T(8,128)(2,1)S(1)} %get-tuple-element.63), channel_id=1, source_target_pairs={{0,1},{1,0},{2,3},{3,2},{4,5},{5,4},{6,7},{7,6},{8,9},{9,8},{10,11... | collective-permute-start | bytes 2359304 | tf_op jit(solution)/shard_map/ppermute | solution.py:47
  138.0 8.4 %collective-permute-start.25 = (bf16[384,1024]{1,0:T(8,128)(2,1)S(1)}, bf16[384,1024]{1,0:T(8,128)(2,1)S(1)}, u32[]{:S(2)}, u32[]{:S(2)}) collective-permute-start(bf16[384,1024]{1,0:T(8,128)(2,1)S(1)} %copy-done.4), channel_id=1, source_target_pairs={{0,1},{1,0},{2,3},{3,2},{4,5},{5,4},{6,7},{7,6},{8,9},{9,8},{10,11... | collective-permute-start | bytes 2359304 | tf_op jit(solution)/shard_map/ppermute | solution.py:47
  138.0 8.3 %collective-permute-start.26 = (bf16[384,1024]{1,0:T(8,128)(2,1)S(1)}, bf16[384,1024]{1,0:T(8,128)(2,1)S(1)}, u32[]{:S(2)}, u32[]{:S(2)}) collective-permute-start(bf16[384,1024]{1,0:T(8,128)(2,1)S(1)} %get-tuple-element.78), channel_id=1, source_target_pairs={{0,1},{1,0},{2,3},{3,2},{4,5},{5,4},{6,7},{7,6},{8,9},{9,8},{10,11... | collective-permute-start | bytes 2359304 | tf_op jit(solution)/shard_map/ppermute | solution.py:47
  143.9 4.9 %collective-permute-start.19 = (bf16[384,1024]{1,0:T(8,128)(2,1)S(1)}, bf16[384,1024]{1,0:T(8,128)(2,1)S(1)}, u32[]{:S(2)}, u32[]{:S(2)}) collective-permute-start(bf16[384,1024]{1,0:T(8,128)(2,1)S(1)} %get-tuple-element.83), channel_id=1, source_target_pairs={{0,1},{1,0},{2,3},{3,2},{4,5},{5,4},{6,7},{7,6},{8,9},{9,8},{10,11... | collective-permute-start | bytes 2359304 | tf_op jit(solution)/shard_map/ppermute | solution.py:47
  144.8 9.2 %collective-permute-start.23 = (bf16[256,1024]{1,0:T(8,128)(2,1)S(1)}, bf16[256,1024]{1,0:T(8,128)(2,1)S(1)}, u32[]{:S(2)}, u32[]{:S(2)}) collective-permute-start(bf16[256,1024]{1,0:T(8,128)(2,1)S(1)} %get-tuple-element.93), channel_id=1, source_target_pairs={{0,8},{1,17},{2,10},{3,19},{4,12},{5,21},{6,14},{7,23},{8,0},{9,25... | collective-permute-start | bytes 1572872 | tf_op jit(solution)/shard_map/ppermute | solution.py:47

commit v12 on v11

--- a/solution.py
+++ b/solution.py
@@ -340,40 +340,50 @@
     far = sent(sum3, IN)
     two_mid = sent(after(one, first, sum3), MID)
     two_end = sent(after(mid, sum3), OUT)
-    got2 = sent(after(send2, sum3), FLIP_B)
+    got2 = sent(send2, FLIP_B)
+    sum2 = added(keep2, got2)
     one_b = sent(after(one, sum3), FLIP_B)
+    got1 = sent(after(send1, sum2), FLIP_B)
     whole, out0, keys = projected(
-        first, 0, after(activations, keep0, sum3), other, cots, base, base_b
-    )
-
-    sum2_far = added(after(far, two_mid, two_end, one_b, out0), keep2, got2)
+        first, 0, after(activations, keep0, sum3, sum2), other, cots, base, base_b
+    )
+
+    sum2_far = added(after(sum2, out0), far)
     mid_far = sent(sum2_far, MID)
-    near = sent(after(added(keep2, got2), sum2_far), IN)
+    near = sent(after(sum2, sum2_far, two_mid, two_end, one_b), IN)
     three_end = sent(after(two_mid, sum2_far), OUT)
-    got1 = sent(after(send1, sum2_far), FLIP_B)
     two = after(two_mid, sum2_far) + two_end
     two_b = sent(two, FLIP_B)
+    sum1 = added(keep1, got1)
+    got0 = sent(after(send0, sum1), FLIP_B)
     whole, out1, keys = projected(
-        place, 1, after(activations, sum2_far), other, cots, one, one_b, (whole, None, keys)
+        place, 1, after(activations, sum2_far, sum1), other, cots, one, one_b, (whole, None, keys)
     )
 
     sum3_near = added(sum3, near)
     sum_mid = sent(sum3_near, MID)
-    part1 = added(after(keep1, sum3_near), mid_far)
-    sum1 = added(after(part1, three_end, two_b, out1), got1)
-    sum_one = sent(sum1, PAIR)
-    three = after(mid, sum1) + three_end
+    sum1_far = added(after(sum1, sum3_near, out1), mid_far)
+    sum_one = sent(after(sum1_far, three_end, two_b), PAIR)
+    three = after(mid, sum1_far) + three_end
     three_b = sent(three, FLIP_B)
+    sum0 = added(keep0, got0)
     whole, out2, keys = projected(
-        place, 2, after(activations, sum1), other, cots, two, two_b, (whole, None, keys)
-    )
-    got0 = sent(after(send0, three_b, out2), FLIP_B)
-    part0 = [keep0[a].astype(F32) + sum_mid[a].astype(F32) for a in (0, 1)]
+        place,
+        2,
+        after(activations, sum1_far, sum0),
+        other,
+        cots,
+        two,
+        two_b,
+        (whole, None, keys),
+    )
     whole, out3, keys, keys_far = projected(
-        place, 3, after(activations, out2, *part0), other, cots, three, three_b, (whole, None, keys)
+        place, 3, after(activations, out2), other, cots, three, three_b, (whole, None, keys)
     )
     sum_one = after(sum_one, out3)
-    last = [part0[a] + got0[a].astype(F32) + sum_one[a].astype(F32) for a in (0, 1)]
+    last = [
+        sum0[a].astype(F32) + sum_mid[a].astype(F32) + sum_one[a].astype(F32) for a in (0, 1)
+    ]
     over = last[1].astype(BF16)
     whole = laid(
         place,

time: 157 us -> 142 us (0.904)
  waiting for transfers between devices: 58.6 us -> 44.8 us
  starting transfers between devices: 39 us -> 37.1 us
    ppermute x27, waiting for transfers between devices: 58.6 us -> 44.8 us  [sent(): return lax.ppermute(array, AXES, pairs)]
    ppermute x27, starting transfers between devices: 39 us -> 37.1 us  [sent(): return lax.ppermute(array, AXES, pairs)]
    convert_element_type x5 -> x7, other arithmetic: 6.81 us -> 6.25 us  [added(): return total.astype(BF16)]
  transfers between devices with their start and end apart: 27 -> 27, of which waited for: 12 -> 14; matrix products, arithmetic and copies ran while one was open for 4% -> 7% of each run, Pallas kernels for 28% -> 31%
where the time goes in v12:
time: 142 us; the launch traced here: 141 us
  Pallas kernels  45.9 us (32%)
  waiting for transfers between devices  44.8 us (32%)
  starting transfers between devices  37.1 us (26%)
  other arithmetic  9.87 us (7%)
  local copies, waits for them, and re-layouts  2.79 us (2%)
    ppermute x27, waiting for transfers between devices, sent(): return lax.ppermute(array, AXES, pairs)  44.8 us
    ppermute x27, starting transfers between devices, sent(): return lax.ppermute(array, AXES, pairs)  37.1 us
    pallas_call x4, Pallas kernels, projected(): pl.pallas_call(lambda *refs: project_kernel(*refs, first=first, last=last...  26.7 us
    pallas_call x1, Pallas kernels, terms(): pl.pallas_call(term_kernel, grid_spec=pltpu.PrefetchScalarGridSpec(num_sc...  8.66 us
    convert_element_type x7, other arithmetic, added(): return total.astype(BF16)  6.25 us
    pallas_call x1, Pallas kernels, first_terms(): pl.pallas_call(first_term_kernel, grid_spec=pltpu.PrefetchScalarGridSpec(...  4.49 us
  transfers between devices with their start and end apart: 27, of which 14 were waited for; matrix products, arithmetic and copies ran while one was open for 7% of the time, Pallas kernels for 31%

profile of v12, /device:TPU:0, one launch (start us, length us, event | category | flops | bytes accessed | tf_op | source)
XLA Modules:
  0.0 141.3 jit_solution(4873886535043153586)
XLA Ops:
  1.2 2.9 %collective-permute-start.4 = (bf16[1024,256]{1,0:T(8,128)(2,1)}, bf16[1024,256]{1,0:T(8,128)(2,1)S(1)}, u32[]{:S(2)}, u32[]{:S(2)}) collective-permute-start(bf16[1024,256]{1,0:T(8,128)(2,1)} %param.5), channel_id=1, source_target_pairs={{0,8},{1,17},{2,10},{3,19},{4,12},{5,21},{6,14},{7,23},{8,0},{9,25... | collective-permute-start | bytes 1572872 | tf_op jit(solution)/shard_map/ppermute | solution.py:47
  4.2 7.4 %collective-permute-done.4 = bf16[1024,256]{1,0:T(8,128)(2,1)S(1)} collective-permute-done((bf16[1024,256]{1,0:T(8,128)(2,1)}, bf16[1024,256]{1,0:T(8,128)(2,1)S(1)}, u32[]{:S(2)}, u32[]{:S(2)}) %collective-permute-start.4) | collective-permute-done | bytes 524320 | tf_op jit(solution)/shard_map/ppermute | solution.py:47
  11.5 1.1 pad_maximum_fusion.refs_4_
  12.7 2.2 %collective-permute-start.5 = (bf16[2,1024,256]{2,1,0:T(8,128)(2,1)S(1)}, bf16[2,1024,256]{2,1,0:T(8,128)(2,1)S(1)}, u32[]{:S(2)}, u32[]{:S(2)}) collective-permute-start(bf16[2,1024,256]{2,1,0:T(8,128)(2,1)S(1)} %pad_maximum_fusion.refs_4_), channel_id=1, source_target_pairs={{0,2},{1,3},{2,0},{3,1},{4,6},{5,7},{6,4},{7,5},{8,10},{9,11},{10,... | collective-permute-start | bytes 3145736 | tf_op jit(solution)/shard_map/ppermute | solution.py:47
  14.9 1.5 %collective-permute-start.7 = (bf16[2,1024,256]{2,1,0:T(8,128)(2,1)S(1)}, bf16[2,1024,256]{2,1,0:T(8,128)(2,1)S(1)}, u32[]{:S(2)}, u32[]{:S(2)}) collective-permute-start(bf16[2,1024,256]{2,1,0:T(8,128)(2,1)S(1)} %pad_maximum_fusion.refs_4_), channel_id=1, source_target_pairs={{0,16},{1,9},{2,18},{3,11},{4,20},{5,13},{6,22},{7,15},{8,24},{9,1... | collective-permute-start | bytes 3145736 | tf_op jit(solution)/shard_map/ppermute | solution.py:47
  16.4 0.7 collective-permute-start.6
  17.2 2.8 %copy-done = bf16[384,8192]{1,0:T(8,128)(2,1)S(1)} copy-done((bf16[384,8192]{1,0:T(8,128)(2,1)S(1)}, bf16[384,8192]{1,0:T(8,128)(2,1)}, u32[]{:S(2)}) %copy-start) | copy-done | bytes 6291480
  20.0 4.5 %terms.2 = (bf16[2,256,1024]{2,1,0:T(8,128)(2,1)S(1)}, bf16[2,256,1024]{2,1,0:T(8,128)(2,1)S(1)}, bf16[768,1024]{1,0:T(8,128)(2,1)S(1)}, bf16[1024,768]{1,0:T(8,128)(2,1)S(1)}) custom-call(s32[3]{0:T(128)S(1)} %pad_add_fusion.place.refs_0_, bf16[384,8192]{1,0:T(8,128)(2,1)S(1)} %copy-done, bf16[384,8192]{1,0:T(8,128)(2,1)} %collective-permute-done.other.refs_2_, ...), custom_call_target="tpu_custom_call" | custom-call | flops 1610612 | bytes 5767 | tf_op jit(solution)/shard_map/terms/pallas_call | solution.py:107
  24.5 0.6 collective-permute-start.8
  25.1 8.7 %terms.3 = (bf16[2,256,1024]{2,1,0:T(8,128)(2,1)S(1)}, bf16[2,256,1024]{2,1,0:T(8,128)(2,1)S(1)}, bf16[2,256,1024]{2,1,0:T(8,128)(2,1)S(1)}, bf16[2,256,1024]{2,...) custom-call(s32[3]{0:T(128)S(1)} %pad_add_fusion.place.refs_0_, ...), custom_call_target="tpu_custom_call" | custom-call | flops 4831838 | bytes 17301 | tf_op jit(solution)/shard_map/terms/pallas_call | solution.py:149
  33.7 1.6 %collective-permute-start.2 = (bf16[2,256,1024]{2,1,0:T(8,128)(2,1)S(1)}, bf16[2,256,1024]{2,1,0:T(8,128)(2,1)S(1)}, u32[]{:S(2)}, u32[]{:S(2)}) collective-permute-start(bf16[2,256,1024]{2,1,0:T(8,128)(2,1)S(1)} %get-tuple-element.51), channel_id=1, source_target_pairs={{0,16},{1,9},{2,18},{3,11},{4,20},{5,13},{6,22},{7,15},{8,24},{9,1... | collective-permute-start | bytes 3145736 | tf_op jit(solution)/shard_map/ppermute | solution.py:47
  35.3 2.1 %collective-permute-done.5.refs_1_.refs_4_ = bf16[2,1024,256]{2,1,0:T(8,128)(2,1)S(1)} collective-permute-done((bf16[2,1024,256]{2,1,0:T(8,128)(2,1)S(1)}, bf16[2,1024,256]{2,1,0:T(8,128)(2,1)S(1)}, u32[]{:S(2)}, u32[]{:S(2)}) %collective-permute-start.5) | collective-permute-done | bytes 1048608 | tf_op jit(solution)/shard_map/ppermute | solution.py:47
  37.4 1.1 gate.1.refs_0_
  38.5 2.4 %collective-permute-done.8 = bf16[2,256,1024]{2,1,0:T(8,128)(2,1)S(1)} collective-permute-done((bf16[2,256,1024]{2,1,0:T(8,128)(2,1)S(1)}, bf16[2,256,1024]{2,1,0:T(8,128)(2,1)S(1)}, u32[]{:S(2)}, u32[]{:S(2)}) %collective-permute-start.8) | collective-permute-done | bytes 1048608 | tf_op jit(solution)/shard_map/ppermute | solution.py:47
  41.4 5.6 %collective-permute-start.9 = (bf16[2,256,1024]{2,1,0:T(8,128)(2,1)S(1)}, bf16[2,256,1024]{2,1,0:T(8,128)(2,1)S(1)}, u32[]{:S(2)}, u32[]{:S(2)}) collective-permute-start(bf16[2,256,1024]{2,1,0:T(8,128)(2,1)S(1)} %add_convert_fusion.4), channel_id=1, source_target_pairs={{0,2},{1,3},{6,4},{7,5},{8,10},{9,11},{14,12},{15,13},{16,18},{17,... | collective-permute-start | bytes 3145736 | tf_op jit(solution)/shard_map/ppermute | solution.py:47
  47.0 0.7 collective-permute-start.10
  47.7 1.3 collective-permute-start.11
  49.0 1.6 %collective-permute-start.12 = (bf16[2,1024,256]{2,1,0:T(8,128)(2,1)S(1)}, bf16[2,1024,256]{2,1,0:T(8,128)(2,1)S(1)}, u32[]{:S(2)}, u32[]{:S(2)}) collective-permute-start(bf16[2,1024,256]{2,1,0:T(8,128)(2,1)S(1)} %collective-permute-done.5.refs_1_.refs_4_), channel_id=1, source_target_pairs={{0,16},{1,9},{2,18},{3,11},{4,20},{5,13},{6,22},{7,15},{8,24},{9,1... | collective-permute-start | bytes 3145736 | tf_op jit(solution)/shard_map/ppermute | solution.py:47
  50.6 1.6 %collective-permute-done.2 = bf16[2,256,1024]{2,1,0:T(8,128)(2,1)S(1)} collective-permute-done((bf16[2,256,1024]{2,1,0:T(8,128)(2,1)S(1)}, bf16[2,256,1024]{2,1,0:T(8,128)(2,1)S(1)}, u32[]{:S(2)}, u32[]{:S(2)}) %collective-permute-start.2) | collective-permute-done | bytes 1048608 | tf_op jit(solution)/shard_map/ppermute | solution.py:47
  52.6 1.6 %collective-permute-start.3 = (bf16[2,256,1024]{2,1,0:T(8,128)(2,1)S(1)}, bf16[2,256,1024]{2,1,0:T(8,128)(2,1)S(1)}, u32[]{:S(2)}, u32[]{:S(2)}) collective-permute-start(bf16[2,256,1024]{2,1,0:T(8,128)(2,1)S(1)} %get-tuple-element.52), channel_id=1, source_target_pairs={{0,16},{1,9},{2,18},{3,11},{4,20},{5,13},{6,22},{7,15},{8,24},{9,1... | collective-permute-start | bytes 3145736 | tf_op jit(solution)/shard_map/ppermute | solution.py:47
  54.2 6.5 %project.4 = (bf16[384,8192]{1,0:T(8,128)(2,1)}, bf16[384,1024]{1,0:T(8,128)(2,1)S(1)}, f32[768,1024]{1,0:T(8,128)S(1)}) custom-call(s32[3]{0:T(128)S(1)} %gate.1.refs_0_, bf16[384,8192]{1,0:T(8,128)(2,1)S(1)} %copy-done.1, bf16[384,8192]{1,0:T(8,128)(2,1)} %collective-permute-done.other.refs_2_, bf16[768,1024]{1,0:T(8,128)(2,1)S(1)} %get-tuple-element.59.refs_3_, ...), custom_call_target="tpu_custom_call" | custom-call | flops 3221225 | bytes 8388 | tf_op jit(solution)/shard_map/project/pallas_call | solution.py:216
  60.7 6.8 %collective-permute-done.9 = bf16[2,256,1024]{2,1,0:T(8,128)(2,1)S(1)} collective-permute-done((bf16[2,256,1024]{2,1,0:T(8,128)(2,1)S(1)}, bf16[2,256,1024]{2,1,0:T(8,128)(2,1)S(1)}, u32[]{:S(2)}, u32[]{:S(2)}) %collective-permute-start.9) | collective-permute-done | bytes 1048608 | tf_op jit(solution)/shard_map/ppermute | solution.py:47
  67.5 1.4 add_convert_fusion.3
  68.9 3.5 %collective-permute-done.11 = bf16[2,1024,256]{2,1,0:T(8,128)(2,1)S(1)} collective-permute-done((bf16[2,1024,256]{2,1,0:T(8,128)(2,1)S(1)}, bf16[2,1024,256]{2,1,0:T(8,128)(2,1)S(1)}, u32[]{:S(2)}, u32[]{:S(2)}) %collective-permute-start.11) | collective-permute-done | bytes 1048608 | tf_op jit(solution)/shard_map/ppermute | solution.py:47
  72.4 2.4 %collective-permute-start.13 = (bf16[2,256,1024]{2,1,0:T(8,128)(2,1)S(1)}, bf16[2,256,1024]{2,1,0:T(8,128)(2,1)}, u32[]{:S(2)}, u32[]{:S(2)}) collective-permute-start(bf16[2,256,1024]{2,1,0:T(8,128)(2,1)S(1)} %add_convert_fusion.6), channel_id=1, source_target_pairs={{0,2},{1,3},{6,4},{7,5},{8,10},{9,11},{14,12},{15,13},{16,18},{17,... | collective-permute-start | bytes 3145736 | tf_op jit(solution)/shard_map/ppermute | solution.py:47
  74.8 1.7 %collective-permute-start.14 = (bf16[2,256,1024]{2,1,0:T(8,128)(2,1)}, bf16[2,256,1024]{2,1,0:T(8,128)(2,1)}, u32[]{:S(2)}, u32[]{:S(2)}) collective-permute-start(bf16[2,256,1024]{2,1,0:T(8,128)(2,1)} %add_convert_fusion.3), channel_id=1, source_target_pairs={{2,4},{3,5},{4,2},{5,3},{10,12},{11,13},{12,10},{13,11},{18,20},{1... | collective-permute-start | bytes 3145736 | tf_op jit(solution)/shard_map/ppermute | solution.py:47
  76.5 1.5 %collective-permute-start.17 = (bf16[2,1024,256]{2,1,0:T(8,128)(2,1)S(1)}, bf16[2,1024,256]{2,1,0:T(8,128)(2,1)}, u32[]{:S(2)}, u32[]{:S(2)}) collective-permute-start(bf16[2,1024,256]{2,1,0:T(8,128)(2,1)S(1)} %collective-permute-done.10), channel_id=1, source_target_pairs={{2,0},{3,1},{4,6},{5,7},{10,8},{11,9},{12,14},{13,15},{18,16},{19,... | collective-permute-start | bytes 3145736 | tf_op jit(solution)/shard_map/ppermute | solution.py:47
  78.4 2.7 %collective-permute-start.15 = (bf16[2,256,1024]{2,1,0:T(8,128)(2,1)S(1)}, bf16[2,256,1024]{2,1,0:T(8,128)(2,1)S(1)}, u32[]{:S(2)}, u32[]{:S(2)}) collective-permute-start(bf16[2,256,1024]{2,1,0:T(8,128)(2,1)S(1)} %get-tuple-element.72), channel_id=1, source_target_pairs={{0,16},{1,9},{2,18},{3,11},{4,20},{5,13},{6,22},{7,15},{8,24},{9,1... | collective-permute-start | bytes 3145736 | tf_op jit(solution)/shard_map/ppermute | solution.py:47
  81.4 6.7 %project.5 = (bf16[384,8192]{1,0:T(8,128)(2,1)}, bf16[384,1024]{1,0:T(8,128)(2,1)S(1)}, f32[768,1024]{1,0:T(8,128)S(1)}) custom-call(s32[3]{0:T(128)S(1)} %pad_add_fusion.place.refs_0_, bf16[384,8192]{1,0:T(8,128)(2,1)S(1)} %copy-done.1, bf16[384,8192]{1,0:T(8,128)(2,1)} %collective-permute-done.other.refs_2_, ...), custom_call_target="tpu_custom_call", output_to_operand_aliasing={{0}: (7, {})} | custom-call | flops 3221225 | bytes 8388 | tf_op jit(solution)/shard_map/project/pallas_call | solution.py:216
  88.1 5.2 %collective-permute-done.13 = bf16[2,256,1024]{2,1,0:T(8,128)(2,1)} collective-permute-done((bf16[2,256,1024]{2,1,0:T(8,128)(2,1)S(1)}, bf16[2,256,1024]{2,1,0:T(8,128)(2,1)}, u32[]{:S(2)}, u32[]{:S(2)}) %collective-permute-start.13) | collective-permute-done | bytes 1048608 | tf_op jit(solution)/shard_map/ppermute | solution.py:47
  93.3 1.6 %add_convert_fusion.2 = bf16[2,256,1024]{2,1,0:T(8,128)(2,1)S(1)} fusion(bf16[2,256,1024]{2,1,0:T(8,128)(2,1)} %collective-permute-done.13, bf16[2,256,1024]{2,1,0:T(8,128)(2,1)S(1)} %add_convert_fusion.4), kind=kLoop, calls=%fused_computation.2 | loop fusion | flops 2097152 | bytes 3145728 | tf_op jit(solution)/shard_map/convert_element_type | solution.py:319
  95.0 1.6 %add_convert_fusion.1 = bf16[2,256,1024]{2,1,0:T(8,128)(2,1)S(1)} fusion(bf16[2,256,1024]{2,1,0:T(8,128)(2,1)} %collective-permute-done.14, bf16[2,256,1024]{2,1,0:T(8,128)(2,1)S(1)} %add_convert_fusion.5), kind=kLoop, calls=%fused_computation.1 | loop fusion | flops 2097152 | bytes 3145728 | tf_op jit(solution)/shard_map/convert_element_type | solution.py:319
  96.6 3.6 %collective-permute-done.17 = bf16[2,1024,256]{2,1,0:T(8,128)(2,1)} collective-permute-done((bf16[2,1024,256]{2,1,0:T(8,128)(2,1)S(1)}, bf16[2,1024,256]{2,1,0:T(8,128)(2,1)}, u32[]{:S(2)}, u32[]{:S(2)}) %collective-permute-start.17) | collective-permute-done | bytes 1048608 | tf_op jit(solution)/shard_map/ppermute | solution.py:47
  100.2 1.5 %add.52.refs_4_ = bf16[2,1024,256]{2,1,0:T(8,128)(2,1)S(1)} add(bf16[2,1024,256]{2,1,0:T(8,128)(2,1)S(1)} %collective-permute-done.6.refs_2_, bf16[2,1024,256]{2,1,0:T(8,128)(2,1)} %collective-permute-done.17) | non-fusion elementwise | flops 524288 | bytes 3145728 | tf_op jit(solution)/shard_map/add | solution.py:367
  101.7 3.7 %collective-permute-start.18 = (bf16[2,1024,256]{2,1,0:T(8,128)(2,1)S(1)}, bf16[2,1024,256]{2,1,0:T(8,128)(2,1)S(1)}, u32[]{:S(2)}, u32[]{:S(2)}) collective-permute-start(bf16[2,1024,256]{2,1,0:T(8,128)(2,1)S(1)} %add.52.refs_4_), channel_id=1, source_target_pairs={{0,16},{1,9},{2,18},{3,11},{4,20},{5,13},{6,22},{7,15},{8,24},{9,1... | collective-permute-start | bytes 3145736 | tf_op jit(solution)/shard_map/ppermute | solution.py:47
  105.5 0.7 collective-permute-start.21
  106.2 2.4 %collective-permute-start.22 = (bf16[2,256,1024]{2,1,0:T(8,128)(2,1)S(1)}, bf16[2,256,1024]{2,1,0:T(8,128)(2,1)S(1)}, u32[]{:S(2)}, u32[]{:S(2)}) collective-permute-start(bf16[2,256,1024]{2,1,0:T(8,128)(2,1)S(1)} %add_convert_fusion.1), channel_id=1, source_target_pairs={{0,2},{1,3},{2,0},{3,1},{4,6},{5,7},{6,4},{7,5},{8,10},{9,11},{10,... | collective-permute-start | bytes 3145736 | tf_op jit(solution)/shard_map/ppermute | solution.py:47
  109.0 6.7 %project.6 = (bf16[384,8192]{1,0:T(8,128)(2,1)}, bf16[384,1024]{1,0:T(8,128)(2,1)S(1)}, f32[768,1024]{1,0:T(8,128)S(1)}) custom-call(s32[3]{0:T(128)S(1)} %pad_add_fusion.place.refs_0_, bf16[384,8192]{1,0:T(8,128)(2,1)S(1)} %copy-done.1, bf16[384,8192]{1,0:T(8,128)(2,1)} %collective-permute-done.other.refs_2_, ...), custom_call_target="tpu_custom_call", output_to_operand_aliasing={{0}: (7, {})} | custom-call | flops 3221225 | bytes 8388 | tf_op jit(solution)/shard_map/project/pallas_call | solution.py:216
  115.7 2.5 %collective-permute-done.18.refs_5_ = bf16[2,1024,256]{2,1,0:T(8,128)(2,1)S(1)} collective-permute-done((bf16[2,1024,256]{2,1,0:T(8,128)(2,1)S(1)}, bf16[2,1024,256]{2,1,0:T(8,128)(2,1)S(1)}, u32[]{:S(2)}, u32[]{:S(2)}) %collective-permute-start.18) | collective-permute-done | bytes 1048608 | tf_op jit(solution)/shard_map/ppermute | solution.py:47
  118.2 6.8 %project.7 = (bf16[384,8192]{1,0:T(8,128)(2,1)}, bf16[384,1024]{1,0:T(8,128)(2,1)S(1)}, f32[384,1024]{1,0:T(8,128)S(1)}, f32[384,1024]{1,0:T(8,128)S(1)}) custom-call(s32[3]{0:T(128)S(1)} %pad_add_fusion.place.refs_0_, bf16[384,8192]{1,0:T(8,128)(2,1)S(1)} %copy-done.1, ...), custom_call_target="tpu_custom_call", output_to_operand_aliasing={{0}: (7, {})} | custom-call | flops 3221225 | bytes 8388 | tf_op jit(solution)/shard_map/project/pallas_call | solution.py:216
  125.6 1.3 collective-permute-done.22
  127.4 0.6 fusion
  128.0 1.6 %collective-permute-done.24.refs_0_ = bf16[384,1024]{1,0:T(8,128)(2,1)S(1)} collective-permute-done((bf16[384,1024]{1,0:T(8,128)(2,1)S(1)}, bf16[384,1024]{1,0:T(8,128)(2,1)S(1)}, u32[]{:S(2)}, u32[]{:S(2)}) %collective-permute-start.24) | collective-permute-done | bytes 786464 | tf_op jit(solution)/shard_map/ppermute | solution.py:47
  129.6 1.1 collective-permute-done.25.refs_1_
  130.7 1.1 collective-permute-done.26.refs_2_
  131.9 2.4 %lay.1.refs_6_ = bf16[384,8192]{1,0:T(8,128)(2,1)} custom-call(s32[3]{0:T(128)S(1)} %pad_add_fusion.place.refs_0_, bf16[384,1024]{1,0:T(8,128)(2,1)S(1)} %collective-permute-done.24.refs_0_, bf16[384,1024]{1,0:T(8,128)(2,1)S(1)} %collective-permute-done.25.refs_1_, ...), custom_call_target="tpu_custom_call", output_to_operand_aliasing={{}: (4, {})} | custom-call | bytes 4718 | tf_op jit(solution)/shard_map/lay/pallas_call | solution.py:255
  134.3 4.5 %collective-permute-done.23.refs_5_ = bf16[256,1024]{1,0:T(8,128)(2,1)S(1)} collective-permute-done((bf16[256,1024]{1,0:T(8,128)(2,1)S(1)}, bf16[256,1024]{1,0:T(8,128)(2,1)S(1)}, u32[]{:S(2)}, u32[]{:S(2)}) %collective-permute-start.23) | collective-permute-done | bytes 524320 | tf_op jit(solution)/shard_map/ppermute | solution.py:47
  138.8 2.5 %finish.1 = (bf16[384,8192]{1,0:T(8,128)(2,1)}, bf16[384,1024]{1,0:T(8,128)(2,1)}, bf16[1024,256]{1,0:T(8,128)(2,1)}) custom-call(s32[3]{0:T(128)S(1)} %pad_add_fusion.place.refs_0_, bf16[384,1024]{1,0:T(8,128)(2,1)S(1)} %collective-permute-done.19.refs_1_, f32[384,1024]{1,0:T(8,128)S(1)} %get-tuple-element.83.refs_2_, ...), custom_call_target="tpu_custom_call", output_to_operand_aliasing={{0}: (6, {})} | custom-call | bytes 5505 | tf_op jit(solution)/shard_map/finish/pallas_call | solution.py:284
  (33 shorter events, 3.7 us)
Async XLA Ops:
  0.6 16.6 %copy-start.2 = (bf16[384,1024]{1,0:T(8,128)(2,1)S(1)}, bf16[384,1024]{1,0:T(8,128)(2,1)}, u32[]{:S(2)}) copy-start(bf16[384,1024]{1,0:T(8,128)(2,1)} %cot_mine.1) | copy-start | bytes 2359300
  0.6 16.5 %collective-permute-start = (bf16[384,8192]{1,0:T(8,128)(2,1)}, bf16[384,8192]{1,0:T(8,128)(2,1)}, u32[]{:S(2)}, u32[]{:S(2)}) collective-permute-start(bf16[384,8192]{1,0:T(8,128)(2,1)} %refs_1_.3), channel_id=1, source_target_pairs={{0,1},{1,0},{2,3},{3,2},{4,5},{5,4},{6,7},{7,6},{8,9},{9,8},{10,11... | collective-permute-start | bytes 18874376 | tf_op jit(solution)/shard_map/ppermute | solution.py:47
  1.2 16.0 %collective-permute-start.1 = (bf16[384,1024]{1,0:T(8,128)(2,1)}, bf16[384,1024]{1,0:T(8,128)(2,1)S(1)}, u32[]{:S(2)}, u32[]{:S(2)}) collective-permute-start(bf16[384,1024]{1,0:T(8,128)(2,1)} %cot_mine.1), channel_id=1, source_target_pairs={{0,1},{1,0},{2,3},{3,2},{4,5},{5,4},{6,7},{7,6},{8,9},{9,8},{10,11... | collective-permute-start | bytes 2359304 | tf_op jit(solution)/shard_map/ppermute | solution.py:47
  1.2 10.3 %collective-permute-start.4 = (bf16[1024,256]{1,0:T(8,128)(2,1)}, bf16[1024,256]{1,0:T(8,128)(2,1)S(1)}, u32[]{:S(2)}, u32[]{:S(2)}) collective-permute-start(bf16[1024,256]{1,0:T(8,128)(2,1)} %param.5), channel_id=1, source_target_pairs={{0,8},{1,17},{2,10},{3,19},{4,12},{5,21},{6,14},{7,23},{8,0},{9,25... | collective-permute-start | bytes 1572872 | tf_op jit(solution)/shard_map/ppermute | solution.py:47
  12.7 24.7 %collective-permute-start.5 = (bf16[2,1024,256]{2,1,0:T(8,128)(2,1)S(1)}, bf16[2,1024,256]{2,1,0:T(8,128)(2,1)S(1)}, u32[]{:S(2)}, u32[]{:S(2)}) collective-permute-start(bf16[2,1024,256]{2,1,0:T(8,128)(2,1)S(1)} %pad_maximum_fusion.refs_4_), channel_id=1, source_target_pairs={{0,2},{1,3},{2,0},{3,1},{4,6},{5,7},{6,4},{7,5},{8,10},{9,11},{10,... | collective-permute-start | bytes 3145736 | tf_op jit(solution)/shard_map/ppermute | solution.py:47
  14.9 22.5 %collective-permute-start.7 = (bf16[2,1024,256]{2,1,0:T(8,128)(2,1)S(1)}, bf16[2,1024,256]{2,1,0:T(8,128)(2,1)S(1)}, u32[]{:S(2)}, u32[]{:S(2)}) collective-permute-start(bf16[2,1024,256]{2,1,0:T(8,128)(2,1)S(1)} %pad_maximum_fusion.refs_4_), channel_id=1, source_target_pairs={{0,16},{1,9},{2,18},{3,11},{4,20},{5,13},{6,22},{7,15},{8,24},{9,1... | collective-permute-start | bytes 3145736 | tf_op jit(solution)/shard_map/ppermute | solution.py:47
  16.4 21.0 %collective-permute-start.6 = (bf16[2,1024,256]{2,1,0:T(8,128)(2,1)S(1)}, bf16[2,1024,256]{2,1,0:T(8,128)(2,1)S(1)}, u32[]{:S(2)}, u32[]{:S(2)}) collective-permute-start(bf16[2,1024,256]{2,1,0:T(8,128)(2,1)S(1)} %pad_maximum_fusion.refs_4_), channel_id=1, source_target_pairs={{2,4},{3,5},{4,2},{5,3},{10,12},{11,13},{12,10},{13,11},{18,20},{1... | collective-permute-start | bytes 3145736 | tf_op jit(solution)/shard_map/ppermute | solution.py:47
  17.2 2.8 %copy-start = (bf16[384,8192]{1,0:T(8,128)(2,1)S(1)}, bf16[384,8192]{1,0:T(8,128)(2,1)}, u32[]{:S(2)}) copy-start(bf16[384,8192]{1,0:T(8,128)(2,1)} %refs_1_.3) | copy-start | bytes 18874372
  20.0 5.1 %copy-start.1 = (bf16[384,8192]{1,0:T(8,128)(2,1)S(1)}, bf16[384,8192]{1,0:T(8,128)(2,1)}, u32[]{:S(2)}) copy-start(bf16[384,8192]{1,0:T(8,128)(2,1)} %refs_1_.3) | copy-start | bytes 18874372
  24.5 16.5 %collective-permute-start.8 = (bf16[2,256,1024]{2,1,0:T(8,128)(2,1)S(1)}, bf16[2,256,1024]{2,1,0:T(8,128)(2,1)S(1)}, u32[]{:S(2)}, u32[]{:S(2)}) collective-permute-start(bf16[2,256,1024]{2,1,0:T(8,128)(2,1)S(1)} %get-tuple-element.57), channel_id=1, source_target_pairs={{0,16},{1,9},{2,18},{3,11},{4,20},{5,13},{6,22},{7,15},{8,24},{9,1... | collective-permute-start | bytes 3145736 | tf_op jit(solution)/shard_map/ppermute | solution.py:47
  33.7 18.5 %collective-permute-start.2 = (bf16[2,256,1024]{2,1,0:T(8,128)(2,1)S(1)}, bf16[2,256,1024]{2,1,0:T(8,128)(2,1)S(1)}, u32[]{:S(2)}, u32[]{:S(2)}) collective-permute-start(bf16[2,256,1024]{2,1,0:T(8,128)(2,1)S(1)} %get-tuple-element.51), channel_id=1, source_target_pairs={{0,16},{1,9},{2,18},{3,11},{4,20},{5,13},{6,22},{7,15},{8,24},{9,1... | collective-permute-start | bytes 3145736 | tf_op jit(solution)/shard_map/ppermute | solution.py:47
  41.4 26.1 %collective-permute-start.9 = (bf16[2,256,1024]{2,1,0:T(8,128)(2,1)S(1)}, bf16[2,256,1024]{2,1,0:T(8,128)(2,1)S(1)}, u32[]{:S(2)}, u32[]{:S(2)}) collective-permute-start(bf16[2,256,1024]{2,1,0:T(8,128)(2,1)S(1)} %add_convert_fusion.4), channel_id=1, source_target_pairs={{0,2},{1,3},{6,4},{7,5},{8,10},{9,11},{14,12},{15,13},{16,18},{17,... | collective-permute-start | bytes 3145736 | tf_op jit(solution)/shard_map/ppermute | solution.py:47
  47.0 21.9 %collective-permute-start.10 = (bf16[2,1024,256]{2,1,0:T(8,128)(2,1)S(1)}, bf16[2,1024,256]{2,1,0:T(8,128)(2,1)S(1)}, u32[]{:S(2)}, u32[]{:S(2)}) collective-permute-start(bf16[2,1024,256]{2,1,0:T(8,128)(2,1)S(1)} %collective-permute-done.5.refs_1_.refs_4_), channel_id=1, source_target_pairs={{2,4},{3,5},{4,2},{5,3},{10,12},{11,13},{12,10},{13,11},{18,20},{1... | collective-permute-start | bytes 3145736 | tf_op jit(solution)/shard_map/ppermute | solution.py:47
  47.7 24.7 %collective-permute-start.11 = (bf16[2,1024,256]{2,1,0:T(8,128)(2,1)S(1)}, bf16[2,1024,256]{2,1,0:T(8,128)(2,1)S(1)}, u32[]{:S(2)}, u32[]{:S(2)}) collective-permute-start(bf16[2,1024,256]{2,1,0:T(8,128)(2,1)S(1)} %collective-permute-done.6.refs_2_), channel_id=1, source_target_pairs={{2,0},{3,1},{4,6},{5,7},{10,8},{11,9},{12,14},{13,15},{18,16},{19,... | collective-permute-start | bytes 3145736 | tf_op jit(solution)/shard_map/ppermute | solution.py:47
  49.0 23.4 %collective-permute-start.12 = (bf16[2,1024,256]{2,1,0:T(8,128)(2,1)S(1)}, bf16[2,1024,256]{2,1,0:T(8,128)(2,1)S(1)}, u32[]{:S(2)}, u32[]{:S(2)}) collective-permute-start(bf16[2,1024,256]{2,1,0:T(8,128)(2,1)S(1)} %collective-permute-done.5.refs_1_.refs_4_), channel_id=1, source_target_pairs={{0,16},{1,9},{2,18},{3,11},{4,20},{5,13},{6,22},{7,15},{8,24},{9,1... | collective-permute-start | bytes 3145736 | tf_op jit(solution)/shard_map/ppermute | solution.py:47
  52.6 25.4 %collective-permute-start.3 = (bf16[2,256,1024]{2,1,0:T(8,128)(2,1)S(1)}, bf16[2,256,1024]{2,1,0:T(8,128)(2,1)S(1)}, u32[]{:S(2)}, u32[]{:S(2)}) collective-permute-start(bf16[2,256,1024]{2,1,0:T(8,128)(2,1)S(1)} %get-tuple-element.52), channel_id=1, source_target_pairs={{0,16},{1,9},{2,18},{3,11},{4,20},{5,13},{6,22},{7,15},{8,24},{9,1... | collective-permute-start | bytes 3145736 | tf_op jit(solution)/shard_map/ppermute | solution.py:47
  72.4 20.9 %collective-permute-start.13 = (bf16[2,256,1024]{2,1,0:T(8,128)(2,1)S(1)}, bf16[2,256,1024]{2,1,0:T(8,128)(2,1)}, u32[]{:S(2)}, u32[]{:S(2)}) collective-permute-start(bf16[2,256,1024]{2,1,0:T(8,128)(2,1)S(1)} %add_convert_fusion.6), channel_id=1, source_target_pairs={{0,2},{1,3},{6,4},{7,5},{8,10},{9,11},{14,12},{15,13},{16,18},{17,... | collective-permute-start | bytes 3145736 | tf_op jit(solution)/shard_map/ppermute | solution.py:47
  74.8 20.1 %collective-permute-start.14 = (bf16[2,256,1024]{2,1,0:T(8,128)(2,1)}, bf16[2,256,1024]{2,1,0:T(8,128)(2,1)}, u32[]{:S(2)}, u32[]{:S(2)}) collective-permute-start(bf16[2,256,1024]{2,1,0:T(8,128)(2,1)} %add_convert_fusion.3), channel_id=1, source_target_pairs={{2,4},{3,5},{4,2},{5,3},{10,12},{11,13},{12,10},{13,11},{18,20},{1... | collective-permute-start | bytes 3145736 | tf_op jit(solution)/shard_map/ppermute | solution.py:47
  76.5 23.7 %collective-permute-start.17 = (bf16[2,1024,256]{2,1,0:T(8,128)(2,1)S(1)}, bf16[2,1024,256]{2,1,0:T(8,128)(2,1)}, u32[]{:S(2)}, u32[]{:S(2)}) collective-permute-start(bf16[2,1024,256]{2,1,0:T(8,128)(2,1)S(1)} %collective-permute-done.10), channel_id=1, source_target_pairs={{2,0},{3,1},{4,6},{5,7},{10,8},{11,9},{12,14},{13,15},{18,16},{19,... | collective-permute-start | bytes 3145736 | tf_op jit(solution)/shard_map/ppermute | solution.py:47
  78.4 30.2 %collective-permute-start.15 = (bf16[2,256,1024]{2,1,0:T(8,128)(2,1)S(1)}, bf16[2,256,1024]{2,1,0:T(8,128)(2,1)S(1)}, u32[]{:S(2)}, u32[]{:S(2)}) collective-permute-start(bf16[2,256,1024]{2,1,0:T(8,128)(2,1)S(1)} %get-tuple-element.72), channel_id=1, source_target_pairs={{0,16},{1,9},{2,18},{3,11},{4,20},{5,13},{6,22},{7,15},{8,24},{9,1... | collective-permute-start | bytes 3145736 | tf_op jit(solution)/shard_map/ppermute | solution.py:47
  81.3 24.8 %collective-permute-start.16 = (bf16[2,1024,256]{2,1,0:T(8,128)(2,1)S(1)}, bf16[2,1024,256]{2,1,0:T(8,128)(2,1)S(1)}, u32[]{:S(2)}, u32[]{:S(2)}) collective-permute-start(bf16[2,1024,256]{2,1,0:T(8,128)(2,1)S(1)} %add.51.refs_4_), channel_id=1, source_target_pairs={{0,16},{1,9},{2,18},{3,11},{4,20},{5,13},{6,22},{7,15},{8,24},{9,1... | collective-permute-start | bytes 3145736 | tf_op jit(solution)/shard_map/ppermute | solution.py:47
  101.7 16.5 %collective-permute-start.18 = (bf16[2,1024,256]{2,1,0:T(8,128)(2,1)S(1)}, bf16[2,1024,256]{2,1,0:T(8,128)(2,1)S(1)}, u32[]{:S(2)}, u32[]{:S(2)}) collective-permute-start(bf16[2,1024,256]{2,1,0:T(8,128)(2,1)S(1)} %add.52.refs_4_), channel_id=1, source_target_pairs={{0,16},{1,9},{2,18},{3,11},{4,20},{5,13},{6,22},{7,15},{8,24},{9,1... | collective-permute-start | bytes 3145736 | tf_op jit(solution)/shard_map/ppermute | solution.py:47
  105.5 21.4 %collective-permute-start.21 = (bf16[2,256,1024]{2,1,0:T(8,128)(2,1)S(1)}, bf16[2,256,1024]{2,1,0:T(8,128)(2,1)S(1)}, u32[]{:S(2)}, u32[]{:S(2)}) collective-permute-start(bf16[2,256,1024]{2,1,0:T(8,128)(2,1)S(1)} %add_convert_fusion.2), channel_id=1, source_target_pairs={{2,4},{3,5},{4,2},{5,3},{10,12},{11,13},{12,10},{13,11},{18,20},{1... | collective-permute-start | bytes 3145736 | tf_op jit(solution)/shard_map/ppermute | solution.py:47
  106.2 20.7 %collective-permute-start.22 = (bf16[2,256,1024]{2,1,0:T(8,128)(2,1)S(1)}, bf16[2,256,1024]{2,1,0:T(8,128)(2,1)S(1)}, u32[]{:S(2)}, u32[]{:S(2)}) collective-permute-start(bf16[2,256,1024]{2,1,0:T(8,128)(2,1)S(1)} %add_convert_fusion.1), channel_id=1, source_target_pairs={{0,2},{1,3},{2,0},{3,1},{4,6},{5,7},{6,4},{7,5},{8,10},{9,11},{10,... | collective-permute-start | bytes 3145736 | tf_op jit(solution)/shard_map/ppermute | solution.py:47
  125.1 13.7 %collective-permute-start.20 = (f32[384,1024]{1,0:T(8,128)S(1)}, f32[384,1024]{1,0:T(8,128)S(1)}, u32[]{:S(2)}, u32[]{:S(2)}) collective-permute-start(f32[384,1024]{1,0:T(8,128)S(1)} %get-tuple-element.84), channel_id=1, source_target_pairs={{0,1},{1,0},{2,3},{3,2},{4,5},{5,4},{6,7},{7,6},{8,9},{9,8},{10,11... | collective-permute-start | bytes 4718600 | tf_op jit(solution)/shard_map/ppermute | solution.py:47
  125.1 4.5 %collective-permute-start.24 = (bf16[384,1024]{1,0:T(8,128)(2,1)S(1)}, bf16[384,1024]{1,0:T(8,128)(2,1)S(1)}, u32[]{:S(2)}, u32[]{:S(2)}) collective-permute-start(bf16[384,1024]{1,0:T(8,128)(2,1)S(1)} %get-tuple-element.60), channel_id=1, source_target_pairs={{0,1},{1,0},{2,3},{3,2},{4,5},{5,4},{6,7},{7,6},{8,9},{9,8},{10,11... | collective-permute-start | bytes 2359304 | tf_op jit(solution)/shard_map/ppermute | solution.py:47
  125.6 5.1 %collective-permute-start.25 = (bf16[384,1024]{1,0:T(8,128)(2,1)S(1)}, bf16[384,1024]{1,0:T(8,128)(2,1)S(1)}, u32[]{:S(2)}, u32[]{:S(2)}) collective-permute-start(bf16[384,1024]{1,0:T(8,128)(2,1)S(1)} %get-tuple-element.69), channel_id=1, source_target_pairs={{0,1},{1,0},{2,3},{3,2},{4,5},{5,4},{6,7},{7,6},{8,9},{9,8},{10,11... | collective-permute-start | bytes 2359304 | tf_op jit(solution)/shard_map/ppermute | solution.py:47
  126.9 5.0 %collective-permute-start.26 = (bf16[384,1024]{1,0:T(8,128)(2,1)S(1)}, bf16[384,1024]{1,0:T(8,128)(2,1)S(1)}, u32[]{:S(2)}, u32[]{:S(2)}) collective-permute-start(bf16[384,1024]{1,0:T(8,128)(2,1)S(1)} %get-tuple-element.77), channel_id=1, source_target_pairs={{0,1},{1,0},{2,3},{3,2},{4,5},{5,4},{6,7},{7,6},{8,9},{9,8},{10,11... | collective-permute-start | bytes 2359304 | tf_op jit(solution)/shard_map/ppermute | solution.py:47
  126.9 11.9 %collective-permute-start.19 = (bf16[384,1024]{1,0:T(8,128)(2,1)S(1)}, bf16[384,1024]{1,0:T(8,128)(2,1)S(1)}, u32[]{:S(2)}, u32[]{:S(2)}) collective-permute-start(bf16[384,1024]{1,0:T(8,128)(2,1)S(1)} %get-tuple-element.82), channel_id=1, source_target_pairs={{0,1},{1,0},{2,3},{3,2},{4,5},{5,4},{6,7},{7,6},{8,9},{9,8},{10,11... | collective-permute-start | bytes 2359304 | tf_op jit(solution)/shard_map/ppermute | solution.py:47
  129.6 9.2 %collective-permute-start.23 = (bf16[256,1024]{1,0:T(8,128)(2,1)S(1)}, bf16[256,1024]{1,0:T(8,128)(2,1)S(1)}, u32[]{:S(2)}, u32[]{:S(2)}) collective-permute-start(bf16[256,1024]{1,0:T(8,128)(2,1)S(1)} %get-tuple-element.91), channel_id=1, source_target_pairs={{0,8},{1,17},{2,10},{3,19},{4,12},{5,21},{6,14},{7,23},{8,0},{9,25... | collective-permute-start | bytes 1572872 | tf_op jit(solution)/shard_map/ppermute | solution.py:47

commit v13 on v12

--- a/solution.py
+++ b/solution.py
@@ -363,28 +363,35 @@
     sum3_near = added(sum3, near)
     sum_mid = sent(sum3_near, MID)
     sum1_far = added(after(sum1, sum3_near, out1), mid_far)
-    sum_one = sent(after(sum1_far, three_end, two_b), PAIR)
+    sum_one = sent(sum1_far, PAIR)
     three = after(mid, sum1_far) + three_end
     three_b = sent(three, FLIP_B)
     sum0 = added(keep0, got0)
     whole, out2, keys = projected(
         place,
         2,
-        after(activations, sum1_far, sum0),
+        after(activations, sum1_far, sum0, three),
         other,
         cots,
         two,
         two_b,
         (whole, None, keys),
     )
-    whole, out3, keys, keys_far = projected(
-        place, 3, after(activations, out2), other, cots, three, three_b, (whole, None, keys)
-    )
-    sum_one = after(sum_one, out3)
     last = [
         sum0[a].astype(F32) + sum_mid[a].astype(F32) + sum_one[a].astype(F32) for a in (0, 1)
     ]
     over = last[1].astype(BF16)
+    arrived = sent(over, FLIP_A)
+    whole, out3, keys, keys_far = projected(
+        place,
+        3,
+        after(activations, out2, over),
+        other,
+        cots,
+        three,
+        three_b,
+        (whole, None, keys),
+    )
     whole = laid(
         place,
         whole,
@@ -395,9 +402,9 @@
         whole,
         sent(out3, SWAP),
         keys,
-        sent(keys_far, SWAP),
+        sent(after(keys_far, arrived), SWAP),
         last[0],
-        sent(over, FLIP_A),
+        arrived,
         1.0 / math.sqrt(32 * tokens),
     )
     return (key_values, grad_input, grad_weight)

time: 142 us -> 154 us (1.085)
  waiting for transfers between devices: 44.8 us -> 55.8 us
  starting transfers between devices: 37.1 us -> 39.2 us
    ppermute x27, waiting for transfers between devices: 44.8 us -> 55.8 us  [sent(): return lax.ppermute(array, AXES, pairs)]
    ppermute x27, starting transfers between devices: 37.1 us -> 39.2 us  [sent(): return lax.ppermute(array, AXES, pairs)]
  transfers between devices with their start and end apart: 27 -> 27, of which waited for: 14 -> 12; matrix products, arithmetic and copies ran while one was open for 7% -> 6% of each run, Pallas kernels for 31% -> 28%
where the time goes in v13:
time: 154 us
  waiting for transfers between devices  55.8 us (36%)
  Pallas kernels  46 us (30%)
  starting transfers between devices  39.2 us (25%)
  other arithmetic  8.97 us (6%)
  local copies, waits for them, and re-layouts  2.8 us (2%)
    ppermute x27, waiting for transfers between devices, sent(): return lax.ppermute(array, AXES, pairs)  55.8 us
    ppermute x27, starting transfers between devices, sent(): return lax.ppermute(array, AXES, pairs)  39.2 us
    pallas_call x4, Pallas kernels, projected(): pl.pallas_call(lambda *refs: project_kernel(*refs, first=first, last=last...  26.8 us
    pallas_call x1, Pallas kernels, terms(): pl.pallas_call(term_kernel, grid_spec=pltpu.PrefetchScalarGridSpec(num_sc...  8.66 us
    convert_element_type x7, other arithmetic, added(): return total.astype(BF16)  6.6 us
    pallas_call x1, Pallas kernels, first_terms(): pl.pallas_call(first_term_kernel, grid_spec=pltpu.PrefetchScalarGridSpec(...  4.49 us
  transfers between devices with their start and end apart: 27, of which 12 were waited for; matrix products, arithmetic and copies ran while one was open for 6% of the time, Pallas kernels for 28%

profile of v13, /device:TPU:0, one launch (start us, length us, event | category | flops | bytes accessed | tf_op | source)
XLA Modules:
  0.0 153.7 jit_solution(2359574937921870410)
XLA Ops:
  0.6 0.5 collective-permute-start
  1.2 2.9 %collective-permute-start.4 = (bf16[1024,256]{1,0:T(8,128)(2,1)}, bf16[1024,256]{1,0:T(8,128)(2,1)S(1)}, u32[]{:S(2)}, u32[]{:S(2)}) collective-permute-start(bf16[1024,256]{1,0:T(8,128)(2,1)} %param.5), channel_id=1, source_target_pairs={{0,8},{1,17},{2,10},{3,19},{4,12},{5,21},{6,14},{7,23},{8,0},{9,25... | collective-permute-start | bytes 1572872 | tf_op jit(solution)/shard_map/ppermute | solution.py:47
  4.2 7.4 %collective-permute-done.4 = bf16[1024,256]{1,0:T(8,128)(2,1)S(1)} collective-permute-done((bf16[1024,256]{1,0:T(8,128)(2,1)}, bf16[1024,256]{1,0:T(8,128)(2,1)S(1)}, u32[]{:S(2)}, u32[]{:S(2)}) %collective-permute-start.4) | collective-permute-done | bytes 524320 | tf_op jit(solution)/shard_map/ppermute | solution.py:47
  11.5 1.1 pad_maximum_fusion.refs_4_
  12.7 2.2 %collective-permute-start.5 = (bf16[2,1024,256]{2,1,0:T(8,128)(2,1)S(1)}, bf16[2,1024,256]{2,1,0:T(8,128)(2,1)S(1)}, u32[]{:S(2)}, u32[]{:S(2)}) collective-permute-start(bf16[2,1024,256]{2,1,0:T(8,128)(2,1)S(1)} %pad_maximum_fusion.refs_4_), channel_id=1, source_target_pairs={{0,2},{1,3},{2,0},{3,1},{4,6},{5,7},{6,4},{7,5},{8,10},{9,11},{10,... | collective-permute-start | bytes 3145736 | tf_op jit(solution)/shard_map/ppermute | solution.py:47
  14.9 0.7 collective-permute-start.6
  15.6 1.6 %collective-permute-start.7 = (bf16[2,1024,256]{2,1,0:T(8,128)(2,1)S(1)}, bf16[2,1024,256]{2,1,0:T(8,128)(2,1)S(1)}, u32[]{:S(2)}, u32[]{:S(2)}) collective-permute-start(bf16[2,1024,256]{2,1,0:T(8,128)(2,1)S(1)} %pad_maximum_fusion.refs_4_), channel_id=1, source_target_pairs={{0,16},{1,9},{2,18},{3,11},{4,20},{5,13},{6,22},{7,15},{8,24},{9,1... | collective-permute-start | bytes 3145736 | tf_op jit(solution)/shard_map/ppermute | solution.py:47
  17.2 2.8 %copy-done = bf16[384,8192]{1,0:T(8,128)(2,1)S(1)} copy-done((bf16[384,8192]{1,0:T(8,128)(2,1)S(1)}, bf16[384,8192]{1,0:T(8,128)(2,1)}, u32[]{:S(2)}) %copy-start) | copy-done | bytes 6291480
  20.0 4.5 %terms.2 = (bf16[2,256,1024]{2,1,0:T(8,128)(2,1)S(1)}, bf16[2,256,1024]{2,1,0:T(8,128)(2,1)S(1)}, bf16[768,1024]{1,0:T(8,128)(2,1)S(1)}, bf16[1024,768]{1,0:T(8,128)(2,1)S(1)}) custom-call(s32[3]{0:T(128)S(1)} %pad_add_fusion.place.refs_0_, bf16[384,8192]{1,0:T(8,128)(2,1)S(1)} %copy-done, bf16[384,8192]{1,0:T(8,128)(2,1)} %collective-permute-done.other.refs_2_, ...), custom_call_target="tpu_custom_call" | custom-call | flops 1610612 | bytes 5767 | tf_op jit(solution)/shard_map/terms/pallas_call | solution.py:107
  24.5 0.6 collective-permute-start.8
  25.1 8.7 %terms.3 = (bf16[2,256,1024]{2,1,0:T(8,128)(2,1)S(1)}, bf16[2,256,1024]{2,1,0:T(8,128)(2,1)S(1)}, bf16[2,256,1024]{2,1,0:T(8,128)(2,1)S(1)}, bf16[2,256,1024]{2,...) custom-call(s32[3]{0:T(128)S(1)} %pad_add_fusion.place.refs_0_, ...), custom_call_target="tpu_custom_call" | custom-call | flops 4831838 | bytes 17301 | tf_op jit(solution)/shard_map/terms/pallas_call | solution.py:149
  33.8 1.6 %collective-permute-start.2 = (bf16[2,256,1024]{2,1,0:T(8,128)(2,1)S(1)}, bf16[2,256,1024]{2,1,0:T(8,128)(2,1)S(1)}, u32[]{:S(2)}, u32[]{:S(2)}) collective-permute-start(bf16[2,256,1024]{2,1,0:T(8,128)(2,1)S(1)} %get-tuple-element.50), channel_id=1, source_target_pairs={{0,16},{1,9},{2,18},{3,11},{4,20},{5,13},{6,22},{7,15},{8,24},{9,1... | collective-permute-start | bytes 3145736 | tf_op jit(solution)/shard_map/ppermute | solution.py:47
  35.4 2.0 %collective-permute-done.5.refs_1_.refs_4_ = bf16[2,1024,256]{2,1,0:T(8,128)(2,1)S(1)} collective-permute-done((bf16[2,1024,256]{2,1,0:T(8,128)(2,1)S(1)}, bf16[2,1024,256]{2,1,0:T(8,128)(2,1)S(1)}, u32[]{:S(2)}, u32[]{:S(2)}) %collective-permute-start.5) | collective-permute-done | bytes 1048608 | tf_op jit(solution)/shard_map/ppermute | solution.py:47
  37.4 1.1 gate.1.refs_0_
  38.5 3.2 %collective-permute-done.8 = bf16[2,256,1024]{2,1,0:T(8,128)(2,1)S(1)} collective-permute-done((bf16[2,256,1024]{2,1,0:T(8,128)(2,1)S(1)}, bf16[2,256,1024]{2,1,0:T(8,128)(2,1)S(1)}, u32[]{:S(2)}, u32[]{:S(2)}) %collective-permute-start.8) | collective-permute-done | bytes 1048608 | tf_op jit(solution)/shard_map/ppermute | solution.py:47
  42.2 7.2 %collective-permute-start.9 = (bf16[2,256,1024]{2,1,0:T(8,128)(2,1)S(1)}, bf16[2,256,1024]{2,1,0:T(8,128)(2,1)}, u32[]{:S(2)}, u32[]{:S(2)}) collective-permute-start(bf16[2,256,1024]{2,1,0:T(8,128)(2,1)S(1)} %add_convert_fusion.4), channel_id=1, source_target_pairs={{0,2},{1,3},{6,4},{7,5},{8,10},{9,11},{14,12},{15,13},{16,18},{17,... | collective-permute-start | bytes 3145736 | tf_op jit(solution)/shard_map/ppermute | solution.py:47
  49.4 1.5 collective-permute-start.12
  50.9 0.7 collective-permute-start.10
  51.6 1.3 collective-permute-start.11
  53.4 1.6 %collective-permute-start.3 = (bf16[2,256,1024]{2,1,0:T(8,128)(2,1)S(1)}, bf16[2,256,1024]{2,1,0:T(8,128)(2,1)S(1)}, u32[]{:S(2)}, u32[]{:S(2)}) collective-permute-start(bf16[2,256,1024]{2,1,0:T(8,128)(2,1)S(1)} %get-tuple-element.51), channel_id=1, source_target_pairs={{0,16},{1,9},{2,18},{3,11},{4,20},{5,13},{6,22},{7,15},{8,24},{9,1... | collective-permute-start | bytes 3145736 | tf_op jit(solution)/shard_map/ppermute | solution.py:47
  55.0 6.5 %project.4 = (bf16[384,8192]{1,0:T(8,128)(2,1)}, bf16[384,1024]{1,0:T(8,128)(2,1)S(1)}, f32[768,1024]{1,0:T(8,128)S(1)}) custom-call(s32[3]{0:T(128)S(1)} %gate.1.refs_0_, bf16[384,8192]{1,0:T(8,128)(2,1)S(1)} %copy-done.1, bf16[384,8192]{1,0:T(8,128)(2,1)} %collective-permute-done.other.refs_2_, bf16[768,1024]{1,0:T(8,128)(2,1)S(1)} %get-tuple-element.58.refs_3_, ...), custom_call_target="tpu_custom_call" | custom-call | flops 3221225 | bytes 8388 | tf_op jit(solution)/shard_map/project/pallas_call | solution.py:216
  61.4 7.3 %collective-permute-done.9 = bf16[2,256,1024]{2,1,0:T(8,128)(2,1)} collective-permute-done((bf16[2,256,1024]{2,1,0:T(8,128)(2,1)S(1)}, bf16[2,256,1024]{2,1,0:T(8,128)(2,1)}, u32[]{:S(2)}, u32[]{:S(2)}) %collective-permute-start.9) | collective-permute-done | bytes 1048608 | tf_op jit(solution)/shard_map/ppermute | solution.py:47
  68.8 1.6 %add_convert_fusion.3 = bf16[2,256,1024]{2,1,0:T(8,128)(2,1)S(1)} fusion(bf16[2,256,1024]{2,1,0:T(8,128)(2,1)} %collective-permute-done.9, bf16[2,256,1024]{2,1,0:T(8,128)(2,1)S(1)} %add_convert_fusion.6), kind=kLoop, calls=%fused_computation.3 | loop fusion | flops 2097152 | bytes 3145728 | tf_op jit(solution)/shard_map/convert_element_type | solution.py:319
  70.4 5.4 %collective-permute-done.11 = bf16[2,1024,256]{2,1,0:T(8,128)(2,1)S(1)} collective-permute-done((bf16[2,1024,256]{2,1,0:T(8,128)(2,1)S(1)}, bf16[2,1024,256]{2,1,0:T(8,128)(2,1)S(1)}, u32[]{:S(2)}, u32[]{:S(2)}) %collective-permute-start.11) | collective-permute-done | bytes 1048608 | tf_op jit(solution)/shard_map/ppermute | solution.py:47
  75.8 2.4 %collective-permute-start.13 = (bf16[2,256,1024]{2,1,0:T(8,128)(2,1)S(1)}, bf16[2,256,1024]{2,1,0:T(8,128)(2,1)}, u32[]{:S(2)}, u32[]{:S(2)}) collective-permute-start(bf16[2,256,1024]{2,1,0:T(8,128)(2,1)S(1)} %add_convert_fusion.6), channel_id=1, source_target_pairs={{0,2},{1,3},{6,4},{7,5},{8,10},{9,11},{14,12},{15,13},{16,18},{17,... | collective-permute-start | bytes 3145736 | tf_op jit(solution)/shard_map/ppermute | solution.py:47
  78.2 1.7 %collective-permute-start.14 = (bf16[2,256,1024]{2,1,0:T(8,128)(2,1)S(1)}, bf16[2,256,1024]{2,1,0:T(8,128)(2,1)}, u32[]{:S(2)}, u32[]{:S(2)}) collective-permute-start(bf16[2,256,1024]{2,1,0:T(8,128)(2,1)S(1)} %add_convert_fusion.3), channel_id=1, source_target_pairs={{2,4},{3,5},{4,2},{5,3},{10,12},{11,13},{12,10},{13,11},{18,20},{1... | collective-permute-start | bytes 3145736 | tf_op jit(solution)/shard_map/ppermute | solution.py:47
  80.4 1.6 %collective-permute-start.15 = (bf16[2,256,1024]{2,1,0:T(8,128)(2,1)S(1)}, bf16[2,256,1024]{2,1,0:T(8,128)(2,1)S(1)}, u32[]{:S(2)}, u32[]{:S(2)}) collective-permute-start(bf16[2,256,1024]{2,1,0:T(8,128)(2,1)S(1)} %get-tuple-element.71), channel_id=1, source_target_pairs={{0,16},{1,9},{2,18},{3,11},{4,20},{5,13},{6,22},{7,15},{8,24},{9,1... | collective-permute-start | bytes 3145736 | tf_op jit(solution)/shard_map/ppermute | solution.py:47
  82.0 1.3 collective-permute-start.16
  83.3 6.8 %project.5 = (bf16[384,8192]{1,0:T(8,128)(2,1)}, bf16[384,1024]{1,0:T(8,128)(2,1)}, f32[768,1024]{1,0:T(8,128)S(1)}) custom-call(s32[3]{0:T(128)S(1)} %pad_add_fusion.place.refs_0_, bf16[384,8192]{1,0:T(8,128)(2,1)S(1)} %copy-done.1, bf16[384,8192]{1,0:T(8,128)(2,1)} %collective-permute-done.other.refs_2_, ...), custom_call_target="tpu_custom_call", output_to_operand_aliasing={{0}: (7, {})} | custom-call | flops 3221225 | bytes 8388 | tf_op jit(solution)/shard_map/project/pallas_call | solution.py:216
  90.1 6.1 %collective-permute-done.13 = bf16[2,256,1024]{2,1,0:T(8,128)(2,1)} collective-permute-done((bf16[2,256,1024]{2,1,0:T(8,128)(2,1)S(1)}, bf16[2,256,1024]{2,1,0:T(8,128)(2,1)}, u32[]{:S(2)}, u32[]{:S(2)}) %collective-permute-start.13) | collective-permute-done | bytes 1048608 | tf_op jit(solution)/shard_map/ppermute | solution.py:47
  96.2 1.6 %add_convert_fusion.2 = bf16[2,256,1024]{2,1,0:T(8,128)(2,1)S(1)} fusion(bf16[2,256,1024]{2,1,0:T(8,128)(2,1)} %collective-permute-done.13, bf16[2,256,1024]{2,1,0:T(8,128)(2,1)S(1)} %add_convert_fusion.4), kind=kLoop, calls=%fused_computation.2 | loop fusion | flops 2097152 | bytes 3145728 | tf_op jit(solution)/shard_map/convert_element_type | solution.py:319
  97.9 1.7 %add_convert_fusion.1 = bf16[2,256,1024]{2,1,0:T(8,128)(2,1)S(1)} fusion(bf16[2,256,1024]{2,1,0:T(8,128)(2,1)} %collective-permute-done.14, bf16[2,256,1024]{2,1,0:T(8,128)(2,1)S(1)} %add_convert_fusion.5), kind=kLoop, calls=%fused_computation.1 | loop fusion | flops 2097152 | bytes 3145728 | tf_op jit(solution)/shard_map/convert_element_type | solution.py:319
  99.6 2.7 %collective-permute-start.19 = (bf16[2,256,1024]{2,1,0:T(8,128)(2,1)S(1)}, bf16[2,256,1024]{2,1,0:T(8,128)(2,1)S(1)}, u32[]{:S(2)}, u32[]{:S(2)}) collective-permute-start(bf16[2,256,1024]{2,1,0:T(8,128)(2,1)S(1)} %add_convert_fusion.1), channel_id=1, source_target_pairs={{0,2},{1,3},{2,0},{3,1},{4,6},{5,7},{6,4},{7,5},{8,10},{9,11},{10,... | collective-permute-start | bytes 3145736 | tf_op jit(solution)/shard_map/ppermute | solution.py:47
  102.3 0.9 collective-permute-start.18
  103.4 2.6 %collective-permute-start.17 = (bf16[2,1024,256]{2,1,0:T(8,128)(2,1)S(1)}, bf16[2,1024,256]{2,1,0:T(8,128)(2,1)S(1)}, u32[]{:S(2)}, u32[]{:S(2)}) collective-permute-start(bf16[2,1024,256]{2,1,0:T(8,128)(2,1)S(1)} %add.52.refs_4_), channel_id=1, source_target_pairs={{0,16},{1,9},{2,18},{3,11},{4,20},{5,13},{6,22},{7,15},{8,24},{9,1... | collective-permute-start | bytes 3145736 | tf_op jit(solution)/shard_map/ppermute | solution.py:47
  106.0 3.0 %collective-permute-done.16 = bf16[2,1024,256]{2,1,0:T(8,128)(2,1)S(1)} collective-permute-done((bf16[2,1024,256]{2,1,0:T(8,128)(2,1)S(1)}, bf16[2,1024,256]{2,1,0:T(8,128)(2,1)S(1)}, u32[]{:S(2)}, u32[]{:S(2)}) %collective-permute-start.16) | collective-permute-done | bytes 1048608 | tf_op jit(solution)/shard_map/ppermute | solution.py:47
  109.3 1.0 collective-permute-start.20
  110.8 15.6 %collective-permute-done.19 = bf16[2,256,1024]{2,1,0:T(8,128)(2,1)S(1)} collective-permute-done((bf16[2,256,1024]{2,1,0:T(8,128)(2,1)S(1)}, bf16[2,256,1024]{2,1,0:T(8,128)(2,1)S(1)}, u32[]{:S(2)}, u32[]{:S(2)}) %collective-permute-start.19) | collective-permute-done | bytes 1048608 | tf_op jit(solution)/shard_map/ppermute | solution.py:47
  126.3 0.6 add_bitcast_fusion
  127.0 1.5 collective-permute-start.22
  128.5 6.7 %project.6 = (bf16[384,8192]{1,0:T(8,128)(2,1)}, bf16[384,1024]{1,0:T(8,128)(2,1)S(1)}, f32[768,1024]{1,0:T(8,128)S(1)}) custom-call(s32[3]{0:T(128)S(1)} %pad_add_fusion.place.refs_0_, bf16[384,8192]{1,0:T(8,128)(2,1)S(1)} %copy-done.1, bf16[384,8192]{1,0:T(8,128)(2,1)} %collective-permute-done.other.refs_2_, ...), custom_call_target="tpu_custom_call", output_to_operand_aliasing={{0}: (7, {})} | custom-call | flops 3221225 | bytes 8388 | tf_op jit(solution)/shard_map/project/pallas_call | solution.py:216
  135.2 6.8 %project.7 = (bf16[384,8192]{1,0:T(8,128)(2,1)}, bf16[384,1024]{1,0:T(8,128)(2,1)S(1)}, f32[384,1024]{1,0:T(8,128)S(1)}, f32[384,1024]{1,0:T(8,128)S(1)}) custom-call(s32[3]{0:T(128)S(1)} %pad_add_fusion.place.refs_0_, bf16[384,8192]{1,0:T(8,128)(2,1)S(1)} %copy-done.1, ...), custom_call_target="tpu_custom_call", output_to_operand_aliasing={{0}: (7, {})} | custom-call | flops 3221225 | bytes 8388 | tf_op jit(solution)/shard_map/project/pallas_call | solution.py:216
  142.0 0.5 collective-permute-start.24
  142.6 0.4 collective-permute-start.26
  143.1 4.6 %collective-permute-done.24.refs_0_ = bf16[384,1024]{1,0:T(8,128)(2,1)S(1)} collective-permute-done((bf16[384,1024]{1,0:T(8,128)(2,1)S(1)}, bf16[384,1024]{1,0:T(8,128)(2,1)S(1)}, u32[]{:S(2)}, u32[]{:S(2)}) %collective-permute-start.24) | collective-permute-done | bytes 786464 | tf_op jit(solution)/shard_map/ppermute | solution.py:47
  147.9 0.9 collective-permute-done.26.refs_2_
  148.8 2.4 %lay.1.refs_6_ = bf16[384,8192]{1,0:T(8,128)(2,1)} custom-call(s32[3]{0:T(128)S(1)} %pad_add_fusion.place.refs_0_, bf16[384,1024]{1,0:T(8,128)(2,1)S(1)} %collective-permute-done.24.refs_0_, bf16[384,1024]{1,0:T(8,128)(2,1)S(1)} %collective-permute-done.25.refs_1_, ...), custom_call_target="tpu_custom_call", output_to_operand_aliasing={{}: (4, {})} | custom-call | bytes 4718 | tf_op jit(solution)/shard_map/lay/pallas_call | solution.py:255
  151.2 2.5 %finish.1 = (bf16[384,8192]{1,0:T(8,128)(2,1)}, bf16[384,1024]{1,0:T(8,128)(2,1)}, bf16[1024,256]{1,0:T(8,128)(2,1)}) custom-call(s32[3]{0:T(128)S(1)} %pad_add_fusion.place.refs_0_, bf16[384,1024]{1,0:T(8,128)(2,1)S(1)} %collective-permute-done.21.refs_1_, f32[384,1024]{1,0:T(8,128)S(1)} %get-tuple-element.82.refs_2_, ...), custom_call_target="tpu_custom_call", output_to_operand_aliasing={{0}: (6, {})} | custom-call | bytes 5505 | tf_op jit(solution)/shard_map/finish/pallas_call | solution.py:284
  (37 shorter events, 2.8 us)
Async XLA Ops:
  0.6 16.6 %copy-start.2 = (bf16[384,1024]{1,0:T(8,128)(2,1)S(1)}, bf16[384,1024]{1,0:T(8,128)(2,1)}, u32[]{:S(2)}) copy-start(bf16[384,1024]{1,0:T(8,128)(2,1)} %cot_mine.1) | copy-start | bytes 2359300
  0.6 16.6 %collective-permute-start = (bf16[384,8192]{1,0:T(8,128)(2,1)}, bf16[384,8192]{1,0:T(8,128)(2,1)}, u32[]{:S(2)}, u32[]{:S(2)}) collective-permute-start(bf16[384,8192]{1,0:T(8,128)(2,1)} %refs_1_.3), channel_id=1, source_target_pairs={{0,1},{1,0},{2,3},{3,2},{4,5},{5,4},{6,7},{7,6},{8,9},{9,8},{10,11... | collective-permute-start | bytes 18874376 | tf_op jit(solution)/shard_map/ppermute | solution.py:47
  1.2 16.1 %collective-permute-start.1 = (bf16[384,1024]{1,0:T(8,128)(2,1)}, bf16[384,1024]{1,0:T(8,128)(2,1)S(1)}, u32[]{:S(2)}, u32[]{:S(2)}) collective-permute-start(bf16[384,1024]{1,0:T(8,128)(2,1)} %cot_mine.1), channel_id=1, source_target_pairs={{0,1},{1,0},{2,3},{3,2},{4,5},{5,4},{6,7},{7,6},{8,9},{9,8},{10,11... | collective-permute-start | bytes 2359304 | tf_op jit(solution)/shard_map/ppermute | solution.py:47
  1.2 10.3 %collective-permute-start.4 = (bf16[1024,256]{1,0:T(8,128)(2,1)}, bf16[1024,256]{1,0:T(8,128)(2,1)S(1)}, u32[]{:S(2)}, u32[]{:S(2)}) collective-permute-start(bf16[1024,256]{1,0:T(8,128)(2,1)} %param.5), channel_id=1, source_target_pairs={{0,8},{1,17},{2,10},{3,19},{4,12},{5,21},{6,14},{7,23},{8,0},{9,25... | collective-permute-start | bytes 1572872 | tf_op jit(solution)/shard_map/ppermute | solution.py:47
  12.7 24.7 %collective-permute-start.5 = (bf16[2,1024,256]{2,1,0:T(8,128)(2,1)S(1)}, bf16[2,1024,256]{2,1,0:T(8,128)(2,1)S(1)}, u32[]{:S(2)}, u32[]{:S(2)}) collective-permute-start(bf16[2,1024,256]{2,1,0:T(8,128)(2,1)S(1)} %pad_maximum_fusion.refs_4_), channel_id=1, source_target_pairs={{0,2},{1,3},{2,0},{3,1},{4,6},{5,7},{6,4},{7,5},{8,10},{9,11},{10,... | collective-permute-start | bytes 3145736 | tf_op jit(solution)/shard_map/ppermute | solution.py:47
  14.9 22.5 %collective-permute-start.6 = (bf16[2,1024,256]{2,1,0:T(8,128)(2,1)S(1)}, bf16[2,1024,256]{2,1,0:T(8,128)(2,1)S(1)}, u32[]{:S(2)}, u32[]{:S(2)}) collective-permute-start(bf16[2,1024,256]{2,1,0:T(8,128)(2,1)S(1)} %pad_maximum_fusion.refs_4_), channel_id=1, source_target_pairs={{2,4},{3,5},{4,2},{5,3},{10,12},{11,13},{12,10},{13,11},{18,20},{1... | collective-permute-start | bytes 3145736 | tf_op jit(solution)/shard_map/ppermute | solution.py:47
  15.6 21.8 %collective-permute-start.7 = (bf16[2,1024,256]{2,1,0:T(8,128)(2,1)S(1)}, bf16[2,1024,256]{2,1,0:T(8,128)(2,1)S(1)}, u32[]{:S(2)}, u32[]{:S(2)}) collective-permute-start(bf16[2,1024,256]{2,1,0:T(8,128)(2,1)S(1)} %pad_maximum_fusion.refs_4_), channel_id=1, source_target_pairs={{0,16},{1,9},{2,18},{3,11},{4,20},{5,13},{6,22},{7,15},{8,24},{9,1... | collective-permute-start | bytes 3145736 | tf_op jit(solution)/shard_map/ppermute | solution.py:47
  17.2 2.8 %copy-start = (bf16[384,8192]{1,0:T(8,128)(2,1)S(1)}, bf16[384,8192]{1,0:T(8,128)(2,1)}, u32[]{:S(2)}) copy-start(bf16[384,8192]{1,0:T(8,128)(2,1)} %refs_1_.3) | copy-start | bytes 18874372
  20.0 5.1 %copy-start.1 = (bf16[384,8192]{1,0:T(8,128)(2,1)S(1)}, bf16[384,8192]{1,0:T(8,128)(2,1)}, u32[]{:S(2)}) copy-start(bf16[384,8192]{1,0:T(8,128)(2,1)} %refs_1_.3) | copy-start | bytes 18874372
  24.5 17.2 %collective-permute-start.8 = (bf16[2,256,1024]{2,1,0:T(8,128)(2,1)S(1)}, bf16[2,256,1024]{2,1,0:T(8,128)(2,1)S(1)}, u32[]{:S(2)}, u32[]{:S(2)}) collective-permute-start(bf16[2,256,1024]{2,1,0:T(8,128)(2,1)S(1)} %get-tuple-element.56), channel_id=1, source_target_pairs={{0,16},{1,9},{2,18},{3,11},{4,20},{5,13},{6,22},{7,15},{8,24},{9,1... | collective-permute-start | bytes 3145736 | tf_op jit(solution)/shard_map/ppermute | solution.py:47
  33.8 19.2 %collective-permute-start.2 = (bf16[2,256,1024]{2,1,0:T(8,128)(2,1)S(1)}, bf16[2,256,1024]{2,1,0:T(8,128)(2,1)S(1)}, u32[]{:S(2)}, u32[]{:S(2)}) collective-permute-start(bf16[2,256,1024]{2,1,0:T(8,128)(2,1)S(1)} %get-tuple-element.50), channel_id=1, source_target_pairs={{0,16},{1,9},{2,18},{3,11},{4,20},{5,13},{6,22},{7,15},{8,24},{9,1... | collective-permute-start | bytes 3145736 | tf_op jit(solution)/shard_map/ppermute | solution.py:47
  42.2 26.6 %collective-permute-start.9 = (bf16[2,256,1024]{2,1,0:T(8,128)(2,1)S(1)}, bf16[2,256,1024]{2,1,0:T(8,128)(2,1)}, u32[]{:S(2)}, u32[]{:S(2)}) collective-permute-start(bf16[2,256,1024]{2,1,0:T(8,128)(2,1)S(1)} %add_convert_fusion.4), channel_id=1, source_target_pairs={{0,2},{1,3},{6,4},{7,5},{8,10},{9,11},{14,12},{15,13},{16,18},{17,... | collective-permute-start | bytes 3145736 | tf_op jit(solution)/shard_map/ppermute | solution.py:47
  49.4 21.0 %collective-permute-start.12 = (bf16[2,1024,256]{2,1,0:T(8,128)(2,1)S(1)}, bf16[2,1024,256]{2,1,0:T(8,128)(2,1)S(1)}, u32[]{:S(2)}, u32[]{:S(2)}) collective-permute-start(bf16[2,1024,256]{2,1,0:T(8,128)(2,1)S(1)} %collective-permute-done.5.refs_1_.refs_4_), channel_id=1, source_target_pairs={{0,16},{1,9},{2,18},{3,11},{4,20},{5,13},{6,22},{7,15},{8,24},{9,1... | collective-permute-start | bytes 3145736 | tf_op jit(solution)/shard_map/ppermute | solution.py:47
  50.9 19.5 %collective-permute-start.10 = (bf16[2,1024,256]{2,1,0:T(8,128)(2,1)S(1)}, bf16[2,1024,256]{2,1,0:T(8,128)(2,1)S(1)}, u32[]{:S(2)}, u32[]{:S(2)}) collective-permute-start(bf16[2,1024,256]{2,1,0:T(8,128)(2,1)S(1)} %collective-permute-done.5.refs_1_.refs_4_), channel_id=1, source_target_pairs={{2,4},{3,5},{4,2},{5,3},{10,12},{11,13},{12,10},{13,11},{18,20},{1... | collective-permute-start | bytes 3145736 | tf_op jit(solution)/shard_map/ppermute | solution.py:47
  51.6 24.2 %collective-permute-start.11 = (bf16[2,1024,256]{2,1,0:T(8,128)(2,1)S(1)}, bf16[2,1024,256]{2,1,0:T(8,128)(2,1)S(1)}, u32[]{:S(2)}, u32[]{:S(2)}) collective-permute-start(bf16[2,1024,256]{2,1,0:T(8,128)(2,1)S(1)} %collective-permute-done.6.refs_2_), channel_id=1, source_target_pairs={{2,0},{3,1},{4,6},{5,7},{10,8},{11,9},{12,14},{13,15},{18,16},{19,... | collective-permute-start | bytes 3145736 | tf_op jit(solution)/shard_map/ppermute | solution.py:47
  53.4 26.6 %collective-permute-start.3 = (bf16[2,256,1024]{2,1,0:T(8,128)(2,1)S(1)}, bf16[2,256,1024]{2,1,0:T(8,128)(2,1)S(1)}, u32[]{:S(2)}, u32[]{:S(2)}) collective-permute-start(bf16[2,256,1024]{2,1,0:T(8,128)(2,1)S(1)} %get-tuple-element.51), channel_id=1, source_target_pairs={{0,16},{1,9},{2,18},{3,11},{4,20},{5,13},{6,22},{7,15},{8,24},{9,1... | collective-permute-start | bytes 3145736 | tf_op jit(solution)/shard_map/ppermute | solution.py:47
  75.8 7.5 %copy-start.3 = (bf16[2,1024,256]{2,1,0:T(8,128)(2,1)}, bf16[2,1024,256]{2,1,0:T(8,128)(2,1)S(1)}, u32[]{:S(2)}) copy-start(bf16[2,1024,256]{2,1,0:T(8,128)(2,1)S(1)} %collective-permute-done.11) | copy-start | bytes 3145732
  75.8 20.4 %collective-permute-start.13 = (bf16[2,256,1024]{2,1,0:T(8,128)(2,1)S(1)}, bf16[2,256,1024]{2,1,0:T(8,128)(2,1)}, u32[]{:S(2)}, u32[]{:S(2)}) collective-permute-start(bf16[2,256,1024]{2,1,0:T(8,128)(2,1)S(1)} %add_convert_fusion.6), channel_id=1, source_target_pairs={{0,2},{1,3},{6,4},{7,5},{8,10},{9,11},{14,12},{15,13},{16,18},{17,... | collective-permute-start | bytes 3145736 | tf_op jit(solution)/shard_map/ppermute | solution.py:47
  78.2 19.6 %collective-permute-start.14 = (bf16[2,256,1024]{2,1,0:T(8,128)(2,1)S(1)}, bf16[2,256,1024]{2,1,0:T(8,128)(2,1)}, u32[]{:S(2)}, u32[]{:S(2)}) collective-permute-start(bf16[2,256,1024]{2,1,0:T(8,128)(2,1)S(1)} %add_convert_fusion.3), channel_id=1, source_target_pairs={{2,4},{3,5},{4,2},{5,3},{10,12},{11,13},{12,10},{13,11},{18,20},{1... | collective-permute-start | bytes 3145736 | tf_op jit(solution)/shard_map/ppermute | solution.py:47
  80.4 30.0 %collective-permute-start.15 = (bf16[2,256,1024]{2,1,0:T(8,128)(2,1)S(1)}, bf16[2,256,1024]{2,1,0:T(8,128)(2,1)S(1)}, u32[]{:S(2)}, u32[]{:S(2)}) collective-permute-start(bf16[2,256,1024]{2,1,0:T(8,128)(2,1)S(1)} %get-tuple-element.71), channel_id=1, source_target_pairs={{0,16},{1,9},{2,18},{3,11},{4,20},{5,13},{6,22},{7,15},{8,24},{9,1... | collective-permute-start | bytes 3145736 | tf_op jit(solution)/shard_map/ppermute | solution.py:47
  82.0 27.1 %collective-permute-start.16 = (bf16[2,1024,256]{2,1,0:T(8,128)(2,1)S(1)}, bf16[2,1024,256]{2,1,0:T(8,128)(2,1)S(1)}, u32[]{:S(2)}, u32[]{:S(2)}) collective-permute-start(bf16[2,1024,256]{2,1,0:T(8,128)(2,1)S(1)} %collective-permute-done.10), channel_id=1, source_target_pairs={{2,0},{3,1},{4,6},{5,7},{10,8},{11,9},{12,14},{13,15},{18,16},{19,... | collective-permute-start | bytes 3145736 | tf_op jit(solution)/shard_map/ppermute | solution.py:47
  97.9 5.3 %copy-start.4 = (bf16[2,1024,256]{2,1,0:T(8,128)(2,1)S(1)}, bf16[2,1024,256]{2,1,0:T(8,128)(2,1)}, u32[]{:S(2)}) copy-start(bf16[2,1024,256]{2,1,0:T(8,128)(2,1)} %copy-done.3) | copy-start | bytes 3145732
  99.6 26.7 %collective-permute-start.19 = (bf16[2,256,1024]{2,1,0:T(8,128)(2,1)S(1)}, bf16[2,256,1024]{2,1,0:T(8,128)(2,1)S(1)}, u32[]{:S(2)}, u32[]{:S(2)}) collective-permute-start(bf16[2,256,1024]{2,1,0:T(8,128)(2,1)S(1)} %add_convert_fusion.1), channel_id=1, source_target_pairs={{0,2},{1,3},{2,0},{3,1},{4,6},{5,7},{6,4},{7,5},{8,10},{9,11},{10,... | collective-permute-start | bytes 3145736 | tf_op jit(solution)/shard_map/ppermute | solution.py:47
  102.3 24.1 %collective-permute-start.18 = (bf16[2,256,1024]{2,1,0:T(8,128)(2,1)S(1)}, bf16[2,256,1024]{2,1,0:T(8,128)(2,1)S(1)}, u32[]{:S(2)}, u32[]{:S(2)}) collective-permute-start(bf16[2,256,1024]{2,1,0:T(8,128)(2,1)S(1)} %add_convert_fusion.2), channel_id=1, source_target_pairs={{2,4},{3,5},{4,2},{5,3},{10,12},{11,13},{12,10},{13,11},{18,20},{1... | collective-permute-start | bytes 3145736 | tf_op jit(solution)/shard_map/ppermute | solution.py:47
  103.4 25.0 %collective-permute-start.17 = (bf16[2,1024,256]{2,1,0:T(8,128)(2,1)S(1)}, bf16[2,1024,256]{2,1,0:T(8,128)(2,1)S(1)}, u32[]{:S(2)}, u32[]{:S(2)}) collective-permute-start(bf16[2,1024,256]{2,1,0:T(8,128)(2,1)S(1)} %add.52.refs_4_), channel_id=1, source_target_pairs={{0,16},{1,9},{2,18},{3,11},{4,20},{5,13},{6,22},{7,15},{8,24},{9,1... | collective-permute-start | bytes 3145736 | tf_op jit(solution)/shard_map/ppermute | solution.py:47
  109.3 25.8 %collective-permute-start.20 = (bf16[2,1024,256]{2,1,0:T(8,128)(2,1)S(1)}, bf16[2,1024,256]{2,1,0:T(8,128)(2,1)S(1)}, u32[]{:S(2)}, u32[]{:S(2)}) collective-permute-start(bf16[2,1024,256]{2,1,0:T(8,128)(2,1)S(1)} %add.51.refs_4_), channel_id=1, source_target_pairs={{0,16},{1,9},{2,18},{3,11},{4,20},{5,13},{6,22},{7,15},{8,24},{9,1... | collective-permute-start | bytes 3145736 | tf_op jit(solution)/shard_map/ppermute | solution.py:47
  127.0 15.0 %collective-permute-start.22 = (bf16[256,1024]{1,0:T(8,128)(2,1)S(1)}, bf16[256,1024]{1,0:T(8,128)(2,1)S(1)}, u32[]{:S(2)}, u32[]{:S(2)}) collective-permute-start(bf16[256,1024]{1,0:T(8,128)(2,1)S(1)} %get-tuple-element.90), channel_id=1, source_target_pairs={{0,8},{1,17},{2,10},{3,19},{4,12},{5,21},{6,14},{7,23},{8,0},{9,25... | collective-permute-start | bytes 1572872 | tf_op jit(solution)/shard_map/ppermute | solution.py:47
  142.0 9.2 %collective-permute-start.23 = (f32[384,1024]{1,0:T(8,128)S(1)}, f32[384,1024]{1,0:T(8,128)S(1)}, u32[]{:S(2)}, u32[]{:S(2)}) collective-permute-start(f32[384,1024]{1,0:T(8,128)S(1)} %get-tuple-element.84), channel_id=1, source_target_pairs={{0,1},{1,0},{2,3},{3,2},{4,5},{5,4},{6,7},{7,6},{8,9},{9,8},{10,11... | collective-permute-start | bytes 4718600 | tf_op jit(solution)/shard_map/ppermute | solution.py:47
  142.0 5.7 %collective-permute-start.24 = (bf16[384,1024]{1,0:T(8,128)(2,1)S(1)}, bf16[384,1024]{1,0:T(8,128)(2,1)S(1)}, u32[]{:S(2)}, u32[]{:S(2)}) collective-permute-start(bf16[384,1024]{1,0:T(8,128)(2,1)S(1)} %get-tuple-element.59), channel_id=1, source_target_pairs={{0,1},{1,0},{2,3},{3,2},{4,5},{5,4},{6,7},{7,6},{8,9},{9,8},{10,11... | collective-permute-start | bytes 2359304 | tf_op jit(solution)/shard_map/ppermute | solution.py:47
  142.5 5.4 %collective-permute-start.25 = (bf16[384,1024]{1,0:T(8,128)(2,1)}, bf16[384,1024]{1,0:T(8,128)(2,1)S(1)}, u32[]{:S(2)}, u32[]{:S(2)}) collective-permute-start(bf16[384,1024]{1,0:T(8,128)(2,1)} %get-tuple-element.68), channel_id=1, source_target_pairs={{0,1},{1,0},{2,3},{3,2},{4,5},{5,4},{6,7},{7,6},{8,9},{9,8},{10,11... | collective-permute-start | bytes 2359304 | tf_op jit(solution)/shard_map/ppermute | solution.py:47
  142.6 6.2 %collective-permute-start.26 = (bf16[384,1024]{1,0:T(8,128)(2,1)S(1)}, bf16[384,1024]{1,0:T(8,128)(2,1)S(1)}, u32[]{:S(2)}, u32[]{:S(2)}) collective-permute-start(bf16[384,1024]{1,0:T(8,128)(2,1)S(1)} %get-tuple-element.77), channel_id=1, source_target_pairs={{0,1},{1,0},{2,3},{3,2},{4,5},{5,4},{6,7},{7,6},{8,9},{9,8},{10,11... | collective-permute-start | bytes 2359304 | tf_op jit(solution)/shard_map/ppermute | solution.py:47
  143.0 8.2 %collective-permute-start.21 = (bf16[384,1024]{1,0:T(8,128)(2,1)S(1)}, bf16[384,1024]{1,0:T(8,128)(2,1)S(1)}, u32[]{:S(2)}, u32[]{:S(2)}) collective-permute-start(bf16[384,1024]{1,0:T(8,128)(2,1)S(1)} %get-tuple-element.81), channel_id=1, source_target_pairs={{0,1},{1,0},{2,3},{3,2},{4,5},{5,4},{6,7},{7,6},{8,9},{9,8},{10,11... | collective-permute-start | bytes 2359304 | tf_op jit(solution)/shard_map/ppermute | solution.py:47

commit v14 on v13

--- a/solution.py
+++ b/solution.py
@@ -377,6 +377,7 @@
         two_b,
         (whole, None, keys),
     )
+    sum_one = after(sum_one, out2)
     last = [
         sum0[a].astype(F32) + sum_mid[a].astype(F32) + sum_one[a].astype(F32) for a in (0, 1)
     ]

time: 154 us -> 150 us (0.974)
  waiting for transfers between devices: 55.8 us -> 47.6 us
  other arithmetic: 8.97 us -> 12.5 us
    ppermute x27, waiting for transfers between devices: 55.8 us -> 47.6 us  [sent(): return lax.ppermute(array, AXES, pairs)]
  transfers between devices with their start and end apart: 27 -> 27, of which waited for: 12 -> 13; matrix products, arithmetic and copies ran while one was open for 6% -> 8% of each run, Pallas kernels for 28% -> 29%
where the time goes in v14:
time: 150 us; the launch traced here: 148 us
  waiting for transfers between devices  47.6 us (32%)
  Pallas kernels  45.9 us (31%)
  starting transfers between devices  38.6 us (26%)
  other arithmetic  12.5 us (8%)
  local copies, waits for them, and re-layouts  2.79 us (2%)
    ppermute x27, waiting for transfers between devices, sent(): return lax.ppermute(array, AXES, pairs)  47.6 us
    ppermute x27, starting transfers between devices, sent(): return lax.ppermute(array, AXES, pairs)  38.6 us
    pallas_call x4, Pallas kernels, projected(): pl.pallas_call(lambda *refs: project_kernel(*refs, first=first, last=last...  26.7 us
    pallas_call x1, Pallas kernels, terms(): pl.pallas_call(term_kernel, grid_spec=pltpu.PrefetchScalarGridSpec(num_sc...  8.66 us
    convert_element_type x7, other arithmetic, added(): return total.astype(BF16)  7.72 us
    pallas_call x1, Pallas kernels, first_terms(): pl.pallas_call(first_term_kernel, grid_spec=pltpu.PrefetchScalarGridSpec(...  4.49 us
  transfers between devices with their start and end apart: 27, of which 13 were waited for; matrix products, arithmetic and copies ran while one was open for 8% of the time, Pallas kernels for 29%

profile of v14, /device:TPU:0, one launch (start us, length us, event | category | flops | bytes accessed | tf_op | source)
XLA Modules:
  0.0 148.3 jit_solution(7245733130448959280)
XLA Ops:
  1.2 2.9 %collective-permute-start.4 = (bf16[1024,256]{1,0:T(8,128)(2,1)}, bf16[1024,256]{1,0:T(8,128)(2,1)S(1)}, u32[]{:S(2)}, u32[]{:S(2)}) collective-permute-start(bf16[1024,256]{1,0:T(8,128)(2,1)} %param.5), channel_id=1, source_target_pairs={{0,8},{1,17},{2,10},{3,19},{4,12},{5,21},{6,14},{7,23},{8,0},{9,25... | collective-permute-start | bytes 1572872 | tf_op jit(solution)/shard_map/ppermute | solution.py:47
  4.2 7.4 %collective-permute-done.4 = bf16[1024,256]{1,0:T(8,128)(2,1)S(1)} collective-permute-done((bf16[1024,256]{1,0:T(8,128)(2,1)}, bf16[1024,256]{1,0:T(8,128)(2,1)S(1)}, u32[]{:S(2)}, u32[]{:S(2)}) %collective-permute-start.4) | collective-permute-done | bytes 524320 | tf_op jit(solution)/shard_map/ppermute | solution.py:47
  11.5 1.1 pad_maximum_fusion.refs_4_
  12.7 2.2 %collective-permute-start.5 = (bf16[2,1024,256]{2,1,0:T(8,128)(2,1)S(1)}, bf16[2,1024,256]{2,1,0:T(8,128)(2,1)S(1)}, u32[]{:S(2)}, u32[]{:S(2)}) collective-permute-start(bf16[2,1024,256]{2,1,0:T(8,128)(2,1)S(1)} %pad_maximum_fusion.refs_4_), channel_id=1, source_target_pairs={{0,2},{1,3},{2,0},{3,1},{4,6},{5,7},{6,4},{7,5},{8,10},{9,11},{10,... | collective-permute-start | bytes 3145736 | tf_op jit(solution)/shard_map/ppermute | solution.py:47
  14.9 1.5 %collective-permute-start.7 = (bf16[2,1024,256]{2,1,0:T(8,128)(2,1)S(1)}, bf16[2,1024,256]{2,1,0:T(8,128)(2,1)S(1)}, u32[]{:S(2)}, u32[]{:S(2)}) collective-permute-start(bf16[2,1024,256]{2,1,0:T(8,128)(2,1)S(1)} %pad_maximum_fusion.refs_4_), channel_id=1, source_target_pairs={{0,16},{1,9},{2,18},{3,11},{4,20},{5,13},{6,22},{7,15},{8,24},{9,1... | collective-permute-start | bytes 3145736 | tf_op jit(solution)/shard_map/ppermute | solution.py:47
  16.4 0.7 collective-permute-start.6
  17.2 2.8 %copy-done = bf16[384,8192]{1,0:T(8,128)(2,1)S(1)} copy-done((bf16[384,8192]{1,0:T(8,128)(2,1)S(1)}, bf16[384,8192]{1,0:T(8,128)(2,1)}, u32[]{:S(2)}) %copy-start) | copy-done | bytes 6291480
  20.0 4.5 %terms.2 = (bf16[2,256,1024]{2,1,0:T(8,128)(2,1)S(1)}, bf16[2,256,1024]{2,1,0:T(8,128)(2,1)S(1)}, bf16[768,1024]{1,0:T(8,128)(2,1)S(1)}, bf16[1024,768]{1,0:T(8,128)(2,1)S(1)}) custom-call(s32[3]{0:T(128)S(1)} %pad_add_fusion.place.refs_0_, bf16[384,8192]{1,0:T(8,128)(2,1)S(1)} %copy-done, bf16[384,8192]{1,0:T(8,128)(2,1)} %collective-permute-done.other.refs_2_, ...), custom_call_target="tpu_custom_call" | custom-call | flops 1610612 | bytes 5767 | tf_op jit(solution)/shard_map/terms/pallas_call | solution.py:107
  24.5 0.6 collective-permute-start.8
  25.1 8.7 %terms.3 = (bf16[2,256,1024]{2,1,0:T(8,128)(2,1)S(1)}, bf16[2,256,1024]{2,1,0:T(8,128)(2,1)S(1)}, bf16[2,256,1024]{2,1,0:T(8,128)(2,1)S(1)}, bf16[2,256,1024]{2,...) custom-call(s32[3]{0:T(128)S(1)} %pad_add_fusion.place.refs_0_, ...), custom_call_target="tpu_custom_call" | custom-call | flops 4831838 | bytes 17301 | tf_op jit(solution)/shard_map/terms/pallas_call | solution.py:149
  33.7 1.6 %collective-permute-start.2 = (bf16[2,256,1024]{2,1,0:T(8,128)(2,1)S(1)}, bf16[2,256,1024]{2,1,0:T(8,128)(2,1)S(1)}, u32[]{:S(2)}, u32[]{:S(2)}) collective-permute-start(bf16[2,256,1024]{2,1,0:T(8,128)(2,1)S(1)} %get-tuple-element.51), channel_id=1, source_target_pairs={{0,16},{1,9},{2,18},{3,11},{4,20},{5,13},{6,22},{7,15},{8,24},{9,1... | collective-permute-start | bytes 3145736 | tf_op jit(solution)/shard_map/ppermute | solution.py:47
  35.3 2.1 %collective-permute-done.5.refs_1_.refs_4_ = bf16[2,1024,256]{2,1,0:T(8,128)(2,1)S(1)} collective-permute-done((bf16[2,1024,256]{2,1,0:T(8,128)(2,1)S(1)}, bf16[2,1024,256]{2,1,0:T(8,128)(2,1)S(1)}, u32[]{:S(2)}, u32[]{:S(2)}) %collective-permute-start.5) | collective-permute-done | bytes 1048608 | tf_op jit(solution)/shard_map/ppermute | solution.py:47
  37.4 1.1 gate.1.refs_0_
  38.5 2.4 %collective-permute-done.8 = bf16[2,256,1024]{2,1,0:T(8,128)(2,1)S(1)} collective-permute-done((bf16[2,256,1024]{2,1,0:T(8,128)(2,1)S(1)}, bf16[2,256,1024]{2,1,0:T(8,128)(2,1)S(1)}, u32[]{:S(2)}, u32[]{:S(2)}) %collective-permute-start.8) | collective-permute-done | bytes 1048608 | tf_op jit(solution)/shard_map/ppermute | solution.py:47
  41.4 6.6 %collective-permute-start.9 = (bf16[2,256,1024]{2,1,0:T(8,128)(2,1)S(1)}, bf16[2,256,1024]{2,1,0:T(8,128)(2,1)}, u32[]{:S(2)}, u32[]{:S(2)}) collective-permute-start(bf16[2,256,1024]{2,1,0:T(8,128)(2,1)S(1)} %add_convert_fusion.4), channel_id=1, source_target_pairs={{0,2},{1,3},{6,4},{7,5},{8,10},{9,11},{14,12},{15,13},{16,18},{17,... | collective-permute-start | bytes 3145736 | tf_op jit(solution)/shard_map/ppermute | solution.py:47
  48.0 0.7 collective-permute-start.10
  48.7 1.3 collective-permute-start.11
  50.0 1.6 %collective-permute-start.12 = (bf16[2,1024,256]{2,1,0:T(8,128)(2,1)S(1)}, bf16[2,1024,256]{2,1,0:T(8,128)(2,1)S(1)}, u32[]{:S(2)}, u32[]{:S(2)}) collective-permute-start(bf16[2,1024,256]{2,1,0:T(8,128)(2,1)S(1)} %collective-permute-done.5.refs_1_.refs_4_), channel_id=1, source_target_pairs={{0,16},{1,9},{2,18},{3,11},{4,20},{5,13},{6,22},{7,15},{8,24},{9,1... | collective-permute-start | bytes 3145736 | tf_op jit(solution)/shard_map/ppermute | solution.py:47
  52.6 1.6 %collective-permute-start.3 = (bf16[2,256,1024]{2,1,0:T(8,128)(2,1)S(1)}, bf16[2,256,1024]{2,1,0:T(8,128)(2,1)}, u32[]{:S(2)}, u32[]{:S(2)}) collective-permute-start(bf16[2,256,1024]{2,1,0:T(8,128)(2,1)S(1)} %get-tuple-element.52), channel_id=1, source_target_pairs={{0,16},{1,9},{2,18},{3,11},{4,20},{5,13},{6,22},{7,15},{8,24},{9,1... | collective-permute-start | bytes 3145736 | tf_op jit(solution)/shard_map/ppermute | solution.py:47
  54.2 6.5 %project.4 = (bf16[384,8192]{1,0:T(8,128)(2,1)}, bf16[384,1024]{1,0:T(8,128)(2,1)S(1)}, f32[768,1024]{1,0:T(8,128)S(1)}) custom-call(s32[3]{0:T(128)S(1)} %gate.1.refs_0_, bf16[384,8192]{1,0:T(8,128)(2,1)S(1)} %copy-done.1, bf16[384,8192]{1,0:T(8,128)(2,1)} %collective-permute-done.other.refs_2_, bf16[768,1024]{1,0:T(8,128)(2,1)S(1)} %get-tuple-element.59.refs_3_, ...), custom_call_target="tpu_custom_call" | custom-call | flops 3221225 | bytes 8388 | tf_op jit(solution)/shard_map/project/pallas_call | solution.py:216
  60.7 6.8 %collective-permute-done.9 = bf16[2,256,1024]{2,1,0:T(8,128)(2,1)} collective-permute-done((bf16[2,256,1024]{2,1,0:T(8,128)(2,1)S(1)}, bf16[2,256,1024]{2,1,0:T(8,128)(2,1)}, u32[]{:S(2)}, u32[]{:S(2)}) %collective-permute-start.9) | collective-permute-done | bytes 1048608 | tf_op jit(solution)/shard_map/ppermute | solution.py:47
  67.5 1.6 %add_convert_fusion.3 = bf16[2,256,1024]{2,1,0:T(8,128)(2,1)S(1)} fusion(bf16[2,256,1024]{2,1,0:T(8,128)(2,1)} %collective-permute-done.9, bf16[2,256,1024]{2,1,0:T(8,128)(2,1)S(1)} %add_convert_fusion.6), kind=kLoop, calls=%fused_computation.3 | loop fusion | flops 2097152 | bytes 3145728 | tf_op jit(solution)/shard_map/convert_element_type | solution.py:319
  69.1 4.3 %collective-permute-done.11 = bf16[2,1024,256]{2,1,0:T(8,128)(2,1)S(1)} collective-permute-done((bf16[2,1024,256]{2,1,0:T(8,128)(2,1)S(1)}, bf16[2,1024,256]{2,1,0:T(8,128)(2,1)S(1)}, u32[]{:S(2)}, u32[]{:S(2)}) %collective-permute-start.11) | collective-permute-done | bytes 1048608 | tf_op jit(solution)/shard_map/ppermute | solution.py:47
  73.4 2.5 %collective-permute-start.13 = (bf16[2,256,1024]{2,1,0:T(8,128)(2,1)S(1)}, bf16[2,256,1024]{2,1,0:T(8,128)(2,1)}, u32[]{:S(2)}, u32[]{:S(2)}) collective-permute-start(bf16[2,256,1024]{2,1,0:T(8,128)(2,1)S(1)} %add_convert_fusion.6), channel_id=1, source_target_pairs={{0,2},{1,3},{6,4},{7,5},{8,10},{9,11},{14,12},{15,13},{16,18},{17,... | collective-permute-start | bytes 3145736 | tf_op jit(solution)/shard_map/ppermute | solution.py:47
  75.9 1.7 %collective-permute-start.14 = (bf16[2,256,1024]{2,1,0:T(8,128)(2,1)S(1)}, bf16[2,256,1024]{2,1,0:T(8,128)(2,1)}, u32[]{:S(2)}, u32[]{:S(2)}) collective-permute-start(bf16[2,256,1024]{2,1,0:T(8,128)(2,1)S(1)} %add_convert_fusion.3), channel_id=1, source_target_pairs={{2,4},{3,5},{4,2},{5,3},{10,12},{11,13},{12,10},{13,11},{18,20},{1... | collective-permute-start | bytes 3145736 | tf_op jit(solution)/shard_map/ppermute | solution.py:47
  77.6 1.6 %add_convert_fusion.5 = bf16[2,256,1024]{2,1,0:T(8,128)(2,1)S(1)} fusion(bf16[2,256,1024]{2,1,0:T(8,128)(2,1)} %collective-permute-done.3, bf16[2,256,1024]{2,1,0:T(8,128)(2,1)S(1)} %get-tuple-element.48), kind=kLoop, calls=%fused_computation.5 | loop fusion | flops 2097152 | bytes 3145728 | tf_op jit(solution)/shard_map/convert_element_type | solution.py:319
  79.2 2.7 %collective-permute-start.15 = (bf16[2,256,1024]{2,1,0:T(8,128)(2,1)S(1)}, bf16[2,256,1024]{2,1,0:T(8,128)(2,1)S(1)}, u32[]{:S(2)}, u32[]{:S(2)}) collective-permute-start(bf16[2,256,1024]{2,1,0:T(8,128)(2,1)S(1)} %get-tuple-element.72), channel_id=1, source_target_pairs={{0,16},{1,9},{2,18},{3,11},{4,20},{5,13},{6,22},{7,15},{8,24},{9,1... | collective-permute-start | bytes 3145736 | tf_op jit(solution)/shard_map/ppermute | solution.py:47
  81.9 1.3 collective-permute-start.16
  83.6 6.7 %project.5 = (bf16[384,8192]{1,0:T(8,128)(2,1)}, bf16[384,1024]{1,0:T(8,128)(2,1)S(1)}, f32[768,1024]{1,0:T(8,128)S(1)}) custom-call(s32[3]{0:T(128)S(1)} %pad_add_fusion.place.refs_0_, bf16[384,8192]{1,0:T(8,128)(2,1)S(1)} %copy-done.1, bf16[384,8192]{1,0:T(8,128)(2,1)} %collective-permute-done.other.refs_2_, ...), custom_call_target="tpu_custom_call", output_to_operand_aliasing={{0}: (7, {})} | custom-call | flops 3221225 | bytes 8388 | tf_op jit(solution)/shard_map/project/pallas_call | solution.py:216
  90.2 4.2 %collective-permute-done.13 = bf16[2,256,1024]{2,1,0:T(8,128)(2,1)} collective-permute-done((bf16[2,256,1024]{2,1,0:T(8,128)(2,1)S(1)}, bf16[2,256,1024]{2,1,0:T(8,128)(2,1)}, u32[]{:S(2)}, u32[]{:S(2)}) %collective-permute-start.13) | collective-permute-done | bytes 1048608 | tf_op jit(solution)/shard_map/ppermute | solution.py:47
  94.4 1.6 %add_convert_fusion.2 = bf16[2,256,1024]{2,1,0:T(8,128)(2,1)S(1)} fusion(bf16[2,256,1024]{2,1,0:T(8,128)(2,1)} %collective-permute-done.13, bf16[2,256,1024]{2,1,0:T(8,128)(2,1)S(1)} %add_convert_fusion.4), kind=kLoop, calls=%fused_computation.2 | loop fusion | flops 2097152 | bytes 3145728 | tf_op jit(solution)/shard_map/convert_element_type | solution.py:319
  96.1 1.6 %add_convert_fusion.1 = bf16[2,256,1024]{2,1,0:T(8,128)(2,1)S(1)} fusion(bf16[2,256,1024]{2,1,0:T(8,128)(2,1)} %collective-permute-done.14, bf16[2,256,1024]{2,1,0:T(8,128)(2,1)S(1)} %add_convert_fusion.5), kind=kLoop, calls=%fused_computation.1 | loop fusion | flops 2097152 | bytes 3145728 | tf_op jit(solution)/shard_map/convert_element_type | solution.py:319
  97.7 2.7 %collective-permute-start.19 = (bf16[2,256,1024]{2,1,0:T(8,128)(2,1)S(1)}, bf16[2,256,1024]{2,1,0:T(8,128)(2,1)S(1)}, u32[]{:S(2)}, u32[]{:S(2)}) collective-permute-start(bf16[2,256,1024]{2,1,0:T(8,128)(2,1)S(1)} %add_convert_fusion.1), channel_id=1, source_target_pairs={{0,2},{1,3},{2,0},{3,1},{4,6},{5,7},{6,4},{7,5},{8,10},{9,11},{10,... | collective-permute-start | bytes 3145736 | tf_op jit(solution)/shard_map/ppermute | solution.py:47
  100.4 1.7 %collective-permute-start.18 = (bf16[2,256,1024]{2,1,0:T(8,128)(2,1)S(1)}, bf16[2,256,1024]{2,1,0:T(8,128)(2,1)}, u32[]{:S(2)}, u32[]{:S(2)}) collective-permute-start(bf16[2,256,1024]{2,1,0:T(8,128)(2,1)S(1)} %add_convert_fusion.2), channel_id=1, source_target_pairs={{2,4},{3,5},{4,2},{5,3},{10,12},{11,13},{12,10},{13,11},{18,20},{1... | collective-permute-start | bytes 3145736 | tf_op jit(solution)/shard_map/ppermute | solution.py:47
  102.1 6.7 %collective-permute-done.16 = bf16[2,1024,256]{2,1,0:T(8,128)(2,1)} collective-permute-done((bf16[2,1024,256]{2,1,0:T(8,128)(2,1)S(1)}, bf16[2,1024,256]{2,1,0:T(8,128)(2,1)}, u32[]{:S(2)}, u32[]{:S(2)}) %collective-permute-start.16) | collective-permute-done | bytes 1048608 | tf_op jit(solution)/shard_map/ppermute | solution.py:47
  108.8 1.5 %add.51.refs_4_ = bf16[2,1024,256]{2,1,0:T(8,128)(2,1)S(1)} add(bf16[2,1024,256]{2,1,0:T(8,128)(2,1)S(1)} %collective-permute-done.6.refs_2_, bf16[2,1024,256]{2,1,0:T(8,128)(2,1)} %collective-permute-done.16) | non-fusion elementwise | flops 524288 | bytes 3145728 | tf_op jit(solution)/shard_map/add | solution.py:367
  110.3 1.3 collective-permute-start.20
  112.0 6.7 %project.6 = (bf16[384,8192]{1,0:T(8,128)(2,1)}, bf16[384,1024]{1,0:T(8,128)(2,1)S(1)}, f32[768,1024]{1,0:T(8,128)S(1)}) custom-call(s32[3]{0:T(128)S(1)} %pad_add_fusion.place.refs_0_, bf16[384,8192]{1,0:T(8,128)(2,1)S(1)} %copy-done.1, bf16[384,8192]{1,0:T(8,128)(2,1)} %collective-permute-done.other.refs_2_, ...), custom_call_target="tpu_custom_call", output_to_operand_aliasing={{0}: (7, {})} | custom-call | flops 3221225 | bytes 8388 | tf_op jit(solution)/shard_map/project/pallas_call | solution.py:216
  118.7 6.8 %collective-permute-done.19 = bf16[2,256,1024]{2,1,0:T(8,128)(2,1)S(1)} collective-permute-done((bf16[2,256,1024]{2,1,0:T(8,128)(2,1)S(1)}, bf16[2,256,1024]{2,1,0:T(8,128)(2,1)S(1)}, u32[]{:S(2)}, u32[]{:S(2)}) %collective-permute-start.19) | collective-permute-done | bytes 1048608 | tf_op jit(solution)/shard_map/ppermute | solution.py:47
  125.5 1.8 %add_bitcast_fusion = (f32[256,1024]{1,0:T(8,128)S(1)}, bf16[256,1024]{1,0:T(8,128)(2,1)S(1)}) fusion(bf16[2,256,1024]{2,1,0:T(8,128)(2,1)} %collective-permute-done.18, bf16[2,256,1024]{2,1,0:T(8,128)(2,1)S(1)} %add_convert_fusion, bf16[2,256,1024]{2,1,0:T(8,128)(2,1)S(1)} %collective-permute-done.19), kind=kLoop, calls=%fused_computation.8 | loop fusion | flops 2883584 | bytes 4718592 | tf_op jit(solution)/shard_map/add | solution.py:382
  127.3 1.8 %collective-permute-start.22 = (bf16[256,1024]{1,0:T(8,128)(2,1)S(1)}, bf16[256,1024]{1,0:T(8,128)(2,1)S(1)}, u32[]{:S(2)}, u32[]{:S(2)}) collective-permute-start(bf16[256,1024]{1,0:T(8,128)(2,1)S(1)} %get-tuple-element.92), channel_id=1, source_target_pairs={{0,8},{1,17},{2,10},{3,19},{4,12},{5,21},{6,14},{7,23},{8,0},{9,25... | collective-permute-start | bytes 1572872 | tf_op jit(solution)/shard_map/ppermute | solution.py:47
  129.1 6.8 %project.7 = (bf16[384,8192]{1,0:T(8,128)(2,1)}, bf16[384,1024]{1,0:T(8,128)(2,1)S(1)}, f32[384,1024]{1,0:T(8,128)S(1)}, f32[384,1024]{1,0:T(8,128)S(1)}) custom-call(s32[3]{0:T(128)S(1)} %pad_add_fusion.place.refs_0_, bf16[384,8192]{1,0:T(8,128)(2,1)S(1)} %copy-done.1, ...), custom_call_target="tpu_custom_call", output_to_operand_aliasing={{0}: (7, {})} | custom-call | flops 3221225 | bytes 8388 | tf_op jit(solution)/shard_map/project/pallas_call | solution.py:216
  135.9 0.6 collective-permute-done.22.refs_5_
  137.6 3.5 %collective-permute-done.24.refs_0_ = bf16[384,1024]{1,0:T(8,128)(2,1)S(1)} collective-permute-done((bf16[384,1024]{1,0:T(8,128)(2,1)S(1)}, bf16[384,1024]{1,0:T(8,128)(2,1)S(1)}, u32[]{:S(2)}, u32[]{:S(2)}) %collective-permute-start.24) | collective-permute-done | bytes 786464 | tf_op jit(solution)/shard_map/ppermute | solution.py:47
  141.1 1.1 collective-permute-done.25.refs_1_
  142.2 1.1 collective-permute-done.26.refs_2_
  143.3 2.4 %lay.1.refs_6_ = bf16[384,8192]{1,0:T(8,128)(2,1)} custom-call(s32[3]{0:T(128)S(1)} %pad_add_fusion.place.refs_0_, bf16[384,1024]{1,0:T(8,128)(2,1)S(1)} %collective-permute-done.24.refs_0_, bf16[384,1024]{1,0:T(8,128)(2,1)S(1)} %collective-permute-done.25.refs_1_, ...), custom_call_target="tpu_custom_call", output_to_operand_aliasing={{}: (4, {})} | custom-call | bytes 4718 | tf_op jit(solution)/shard_map/lay/pallas_call | solution.py:255
  145.8 2.5 %finish.1 = (bf16[384,8192]{1,0:T(8,128)(2,1)}, bf16[384,1024]{1,0:T(8,128)(2,1)}, bf16[1024,256]{1,0:T(8,128)(2,1)}) custom-call(s32[3]{0:T(128)S(1)} %pad_add_fusion.place.refs_0_, bf16[384,1024]{1,0:T(8,128)(2,1)S(1)} %collective-permute-done.21.refs_1_, f32[384,1024]{1,0:T(8,128)S(1)} %get-tuple-element.84.refs_2_, ...), custom_call_target="tpu_custom_call", output_to_operand_aliasing={{0}: (6, {})} | custom-call | bytes 5505 | tf_op jit(solution)/shard_map/finish/pallas_call | solution.py:284
  (33 shorter events, 3.9 us)
Async XLA Ops:
  0.6 16.6 %copy-start.2 = (bf16[384,1024]{1,0:T(8,128)(2,1)S(1)}, bf16[384,1024]{1,0:T(8,128)(2,1)}, u32[]{:S(2)}) copy-start(bf16[384,1024]{1,0:T(8,128)(2,1)} %cot_mine.1) | copy-start | bytes 2359300
  0.6 16.5 %collective-permute-start = (bf16[384,8192]{1,0:T(8,128)(2,1)}, bf16[384,8192]{1,0:T(8,128)(2,1)}, u32[]{:S(2)}, u32[]{:S(2)}) collective-permute-start(bf16[384,8192]{1,0:T(8,128)(2,1)} %refs_1_.3), channel_id=1, source_target_pairs={{0,1},{1,0},{2,3},{3,2},{4,5},{5,4},{6,7},{7,6},{8,9},{9,8},{10,11... | collective-permute-start | bytes 18874376 | tf_op jit(solution)/shard_map/ppermute | solution.py:47
  1.2 16.0 %collective-permute-start.1 = (bf16[384,1024]{1,0:T(8,128)(2,1)}, bf16[384,1024]{1,0:T(8,128)(2,1)S(1)}, u32[]{:S(2)}, u32[]{:S(2)}) collective-permute-start(bf16[384,1024]{1,0:T(8,128)(2,1)} %cot_mine.1), channel_id=1, source_target_pairs={{0,1},{1,0},{2,3},{3,2},{4,5},{5,4},{6,7},{7,6},{8,9},{9,8},{10,11... | collective-permute-start | bytes 2359304 | tf_op jit(solution)/shard_map/ppermute | solution.py:47
  1.2 10.3 %collective-permute-start.4 = (bf16[1024,256]{1,0:T(8,128)(2,1)}, bf16[1024,256]{1,0:T(8,128)(2,1)S(1)}, u32[]{:S(2)}, u32[]{:S(2)}) collective-permute-start(bf16[1024,256]{1,0:T(8,128)(2,1)} %param.5), channel_id=1, source_target_pairs={{0,8},{1,17},{2,10},{3,19},{4,12},{5,21},{6,14},{7,23},{8,0},{9,25... | collective-permute-start | bytes 1572872 | tf_op jit(solution)/shard_map/ppermute | solution.py:47
  12.7 24.7 %collective-permute-start.5 = (bf16[2,1024,256]{2,1,0:T(8,128)(2,1)S(1)}, bf16[2,1024,256]{2,1,0:T(8,128)(2,1)S(1)}, u32[]{:S(2)}, u32[]{:S(2)}) collective-permute-start(bf16[2,1024,256]{2,1,0:T(8,128)(2,1)S(1)} %pad_maximum_fusion.refs_4_), channel_id=1, source_target_pairs={{0,2},{1,3},{2,0},{3,1},{4,6},{5,7},{6,4},{7,5},{8,10},{9,11},{10,... | collective-permute-start | bytes 3145736 | tf_op jit(solution)/shard_map/ppermute | solution.py:47
  14.9 22.5 %collective-permute-start.7 = (bf16[2,1024,256]{2,1,0:T(8,128)(2,1)S(1)}, bf16[2,1024,256]{2,1,0:T(8,128)(2,1)S(1)}, u32[]{:S(2)}, u32[]{:S(2)}) collective-permute-start(bf16[2,1024,256]{2,1,0:T(8,128)(2,1)S(1)} %pad_maximum_fusion.refs_4_), channel_id=1, source_target_pairs={{0,16},{1,9},{2,18},{3,11},{4,20},{5,13},{6,22},{7,15},{8,24},{9,1... | collective-permute-start | bytes 3145736 | tf_op jit(solution)/shard_map/ppermute | solution.py:47
  16.4 21.0 %collective-permute-start.6 = (bf16[2,1024,256]{2,1,0:T(8,128)(2,1)S(1)}, bf16[2,1024,256]{2,1,0:T(8,128)(2,1)S(1)}, u32[]{:S(2)}, u32[]{:S(2)}) collective-permute-start(bf16[2,1024,256]{2,1,0:T(8,128)(2,1)S(1)} %pad_maximum_fusion.refs_4_), channel_id=1, source_target_pairs={{2,4},{3,5},{4,2},{5,3},{10,12},{11,13},{12,10},{13,11},{18,20},{1... | collective-permute-start | bytes 3145736 | tf_op jit(solution)/shard_map/ppermute | solution.py:47
  17.2 2.8 %copy-start = (bf16[384,8192]{1,0:T(8,128)(2,1)S(1)}, bf16[384,8192]{1,0:T(8,128)(2,1)}, u32[]{:S(2)}) copy-start(bf16[384,8192]{1,0:T(8,128)(2,1)} %refs_1_.3) | copy-start | bytes 18874372
  20.0 5.1 %copy-start.1 = (bf16[384,8192]{1,0:T(8,128)(2,1)S(1)}, bf16[384,8192]{1,0:T(8,128)(2,1)}, u32[]{:S(2)}) copy-start(bf16[384,8192]{1,0:T(8,128)(2,1)} %refs_1_.3) | copy-start | bytes 18874372
  24.5 16.5 %collective-permute-start.8 = (bf16[2,256,1024]{2,1,0:T(8,128)(2,1)S(1)}, bf16[2,256,1024]{2,1,0:T(8,128)(2,1)S(1)}, u32[]{:S(2)}, u32[]{:S(2)}) collective-permute-start(bf16[2,256,1024]{2,1,0:T(8,128)(2,1)S(1)} %get-tuple-element.57), channel_id=1, source_target_pairs={{0,16},{1,9},{2,18},{3,11},{4,20},{5,13},{6,22},{7,15},{8,24},{9,1... | collective-permute-start | bytes 3145736 | tf_op jit(solution)/shard_map/ppermute | solution.py:47
  33.7 18.5 %collective-permute-start.2 = (bf16[2,256,1024]{2,1,0:T(8,128)(2,1)S(1)}, bf16[2,256,1024]{2,1,0:T(8,128)(2,1)S(1)}, u32[]{:S(2)}, u32[]{:S(2)}) collective-permute-start(bf16[2,256,1024]{2,1,0:T(8,128)(2,1)S(1)} %get-tuple-element.51), channel_id=1, source_target_pairs={{0,16},{1,9},{2,18},{3,11},{4,20},{5,13},{6,22},{7,15},{8,24},{9,1... | collective-permute-start | bytes 3145736 | tf_op jit(solution)/shard_map/ppermute | solution.py:47
  41.4 26.1 %collective-permute-start.9 = (bf16[2,256,1024]{2,1,0:T(8,128)(2,1)S(1)}, bf16[2,256,1024]{2,1,0:T(8,128)(2,1)}, u32[]{:S(2)}, u32[]{:S(2)}) collective-permute-start(bf16[2,256,1024]{2,1,0:T(8,128)(2,1)S(1)} %add_convert_fusion.4), channel_id=1, source_target_pairs={{0,2},{1,3},{6,4},{7,5},{8,10},{9,11},{14,12},{15,13},{16,18},{17,... | collective-permute-start | bytes 3145736 | tf_op jit(solution)/shard_map/ppermute | solution.py:47
  48.0 21.1 %collective-permute-start.10 = (bf16[2,1024,256]{2,1,0:T(8,128)(2,1)S(1)}, bf16[2,1024,256]{2,1,0:T(8,128)(2,1)S(1)}, u32[]{:S(2)}, u32[]{:S(2)}) collective-permute-start(bf16[2,1024,256]{2,1,0:T(8,128)(2,1)S(1)} %collective-permute-done.5.refs_1_.refs_4_), channel_id=1, source_target_pairs={{2,4},{3,5},{4,2},{5,3},{10,12},{11,13},{12,10},{13,11},{18,20},{1... | collective-permute-start | bytes 3145736 | tf_op jit(solution)/shard_map/ppermute | solution.py:47
  48.7 24.7 %collective-permute-start.11 = (bf16[2,1024,256]{2,1,0:T(8,128)(2,1)S(1)}, bf16[2,1024,256]{2,1,0:T(8,128)(2,1)S(1)}, u32[]{:S(2)}, u32[]{:S(2)}) collective-permute-start(bf16[2,1024,256]{2,1,0:T(8,128)(2,1)S(1)} %collective-permute-done.6.refs_2_), channel_id=1, source_target_pairs={{2,0},{3,1},{4,6},{5,7},{10,8},{11,9},{12,14},{13,15},{18,16},{19,... | collective-permute-start | bytes 3145736 | tf_op jit(solution)/shard_map/ppermute | solution.py:47
  50.0 23.4 %collective-permute-start.12 = (bf16[2,1024,256]{2,1,0:T(8,128)(2,1)S(1)}, bf16[2,1024,256]{2,1,0:T(8,128)(2,1)S(1)}, u32[]{:S(2)}, u32[]{:S(2)}) collective-permute-start(bf16[2,1024,256]{2,1,0:T(8,128)(2,1)S(1)} %collective-permute-done.5.refs_1_.refs_4_), channel_id=1, source_target_pairs={{0,16},{1,9},{2,18},{3,11},{4,20},{5,13},{6,22},{7,15},{8,24},{9,1... | collective-permute-start | bytes 3145736 | tf_op jit(solution)/shard_map/ppermute | solution.py:47
  52.6 25.0 %collective-permute-start.3 = (bf16[2,256,1024]{2,1,0:T(8,128)(2,1)S(1)}, bf16[2,256,1024]{2,1,0:T(8,128)(2,1)}, u32[]{:S(2)}, u32[]{:S(2)}) collective-permute-start(bf16[2,256,1024]{2,1,0:T(8,128)(2,1)S(1)} %get-tuple-element.52), channel_id=1, source_target_pairs={{0,16},{1,9},{2,18},{3,11},{4,20},{5,13},{6,22},{7,15},{8,24},{9,1... | collective-permute-start | bytes 3145736 | tf_op jit(solution)/shard_map/ppermute | solution.py:47
  73.4 21.0 %collective-permute-start.13 = (bf16[2,256,1024]{2,1,0:T(8,128)(2,1)S(1)}, bf16[2,256,1024]{2,1,0:T(8,128)(2,1)}, u32[]{:S(2)}, u32[]{:S(2)}) collective-permute-start(bf16[2,256,1024]{2,1,0:T(8,128)(2,1)S(1)} %add_convert_fusion.6), channel_id=1, source_target_pairs={{0,2},{1,3},{6,4},{7,5},{8,10},{9,11},{14,12},{15,13},{16,18},{17,... | collective-permute-start | bytes 3145736 | tf_op jit(solution)/shard_map/ppermute | solution.py:47
  75.9 20.1 %collective-permute-start.14 = (bf16[2,256,1024]{2,1,0:T(8,128)(2,1)S(1)}, bf16[2,256,1024]{2,1,0:T(8,128)(2,1)}, u32[]{:S(2)}, u32[]{:S(2)}) collective-permute-start(bf16[2,256,1024]{2,1,0:T(8,128)(2,1)S(1)} %add_convert_fusion.3), channel_id=1, source_target_pairs={{2,4},{3,5},{4,2},{5,3},{10,12},{11,13},{12,10},{13,11},{18,20},{1... | collective-permute-start | bytes 3145736 | tf_op jit(solution)/shard_map/ppermute | solution.py:47
  79.2 32.4 %collective-permute-start.15 = (bf16[2,256,1024]{2,1,0:T(8,128)(2,1)S(1)}, bf16[2,256,1024]{2,1,0:T(8,128)(2,1)S(1)}, u32[]{:S(2)}, u32[]{:S(2)}) collective-permute-start(bf16[2,256,1024]{2,1,0:T(8,128)(2,1)S(1)} %get-tuple-element.72), channel_id=1, source_target_pairs={{0,16},{1,9},{2,18},{3,11},{4,20},{5,13},{6,22},{7,15},{8,24},{9,1... | collective-permute-start | bytes 3145736 | tf_op jit(solution)/shard_map/ppermute | solution.py:47
  81.9 26.9 %collective-permute-start.16 = (bf16[2,1024,256]{2,1,0:T(8,128)(2,1)S(1)}, bf16[2,1024,256]{2,1,0:T(8,128)(2,1)}, u32[]{:S(2)}, u32[]{:S(2)}) collective-permute-start(bf16[2,1024,256]{2,1,0:T(8,128)(2,1)S(1)} %collective-permute-done.10), channel_id=1, source_target_pairs={{2,0},{3,1},{4,6},{5,7},{10,8},{11,9},{12,14},{13,15},{18,16},{19,... | collective-permute-start | bytes 3145736 | tf_op jit(solution)/shard_map/ppermute | solution.py:47
  83.5 28.6 %collective-permute-start.17 = (bf16[2,1024,256]{2,1,0:T(8,128)(2,1)S(1)}, bf16[2,1024,256]{2,1,0:T(8,128)(2,1)S(1)}, u32[]{:S(2)}, u32[]{:S(2)}) collective-permute-start(bf16[2,1024,256]{2,1,0:T(8,128)(2,1)S(1)} %add.52.refs_4_), channel_id=1, source_target_pairs={{0,16},{1,9},{2,18},{3,11},{4,20},{5,13},{6,22},{7,15},{8,24},{9,1... | collective-permute-start | bytes 3145736 | tf_op jit(solution)/shard_map/ppermute | solution.py:47
  97.7 27.8 %collective-permute-start.19 = (bf16[2,256,1024]{2,1,0:T(8,128)(2,1)S(1)}, bf16[2,256,1024]{2,1,0:T(8,128)(2,1)S(1)}, u32[]{:S(2)}, u32[]{:S(2)}) collective-permute-start(bf16[2,256,1024]{2,1,0:T(8,128)(2,1)S(1)} %add_convert_fusion.1), channel_id=1, source_target_pairs={{0,2},{1,3},{2,0},{3,1},{4,6},{5,7},{6,4},{7,5},{8,10},{9,11},{10,... | collective-permute-start | bytes 3145736 | tf_op jit(solution)/shard_map/ppermute | solution.py:47
  100.4 25.1 %collective-permute-start.18 = (bf16[2,256,1024]{2,1,0:T(8,128)(2,1)S(1)}, bf16[2,256,1024]{2,1,0:T(8,128)(2,1)}, u32[]{:S(2)}, u32[]{:S(2)}) collective-permute-start(bf16[2,256,1024]{2,1,0:T(8,128)(2,1)S(1)} %add_convert_fusion.2), channel_id=1, source_target_pairs={{2,4},{3,5},{4,2},{5,3},{10,12},{11,13},{12,10},{13,11},{18,20},{1... | collective-permute-start | bytes 3145736 | tf_op jit(solution)/shard_map/ppermute | solution.py:47
  110.3 18.8 %collective-permute-start.20 = (bf16[2,1024,256]{2,1,0:T(8,128)(2,1)S(1)}, bf16[2,1024,256]{2,1,0:T(8,128)(2,1)S(1)}, u32[]{:S(2)}, u32[]{:S(2)}) collective-permute-start(bf16[2,1024,256]{2,1,0:T(8,128)(2,1)S(1)} %add.51.refs_4_), channel_id=1, source_target_pairs={{0,16},{1,9},{2,18},{3,11},{4,20},{5,13},{6,22},{7,15},{8,24},{9,1... | collective-permute-start | bytes 3145736 | tf_op jit(solution)/shard_map/ppermute | solution.py:47
  127.3 9.2 %collective-permute-start.22 = (bf16[256,1024]{1,0:T(8,128)(2,1)S(1)}, bf16[256,1024]{1,0:T(8,128)(2,1)S(1)}, u32[]{:S(2)}, u32[]{:S(2)}) collective-permute-start(bf16[256,1024]{1,0:T(8,128)(2,1)S(1)} %get-tuple-element.92), channel_id=1, source_target_pairs={{0,8},{1,17},{2,10},{3,19},{4,12},{5,21},{6,14},{7,23},{8,0},{9,25... | collective-permute-start | bytes 1572872 | tf_op jit(solution)/shard_map/ppermute | solution.py:47
  136.6 9.2 %collective-permute-start.23 = (f32[384,1024]{1,0:T(8,128)S(1)}, f32[384,1024]{1,0:T(8,128)S(1)}, u32[]{:S(2)}, u32[]{:S(2)}) collective-permute-start(f32[384,1024]{1,0:T(8,128)S(1)} %get-tuple-element.86), channel_id=1, source_target_pairs={{0,1},{1,0},{2,3},{3,2},{4,5},{5,4},{6,7},{7,6},{8,9},{9,8},{10,11... | collective-permute-start | bytes 4718600 | tf_op jit(solution)/shard_map/ppermute | solution.py:47
  136.6 4.5 %collective-permute-start.24 = (bf16[384,1024]{1,0:T(8,128)(2,1)S(1)}, bf16[384,1024]{1,0:T(8,128)(2,1)S(1)}, u32[]{:S(2)}, u32[]{:S(2)}) collective-permute-start(bf16[384,1024]{1,0:T(8,128)(2,1)S(1)} %get-tuple-element.60), channel_id=1, source_target_pairs={{0,1},{1,0},{2,3},{3,2},{4,5},{5,4},{6,7},{7,6},{8,9},{9,8},{10,11... | collective-permute-start | bytes 2359304 | tf_op jit(solution)/shard_map/ppermute | solution.py:47
  137.1 5.1 %collective-permute-start.25 = (bf16[384,1024]{1,0:T(8,128)(2,1)S(1)}, bf16[384,1024]{1,0:T(8,128)(2,1)S(1)}, u32[]{:S(2)}, u32[]{:S(2)}) collective-permute-start(bf16[384,1024]{1,0:T(8,128)(2,1)S(1)} %get-tuple-element.69), channel_id=1, source_target_pairs={{0,1},{1,0},{2,3},{3,2},{4,5},{5,4},{6,7},{7,6},{8,9},{9,8},{10,11... | collective-permute-start | bytes 2359304 | tf_op jit(solution)/shard_map/ppermute | solution.py:47
  137.1 6.3 %collective-permute-start.26 = (bf16[384,1024]{1,0:T(8,128)(2,1)S(1)}, bf16[384,1024]{1,0:T(8,128)(2,1)S(1)}, u32[]{:S(2)}, u32[]{:S(2)}) collective-permute-start(bf16[384,1024]{1,0:T(8,128)(2,1)S(1)} %get-tuple-element.78), channel_id=1, source_target_pairs={{0,1},{1,0},{2,3},{3,2},{4,5},{5,4},{6,7},{7,6},{8,9},{9,8},{10,11... | collective-permute-start | bytes 2359304 | tf_op jit(solution)/shard_map/ppermute | solution.py:47
  137.6 8.2 %collective-permute-start.21 = (bf16[384,1024]{1,0:T(8,128)(2,1)S(1)}, bf16[384,1024]{1,0:T(8,128)(2,1)S(1)}, u32[]{:S(2)}, u32[]{:S(2)}) collective-permute-start(bf16[384,1024]{1,0:T(8,128)(2,1)S(1)} %get-tuple-element.83), channel_id=1, source_target_pairs={{0,1},{1,0},{2,3},{3,2},{4,5},{5,4},{6,7},{7,6},{8,9},{9,8},{10,11... | collective-permute-start | bytes 2359304 | tf_op jit(solution)/shard_map/ppermute | solution.py:47

commit v15 on v12

--- a/solution.py
+++ b/solution.py
@@ -71,6 +71,27 @@
         cost_estimate=cost(0, GATE, 1),
         name="gate",
     )(place, *arrays)
+
+
+def pack_kernel(place, acts, out):
+    out[...] = acts[...]
+
+
+def packed(place, activations, rows):
+    tokens = activations.shape[0]
+    return pl.pallas_call(
+        pack_kernel,
+        grid_spec=pltpu.PrefetchScalarGridSpec(
+            num_scalar_prefetch=1,
+            grid=(1,),
+            in_specs=[pl.BlockSpec((tokens, rows), lambda r, s: (0, 2 * (s[0] ^ 3) + 1 - s[1]))],
+            out_specs=pl.BlockSpec((tokens, rows), lambda r, s: (0, 0)),
+        ),
+        out_shape=jax.ShapeDtypeStruct((tokens, rows), BF16),
+        compiler_params=pltpu.CompilerParams(vmem_limit_bytes=6 * MIB),
+        cost_estimate=cost(0, 4 * tokens * rows),
+        name="pack",
+    )(place, activations)
 
 
 def first_term_kernel(place, mine, other, cot_mine, cot_other, keep, send, cots, turned):
@@ -109,7 +130,7 @@
         grid_spec=pltpu.PrefetchScalarGridSpec(
             num_scalar_prefetch=1,
             grid=(2,),
-            in_specs=[mine, mine, held, held],
+            in_specs=[mine, pl.BlockSpec((tokens, part), lambda r, s: (0, r)), held, held],
             out_specs=[piece, piece, whole(2 * tokens, columns), whole(columns, 2 * tokens)],
         ),
         out_shape=[jax.ShapeDtypeStruct((2, cols, rows), BF16)] * 2
@@ -324,17 +345,22 @@
     tokens = activations.shape[0]
     place = jnp.stack([lax.axis_index(name) for name in ("chip", "core", "blk")]).astype(jnp.int32)
 
-    other, cot_other = sent(activations, SWAP), sent(cotangent, SWAP)
-    base = jnp.stack([kv_weight, sent(kv_weight, FLIP_A)])
-    one, mid = sent(base, PAIR), sent(base, MID)
+    other3 = sent(packed(place, activations, rows), SWAP)
+    other, cot_other = sent(after(activations, other3), SWAP), sent(cotangent, SWAP)
+    next_a = sent(kv_weight, FLIP_A)
+    base = jnp.stack([kv_weight, next_a])
+    one_near, mid_near = sent(kv_weight, PAIR), sent(kv_weight, MID)
+
+    keep3, send3, cots, turned = first_terms(
+        place, activations, other3, cotangent, cot_other, rows
+    )
+    got3 = sent(send3, FLIP_B)
+    next_a = after(next_a, one_near, mid_near, keep3)
+    one = jnp.stack([one_near, sent(next_a, PAIR)])
+    mid = jnp.stack([mid_near, sent(next_a, MID)])
     base_b = sent(base, FLIP_B)
-
-    keep3, send3, cots, turned = first_terms(
-        place, activations, other, cotangent, cot_other, rows
-    )
-    got3 = sent(send3, FLIP_B)
     keep2, keep1, keep0, send2, send1, send0 = terms(place, activations, other, turned, rows)
-    first = gate(place, after(one, keep0), mid, base_b)
+    first = gate(place, got3, after(one, keep0), mid)
 
     sum3 = added(after(keep3, first), got3)
     far = sent(sum3, IN)

time: 142 us -> 149 us (1.049)
  waiting for transfers between devices: 44.8 us -> 54.2 us
  local copies, waits for them, and re-layouts: 2.79 us -> 0.01 us
  other arithmetic: 9.87 us -> 8.08 us
    ppermute x27 -> x30, waiting for transfers between devices: 44.8 us -> 54.2 us  [sent(): return lax.ppermute(array, AXES, pairs)]
    unnamed x6 -> x4, local copies, waits for them, and re-layouts: 2.79 us -> 0.01 us
    pallas_call x0 -> x1, Pallas kernels: none -> 1.73 us  [packed(): pl.pallas_call(pack_kernel, grid_spec=pltpu.PrefetchScalarGridSpec(num_sc...]
    ppermute x27 -> x30, starting transfers between devices: 37.1 us -> 38.5 us  [sent(): return lax.ppermute(array, AXES, pairs)]
  transfers between devices with their start and end apart: 27 -> 30, of which waited for: 14 -> 13; matrix products, arithmetic and copies ran while one was open for 7% -> 5% of each run, Pallas kernels for 31% -> 29%
where the time goes in v15:
time: 149 us
  waiting for transfers between devices  54.2 us (36%)
  Pallas kernels  47.2 us (32%)
  starting transfers between devices  38.5 us (26%)
  other arithmetic  8.08 us (5%)
    ppermute x30, waiting for transfers between devices, sent(): return lax.ppermute(array, AXES, pairs)  54.2 us
    ppermute x30, starting transfers between devices, sent(): return lax.ppermute(array, AXES, pairs)  38.5 us
    pallas_call x4, Pallas kernels, projected(): pl.pallas_call(lambda *refs: project_kernel(*refs, first=first, last=last...  26.6 us
    pallas_call x1, Pallas kernels, terms(): pl.pallas_call(term_kernel, grid_spec=pltpu.PrefetchScalarGridSpec(num_sc...  8.61 us
    convert_element_type x7, other arithmetic, added(): return total.astype(BF16)  5.3 us
    pallas_call x1, Pallas kernels, first_terms(): pl.pallas_call(first_term_kernel, grid_spec=pltpu.PrefetchScalarGridSpec(...  4.22 us
  transfers between devices with their start and end apart: 30, of which 13 were waited for; matrix products, arithmetic and copies ran while one was open for 5% of the time, Pallas kernels for 29%

profile of v15, /device:TPU:0, one launch (start us, length us, event | category | flops | bytes accessed | tf_op | source)
XLA Modules:
  0.0 148.9 jit_solution(5571373680499240242)
XLA Ops:
  0.7 1.7 %pack.1 = bf16[384,1024]{1,0:T(8,128)(2,1)S(1)} custom-call(s32[3]{0:T(128)S(1)} %pad_add_fusion.place.refs_0_, bf16[384,8192]{1,0:T(8,128)(2,1)} %refs_1_.3), custom_call_target="tpu_custom_call" | custom-call | bytes 1572 | tf_op jit(solution)/shard_map/pack/pallas_call | solution.py:82
  2.4 0.5 collective-permute-start
  3.0 1.9 %collective-permute-done.other = bf16[384,1024]{1,0:T(8,128)(2,1)S(1)} collective-permute-done((bf16[384,1024]{1,0:T(8,128)(2,1)S(1)}, bf16[384,1024]{1,0:T(8,128)(2,1)S(1)}, u32[]{:S(2)}, u32[]{:S(2)}) %collective-permute-start) | collective-permute-done | bytes 786464 | tf_op jit(solution)/shard_map/ppermute | solution.py:47
  5.4 2.9 %collective-permute-start.6 = (bf16[1024,256]{1,0:T(8,128)(2,1)S(1)}, bf16[1024,256]{1,0:T(8,128)(2,1)S(1)}, u32[]{:S(2)}, u32[]{:S(2)}) collective-permute-start(bf16[1024,256]{1,0:T(8,128)(2,1)S(1)} %copy-done.1), channel_id=1, source_target_pairs={{0,2},{1,3},{2,0},{3,1},{4,6},{5,7},{6,4},{7,5},{8,10},{9,11},{10,... | collective-permute-start | bytes 1572872 | tf_op jit(solution)/shard_map/ppermute | solution.py:47
  8.3 1.5 %collective-permute-start.7 = (bf16[1024,256]{1,0:T(8,128)(2,1)S(1)}, bf16[1024,256]{1,0:T(8,128)(2,1)S(1)}, u32[]{:S(2)}, u32[]{:S(2)}) collective-permute-start(bf16[1024,256]{1,0:T(8,128)(2,1)S(1)} %copy-done.1), channel_id=1, source_target_pairs={{0,8},{1,17},{2,10},{3,19},{4,12},{5,21},{6,14},{7,23},{8,0},{9,25... | collective-permute-start | bytes 1572872 | tf_op jit(solution)/shard_map/ppermute | solution.py:47
  9.8 0.7 collective-permute-start.8
  10.5 1.5 %collective-permute-done.2.cot_other = bf16[384,1024]{1,0:T(8,128)(2,1)S(1)} collective-permute-done((bf16[384,1024]{1,0:T(8,128)(2,1)S(1)}, bf16[384,1024]{1,0:T(8,128)(2,1)S(1)}, u32[]{:S(2)}, u32[]{:S(2)}) %collective-permute-start.2) | collective-permute-done | bytes 786464 | tf_op jit(solution)/shard_map/ppermute | solution.py:47
  12.1 4.2 %terms.2 = (bf16[2,256,1024]{2,1,0:T(8,128)(2,1)S(1)}, bf16[2,256,1024]{2,1,0:T(8,128)(2,1)S(1)}, bf16[768,1024]{1,0:T(8,128)(2,1)S(1)}, bf16[1024,768]{1,0:T(8,128)(2,1)S(1)}) custom-call(s32[3]{0:T(128)S(1)} %pad_add_fusion.place.refs_0_, bf16[384,8192]{1,0:T(8,128)(2,1)} %refs_1_.3, bf16[384,1024]{1,0:T(8,128)(2,1)S(1)} %collective-permute-done.other, ...), custom_call_target="tpu_custom_call" | custom-call | flops 1610612 | bytes 5767 | tf_op jit(solution)/shard_map/terms/pallas_call | solution.py:128
  16.3 2.7 %collective-permute-start.5 = (bf16[2,256,1024]{2,1,0:T(8,128)(2,1)S(1)}, bf16[2,256,1024]{2,1,0:T(8,128)(2,1)S(1)}, u32[]{:S(2)}, u32[]{:S(2)}) collective-permute-start(bf16[2,256,1024]{2,1,0:T(8,128)(2,1)S(1)} %get-tuple-element.57), channel_id=1, source_target_pairs={{0,16},{1,9},{2,18},{3,11},{4,20},{5,13},{6,22},{7,15},{8,24},{9,1... | collective-permute-start | bytes 3145736 | tf_op jit(solution)/shard_map/ppermute | solution.py:47
  19.0 1.6 %collective-permute-done.6 = bf16[1024,256]{1,0:T(8,128)(2,1)S(1)} collective-permute-done((bf16[1024,256]{1,0:T(8,128)(2,1)S(1)}, bf16[1024,256]{1,0:T(8,128)(2,1)S(1)}, u32[]{:S(2)}, u32[]{:S(2)}) %collective-permute-start.6) | collective-permute-done | bytes 524320 | tf_op jit(solution)/shard_map/ppermute | solution.py:47
  20.6 6.0 %collective-permute-start.9 = (bf16[1024,256]{1,0:T(8,128)(2,1)S(1)}, bf16[1024,256]{1,0:T(8,128)(2,1)S(1)}, u32[]{:S(2)}, u32[]{:S(2)}) collective-permute-start(bf16[1024,256]{1,0:T(8,128)(2,1)S(1)} %collective-permute-done.7), channel_id=1, source_target_pairs={{0,2},{1,3},{2,0},{3,1},{4,6},{5,7},{6,4},{7,5},{8,10},{9,11},{10,... | collective-permute-start | bytes 1572872 | tf_op jit(solution)/shard_map/ppermute | solution.py:47
  26.6 0.7 collective-permute-start.10
  27.3 8.6 %terms.3 = (bf16[2,256,1024]{2,1,0:T(8,128)(2,1)S(1)}, bf16[2,256,1024]{2,1,0:T(8,128)(2,1)S(1)}, bf16[2,256,1024]{2,1,0:T(8,128)(2,1)S(1)}, bf16[2,256,1024]{2,...) custom-call(s32[3]{0:T(128)S(1)} %pad_add_fusion.place.refs_0_, ...), custom_call_target="tpu_custom_call" | custom-call | flops 4831838 | bytes 17301 | tf_op jit(solution)/shard_map/terms/pallas_call | solution.py:170
  35.9 0.6 collective-permute-start.3
  36.6 1.6 %collective-permute-start.11 = (bf16[2,1024,256]{2,1,0:T(8,128)(2,1)S(1)}, bf16[2,1024,256]{2,1,0:T(8,128)(2,1)S(1)}, u32[]{:S(2)}, u32[]{:S(2)}) collective-permute-start(bf16[2,1024,256]{2,1,0:T(8,128)(2,1)S(1)} %pad_maximum_fusion.2.refs_4_), channel_id=1, source_target_pairs={{0,16},{1,9},{2,18},{3,11},{4,20},{5,13},{6,22},{7,15},{8,24},{9,1... | collective-permute-start | bytes 3145736 | tf_op jit(solution)/shard_map/ppermute | solution.py:47
  38.4 1.1 gate.1.refs_0_
  39.9 5.9 %collective-permute-start.12 = (bf16[2,256,1024]{2,1,0:T(8,128)(2,1)S(1)}, bf16[2,256,1024]{2,1,0:T(8,128)(2,1)}, u32[]{:S(2)}, u32[]{:S(2)}) collective-permute-start(bf16[2,256,1024]{2,1,0:T(8,128)(2,1)S(1)} %add_convert_fusion.4), channel_id=1, source_target_pairs={{0,2},{1,3},{6,4},{7,5},{8,10},{9,11},{14,12},{15,13},{16,18},{17,... | collective-permute-start | bytes 3145736 | tf_op jit(solution)/shard_map/ppermute | solution.py:47
  46.3 0.7 collective-permute-start.13
  47.0 3.7 %collective-permute-done.3 = bf16[2,256,1024]{2,1,0:T(8,128)(2,1)S(1)} collective-permute-done((bf16[2,256,1024]{2,1,0:T(8,128)(2,1)S(1)}, bf16[2,256,1024]{2,1,0:T(8,128)(2,1)S(1)}, u32[]{:S(2)}, u32[]{:S(2)}) %collective-permute-start.3) | collective-permute-done | bytes 1048608 | tf_op jit(solution)/shard_map/ppermute | solution.py:47
  50.7 1.3 collective-permute-start.14
  52.5 9.5 %collective-permute-done.11.refs_5_ = bf16[2,1024,256]{2,1,0:T(8,128)(2,1)S(1)} collective-permute-done((bf16[2,1024,256]{2,1,0:T(8,128)(2,1)S(1)}, bf16[2,1024,256]{2,1,0:T(8,128)(2,1)S(1)}, u32[]{:S(2)}, u32[]{:S(2)}) %collective-permute-start.11) | collective-permute-done | bytes 1048608 | tf_op jit(solution)/shard_map/ppermute | solution.py:47
  62.0 0.5 collective-permute-start.4
  62.5 6.4 %project.4 = (bf16[384,8192]{1,0:T(8,128)(2,1)}, bf16[384,1024]{1,0:T(8,128)(2,1)S(1)}, f32[768,1024]{1,0:T(8,128)S(1)}) custom-call(s32[3]{0:T(128)S(1)} %gate.1.refs_0_, bf16[384,8192]{1,0:T(8,128)(2,1)} %refs_1_.3, bf16[384,8192]{1,0:T(8,128)(2,1)S(1)} %collective-permute-done.1.other.refs_2_, bf16[768,1024]{1,0:T(8,128)(2,1)S(1)} %get-tuple-element.63.refs_3_, ...), custom_call_target="tpu_custom_call" | custom-call | flops 3221225 | bytes 8388 | tf_op jit(solution)/shard_map/project/pallas_call | solution.py:237
  68.9 1.6 %add_convert_fusion.3 = bf16[2,256,1024]{2,1,0:T(8,128)(2,1)S(1)} fusion(bf16[2,256,1024]{2,1,0:T(8,128)(2,1)} %collective-permute-done.12, bf16[2,256,1024]{2,1,0:T(8,128)(2,1)S(1)} %add_convert_fusion.6), kind=kLoop, calls=%fused_computation.3 | loop fusion | flops 2097152 | bytes 3145728 | tf_op jit(solution)/shard_map/convert_element_type | solution.py:340
  70.6 2.7 %collective-permute-done.15.refs_5_ = bf16[2,1024,256]{2,1,0:T(8,128)(2,1)S(1)} collective-permute-done((bf16[2,1024,256]{2,1,0:T(8,128)(2,1)S(1)}, bf16[2,1024,256]{2,1,0:T(8,128)(2,1)S(1)}, u32[]{:S(2)}, u32[]{:S(2)}) %collective-permute-start.15) | collective-permute-done | bytes 1048608 | tf_op jit(solution)/shard_map/ppermute | solution.py:47
  73.2 3.6 %collective-permute-done.14 = bf16[2,1024,256]{2,1,0:T(8,128)(2,1)S(1)} collective-permute-done((bf16[2,1024,256]{2,1,0:T(8,128)(2,1)S(1)}, bf16[2,1024,256]{2,1,0:T(8,128)(2,1)S(1)}, u32[]{:S(2)}, u32[]{:S(2)}) %collective-permute-start.14) | collective-permute-done | bytes 1048608 | tf_op jit(solution)/shard_map/ppermute | solution.py:47
  76.8 1.5 %collective-permute-start.16 = (bf16[2,256,1024]{2,1,0:T(8,128)(2,1)S(1)}, bf16[2,256,1024]{2,1,0:T(8,128)(2,1)S(1)}, u32[]{:S(2)}, u32[]{:S(2)}) collective-permute-start(bf16[2,256,1024]{2,1,0:T(8,128)(2,1)S(1)} %add_convert_fusion.6), channel_id=1, source_target_pairs={{0,2},{1,3},{6,4},{7,5},{8,10},{9,11},{14,12},{15,13},{16,18},{17,... | collective-permute-start | bytes 3145736 | tf_op jit(solution)/shard_map/ppermute | solution.py:47
  78.3 1.6 %collective-permute-start.17 = (bf16[2,256,1024]{2,1,0:T(8,128)(2,1)S(1)}, bf16[2,256,1024]{2,1,0:T(8,128)(2,1)}, u32[]{:S(2)}, u32[]{:S(2)}) collective-permute-start(bf16[2,256,1024]{2,1,0:T(8,128)(2,1)S(1)} %add_convert_fusion.3), channel_id=1, source_target_pairs={{2,4},{3,5},{4,2},{5,3},{10,12},{11,13},{12,10},{13,11},{18,20},{1... | collective-permute-start | bytes 3145736 | tf_op jit(solution)/shard_map/ppermute | solution.py:47
  80.0 1.5 collective-permute-start.20
  82.1 2.3 %collective-permute-done.4 = bf16[2,256,1024]{2,1,0:T(8,128)(2,1)S(1)} collective-permute-done((bf16[2,256,1024]{2,1,0:T(8,128)(2,1)S(1)}, bf16[2,256,1024]{2,1,0:T(8,128)(2,1)S(1)}, u32[]{:S(2)}, u32[]{:S(2)}) %collective-permute-start.4) | collective-permute-done | bytes 1048608 | tf_op jit(solution)/shard_map/ppermute | solution.py:47
  84.9 0.6 collective-permute-start.18
  85.4 13.6 %collective-permute-done.16 = bf16[2,256,1024]{2,1,0:T(8,128)(2,1)S(1)} collective-permute-done((bf16[2,256,1024]{2,1,0:T(8,128)(2,1)S(1)}, bf16[2,256,1024]{2,1,0:T(8,128)(2,1)S(1)}, u32[]{:S(2)}, u32[]{:S(2)}) %collective-permute-start.16) | collective-permute-done | bytes 1048608 | tf_op jit(solution)/shard_map/ppermute | solution.py:47
  99.5 6.7 %project.5 = (bf16[384,8192]{1,0:T(8,128)(2,1)}, bf16[384,1024]{1,0:T(8,128)(2,1)S(1)}, f32[768,1024]{1,0:T(8,128)S(1)}) custom-call(s32[3]{0:T(128)S(1)} %pad_add_fusion.place.refs_0_, bf16[384,8192]{1,0:T(8,128)(2,1)} %refs_1_.3, bf16[384,8192]{1,0:T(8,128)(2,1)S(1)} %collective-permute-done.1.other.refs_2_, ...), custom_call_target="tpu_custom_call", output_to_operand_aliasing={{0}: (7, {})} | custom-call | flops 3221225 | bytes 8388 | tf_op jit(solution)/shard_map/project/pallas_call | solution.py:237
  106.1 1.6 %add_convert_fusion.1 = bf16[2,256,1024]{2,1,0:T(8,128)(2,1)S(1)} fusion(bf16[2,256,1024]{2,1,0:T(8,128)(2,1)} %collective-permute-done.17, bf16[2,256,1024]{2,1,0:T(8,128)(2,1)S(1)} %add_convert_fusion.5), kind=kLoop, calls=%fused_computation.1 | loop fusion | flops 2097152 | bytes 3145728 | tf_op jit(solution)/shard_map/convert_element_type | solution.py:340
  107.8 1.5 %add.52.refs_4_ = bf16[2,1024,256]{2,1,0:T(8,128)(2,1)S(1)} add(bf16[2,1024,256]{2,1,0:T(8,128)(2,1)S(1)} %pad_maximum_fusion.1.refs_3_, bf16[2,1024,256]{2,1,0:T(8,128)(2,1)} %collective-permute-done.20) | non-fusion elementwise | flops 524288 | bytes 3145728 | tf_op jit(solution)/shard_map/add | solution.py:393
  109.4 0.7 collective-permute-start.24
  110.1 4.2 %collective-permute-start.25 = (bf16[2,256,1024]{2,1,0:T(8,128)(2,1)S(1)}, bf16[2,256,1024]{2,1,0:T(8,128)(2,1)S(1)}, u32[]{:S(2)}, u32[]{:S(2)}) collective-permute-start(bf16[2,256,1024]{2,1,0:T(8,128)(2,1)S(1)} %add_convert_fusion.1), channel_id=1, source_target_pairs={{0,2},{1,3},{2,0},{3,1},{4,6},{5,7},{6,4},{7,5},{8,10},{9,11},{10,... | collective-permute-start | bytes 3145736 | tf_op jit(solution)/shard_map/ppermute | solution.py:47
  114.8 6.7 %project.6 = (bf16[384,8192]{1,0:T(8,128)(2,1)}, bf16[384,1024]{1,0:T(8,128)(2,1)S(1)}, f32[768,1024]{1,0:T(8,128)S(1)}) custom-call(s32[3]{0:T(128)S(1)} %pad_add_fusion.place.refs_0_, bf16[384,8192]{1,0:T(8,128)(2,1)} %refs_1_.3, bf16[384,8192]{1,0:T(8,128)(2,1)S(1)} %collective-permute-done.1.other.refs_2_, ...), custom_call_target="tpu_custom_call", output_to_operand_aliasing={{0}: (7, {})} | custom-call | flops 3221225 | bytes 8388 | tf_op jit(solution)/shard_map/project/pallas_call | solution.py:237
  121.4 2.7 %collective-permute-done.21.refs_5_ = bf16[2,1024,256]{2,1,0:T(8,128)(2,1)S(1)} collective-permute-done((bf16[2,1024,256]{2,1,0:T(8,128)(2,1)S(1)}, bf16[2,1024,256]{2,1,0:T(8,128)(2,1)S(1)}, u32[]{:S(2)}, u32[]{:S(2)}) %collective-permute-start.21) | collective-permute-done | bytes 1048608 | tf_op jit(solution)/shard_map/ppermute | solution.py:47
  124.2 6.8 %project.7 = (bf16[384,8192]{1,0:T(8,128)(2,1)}, bf16[384,1024]{1,0:T(8,128)(2,1)S(1)}, f32[384,1024]{1,0:T(8,128)S(1)}, f32[384,1024]{1,0:T(8,128)S(1)}) custom-call(s32[3]{0:T(128)S(1)} %pad_add_fusion.place.refs_0_, bf16[384,8192]{1,0:T(8,128)(2,1)} %refs_1_.3, ...), custom_call_target="tpu_custom_call", output_to_operand_aliasing={{0}: (7, {})} | custom-call | flops 3221225 | bytes 8388 | tf_op jit(solution)/shard_map/project/pallas_call | solution.py:237
  131.0 0.5 collective-permute-start.27
  131.5 4.5 %collective-permute-done.25 = bf16[2,256,1024]{2,1,0:T(8,128)(2,1)S(1)} collective-permute-done((bf16[2,256,1024]{2,1,0:T(8,128)(2,1)S(1)}, bf16[2,256,1024]{2,1,0:T(8,128)(2,1)S(1)}, u32[]{:S(2)}, u32[]{:S(2)}) %collective-permute-start.25) | collective-permute-done | bytes 1048608 | tf_op jit(solution)/shard_map/ppermute | solution.py:47
  136.1 0.5 collective-permute-start.22
  136.6 0.6 fusion
  137.6 0.8 collective-permute-done.29.refs_2_
  138.3 2.4 %lay.1.refs_6_ = bf16[384,8192]{1,0:T(8,128)(2,1)} custom-call(s32[3]{0:T(128)S(1)} %pad_add_fusion.place.refs_0_, bf16[384,1024]{1,0:T(8,128)(2,1)S(1)} %collective-permute-done.27.refs_0_, bf16[384,1024]{1,0:T(8,128)(2,1)S(1)} %collective-permute-done.28.refs_1_, ...), custom_call_target="tpu_custom_call", output_to_operand_aliasing={{}: (4, {})} | custom-call | bytes 4718 | tf_op jit(solution)/shard_map/lay/pallas_call | solution.py:276
  140.8 5.6 %collective-permute-done.26.refs_5_ = bf16[256,1024]{1,0:T(8,128)(2,1)S(1)} collective-permute-done((bf16[256,1024]{1,0:T(8,128)(2,1)S(1)}, bf16[256,1024]{1,0:T(8,128)(2,1)S(1)}, u32[]{:S(2)}, u32[]{:S(2)}) %collective-permute-start.26) | collective-permute-done | bytes 524320 | tf_op jit(solution)/shard_map/ppermute | solution.py:47
  146.4 2.5 %finish.1 = (bf16[384,8192]{1,0:T(8,128)(2,1)}, bf16[384,1024]{1,0:T(8,128)(2,1)}, bf16[1024,256]{1,0:T(8,128)(2,1)}) custom-call(s32[3]{0:T(128)S(1)} %pad_add_fusion.place.refs_0_, bf16[384,1024]{1,0:T(8,128)(2,1)S(1)} %collective-permute-done.22.refs_1_, f32[384,1024]{1,0:T(8,128)S(1)} %get-tuple-element.87.refs_2_, ...), custom_call_target="tpu_custom_call", output_to_operand_aliasing={{0}: (6, {})} | custom-call | bytes 5505 | tf_op jit(solution)/shard_map/finish/pallas_call | solution.py:305
  (40 shorter events, 4.5 us)
Async XLA Ops:
  0.7 4.5 %copy-start = (bf16[384,1024]{1,0:T(8,128)(2,1)S(1)}, bf16[384,1024]{1,0:T(8,128)(2,1)}, u32[]{:S(2)}) copy-start(bf16[384,1024]{1,0:T(8,128)(2,1)} %cot_mine.1) | copy-start | bytes 2359300
  0.7 4.7 %copy-start.1 = (bf16[1024,256]{1,0:T(8,128)(2,1)S(1)}, bf16[1024,256]{1,0:T(8,128)(2,1)}, u32[]{:S(2)}) copy-start(bf16[1024,256]{1,0:T(8,128)(2,1)} %param.5) | copy-start | bytes 1572868
  2.4 2.4 %collective-permute-start = (bf16[384,1024]{1,0:T(8,128)(2,1)S(1)}, bf16[384,1024]{1,0:T(8,128)(2,1)S(1)}, u32[]{:S(2)}, u32[]{:S(2)}) collective-permute-start(bf16[384,1024]{1,0:T(8,128)(2,1)S(1)} %pack.1), channel_id=1, source_target_pairs={{0,1},{1,0},{2,3},{3,2},{4,5},{5,4},{6,7},{7,6},{8,9},{9,8},{10,11... | collective-permute-start | bytes 2359304 | tf_op jit(solution)/shard_map/ppermute | solution.py:47
  4.9 22.4 %collective-permute-start.1 = (bf16[384,8192]{1,0:T(8,128)(2,1)}, bf16[384,8192]{1,0:T(8,128)(2,1)S(1)}, u32[]{:S(2)}, u32[]{:S(2)}) collective-permute-start(bf16[384,8192]{1,0:T(8,128)(2,1)} %refs_1_.3), channel_id=1, source_target_pairs={{0,1},{1,0},{2,3},{3,2},{4,5},{5,4},{6,7},{7,6},{8,9},{9,8},{10,11... | collective-permute-start | bytes 18874376 | tf_op jit(solution)/shard_map/ppermute | solution.py:47
  5.3 6.8 %collective-permute-start.2 = (bf16[384,1024]{1,0:T(8,128)(2,1)S(1)}, bf16[384,1024]{1,0:T(8,128)(2,1)S(1)}, u32[]{:S(2)}, u32[]{:S(2)}) collective-permute-start(bf16[384,1024]{1,0:T(8,128)(2,1)S(1)} %copy-done), channel_id=1, source_target_pairs={{0,1},{1,0},{2,3},{3,2},{4,5},{5,4},{6,7},{7,6},{8,9},{9,8},{10,11... | collective-permute-start | bytes 2359304 | tf_op jit(solution)/shard_map/ppermute | solution.py:47
  5.4 15.2 %collective-permute-start.6 = (bf16[1024,256]{1,0:T(8,128)(2,1)S(1)}, bf16[1024,256]{1,0:T(8,128)(2,1)S(1)}, u32[]{:S(2)}, u32[]{:S(2)}) collective-permute-start(bf16[1024,256]{1,0:T(8,128)(2,1)S(1)} %copy-done.1), channel_id=1, source_target_pairs={{0,2},{1,3},{2,0},{3,1},{4,6},{5,7},{6,4},{7,5},{8,10},{9,11},{10,... | collective-permute-start | bytes 1572872 | tf_op jit(solution)/shard_map/ppermute | solution.py:47
  8.3 12.2 %collective-permute-start.7 = (bf16[1024,256]{1,0:T(8,128)(2,1)S(1)}, bf16[1024,256]{1,0:T(8,128)(2,1)S(1)}, u32[]{:S(2)}, u32[]{:S(2)}) collective-permute-start(bf16[1024,256]{1,0:T(8,128)(2,1)S(1)} %copy-done.1), channel_id=1, source_target_pairs={{0,8},{1,17},{2,10},{3,19},{4,12},{5,21},{6,14},{7,23},{8,0},{9,25... | collective-permute-start | bytes 1572872 | tf_op jit(solution)/shard_map/ppermute | solution.py:47
  9.8 10.7 %collective-permute-start.8 = (bf16[1024,256]{1,0:T(8,128)(2,1)S(1)}, bf16[1024,256]{1,0:T(8,128)(2,1)S(1)}, u32[]{:S(2)}, u32[]{:S(2)}) collective-permute-start(bf16[1024,256]{1,0:T(8,128)(2,1)S(1)} %copy-done.1), channel_id=1, source_target_pairs={{2,4},{3,5},{4,2},{5,3},{10,12},{11,13},{12,10},{13,11},{18,20},{1... | collective-permute-start | bytes 1572872 | tf_op jit(solution)/shard_map/ppermute | solution.py:47
  16.3 22.1 %collective-permute-start.5 = (bf16[2,256,1024]{2,1,0:T(8,128)(2,1)S(1)}, bf16[2,256,1024]{2,1,0:T(8,128)(2,1)S(1)}, u32[]{:S(2)}, u32[]{:S(2)}) collective-permute-start(bf16[2,256,1024]{2,1,0:T(8,128)(2,1)S(1)} %get-tuple-element.57), channel_id=1, source_target_pairs={{0,16},{1,9},{2,18},{3,11},{4,20},{5,13},{6,22},{7,15},{8,24},{9,1... | collective-permute-start | bytes 3145736 | tf_op jit(solution)/shard_map/ppermute | solution.py:47
  20.6 17.6 %collective-permute-start.9 = (bf16[1024,256]{1,0:T(8,128)(2,1)S(1)}, bf16[1024,256]{1,0:T(8,128)(2,1)S(1)}, u32[]{:S(2)}, u32[]{:S(2)}) collective-permute-start(bf16[1024,256]{1,0:T(8,128)(2,1)S(1)} %collective-permute-done.7), channel_id=1, source_target_pairs={{0,2},{1,3},{2,0},{3,1},{4,6},{5,7},{6,4},{7,5},{8,10},{9,11},{10,... | collective-permute-start | bytes 1572872 | tf_op jit(solution)/shard_map/ppermute | solution.py:47
  26.6 11.7 %collective-permute-start.10 = (bf16[1024,256]{1,0:T(8,128)(2,1)S(1)}, bf16[1024,256]{1,0:T(8,128)(2,1)S(1)}, u32[]{:S(2)}, u32[]{:S(2)}) collective-permute-start(bf16[1024,256]{1,0:T(8,128)(2,1)S(1)} %collective-permute-done.7), channel_id=1, source_target_pairs={{2,4},{3,5},{4,2},{5,3},{10,12},{11,13},{12,10},{13,11},{18,20},{1... | collective-permute-start | bytes 1572872 | tf_op jit(solution)/shard_map/ppermute | solution.py:47
  35.9 14.9 %collective-permute-start.3 = (bf16[2,256,1024]{2,1,0:T(8,128)(2,1)S(1)}, bf16[2,256,1024]{2,1,0:T(8,128)(2,1)S(1)}, u32[]{:S(2)}, u32[]{:S(2)}) collective-permute-start(bf16[2,256,1024]{2,1,0:T(8,128)(2,1)S(1)} %get-tuple-element.54), channel_id=1, source_target_pairs={{0,16},{1,9},{2,18},{3,11},{4,20},{5,13},{6,22},{7,15},{8,24},{9,1... | collective-permute-start | bytes 3145736 | tf_op jit(solution)/shard_map/ppermute | solution.py:47
  36.6 25.4 %collective-permute-start.11 = (bf16[2,1024,256]{2,1,0:T(8,128)(2,1)S(1)}, bf16[2,1024,256]{2,1,0:T(8,128)(2,1)S(1)}, u32[]{:S(2)}, u32[]{:S(2)}) collective-permute-start(bf16[2,1024,256]{2,1,0:T(8,128)(2,1)S(1)} %pad_maximum_fusion.2.refs_4_), channel_id=1, source_target_pairs={{0,16},{1,9},{2,18},{3,11},{4,20},{5,13},{6,22},{7,15},{8,24},{9,1... | collective-permute-start | bytes 3145736 | tf_op jit(solution)/shard_map/ppermute | solution.py:47
  39.9 29.0 %collective-permute-start.12 = (bf16[2,256,1024]{2,1,0:T(8,128)(2,1)S(1)}, bf16[2,256,1024]{2,1,0:T(8,128)(2,1)}, u32[]{:S(2)}, u32[]{:S(2)}) collective-permute-start(bf16[2,256,1024]{2,1,0:T(8,128)(2,1)S(1)} %add_convert_fusion.4), channel_id=1, source_target_pairs={{0,2},{1,3},{6,4},{7,5},{8,10},{9,11},{14,12},{15,13},{16,18},{17,... | collective-permute-start | bytes 3145736 | tf_op jit(solution)/shard_map/ppermute | solution.py:47
  45.9 27.3 %collective-permute-start.15 = (bf16[2,1024,256]{2,1,0:T(8,128)(2,1)S(1)}, bf16[2,1024,256]{2,1,0:T(8,128)(2,1)S(1)}, u32[]{:S(2)}, u32[]{:S(2)}) collective-permute-start(bf16[2,1024,256]{2,1,0:T(8,128)(2,1)S(1)} %pad_maximum_fusion.refs_2_.refs_4_), channel_id=1, source_target_pairs={{0,16},{1,9},{2,18},{3,11},{4,20},{5,13},{6,22},{7,15},{8,24},{9,1... | collective-permute-start | bytes 3145736 | tf_op jit(solution)/shard_map/ppermute | solution.py:47
  46.3 26.9 %collective-permute-start.13 = (bf16[2,1024,256]{2,1,0:T(8,128)(2,1)S(1)}, bf16[2,1024,256]{2,1,0:T(8,128)(2,1)S(1)}, u32[]{:S(2)}, u32[]{:S(2)}) collective-permute-start(bf16[2,1024,256]{2,1,0:T(8,128)(2,1)S(1)} %pad_maximum_fusion.refs_2_.refs_4_), channel_id=1, source_target_pairs={{2,4},{3,5},{4,2},{5,3},{10,12},{11,13},{12,10},{13,11},{18,20},{1... | collective-permute-start | bytes 3145736 | tf_op jit(solution)/shard_map/ppermute | solution.py:47
  50.7 26.1 %collective-permute-start.14 = (bf16[2,1024,256]{2,1,0:T(8,128)(2,1)S(1)}, bf16[2,1024,256]{2,1,0:T(8,128)(2,1)S(1)}, u32[]{:S(2)}, u32[]{:S(2)}) collective-permute-start(bf16[2,1024,256]{2,1,0:T(8,128)(2,1)S(1)} %pad_maximum_fusion.1.refs_3_), channel_id=1, source_target_pairs={{2,0},{3,1},{4,6},{5,7},{10,8},{11,9},{12,14},{13,15},{18,16},{19,... | collective-permute-start | bytes 3145736 | tf_op jit(solution)/shard_map/ppermute | solution.py:47
  62.0 22.5 %collective-permute-start.4 = (bf16[2,256,1024]{2,1,0:T(8,128)(2,1)S(1)}, bf16[2,256,1024]{2,1,0:T(8,128)(2,1)S(1)}, u32[]{:S(2)}, u32[]{:S(2)}) collective-permute-start(bf16[2,256,1024]{2,1,0:T(8,128)(2,1)S(1)} %get-tuple-element.55), channel_id=1, source_target_pairs={{0,16},{1,9},{2,18},{3,11},{4,20},{5,13},{6,22},{7,15},{8,24},{9,1... | collective-permute-start | bytes 3145736 | tf_op jit(solution)/shard_map/ppermute | solution.py:47
  76.8 22.3 %collective-permute-start.16 = (bf16[2,256,1024]{2,1,0:T(8,128)(2,1)S(1)}, bf16[2,256,1024]{2,1,0:T(8,128)(2,1)S(1)}, u32[]{:S(2)}, u32[]{:S(2)}) collective-permute-start(bf16[2,256,1024]{2,1,0:T(8,128)(2,1)S(1)} %add_convert_fusion.6), channel_id=1, source_target_pairs={{0,2},{1,3},{6,4},{7,5},{8,10},{9,11},{14,12},{15,13},{16,18},{17,... | collective-permute-start | bytes 3145736 | tf_op jit(solution)/shard_map/ppermute | solution.py:47
  78.3 27.8 %collective-permute-start.17 = (bf16[2,256,1024]{2,1,0:T(8,128)(2,1)S(1)}, bf16[2,256,1024]{2,1,0:T(8,128)(2,1)}, u32[]{:S(2)}, u32[]{:S(2)}) collective-permute-start(bf16[2,256,1024]{2,1,0:T(8,128)(2,1)S(1)} %add_convert_fusion.3), channel_id=1, source_target_pairs={{2,4},{3,5},{4,2},{5,3},{10,12},{11,13},{12,10},{13,11},{18,20},{1... | collective-permute-start | bytes 3145736 | tf_op jit(solution)/shard_map/ppermute | solution.py:47
  80.0 27.8 %collective-permute-start.20 = (bf16[2,1024,256]{2,1,0:T(8,128)(2,1)S(1)}, bf16[2,1024,256]{2,1,0:T(8,128)(2,1)}, u32[]{:S(2)}, u32[]{:S(2)}) collective-permute-start(bf16[2,1024,256]{2,1,0:T(8,128)(2,1)S(1)} %collective-permute-done.13), channel_id=1, source_target_pairs={{2,0},{3,1},{4,6},{5,7},{10,8},{11,9},{12,14},{13,15},{18,16},{19,... | collective-permute-start | bytes 3145736 | tf_op jit(solution)/shard_map/ppermute | solution.py:47
  81.7 28.4 %collective-permute-start.19 = (bf16[2,1024,256]{2,1,0:T(8,128)(2,1)S(1)}, bf16[2,1024,256]{2,1,0:T(8,128)(2,1)S(1)}, u32[]{:S(2)}, u32[]{:S(2)}) collective-permute-start(bf16[2,1024,256]{2,1,0:T(8,128)(2,1)S(1)} %add.51.refs_4_), channel_id=1, source_target_pairs={{0,16},{1,9},{2,18},{3,11},{4,20},{5,13},{6,22},{7,15},{8,24},{9,1... | collective-permute-start | bytes 3145736 | tf_op jit(solution)/shard_map/ppermute | solution.py:47
  84.9 29.5 %collective-permute-start.18 = (bf16[2,256,1024]{2,1,0:T(8,128)(2,1)S(1)}, bf16[2,256,1024]{2,1,0:T(8,128)(2,1)S(1)}, u32[]{:S(2)}, u32[]{:S(2)}) collective-permute-start(bf16[2,256,1024]{2,1,0:T(8,128)(2,1)S(1)} %get-tuple-element.76), channel_id=1, source_target_pairs={{0,16},{1,9},{2,18},{3,11},{4,20},{5,13},{6,22},{7,15},{8,24},{9,1... | collective-permute-start | bytes 3145736 | tf_op jit(solution)/shard_map/ppermute | solution.py:47
  109.3 14.9 %collective-permute-start.21 = (bf16[2,1024,256]{2,1,0:T(8,128)(2,1)S(1)}, bf16[2,1024,256]{2,1,0:T(8,128)(2,1)S(1)}, u32[]{:S(2)}, u32[]{:S(2)}) collective-permute-start(bf16[2,1024,256]{2,1,0:T(8,128)(2,1)S(1)} %add.52.refs_4_), channel_id=1, source_target_pairs={{0,16},{1,9},{2,18},{3,11},{4,20},{5,13},{6,22},{7,15},{8,24},{9,1... | collective-permute-start | bytes 3145736 | tf_op jit(solution)/shard_map/ppermute | solution.py:47
  109.4 26.7 %collective-permute-start.24 = (bf16[2,256,1024]{2,1,0:T(8,128)(2,1)S(1)}, bf16[2,256,1024]{2,1,0:T(8,128)(2,1)S(1)}, u32[]{:S(2)}, u32[]{:S(2)}) collective-permute-start(bf16[2,256,1024]{2,1,0:T(8,128)(2,1)S(1)} %add_convert_fusion.2), channel_id=1, source_target_pairs={{2,4},{3,5},{4,2},{5,3},{10,12},{11,13},{12,10},{13,11},{18,20},{1... | collective-permute-start | bytes 3145736 | tf_op jit(solution)/shard_map/ppermute | solution.py:47
  110.1 25.9 %collective-permute-start.25 = (bf16[2,256,1024]{2,1,0:T(8,128)(2,1)S(1)}, bf16[2,256,1024]{2,1,0:T(8,128)(2,1)S(1)}, u32[]{:S(2)}, u32[]{:S(2)}) collective-permute-start(bf16[2,256,1024]{2,1,0:T(8,128)(2,1)S(1)} %add_convert_fusion.1), channel_id=1, source_target_pairs={{0,2},{1,3},{2,0},{3,1},{4,6},{5,7},{6,4},{7,5},{8,10},{9,11},{10,... | collective-permute-start | bytes 3145736 | tf_op jit(solution)/shard_map/ppermute | solution.py:47
  131.0 15.4 %collective-permute-start.23 = (f32[384,1024]{1,0:T(8,128)S(1)}, f32[384,1024]{1,0:T(8,128)S(1)}, u32[]{:S(2)}, u32[]{:S(2)}) collective-permute-start(f32[384,1024]{1,0:T(8,128)S(1)} %get-tuple-element.88), channel_id=1, source_target_pairs={{0,1},{1,0},{2,3},{3,2},{4,5},{5,4},{6,7},{7,6},{8,9},{9,8},{10,11... | collective-permute-start | bytes 4718600 | tf_op jit(solution)/shard_map/ppermute | solution.py:47
  131.0 6.2 %collective-permute-start.27 = (bf16[384,1024]{1,0:T(8,128)(2,1)S(1)}, bf16[384,1024]{1,0:T(8,128)(2,1)S(1)}, u32[]{:S(2)}, u32[]{:S(2)}) collective-permute-start(bf16[384,1024]{1,0:T(8,128)(2,1)S(1)} %get-tuple-element.64), channel_id=1, source_target_pairs={{0,1},{1,0},{2,3},{3,2},{4,5},{5,4},{6,7},{7,6},{8,9},{9,8},{10,11... | collective-permute-start | bytes 2359304 | tf_op jit(solution)/shard_map/ppermute | solution.py:47
  131.5 6.1 %collective-permute-start.28 = (bf16[384,1024]{1,0:T(8,128)(2,1)S(1)}, bf16[384,1024]{1,0:T(8,128)(2,1)S(1)}, u32[]{:S(2)}, u32[]{:S(2)}) collective-permute-start(bf16[384,1024]{1,0:T(8,128)(2,1)S(1)} %get-tuple-element.73), channel_id=1, source_target_pairs={{0,1},{1,0},{2,3},{3,2},{4,5},{5,4},{6,7},{7,6},{8,9},{9,8},{10,11... | collective-permute-start | bytes 2359304 | tf_op jit(solution)/shard_map/ppermute | solution.py:47
  136.1 2.3 %collective-permute-start.29 = (bf16[384,1024]{1,0:T(8,128)(2,1)S(1)}, bf16[384,1024]{1,0:T(8,128)(2,1)S(1)}, u32[]{:S(2)}, u32[]{:S(2)}) collective-permute-start(bf16[384,1024]{1,0:T(8,128)(2,1)S(1)} %get-tuple-element.81), channel_id=1, source_target_pairs={{0,1},{1,0},{2,3},{3,2},{4,5},{5,4},{6,7},{7,6},{8,9},{9,8},{10,11... | collective-permute-start | bytes 2359304 | tf_op jit(solution)/shard_map/ppermute | solution.py:47
  136.1 10.4 %collective-permute-start.22 = (bf16[384,1024]{1,0:T(8,128)(2,1)S(1)}, bf16[384,1024]{1,0:T(8,128)(2,1)S(1)}, u32[]{:S(2)}, u32[]{:S(2)}) collective-permute-start(bf16[384,1024]{1,0:T(8,128)(2,1)S(1)} %get-tuple-element.86), channel_id=1, source_target_pairs={{0,1},{1,0},{2,3},{3,2},{4,5},{5,4},{6,7},{7,6},{8,9},{9,8},{10,11... | collective-permute-start | bytes 2359304 | tf_op jit(solution)/shard_map/ppermute | solution.py:47
  137.2 9.2 %collective-permute-start.26 = (bf16[256,1024]{1,0:T(8,128)(2,1)S(1)}, bf16[256,1024]{1,0:T(8,128)(2,1)S(1)}, u32[]{:S(2)}, u32[]{:S(2)}) collective-permute-start(bf16[256,1024]{1,0:T(8,128)(2,1)S(1)} %get-tuple-element.95), channel_id=1, source_target_pairs={{0,8},{1,17},{2,10},{3,19},{4,12},{5,21},{6,14},{7,23},{8,0},{9,25... | collective-permute-start | bytes 1572872 | tf_op jit(solution)/shard_map/ppermute | solution.py:47

commit v16 on v15

--- a/solution.py
+++ b/solution.py
@@ -356,11 +356,11 @@
     )
     got3 = sent(send3, FLIP_B)
     next_a = after(next_a, one_near, mid_near, keep3)
-    one = jnp.stack([one_near, sent(next_a, PAIR)])
-    mid = jnp.stack([mid_near, sent(next_a, MID)])
+    keep2, keep1, keep0, send2, send1, send0 = terms(place, activations, other, turned, rows)
+    one = jnp.stack([after(one_near, keep0), sent(next_a, PAIR)])
+    mid = jnp.stack([after(mid_near, keep0), sent(next_a, MID)])
     base_b = sent(base, FLIP_B)
-    keep2, keep1, keep0, send2, send1, send0 = terms(place, activations, other, turned, rows)
-    first = gate(place, got3, after(one, keep0), mid)
+    first = gate(place, got3, after(one, keep0), mid, base_b)
 
     sum3 = added(after(keep3, first), got3)
     far = sent(sum3, IN)
@@ -386,7 +386,7 @@
         place, 1, after(activations, sum2_far, sum1), other, cots, one, one_b, (whole, None, keys)
     )
 
-    sum3_near = added(sum3, near)
+    sum3_near = added(after(sum3, out1), near)
     sum_mid = sent(sum3_near, MID)
     sum1_far = added(after(sum1, sum3_near, out1), mid_far)
     sum_one = sent(after(sum1_far, three_end, two_b), PAIR)

time: 149 us -> 146 us (0.980)
  waiting for transfers between devices: 54.2 us -> 45.5 us
  starting transfers between devices: 38.5 us -> 42.4 us
    ppermute x30, waiting for transfers between devices: 54.2 us -> 45.5 us  [sent(): return lax.ppermute(array, AXES, pairs)]
    ppermute x30, starting transfers between devices: 38.5 us -> 42.4 us  [sent(): return lax.ppermute(array, AXES, pairs)]
  transfers between devices with their start and end apart: 30 -> 30, of which waited for: 13 -> 14; matrix products, arithmetic and copies ran while one was open for 5% -> 6% of each run, Pallas kernels for 29% -> 30%
where the time goes in v16:
time: 146 us; the launch traced here: 145 us
  Pallas kernels  47.2 us (32%)
  waiting for transfers between devices  45.5 us (31%)
  starting transfers between devices  42.4 us (29%)
  other arithmetic  9.31 us (6%)
    ppermute x30, waiting for transfers between devices, sent(): return lax.ppermute(array, AXES, pairs)  45.5 us
    ppermute x30, starting transfers between devices, sent(): return lax.ppermute(array, AXES, pairs)  42.4 us
    pallas_call x4, Pallas kernels, projected(): pl.pallas_call(lambda *refs: project_kernel(*refs, first=first, last=last...  26.6 us
    pallas_call x1, Pallas kernels, terms(): pl.pallas_call(term_kernel, grid_spec=pltpu.PrefetchScalarGridSpec(num_sc...  8.61 us
    convert_element_type x7, other arithmetic, added(): return total.astype(BF16)  6.51 us
    pallas_call x1, Pallas kernels, first_terms(): pl.pallas_call(first_term_kernel, grid_spec=pltpu.PrefetchScalarGridSpec(...  4.22 us
  transfers between devices with their start and end apart: 30, of which 14 were waited for; matrix products, arithmetic and copies ran while one was open for 6% of the time, Pallas kernels for 30%

profile of v16, /device:TPU:0, one launch (start us, length us, event | category | flops | bytes accessed | tf_op | source)
XLA Modules:
  0.0 145.3 jit_solution(10895631988978441939)
XLA Ops:
  0.7 1.7 %pack.1 = bf16[384,1024]{1,0:T(8,128)(2,1)S(1)} custom-call(s32[3]{0:T(128)S(1)} %pad_add_fusion.place.refs_0_, bf16[384,8192]{1,0:T(8,128)(2,1)} %refs_1_.3), custom_call_target="tpu_custom_call" | custom-call | bytes 1572 | tf_op jit(solution)/shard_map/pack/pallas_call | solution.py:82
  3.0 1.9 %collective-permute-done.other = bf16[384,1024]{1,0:T(8,128)(2,1)S(1)} collective-permute-done((bf16[384,1024]{1,0:T(8,128)(2,1)S(1)}, bf16[384,1024]{1,0:T(8,128)(2,1)S(1)}, u32[]{:S(2)}, u32[]{:S(2)}) %collective-permute-start) | collective-permute-done | bytes 786464 | tf_op jit(solution)/shard_map/ppermute | solution.py:47
  5.4 2.9 %collective-permute-start.7 = (bf16[1024,256]{1,0:T(8,128)(2,1)S(1)}, bf16[1024,256]{1,0:T(8,128)(2,1)S(1)}, u32[]{:S(2)}, u32[]{:S(2)}) collective-permute-start(bf16[1024,256]{1,0:T(8,128)(2,1)S(1)} %copy-done.1), channel_id=1, source_target_pairs={{0,8},{1,17},{2,10},{3,19},{4,12},{5,21},{6,14},{7,23},{8,0},{9,25... | collective-permute-start | bytes 1572872 | tf_op jit(solution)/shard_map/ppermute | solution.py:47
  8.3 1.6 %collective-permute-start.6 = (bf16[1024,256]{1,0:T(8,128)(2,1)S(1)}, bf16[1024,256]{1,0:T(8,128)(2,1)S(1)}, u32[]{:S(2)}, u32[]{:S(2)}) collective-permute-start(bf16[1024,256]{1,0:T(8,128)(2,1)S(1)} %copy-done.1), channel_id=1, source_target_pairs={{0,2},{1,3},{2,0},{3,1},{4,6},{5,7},{6,4},{7,5},{8,10},{9,11},{10,... | collective-permute-start | bytes 1572872 | tf_op jit(solution)/shard_map/ppermute | solution.py:47
  9.8 0.7 collective-permute-start.8
  10.5 4.9 %collective-permute-done.7 = bf16[1024,256]{1,0:T(8,128)(2,1)S(1)} collective-permute-done((bf16[1024,256]{1,0:T(8,128)(2,1)S(1)}, bf16[1024,256]{1,0:T(8,128)(2,1)S(1)}, u32[]{:S(2)}, u32[]{:S(2)}) %collective-permute-start.7) | collective-permute-done | bytes 524320 | tf_op jit(solution)/shard_map/ppermute | solution.py:47
  15.5 2.1 %collective-permute-start.11 = (bf16[2,1024,256]{2,1,0:T(8,128)(2,1)S(1)}, bf16[2,1024,256]{2,1,0:T(8,128)(2,1)S(1)}, u32[]{:S(2)}, u32[]{:S(2)}) collective-permute-start(bf16[2,1024,256]{2,1,0:T(8,128)(2,1)S(1)} %pad_maximum_fusion.2.refs_4_), channel_id=1, source_target_pairs={{0,16},{1,9},{2,18},{3,11},{4,20},{5,13},{6,22},{7,15},{8,24},{9,1... | collective-permute-start | bytes 3145736 | tf_op jit(solution)/shard_map/ppermute | solution.py:47
  17.6 4.2 %terms.2 = (bf16[2,256,1024]{2,1,0:T(8,128)(2,1)S(1)}, bf16[2,256,1024]{2,1,0:T(8,128)(2,1)S(1)}, bf16[768,1024]{1,0:T(8,128)(2,1)S(1)}, bf16[1024,768]{1,0:T(8,128)(2,1)S(1)}) custom-call(s32[3]{0:T(128)S(1)} %pad_add_fusion.place.refs_0_, bf16[384,8192]{1,0:T(8,128)(2,1)} %refs_1_.3, bf16[384,1024]{1,0:T(8,128)(2,1)S(1)} %collective-permute-done.other, ...), custom_call_target="tpu_custom_call" | custom-call | flops 1610612 | bytes 5767 | tf_op jit(solution)/shard_map/terms/pallas_call | solution.py:128
  22.0 4.6 %collective-permute-start.9 = (bf16[1024,256]{1,0:T(8,128)(2,1)S(1)}, bf16[1024,256]{1,0:T(8,128)(2,1)S(1)}, u32[]{:S(2)}, u32[]{:S(2)}) collective-permute-start(bf16[1024,256]{1,0:T(8,128)(2,1)S(1)} %collective-permute-done.7), channel_id=1, source_target_pairs={{0,2},{1,3},{2,0},{3,1},{4,6},{5,7},{6,4},{7,5},{8,10},{9,11},{10,... | collective-permute-start | bytes 1572872 | tf_op jit(solution)/shard_map/ppermute | solution.py:47
  26.6 0.7 collective-permute-start.10
  27.3 8.6 %terms.3 = (bf16[2,256,1024]{2,1,0:T(8,128)(2,1)S(1)}, bf16[2,256,1024]{2,1,0:T(8,128)(2,1)S(1)}, bf16[2,256,1024]{2,1,0:T(8,128)(2,1)S(1)}, bf16[2,256,1024]{2,...) custom-call(s32[3]{0:T(128)S(1)} %pad_add_fusion.place.refs_0_, ...), custom_call_target="tpu_custom_call" | custom-call | flops 4831838 | bytes 17301 | tf_op jit(solution)/shard_map/terms/pallas_call | solution.py:170
  35.9 0.6 collective-permute-start.3
  36.5 1.2 collective-permute-done.9
  37.9 3.7 %collective-permute-done.5.refs_1_ = bf16[2,256,1024]{2,1,0:T(8,128)(2,1)S(1)} collective-permute-done((bf16[2,256,1024]{2,1,0:T(8,128)(2,1)S(1)}, bf16[2,256,1024]{2,1,0:T(8,128)(2,1)S(1)}, u32[]{:S(2)}, u32[]{:S(2)}) %collective-permute-start.5) | collective-permute-done | bytes 1048608 | tf_op jit(solution)/shard_map/ppermute | solution.py:47
  41.6 1.1 gate.1.refs_0_
  43.2 4.0 %collective-permute-start.12 = (bf16[2,256,1024]{2,1,0:T(8,128)(2,1)S(1)}, bf16[2,256,1024]{2,1,0:T(8,128)(2,1)S(1)}, u32[]{:S(2)}, u32[]{:S(2)}) collective-permute-start(bf16[2,256,1024]{2,1,0:T(8,128)(2,1)S(1)} %add_convert_fusion.4), channel_id=1, source_target_pairs={{0,2},{1,3},{6,4},{7,5},{8,10},{9,11},{14,12},{15,13},{16,18},{17,... | collective-permute-start | bytes 3145736 | tf_op jit(solution)/shard_map/ppermute | solution.py:47
  47.3 1.6 %collective-permute-start.13 = (bf16[2,1024,256]{2,1,0:T(8,128)(2,1)S(1)}, bf16[2,1024,256]{2,1,0:T(8,128)(2,1)S(1)}, u32[]{:S(2)}, u32[]{:S(2)}) collective-permute-start(bf16[2,1024,256]{2,1,0:T(8,128)(2,1)S(1)} %pad_maximum_fusion.refs_2_.refs_4_), channel_id=1, source_target_pairs={{0,16},{1,9},{2,18},{3,11},{4,20},{5,13},{6,22},{7,15},{8,24},{9,1... | collective-permute-start | bytes 3145736 | tf_op jit(solution)/shard_map/ppermute | solution.py:47
  48.8 1.3 collective-permute-start.15
  50.1 0.7 collective-permute-start.14
  50.9 2.0 %collective-permute-done.3 = bf16[2,256,1024]{2,1,0:T(8,128)(2,1)S(1)} collective-permute-done((bf16[2,256,1024]{2,1,0:T(8,128)(2,1)S(1)}, bf16[2,256,1024]{2,1,0:T(8,128)(2,1)S(1)}, u32[]{:S(2)}, u32[]{:S(2)}) %collective-permute-start.3) | collective-permute-done | bytes 1048608 | tf_op jit(solution)/shard_map/ppermute | solution.py:47
  53.3 2.1 %collective-permute-start.4 = (bf16[2,256,1024]{2,1,0:T(8,128)(2,1)S(1)}, bf16[2,256,1024]{2,1,0:T(8,128)(2,1)}, u32[]{:S(2)}, u32[]{:S(2)}) collective-permute-start(bf16[2,256,1024]{2,1,0:T(8,128)(2,1)S(1)} %get-tuple-element.58), channel_id=1, source_target_pairs={{0,16},{1,9},{2,18},{3,11},{4,20},{5,13},{6,22},{7,15},{8,24},{9,1... | collective-permute-start | bytes 3145736 | tf_op jit(solution)/shard_map/ppermute | solution.py:47
  55.4 6.4 %project.4 = (bf16[384,8192]{1,0:T(8,128)(2,1)}, bf16[384,1024]{1,0:T(8,128)(2,1)S(1)}, f32[768,1024]{1,0:T(8,128)S(1)}) custom-call(s32[3]{0:T(128)S(1)} %gate.1.refs_0_, bf16[384,8192]{1,0:T(8,128)(2,1)} %refs_1_.3, bf16[384,8192]{1,0:T(8,128)(2,1)S(1)} %collective-permute-done.1.other.refs_2_, bf16[768,1024]{1,0:T(8,128)(2,1)S(1)} %get-tuple-element.68.refs_3_, ...), custom_call_target="tpu_custom_call" | custom-call | flops 3221225 | bytes 8388 | tf_op jit(solution)/shard_map/project/pallas_call | solution.py:237
  61.8 6.4 %collective-permute-done.12 = bf16[2,256,1024]{2,1,0:T(8,128)(2,1)S(1)} collective-permute-done((bf16[2,256,1024]{2,1,0:T(8,128)(2,1)S(1)}, bf16[2,256,1024]{2,1,0:T(8,128)(2,1)S(1)}, u32[]{:S(2)}, u32[]{:S(2)}) %collective-permute-start.12) | collective-permute-done | bytes 1048608 | tf_op jit(solution)/shard_map/ppermute | solution.py:47
  68.6 5.0 %collective-permute-done.15 = bf16[2,1024,256]{2,1,0:T(8,128)(2,1)S(1)} collective-permute-done((bf16[2,1024,256]{2,1,0:T(8,128)(2,1)S(1)}, bf16[2,1024,256]{2,1,0:T(8,128)(2,1)S(1)}, u32[]{:S(2)}, u32[]{:S(2)}) %collective-permute-start.15) | collective-permute-done | bytes 1048608 | tf_op jit(solution)/shard_map/ppermute | solution.py:47
  73.6 6.6 %collective-permute-start.16 = (bf16[2,256,1024]{2,1,0:T(8,128)(2,1)S(1)}, bf16[2,256,1024]{2,1,0:T(8,128)(2,1)}, u32[]{:S(2)}, u32[]{:S(2)}) collective-permute-start(bf16[2,256,1024]{2,1,0:T(8,128)(2,1)S(1)} %add_convert_fusion.6), channel_id=1, source_target_pairs={{0,2},{1,3},{6,4},{7,5},{8,10},{9,11},{14,12},{15,13},{16,18},{17,... | collective-permute-start | bytes 3145736 | tf_op jit(solution)/shard_map/ppermute | solution.py:47
  80.2 1.6 %collective-permute-start.17 = (bf16[2,256,1024]{2,1,0:T(8,128)(2,1)S(1)}, bf16[2,256,1024]{2,1,0:T(8,128)(2,1)}, u32[]{:S(2)}, u32[]{:S(2)}) collective-permute-start(bf16[2,256,1024]{2,1,0:T(8,128)(2,1)S(1)} %add_convert_fusion.3), channel_id=1, source_target_pairs={{2,4},{3,5},{4,2},{5,3},{10,12},{11,13},{12,10},{13,11},{18,20},{1... | collective-permute-start | bytes 3145736 | tf_op jit(solution)/shard_map/ppermute | solution.py:47
  81.9 1.5 %collective-permute-start.20 = (bf16[2,1024,256]{2,1,0:T(8,128)(2,1)S(1)}, bf16[2,1024,256]{2,1,0:T(8,128)(2,1)}, u32[]{:S(2)}, u32[]{:S(2)}) collective-permute-start(bf16[2,1024,256]{2,1,0:T(8,128)(2,1)S(1)} %collective-permute-done.14), channel_id=1, source_target_pairs={{2,0},{3,1},{4,6},{5,7},{10,8},{11,9},{12,14},{13,15},{18,16},{19,... | collective-permute-start | bytes 3145736 | tf_op jit(solution)/shard_map/ppermute | solution.py:47
  83.6 1.6 %collective-permute-start.19 = (bf16[2,1024,256]{2,1,0:T(8,128)(2,1)S(1)}, bf16[2,1024,256]{2,1,0:T(8,128)(2,1)S(1)}, u32[]{:S(2)}, u32[]{:S(2)}) collective-permute-start(bf16[2,1024,256]{2,1,0:T(8,128)(2,1)S(1)} %add.51.refs_4_), channel_id=1, source_target_pairs={{0,16},{1,9},{2,18},{3,11},{4,20},{5,13},{6,22},{7,15},{8,24},{9,1... | collective-permute-start | bytes 3145736 | tf_op jit(solution)/shard_map/ppermute | solution.py:47
  85.2 1.6 %add_convert_fusion.5 = bf16[2,256,1024]{2,1,0:T(8,128)(2,1)S(1)} fusion(bf16[2,256,1024]{2,1,0:T(8,128)(2,1)} %collective-permute-done.4, bf16[2,256,1024]{2,1,0:T(8,128)(2,1)S(1)} %get-tuple-element.54), kind=kLoop, calls=%fused_computation.5 | loop fusion | flops 2097152 | bytes 3145728 | tf_op jit(solution)/shard_map/convert_element_type | solution.py:340
  86.9 6.7 %project.5 = (bf16[384,8192]{1,0:T(8,128)(2,1)}, bf16[384,1024]{1,0:T(8,128)(2,1)S(1)}, f32[768,1024]{1,0:T(8,128)S(1)}) custom-call(s32[3]{0:T(128)S(1)} %pad_add_fusion.place.refs_0_, bf16[384,8192]{1,0:T(8,128)(2,1)} %refs_1_.3, bf16[384,8192]{1,0:T(8,128)(2,1)S(1)} %collective-permute-done.1.other.refs_2_, ...), custom_call_target="tpu_custom_call", output_to_operand_aliasing={{0}: (7, {})} | custom-call | flops 3221225 | bytes 8388 | tf_op jit(solution)/shard_map/project/pallas_call | solution.py:237
  94.0 4.5 %collective-permute-done.16 = bf16[2,256,1024]{2,1,0:T(8,128)(2,1)} collective-permute-done((bf16[2,256,1024]{2,1,0:T(8,128)(2,1)S(1)}, bf16[2,256,1024]{2,1,0:T(8,128)(2,1)}, u32[]{:S(2)}, u32[]{:S(2)}) %collective-permute-start.16) | collective-permute-done | bytes 1048608 | tf_op jit(solution)/shard_map/ppermute | solution.py:47
  98.6 1.6 %add_convert_fusion.2 = bf16[2,256,1024]{2,1,0:T(8,128)(2,1)S(1)} fusion(bf16[2,256,1024]{2,1,0:T(8,128)(2,1)} %collective-permute-done.16, bf16[2,256,1024]{2,1,0:T(8,128)(2,1)S(1)} %add_convert_fusion.4), kind=kLoop, calls=%fused_computation.2 | loop fusion | flops 2097152 | bytes 3145728 | tf_op jit(solution)/shard_map/convert_element_type | solution.py:340
  100.2 1.6 %add_convert_fusion.1 = bf16[2,256,1024]{2,1,0:T(8,128)(2,1)S(1)} fusion(bf16[2,256,1024]{2,1,0:T(8,128)(2,1)} %collective-permute-done.17, bf16[2,256,1024]{2,1,0:T(8,128)(2,1)S(1)} %add_convert_fusion.5), kind=kLoop, calls=%fused_computation.1 | loop fusion | flops 2097152 | bytes 3145728 | tf_op jit(solution)/shard_map/convert_element_type | solution.py:340
  101.8 3.5 %collective-permute-done.20 = bf16[2,1024,256]{2,1,0:T(8,128)(2,1)} collective-permute-done((bf16[2,1024,256]{2,1,0:T(8,128)(2,1)S(1)}, bf16[2,1024,256]{2,1,0:T(8,128)(2,1)}, u32[]{:S(2)}, u32[]{:S(2)}) %collective-permute-start.20) | collective-permute-done | bytes 1048608 | tf_op jit(solution)/shard_map/ppermute | solution.py:47
  105.4 1.5 %add.52.refs_4_ = bf16[2,1024,256]{2,1,0:T(8,128)(2,1)S(1)} add(bf16[2,1024,256]{2,1,0:T(8,128)(2,1)S(1)} %pad_maximum_fusion.1.refs_3_, bf16[2,1024,256]{2,1,0:T(8,128)(2,1)} %collective-permute-done.20) | non-fusion elementwise | flops 524288 | bytes 3145728 | tf_op jit(solution)/shard_map/add | solution.py:393
  106.9 2.6 %collective-permute-start.21 = (bf16[2,1024,256]{2,1,0:T(8,128)(2,1)S(1)}, bf16[2,1024,256]{2,1,0:T(8,128)(2,1)S(1)}, u32[]{:S(2)}, u32[]{:S(2)}) collective-permute-start(bf16[2,1024,256]{2,1,0:T(8,128)(2,1)S(1)} %add.52.refs_4_), channel_id=1, source_target_pairs={{0,16},{1,9},{2,18},{3,11},{4,20},{5,13},{6,22},{7,15},{8,24},{9,1... | collective-permute-start | bytes 3145736 | tf_op jit(solution)/shard_map/ppermute | solution.py:47
  109.5 0.7 collective-permute-start.24
  110.2 2.3 %collective-permute-start.25 = (bf16[2,256,1024]{2,1,0:T(8,128)(2,1)S(1)}, bf16[2,256,1024]{2,1,0:T(8,128)(2,1)S(1)}, u32[]{:S(2)}, u32[]{:S(2)}) collective-permute-start(bf16[2,256,1024]{2,1,0:T(8,128)(2,1)S(1)} %add_convert_fusion.1), channel_id=1, source_target_pairs={{0,2},{1,3},{2,0},{3,1},{4,6},{5,7},{6,4},{7,5},{8,10},{9,11},{10,... | collective-permute-start | bytes 3145736 | tf_op jit(solution)/shard_map/ppermute | solution.py:47
  112.9 6.7 %project.6 = (bf16[384,8192]{1,0:T(8,128)(2,1)}, bf16[384,1024]{1,0:T(8,128)(2,1)S(1)}, f32[768,1024]{1,0:T(8,128)S(1)}) custom-call(s32[3]{0:T(128)S(1)} %pad_add_fusion.place.refs_0_, bf16[384,8192]{1,0:T(8,128)(2,1)} %refs_1_.3, bf16[384,8192]{1,0:T(8,128)(2,1)S(1)} %collective-permute-done.1.other.refs_2_, ...), custom_call_target="tpu_custom_call", output_to_operand_aliasing={{0}: (7, {})} | custom-call | flops 3221225 | bytes 8388 | tf_op jit(solution)/shard_map/project/pallas_call | solution.py:237
  119.6 2.7 %collective-permute-done.21.refs_5_ = bf16[2,1024,256]{2,1,0:T(8,128)(2,1)S(1)} collective-permute-done((bf16[2,1024,256]{2,1,0:T(8,128)(2,1)S(1)}, bf16[2,1024,256]{2,1,0:T(8,128)(2,1)S(1)}, u32[]{:S(2)}, u32[]{:S(2)}) %collective-permute-start.21) | collective-permute-done | bytes 1048608 | tf_op jit(solution)/shard_map/ppermute | solution.py:47
  122.3 6.8 %project.7 = (bf16[384,8192]{1,0:T(8,128)(2,1)}, bf16[384,1024]{1,0:T(8,128)(2,1)S(1)}, f32[384,1024]{1,0:T(8,128)S(1)}, f32[384,1024]{1,0:T(8,128)S(1)}) custom-call(s32[3]{0:T(128)S(1)} %pad_add_fusion.place.refs_0_, bf16[384,8192]{1,0:T(8,128)(2,1)} %refs_1_.3, ...), custom_call_target="tpu_custom_call", output_to_operand_aliasing={{0}: (7, {})} | custom-call | flops 3221225 | bytes 8388 | tf_op jit(solution)/shard_map/project/pallas_call | solution.py:237
  130.2 0.6 fusion
  130.8 2.8 %collective-permute-done.27.refs_0_ = bf16[384,1024]{1,0:T(8,128)(2,1)S(1)} collective-permute-done((bf16[384,1024]{1,0:T(8,128)(2,1)S(1)}, bf16[384,1024]{1,0:T(8,128)(2,1)S(1)}, u32[]{:S(2)}, u32[]{:S(2)}) %collective-permute-start.27) | collective-permute-done | bytes 786464 | tf_op jit(solution)/shard_map/ppermute | solution.py:47
  133.6 1.1 collective-permute-done.28.refs_1_
  134.8 1.1 collective-permute-done.29.refs_2_
  135.9 2.4 %lay.1.refs_6_ = bf16[384,8192]{1,0:T(8,128)(2,1)} custom-call(s32[3]{0:T(128)S(1)} %pad_add_fusion.place.refs_0_, bf16[384,1024]{1,0:T(8,128)(2,1)S(1)} %collective-permute-done.27.refs_0_, bf16[384,1024]{1,0:T(8,128)(2,1)S(1)} %collective-permute-done.28.refs_1_, ...), custom_call_target="tpu_custom_call", output_to_operand_aliasing={{}: (4, {})} | custom-call | bytes 4718 | tf_op jit(solution)/shard_map/lay/pallas_call | solution.py:276
  138.3 4.5 %collective-permute-done.26.refs_5_ = bf16[256,1024]{1,0:T(8,128)(2,1)S(1)} collective-permute-done((bf16[256,1024]{1,0:T(8,128)(2,1)S(1)}, bf16[256,1024]{1,0:T(8,128)(2,1)S(1)}, u32[]{:S(2)}, u32[]{:S(2)}) %collective-permute-start.26) | collective-permute-done | bytes 524320 | tf_op jit(solution)/shard_map/ppermute | solution.py:47
  142.8 2.5 %finish.1 = (bf16[384,8192]{1,0:T(8,128)(2,1)}, bf16[384,1024]{1,0:T(8,128)(2,1)}, bf16[1024,256]{1,0:T(8,128)(2,1)}) custom-call(s32[3]{0:T(128)S(1)} %pad_add_fusion.place.refs_0_, bf16[384,1024]{1,0:T(8,128)(2,1)S(1)} %collective-permute-done.22.refs_1_, f32[384,1024]{1,0:T(8,128)S(1)} %get-tuple-element.93.refs_2_, ...), custom_call_target="tpu_custom_call", output_to_operand_aliasing={{0}: (6, {})} | custom-call | bytes 5505 | tf_op jit(solution)/shard_map/finish/pallas_call | solution.py:305
  (40 shorter events, 5.1 us)
Async XLA Ops:
  0.7 4.5 %copy-start = (bf16[384,1024]{1,0:T(8,128)(2,1)S(1)}, bf16[384,1024]{1,0:T(8,128)(2,1)}, u32[]{:S(2)}) copy-start(bf16[384,1024]{1,0:T(8,128)(2,1)} %cot_mine.1) | copy-start | bytes 2359300
  0.7 4.7 %copy-start.1 = (bf16[1024,256]{1,0:T(8,128)(2,1)S(1)}, bf16[1024,256]{1,0:T(8,128)(2,1)}, u32[]{:S(2)}) copy-start(bf16[1024,256]{1,0:T(8,128)(2,1)} %param.5) | copy-start | bytes 1572868
  2.4 2.4 %collective-permute-start = (bf16[384,1024]{1,0:T(8,128)(2,1)S(1)}, bf16[384,1024]{1,0:T(8,128)(2,1)S(1)}, u32[]{:S(2)}, u32[]{:S(2)}) collective-permute-start(bf16[384,1024]{1,0:T(8,128)(2,1)S(1)} %pack.1), channel_id=1, source_target_pairs={{0,1},{1,0},{2,3},{3,2},{4,5},{5,4},{6,7},{7,6},{8,9},{9,8},{10,11... | collective-permute-start | bytes 2359304 | tf_op jit(solution)/shard_map/ppermute | solution.py:47
  4.9 22.4 %collective-permute-start.1 = (bf16[384,8192]{1,0:T(8,128)(2,1)}, bf16[384,8192]{1,0:T(8,128)(2,1)S(1)}, u32[]{:S(2)}, u32[]{:S(2)}) collective-permute-start(bf16[384,8192]{1,0:T(8,128)(2,1)} %refs_1_.3), channel_id=1, source_target_pairs={{0,1},{1,0},{2,3},{3,2},{4,5},{5,4},{6,7},{7,6},{8,9},{9,8},{10,11... | collective-permute-start | bytes 18874376 | tf_op jit(solution)/shard_map/ppermute | solution.py:47
  5.3 12.4 %collective-permute-start.2 = (bf16[384,1024]{1,0:T(8,128)(2,1)S(1)}, bf16[384,1024]{1,0:T(8,128)(2,1)S(1)}, u32[]{:S(2)}, u32[]{:S(2)}) collective-permute-start(bf16[384,1024]{1,0:T(8,128)(2,1)S(1)} %copy-done), channel_id=1, source_target_pairs={{0,1},{1,0},{2,3},{3,2},{4,5},{5,4},{6,7},{7,6},{8,9},{9,8},{10,11... | collective-permute-start | bytes 2359304 | tf_op jit(solution)/shard_map/ppermute | solution.py:47
  5.4 10.0 %collective-permute-start.7 = (bf16[1024,256]{1,0:T(8,128)(2,1)S(1)}, bf16[1024,256]{1,0:T(8,128)(2,1)S(1)}, u32[]{:S(2)}, u32[]{:S(2)}) collective-permute-start(bf16[1024,256]{1,0:T(8,128)(2,1)S(1)} %copy-done.1), channel_id=1, source_target_pairs={{0,8},{1,17},{2,10},{3,19},{4,12},{5,21},{6,14},{7,23},{8,0},{9,25... | collective-permute-start | bytes 1572872 | tf_op jit(solution)/shard_map/ppermute | solution.py:47
  8.3 13.7 %collective-permute-start.6 = (bf16[1024,256]{1,0:T(8,128)(2,1)S(1)}, bf16[1024,256]{1,0:T(8,128)(2,1)S(1)}, u32[]{:S(2)}, u32[]{:S(2)}) collective-permute-start(bf16[1024,256]{1,0:T(8,128)(2,1)S(1)} %copy-done.1), channel_id=1, source_target_pairs={{0,2},{1,3},{2,0},{3,1},{4,6},{5,7},{6,4},{7,5},{8,10},{9,11},{10,... | collective-permute-start | bytes 1572872 | tf_op jit(solution)/shard_map/ppermute | solution.py:47
  9.8 12.1 %collective-permute-start.8 = (bf16[1024,256]{1,0:T(8,128)(2,1)S(1)}, bf16[1024,256]{1,0:T(8,128)(2,1)S(1)}, u32[]{:S(2)}, u32[]{:S(2)}) collective-permute-start(bf16[1024,256]{1,0:T(8,128)(2,1)S(1)} %copy-done.1), channel_id=1, source_target_pairs={{2,4},{3,5},{4,2},{5,3},{10,12},{11,13},{12,10},{13,11},{18,20},{1... | collective-permute-start | bytes 1572872 | tf_op jit(solution)/shard_map/ppermute | solution.py:47
  15.5 22.4 %collective-permute-start.11 = (bf16[2,1024,256]{2,1,0:T(8,128)(2,1)S(1)}, bf16[2,1024,256]{2,1,0:T(8,128)(2,1)S(1)}, u32[]{:S(2)}, u32[]{:S(2)}) collective-permute-start(bf16[2,1024,256]{2,1,0:T(8,128)(2,1)S(1)} %pad_maximum_fusion.2.refs_4_), channel_id=1, source_target_pairs={{0,16},{1,9},{2,18},{3,11},{4,20},{5,13},{6,22},{7,15},{8,24},{9,1... | collective-permute-start | bytes 3145736 | tf_op jit(solution)/shard_map/ppermute | solution.py:47
  21.9 19.8 %collective-permute-start.5 = (bf16[2,256,1024]{2,1,0:T(8,128)(2,1)S(1)}, bf16[2,256,1024]{2,1,0:T(8,128)(2,1)S(1)}, u32[]{:S(2)}, u32[]{:S(2)}) collective-permute-start(bf16[2,256,1024]{2,1,0:T(8,128)(2,1)S(1)} %get-tuple-element.60), channel_id=1, source_target_pairs={{0,16},{1,9},{2,18},{3,11},{4,20},{5,13},{6,22},{7,15},{8,24},{9,1... | collective-permute-start | bytes 3145736 | tf_op jit(solution)/shard_map/ppermute | solution.py:47
  22.0 15.7 %collective-permute-start.9 = (bf16[1024,256]{1,0:T(8,128)(2,1)S(1)}, bf16[1024,256]{1,0:T(8,128)(2,1)S(1)}, u32[]{:S(2)}, u32[]{:S(2)}) collective-permute-start(bf16[1024,256]{1,0:T(8,128)(2,1)S(1)} %collective-permute-done.7), channel_id=1, source_target_pairs={{0,2},{1,3},{2,0},{3,1},{4,6},{5,7},{6,4},{7,5},{8,10},{9,11},{10,... | collective-permute-start | bytes 1572872 | tf_op jit(solution)/shard_map/ppermute | solution.py:47
  26.6 11.2 %collective-permute-start.10 = (bf16[1024,256]{1,0:T(8,128)(2,1)S(1)}, bf16[1024,256]{1,0:T(8,128)(2,1)S(1)}, u32[]{:S(2)}, u32[]{:S(2)}) collective-permute-start(bf16[1024,256]{1,0:T(8,128)(2,1)S(1)} %collective-permute-done.7), channel_id=1, source_target_pairs={{2,4},{3,5},{4,2},{5,3},{10,12},{11,13},{12,10},{13,11},{18,20},{1... | collective-permute-start | bytes 1572872 | tf_op jit(solution)/shard_map/ppermute | solution.py:47
  35.9 17.0 %collective-permute-start.3 = (bf16[2,256,1024]{2,1,0:T(8,128)(2,1)S(1)}, bf16[2,256,1024]{2,1,0:T(8,128)(2,1)S(1)}, u32[]{:S(2)}, u32[]{:S(2)}) collective-permute-start(bf16[2,256,1024]{2,1,0:T(8,128)(2,1)S(1)} %get-tuple-element.57), channel_id=1, source_target_pairs={{0,16},{1,9},{2,18},{3,11},{4,20},{5,13},{6,22},{7,15},{8,24},{9,1... | collective-permute-start | bytes 3145736 | tf_op jit(solution)/shard_map/ppermute | solution.py:47
  43.2 25.0 %collective-permute-start.12 = (bf16[2,256,1024]{2,1,0:T(8,128)(2,1)S(1)}, bf16[2,256,1024]{2,1,0:T(8,128)(2,1)S(1)}, u32[]{:S(2)}, u32[]{:S(2)}) collective-permute-start(bf16[2,256,1024]{2,1,0:T(8,128)(2,1)S(1)} %add_convert_fusion.4), channel_id=1, source_target_pairs={{0,2},{1,3},{6,4},{7,5},{8,10},{9,11},{14,12},{15,13},{16,18},{17,... | collective-permute-start | bytes 3145736 | tf_op jit(solution)/shard_map/ppermute | solution.py:47
  47.3 21.3 %collective-permute-start.13 = (bf16[2,1024,256]{2,1,0:T(8,128)(2,1)S(1)}, bf16[2,1024,256]{2,1,0:T(8,128)(2,1)S(1)}, u32[]{:S(2)}, u32[]{:S(2)}) collective-permute-start(bf16[2,1024,256]{2,1,0:T(8,128)(2,1)S(1)} %pad_maximum_fusion.refs_2_.refs_4_), channel_id=1, source_target_pairs={{0,16},{1,9},{2,18},{3,11},{4,20},{5,13},{6,22},{7,15},{8,24},{9,1... | collective-permute-start | bytes 3145736 | tf_op jit(solution)/shard_map/ppermute | solution.py:47
  48.8 24.8 %collective-permute-start.15 = (bf16[2,1024,256]{2,1,0:T(8,128)(2,1)S(1)}, bf16[2,1024,256]{2,1,0:T(8,128)(2,1)S(1)}, u32[]{:S(2)}, u32[]{:S(2)}) collective-permute-start(bf16[2,1024,256]{2,1,0:T(8,128)(2,1)S(1)} %pad_maximum_fusion.1.refs_3_), channel_id=1, source_target_pairs={{2,0},{3,1},{4,6},{5,7},{10,8},{11,9},{12,14},{13,15},{18,16},{19,... | collective-permute-start | bytes 3145736 | tf_op jit(solution)/shard_map/ppermute | solution.py:47
  50.1 23.5 %collective-permute-start.14 = (bf16[2,1024,256]{2,1,0:T(8,128)(2,1)S(1)}, bf16[2,1024,256]{2,1,0:T(8,128)(2,1)S(1)}, u32[]{:S(2)}, u32[]{:S(2)}) collective-permute-start(bf16[2,1024,256]{2,1,0:T(8,128)(2,1)S(1)} %pad_maximum_fusion.refs_2_.refs_4_), channel_id=1, source_target_pairs={{2,4},{3,5},{4,2},{5,3},{10,12},{11,13},{12,10},{13,11},{18,20},{1... | collective-permute-start | bytes 3145736 | tf_op jit(solution)/shard_map/ppermute | solution.py:47
  53.3 31.9 %collective-permute-start.4 = (bf16[2,256,1024]{2,1,0:T(8,128)(2,1)S(1)}, bf16[2,256,1024]{2,1,0:T(8,128)(2,1)}, u32[]{:S(2)}, u32[]{:S(2)}) collective-permute-start(bf16[2,256,1024]{2,1,0:T(8,128)(2,1)S(1)} %get-tuple-element.58), channel_id=1, source_target_pairs={{0,16},{1,9},{2,18},{3,11},{4,20},{5,13},{6,22},{7,15},{8,24},{9,1... | collective-permute-start | bytes 3145736 | tf_op jit(solution)/shard_map/ppermute | solution.py:47
  73.6 24.9 %collective-permute-start.16 = (bf16[2,256,1024]{2,1,0:T(8,128)(2,1)S(1)}, bf16[2,256,1024]{2,1,0:T(8,128)(2,1)}, u32[]{:S(2)}, u32[]{:S(2)}) collective-permute-start(bf16[2,256,1024]{2,1,0:T(8,128)(2,1)S(1)} %add_convert_fusion.6), channel_id=1, source_target_pairs={{0,2},{1,3},{6,4},{7,5},{8,10},{9,11},{14,12},{15,13},{16,18},{17,... | collective-permute-start | bytes 3145736 | tf_op jit(solution)/shard_map/ppermute | solution.py:47
  80.2 20.0 %collective-permute-start.17 = (bf16[2,256,1024]{2,1,0:T(8,128)(2,1)S(1)}, bf16[2,256,1024]{2,1,0:T(8,128)(2,1)}, u32[]{:S(2)}, u32[]{:S(2)}) collective-permute-start(bf16[2,256,1024]{2,1,0:T(8,128)(2,1)S(1)} %add_convert_fusion.3), channel_id=1, source_target_pairs={{2,4},{3,5},{4,2},{5,3},{10,12},{11,13},{12,10},{13,11},{18,20},{1... | collective-permute-start | bytes 3145736 | tf_op jit(solution)/shard_map/ppermute | solution.py:47
  81.9 23.5 %collective-permute-start.20 = (bf16[2,1024,256]{2,1,0:T(8,128)(2,1)S(1)}, bf16[2,1024,256]{2,1,0:T(8,128)(2,1)}, u32[]{:S(2)}, u32[]{:S(2)}) collective-permute-start(bf16[2,1024,256]{2,1,0:T(8,128)(2,1)S(1)} %collective-permute-done.14), channel_id=1, source_target_pairs={{2,0},{3,1},{4,6},{5,7},{10,8},{11,9},{12,14},{13,15},{18,16},{19,... | collective-permute-start | bytes 3145736 | tf_op jit(solution)/shard_map/ppermute | solution.py:47
  83.6 26.6 %collective-permute-start.19 = (bf16[2,1024,256]{2,1,0:T(8,128)(2,1)S(1)}, bf16[2,1024,256]{2,1,0:T(8,128)(2,1)S(1)}, u32[]{:S(2)}, u32[]{:S(2)}) collective-permute-start(bf16[2,1024,256]{2,1,0:T(8,128)(2,1)S(1)} %add.51.refs_4_), channel_id=1, source_target_pairs={{0,16},{1,9},{2,18},{3,11},{4,20},{5,13},{6,22},{7,15},{8,24},{9,1... | collective-permute-start | bytes 3145736 | tf_op jit(solution)/shard_map/ppermute | solution.py:47
  93.5 19.0 %collective-permute-start.18 = (bf16[2,256,1024]{2,1,0:T(8,128)(2,1)S(1)}, bf16[2,256,1024]{2,1,0:T(8,128)(2,1)S(1)}, u32[]{:S(2)}, u32[]{:S(2)}) collective-permute-start(bf16[2,256,1024]{2,1,0:T(8,128)(2,1)S(1)} %get-tuple-element.82), channel_id=1, source_target_pairs={{0,16},{1,9},{2,18},{3,11},{4,20},{5,13},{6,22},{7,15},{8,24},{9,1... | collective-permute-start | bytes 3145736 | tf_op jit(solution)/shard_map/ppermute | solution.py:47
  106.9 15.4 %collective-permute-start.21 = (bf16[2,1024,256]{2,1,0:T(8,128)(2,1)S(1)}, bf16[2,1024,256]{2,1,0:T(8,128)(2,1)S(1)}, u32[]{:S(2)}, u32[]{:S(2)}) collective-permute-start(bf16[2,1024,256]{2,1,0:T(8,128)(2,1)S(1)} %add.52.refs_4_), channel_id=1, source_target_pairs={{0,16},{1,9},{2,18},{3,11},{4,20},{5,13},{6,22},{7,15},{8,24},{9,1... | collective-permute-start | bytes 3145736 | tf_op jit(solution)/shard_map/ppermute | solution.py:47
  109.5 20.6 %collective-permute-start.24 = (bf16[2,256,1024]{2,1,0:T(8,128)(2,1)S(1)}, bf16[2,256,1024]{2,1,0:T(8,128)(2,1)S(1)}, u32[]{:S(2)}, u32[]{:S(2)}) collective-permute-start(bf16[2,256,1024]{2,1,0:T(8,128)(2,1)S(1)} %add_convert_fusion.2), channel_id=1, source_target_pairs={{2,4},{3,5},{4,2},{5,3},{10,12},{11,13},{12,10},{13,11},{18,20},{1... | collective-permute-start | bytes 3145736 | tf_op jit(solution)/shard_map/ppermute | solution.py:47
  110.2 19.4 %collective-permute-start.25 = (bf16[2,256,1024]{2,1,0:T(8,128)(2,1)S(1)}, bf16[2,256,1024]{2,1,0:T(8,128)(2,1)S(1)}, u32[]{:S(2)}, u32[]{:S(2)}) collective-permute-start(bf16[2,256,1024]{2,1,0:T(8,128)(2,1)S(1)} %add_convert_fusion.1), channel_id=1, source_target_pairs={{0,2},{1,3},{2,0},{3,1},{4,6},{5,7},{6,4},{7,5},{8,10},{9,11},{10,... | collective-permute-start | bytes 3145736 | tf_op jit(solution)/shard_map/ppermute | solution.py:47
  129.1 13.7 %collective-permute-start.23 = (f32[384,1024]{1,0:T(8,128)S(1)}, f32[384,1024]{1,0:T(8,128)S(1)}, u32[]{:S(2)}, u32[]{:S(2)}) collective-permute-start(f32[384,1024]{1,0:T(8,128)S(1)} %get-tuple-element.94), channel_id=1, source_target_pairs={{0,1},{1,0},{2,3},{3,2},{4,5},{5,4},{6,7},{7,6},{8,9},{9,8},{10,11... | collective-permute-start | bytes 4718600 | tf_op jit(solution)/shard_map/ppermute | solution.py:47
  129.1 4.5 %collective-permute-start.27 = (bf16[384,1024]{1,0:T(8,128)(2,1)S(1)}, bf16[384,1024]{1,0:T(8,128)(2,1)S(1)}, u32[]{:S(2)}, u32[]{:S(2)}) collective-permute-start(bf16[384,1024]{1,0:T(8,128)(2,1)S(1)} %get-tuple-element.69), channel_id=1, source_target_pairs={{0,1},{1,0},{2,3},{3,2},{4,5},{5,4},{6,7},{7,6},{8,9},{9,8},{10,11... | collective-permute-start | bytes 2359304 | tf_op jit(solution)/shard_map/ppermute | solution.py:47
  129.6 5.1 %collective-permute-start.28 = (bf16[384,1024]{1,0:T(8,128)(2,1)S(1)}, bf16[384,1024]{1,0:T(8,128)(2,1)S(1)}, u32[]{:S(2)}, u32[]{:S(2)}) collective-permute-start(bf16[384,1024]{1,0:T(8,128)(2,1)S(1)} %get-tuple-element.75), channel_id=1, source_target_pairs={{0,1},{1,0},{2,3},{3,2},{4,5},{5,4},{6,7},{7,6},{8,9},{9,8},{10,11... | collective-permute-start | bytes 2359304 | tf_op jit(solution)/shard_map/ppermute | solution.py:47
  129.6 6.3 %collective-permute-start.29 = (bf16[384,1024]{1,0:T(8,128)(2,1)S(1)}, bf16[384,1024]{1,0:T(8,128)(2,1)S(1)}, u32[]{:S(2)}, u32[]{:S(2)}) collective-permute-start(bf16[384,1024]{1,0:T(8,128)(2,1)S(1)} %get-tuple-element.87), channel_id=1, source_target_pairs={{0,1},{1,0},{2,3},{3,2},{4,5},{5,4},{6,7},{7,6},{8,9},{9,8},{10,11... | collective-permute-start | bytes 2359304 | tf_op jit(solution)/shard_map/ppermute | solution.py:47
  130.1 12.7 %collective-permute-start.22 = (bf16[384,1024]{1,0:T(8,128)(2,1)S(1)}, bf16[384,1024]{1,0:T(8,128)(2,1)S(1)}, u32[]{:S(2)}, u32[]{:S(2)}) collective-permute-start(bf16[384,1024]{1,0:T(8,128)(2,1)S(1)} %get-tuple-element.92), channel_id=1, source_target_pairs={{0,1},{1,0},{2,3},{3,2},{4,5},{5,4},{6,7},{7,6},{8,9},{9,8},{10,11... | collective-permute-start | bytes 2359304 | tf_op jit(solution)/shard_map/ppermute | solution.py:47
  133.6 9.2 %collective-permute-start.26 = (bf16[256,1024]{1,0:T(8,128)(2,1)S(1)}, bf16[256,1024]{1,0:T(8,128)(2,1)S(1)}, u32[]{:S(2)}, u32[]{:S(2)}) collective-permute-start(bf16[256,1024]{1,0:T(8,128)(2,1)S(1)} %get-tuple-element.101), channel_id=1, source_target_pairs={{0,8},{1,17},{2,10},{3,19},{4,12},{5,21},{6,14},{7,23},{8,0},{9,25... | collective-permute-start | bytes 1572872 | tf_op jit(solution)/shard_map/ppermute | solution.py:47

commit v17 on v12

--- a/solution.py
+++ b/solution.py
@@ -377,8 +377,9 @@
         two_b,
         (whole, None, keys),
     )
+    got_out0 = sent(out0, SWAP)
     whole, out3, keys, keys_far = projected(
-        place, 3, after(activations, out2), other, cots, three, three_b, (whole, None, keys)
+        place, 3, after(activations, out2, got_out0), other, cots, three, three_b, (whole, None, keys)
     )
     sum_one = after(sum_one, out3)
     last = [
@@ -388,7 +389,7 @@
     whole = laid(
         place,
         whole,
-        (sent(out0, SWAP), sent(out1, SWAP), sent(out2, SWAP)),
+        (got_out0, sent(out1, SWAP), sent(out2, SWAP)),
     )
     grad_input, key_values, grad_weight = finished(
         place,

time: 142 us -> 146 us (1.028)
  waiting for transfers between devices: 44.8 us -> 46.7 us
  starting transfers between devices: 37.1 us -> 38.6 us
    ppermute x27, waiting for transfers between devices: 44.8 us -> 46.7 us  [sent(): return lax.ppermute(array, AXES, pairs)]
    ppermute x27, starting transfers between devices: 37.1 us -> 38.6 us  [sent(): return lax.ppermute(array, AXES, pairs)]
  transfers between devices with their start and end apart: 27 -> 27, of which waited for: 14 -> 10; matrix products, arithmetic and copies ran while one was open for 7% -> 7% of each run, Pallas kernels for 31% -> 30%
where the time goes in v17:
time: 146 us; the launch traced here: 145 us
  waiting for transfers between devices  46.7 us (32%)
  Pallas kernels  45.9 us (31%)
  starting transfers between devices  38.6 us (26%)
  other arithmetic  10.2 us (7%)
  local copies, waits for them, and re-layouts  2.79 us (2%)
    ppermute x27, waiting for transfers between devices, sent(): return lax.ppermute(array, AXES, pairs)  46.7 us
    ppermute x27, starting transfers between devices, sent(): return lax.ppermute(array, AXES, pairs)  38.6 us
    pallas_call x4, Pallas kernels, projected(): pl.pallas_call(lambda *refs: project_kernel(*refs, first=first, last=last...  26.7 us
    pallas_call x1, Pallas kernels, terms(): pl.pallas_call(term_kernel, grid_spec=pltpu.PrefetchScalarGridSpec(num_sc...  8.66 us
    convert_element_type x7, other arithmetic, added(): return total.astype(BF16)  6.51 us
    pallas_call x1, Pallas kernels, first_terms(): pl.pallas_call(first_term_kernel, grid_spec=pltpu.PrefetchScalarGridSpec(...  4.49 us
  transfers between devices with their start and end apart: 27, of which 10 were waited for; matrix products, arithmetic and copies ran while one was open for 7% of the time, Pallas kernels for 30%

profile of v17, /device:TPU:0, one launch (start us, length us, event | category | flops | bytes accessed | tf_op | source)
XLA Modules:
  0.0 145.1 jit_solution(4962116647563513145)
XLA Ops:
  0.6 0.5 collective-permute-start
  1.2 2.9 %collective-permute-start.4 = (bf16[1024,256]{1,0:T(8,128)(2,1)}, bf16[1024,256]{1,0:T(8,128)(2,1)S(1)}, u32[]{:S(2)}, u32[]{:S(2)}) collective-permute-start(bf16[1024,256]{1,0:T(8,128)(2,1)} %param.5), channel_id=1, source_target_pairs={{0,8},{1,17},{2,10},{3,19},{4,12},{5,21},{6,14},{7,23},{8,0},{9,25... | collective-permute-start | bytes 1572872 | tf_op jit(solution)/shard_map/ppermute | solution.py:47
  4.2 7.4 %collective-permute-done.4 = bf16[1024,256]{1,0:T(8,128)(2,1)S(1)} collective-permute-done((bf16[1024,256]{1,0:T(8,128)(2,1)}, bf16[1024,256]{1,0:T(8,128)(2,1)S(1)}, u32[]{:S(2)}, u32[]{:S(2)}) %collective-permute-start.4) | collective-permute-done | bytes 524320 | tf_op jit(solution)/shard_map/ppermute | solution.py:47
  11.5 1.1 pad_maximum_fusion.refs_4_
  12.7 2.2 %collective-permute-start.5 = (bf16[2,1024,256]{2,1,0:T(8,128)(2,1)S(1)}, bf16[2,1024,256]{2,1,0:T(8,128)(2,1)S(1)}, u32[]{:S(2)}, u32[]{:S(2)}) collective-permute-start(bf16[2,1024,256]{2,1,0:T(8,128)(2,1)S(1)} %pad_maximum_fusion.refs_4_), channel_id=1, source_target_pairs={{0,2},{1,3},{2,0},{3,1},{4,6},{5,7},{6,4},{7,5},{8,10},{9,11},{10,... | collective-permute-start | bytes 3145736 | tf_op jit(solution)/shard_map/ppermute | solution.py:47
  14.9 1.5 %collective-permute-start.7 = (bf16[2,1024,256]{2,1,0:T(8,128)(2,1)S(1)}, bf16[2,1024,256]{2,1,0:T(8,128)(2,1)S(1)}, u32[]{:S(2)}, u32[]{:S(2)}) collective-permute-start(bf16[2,1024,256]{2,1,0:T(8,128)(2,1)S(1)} %pad_maximum_fusion.refs_4_), channel_id=1, source_target_pairs={{0,16},{1,9},{2,18},{3,11},{4,20},{5,13},{6,22},{7,15},{8,24},{9,1... | collective-permute-start | bytes 3145736 | tf_op jit(solution)/shard_map/ppermute | solution.py:47
  16.4 0.7 collective-permute-start.6
  17.2 2.8 %copy-done = bf16[384,8192]{1,0:T(8,128)(2,1)S(1)} copy-done((bf16[384,8192]{1,0:T(8,128)(2,1)S(1)}, bf16[384,8192]{1,0:T(8,128)(2,1)}, u32[]{:S(2)}) %copy-start) | copy-done | bytes 6291480
  20.0 4.5 %terms.2 = (bf16[2,256,1024]{2,1,0:T(8,128)(2,1)S(1)}, bf16[2,256,1024]{2,1,0:T(8,128)(2,1)S(1)}, bf16[768,1024]{1,0:T(8,128)(2,1)S(1)}, bf16[1024,768]{1,0:T(8,128)(2,1)S(1)}) custom-call(s32[3]{0:T(128)S(1)} %pad_add_fusion.place.refs_0_, bf16[384,8192]{1,0:T(8,128)(2,1)S(1)} %copy-done, bf16[384,8192]{1,0:T(8,128)(2,1)} %collective-permute-done.other.refs_2_, ...), custom_call_target="tpu_custom_call" | custom-call | flops 1610612 | bytes 5767 | tf_op jit(solution)/shard_map/terms/pallas_call | solution.py:107
  24.5 0.6 collective-permute-start.8
  25.1 8.7 %terms.3 = (bf16[2,256,1024]{2,1,0:T(8,128)(2,1)S(1)}, bf16[2,256,1024]{2,1,0:T(8,128)(2,1)S(1)}, bf16[2,256,1024]{2,1,0:T(8,128)(2,1)S(1)}, bf16[2,256,1024]{2,...) custom-call(s32[3]{0:T(128)S(1)} %pad_add_fusion.place.refs_0_, ...), custom_call_target="tpu_custom_call" | custom-call | flops 4831838 | bytes 17301 | tf_op jit(solution)/shard_map/terms/pallas_call | solution.py:149
  33.7 1.6 %collective-permute-start.2 = (bf16[2,256,1024]{2,1,0:T(8,128)(2,1)S(1)}, bf16[2,256,1024]{2,1,0:T(8,128)(2,1)S(1)}, u32[]{:S(2)}, u32[]{:S(2)}) collective-permute-start(bf16[2,256,1024]{2,1,0:T(8,128)(2,1)S(1)} %get-tuple-element.51), channel_id=1, source_target_pairs={{0,16},{1,9},{2,18},{3,11},{4,20},{5,13},{6,22},{7,15},{8,24},{9,1... | collective-permute-start | bytes 3145736 | tf_op jit(solution)/shard_map/ppermute | solution.py:47
  35.3 2.1 %collective-permute-done.5.refs_1_.refs_4_ = bf16[2,1024,256]{2,1,0:T(8,128)(2,1)S(1)} collective-permute-done((bf16[2,1024,256]{2,1,0:T(8,128)(2,1)S(1)}, bf16[2,1024,256]{2,1,0:T(8,128)(2,1)S(1)}, u32[]{:S(2)}, u32[]{:S(2)}) %collective-permute-start.5) | collective-permute-done | bytes 1048608 | tf_op jit(solution)/shard_map/ppermute | solution.py:47
  37.4 1.1 gate.1.refs_0_
  38.5 2.4 %collective-permute-done.8 = bf16[2,256,1024]{2,1,0:T(8,128)(2,1)S(1)} collective-permute-done((bf16[2,256,1024]{2,1,0:T(8,128)(2,1)S(1)}, bf16[2,256,1024]{2,1,0:T(8,128)(2,1)S(1)}, u32[]{:S(2)}, u32[]{:S(2)}) %collective-permute-start.8) | collective-permute-done | bytes 1048608 | tf_op jit(solution)/shard_map/ppermute | solution.py:47
  41.4 6.6 %collective-permute-start.9 = (bf16[2,256,1024]{2,1,0:T(8,128)(2,1)S(1)}, bf16[2,256,1024]{2,1,0:T(8,128)(2,1)}, u32[]{:S(2)}, u32[]{:S(2)}) collective-permute-start(bf16[2,256,1024]{2,1,0:T(8,128)(2,1)S(1)} %add_convert_fusion.4), channel_id=1, source_target_pairs={{0,2},{1,3},{6,4},{7,5},{8,10},{9,11},{14,12},{15,13},{16,18},{17,... | collective-permute-start | bytes 3145736 | tf_op jit(solution)/shard_map/ppermute | solution.py:47
  48.0 1.6 %collective-permute-start.10 = (bf16[2,1024,256]{2,1,0:T(8,128)(2,1)S(1)}, bf16[2,1024,256]{2,1,0:T(8,128)(2,1)}, u32[]{:S(2)}, u32[]{:S(2)}) collective-permute-start(bf16[2,1024,256]{2,1,0:T(8,128)(2,1)S(1)} %collective-permute-done.5.refs_1_.refs_4_), channel_id=1, source_target_pairs={{2,4},{3,5},{4,2},{5,3},{10,12},{11,13},{12,10},{13,11},{18,20},{1... | collective-permute-start | bytes 3145736 | tf_op jit(solution)/shard_map/ppermute | solution.py:47
  49.6 1.3 collective-permute-start.11
  50.9 1.6 %collective-permute-start.12 = (bf16[2,1024,256]{2,1,0:T(8,128)(2,1)S(1)}, bf16[2,1024,256]{2,1,0:T(8,128)(2,1)S(1)}, u32[]{:S(2)}, u32[]{:S(2)}) collective-permute-start(bf16[2,1024,256]{2,1,0:T(8,128)(2,1)S(1)} %collective-permute-done.5.refs_1_.refs_4_), channel_id=1, source_target_pairs={{0,16},{1,9},{2,18},{3,11},{4,20},{5,13},{6,22},{7,15},{8,24},{9,1... | collective-permute-start | bytes 3145736 | tf_op jit(solution)/shard_map/ppermute | solution.py:47
  52.5 0.4 add_convert_fusion.6
  52.9 1.3 collective-permute-start.3
  54.2 6.5 %project.4 = (bf16[384,8192]{1,0:T(8,128)(2,1)}, bf16[384,1024]{1,0:T(8,128)(2,1)S(1)}, f32[768,1024]{1,0:T(8,128)S(1)}) custom-call(s32[3]{0:T(128)S(1)} %gate.1.refs_0_, bf16[384,8192]{1,0:T(8,128)(2,1)S(1)} %copy-done.1, bf16[384,8192]{1,0:T(8,128)(2,1)} %collective-permute-done.other.refs_2_, bf16[768,1024]{1,0:T(8,128)(2,1)S(1)} %get-tuple-element.59.refs_3_, ...), custom_call_target="tpu_custom_call" | custom-call | flops 3221225 | bytes 8388 | tf_op jit(solution)/shard_map/project/pallas_call | solution.py:216
  60.7 6.8 %collective-permute-done.9 = bf16[2,256,1024]{2,1,0:T(8,128)(2,1)} collective-permute-done((bf16[2,256,1024]{2,1,0:T(8,128)(2,1)S(1)}, bf16[2,256,1024]{2,1,0:T(8,128)(2,1)}, u32[]{:S(2)}, u32[]{:S(2)}) %collective-permute-start.9) | collective-permute-done | bytes 1048608 | tf_op jit(solution)/shard_map/ppermute | solution.py:47
  67.5 1.6 %add_convert_fusion.3 = bf16[2,256,1024]{2,1,0:T(8,128)(2,1)S(1)} fusion(bf16[2,256,1024]{2,1,0:T(8,128)(2,1)} %collective-permute-done.9, bf16[2,256,1024]{2,1,0:T(8,128)(2,1)S(1)} %add_convert_fusion.6), kind=kLoop, calls=%fused_computation.3 | loop fusion | flops 2097152 | bytes 3145728 | tf_op jit(solution)/shard_map/convert_element_type | solution.py:319
  69.1 5.2 %collective-permute-done.11 = bf16[2,1024,256]{2,1,0:T(8,128)(2,1)S(1)} collective-permute-done((bf16[2,1024,256]{2,1,0:T(8,128)(2,1)S(1)}, bf16[2,1024,256]{2,1,0:T(8,128)(2,1)S(1)}, u32[]{:S(2)}, u32[]{:S(2)}) %collective-permute-start.11) | collective-permute-done | bytes 1048608 | tf_op jit(solution)/shard_map/ppermute | solution.py:47
  74.3 2.5 %collective-permute-start.13 = (bf16[2,256,1024]{2,1,0:T(8,128)(2,1)S(1)}, bf16[2,256,1024]{2,1,0:T(8,128)(2,1)}, u32[]{:S(2)}, u32[]{:S(2)}) collective-permute-start(bf16[2,256,1024]{2,1,0:T(8,128)(2,1)S(1)} %add_convert_fusion.6), channel_id=1, source_target_pairs={{0,2},{1,3},{6,4},{7,5},{8,10},{9,11},{14,12},{15,13},{16,18},{17,... | collective-permute-start | bytes 3145736 | tf_op jit(solution)/shard_map/ppermute | solution.py:47
  76.8 1.7 %collective-permute-start.14 = (bf16[2,256,1024]{2,1,0:T(8,128)(2,1)S(1)}, bf16[2,256,1024]{2,1,0:T(8,128)(2,1)}, u32[]{:S(2)}, u32[]{:S(2)}) collective-permute-start(bf16[2,256,1024]{2,1,0:T(8,128)(2,1)S(1)} %add_convert_fusion.3), channel_id=1, source_target_pairs={{2,4},{3,5},{4,2},{5,3},{10,12},{11,13},{12,10},{13,11},{18,20},{1... | collective-permute-start | bytes 3145736 | tf_op jit(solution)/shard_map/ppermute | solution.py:47
  78.5 1.5 %collective-permute-start.18 = (bf16[2,1024,256]{2,1,0:T(8,128)(2,1)}, bf16[2,1024,256]{2,1,0:T(8,128)(2,1)S(1)}, u32[]{:S(2)}, u32[]{:S(2)}) collective-permute-start(bf16[2,1024,256]{2,1,0:T(8,128)(2,1)} %collective-permute-done.10), channel_id=1, source_target_pairs={{2,0},{3,1},{4,6},{5,7},{10,8},{11,9},{12,14},{13,15},{18,16},{19,... | collective-permute-start | bytes 3145736 | tf_op jit(solution)/shard_map/ppermute | solution.py:47
  80.4 2.7 %collective-permute-start.15 = (bf16[2,256,1024]{2,1,0:T(8,128)(2,1)S(1)}, bf16[2,256,1024]{2,1,0:T(8,128)(2,1)S(1)}, u32[]{:S(2)}, u32[]{:S(2)}) collective-permute-start(bf16[2,256,1024]{2,1,0:T(8,128)(2,1)S(1)} %get-tuple-element.72), channel_id=1, source_target_pairs={{0,16},{1,9},{2,18},{3,11},{4,20},{5,13},{6,22},{7,15},{8,24},{9,1... | collective-permute-start | bytes 3145736 | tf_op jit(solution)/shard_map/ppermute | solution.py:47
  83.0 1.5 %add.51.refs_4_ = bf16[2,1024,256]{2,1,0:T(8,128)(2,1)S(1)} add(bf16[2,1024,256]{2,1,0:T(8,128)(2,1)} %collective-permute-done.10, bf16[2,1024,256]{2,1,0:T(8,128)(2,1)S(1)} %collective-permute-done.11) | non-fusion elementwise | flops 524288 | bytes 3145728 | tf_op jit(solution)/shard_map/add | solution.py:355
  84.7 6.7 %project.5 = (bf16[384,8192]{1,0:T(8,128)(2,1)}, bf16[384,1024]{1,0:T(8,128)(2,1)S(1)}, f32[768,1024]{1,0:T(8,128)S(1)}) custom-call(s32[3]{0:T(128)S(1)} %pad_add_fusion.place.refs_0_, bf16[384,8192]{1,0:T(8,128)(2,1)S(1)} %copy-done.1, bf16[384,8192]{1,0:T(8,128)(2,1)} %collective-permute-done.other.refs_2_, ...), custom_call_target="tpu_custom_call", output_to_operand_aliasing={{0}: (7, {})} | custom-call | flops 3221225 | bytes 8388 | tf_op jit(solution)/shard_map/project/pallas_call | solution.py:216
  91.3 3.9 %collective-permute-done.13 = bf16[2,256,1024]{2,1,0:T(8,128)(2,1)} collective-permute-done((bf16[2,256,1024]{2,1,0:T(8,128)(2,1)S(1)}, bf16[2,256,1024]{2,1,0:T(8,128)(2,1)}, u32[]{:S(2)}, u32[]{:S(2)}) %collective-permute-start.13) | collective-permute-done | bytes 1048608 | tf_op jit(solution)/shard_map/ppermute | solution.py:47
  95.2 1.6 %add_convert_fusion.2 = bf16[2,256,1024]{2,1,0:T(8,128)(2,1)S(1)} fusion(bf16[2,256,1024]{2,1,0:T(8,128)(2,1)} %collective-permute-done.13, bf16[2,256,1024]{2,1,0:T(8,128)(2,1)S(1)} %add_convert_fusion.4), kind=kLoop, calls=%fused_computation.2 | loop fusion | flops 2097152 | bytes 3145728 | tf_op jit(solution)/shard_map/convert_element_type | solution.py:319
  96.9 1.6 %add_convert_fusion.1 = bf16[2,256,1024]{2,1,0:T(8,128)(2,1)S(1)} fusion(bf16[2,256,1024]{2,1,0:T(8,128)(2,1)} %collective-permute-done.14, bf16[2,256,1024]{2,1,0:T(8,128)(2,1)S(1)} %add_convert_fusion.5), kind=kLoop, calls=%fused_computation.1 | loop fusion | flops 2097152 | bytes 3145728 | tf_op jit(solution)/shard_map/convert_element_type | solution.py:319
  98.5 3.8 %collective-permute-done.18 = bf16[2,1024,256]{2,1,0:T(8,128)(2,1)S(1)} collective-permute-done((bf16[2,1024,256]{2,1,0:T(8,128)(2,1)}, bf16[2,1024,256]{2,1,0:T(8,128)(2,1)S(1)}, u32[]{:S(2)}, u32[]{:S(2)}) %collective-permute-start.18) | collective-permute-done | bytes 1048608 | tf_op jit(solution)/shard_map/ppermute | solution.py:47
  102.6 3.7 %collective-permute-start.19 = (bf16[2,1024,256]{2,1,0:T(8,128)(2,1)S(1)}, bf16[2,1024,256]{2,1,0:T(8,128)(2,1)S(1)}, u32[]{:S(2)}, u32[]{:S(2)}) collective-permute-start(bf16[2,1024,256]{2,1,0:T(8,128)(2,1)S(1)} %add.52.refs_4_), channel_id=1, source_target_pairs={{0,16},{1,9},{2,18},{3,11},{4,20},{5,13},{6,22},{7,15},{8,24},{9,1... | collective-permute-start | bytes 3145736 | tf_op jit(solution)/shard_map/ppermute | solution.py:47
  106.3 0.7 collective-permute-start.22
  107.0 2.7 %collective-permute-start.23 = (bf16[2,256,1024]{2,1,0:T(8,128)(2,1)S(1)}, bf16[2,256,1024]{2,1,0:T(8,128)(2,1)S(1)}, u32[]{:S(2)}, u32[]{:S(2)}) collective-permute-start(bf16[2,256,1024]{2,1,0:T(8,128)(2,1)S(1)} %add_convert_fusion.1), channel_id=1, source_target_pairs={{0,2},{1,3},{2,0},{3,1},{4,6},{5,7},{6,4},{7,5},{8,10},{9,11},{10,... | collective-permute-start | bytes 3145736 | tf_op jit(solution)/shard_map/ppermute | solution.py:47
  109.8 0.4 add_convert_fusion
  110.2 6.7 %project.6 = (bf16[384,8192]{1,0:T(8,128)(2,1)}, bf16[384,1024]{1,0:T(8,128)(2,1)S(1)}, f32[768,1024]{1,0:T(8,128)S(1)}) custom-call(s32[3]{0:T(128)S(1)} %pad_add_fusion.place.refs_0_, bf16[384,8192]{1,0:T(8,128)(2,1)S(1)} %copy-done.1, bf16[384,8192]{1,0:T(8,128)(2,1)} %collective-permute-done.other.refs_2_, ...), custom_call_target="tpu_custom_call", output_to_operand_aliasing={{0}: (7, {})} | custom-call | flops 3221225 | bytes 8388 | tf_op jit(solution)/shard_map/project/pallas_call | solution.py:216
  116.9 2.2 %collective-permute-done.19.refs_5_ = bf16[2,1024,256]{2,1,0:T(8,128)(2,1)S(1)} collective-permute-done((bf16[2,1024,256]{2,1,0:T(8,128)(2,1)S(1)}, bf16[2,1024,256]{2,1,0:T(8,128)(2,1)S(1)}, u32[]{:S(2)}, u32[]{:S(2)}) %collective-permute-start.19) | collective-permute-done | bytes 1048608 | tf_op jit(solution)/shard_map/ppermute | solution.py:47
  119.1 6.8 %project.7 = (bf16[384,8192]{1,0:T(8,128)(2,1)}, bf16[384,1024]{1,0:T(8,128)(2,1)S(1)}, f32[384,1024]{1,0:T(8,128)S(1)}, f32[384,1024]{1,0:T(8,128)S(1)}) custom-call(s32[3]{0:T(128)S(1)} %pad_add_fusion.place.refs_0_, bf16[384,8192]{1,0:T(8,128)(2,1)S(1)} %copy-done.1, ...), custom_call_target="tpu_custom_call", output_to_operand_aliasing={{0}: (7, {})} | custom-call | flops 3221225 | bytes 8388 | tf_op jit(solution)/shard_map/project/pallas_call | solution.py:216
  125.9 0.5 collective-permute-start.25
  126.4 6.2 %collective-permute-done.23 = bf16[2,256,1024]{2,1,0:T(8,128)(2,1)S(1)} collective-permute-done((bf16[2,256,1024]{2,1,0:T(8,128)(2,1)S(1)}, bf16[2,256,1024]{2,1,0:T(8,128)(2,1)S(1)}, u32[]{:S(2)}, u32[]{:S(2)}) %collective-permute-start.23) | collective-permute-done | bytes 1048608 | tf_op jit(solution)/shard_map/ppermute | solution.py:47
  132.7 0.6 fusion
  133.4 2.5 %lay.1.refs_6_ = bf16[384,8192]{1,0:T(8,128)(2,1)} custom-call(s32[3]{0:T(128)S(1)} %pad_add_fusion.place.refs_0_, bf16[384,1024]{1,0:T(8,128)(2,1)S(1)} %collective-permute-done.17.refs_0_, bf16[384,1024]{1,0:T(8,128)(2,1)S(1)} %collective-permute-done.25.refs_1_, ...), custom_call_target="tpu_custom_call", output_to_operand_aliasing={{}: (4, {})} | custom-call | bytes 4718 | tf_op jit(solution)/shard_map/lay/pallas_call | solution.py:255
  135.9 6.7 %collective-permute-done.24.refs_5_ = bf16[256,1024]{1,0:T(8,128)(2,1)S(1)} collective-permute-done((bf16[256,1024]{1,0:T(8,128)(2,1)S(1)}, bf16[256,1024]{1,0:T(8,128)(2,1)S(1)}, u32[]{:S(2)}, u32[]{:S(2)}) %collective-permute-start.24) | collective-permute-done | bytes 524320 | tf_op jit(solution)/shard_map/ppermute | solution.py:47
  142.6 2.5 %finish.1 = (bf16[384,8192]{1,0:T(8,128)(2,1)}, bf16[384,1024]{1,0:T(8,128)(2,1)}, bf16[1024,256]{1,0:T(8,128)(2,1)}) custom-call(s32[3]{0:T(128)S(1)} %pad_add_fusion.place.refs_0_, bf16[384,1024]{1,0:T(8,128)(2,1)S(1)} %collective-permute-done.20.refs_1_, f32[384,1024]{1,0:T(8,128)S(1)} %get-tuple-element.83.refs_2_, ...), custom_call_target="tpu_custom_call", output_to_operand_aliasing={{0}: (6, {})} | custom-call | bytes 5505 | tf_op jit(solution)/shard_map/finish/pallas_call | solution.py:284
  (33 shorter events, 1.5 us)
Async XLA Ops:
  0.6 16.6 %copy-start.2 = (bf16[384,1024]{1,0:T(8,128)(2,1)S(1)}, bf16[384,1024]{1,0:T(8,128)(2,1)}, u32[]{:S(2)}) copy-start(bf16[384,1024]{1,0:T(8,128)(2,1)} %cot_mine.1) | copy-start | bytes 2359300
  0.6 16.5 %collective-permute-start = (bf16[384,8192]{1,0:T(8,128)(2,1)}, bf16[384,8192]{1,0:T(8,128)(2,1)}, u32[]{:S(2)}, u32[]{:S(2)}) collective-permute-start(bf16[384,8192]{1,0:T(8,128)(2,1)} %refs_1_.3), channel_id=1, source_target_pairs={{0,1},{1,0},{2,3},{3,2},{4,5},{5,4},{6,7},{7,6},{8,9},{9,8},{10,11... | collective-permute-start | bytes 18874376 | tf_op jit(solution)/shard_map/ppermute | solution.py:47
  1.2 16.0 %collective-permute-start.1 = (bf16[384,1024]{1,0:T(8,128)(2,1)}, bf16[384,1024]{1,0:T(8,128)(2,1)S(1)}, u32[]{:S(2)}, u32[]{:S(2)}) collective-permute-start(bf16[384,1024]{1,0:T(8,128)(2,1)} %cot_mine.1), channel_id=1, source_target_pairs={{0,1},{1,0},{2,3},{3,2},{4,5},{5,4},{6,7},{7,6},{8,9},{9,8},{10,11... | collective-permute-start | bytes 2359304 | tf_op jit(solution)/shard_map/ppermute | solution.py:47
  1.2 10.3 %collective-permute-start.4 = (bf16[1024,256]{1,0:T(8,128)(2,1)}, bf16[1024,256]{1,0:T(8,128)(2,1)S(1)}, u32[]{:S(2)}, u32[]{:S(2)}) collective-permute-start(bf16[1024,256]{1,0:T(8,128)(2,1)} %param.5), channel_id=1, source_target_pairs={{0,8},{1,17},{2,10},{3,19},{4,12},{5,21},{6,14},{7,23},{8,0},{9,25... | collective-permute-start | bytes 1572872 | tf_op jit(solution)/shard_map/ppermute | solution.py:47
  12.7 24.7 %collective-permute-start.5 = (bf16[2,1024,256]{2,1,0:T(8,128)(2,1)S(1)}, bf16[2,1024,256]{2,1,0:T(8,128)(2,1)S(1)}, u32[]{:S(2)}, u32[]{:S(2)}) collective-permute-start(bf16[2,1024,256]{2,1,0:T(8,128)(2,1)S(1)} %pad_maximum_fusion.refs_4_), channel_id=1, source_target_pairs={{0,2},{1,3},{2,0},{3,1},{4,6},{5,7},{6,4},{7,5},{8,10},{9,11},{10,... | collective-permute-start | bytes 3145736 | tf_op jit(solution)/shard_map/ppermute | solution.py:47
  14.9 22.5 %collective-permute-start.7 = (bf16[2,1024,256]{2,1,0:T(8,128)(2,1)S(1)}, bf16[2,1024,256]{2,1,0:T(8,128)(2,1)S(1)}, u32[]{:S(2)}, u32[]{:S(2)}) collective-permute-start(bf16[2,1024,256]{2,1,0:T(8,128)(2,1)S(1)} %pad_maximum_fusion.refs_4_), channel_id=1, source_target_pairs={{0,16},{1,9},{2,18},{3,11},{4,20},{5,13},{6,22},{7,15},{8,24},{9,1... | collective-permute-start | bytes 3145736 | tf_op jit(solution)/shard_map/ppermute | solution.py:47
  16.4 21.0 %collective-permute-start.6 = (bf16[2,1024,256]{2,1,0:T(8,128)(2,1)S(1)}, bf16[2,1024,256]{2,1,0:T(8,128)(2,1)S(1)}, u32[]{:S(2)}, u32[]{:S(2)}) collective-permute-start(bf16[2,1024,256]{2,1,0:T(8,128)(2,1)S(1)} %pad_maximum_fusion.refs_4_), channel_id=1, source_target_pairs={{2,4},{3,5},{4,2},{5,3},{10,12},{11,13},{12,10},{13,11},{18,20},{1... | collective-permute-start | bytes 3145736 | tf_op jit(solution)/shard_map/ppermute | solution.py:47
  17.2 2.8 %copy-start = (bf16[384,8192]{1,0:T(8,128)(2,1)S(1)}, bf16[384,8192]{1,0:T(8,128)(2,1)}, u32[]{:S(2)}) copy-start(bf16[384,8192]{1,0:T(8,128)(2,1)} %refs_1_.3) | copy-start | bytes 18874372
  20.0 5.1 %copy-start.1 = (bf16[384,8192]{1,0:T(8,128)(2,1)S(1)}, bf16[384,8192]{1,0:T(8,128)(2,1)}, u32[]{:S(2)}) copy-start(bf16[384,8192]{1,0:T(8,128)(2,1)} %refs_1_.3) | copy-start | bytes 18874372
  24.5 16.5 %collective-permute-start.8 = (bf16[2,256,1024]{2,1,0:T(8,128)(2,1)S(1)}, bf16[2,256,1024]{2,1,0:T(8,128)(2,1)S(1)}, u32[]{:S(2)}, u32[]{:S(2)}) collective-permute-start(bf16[2,256,1024]{2,1,0:T(8,128)(2,1)S(1)} %get-tuple-element.57), channel_id=1, source_target_pairs={{0,16},{1,9},{2,18},{3,11},{4,20},{5,13},{6,22},{7,15},{8,24},{9,1... | collective-permute-start | bytes 3145736 | tf_op jit(solution)/shard_map/ppermute | solution.py:47
  33.7 18.8 %collective-permute-start.2 = (bf16[2,256,1024]{2,1,0:T(8,128)(2,1)S(1)}, bf16[2,256,1024]{2,1,0:T(8,128)(2,1)S(1)}, u32[]{:S(2)}, u32[]{:S(2)}) collective-permute-start(bf16[2,256,1024]{2,1,0:T(8,128)(2,1)S(1)} %get-tuple-element.51), channel_id=1, source_target_pairs={{0,16},{1,9},{2,18},{3,11},{4,20},{5,13},{6,22},{7,15},{8,24},{9,1... | collective-permute-start | bytes 3145736 | tf_op jit(solution)/shard_map/ppermute | solution.py:47
  41.4 26.1 %collective-permute-start.9 = (bf16[2,256,1024]{2,1,0:T(8,128)(2,1)S(1)}, bf16[2,256,1024]{2,1,0:T(8,128)(2,1)}, u32[]{:S(2)}, u32[]{:S(2)}) collective-permute-start(bf16[2,256,1024]{2,1,0:T(8,128)(2,1)S(1)} %add_convert_fusion.4), channel_id=1, source_target_pairs={{0,2},{1,3},{6,4},{7,5},{8,10},{9,11},{14,12},{15,13},{16,18},{17,... | collective-permute-start | bytes 3145736 | tf_op jit(solution)/shard_map/ppermute | solution.py:47
  48.0 21.1 %collective-permute-start.10 = (bf16[2,1024,256]{2,1,0:T(8,128)(2,1)S(1)}, bf16[2,1024,256]{2,1,0:T(8,128)(2,1)}, u32[]{:S(2)}, u32[]{:S(2)}) collective-permute-start(bf16[2,1024,256]{2,1,0:T(8,128)(2,1)S(1)} %collective-permute-done.5.refs_1_.refs_4_), channel_id=1, source_target_pairs={{2,4},{3,5},{4,2},{5,3},{10,12},{11,13},{12,10},{13,11},{18,20},{1... | collective-permute-start | bytes 3145736 | tf_op jit(solution)/shard_map/ppermute | solution.py:47
  49.6 24.7 %collective-permute-start.11 = (bf16[2,1024,256]{2,1,0:T(8,128)(2,1)S(1)}, bf16[2,1024,256]{2,1,0:T(8,128)(2,1)S(1)}, u32[]{:S(2)}, u32[]{:S(2)}) collective-permute-start(bf16[2,1024,256]{2,1,0:T(8,128)(2,1)S(1)} %collective-permute-done.6.refs_2_), channel_id=1, source_target_pairs={{2,0},{3,1},{4,6},{5,7},{10,8},{11,9},{12,14},{13,15},{18,16},{19,... | collective-permute-start | bytes 3145736 | tf_op jit(solution)/shard_map/ppermute | solution.py:47
  50.9 23.4 %collective-permute-start.12 = (bf16[2,1024,256]{2,1,0:T(8,128)(2,1)S(1)}, bf16[2,1024,256]{2,1,0:T(8,128)(2,1)S(1)}, u32[]{:S(2)}, u32[]{:S(2)}) collective-permute-start(bf16[2,1024,256]{2,1,0:T(8,128)(2,1)S(1)} %collective-permute-done.5.refs_1_.refs_4_), channel_id=1, source_target_pairs={{0,16},{1,9},{2,18},{3,11},{4,20},{5,13},{6,22},{7,15},{8,24},{9,1... | collective-permute-start | bytes 3145736 | tf_op jit(solution)/shard_map/ppermute | solution.py:47
  52.9 27.0 %collective-permute-start.3 = (bf16[2,256,1024]{2,1,0:T(8,128)(2,1)S(1)}, bf16[2,256,1024]{2,1,0:T(8,128)(2,1)S(1)}, u32[]{:S(2)}, u32[]{:S(2)}) collective-permute-start(bf16[2,256,1024]{2,1,0:T(8,128)(2,1)S(1)} %get-tuple-element.52), channel_id=1, source_target_pairs={{0,16},{1,9},{2,18},{3,11},{4,20},{5,13},{6,22},{7,15},{8,24},{9,1... | collective-permute-start | bytes 3145736 | tf_op jit(solution)/shard_map/ppermute | solution.py:47
  74.3 20.9 %collective-permute-start.13 = (bf16[2,256,1024]{2,1,0:T(8,128)(2,1)S(1)}, bf16[2,256,1024]{2,1,0:T(8,128)(2,1)}, u32[]{:S(2)}, u32[]{:S(2)}) collective-permute-start(bf16[2,256,1024]{2,1,0:T(8,128)(2,1)S(1)} %add_convert_fusion.6), channel_id=1, source_target_pairs={{0,2},{1,3},{6,4},{7,5},{8,10},{9,11},{14,12},{15,13},{16,18},{17,... | collective-permute-start | bytes 3145736 | tf_op jit(solution)/shard_map/ppermute | solution.py:47
  76.8 20.0 %collective-permute-start.14 = (bf16[2,256,1024]{2,1,0:T(8,128)(2,1)S(1)}, bf16[2,256,1024]{2,1,0:T(8,128)(2,1)}, u32[]{:S(2)}, u32[]{:S(2)}) collective-permute-start(bf16[2,256,1024]{2,1,0:T(8,128)(2,1)S(1)} %add_convert_fusion.3), channel_id=1, source_target_pairs={{2,4},{3,5},{4,2},{5,3},{10,12},{11,13},{12,10},{13,11},{18,20},{1... | collective-permute-start | bytes 3145736 | tf_op jit(solution)/shard_map/ppermute | solution.py:47
  78.5 23.8 %collective-permute-start.18 = (bf16[2,1024,256]{2,1,0:T(8,128)(2,1)}, bf16[2,1024,256]{2,1,0:T(8,128)(2,1)S(1)}, u32[]{:S(2)}, u32[]{:S(2)}) collective-permute-start(bf16[2,1024,256]{2,1,0:T(8,128)(2,1)} %collective-permute-done.10), channel_id=1, source_target_pairs={{2,0},{3,1},{4,6},{5,7},{10,8},{11,9},{12,14},{13,15},{18,16},{19,... | collective-permute-start | bytes 3145736 | tf_op jit(solution)/shard_map/ppermute | solution.py:47
  80.4 29.4 %collective-permute-start.15 = (bf16[2,256,1024]{2,1,0:T(8,128)(2,1)S(1)}, bf16[2,256,1024]{2,1,0:T(8,128)(2,1)S(1)}, u32[]{:S(2)}, u32[]{:S(2)}) collective-permute-start(bf16[2,256,1024]{2,1,0:T(8,128)(2,1)S(1)} %get-tuple-element.72), channel_id=1, source_target_pairs={{0,16},{1,9},{2,18},{3,11},{4,20},{5,13},{6,22},{7,15},{8,24},{9,1... | collective-permute-start | bytes 3145736 | tf_op jit(solution)/shard_map/ppermute | solution.py:47
  84.6 22.5 %collective-permute-start.16 = (bf16[2,1024,256]{2,1,0:T(8,128)(2,1)S(1)}, bf16[2,1024,256]{2,1,0:T(8,128)(2,1)S(1)}, u32[]{:S(2)}, u32[]{:S(2)}) collective-permute-start(bf16[2,1024,256]{2,1,0:T(8,128)(2,1)S(1)} %add.51.refs_4_), channel_id=1, source_target_pairs={{0,16},{1,9},{2,18},{3,11},{4,20},{5,13},{6,22},{7,15},{8,24},{9,1... | collective-permute-start | bytes 3145736 | tf_op jit(solution)/shard_map/ppermute | solution.py:47
  102.6 16.5 %collective-permute-start.19 = (bf16[2,1024,256]{2,1,0:T(8,128)(2,1)S(1)}, bf16[2,1024,256]{2,1,0:T(8,128)(2,1)S(1)}, u32[]{:S(2)}, u32[]{:S(2)}) collective-permute-start(bf16[2,1024,256]{2,1,0:T(8,128)(2,1)S(1)} %add.52.refs_4_), channel_id=1, source_target_pairs={{0,16},{1,9},{2,18},{3,11},{4,20},{5,13},{6,22},{7,15},{8,24},{9,1... | collective-permute-start | bytes 3145736 | tf_op jit(solution)/shard_map/ppermute | solution.py:47
  106.3 10.6 %collective-permute-start.17 = (bf16[384,1024]{1,0:T(8,128)(2,1)S(1)}, bf16[384,1024]{1,0:T(8,128)(2,1)S(1)}, u32[]{:S(2)}, u32[]{:S(2)}) collective-permute-start(bf16[384,1024]{1,0:T(8,128)(2,1)S(1)} %get-tuple-element.60), channel_id=1, source_target_pairs={{0,1},{1,0},{2,3},{3,2},{4,5},{5,4},{6,7},{7,6},{8,9},{9,8},{10,11... | collective-permute-start | bytes 2359304 | tf_op jit(solution)/shard_map/ppermute | solution.py:47
  106.3 26.4 %collective-permute-start.22 = (bf16[2,256,1024]{2,1,0:T(8,128)(2,1)S(1)}, bf16[2,256,1024]{2,1,0:T(8,128)(2,1)S(1)}, u32[]{:S(2)}, u32[]{:S(2)}) collective-permute-start(bf16[2,256,1024]{2,1,0:T(8,128)(2,1)S(1)} %add_convert_fusion.2), channel_id=1, source_target_pairs={{2,4},{3,5},{4,2},{5,3},{10,12},{11,13},{12,10},{13,11},{18,20},{1... | collective-permute-start | bytes 3145736 | tf_op jit(solution)/shard_map/ppermute | solution.py:47
  107.0 25.6 %collective-permute-start.23 = (bf16[2,256,1024]{2,1,0:T(8,128)(2,1)S(1)}, bf16[2,256,1024]{2,1,0:T(8,128)(2,1)S(1)}, u32[]{:S(2)}, u32[]{:S(2)}) collective-permute-start(bf16[2,256,1024]{2,1,0:T(8,128)(2,1)S(1)} %add_convert_fusion.1), channel_id=1, source_target_pairs={{0,2},{1,3},{2,0},{3,1},{4,6},{5,7},{6,4},{7,5},{8,10},{9,11},{10,... | collective-permute-start | bytes 3145736 | tf_op jit(solution)/shard_map/ppermute | solution.py:47
  125.9 16.6 %collective-permute-start.21 = (f32[384,1024]{1,0:T(8,128)S(1)}, f32[384,1024]{1,0:T(8,128)S(1)}, u32[]{:S(2)}, u32[]{:S(2)}) collective-permute-start(f32[384,1024]{1,0:T(8,128)S(1)} %get-tuple-element.84), channel_id=1, source_target_pairs={{0,1},{1,0},{2,3},{3,2},{4,5},{5,4},{6,7},{7,6},{8,9},{9,8},{10,11... | collective-permute-start | bytes 4718600 | tf_op jit(solution)/shard_map/ppermute | solution.py:47
  125.9 7.5 %collective-permute-start.25 = (bf16[384,1024]{1,0:T(8,128)(2,1)S(1)}, bf16[384,1024]{1,0:T(8,128)(2,1)S(1)}, u32[]{:S(2)}, u32[]{:S(2)}) collective-permute-start(bf16[384,1024]{1,0:T(8,128)(2,1)S(1)} %get-tuple-element.69), channel_id=1, source_target_pairs={{0,1},{1,0},{2,3},{3,2},{4,5},{5,4},{6,7},{7,6},{8,9},{9,8},{10,11... | collective-permute-start | bytes 2359304 | tf_op jit(solution)/shard_map/ppermute | solution.py:47
  126.4 7.0 %collective-permute-start.26 = (bf16[384,1024]{1,0:T(8,128)(2,1)S(1)}, bf16[384,1024]{1,0:T(8,128)(2,1)S(1)}, u32[]{:S(2)}, u32[]{:S(2)}) collective-permute-start(bf16[384,1024]{1,0:T(8,128)(2,1)S(1)} %get-tuple-element.77), channel_id=1, source_target_pairs={{0,1},{1,0},{2,3},{3,2},{4,5},{5,4},{6,7},{7,6},{8,9},{9,8},{10,11... | collective-permute-start | bytes 2359304 | tf_op jit(solution)/shard_map/ppermute | solution.py:47
  132.7 9.9 %collective-permute-start.20 = (bf16[384,1024]{1,0:T(8,128)(2,1)S(1)}, bf16[384,1024]{1,0:T(8,128)(2,1)S(1)}, u32[]{:S(2)}, u32[]{:S(2)}) collective-permute-start(bf16[384,1024]{1,0:T(8,128)(2,1)S(1)} %get-tuple-element.82), channel_id=1, source_target_pairs={{0,1},{1,0},{2,3},{3,2},{4,5},{5,4},{6,7},{7,6},{8,9},{9,8},{10,11... | collective-permute-start | bytes 2359304 | tf_op jit(solution)/shard_map/ppermute | solution.py:47
  133.3 9.2 %collective-permute-start.24 = (bf16[256,1024]{1,0:T(8,128)(2,1)S(1)}, bf16[256,1024]{1,0:T(8,128)(2,1)S(1)}, u32[]{:S(2)}, u32[]{:S(2)}) collective-permute-start(bf16[256,1024]{1,0:T(8,128)(2,1)S(1)} %get-tuple-element.91), channel_id=1, source_target_pairs={{0,8},{1,17},{2,10},{3,19},{4,12},{5,21},{6,14},{7,23},{8,0},{9,25... | collective-permute-start | bytes 1572872 | tf_op jit(solution)/shard_map/ppermute | solution.py:47

commit v18 on v12

--- a/solution.py
+++ b/solution.py
@@ -334,7 +334,7 @@
     )
     got3 = sent(send3, FLIP_B)
     keep2, keep1, keep0, send2, send1, send0 = terms(place, activations, other, turned, rows)
-    first = gate(place, after(one, keep0), mid, base_b)
+    first = gate(place, after(mid, keep0), one, base_b)
 
     sum3 = added(after(keep3, first), got3)
     far = sent(sum3, IN)

time: 142 us -> 141 us (level)
  transfers between devices with their start and end apart: 27 -> 27, of which waited for: 14 -> 13; matrix products, arithmetic and copies ran while one was open for 7% -> 7% of each run, Pallas kernels for 31% -> 31%
where the time goes in v18:
time: 141 us
  Pallas kernels  45.9 us (33%)
  waiting for transfers between devices  44 us (31%)
  starting transfers between devices  37.4 us (27%)
  other arithmetic  9.88 us (7%)
  local copies, waits for them, and re-layouts  2.79 us (2%)
    ppermute x27, waiting for transfers between devices, sent(): return lax.ppermute(array, AXES, pairs)  44 us
    ppermute x27, starting transfers between devices, sent(): return lax.ppermute(array, AXES, pairs)  37.4 us
    pallas_call x4, Pallas kernels, projected(): pl.pallas_call(lambda *refs: project_kernel(*refs, first=first, last=last...  26.7 us
    pallas_call x1, Pallas kernels, terms(): pl.pallas_call(term_kernel, grid_spec=pltpu.PrefetchScalarGridSpec(num_sc...  8.66 us
    convert_element_type x7, other arithmetic, added(): return total.astype(BF16)  6.25 us
    pallas_call x1, Pallas kernels, first_terms(): pl.pallas_call(first_term_kernel, grid_spec=pltpu.PrefetchScalarGridSpec(...  4.49 us
  transfers between devices with their start and end apart: 27, of which 13 were waited for; matrix products, arithmetic and copies ran while one was open for 7% of the time, Pallas kernels for 31%

profile of v18, /device:TPU:0, one launch (start us, length us, event | category | flops | bytes accessed | tf_op | source)
XLA Modules:
  0.0 140.8 jit_solution(3974446748798014560)
XLA Ops:
  0.6 0.5 collective-permute-start
  1.2 2.9 %collective-permute-start.4 = (bf16[1024,256]{1,0:T(8,128)(2,1)}, bf16[1024,256]{1,0:T(8,128)(2,1)S(1)}, u32[]{:S(2)}, u32[]{:S(2)}) collective-permute-start(bf16[1024,256]{1,0:T(8,128)(2,1)} %param.5), channel_id=1, source_target_pairs={{0,8},{1,17},{2,10},{3,19},{4,12},{5,21},{6,14},{7,23},{8,0},{9,25... | collective-permute-start | bytes 1572872 | tf_op jit(solution)/shard_map/ppermute | solution.py:47
  4.2 7.4 %collective-permute-done.4 = bf16[1024,256]{1,0:T(8,128)(2,1)S(1)} collective-permute-done((bf16[1024,256]{1,0:T(8,128)(2,1)}, bf16[1024,256]{1,0:T(8,128)(2,1)S(1)}, u32[]{:S(2)}, u32[]{:S(2)}) %collective-permute-start.4) | collective-permute-done | bytes 524320 | tf_op jit(solution)/shard_map/ppermute | solution.py:47
  11.5 1.1 pad_maximum_fusion.refs_4_
  12.7 0.7 collective-permute-start.5
  13.5 2.1 %collective-permute-start.7 = (bf16[2,1024,256]{2,1,0:T(8,128)(2,1)S(1)}, bf16[2,1024,256]{2,1,0:T(8,128)(2,1)S(1)}, u32[]{:S(2)}, u32[]{:S(2)}) collective-permute-start(bf16[2,1024,256]{2,1,0:T(8,128)(2,1)S(1)} %pad_maximum_fusion.refs_4_), channel_id=1, source_target_pairs={{0,16},{1,9},{2,18},{3,11},{4,20},{5,13},{6,22},{7,15},{8,24},{9,1... | collective-permute-start | bytes 3145736 | tf_op jit(solution)/shard_map/ppermute | solution.py:47
  15.5 4.3 %collective-permute-start.6 = (bf16[2,1024,256]{2,1,0:T(8,128)(2,1)S(1)}, bf16[2,1024,256]{2,1,0:T(8,128)(2,1)S(1)}, u32[]{:S(2)}, u32[]{:S(2)}) collective-permute-start(bf16[2,1024,256]{2,1,0:T(8,128)(2,1)S(1)} %pad_maximum_fusion.refs_4_), channel_id=1, source_target_pairs={{0,2},{1,3},{2,0},{3,1},{4,6},{5,7},{6,4},{7,5},{8,10},{9,11},{10,... | collective-permute-start | bytes 3145736 | tf_op jit(solution)/shard_map/ppermute | solution.py:47
  19.9 2.8 %copy-done = bf16[384,8192]{1,0:T(8,128)(2,1)S(1)} copy-done((bf16[384,8192]{1,0:T(8,128)(2,1)S(1)}, bf16[384,8192]{1,0:T(8,128)(2,1)}, u32[]{:S(2)}) %copy-start) | copy-done | bytes 6291480
  22.7 4.5 %terms.2 = (bf16[2,256,1024]{2,1,0:T(8,128)(2,1)S(1)}, bf16[2,256,1024]{2,1,0:T(8,128)(2,1)S(1)}, bf16[768,1024]{1,0:T(8,128)(2,1)S(1)}, bf16[1024,768]{1,0:T(8,128)(2,1)S(1)}) custom-call(s32[3]{0:T(128)S(1)} %pad_add_fusion.place.refs_0_, bf16[384,8192]{1,0:T(8,128)(2,1)S(1)} %copy-done, bf16[384,8192]{1,0:T(8,128)(2,1)} %collective-permute-done.other.refs_2_, ...), custom_call_target="tpu_custom_call" | custom-call | flops 1610612 | bytes 5767 | tf_op jit(solution)/shard_map/terms/pallas_call | solution.py:107
  27.2 0.6 collective-permute-start.8
  27.7 8.7 %terms.3 = (bf16[2,256,1024]{2,1,0:T(8,128)(2,1)S(1)}, bf16[2,256,1024]{2,1,0:T(8,128)(2,1)S(1)}, bf16[2,256,1024]{2,1,0:T(8,128)(2,1)S(1)}, bf16[2,256,1024]{2,...) custom-call(s32[3]{0:T(128)S(1)} %pad_add_fusion.place.refs_0_, ...), custom_call_target="tpu_custom_call" | custom-call | flops 4831838 | bytes 17301 | tf_op jit(solution)/shard_map/terms/pallas_call | solution.py:149
  36.4 1.6 %collective-permute-start.2 = (bf16[2,256,1024]{2,1,0:T(8,128)(2,1)S(1)}, bf16[2,256,1024]{2,1,0:T(8,128)(2,1)S(1)}, u32[]{:S(2)}, u32[]{:S(2)}) collective-permute-start(bf16[2,256,1024]{2,1,0:T(8,128)(2,1)S(1)} %get-tuple-element.51), channel_id=1, source_target_pairs={{0,16},{1,9},{2,18},{3,11},{4,20},{5,13},{6,22},{7,15},{8,24},{9,1... | collective-permute-start | bytes 3145736 | tf_op jit(solution)/shard_map/ppermute | solution.py:47
  38.0 3.8 %collective-permute-done.6.refs_2_.refs_4_ = bf16[2,1024,256]{2,1,0:T(8,128)(2,1)S(1)} collective-permute-done((bf16[2,1024,256]{2,1,0:T(8,128)(2,1)S(1)}, bf16[2,1024,256]{2,1,0:T(8,128)(2,1)S(1)}, u32[]{:S(2)}, u32[]{:S(2)}) %collective-permute-start.6) | collective-permute-done | bytes 1048608 | tf_op jit(solution)/shard_map/ppermute | solution.py:47
  41.8 1.1 gate.1.refs_0_
  43.4 3.7 %collective-permute-start.9 = (bf16[2,256,1024]{2,1,0:T(8,128)(2,1)S(1)}, bf16[2,256,1024]{2,1,0:T(8,128)(2,1)S(1)}, u32[]{:S(2)}, u32[]{:S(2)}) collective-permute-start(bf16[2,256,1024]{2,1,0:T(8,128)(2,1)S(1)} %add_convert_fusion.4), channel_id=1, source_target_pairs={{0,2},{1,3},{6,4},{7,5},{8,10},{9,11},{14,12},{15,13},{16,18},{17,... | collective-permute-start | bytes 3145736 | tf_op jit(solution)/shard_map/ppermute | solution.py:47
  47.1 0.7 collective-permute-start.10
  47.9 1.3 collective-permute-start.11
  49.2 1.6 %collective-permute-start.12 = (bf16[2,1024,256]{2,1,0:T(8,128)(2,1)S(1)}, bf16[2,1024,256]{2,1,0:T(8,128)(2,1)S(1)}, u32[]{:S(2)}, u32[]{:S(2)}) collective-permute-start(bf16[2,1024,256]{2,1,0:T(8,128)(2,1)S(1)} %collective-permute-done.6.refs_2_.refs_4_), channel_id=1, source_target_pairs={{0,16},{1,9},{2,18},{3,11},{4,20},{5,13},{6,22},{7,15},{8,24},{9,1... | collective-permute-start | bytes 3145736 | tf_op jit(solution)/shard_map/ppermute | solution.py:47
  50.7 2.5 %collective-permute-done.2 = bf16[2,256,1024]{2,1,0:T(8,128)(2,1)S(1)} collective-permute-done((bf16[2,256,1024]{2,1,0:T(8,128)(2,1)S(1)}, bf16[2,256,1024]{2,1,0:T(8,128)(2,1)S(1)}, u32[]{:S(2)}, u32[]{:S(2)}) %collective-permute-start.2) | collective-permute-done | bytes 1048608 | tf_op jit(solution)/shard_map/ppermute | solution.py:47
  53.7 0.6 collective-permute-start.3
  54.3 6.5 %project.4 = (bf16[384,8192]{1,0:T(8,128)(2,1)}, bf16[384,1024]{1,0:T(8,128)(2,1)S(1)}, f32[768,1024]{1,0:T(8,128)S(1)}) custom-call(s32[3]{0:T(128)S(1)} %gate.1.refs_0_, bf16[384,8192]{1,0:T(8,128)(2,1)S(1)} %copy-done.1, bf16[384,8192]{1,0:T(8,128)(2,1)} %collective-permute-done.other.refs_2_, bf16[768,1024]{1,0:T(8,128)(2,1)S(1)} %get-tuple-element.59.refs_3_, ...), custom_call_target="tpu_custom_call" | custom-call | flops 3221225 | bytes 8388 | tf_op jit(solution)/shard_map/project/pallas_call | solution.py:216
  60.7 6.6 %collective-permute-done.9 = bf16[2,256,1024]{2,1,0:T(8,128)(2,1)S(1)} collective-permute-done((bf16[2,256,1024]{2,1,0:T(8,128)(2,1)S(1)}, bf16[2,256,1024]{2,1,0:T(8,128)(2,1)S(1)}, u32[]{:S(2)}, u32[]{:S(2)}) %collective-permute-start.9) | collective-permute-done | bytes 1048608 | tf_op jit(solution)/shard_map/ppermute | solution.py:47
  67.4 1.4 add_convert_fusion.3
  68.7 3.5 %collective-permute-done.11 = bf16[2,1024,256]{2,1,0:T(8,128)(2,1)S(1)} collective-permute-done((bf16[2,1024,256]{2,1,0:T(8,128)(2,1)S(1)}, bf16[2,1024,256]{2,1,0:T(8,128)(2,1)S(1)}, u32[]{:S(2)}, u32[]{:S(2)}) %collective-permute-start.11) | collective-permute-done | bytes 1048608 | tf_op jit(solution)/shard_map/ppermute | solution.py:47
  72.3 2.4 %collective-permute-start.13 = (bf16[2,256,1024]{2,1,0:T(8,128)(2,1)S(1)}, bf16[2,256,1024]{2,1,0:T(8,128)(2,1)}, u32[]{:S(2)}, u32[]{:S(2)}) collective-permute-start(bf16[2,256,1024]{2,1,0:T(8,128)(2,1)S(1)} %add_convert_fusion.6), channel_id=1, source_target_pairs={{0,2},{1,3},{6,4},{7,5},{8,10},{9,11},{14,12},{15,13},{16,18},{17,... | collective-permute-start | bytes 3145736 | tf_op jit(solution)/shard_map/ppermute | solution.py:47
  74.7 1.7 %collective-permute-start.14 = (bf16[2,256,1024]{2,1,0:T(8,128)(2,1)}, bf16[2,256,1024]{2,1,0:T(8,128)(2,1)}, u32[]{:S(2)}, u32[]{:S(2)}) collective-permute-start(bf16[2,256,1024]{2,1,0:T(8,128)(2,1)} %add_convert_fusion.3), channel_id=1, source_target_pairs={{2,4},{3,5},{4,2},{5,3},{10,12},{11,13},{12,10},{13,11},{18,20},{1... | collective-permute-start | bytes 3145736 | tf_op jit(solution)/shard_map/ppermute | solution.py:47
  76.4 1.5 %collective-permute-start.17 = (bf16[2,1024,256]{2,1,0:T(8,128)(2,1)S(1)}, bf16[2,1024,256]{2,1,0:T(8,128)(2,1)}, u32[]{:S(2)}, u32[]{:S(2)}) collective-permute-start(bf16[2,1024,256]{2,1,0:T(8,128)(2,1)S(1)} %collective-permute-done.10), channel_id=1, source_target_pairs={{2,0},{3,1},{4,6},{5,7},{10,8},{11,9},{12,14},{13,15},{18,16},{19,... | collective-permute-start | bytes 3145736 | tf_op jit(solution)/shard_map/ppermute | solution.py:47
  78.3 2.6 %collective-permute-start.15 = (bf16[2,256,1024]{2,1,0:T(8,128)(2,1)S(1)}, bf16[2,256,1024]{2,1,0:T(8,128)(2,1)S(1)}, u32[]{:S(2)}, u32[]{:S(2)}) collective-permute-start(bf16[2,256,1024]{2,1,0:T(8,128)(2,1)S(1)} %get-tuple-element.72), channel_id=1, source_target_pairs={{0,16},{1,9},{2,18},{3,11},{4,20},{5,13},{6,22},{7,15},{8,24},{9,1... | collective-permute-start | bytes 3145736 | tf_op jit(solution)/shard_map/ppermute | solution.py:47
  81.2 6.7 %project.5 = (bf16[384,8192]{1,0:T(8,128)(2,1)}, bf16[384,1024]{1,0:T(8,128)(2,1)S(1)}, f32[768,1024]{1,0:T(8,128)S(1)}) custom-call(s32[3]{0:T(128)S(1)} %pad_add_fusion.place.refs_0_, bf16[384,8192]{1,0:T(8,128)(2,1)S(1)} %copy-done.1, bf16[384,8192]{1,0:T(8,128)(2,1)} %collective-permute-done.other.refs_2_, ...), custom_call_target="tpu_custom_call", output_to_operand_aliasing={{0}: (7, {})} | custom-call | flops 3221225 | bytes 8388 | tf_op jit(solution)/shard_map/project/pallas_call | solution.py:216
  87.9 5.0 %collective-permute-done.13 = bf16[2,256,1024]{2,1,0:T(8,128)(2,1)} collective-permute-done((bf16[2,256,1024]{2,1,0:T(8,128)(2,1)S(1)}, bf16[2,256,1024]{2,1,0:T(8,128)(2,1)}, u32[]{:S(2)}, u32[]{:S(2)}) %collective-permute-start.13) | collective-permute-done | bytes 1048608 | tf_op jit(solution)/shard_map/ppermute | solution.py:47
  93.0 1.6 %add_convert_fusion.2 = bf16[2,256,1024]{2,1,0:T(8,128)(2,1)S(1)} fusion(bf16[2,256,1024]{2,1,0:T(8,128)(2,1)} %collective-permute-done.13, bf16[2,256,1024]{2,1,0:T(8,128)(2,1)S(1)} %add_convert_fusion.4), kind=kLoop, calls=%fused_computation.2 | loop fusion | flops 2097152 | bytes 3145728 | tf_op jit(solution)/shard_map/convert_element_type | solution.py:319
  94.6 1.6 %add_convert_fusion.1 = bf16[2,256,1024]{2,1,0:T(8,128)(2,1)S(1)} fusion(bf16[2,256,1024]{2,1,0:T(8,128)(2,1)} %collective-permute-done.14, bf16[2,256,1024]{2,1,0:T(8,128)(2,1)S(1)} %add_convert_fusion.5), kind=kLoop, calls=%fused_computation.1 | loop fusion | flops 2097152 | bytes 3145728 | tf_op jit(solution)/shard_map/convert_element_type | solution.py:319
  96.2 3.6 %collective-permute-done.17 = bf16[2,1024,256]{2,1,0:T(8,128)(2,1)} collective-permute-done((bf16[2,1024,256]{2,1,0:T(8,128)(2,1)S(1)}, bf16[2,1024,256]{2,1,0:T(8,128)(2,1)}, u32[]{:S(2)}, u32[]{:S(2)}) %collective-permute-start.17) | collective-permute-done | bytes 1048608 | tf_op jit(solution)/shard_map/ppermute | solution.py:47
  99.8 1.5 %add.52.refs_4_ = bf16[2,1024,256]{2,1,0:T(8,128)(2,1)S(1)} add(bf16[2,1024,256]{2,1,0:T(8,128)(2,1)S(1)} %collective-permute-done.5.refs_1_, bf16[2,1024,256]{2,1,0:T(8,128)(2,1)} %collective-permute-done.17) | non-fusion elementwise | flops 524288 | bytes 3145728 | tf_op jit(solution)/shard_map/add | solution.py:367
  101.4 3.6 %collective-permute-start.18 = (bf16[2,1024,256]{2,1,0:T(8,128)(2,1)S(1)}, bf16[2,1024,256]{2,1,0:T(8,128)(2,1)S(1)}, u32[]{:S(2)}, u32[]{:S(2)}) collective-permute-start(bf16[2,1024,256]{2,1,0:T(8,128)(2,1)S(1)} %add.52.refs_4_), channel_id=1, source_target_pairs={{0,16},{1,9},{2,18},{3,11},{4,20},{5,13},{6,22},{7,15},{8,24},{9,1... | collective-permute-start | bytes 3145736 | tf_op jit(solution)/shard_map/ppermute | solution.py:47
  105.0 0.7 collective-permute-start.21
  105.7 2.7 %collective-permute-start.22 = (bf16[2,256,1024]{2,1,0:T(8,128)(2,1)S(1)}, bf16[2,256,1024]{2,1,0:T(8,128)(2,1)S(1)}, u32[]{:S(2)}, u32[]{:S(2)}) collective-permute-start(bf16[2,256,1024]{2,1,0:T(8,128)(2,1)S(1)} %add_convert_fusion.1), channel_id=1, source_target_pairs={{0,2},{1,3},{2,0},{3,1},{4,6},{5,7},{6,4},{7,5},{8,10},{9,11},{10,... | collective-permute-start | bytes 3145736 | tf_op jit(solution)/shard_map/ppermute | solution.py:47
  108.9 6.7 %project.6 = (bf16[384,8192]{1,0:T(8,128)(2,1)}, bf16[384,1024]{1,0:T(8,128)(2,1)S(1)}, f32[768,1024]{1,0:T(8,128)S(1)}) custom-call(s32[3]{0:T(128)S(1)} %pad_add_fusion.place.refs_0_, bf16[384,8192]{1,0:T(8,128)(2,1)S(1)} %copy-done.1, bf16[384,8192]{1,0:T(8,128)(2,1)} %collective-permute-done.other.refs_2_, ...), custom_call_target="tpu_custom_call", output_to_operand_aliasing={{0}: (7, {})} | custom-call | flops 3221225 | bytes 8388 | tf_op jit(solution)/shard_map/project/pallas_call | solution.py:216
  115.6 2.2 %collective-permute-done.18.refs_5_ = bf16[2,1024,256]{2,1,0:T(8,128)(2,1)S(1)} collective-permute-done((bf16[2,1024,256]{2,1,0:T(8,128)(2,1)S(1)}, bf16[2,1024,256]{2,1,0:T(8,128)(2,1)S(1)}, u32[]{:S(2)}, u32[]{:S(2)}) %collective-permute-start.18) | collective-permute-done | bytes 1048608 | tf_op jit(solution)/shard_map/ppermute | solution.py:47
  117.7 6.8 %project.7 = (bf16[384,8192]{1,0:T(8,128)(2,1)}, bf16[384,1024]{1,0:T(8,128)(2,1)S(1)}, f32[384,1024]{1,0:T(8,128)S(1)}, f32[384,1024]{1,0:T(8,128)S(1)}) custom-call(s32[3]{0:T(128)S(1)} %pad_add_fusion.place.refs_0_, bf16[384,8192]{1,0:T(8,128)(2,1)S(1)} %copy-done.1, ...), custom_call_target="tpu_custom_call", output_to_operand_aliasing={{0}: (7, {})} | custom-call | flops 3221225 | bytes 8388 | tf_op jit(solution)/shard_map/project/pallas_call | solution.py:216
  125.1 1.5 %collective-permute-done.22 = bf16[2,256,1024]{2,1,0:T(8,128)(2,1)S(1)} collective-permute-done((bf16[2,256,1024]{2,1,0:T(8,128)(2,1)S(1)}, bf16[2,256,1024]{2,1,0:T(8,128)(2,1)S(1)}, u32[]{:S(2)}, u32[]{:S(2)}) %collective-permute-start.22) | collective-permute-done | bytes 1048608 | tf_op jit(solution)/shard_map/ppermute | solution.py:47
  127.1 0.6 fusion
  127.7 1.4 collective-permute-done.24.refs_0_
  129.5 0.7 collective-permute-done.25.refs_1_
  130.2 1.1 collective-permute-done.26.refs_2_
  131.4 2.4 %lay.1.refs_6_ = bf16[384,8192]{1,0:T(8,128)(2,1)} custom-call(s32[3]{0:T(128)S(1)} %pad_add_fusion.place.refs_0_, bf16[384,1024]{1,0:T(8,128)(2,1)S(1)} %collective-permute-done.24.refs_0_, bf16[384,1024]{1,0:T(8,128)(2,1)S(1)} %collective-permute-done.25.refs_1_, ...), custom_call_target="tpu_custom_call", output_to_operand_aliasing={{}: (4, {})} | custom-call | bytes 4718 | tf_op jit(solution)/shard_map/lay/pallas_call | solution.py:255
  133.8 4.5 %collective-permute-done.23.refs_5_ = bf16[256,1024]{1,0:T(8,128)(2,1)S(1)} collective-permute-done((bf16[256,1024]{1,0:T(8,128)(2,1)S(1)}, bf16[256,1024]{1,0:T(8,128)(2,1)S(1)}, u32[]{:S(2)}, u32[]{:S(2)}) %collective-permute-start.23) | collective-permute-done | bytes 524320 | tf_op jit(solution)/shard_map/ppermute | solution.py:47
  138.3 2.5 %finish.1 = (bf16[384,8192]{1,0:T(8,128)(2,1)}, bf16[384,1024]{1,0:T(8,128)(2,1)}, bf16[1024,256]{1,0:T(8,128)(2,1)}) custom-call(s32[3]{0:T(128)S(1)} %pad_add_fusion.place.refs_0_, bf16[384,1024]{1,0:T(8,128)(2,1)S(1)} %collective-permute-done.19.refs_1_, f32[384,1024]{1,0:T(8,128)S(1)} %get-tuple-element.83.refs_2_, ...), custom_call_target="tpu_custom_call", output_to_operand_aliasing={{0}: (6, {})} | custom-call | bytes 5505 | tf_op jit(solution)/shard_map/finish/pallas_call | solution.py:284
  (33 shorter events, 3.7 us)
Async XLA Ops:
  0.6 19.3 %copy-start.2 = (bf16[384,1024]{1,0:T(8,128)(2,1)S(1)}, bf16[384,1024]{1,0:T(8,128)(2,1)}, u32[]{:S(2)}) copy-start(bf16[384,1024]{1,0:T(8,128)(2,1)} %cot_mine.1) | copy-start | bytes 2359300
  0.6 19.2 %collective-permute-start = (bf16[384,8192]{1,0:T(8,128)(2,1)}, bf16[384,8192]{1,0:T(8,128)(2,1)}, u32[]{:S(2)}, u32[]{:S(2)}) collective-permute-start(bf16[384,8192]{1,0:T(8,128)(2,1)} %refs_1_.3), channel_id=1, source_target_pairs={{0,1},{1,0},{2,3},{3,2},{4,5},{5,4},{6,7},{7,6},{8,9},{9,8},{10,11... | collective-permute-start | bytes 18874376 | tf_op jit(solution)/shard_map/ppermute | solution.py:47
  1.2 18.7 %collective-permute-start.1 = (bf16[384,1024]{1,0:T(8,128)(2,1)}, bf16[384,1024]{1,0:T(8,128)(2,1)S(1)}, u32[]{:S(2)}, u32[]{:S(2)}) collective-permute-start(bf16[384,1024]{1,0:T(8,128)(2,1)} %cot_mine.1), channel_id=1, source_target_pairs={{0,1},{1,0},{2,3},{3,2},{4,5},{5,4},{6,7},{7,6},{8,9},{9,8},{10,11... | collective-permute-start | bytes 2359304 | tf_op jit(solution)/shard_map/ppermute | solution.py:47
  1.2 10.3 %collective-permute-start.4 = (bf16[1024,256]{1,0:T(8,128)(2,1)}, bf16[1024,256]{1,0:T(8,128)(2,1)S(1)}, u32[]{:S(2)}, u32[]{:S(2)}) collective-permute-start(bf16[1024,256]{1,0:T(8,128)(2,1)} %param.5), channel_id=1, source_target_pairs={{0,8},{1,17},{2,10},{3,19},{4,12},{5,21},{6,14},{7,23},{8,0},{9,25... | collective-permute-start | bytes 1572872 | tf_op jit(solution)/shard_map/ppermute | solution.py:47
  12.7 25.3 %collective-permute-start.5 = (bf16[2,1024,256]{2,1,0:T(8,128)(2,1)S(1)}, bf16[2,1024,256]{2,1,0:T(8,128)(2,1)S(1)}, u32[]{:S(2)}, u32[]{:S(2)}) collective-permute-start(bf16[2,1024,256]{2,1,0:T(8,128)(2,1)S(1)} %pad_maximum_fusion.refs_4_), channel_id=1, source_target_pairs={{2,4},{3,5},{4,2},{5,3},{10,12},{11,13},{12,10},{13,11},{18,20},{1... | collective-permute-start | bytes 3145736 | tf_op jit(solution)/shard_map/ppermute | solution.py:47
  13.5 24.5 %collective-permute-start.7 = (bf16[2,1024,256]{2,1,0:T(8,128)(2,1)S(1)}, bf16[2,1024,256]{2,1,0:T(8,128)(2,1)S(1)}, u32[]{:S(2)}, u32[]{:S(2)}) collective-permute-start(bf16[2,1024,256]{2,1,0:T(8,128)(2,1)S(1)} %pad_maximum_fusion.refs_4_), channel_id=1, source_target_pairs={{0,16},{1,9},{2,18},{3,11},{4,20},{5,13},{6,22},{7,15},{8,24},{9,1... | collective-permute-start | bytes 3145736 | tf_op jit(solution)/shard_map/ppermute | solution.py:47
  15.5 26.3 %collective-permute-start.6 = (bf16[2,1024,256]{2,1,0:T(8,128)(2,1)S(1)}, bf16[2,1024,256]{2,1,0:T(8,128)(2,1)S(1)}, u32[]{:S(2)}, u32[]{:S(2)}) collective-permute-start(bf16[2,1024,256]{2,1,0:T(8,128)(2,1)S(1)} %pad_maximum_fusion.refs_4_), channel_id=1, source_target_pairs={{0,2},{1,3},{2,0},{3,1},{4,6},{5,7},{6,4},{7,5},{8,10},{9,11},{10,... | collective-permute-start | bytes 3145736 | tf_op jit(solution)/shard_map/ppermute | solution.py:47
  19.9 2.8 %copy-start = (bf16[384,8192]{1,0:T(8,128)(2,1)S(1)}, bf16[384,8192]{1,0:T(8,128)(2,1)}, u32[]{:S(2)}) copy-start(bf16[384,8192]{1,0:T(8,128)(2,1)} %refs_1_.3) | copy-start | bytes 18874372
  22.7 5.1 %copy-start.1 = (bf16[384,8192]{1,0:T(8,128)(2,1)S(1)}, bf16[384,8192]{1,0:T(8,128)(2,1)}, u32[]{:S(2)}) copy-start(bf16[384,8192]{1,0:T(8,128)(2,1)} %refs_1_.3) | copy-start | bytes 18874372
  27.2 15.8 %collective-permute-start.8 = (bf16[2,256,1024]{2,1,0:T(8,128)(2,1)S(1)}, bf16[2,256,1024]{2,1,0:T(8,128)(2,1)S(1)}, u32[]{:S(2)}, u32[]{:S(2)}) collective-permute-start(bf16[2,256,1024]{2,1,0:T(8,128)(2,1)S(1)} %get-tuple-element.57), channel_id=1, source_target_pairs={{0,16},{1,9},{2,18},{3,11},{4,20},{5,13},{6,22},{7,15},{8,24},{9,1... | collective-permute-start | bytes 3145736 | tf_op jit(solution)/shard_map/ppermute | solution.py:47
  36.4 16.9 %collective-permute-start.2 = (bf16[2,256,1024]{2,1,0:T(8,128)(2,1)S(1)}, bf16[2,256,1024]{2,1,0:T(8,128)(2,1)S(1)}, u32[]{:S(2)}, u32[]{:S(2)}) collective-permute-start(bf16[2,256,1024]{2,1,0:T(8,128)(2,1)S(1)} %get-tuple-element.51), channel_id=1, source_target_pairs={{0,16},{1,9},{2,18},{3,11},{4,20},{5,13},{6,22},{7,15},{8,24},{9,1... | collective-permute-start | bytes 3145736 | tf_op jit(solution)/shard_map/ppermute | solution.py:47
  43.4 24.0 %collective-permute-start.9 = (bf16[2,256,1024]{2,1,0:T(8,128)(2,1)S(1)}, bf16[2,256,1024]{2,1,0:T(8,128)(2,1)S(1)}, u32[]{:S(2)}, u32[]{:S(2)}) collective-permute-start(bf16[2,256,1024]{2,1,0:T(8,128)(2,1)S(1)} %add_convert_fusion.4), channel_id=1, source_target_pairs={{0,2},{1,3},{6,4},{7,5},{8,10},{9,11},{14,12},{15,13},{16,18},{17,... | collective-permute-start | bytes 3145736 | tf_op jit(solution)/shard_map/ppermute | solution.py:47
  47.1 21.6 %collective-permute-start.10 = (bf16[2,1024,256]{2,1,0:T(8,128)(2,1)S(1)}, bf16[2,1024,256]{2,1,0:T(8,128)(2,1)S(1)}, u32[]{:S(2)}, u32[]{:S(2)}) collective-permute-start(bf16[2,1024,256]{2,1,0:T(8,128)(2,1)S(1)} %collective-permute-done.6.refs_2_.refs_4_), channel_id=1, source_target_pairs={{2,4},{3,5},{4,2},{5,3},{10,12},{11,13},{12,10},{13,11},{18,20},{1... | collective-permute-start | bytes 3145736 | tf_op jit(solution)/shard_map/ppermute | solution.py:47
  47.9 24.4 %collective-permute-start.11 = (bf16[2,1024,256]{2,1,0:T(8,128)(2,1)S(1)}, bf16[2,1024,256]{2,1,0:T(8,128)(2,1)S(1)}, u32[]{:S(2)}, u32[]{:S(2)}) collective-permute-start(bf16[2,1024,256]{2,1,0:T(8,128)(2,1)S(1)} %collective-permute-done.5.refs_1_), channel_id=1, source_target_pairs={{2,0},{3,1},{4,6},{5,7},{10,8},{11,9},{12,14},{13,15},{18,16},{19,... | collective-permute-start | bytes 3145736 | tf_op jit(solution)/shard_map/ppermute | solution.py:47
  49.2 23.1 %collective-permute-start.12 = (bf16[2,1024,256]{2,1,0:T(8,128)(2,1)S(1)}, bf16[2,1024,256]{2,1,0:T(8,128)(2,1)S(1)}, u32[]{:S(2)}, u32[]{:S(2)}) collective-permute-start(bf16[2,1024,256]{2,1,0:T(8,128)(2,1)S(1)} %collective-permute-done.6.refs_2_.refs_4_), channel_id=1, source_target_pairs={{0,16},{1,9},{2,18},{3,11},{4,20},{5,13},{6,22},{7,15},{8,24},{9,1... | collective-permute-start | bytes 3145736 | tf_op jit(solution)/shard_map/ppermute | solution.py:47
  53.7 24.2 %collective-permute-start.3 = (bf16[2,256,1024]{2,1,0:T(8,128)(2,1)S(1)}, bf16[2,256,1024]{2,1,0:T(8,128)(2,1)S(1)}, u32[]{:S(2)}, u32[]{:S(2)}) collective-permute-start(bf16[2,256,1024]{2,1,0:T(8,128)(2,1)S(1)} %get-tuple-element.52), channel_id=1, source_target_pairs={{0,16},{1,9},{2,18},{3,11},{4,20},{5,13},{6,22},{7,15},{8,24},{9,1... | collective-permute-start | bytes 3145736 | tf_op jit(solution)/shard_map/ppermute | solution.py:47
  72.3 20.7 %collective-permute-start.13 = (bf16[2,256,1024]{2,1,0:T(8,128)(2,1)S(1)}, bf16[2,256,1024]{2,1,0:T(8,128)(2,1)}, u32[]{:S(2)}, u32[]{:S(2)}) collective-permute-start(bf16[2,256,1024]{2,1,0:T(8,128)(2,1)S(1)} %add_convert_fusion.6), channel_id=1, source_target_pairs={{0,2},{1,3},{6,4},{7,5},{8,10},{9,11},{14,12},{15,13},{16,18},{17,... | collective-permute-start | bytes 3145736 | tf_op jit(solution)/shard_map/ppermute | solution.py:47
  74.7 19.9 %collective-permute-start.14 = (bf16[2,256,1024]{2,1,0:T(8,128)(2,1)}, bf16[2,256,1024]{2,1,0:T(8,128)(2,1)}, u32[]{:S(2)}, u32[]{:S(2)}) collective-permute-start(bf16[2,256,1024]{2,1,0:T(8,128)(2,1)} %add_convert_fusion.3), channel_id=1, source_target_pairs={{2,4},{3,5},{4,2},{5,3},{10,12},{11,13},{12,10},{13,11},{18,20},{1... | collective-permute-start | bytes 3145736 | tf_op jit(solution)/shard_map/ppermute | solution.py:47
  76.4 23.4 %collective-permute-start.17 = (bf16[2,1024,256]{2,1,0:T(8,128)(2,1)S(1)}, bf16[2,1024,256]{2,1,0:T(8,128)(2,1)}, u32[]{:S(2)}, u32[]{:S(2)}) collective-permute-start(bf16[2,1024,256]{2,1,0:T(8,128)(2,1)S(1)} %collective-permute-done.10), channel_id=1, source_target_pairs={{2,0},{3,1},{4,6},{5,7},{10,8},{11,9},{12,14},{13,15},{18,16},{19,... | collective-permute-start | bytes 3145736 | tf_op jit(solution)/shard_map/ppermute | solution.py:47
  78.3 30.1 %collective-permute-start.15 = (bf16[2,256,1024]{2,1,0:T(8,128)(2,1)S(1)}, bf16[2,256,1024]{2,1,0:T(8,128)(2,1)S(1)}, u32[]{:S(2)}, u32[]{:S(2)}) collective-permute-start(bf16[2,256,1024]{2,1,0:T(8,128)(2,1)S(1)} %get-tuple-element.72), channel_id=1, source_target_pairs={{0,16},{1,9},{2,18},{3,11},{4,20},{5,13},{6,22},{7,15},{8,24},{9,1... | collective-permute-start | bytes 3145736 | tf_op jit(solution)/shard_map/ppermute | solution.py:47
  81.2 24.5 %collective-permute-start.16 = (bf16[2,1024,256]{2,1,0:T(8,128)(2,1)S(1)}, bf16[2,1024,256]{2,1,0:T(8,128)(2,1)S(1)}, u32[]{:S(2)}, u32[]{:S(2)}) collective-permute-start(bf16[2,1024,256]{2,1,0:T(8,128)(2,1)S(1)} %add.51.refs_4_), channel_id=1, source_target_pairs={{0,16},{1,9},{2,18},{3,11},{4,20},{5,13},{6,22},{7,15},{8,24},{9,1... | collective-permute-start | bytes 3145736 | tf_op jit(solution)/shard_map/ppermute | solution.py:47
  101.4 16.4 %collective-permute-start.18 = (bf16[2,1024,256]{2,1,0:T(8,128)(2,1)S(1)}, bf16[2,1024,256]{2,1,0:T(8,128)(2,1)S(1)}, u32[]{:S(2)}, u32[]{:S(2)}) collective-permute-start(bf16[2,1024,256]{2,1,0:T(8,128)(2,1)S(1)} %add.52.refs_4_), channel_id=1, source_target_pairs={{0,16},{1,9},{2,18},{3,11},{4,20},{5,13},{6,22},{7,15},{8,24},{9,1... | collective-permute-start | bytes 3145736 | tf_op jit(solution)/shard_map/ppermute | solution.py:47
  105.0 21.6 %collective-permute-start.21 = (bf16[2,256,1024]{2,1,0:T(8,128)(2,1)S(1)}, bf16[2,256,1024]{2,1,0:T(8,128)(2,1)S(1)}, u32[]{:S(2)}, u32[]{:S(2)}) collective-permute-start(bf16[2,256,1024]{2,1,0:T(8,128)(2,1)S(1)} %add_convert_fusion.2), channel_id=1, source_target_pairs={{2,4},{3,5},{4,2},{5,3},{10,12},{11,13},{12,10},{13,11},{18,20},{1... | collective-permute-start | bytes 3145736 | tf_op jit(solution)/shard_map/ppermute | solution.py:47
  105.7 20.9 %collective-permute-start.22 = (bf16[2,256,1024]{2,1,0:T(8,128)(2,1)S(1)}, bf16[2,256,1024]{2,1,0:T(8,128)(2,1)S(1)}, u32[]{:S(2)}, u32[]{:S(2)}) collective-permute-start(bf16[2,256,1024]{2,1,0:T(8,128)(2,1)S(1)} %add_convert_fusion.1), channel_id=1, source_target_pairs={{0,2},{1,3},{2,0},{3,1},{4,6},{5,7},{6,4},{7,5},{8,10},{9,11},{10,... | collective-permute-start | bytes 3145736 | tf_op jit(solution)/shard_map/ppermute | solution.py:47
  124.6 13.7 %collective-permute-start.20 = (f32[384,1024]{1,0:T(8,128)S(1)}, f32[384,1024]{1,0:T(8,128)S(1)}, u32[]{:S(2)}, u32[]{:S(2)}) collective-permute-start(f32[384,1024]{1,0:T(8,128)S(1)} %get-tuple-element.84), channel_id=1, source_target_pairs={{0,1},{1,0},{2,3},{3,2},{4,5},{5,4},{6,7},{7,6},{8,9},{9,8},{10,11... | collective-permute-start | bytes 4718600 | tf_op jit(solution)/shard_map/ppermute | solution.py:47
  124.6 4.5 %collective-permute-start.24 = (bf16[384,1024]{1,0:T(8,128)(2,1)S(1)}, bf16[384,1024]{1,0:T(8,128)(2,1)S(1)}, u32[]{:S(2)}, u32[]{:S(2)}) collective-permute-start(bf16[384,1024]{1,0:T(8,128)(2,1)S(1)} %get-tuple-element.60), channel_id=1, source_target_pairs={{0,1},{1,0},{2,3},{3,2},{4,5},{5,4},{6,7},{7,6},{8,9},{9,8},{10,11... | collective-permute-start | bytes 2359304 | tf_op jit(solution)/shard_map/ppermute | solution.py:47
  125.1 5.1 %collective-permute-start.25 = (bf16[384,1024]{1,0:T(8,128)(2,1)S(1)}, bf16[384,1024]{1,0:T(8,128)(2,1)S(1)}, u32[]{:S(2)}, u32[]{:S(2)}) collective-permute-start(bf16[384,1024]{1,0:T(8,128)(2,1)S(1)} %get-tuple-element.69), channel_id=1, source_target_pairs={{0,1},{1,0},{2,3},{3,2},{4,5},{5,4},{6,7},{7,6},{8,9},{9,8},{10,11... | collective-permute-start | bytes 2359304 | tf_op jit(solution)/shard_map/ppermute | solution.py:47
  126.6 4.8 %collective-permute-start.26 = (bf16[384,1024]{1,0:T(8,128)(2,1)S(1)}, bf16[384,1024]{1,0:T(8,128)(2,1)S(1)}, u32[]{:S(2)}, u32[]{:S(2)}) collective-permute-start(bf16[384,1024]{1,0:T(8,128)(2,1)S(1)} %get-tuple-element.77), channel_id=1, source_target_pairs={{0,1},{1,0},{2,3},{3,2},{4,5},{5,4},{6,7},{7,6},{8,9},{9,8},{10,11... | collective-permute-start | bytes 2359304 | tf_op jit(solution)/shard_map/ppermute | solution.py:47
  126.6 11.7 %collective-permute-start.19 = (bf16[384,1024]{1,0:T(8,128)(2,1)S(1)}, bf16[384,1024]{1,0:T(8,128)(2,1)S(1)}, u32[]{:S(2)}, u32[]{:S(2)}) collective-permute-start(bf16[384,1024]{1,0:T(8,128)(2,1)S(1)} %get-tuple-element.82), channel_id=1, source_target_pairs={{0,1},{1,0},{2,3},{3,2},{4,5},{5,4},{6,7},{7,6},{8,9},{9,8},{10,11... | collective-permute-start | bytes 2359304 | tf_op jit(solution)/shard_map/ppermute | solution.py:47
  129.1 9.2 %collective-permute-start.23 = (bf16[256,1024]{1,0:T(8,128)(2,1)S(1)}, bf16[256,1024]{1,0:T(8,128)(2,1)S(1)}, u32[]{:S(2)}, u32[]{:S(2)}) collective-permute-start(bf16[256,1024]{1,0:T(8,128)(2,1)S(1)} %get-tuple-element.91), channel_id=1, source_target_pairs={{0,8},{1,17},{2,10},{3,19},{4,12},{5,21},{6,14},{7,23},{8,0},{9,25... | collective-permute-start | bytes 1572872 | tf_op jit(solution)/shard_map/ppermute | solution.py:47
